TPU v7x, 32 devices: a whole 2x2x4 slice. The times are simulated.
32 devices in a mesh: group: 2 (over x), loop: 16 (over z, y, core).
Axes of the slice: x: 2, y: 2, z: 4, core: 2. Of those that a mesh axis runs over, the one named last changes fastest.
Arguments:
- users: float32 [8192, 512], P(('group', 'loop')), parts along dimension 0, may hold values from -1.3 to 1.3
- items: bfloat16 [4096, 512], P(('group', 'loop')), parts along dimension 0, may hold values from -1.296875 to 1.296875
- tile_blocks: int32 [32, 8], P(('group', 'loop')), parts along dimension 0, may hold values from 0 to 15, as said below
- tile_count: int32 [32], P(('group', 'loop')), parts along dimension 0, may hold values from 1 to 8, as said below
- labels: int32 [8192, 1024], P(('group', 'loop')), parts along dimension 0, may hold values 0 or 1
Outputs:
- new_users: float32 [8192, 512], P(('group', 'loop')), parts along dimension 0
There are 2 independent parts, one for each index of `group`. A program takes and returns all parts, laid end to end along the dimension named above; each array names one. Nothing has to cross between parts.
Inputs may be any that keep to these rules, and one draw needn't show every extreme that they name: `tile_blocks`: in each row the entries are distinct item blocks; only the first tile_count of them are used. `tile_count`: some user block has all 8 tiles live.
All inputs are finite; a program needn't handle non-finite values. No bound on the sum of `labels` on one device may be relied on, other than what follows from the above.
Results may differ from a plain program's by a relative error of at most 0.0003.
Values may be sent and summed in bfloat16 or wider, within the bound.
No kernel may reach another device: no remote copies, remote signals or barrier semaphores. Data moves between devices by JAX's collectives and lax.ppermute only.
A program may use at most 64 MiB of HBM per device.

v0:
```python
import jax
import jax.numpy as jnp
from jax import lax
from jax.sharding import PartitionSpec as P


def slot_table(block_list, live_count, lowest, loop_size):
    slot_ids = jnp.arange(block_list.shape[0], dtype=jnp.int32)
    block_ids = jnp.arange(loop_size, dtype=jnp.int32)
    usable = (slot_ids >= lowest) & (slot_ids < live_count)
    matches = (block_list[None, :] == block_ids[:, None]) & usable[None, :]
    return jnp.sum(jnp.where(matches, slot_ids[None, :] + 1, 0), axis=1) - 1


def score_tile(user_rows, item_block):
    return jnp.dot(
        user_rows, item_block.T, precision=lax.Precision.HIGHEST, preferred_element_type=jnp.float32
    )


def apply_tile(weights, item_block):
    return jnp.dot(
        weights, item_block, precision=lax.Precision.HIGHEST, preferred_element_type=jnp.float32
    )


def label_slice(labels, slot_index, tile_width):
    return lax.dynamic_slice_in_dim(labels, slot_index * tile_width, tile_width, 1).astype(
        jnp.float32
    )


def take_block(piece, index, tile_width):
    return lax.dynamic_slice_in_dim(piece, index * tile_width, tile_width, 0).astype(jnp.float32)


def local(users, items, tile_blocks, tile_count, labels):
    tile_width = items.shape[0]
    loop_size = lax.axis_size("loop")
    block_list = tile_blocks[0]
    live_count = tile_count[0]
    zero_grad = jnp.zeros(users.shape, jnp.float32)
    own_slots = slot_table(block_list, live_count, 0, loop_size)
    piece = lax.all_gather(items, "loop", axis=0, tiled=True)

    def sweep_blocks(index, current):
        item_block = take_block(piece, index, tile_width)
        own_index = own_slots[index]

        def full_work(values):
            residual = jax.nn.sigmoid(score_tile(users, item_block)) - label_slice(
                labels, own_index, tile_width
            )
            return values + apply_tile(residual, item_block)

        return lax.cond(own_index >= 0, full_work, lambda values: values, current)

    gradient = lax.fori_loop(0, piece.shape[0] // tile_width, sweep_blocks, zero_grad)
    squares = lax.psum(jnp.sum(gradient * gradient), "loop")
    entries = users.shape[0] * loop_size * users.shape[1]
    grad_rms = jnp.sqrt(squares / entries + 1e-06)
    step_scale = 0.5 / grad_rms
    return users - step_scale * gradient


def solution(mesh):
    in_specs = (
        P(("group", "loop"), None),
        P(("group", "loop"), None),
        P(("group", "loop"), None),
        P(("group", "loop")),
        P(("group", "loop"), None),
    )
    out_specs = P(("group", "loop"), None)
    return jax.shard_map(local, mesh=mesh, in_specs=in_specs, out_specs=out_specs, check_vma=False)
```

profile of v0, /device:TPU:0, one launch (start us, length us, event | category | flops | bytes accessed | tf_op | source)
XLA Modules:
  0.0 151.2 jit_solution(4210043578784997191)
XLA Ops:
  6.5 0.0 all-gather.2.cloned.1.call-start
  6.5 0.7 all-gather.2.cloned.1.call-update
  7.9 0.7 select_reduce_fusion
  8.7 45.0 %all-gather.2.cloned.1.call-done = bf16[2048,512]{1,0:T(8,128)(2,1)} async-done(((bf16[128,512]{1,0:T(8,128)(2,1)}), bf16[2048,512]{1,0:T(8,128)(2,1)}) %all-gather.2.cloned.1.call-update) | async-done | bytes 2097168 | tf_op jit(solution)/shard_map/all_gather | solution.py:44
  53.7 41.1 %while.16 = (s32[]{:T(128)}, f32[256,512]{1,0:T(8,128)S(1)}, s32[16]{0:T(128)S(1)}, bf16[2048,512]{1,0:T(8,128)(2,1)}, f32[256,512]{1,0:T(8,128)}, /*index=5*/s3...) while((s32[]{:T(128)}, f32[256,512]{1,0:T(8,128)S(1)}, s32[16]{0:T(128)S(1)}, ...), condition=%wide.region_4.5_spmd, body=%wide.region_1.4_spmd.sunk | while | flops 403013632 | bytes 2883867 | solution.py:58
  53.7 0.6 dynamic_slice.22
  55.0 0.9 dynamic-slice_convert_fusion.2
  55.9 0.6 dynamic_slice.22
  57.2 0.9 dynamic-slice_convert_fusion.2
  58.1 0.6 dynamic_slice.22
  59.4 0.9 dynamic-slice_convert_fusion.2
  60.3 0.6 dynamic_slice.22
  61.6 0.9 dynamic-slice_convert_fusion.2
  62.5 0.6 dynamic_slice.22
  63.8 0.9 dynamic-slice_convert_fusion.2
  64.7 2.9 %conditional.2 = (f32[256,512]{1,0:T(8,128)S(1)}) conditional(s32[]{:T(128)} %convert_element_type.22, f32[256,512]{1,0:T(8,128)S(1)} %get-tuple-element.198, (f32[256,512]{1,0:T(8,128)}, f32[128,512]{1,0:T(8,128)S(1)}, s32[]{:T(128)}, s32[256,1024]{1,0:T(8,128)}, f32[256,512]{1,0:T(8,128)S(1)}) %tuple.39), branch_computations={%region_2.2_spmd, %region_3.3_spmd} | conditional | flops 402948096 | bytes 2490426 | solution.py:56
  65.3 1.7 %fusion.3 = f32[256,128]{1,0:T(8,128)S(1)} fusion(f32[256,512]{1,0:T(8,128)} %get-tuple-element.125, f32[128,512]{1,0:T(8,128)S(1)} %get-tuple-element.126, s32[256,1024]{1,0:T(8,128)} %get-tuple-element.127, s32[]{:T(128)S(6)} %select_n.16), kind=kOutput, calls=%fused_computation.5 | convolution fusion | flops 201490432 | bytes 1048580 | tf_op jit(solution)/shard_map/while/body/eval_jaxpr/cond/branch_1_fun/dot_general | solution.py:16
  67.0 0.6 convolution_add_fusion
  67.7 0.6 dynamic_slice.22
  68.9 0.9 dynamic-slice_convert_fusion.2
  69.9 0.6 dynamic_slice.22
  71.1 0.9 dynamic-slice_convert_fusion.2
  72.1 0.6 dynamic_slice.22
  73.3 0.9 dynamic-slice_convert_fusion.2
  74.3 0.6 dynamic_slice.22
  75.5 0.9 dynamic-slice_convert_fusion.2
  76.5 0.6 dynamic_slice.22
  77.7 0.9 dynamic-slice_convert_fusion.2
  78.6 2.9 %conditional.2 = (f32[256,512]{1,0:T(8,128)S(1)}) conditional(s32[]{:T(128)} %convert_element_type.22, f32[256,512]{1,0:T(8,128)S(1)} %get-tuple-element.198, (f32[256,512]{1,0:T(8,128)}, f32[128,512]{1,0:T(8,128)S(1)}, s32[]{:T(128)}, s32[256,1024]{1,0:T(8,128)}, f32[256,512]{1,0:T(8,128)S(1)}) %tuple.39), branch_computations={%region_2.2_spmd, %region_3.3_spmd} | conditional | flops 402948096 | bytes 2490426 | solution.py:56
  79.3 1.7 %fusion.3 = f32[256,128]{1,0:T(8,128)S(1)} fusion(f32[256,512]{1,0:T(8,128)} %get-tuple-element.125, f32[128,512]{1,0:T(8,128)S(1)} %get-tuple-element.126, s32[256,1024]{1,0:T(8,128)} %get-tuple-element.127, s32[]{:T(128)S(6)} %select_n.16), kind=kOutput, calls=%fused_computation.5 | convolution fusion | flops 201490432 | bytes 1048580 | tf_op jit(solution)/shard_map/while/body/eval_jaxpr/cond/branch_1_fun/dot_general | solution.py:16
  80.9 0.6 convolution_add_fusion
  81.6 0.6 dynamic_slice.22
  82.8 0.9 dynamic-slice_convert_fusion.2
  83.8 0.6 dynamic_slice.22
  85.0 0.9 dynamic-slice_convert_fusion.2
  86.0 0.6 dynamic_slice.22
  87.2 0.9 dynamic-slice_convert_fusion.2
  88.2 0.6 dynamic_slice.22
  89.4 0.9 dynamic-slice_convert_fusion.2
  90.4 0.6 dynamic_slice.22
  91.6 0.9 dynamic-slice_convert_fusion.2
  92.6 0.6 dynamic_slice.22
  93.8 0.9 dynamic-slice_convert_fusion.2
  94.8 0.7 multiply_reduce_fusion
  95.5 46.2 %psum.7 = f32[]{:T(128)} all-reduce(f32[]{:T(128)} %multiply_reduce_fusion), channel_id=1, replica_groups=mesh['group'=2,'loop'=16] {'loop'}, use_global_device_ids=true, to_apply=%region_6.7 | all-reduce | flops 1 | bytes 8 | tf_op jit(solution)/shard_map/psum | solution.py:59
  142.4 1.9 %multiply_subtract_fusion = f32[256,512]{1,0:T(8,128)} fusion(f32[256,512]{1,0:T(8,128)} %get-tuple-element.219, f32[256,512]{1,0:T(8,128)S(1)} %get-tuple-element.137, f32[]{:T(128)S(6)} %div.10), kind=kLoop, calls=%fused_computation.7 | loop fusion | flops 262144 | bytes 1572868 | tf_op jit(solution)/shard_map/sub | solution.py:63
  (18 shorter events, 0.3 us)
Async XLA Ops:
  6.5 47.1 %all-gather.2.cloned.1.call-start = ((), (), s32[]{:S(2)}) async-start(), calls=%async_computation | async-start | bytes 2228224 | tf_op jit(solution)/shard_map/all_gather | solution.py:44
Sparse Core Ops, SparseCore 0:
  9.5 44.0 all-gather.1
where the time goes:
time: 153 us; the launch traced here: 151 us
  blocking collectives  46.2 us (30%)
  waiting for transfers between devices  45.7 us (30%)
  other arithmetic  18.3 us (12%)
  between operations  14.8 us (10%)
  loops' own time  12.1 us (8%)
  local copies, waits for them, and re-layouts  9.56 us (6%)
  matrix products  4.6 us (3%)
    psum x1, blocking collectives, local(): squares = lax.psum(jnp.sum(gradient * gradient), 'loop')  46.2 us
    all_gather x1, waiting for transfers between devices, local(): piece = lax.all_gather(items, 'loop', axis=0, tiled=True)  45 us
    convert_element_type x16, other arithmetic, take_block(): lax.dynamic_slice_in_dim(piece, index * tile_width, tile_width, 0)  14.9 us
    another operation x1, loops' own time, local(): lax.fori_loop(0, piece.shape[0] // tile_width, sweep_blocks, zero_grad)  10.5 us
    dynamic_slice x16, local copies, waits for them, and re-layouts, sweep_blocks(): own_index = own_slots[index]  9.51 us
    dot_general x2, matrix products, score_tile(): jnp.dot(user_rows, item_block.T, precision=lax.Precision.HIGHEST, preferr...  3.32 us
  transfers between devices with their start and end apart: 1, of which 1 were waited for; matrix products, arithmetic and copies ran while one was open for 1% of the time, Pallas kernels for 0%

commit v1 on v0

v1 whole, which is shorter than its diff:
```python
import functools

import jax
import jax.numpy as jnp
from jax import lax
from jax.experimental import pallas as pl
from jax.experimental.pallas import tpu as pltpu
from jax.sharding import PartitionSpec as P

CHUNK = 8
DIRECT_LIMIT = 16


def split_loop(loop_size):
    cores = 2 if loop_size % 2 == 0 else 1
    chips = loop_size // cores
    inner = 1
    while inner * inner * 4 <= chips:
        inner *= 2
    if chips % inner:
        inner = 1
    return chips // inner, inner, cores


def shifted(array, dims, axis, shift):
    outer, inner, cores = dims
    pairs = []
    for source in range(outer * inner * cores):
        place = [source // (inner * cores), source // cores % inner, source % cores]
        place[axis] = (place[axis] + shift) % dims[axis]
        pairs.append((source, (place[0] * inner + place[1]) * cores + place[2]))
    return lax.ppermute(array, "loop", pairs)


def spread(array, dims):
    held = [((0, 0, 0), array)]
    for axis in range(3):
        for shifts, piece in list(held):
            for shift in range(1, dims[axis]):
                moved = list(shifts)
                moved[axis] = shift
                held.append((tuple(moved), shifted(piece, dims, axis, shift)))
    return held


def halves(values):
    upper = values.astype(jnp.bfloat16)
    return jnp.concatenate([upper, (values - upper.astype(jnp.float32)).astype(jnp.bfloat16)], 0)


def gradient_kernel(
    fetch, refs, list_ref, count_ref, users_ref, labels_ref, *rest
):
    pieces = rest[:refs]
    grad_ref, square_ref, tiles, parts, sems = rest[refs:]
    rows, width = users_ref.shape
    tile = tiles.shape[0] // CHUNK
    step = pl.program_id(0)
    live = jnp.minimum(count_ref[0] - step * CHUNK, CHUNK)

    @pl.when(step == 0)
    def _():
        grad_ref[...] = jnp.zeros_like(grad_ref)

    fetch(list_ref, step, live, pieces, tiles, sems, False)

    @pl.when(step == 0)
    def _():
        parts[...] = halves(users_ref[...])

    @pl.when((live > 0) & (live % 2 == 1))
    def _():
        blank = pl.multiple_of(live * tile, tile)
        tiles[pl.ds(blank, tile), :] = jnp.zeros((tile, width), tiles.dtype)

    fetch(list_ref, step, live, pieces, tiles, sems, True)

    def pair(index, carry):
        start = pl.multiple_of(index * 2 * tile, 2 * tile)
        block = tiles[pl.ds(start, 2 * tile), :]
        both = lax.dot_general(
            parts[...], block, (((1,), (1,)), ((), ())), preferred_element_type=jnp.float32
        )
        scores = both[:rows] + both[rows:]
        chance = 0.5 * jnp.tanh(0.5 * scores) + 0.5
        labels = labels_ref[:, pl.ds(start, 2 * tile)].astype(jnp.float32)
        column = start + lax.broadcasted_iota(jnp.int32, scores.shape, 1)
        residual = jnp.where(column < live * tile, chance - labels, 0.0)
        both = jnp.dot(halves(residual), block, preferred_element_type=jnp.float32)
        grad_ref[...] += both[:rows] + both[rows:]
        return carry

    lax.fori_loop(0, (jnp.maximum(live, 0) + 1) // 2, pair, 0)

    @pl.when(step == pl.num_programs(0) - 1)
    def _():
        gradient = grad_ref[...]
        square = jnp.sum(gradient * gradient, axis=0, keepdims=True)
        square_ref[...] = sum(square[:, at : at + 128] for at in range(0, width, 128))


def fetch_list(dims, shifts, list_ref, step, live, pieces, tiles, sems, wait):
    tile = pieces[0].shape[0]
    outer, inner, cores = dims
    me = lax.axis_index("loop")
    place = (me // (inner * cores), me // cores % inner, me % cores)
    wanted = [jnp.where(slot < live, list_ref[0, step * CHUNK + slot], -1) for slot in range(CHUNK)]
    for piece, shift in zip(pieces, shifts):
        at = [lax.rem(p - s + d, d) for p, s, d in zip(place, shift, dims)]
        block = (at[0] * inner + at[1]) * cores + at[2]
        found = jnp.int32(-1)
        for slot in range(CHUNK):
            found = jnp.where(wanted[slot] == block, slot, found)

        @pl.when(found >= 0)
        def _():
            start = pl.multiple_of(found * tile, tile)
            copy = pltpu.make_async_copy(piece, tiles.at[pl.ds(start, tile), :], sems.at[found])
            if wait:
                copy.wait()
            else:
                copy.start()


def fetch_whole(list_ref, step, live, pieces, tiles, sems, wait):
    tile = tiles.shape[0] // CHUNK
    for slot in range(CHUNK):

        @pl.when(slot < live)
        def _():
            start = pl.multiple_of(list_ref[0, step * CHUNK + slot] * tile, tile)
            copy = pltpu.make_async_copy(
                pieces[0].at[pl.ds(start, tile), :], tiles.at[pl.ds(slot * tile, tile), :], sems.at[slot]
            )
            if wait:
                copy.wait()
            else:
                copy.start()


def update_kernel(entries, users_ref, grad_ref, *rest):
    squares, out_ref = rest[:-1], rest[-1]
    total = squares[0][...]
    for square in squares[1:]:
        total = total + square[...]
    total = jnp.sum(total, axis=1, keepdims=True)
    scale = 0.5 / jnp.sqrt(total / entries + 1e-06)
    out_ref[...] = users_ref[...] - scale * grad_ref[...]


def local(users, items, tile_blocks, tile_count, labels):
    loop_size = lax.axis_size("loop")
    rows, width = users.shape
    tile = items.shape[0]
    slots = tile_blocks.shape[1]
    dims = split_loop(loop_size)
    direct = loop_size <= DIRECT_LIMIT
    if direct:
        held = spread(items, dims)
        pieces = [piece for _, piece in held]
        fetch = functools.partial(fetch_list, dims, [shifts for shifts, _ in held])
    else:
        pieces = [lax.all_gather(items, "loop", axis=0, tiled=True)]
        fetch = fetch_whole

    gradient, square = pl.pallas_call(
        functools.partial(gradient_kernel, fetch, len(pieces)),
        grid=(slots // CHUNK,),
        out_shape=[
            jax.ShapeDtypeStruct((rows, width), jnp.float32),
            jax.ShapeDtypeStruct((1, 128), jnp.float32),
        ],
        in_specs=[
            pl.BlockSpec(memory_space=pltpu.SMEM),
            pl.BlockSpec(memory_space=pltpu.SMEM),
            pl.BlockSpec((rows, width), lambda step: (0, 0)),
            pl.BlockSpec((rows, CHUNK * tile), lambda step: (0, step)),
        ]
        + [pl.BlockSpec(memory_space=pl.ANY)] * len(pieces),
        out_specs=[
            pl.BlockSpec((rows, width), lambda step: (0, 0)),
            pl.BlockSpec((1, 128), lambda step: (0, 0)),
        ],
        scratch_shapes=[
            pltpu.VMEM((CHUNK * tile, width), jnp.bfloat16),
            pltpu.VMEM((2 * rows, width), jnp.bfloat16),
            pltpu.SemaphoreType.DMA((CHUNK,)),
        ],
        compiler_params=pltpu.CompilerParams(vmem_limit_bytes=32 * 1024 * 1024),
        cost_estimate=pl.CostEstimate(
            flops=8 * rows * width * slots * tile,
            bytes_accessed=4 * rows * (slots * tile + 2 * width) + 2 * slots * tile * width,
            transcendentals=rows * slots * tile,
        ),
        name="gradient",
    )(tile_blocks, tile_count, users, labels, *pieces)

    if direct:
        squares = [piece for _, piece in [((0, 0, 0), square)]]
        squares += [
            lax.ppermute(square, "loop", [(at, (at + shift) % loop_size) for at in range(loop_size)])
            for shift in range(1, loop_size)
        ]
    else:
        squares = [lax.psum(square, "loop")]

    return pl.pallas_call(
        functools.partial(update_kernel, rows * loop_size * width),
        out_shape=jax.ShapeDtypeStruct((rows, width), jnp.float32),
        in_specs=[pl.BlockSpec(memory_space=pltpu.VMEM)] * (2 + len(squares)),
        out_specs=pl.BlockSpec(memory_space=pltpu.VMEM),
        compiler_params=pltpu.CompilerParams(vmem_limit_bytes=16 * 1024 * 1024),
        cost_estimate=pl.CostEstimate(
            flops=2 * rows * width, bytes_accessed=12 * rows * width, transcendentals=0
        ),
        name="update",
    )(users, gradient, *squares)


def solution(mesh):
    in_specs = (
        P(("group", "loop"), None),
        P(("group", "loop"), None),
        P(("group", "loop"), None),
        P(("group", "loop")),
        P(("group", "loop"), None),
    )
    out_specs = P(("group", "loop"), None)
    return jax.shard_map(local, mesh=mesh, in_specs=in_specs, out_specs=out_specs, check_vma=False)
```

time: 153 us -> 62.6 us (0.41); the launches traced: 151 us -> 62.3 us
  blocking collectives: 46.2 us -> 0 us
  starting transfers between devices: 0.01 us -> 28.4 us
  waiting for transfers between devices: 45.7 us -> 23 us
  other arithmetic: 18.3 us -> 0 us
  between operations: 14.8 us -> 0.75 us
  loops' own time: 12.1 us -> 0 us
  Pallas kernels: 0 us -> 6.93 us
  local copies, waits for them, and re-layouts: 9.56 us -> 3.17 us
  matrix products: 4.6 us -> 0 us
    psum x1 -> x0, blocking collectives: 46.2 us -> none  [local(): squares = lax.psum(jnp.sum(gradient * gradient), 'loop')]
    all_gather x1 -> x0, waiting for transfers between devices: 45 us -> none  [local(): piece = lax.all_gather(items, 'loop', axis=0, tiled=True)]
    ppermute x0 -> x30, starting transfers between devices: none -> 28.4 us  [the longest x15 17.3 us: local(): lax.ppermute(square, 'loop', [(at, (at + shift) % loop_size) for at in ra...]
    ppermute x0 -> x30, waiting for transfers between devices: none -> 23 us  [the longest x15 17.3 us: shifted(): return lax.ppermute(array, 'loop', pairs)]
    convert_element_type x16 -> x0, other arithmetic: 14.9 us -> none  [take_block(): lax.dynamic_slice_in_dim(piece, index * tile_width, tile_width, 0)]
    another operation x17 -> x0, loops' own time: 12.1 us -> none  [the longest x1 10.5 us: local(): lax.fori_loop(0, piece.shape[0] // tile_width, sweep_blocks, zero_grad)]
    dynamic_slice x16 -> x0, local copies, waits for them, and re-layouts: 9.51 us -> none  [sweep_blocks(): own_index = own_slots[index]]
    pallas_call x0 -> x2, Pallas kernels: none -> 6.93 us  [the longest x1 5.94 us: local(): pl.pallas_call(functools.partial(gradient_kernel, fetch, len(pieces)), gr...]
  transfers between devices with their start and end apart: 1 -> 30, of which waited for: 1 -> 9; matrix products, arithmetic and copies ran while one was open for 1% -> 0% of each run, Pallas kernels for 0% -> 0%
where the time goes in v1:
time: 62.6 us; the launch traced here: 62.3 us
  starting transfers between devices  28.4 us (45%)
  waiting for transfers between devices  23 us (37%)
  Pallas kernels  6.93 us (11%)
  local copies, waits for them, and re-layouts  3.17 us (5%)
  between operations  0.75 us (1%)
    ppermute x15, waiting for transfers between devices, shifted(): return lax.ppermute(array, 'loop', pairs)  17.3 us
    ppermute x15, starting transfers between devices, local(): lax.ppermute(square, 'loop', [(at, (at + shift) % loop_size) for at in ra...  17.3 us
    ppermute x15, starting transfers between devices, shifted(): return lax.ppermute(array, 'loop', pairs)  11.1 us
    pallas_call x1, Pallas kernels, local(): pl.pallas_call(functools.partial(gradient_kernel, fetch, len(pieces)), gr...  5.94 us
    ppermute x15, waiting for transfers between devices, local(): lax.ppermute(square, 'loop', [(at, (at + shift) % loop_size) for at in ra...  5.67 us
    unnamed x8, local copies, waits for them, and re-layouts  3.17 us
  transfers between devices with their start and end apart: 30, of which 9 were waited for; matrix products, arithmetic and copies ran while one was open for 0% of the time, Pallas kernels for 0%

profile of v1, /device:TPU:0, one launch (start us, length us, event | category | flops | bytes accessed | tf_op | source)
XLA Modules:
  0.0 62.3 jit_solution(12795278241309749847)
XLA Ops:
  0.0 3.0 %collective-permute-start.3 = (bf16[128,512]{1,0:T(8,128)(2,1)}, bf16[128,512]{1,0:T(8,128)(2,1)S(1)}, u32[]{:S(2)}, u32[]{:S(2)}) collective-permute-start(bf16[128,512]{1,0:T(8,128)(2,1)} %rest_0_.1), channel_id=1, source_target_pairs={{0,2},{1,3},{2,0},{3,1},{4,6},{5,7},{6,4},{7,5},{8,10},{9,11},{10,... | collective-permute-start | bytes 393224 | tf_op jit(solution)/shard_map/ppermute | solution.py:32
  3.0 3.6 %collective-permute-start.2 = (bf16[128,512]{1,0:T(8,128)(2,1)}, bf16[128,512]{1,0:T(8,128)(2,1)S(1)}, u32[]{:S(2)}, u32[]{:S(2)}) collective-permute-start(bf16[128,512]{1,0:T(8,128)(2,1)} %rest_0_.1), channel_id=1, source_target_pairs={{0,12},{1,13},{2,14},{3,15},{4,0},{5,1},{6,2},{7,3},{8,4},{9,5},{1... | collective-permute-start | bytes 393224 | tf_op jit(solution)/shard_map/ppermute | solution.py:32
  6.6 0.0 collective-permute-start.1
  6.6 1.0 %collective-permute-start = (bf16[128,512]{1,0:T(8,128)(2,1)}, bf16[128,512]{1,0:T(8,128)(2,1)S(1)}, u32[]{:S(2)}, u32[]{:S(2)}) collective-permute-start(bf16[128,512]{1,0:T(8,128)(2,1)} %rest_0_.1), channel_id=1, source_target_pairs={{0,4},{1,5},{2,6},{3,7},{4,8},{5,9},{6,10},{7,11},{8,12},{9,13},{1... | collective-permute-start | bytes 393224 | tf_op jit(solution)/shard_map/ppermute | solution.py:32
  7.6 0.0 collective-permute-start.7
  7.6 0.0 collective-permute-done.3.rest_4_
  7.6 0.5 collective-permute-start.11
  8.1 2.7 %collective-permute-done.2.rest_3_ = bf16[128,512]{1,0:T(8,128)(2,1)S(1)} collective-permute-done((bf16[128,512]{1,0:T(8,128)(2,1)}, bf16[128,512]{1,0:T(8,128)(2,1)S(1)}, u32[]{:S(2)}, u32[]{:S(2)}) %collective-permute-start.2) | collective-permute-done | bytes 131104 | tf_op jit(solution)/shard_map/ppermute | solution.py:32
  10.8 6.8 %collective-permute-done.1.rest_2_ = bf16[128,512]{1,0:T(8,128)(2,1)S(1)} collective-permute-done((bf16[128,512]{1,0:T(8,128)(2,1)}, bf16[128,512]{1,0:T(8,128)(2,1)S(1)}, u32[]{:S(2)}, u32[]{:S(2)}) %collective-permute-start.1) | collective-permute-done | bytes 131104 | tf_op jit(solution)/shard_map/ppermute | solution.py:32
  17.6 0.5 collective-permute-start.6
  18.1 1.5 %collective-permute-start.5 = (bf16[128,512]{1,0:T(8,128)(2,1)S(1)}, bf16[128,512]{1,0:T(8,128)(2,1)S(1)}, u32[]{:S(2)}, u32[]{:S(2)}) collective-permute-start(bf16[128,512]{1,0:T(8,128)(2,1)S(1)} %collective-permute-done.1.rest_2_), channel_id=1, source_target_pairs={{0,2},{1,3},{2,0},{3,1},{4,6},{5,7},{6,4},{7,5},{8,10},{9,11},{10,... | collective-permute-start | bytes 393224 | tf_op jit(solution)/shard_map/ppermute | solution.py:32
  19.6 0.5 collective-permute-start.4
  20.1 0.0 collective-permute-done.11.rest_12_
  20.1 0.0 collective-permute-start.9
  20.1 0.5 collective-permute-start.8
  20.6 3.4 %collective-permute-done.6.rest_7_ = bf16[128,512]{1,0:T(8,128)(2,1)S(1)} collective-permute-done((bf16[128,512]{1,0:T(8,128)(2,1)S(1)}, bf16[128,512]{1,0:T(8,128)(2,1)S(1)}, u32[]{:S(2)}, u32[]{:S(2)}) %collective-permute-start.6) | collective-permute-done | bytes 131104 | tf_op jit(solution)/shard_map/ppermute | solution.py:32
  24.0 0.0 collective-permute-start.14
  24.0 2.4 %collective-permute-done.5.rest_6_ = bf16[128,512]{1,0:T(8,128)(2,1)S(1)} collective-permute-done((bf16[128,512]{1,0:T(8,128)(2,1)S(1)}, bf16[128,512]{1,0:T(8,128)(2,1)S(1)}, u32[]{:S(2)}, u32[]{:S(2)}) %collective-permute-start.5) | collective-permute-done | bytes 131104 | tf_op jit(solution)/shard_map/ppermute | solution.py:32
  26.4 0.0 collective-permute-start.13
  26.4 1.4 %collective-permute-done.4.rest_5_ = bf16[128,512]{1,0:T(8,128)(2,1)S(1)} collective-permute-done((bf16[128,512]{1,0:T(8,128)(2,1)S(1)}, bf16[128,512]{1,0:T(8,128)(2,1)S(1)}, u32[]{:S(2)}, u32[]{:S(2)}) %collective-permute-start.4) | collective-permute-done | bytes 131104 | tf_op jit(solution)/shard_map/ppermute | solution.py:32
  27.8 0.0 collective-permute-start.12
  28.5 0.0 collective-permute-done.8.rest_9_
  28.5 0.0 collective-permute-done.14.rest_15_
  28.5 0.7 %collective-permute-done.12.rest_13_ = bf16[128,512]{1,0:T(8,128)(2,1)S(1)} collective-permute-done((bf16[128,512]{1,0:T(8,128)(2,1)S(1)}, bf16[128,512]{1,0:T(8,128)(2,1)S(1)}, u32[]{:S(2)}, u32[]{:S(2)}) %collective-permute-start.12) | collective-permute-done | bytes 131104 | tf_op jit(solution)/shard_map/ppermute | solution.py:32
  29.2 1.0 %copy-done = f32[256,512]{1,0:T(8,128)S(1)} copy-done((f32[256,512]{1,0:T(8,128)S(1)}, f32[256,512]{1,0:T(8,128)}, u32[]{:S(2)}) %copy-start) | copy-done | bytes 524312
  30.2 1.2 %copy-done.1 = s32[256,1024]{1,0:T(8,128)S(1)} copy-done((s32[256,1024]{1,0:T(8,128)S(1)}, s32[256,1024]{1,0:T(8,128)}, u32[]{:S(2)}) %copy-start.1) | copy-done | bytes 1048600
  31.5 0.9 %copy-done.2 = bf16[128,512]{1,0:T(8,128)(2,1)S(1)} copy-done((bf16[128,512]{1,0:T(8,128)(2,1)S(1)}, bf16[128,512]{1,0:T(8,128)(2,1)}, u32[]{:S(2)}) %copy-start.2) | copy-done | bytes 131096
  32.4 5.9 %gradient.1 = (f32[256,512]{1,0:T(8,128)S(1)}, f32[1,128]{1,0:T(1,128)S(1)}) custom-call(s32[1,8]{1,0:T(1,128)S(1)} %copy-done.3, s32[1]{0:T(128)S(6)} %copy.6.count_ref, f32[256,512]{1,0:T(8,128)S(1)} %copy-done, s32[256,1024]{1,0:T(8,128)S(1)} %copy-done.1, bf16[128,512]{1,0:T(8,128)(2,1)S(1)} %copy-done.2, ...), custom_call_target="tpu_custom_call" | custom-call | flops 1073741824 | bytes 3145728 | tf_op jit(solution)/shard_map/gradient/pallas_call | solution.py:166
  38.3 0.1 collective-permute-start.29
  38.4 0.5 collective-permute-start.28
  38.9 0.1 collective-permute-start.27
  39.0 1.1 %collective-permute-start.26 = (f32[1,128]{1,0:T(1,128)S(1)}, f32[1,128]{1,0:T(1,128)S(1)}, u32[]{:S(2)}, u32[]{:S(2)}) collective-permute-start(f32[1,128]{1,0:T(1,128)S(1)} %get-tuple-element.8.rest_0_), channel_id=1, source_target_pairs={{0,12},{1,13},{2,14},{3,15},{4,0},{5,1},{6,2},{7,3},{8,4},{9,5},{1... | collective-permute-start | bytes 1544 | tf_op jit(solution)/shard_map/ppermute | solution.py:201
  40.1 2.7 %collective-permute-start.25 = (f32[1,128]{1,0:T(1,128)S(1)}, f32[1,128]{1,0:T(1,128)S(1)}, u32[]{:S(2)}, u32[]{:S(2)}) collective-permute-start(f32[1,128]{1,0:T(1,128)S(1)} %get-tuple-element.8.rest_0_), channel_id=1, source_target_pairs={{0,11},{1,12},{2,13},{3,14},{4,15},{5,0},{6,1},{7,2},{8,3},{9,4},{... | collective-permute-start | bytes 1544 | tf_op jit(solution)/shard_map/ppermute | solution.py:201
  42.8 0.0 collective-permute-done.29.rest_15_
  42.8 1.5 %collective-permute-start.24 = (f32[1,128]{1,0:T(1,128)S(1)}, f32[1,128]{1,0:T(1,128)S(1)}, u32[]{:S(2)}, u32[]{:S(2)}) collective-permute-start(f32[1,128]{1,0:T(1,128)S(1)} %get-tuple-element.8.rest_0_), channel_id=1, source_target_pairs={{0,10},{1,11},{2,12},{3,13},{4,14},{5,15},{6,0},{7,1},{8,2},{9,3},... | collective-permute-start | bytes 1544 | tf_op jit(solution)/shard_map/ppermute | solution.py:201
  44.3 1.8 %collective-permute-start.22 = (f32[1,128]{1,0:T(1,128)S(1)}, f32[1,128]{1,0:T(1,128)S(1)}, u32[]{:S(2)}, u32[]{:S(2)}) collective-permute-start(f32[1,128]{1,0:T(1,128)S(1)} %get-tuple-element.8.rest_0_), channel_id=1, source_target_pairs={{0,8},{1,9},{2,10},{3,11},{4,12},{5,13},{6,14},{7,15},{8,0},{9,1},... | collective-permute-start | bytes 1544 | tf_op jit(solution)/shard_map/ppermute | solution.py:201
  46.0 0.0 collective-permute-done.26.rest_12_
  46.0 1.7 %collective-permute-start.21 = (f32[1,128]{1,0:T(1,128)S(1)}, f32[1,128]{1,0:T(1,128)S(1)}, u32[]{:S(2)}, u32[]{:S(2)}) collective-permute-start(f32[1,128]{1,0:T(1,128)S(1)} %get-tuple-element.8.rest_0_), channel_id=1, source_target_pairs={{0,7},{1,8},{2,9},{3,10},{4,11},{5,12},{6,13},{7,14},{8,15},{9,0},... | collective-permute-start | bytes 1544 | tf_op jit(solution)/shard_map/ppermute | solution.py:201
  47.8 0.0 collective-permute-done.25.rest_11_
  47.8 1.5 %collective-permute-start.20 = (f32[1,128]{1,0:T(1,128)S(1)}, f32[1,128]{1,0:T(1,128)S(1)}, u32[]{:S(2)}, u32[]{:S(2)}) collective-permute-start(f32[1,128]{1,0:T(1,128)S(1)} %get-tuple-element.8.rest_0_), channel_id=1, source_target_pairs={{0,6},{1,7},{2,8},{3,9},{4,10},{5,11},{6,12},{7,13},{8,14},{9,15},... | collective-permute-start | bytes 1544 | tf_op jit(solution)/shard_map/ppermute | solution.py:201
  49.3 0.8 %collective-permute-start.19 = (f32[1,128]{1,0:T(1,128)S(1)}, f32[1,128]{1,0:T(1,128)S(1)}, u32[]{:S(2)}, u32[]{:S(2)}) collective-permute-start(f32[1,128]{1,0:T(1,128)S(1)} %get-tuple-element.8.rest_0_), channel_id=1, source_target_pairs={{0,5},{1,6},{2,7},{3,8},{4,9},{5,10},{6,11},{7,12},{8,13},{9,14},{... | collective-permute-start | bytes 1544 | tf_op jit(solution)/shard_map/ppermute | solution.py:201
  50.1 1.8 %collective-permute-start.18 = (f32[1,128]{1,0:T(1,128)S(1)}, f32[1,128]{1,0:T(1,128)S(1)}, u32[]{:S(2)}, u32[]{:S(2)}) collective-permute-start(f32[1,128]{1,0:T(1,128)S(1)} %get-tuple-element.8.rest_0_), channel_id=1, source_target_pairs={{0,4},{1,5},{2,6},{3,7},{4,8},{5,9},{6,10},{7,11},{8,12},{9,13},{1... | collective-permute-start | bytes 1544 | tf_op jit(solution)/shard_map/ppermute | solution.py:201
  51.9 2.1 %collective-permute-start.17 = (f32[1,128]{1,0:T(1,128)S(1)}, f32[1,128]{1,0:T(1,128)S(1)}, u32[]{:S(2)}, u32[]{:S(2)}) collective-permute-start(f32[1,128]{1,0:T(1,128)S(1)} %get-tuple-element.8.rest_0_), channel_id=1, source_target_pairs={{0,3},{1,4},{2,5},{3,6},{4,7},{5,8},{6,9},{7,10},{8,11},{9,12},{10... | collective-permute-start | bytes 1544 | tf_op jit(solution)/shard_map/ppermute | solution.py:201
  54.0 1.6 %collective-permute-start.16 = (f32[1,128]{1,0:T(1,128)S(1)}, f32[1,128]{1,0:T(1,128)S(1)}, u32[]{:S(2)}, u32[]{:S(2)}) collective-permute-start(f32[1,128]{1,0:T(1,128)S(1)} %get-tuple-element.8.rest_0_), channel_id=1, source_target_pairs={{0,2},{1,3},{2,4},{3,5},{4,6},{5,7},{6,8},{7,9},{8,10},{9,11},{10,... | collective-permute-start | bytes 1544 | tf_op jit(solution)/shard_map/ppermute | solution.py:201
  55.7 1.7 %collective-permute-done.17.rest_3_ = f32[1,128]{1,0:T(1,128)S(1)} collective-permute-done((f32[1,128]{1,0:T(1,128)S(1)}, f32[1,128]{1,0:T(1,128)S(1)}, u32[]{:S(2)}, u32[]{:S(2)}) %collective-permute-start.17) | collective-permute-done | bytes 544 | tf_op jit(solution)/shard_map/ppermute | solution.py:201
  57.4 2.9 %collective-permute-done.16.rest_2_ = f32[1,128]{1,0:T(1,128)S(1)} collective-permute-done((f32[1,128]{1,0:T(1,128)S(1)}, f32[1,128]{1,0:T(1,128)S(1)}, u32[]{:S(2)}, u32[]{:S(2)}) %collective-permute-start.16) | collective-permute-done | bytes 544 | tf_op jit(solution)/shard_map/ppermute | solution.py:201
  60.3 1.0 %collective-permute-done.15.rest_1_ = f32[1,128]{1,0:T(1,128)S(1)} collective-permute-done((f32[1,128]{1,0:T(1,128)S(1)}, f32[1,128]{1,0:T(1,128)S(1)}, u32[]{:S(2)}, u32[]{:S(2)}) %collective-permute-start.15) | collective-permute-done | bytes 544 | tf_op jit(solution)/shard_map/ppermute | solution.py:201
  61.3 1.0 %update.1 = f32[256,512]{1,0:T(8,128)} custom-call(f32[256,512]{1,0:T(8,128)S(1)} %copy-done, f32[256,512]{1,0:T(8,128)S(1)} %get-tuple-element.7.grad_ref, f32[1,128]{1,0:T(1,128)S(1)} %get-tuple-element.8.rest_0_, f32[1,128]{1,0:T(1,128)S(1)} %collective-permute-done.15.rest_1_, f32[1,128]{1,0:T(1,128)S(1)} %collective-permute-done.16.rest_2_, ...), custom_call_target="tpu_custom_call" | custom-call | flops 262144 | bytes 1572864 | tf_op jit(solution)/shard_map/update/pallas_call | solution.py:207
  (22 shorter events, 0.1 us)
Async XLA Ops:
  0.0 29.2 %copy-start.3 = (s32[1,8]{1,0:T(1,128)S(1)}, s32[1,8]{1,0:T(1,128)}, u32[]{:S(2)}) copy-start(s32[1,8]{1,0:T(1,128)} %list_ref.1) | copy-start | bytes 100
  0.0 7.6 %collective-permute-start.3 = (bf16[128,512]{1,0:T(8,128)(2,1)}, bf16[128,512]{1,0:T(8,128)(2,1)S(1)}, u32[]{:S(2)}, u32[]{:S(2)}) collective-permute-start(bf16[128,512]{1,0:T(8,128)(2,1)} %rest_0_.1), channel_id=1, source_target_pairs={{0,2},{1,3},{2,0},{3,1},{4,6},{5,7},{6,4},{7,5},{8,10},{9,11},{10,... | collective-permute-start | bytes 393224 | tf_op jit(solution)/shard_map/ppermute | solution.py:32
  3.0 7.9 %collective-permute-start.2 = (bf16[128,512]{1,0:T(8,128)(2,1)}, bf16[128,512]{1,0:T(8,128)(2,1)S(1)}, u32[]{:S(2)}, u32[]{:S(2)}) collective-permute-start(bf16[128,512]{1,0:T(8,128)(2,1)} %rest_0_.1), channel_id=1, source_target_pairs={{0,12},{1,13},{2,14},{3,15},{4,0},{5,1},{6,2},{7,3},{8,4},{9,5},{1... | collective-permute-start | bytes 393224 | tf_op jit(solution)/shard_map/ppermute | solution.py:32
  6.6 11.0 %collective-permute-start.1 = (bf16[128,512]{1,0:T(8,128)(2,1)}, bf16[128,512]{1,0:T(8,128)(2,1)S(1)}, u32[]{:S(2)}, u32[]{:S(2)}) collective-permute-start(bf16[128,512]{1,0:T(8,128)(2,1)} %rest_0_.1), channel_id=1, source_target_pairs={{0,8},{1,9},{2,10},{3,11},{4,12},{5,13},{6,14},{7,15},{8,0},{9,1},... | collective-permute-start | bytes 393224 | tf_op jit(solution)/shard_map/ppermute | solution.py:32
  6.6 11.5 %collective-permute-start = (bf16[128,512]{1,0:T(8,128)(2,1)}, bf16[128,512]{1,0:T(8,128)(2,1)S(1)}, u32[]{:S(2)}, u32[]{:S(2)}) collective-permute-start(bf16[128,512]{1,0:T(8,128)(2,1)} %rest_0_.1), channel_id=1, source_target_pairs={{0,4},{1,5},{2,6},{3,7},{4,8},{5,9},{6,10},{7,11},{8,12},{9,13},{1... | collective-permute-start | bytes 393224 | tf_op jit(solution)/shard_map/ppermute | solution.py:32
  7.6 12.0 %collective-permute-start.7 = (bf16[128,512]{1,0:T(8,128)(2,1)}, bf16[128,512]{1,0:T(8,128)(2,1)S(1)}, u32[]{:S(2)}, u32[]{:S(2)}) collective-permute-start(bf16[128,512]{1,0:T(8,128)(2,1)} %rest_0_.1), channel_id=1, source_target_pairs={{0,1},{1,0},{2,3},{3,2},{4,5},{5,4},{6,7},{7,6},{8,9},{9,8},{10,11... | collective-permute-start | bytes 393224 | tf_op jit(solution)/shard_map/ppermute | solution.py:32
  7.6 12.5 %collective-permute-start.11 = (bf16[128,512]{1,0:T(8,128)(2,1)S(1)}, bf16[128,512]{1,0:T(8,128)(2,1)S(1)}, u32[]{:S(2)}, u32[]{:S(2)}) collective-permute-start(bf16[128,512]{1,0:T(8,128)(2,1)S(1)} %collective-permute-done.3.rest_4_), channel_id=1, source_target_pairs={{0,1},{1,0},{2,3},{3,2},{4,5},{5,4},{6,7},{7,6},{8,9},{9,8},{10,11... | collective-permute-start | bytes 393224 | tf_op jit(solution)/shard_map/ppermute | solution.py:32
  10.8 9.3 %collective-permute-start.10 = (bf16[128,512]{1,0:T(8,128)(2,1)S(1)}, bf16[128,512]{1,0:T(8,128)(2,1)S(1)}, u32[]{:S(2)}, u32[]{:S(2)}) collective-permute-start(bf16[128,512]{1,0:T(8,128)(2,1)S(1)} %collective-permute-done.2.rest_3_), channel_id=1, source_target_pairs={{0,1},{1,0},{2,3},{3,2},{4,5},{5,4},{6,7},{7,6},{8,9},{9,8},{10,11... | collective-permute-start | bytes 393224 | tf_op jit(solution)/shard_map/ppermute | solution.py:32
  17.6 6.4 %collective-permute-start.6 = (bf16[128,512]{1,0:T(8,128)(2,1)S(1)}, bf16[128,512]{1,0:T(8,128)(2,1)S(1)}, u32[]{:S(2)}, u32[]{:S(2)}) collective-permute-start(bf16[128,512]{1,0:T(8,128)(2,1)S(1)} %collective-permute-done.2.rest_3_), channel_id=1, source_target_pairs={{0,2},{1,3},{2,0},{3,1},{4,6},{5,7},{6,4},{7,5},{8,10},{9,11},{10,... | collective-permute-start | bytes 393224 | tf_op jit(solution)/shard_map/ppermute | solution.py:32
  18.1 8.3 %collective-permute-start.5 = (bf16[128,512]{1,0:T(8,128)(2,1)S(1)}, bf16[128,512]{1,0:T(8,128)(2,1)S(1)}, u32[]{:S(2)}, u32[]{:S(2)}) collective-permute-start(bf16[128,512]{1,0:T(8,128)(2,1)S(1)} %collective-permute-done.1.rest_2_), channel_id=1, source_target_pairs={{0,2},{1,3},{2,0},{3,1},{4,6},{5,7},{6,4},{7,5},{8,10},{9,11},{10,... | collective-permute-start | bytes 393224 | tf_op jit(solution)/shard_map/ppermute | solution.py:32
  19.6 8.2 %collective-permute-start.4 = (bf16[128,512]{1,0:T(8,128)(2,1)S(1)}, bf16[128,512]{1,0:T(8,128)(2,1)S(1)}, u32[]{:S(2)}, u32[]{:S(2)}) collective-permute-start(bf16[128,512]{1,0:T(8,128)(2,1)S(1)} %collective-permute-done.rest_1_), channel_id=1, source_target_pairs={{0,2},{1,3},{2,0},{3,1},{4,6},{5,7},{6,4},{7,5},{8,10},{9,11},{10,... | collective-permute-start | bytes 393224 | tf_op jit(solution)/shard_map/ppermute | solution.py:32
  20.1 8.4 %collective-permute-start.9 = (bf16[128,512]{1,0:T(8,128)(2,1)S(1)}, bf16[128,512]{1,0:T(8,128)(2,1)S(1)}, u32[]{:S(2)}, u32[]{:S(2)}) collective-permute-start(bf16[128,512]{1,0:T(8,128)(2,1)S(1)} %collective-permute-done.1.rest_2_), channel_id=1, source_target_pairs={{0,1},{1,0},{2,3},{3,2},{4,5},{5,4},{6,7},{7,6},{8,9},{9,8},{10,11... | collective-permute-start | bytes 393224 | tf_op jit(solution)/shard_map/ppermute | solution.py:32
  20.1 8.4 %collective-permute-start.8 = (bf16[128,512]{1,0:T(8,128)(2,1)S(1)}, bf16[128,512]{1,0:T(8,128)(2,1)S(1)}, u32[]{:S(2)}, u32[]{:S(2)}) collective-permute-start(bf16[128,512]{1,0:T(8,128)(2,1)S(1)} %collective-permute-done.rest_1_), channel_id=1, source_target_pairs={{0,1},{1,0},{2,3},{3,2},{4,5},{5,4},{6,7},{7,6},{8,9},{9,8},{10,11... | collective-permute-start | bytes 393224 | tf_op jit(solution)/shard_map/ppermute | solution.py:32
  24.0 4.5 %collective-permute-start.14 = (bf16[128,512]{1,0:T(8,128)(2,1)S(1)}, bf16[128,512]{1,0:T(8,128)(2,1)S(1)}, u32[]{:S(2)}, u32[]{:S(2)}) collective-permute-start(bf16[128,512]{1,0:T(8,128)(2,1)S(1)} %collective-permute-done.6.rest_7_), channel_id=1, source_target_pairs={{0,1},{1,0},{2,3},{3,2},{4,5},{5,4},{6,7},{7,6},{8,9},{9,8},{10,11... | collective-permute-start | bytes 393224 | tf_op jit(solution)/shard_map/ppermute | solution.py:32
  26.4 2.1 %collective-permute-start.13 = (bf16[128,512]{1,0:T(8,128)(2,1)S(1)}, bf16[128,512]{1,0:T(8,128)(2,1)S(1)}, u32[]{:S(2)}, u32[]{:S(2)}) collective-permute-start(bf16[128,512]{1,0:T(8,128)(2,1)S(1)} %collective-permute-done.5.rest_6_), channel_id=1, source_target_pairs={{0,1},{1,0},{2,3},{3,2},{4,5},{5,4},{6,7},{7,6},{8,9},{9,8},{10,11... | collective-permute-start | bytes 393224 | tf_op jit(solution)/shard_map/ppermute | solution.py:32
  27.8 1.3 %collective-permute-start.12 = (bf16[128,512]{1,0:T(8,128)(2,1)S(1)}, bf16[128,512]{1,0:T(8,128)(2,1)S(1)}, u32[]{:S(2)}, u32[]{:S(2)}) collective-permute-start(bf16[128,512]{1,0:T(8,128)(2,1)S(1)} %collective-permute-done.4.rest_5_), channel_id=1, source_target_pairs={{0,1},{1,0},{2,3},{3,2},{4,5},{5,4},{6,7},{7,6},{8,9},{9,8},{10,11... | collective-permute-start | bytes 393224 | tf_op jit(solution)/shard_map/ppermute | solution.py:32
  29.2 1.0 %copy-start = (f32[256,512]{1,0:T(8,128)S(1)}, f32[256,512]{1,0:T(8,128)}, u32[]{:S(2)}) copy-start(f32[256,512]{1,0:T(8,128)} %users_ref.3) | copy-start | bytes 1572868
  30.2 1.2 %copy-start.1 = (s32[256,1024]{1,0:T(8,128)S(1)}, s32[256,1024]{1,0:T(8,128)}, u32[]{:S(2)}) copy-start(s32[256,1024]{1,0:T(8,128)} %labels_ref.1) | copy-start | bytes 3145732
  31.5 0.9 %copy-start.2 = (bf16[128,512]{1,0:T(8,128)(2,1)S(1)}, bf16[128,512]{1,0:T(8,128)(2,1)}, u32[]{:S(2)}) copy-start(bf16[128,512]{1,0:T(8,128)(2,1)} %rest_0_.1) | copy-start | bytes 393220
  38.3 4.5 %collective-permute-start.29 = (f32[1,128]{1,0:T(1,128)S(1)}, f32[1,128]{1,0:T(1,128)S(1)}, u32[]{:S(2)}, u32[]{:S(2)}) collective-permute-start(f32[1,128]{1,0:T(1,128)S(1)} %get-tuple-element.8.rest_0_), channel_id=1, source_target_pairs={{0,15},{1,0},{2,1},{3,2},{4,3},{5,4},{6,5},{7,6},{8,7},{9,8},{10,9... | collective-permute-start | bytes 1544 | tf_op jit(solution)/shard_map/ppermute | solution.py:201
  38.4 5.9 %collective-permute-start.28 = (f32[1,128]{1,0:T(1,128)S(1)}, f32[1,128]{1,0:T(1,128)S(1)}, u32[]{:S(2)}, u32[]{:S(2)}) collective-permute-start(f32[1,128]{1,0:T(1,128)S(1)} %get-tuple-element.8.rest_0_), channel_id=1, source_target_pairs={{0,14},{1,15},{2,0},{3,1},{4,2},{5,3},{6,4},{7,5},{8,6},{9,7},{10,... | collective-permute-start | bytes 1544 | tf_op jit(solution)/shard_map/ppermute | solution.py:201
  38.9 5.3 %collective-permute-start.27 = (f32[1,128]{1,0:T(1,128)S(1)}, f32[1,128]{1,0:T(1,128)S(1)}, u32[]{:S(2)}, u32[]{:S(2)}) collective-permute-start(f32[1,128]{1,0:T(1,128)S(1)} %get-tuple-element.8.rest_0_), channel_id=1, source_target_pairs={{0,13},{1,14},{2,15},{3,0},{4,1},{5,2},{6,3},{7,4},{8,5},{9,6},{10... | collective-permute-start | bytes 1544 | tf_op jit(solution)/shard_map/ppermute | solution.py:201
  39.0 7.0 %collective-permute-start.26 = (f32[1,128]{1,0:T(1,128)S(1)}, f32[1,128]{1,0:T(1,128)S(1)}, u32[]{:S(2)}, u32[]{:S(2)}) collective-permute-start(f32[1,128]{1,0:T(1,128)S(1)} %get-tuple-element.8.rest_0_), channel_id=1, source_target_pairs={{0,12},{1,13},{2,14},{3,15},{4,0},{5,1},{6,2},{7,3},{8,4},{9,5},{1... | collective-permute-start | bytes 1544 | tf_op jit(solution)/shard_map/ppermute | solution.py:201
  40.1 7.7 %collective-permute-start.25 = (f32[1,128]{1,0:T(1,128)S(1)}, f32[1,128]{1,0:T(1,128)S(1)}, u32[]{:S(2)}, u32[]{:S(2)}) collective-permute-start(f32[1,128]{1,0:T(1,128)S(1)} %get-tuple-element.8.rest_0_), channel_id=1, source_target_pairs={{0,11},{1,12},{2,13},{3,14},{4,15},{5,0},{6,1},{7,2},{8,3},{9,4},{... | collective-permute-start | bytes 1544 | tf_op jit(solution)/shard_map/ppermute | solution.py:201
  42.8 6.5 %collective-permute-start.24 = (f32[1,128]{1,0:T(1,128)S(1)}, f32[1,128]{1,0:T(1,128)S(1)}, u32[]{:S(2)}, u32[]{:S(2)}) collective-permute-start(f32[1,128]{1,0:T(1,128)S(1)} %get-tuple-element.8.rest_0_), channel_id=1, source_target_pairs={{0,10},{1,11},{2,12},{3,13},{4,14},{5,15},{6,0},{7,1},{8,2},{9,3},... | collective-permute-start | bytes 1544 | tf_op jit(solution)/shard_map/ppermute | solution.py:201
  44.3 5.9 %collective-permute-start.23 = (f32[1,128]{1,0:T(1,128)S(1)}, f32[1,128]{1,0:T(1,128)S(1)}, u32[]{:S(2)}, u32[]{:S(2)}) collective-permute-start(f32[1,128]{1,0:T(1,128)S(1)} %get-tuple-element.8.rest_0_), channel_id=1, source_target_pairs={{0,9},{1,10},{2,11},{3,12},{4,13},{5,14},{6,15},{7,0},{8,1},{9,2},... | collective-permute-start | bytes 1544 | tf_op jit(solution)/shard_map/ppermute | solution.py:201
  44.3 7.7 %collective-permute-start.22 = (f32[1,128]{1,0:T(1,128)S(1)}, f32[1,128]{1,0:T(1,128)S(1)}, u32[]{:S(2)}, u32[]{:S(2)}) collective-permute-start(f32[1,128]{1,0:T(1,128)S(1)} %get-tuple-element.8.rest_0_), channel_id=1, source_target_pairs={{0,8},{1,9},{2,10},{3,11},{4,12},{5,13},{6,14},{7,15},{8,0},{9,1},... | collective-permute-start | bytes 1544 | tf_op jit(solution)/shard_map/ppermute | solution.py:201
  46.0 8.0 %collective-permute-start.21 = (f32[1,128]{1,0:T(1,128)S(1)}, f32[1,128]{1,0:T(1,128)S(1)}, u32[]{:S(2)}, u32[]{:S(2)}) collective-permute-start(f32[1,128]{1,0:T(1,128)S(1)} %get-tuple-element.8.rest_0_), channel_id=1, source_target_pairs={{0,7},{1,8},{2,9},{3,10},{4,11},{5,12},{6,13},{7,14},{8,15},{9,0},... | collective-permute-start | bytes 1544 | tf_op jit(solution)/shard_map/ppermute | solution.py:201
  47.8 7.9 %collective-permute-start.20 = (f32[1,128]{1,0:T(1,128)S(1)}, f32[1,128]{1,0:T(1,128)S(1)}, u32[]{:S(2)}, u32[]{:S(2)}) collective-permute-start(f32[1,128]{1,0:T(1,128)S(1)} %get-tuple-element.8.rest_0_), channel_id=1, source_target_pairs={{0,6},{1,7},{2,8},{3,9},{4,10},{5,11},{6,12},{7,13},{8,14},{9,15},... | collective-permute-start | bytes 1544 | tf_op jit(solution)/shard_map/ppermute | solution.py:201
  49.3 6.3 %collective-permute-start.19 = (f32[1,128]{1,0:T(1,128)S(1)}, f32[1,128]{1,0:T(1,128)S(1)}, u32[]{:S(2)}, u32[]{:S(2)}) collective-permute-start(f32[1,128]{1,0:T(1,128)S(1)} %get-tuple-element.8.rest_0_), channel_id=1, source_target_pairs={{0,5},{1,6},{2,7},{3,8},{4,9},{5,10},{6,11},{7,12},{8,13},{9,14},{... | collective-permute-start | bytes 1544 | tf_op jit(solution)/shard_map/ppermute | solution.py:201
  50.1 5.5 %collective-permute-start.18 = (f32[1,128]{1,0:T(1,128)S(1)}, f32[1,128]{1,0:T(1,128)S(1)}, u32[]{:S(2)}, u32[]{:S(2)}) collective-permute-start(f32[1,128]{1,0:T(1,128)S(1)} %get-tuple-element.8.rest_0_), channel_id=1, source_target_pairs={{0,4},{1,5},{2,6},{3,7},{4,8},{5,9},{6,10},{7,11},{8,12},{9,13},{1... | collective-permute-start | bytes 1544 | tf_op jit(solution)/shard_map/ppermute | solution.py:201
  51.9 5.4 %collective-permute-start.17 = (f32[1,128]{1,0:T(1,128)S(1)}, f32[1,128]{1,0:T(1,128)S(1)}, u32[]{:S(2)}, u32[]{:S(2)}) collective-permute-start(f32[1,128]{1,0:T(1,128)S(1)} %get-tuple-element.8.rest_0_), channel_id=1, source_target_pairs={{0,3},{1,4},{2,5},{3,6},{4,7},{5,8},{6,9},{7,10},{8,11},{9,12},{10... | collective-permute-start | bytes 1544 | tf_op jit(solution)/shard_map/ppermute | solution.py:201
  54.0 6.2 %collective-permute-start.16 = (f32[1,128]{1,0:T(1,128)S(1)}, f32[1,128]{1,0:T(1,128)S(1)}, u32[]{:S(2)}, u32[]{:S(2)}) collective-permute-start(f32[1,128]{1,0:T(1,128)S(1)} %get-tuple-element.8.rest_0_), channel_id=1, source_target_pairs={{0,2},{1,3},{2,4},{3,5},{4,6},{5,7},{6,8},{7,9},{8,10},{9,11},{10,... | collective-permute-start | bytes 1544 | tf_op jit(solution)/shard_map/ppermute | solution.py:201
  55.6 5.7 %collective-permute-start.15 = (f32[1,128]{1,0:T(1,128)S(1)}, f32[1,128]{1,0:T(1,128)S(1)}, u32[]{:S(2)}, u32[]{:S(2)}) collective-permute-start(f32[1,128]{1,0:T(1,128)S(1)} %get-tuple-element.8.rest_0_), channel_id=1, source_target_pairs={{0,1},{1,2},{2,3},{3,4},{4,5},{5,6},{6,7},{7,8},{8,9},{9,10},{10,1... | collective-permute-start | bytes 1544 | tf_op jit(solution)/shard_map/ppermute | solution.py:201

commit v2 on v1

--- a/solution.py
+++ b/solution.py
@@ -96,7 +96,8 @@
     def _():
         gradient = grad_ref[...]
         square = jnp.sum(gradient * gradient, axis=0, keepdims=True)
-        square_ref[...] = sum(square[:, at : at + 128] for at in range(0, width, 128))
+        square = sum(square[:, at : at + 128] for at in range(0, width, 128))
+        square_ref[...] = jnp.broadcast_to(square, square_ref.shape)
 
 
 def fetch_list(dims, shifts, list_ref, step, live, pieces, tiles, sems, wait):
@@ -138,11 +139,8 @@
                 copy.start()
 
 
-def update_kernel(entries, users_ref, grad_ref, *rest):
-    squares, out_ref = rest[:-1], rest[-1]
-    total = squares[0][...]
-    for square in squares[1:]:
-        total = total + square[...]
+def update_kernel(entries, users_ref, grad_ref, squares_ref, out_ref):
+    total = jnp.sum(squares_ref[...], axis=0, keepdims=True)
     total = jnp.sum(total, axis=1, keepdims=True)
     scale = 0.5 / jnp.sqrt(total / entries + 1e-06)
     out_ref[...] = users_ref[...] - scale * grad_ref[...]
@@ -168,7 +166,7 @@
         grid=(slots // CHUNK,),
         out_shape=[
             jax.ShapeDtypeStruct((rows, width), jnp.float32),
-            jax.ShapeDtypeStruct((1, 128), jnp.float32),
+            jax.ShapeDtypeStruct((loop_size, 128), jnp.float32),
         ],
         in_specs=[
             pl.BlockSpec(memory_space=pltpu.SMEM),
@@ -179,7 +177,7 @@
         + [pl.BlockSpec(memory_space=pl.ANY)] * len(pieces),
         out_specs=[
             pl.BlockSpec((rows, width), lambda step: (0, 0)),
-            pl.BlockSpec((1, 128), lambda step: (0, 0)),
+            pl.BlockSpec((loop_size, 128), lambda step: (0, 0)),
         ],
         scratch_shapes=[
             pltpu.VMEM((CHUNK * tile, width), jnp.bfloat16),
@@ -195,26 +193,19 @@
         name="gradient",
     )(tile_blocks, tile_count, users, labels, *pieces)
 
-    if direct:
-        squares = [piece for _, piece in [((0, 0, 0), square)]]
-        squares += [
-            lax.ppermute(square, "loop", [(at, (at + shift) % loop_size) for at in range(loop_size)])
-            for shift in range(1, loop_size)
-        ]
-    else:
-        squares = [lax.psum(square, "loop")]
+    squares = lax.all_to_all(square, "loop", 0, 0, tiled=True)
 
     return pl.pallas_call(
         functools.partial(update_kernel, rows * loop_size * width),
         out_shape=jax.ShapeDtypeStruct((rows, width), jnp.float32),
-        in_specs=[pl.BlockSpec(memory_space=pltpu.VMEM)] * (2 + len(squares)),
+        in_specs=[pl.BlockSpec(memory_space=pltpu.VMEM)] * 3,
         out_specs=pl.BlockSpec(memory_space=pltpu.VMEM),
         compiler_params=pltpu.CompilerParams(vmem_limit_bytes=16 * 1024 * 1024),
         cost_estimate=pl.CostEstimate(
             flops=2 * rows * width, bytes_accessed=12 * rows * width, transcendentals=0
         ),
         name="update",
-    )(users, gradient, *squares)
+    )(users, gradient, squares)
 
 
 def solution(mesh):

time: 62.6 us -> 47.5 us (0.76)
  starting transfers between devices: 28.4 us -> 11.1 us
  blocking collectives: 0 us -> 11.5 us
  waiting for transfers between devices: 23 us -> 17.3 us
  Pallas kernels: 6.93 us -> 3.17 us
    ppermute x15 -> x0, starting transfers between devices: 17.3 us -> none  [local(): lax.ppermute(square, 'loop', [(at, (at + shift) % loop_size) for at in ra...]
    all_to_all x0 -> x1, blocking collectives: none -> 11.5 us  [local(): squares = lax.all_to_all(square, 'loop', 0, 0, tiled=True)]
    ppermute x15 -> x0, waiting for transfers between devices: 5.67 us -> none  [local(): lax.ppermute(square, 'loop', [(at, (at + shift) % loop_size) for at in ra...]
    pallas_call x1, Pallas kernels: 5.94 us -> 2.19 us  [local(): pl.pallas_call(functools.partial(gradient_kernel, fetch, len(pieces)), gr...]
  transfers between devices with their start and end apart: 30 -> 15, of which waited for: 9 -> 6; matrix products, arithmetic and copies ran while one was open for 0% -> 0% of each run, Pallas kernels for 0% -> 0%
where the time goes in v2:
time: 47.5 us; the launch traced here: 47 us
  waiting for transfers between devices  17.3 us (36%)
  blocking collectives  11.5 us (24%)
  starting transfers between devices  11.1 us (23%)
  local copies, waits for them, and re-layouts  3.17 us (7%)
  Pallas kernels  3.17 us (7%)
  between operations  0.71 us (1%)
    ppermute x15, waiting for transfers between devices, shifted(): return lax.ppermute(array, 'loop', pairs)  17.3 us
    all_to_all x1, blocking collectives, local(): squares = lax.all_to_all(square, 'loop', 0, 0, tiled=True)  11.5 us
    ppermute x15, starting transfers between devices, shifted(): return lax.ppermute(array, 'loop', pairs)  11.1 us
    unnamed x8, local copies, waits for them, and re-layouts  3.17 us
    pallas_call x1, Pallas kernels, local(): pl.pallas_call(functools.partial(gradient_kernel, fetch, len(pieces)), gr...  2.19 us
    pallas_call x1, Pallas kernels, local(): pl.pallas_call(functools.partial(update_kernel, rows * loop_size * width)...  0.98 us
  transfers between devices with their start and end apart: 15, of which 6 were waited for; matrix products, arithmetic and copies ran while one was open for 0% of the time, Pallas kernels for 0%

profile of v2, /device:TPU:0, one launch (start us, length us, event | category | flops | bytes accessed | tf_op | source)
XLA Modules:
  0.0 47.0 jit_solution(1613734179268993259)
XLA Ops:
  0.0 0.0 copy-start.3
  0.0 3.0 %collective-permute-start.3 = (bf16[128,512]{1,0:T(8,128)(2,1)}, bf16[128,512]{1,0:T(8,128)(2,1)S(1)}, u32[]{:S(2)}, u32[]{:S(2)}) collective-permute-start(bf16[128,512]{1,0:T(8,128)(2,1)} %rest_0_.1), channel_id=1, source_target_pairs={{0,2},{1,3},{2,0},{3,1},{4,6},{5,7},{6,4},{7,5},{8,10},{9,11},{10,... | collective-permute-start | bytes 393224 | tf_op jit(solution)/shard_map/ppermute | solution.py:32
  3.0 3.6 %collective-permute-start.2 = (bf16[128,512]{1,0:T(8,128)(2,1)}, bf16[128,512]{1,0:T(8,128)(2,1)S(1)}, u32[]{:S(2)}, u32[]{:S(2)}) collective-permute-start(bf16[128,512]{1,0:T(8,128)(2,1)} %rest_0_.1), channel_id=1, source_target_pairs={{0,12},{1,13},{2,14},{3,15},{4,0},{5,1},{6,2},{7,3},{8,4},{9,5},{1... | collective-permute-start | bytes 393224 | tf_op jit(solution)/shard_map/ppermute | solution.py:32
  6.6 0.0 collective-permute-start.1
  6.6 1.0 %collective-permute-start = (bf16[128,512]{1,0:T(8,128)(2,1)}, bf16[128,512]{1,0:T(8,128)(2,1)S(1)}, u32[]{:S(2)}, u32[]{:S(2)}) collective-permute-start(bf16[128,512]{1,0:T(8,128)(2,1)} %rest_0_.1), channel_id=1, source_target_pairs={{0,4},{1,5},{2,6},{3,7},{4,8},{5,9},{6,10},{7,11},{8,12},{9,13},{1... | collective-permute-start | bytes 393224 | tf_op jit(solution)/shard_map/ppermute | solution.py:32
  7.6 0.0 collective-permute-start.7
  7.6 0.0 collective-permute-done.3.rest_4_
  7.6 0.5 %collective-permute-start.11 = (bf16[128,512]{1,0:T(8,128)(2,1)S(1)}, bf16[128,512]{1,0:T(8,128)(2,1)S(1)}, u32[]{:S(2)}, u32[]{:S(2)}) collective-permute-start(bf16[128,512]{1,0:T(8,128)(2,1)S(1)} %collective-permute-done.3.rest_4_), channel_id=1, source_target_pairs={{0,1},{1,0},{2,3},{3,2},{4,5},{5,4},{6,7},{7,6},{8,9},{9,8},{10,11... | collective-permute-start | bytes 393224 | tf_op jit(solution)/shard_map/ppermute | solution.py:32
  8.1 2.7 %collective-permute-done.2.rest_3_ = bf16[128,512]{1,0:T(8,128)(2,1)S(1)} collective-permute-done((bf16[128,512]{1,0:T(8,128)(2,1)}, bf16[128,512]{1,0:T(8,128)(2,1)S(1)}, u32[]{:S(2)}, u32[]{:S(2)}) %collective-permute-start.2) | collective-permute-done | bytes 131104 | tf_op jit(solution)/shard_map/ppermute | solution.py:32
  10.8 0.0 collective-permute-start.10
  10.8 6.8 %collective-permute-done.1.rest_2_ = bf16[128,512]{1,0:T(8,128)(2,1)S(1)} collective-permute-done((bf16[128,512]{1,0:T(8,128)(2,1)}, bf16[128,512]{1,0:T(8,128)(2,1)S(1)}, u32[]{:S(2)}, u32[]{:S(2)}) %collective-permute-start.1) | collective-permute-done | bytes 131104 | tf_op jit(solution)/shard_map/ppermute | solution.py:32
  17.6 0.5 %collective-permute-start.6 = (bf16[128,512]{1,0:T(8,128)(2,1)S(1)}, bf16[128,512]{1,0:T(8,128)(2,1)S(1)}, u32[]{:S(2)}, u32[]{:S(2)}) collective-permute-start(bf16[128,512]{1,0:T(8,128)(2,1)S(1)} %collective-permute-done.2.rest_3_), channel_id=1, source_target_pairs={{0,2},{1,3},{2,0},{3,1},{4,6},{5,7},{6,4},{7,5},{8,10},{9,11},{10,... | collective-permute-start | bytes 393224 | tf_op jit(solution)/shard_map/ppermute | solution.py:32
  18.1 0.0 collective-permute-done.rest_1_
  18.1 1.5 %collective-permute-start.5 = (bf16[128,512]{1,0:T(8,128)(2,1)S(1)}, bf16[128,512]{1,0:T(8,128)(2,1)S(1)}, u32[]{:S(2)}, u32[]{:S(2)}) collective-permute-start(bf16[128,512]{1,0:T(8,128)(2,1)S(1)} %collective-permute-done.1.rest_2_), channel_id=1, source_target_pairs={{0,2},{1,3},{2,0},{3,1},{4,6},{5,7},{6,4},{7,5},{8,10},{9,11},{10,... | collective-permute-start | bytes 393224 | tf_op jit(solution)/shard_map/ppermute | solution.py:32
  19.6 0.0 collective-permute-done.7.rest_8_
  19.6 0.5 %collective-permute-start.4 = (bf16[128,512]{1,0:T(8,128)(2,1)S(1)}, bf16[128,512]{1,0:T(8,128)(2,1)S(1)}, u32[]{:S(2)}, u32[]{:S(2)}) collective-permute-start(bf16[128,512]{1,0:T(8,128)(2,1)S(1)} %collective-permute-done.rest_1_), channel_id=1, source_target_pairs={{0,2},{1,3},{2,0},{3,1},{4,6},{5,7},{6,4},{7,5},{8,10},{9,11},{10,... | collective-permute-start | bytes 393224 | tf_op jit(solution)/shard_map/ppermute | solution.py:32
  20.1 0.0 collective-permute-done.11.rest_12_
  20.1 0.0 collective-permute-start.9
  20.1 0.0 collective-permute-done.10.rest_11_
  20.1 0.5 %collective-permute-start.8 = (bf16[128,512]{1,0:T(8,128)(2,1)S(1)}, bf16[128,512]{1,0:T(8,128)(2,1)S(1)}, u32[]{:S(2)}, u32[]{:S(2)}) collective-permute-start(bf16[128,512]{1,0:T(8,128)(2,1)S(1)} %collective-permute-done.rest_1_), channel_id=1, source_target_pairs={{0,1},{1,0},{2,3},{3,2},{4,5},{5,4},{6,7},{7,6},{8,9},{9,8},{10,11... | collective-permute-start | bytes 393224 | tf_op jit(solution)/shard_map/ppermute | solution.py:32
  20.6 3.4 %collective-permute-done.6.rest_7_ = bf16[128,512]{1,0:T(8,128)(2,1)S(1)} collective-permute-done((bf16[128,512]{1,0:T(8,128)(2,1)S(1)}, bf16[128,512]{1,0:T(8,128)(2,1)S(1)}, u32[]{:S(2)}, u32[]{:S(2)}) %collective-permute-start.6) | collective-permute-done | bytes 131104 | tf_op jit(solution)/shard_map/ppermute | solution.py:32
  24.0 0.0 collective-permute-start.14
  24.0 2.4 %collective-permute-done.5.rest_6_ = bf16[128,512]{1,0:T(8,128)(2,1)S(1)} collective-permute-done((bf16[128,512]{1,0:T(8,128)(2,1)S(1)}, bf16[128,512]{1,0:T(8,128)(2,1)S(1)}, u32[]{:S(2)}, u32[]{:S(2)}) %collective-permute-start.5) | collective-permute-done | bytes 131104 | tf_op jit(solution)/shard_map/ppermute | solution.py:32
  26.4 0.0 collective-permute-start.13
  26.4 1.4 %collective-permute-done.4.rest_5_ = bf16[128,512]{1,0:T(8,128)(2,1)S(1)} collective-permute-done((bf16[128,512]{1,0:T(8,128)(2,1)S(1)}, bf16[128,512]{1,0:T(8,128)(2,1)S(1)}, u32[]{:S(2)}, u32[]{:S(2)}) %collective-permute-start.4) | collective-permute-done | bytes 131104 | tf_op jit(solution)/shard_map/ppermute | solution.py:32
  27.8 0.0 collective-permute-start.12
  28.5 0.0 collective-permute-done.9.rest_10_
  28.5 0.0 collective-permute-done.8.rest_9_
  28.5 0.0 collective-permute-done.14.rest_15_
  28.5 0.0 collective-permute-done.13.rest_14_
  28.5 0.7 %collective-permute-done.12.rest_13_ = bf16[128,512]{1,0:T(8,128)(2,1)S(1)} collective-permute-done((bf16[128,512]{1,0:T(8,128)(2,1)S(1)}, bf16[128,512]{1,0:T(8,128)(2,1)S(1)}, u32[]{:S(2)}, u32[]{:S(2)}) %collective-permute-start.12) | collective-permute-done | bytes 131104 | tf_op jit(solution)/shard_map/ppermute | solution.py:32
  29.2 0.0 copy-done.3
  29.2 0.0 copy-start
  29.2 1.0 %copy-done = f32[256,512]{1,0:T(8,128)S(1)} copy-done((f32[256,512]{1,0:T(8,128)S(1)}, f32[256,512]{1,0:T(8,128)}, u32[]{:S(2)}) %copy-start) | copy-done | bytes 524312
  30.2 0.0 copy-start.1
  30.2 1.2 %copy-done.1 = s32[256,1024]{1,0:T(8,128)S(1)} copy-done((s32[256,1024]{1,0:T(8,128)S(1)}, s32[256,1024]{1,0:T(8,128)}, u32[]{:S(2)}) %copy-start.1) | copy-done | bytes 1048600
  31.5 0.0 copy-start.2
  31.5 0.9 %copy-done.2 = bf16[128,512]{1,0:T(8,128)(2,1)S(1)} copy-done((bf16[128,512]{1,0:T(8,128)(2,1)S(1)}, bf16[128,512]{1,0:T(8,128)(2,1)}, u32[]{:S(2)}) %copy-start.2) | copy-done | bytes 131096
  32.4 2.2 %gradient.1 = (f32[256,512]{1,0:T(8,128)S(1)}, f32[16,128]{1,0:T(8,128)S(1)}) custom-call(s32[1,8]{1,0:T(1,128)S(1)} %copy-done.3, s32[1]{0:T(128)S(6)} %copy.7.count_ref, f32[256,512]{1,0:T(8,128)S(1)} %copy-done, s32[256,1024]{1,0:T(8,128)S(1)} %copy-done.1, bf16[128,512]{1,0:T(8,128)(2,1)S(1)} %copy-done.2, ...), custom_call_target="tpu_custom_call" | custom-call | flops 1073741824 | bytes 3145728 | tf_op jit(solution)/shard_map/gradient/pallas_call | solution.py:164
  34.6 11.5 %all_to_all.11 = f32[16,1,128]{2,1,0:T(1,128)S(1)} all-to-all(f32[16,1,128]{2,1,0:T(1,128)S(1)} %bitcast.5), channel_id=1, replica_groups=mesh['group'=2,'loop'=16] {'loop'}, dimensions={0} | all-to-all | bytes 16384 | tf_op jit(solution)/shard_map/all_to_all | solution.py:196
  46.0 1.0 %update.1 = f32[256,512]{1,0:T(8,128)} custom-call(f32[256,512]{1,0:T(8,128)S(1)} %copy-done, f32[256,512]{1,0:T(8,128)S(1)} %get-tuple-element.7.grad_ref, f32[16,128]{1,0:T(8,128)S(1)} %bitcast.4), custom_call_target="tpu_custom_call" | custom-call | flops 262144 | bytes 1572864 | tf_op jit(solution)/shard_map/update/pallas_call | solution.py:198
Async XLA Ops:
  0.0 29.2 %copy-start.3 = (s32[1,8]{1,0:T(1,128)S(1)}, s32[1,8]{1,0:T(1,128)}, u32[]{:S(2)}) copy-start(s32[1,8]{1,0:T(1,128)} %list_ref.1) | copy-start | bytes 100
  0.0 7.6 %collective-permute-start.3 = (bf16[128,512]{1,0:T(8,128)(2,1)}, bf16[128,512]{1,0:T(8,128)(2,1)S(1)}, u32[]{:S(2)}, u32[]{:S(2)}) collective-permute-start(bf16[128,512]{1,0:T(8,128)(2,1)} %rest_0_.1), channel_id=1, source_target_pairs={{0,2},{1,3},{2,0},{3,1},{4,6},{5,7},{6,4},{7,5},{8,10},{9,11},{10,... | collective-permute-start | bytes 393224 | tf_op jit(solution)/shard_map/ppermute | solution.py:32
  3.0 7.9 %collective-permute-start.2 = (bf16[128,512]{1,0:T(8,128)(2,1)}, bf16[128,512]{1,0:T(8,128)(2,1)S(1)}, u32[]{:S(2)}, u32[]{:S(2)}) collective-permute-start(bf16[128,512]{1,0:T(8,128)(2,1)} %rest_0_.1), channel_id=1, source_target_pairs={{0,12},{1,13},{2,14},{3,15},{4,0},{5,1},{6,2},{7,3},{8,4},{9,5},{1... | collective-permute-start | bytes 393224 | tf_op jit(solution)/shard_map/ppermute | solution.py:32
  6.6 11.0 %collective-permute-start.1 = (bf16[128,512]{1,0:T(8,128)(2,1)}, bf16[128,512]{1,0:T(8,128)(2,1)S(1)}, u32[]{:S(2)}, u32[]{:S(2)}) collective-permute-start(bf16[128,512]{1,0:T(8,128)(2,1)} %rest_0_.1), channel_id=1, source_target_pairs={{0,8},{1,9},{2,10},{3,11},{4,12},{5,13},{6,14},{7,15},{8,0},{9,1},... | collective-permute-start | bytes 393224 | tf_op jit(solution)/shard_map/ppermute | solution.py:32
  6.6 11.5 %collective-permute-start = (bf16[128,512]{1,0:T(8,128)(2,1)}, bf16[128,512]{1,0:T(8,128)(2,1)S(1)}, u32[]{:S(2)}, u32[]{:S(2)}) collective-permute-start(bf16[128,512]{1,0:T(8,128)(2,1)} %rest_0_.1), channel_id=1, source_target_pairs={{0,4},{1,5},{2,6},{3,7},{4,8},{5,9},{6,10},{7,11},{8,12},{9,13},{1... | collective-permute-start | bytes 393224 | tf_op jit(solution)/shard_map/ppermute | solution.py:32
  7.6 12.0 %collective-permute-start.7 = (bf16[128,512]{1,0:T(8,128)(2,1)}, bf16[128,512]{1,0:T(8,128)(2,1)S(1)}, u32[]{:S(2)}, u32[]{:S(2)}) collective-permute-start(bf16[128,512]{1,0:T(8,128)(2,1)} %rest_0_.1), channel_id=1, source_target_pairs={{0,1},{1,0},{2,3},{3,2},{4,5},{5,4},{6,7},{7,6},{8,9},{9,8},{10,11... | collective-permute-start | bytes 393224 | tf_op jit(solution)/shard_map/ppermute | solution.py:32
  7.6 12.5 %collective-permute-start.11 = (bf16[128,512]{1,0:T(8,128)(2,1)S(1)}, bf16[128,512]{1,0:T(8,128)(2,1)S(1)}, u32[]{:S(2)}, u32[]{:S(2)}) collective-permute-start(bf16[128,512]{1,0:T(8,128)(2,1)S(1)} %collective-permute-done.3.rest_4_), channel_id=1, source_target_pairs={{0,1},{1,0},{2,3},{3,2},{4,5},{5,4},{6,7},{7,6},{8,9},{9,8},{10,11... | collective-permute-start | bytes 393224 | tf_op jit(solution)/shard_map/ppermute | solution.py:32
  10.8 9.3 %collective-permute-start.10 = (bf16[128,512]{1,0:T(8,128)(2,1)S(1)}, bf16[128,512]{1,0:T(8,128)(2,1)S(1)}, u32[]{:S(2)}, u32[]{:S(2)}) collective-permute-start(bf16[128,512]{1,0:T(8,128)(2,1)S(1)} %collective-permute-done.2.rest_3_), channel_id=1, source_target_pairs={{0,1},{1,0},{2,3},{3,2},{4,5},{5,4},{6,7},{7,6},{8,9},{9,8},{10,11... | collective-permute-start | bytes 393224 | tf_op jit(solution)/shard_map/ppermute | solution.py:32
  17.6 6.4 %collective-permute-start.6 = (bf16[128,512]{1,0:T(8,128)(2,1)S(1)}, bf16[128,512]{1,0:T(8,128)(2,1)S(1)}, u32[]{:S(2)}, u32[]{:S(2)}) collective-permute-start(bf16[128,512]{1,0:T(8,128)(2,1)S(1)} %collective-permute-done.2.rest_3_), channel_id=1, source_target_pairs={{0,2},{1,3},{2,0},{3,1},{4,6},{5,7},{6,4},{7,5},{8,10},{9,11},{10,... | collective-permute-start | bytes 393224 | tf_op jit(solution)/shard_map/ppermute | solution.py:32
  18.1 8.3 %collective-permute-start.5 = (bf16[128,512]{1,0:T(8,128)(2,1)S(1)}, bf16[128,512]{1,0:T(8,128)(2,1)S(1)}, u32[]{:S(2)}, u32[]{:S(2)}) collective-permute-start(bf16[128,512]{1,0:T(8,128)(2,1)S(1)} %collective-permute-done.1.rest_2_), channel_id=1, source_target_pairs={{0,2},{1,3},{2,0},{3,1},{4,6},{5,7},{6,4},{7,5},{8,10},{9,11},{10,... | collective-permute-start | bytes 393224 | tf_op jit(solution)/shard_map/ppermute | solution.py:32
  19.6 8.2 %collective-permute-start.4 = (bf16[128,512]{1,0:T(8,128)(2,1)S(1)}, bf16[128,512]{1,0:T(8,128)(2,1)S(1)}, u32[]{:S(2)}, u32[]{:S(2)}) collective-permute-start(bf16[128,512]{1,0:T(8,128)(2,1)S(1)} %collective-permute-done.rest_1_), channel_id=1, source_target_pairs={{0,2},{1,3},{2,0},{3,1},{4,6},{5,7},{6,4},{7,5},{8,10},{9,11},{10,... | collective-permute-start | bytes 393224 | tf_op jit(solution)/shard_map/ppermute | solution.py:32
  20.1 8.4 %collective-permute-start.9 = (bf16[128,512]{1,0:T(8,128)(2,1)S(1)}, bf16[128,512]{1,0:T(8,128)(2,1)S(1)}, u32[]{:S(2)}, u32[]{:S(2)}) collective-permute-start(bf16[128,512]{1,0:T(8,128)(2,1)S(1)} %collective-permute-done.1.rest_2_), channel_id=1, source_target_pairs={{0,1},{1,0},{2,3},{3,2},{4,5},{5,4},{6,7},{7,6},{8,9},{9,8},{10,11... | collective-permute-start | bytes 393224 | tf_op jit(solution)/shard_map/ppermute | solution.py:32
  20.1 8.4 %collective-permute-start.8 = (bf16[128,512]{1,0:T(8,128)(2,1)S(1)}, bf16[128,512]{1,0:T(8,128)(2,1)S(1)}, u32[]{:S(2)}, u32[]{:S(2)}) collective-permute-start(bf16[128,512]{1,0:T(8,128)(2,1)S(1)} %collective-permute-done.rest_1_), channel_id=1, source_target_pairs={{0,1},{1,0},{2,3},{3,2},{4,5},{5,4},{6,7},{7,6},{8,9},{9,8},{10,11... | collective-permute-start | bytes 393224 | tf_op jit(solution)/shard_map/ppermute | solution.py:32
  24.0 4.5 %collective-permute-start.14 = (bf16[128,512]{1,0:T(8,128)(2,1)S(1)}, bf16[128,512]{1,0:T(8,128)(2,1)S(1)}, u32[]{:S(2)}, u32[]{:S(2)}) collective-permute-start(bf16[128,512]{1,0:T(8,128)(2,1)S(1)} %collective-permute-done.6.rest_7_), channel_id=1, source_target_pairs={{0,1},{1,0},{2,3},{3,2},{4,5},{5,4},{6,7},{7,6},{8,9},{9,8},{10,11... | collective-permute-start | bytes 393224 | tf_op jit(solution)/shard_map/ppermute | solution.py:32
  26.4 2.1 %collective-permute-start.13 = (bf16[128,512]{1,0:T(8,128)(2,1)S(1)}, bf16[128,512]{1,0:T(8,128)(2,1)S(1)}, u32[]{:S(2)}, u32[]{:S(2)}) collective-permute-start(bf16[128,512]{1,0:T(8,128)(2,1)S(1)} %collective-permute-done.5.rest_6_), channel_id=1, source_target_pairs={{0,1},{1,0},{2,3},{3,2},{4,5},{5,4},{6,7},{7,6},{8,9},{9,8},{10,11... | collective-permute-start | bytes 393224 | tf_op jit(solution)/shard_map/ppermute | solution.py:32
  27.8 1.3 %collective-permute-start.12 = (bf16[128,512]{1,0:T(8,128)(2,1)S(1)}, bf16[128,512]{1,0:T(8,128)(2,1)S(1)}, u32[]{:S(2)}, u32[]{:S(2)}) collective-permute-start(bf16[128,512]{1,0:T(8,128)(2,1)S(1)} %collective-permute-done.4.rest_5_), channel_id=1, source_target_pairs={{0,1},{1,0},{2,3},{3,2},{4,5},{5,4},{6,7},{7,6},{8,9},{9,8},{10,11... | collective-permute-start | bytes 393224 | tf_op jit(solution)/shard_map/ppermute | solution.py:32
  29.2 1.0 %copy-start = (f32[256,512]{1,0:T(8,128)S(1)}, f32[256,512]{1,0:T(8,128)}, u32[]{:S(2)}) copy-start(f32[256,512]{1,0:T(8,128)} %users_ref.3) | copy-start | bytes 1572868
  30.2 1.2 %copy-start.1 = (s32[256,1024]{1,0:T(8,128)S(1)}, s32[256,1024]{1,0:T(8,128)}, u32[]{:S(2)}) copy-start(s32[256,1024]{1,0:T(8,128)} %labels_ref.1) | copy-start | bytes 3145732
  31.5 0.9 %copy-start.2 = (bf16[128,512]{1,0:T(8,128)(2,1)S(1)}, bf16[128,512]{1,0:T(8,128)(2,1)}, u32[]{:S(2)}) copy-start(bf16[128,512]{1,0:T(8,128)(2,1)} %rest_0_.1) | copy-start | bytes 393220

commit v3 on v0

v3 whole, which is shorter than its diff:
```python
import functools

import jax
import jax.numpy as jnp
from jax import lax
from jax.experimental import pallas as pl
from jax.experimental.pallas import tpu as pltpu
from jax.sharding import PartitionSpec as P

CHUNK = 8
RING_LIMIT = 16


def ring_place(loop_size):
    outer = loop_size // 4

    def device(position, core):
        position = position % (2 * outer)
        chip = 2 * position if position < outer else 2 * (2 * outer - 1 - position) + 1
        return 2 * chip + core

    return 2 * outer, device


def to_next(array, loop_size):
    chips, device = ring_place(loop_size)
    pairs = [(device(at, 0), device(at + 1, 0)) for at in range(chips)]
    pairs += [(device(at, 1), device(at - 1, 1)) for at in range(chips)]
    return lax.ppermute(array, "loop", pairs)


def to_other_core(array, loop_size):
    return lax.ppermute(array, "loop", [(at, at ^ 1) for at in range(loop_size)])


def join_kernel(own_ref, other_ref, both_ref):
    tile = own_ref.shape[0]
    core = lax.axis_index("loop") % 2
    both_ref[pl.ds(pl.multiple_of(core * tile, tile), tile), :] = own_ref[...]
    both_ref[pl.ds(pl.multiple_of((1 - core) * tile, tile), tile), :] = other_ref[...]


def join(own, other):
    tile, width = own.shape
    return pl.pallas_call(
        join_kernel,
        out_shape=jax.ShapeDtypeStruct((2 * tile, width), own.dtype),
        in_specs=[pl.BlockSpec(memory_space=pltpu.VMEM)] * 2,
        out_specs=pl.BlockSpec(memory_space=pltpu.VMEM),
        cost_estimate=pl.CostEstimate(
            flops=0, bytes_accessed=8 * tile * width, transcendentals=0
        ),
        name="join",
    )(own, other)


def halves(values):
    upper = values.astype(jnp.bfloat16)
    return jnp.concatenate([upper, (values - upper.astype(jnp.float32)).astype(jnp.bfloat16)], 0)


def add_tiles(grad_ref, parts_ref, tiles, live, labels_at):
    rows = grad_ref.shape[0]
    tile = tiles.shape[0] // CHUNK

    @pl.when(live % 2 == 1)
    def _():
        blank = pl.multiple_of(live * tile, tile)
        tiles[pl.ds(blank, tile), :] = jnp.zeros((tile, tiles.shape[1]), tiles.dtype)

    def pair(index, carry):
        block = tiles[pl.ds(pl.multiple_of(index * 2 * tile, 2 * tile), 2 * tile), :]
        both = lax.dot_general(
            parts_ref[...], block, (((1,), (1,)), ((), ())), preferred_element_type=jnp.float32
        )
        chance = 0.5 * jnp.tanh(0.5 * (both[:rows] + both[rows:])) + 0.5
        labels = jnp.concatenate([labels_at(2 * index), labels_at(2 * index + 1)], 1)
        position = 2 * index + lax.broadcasted_iota(jnp.int32, chance.shape, 1) // tile
        residual = jnp.where(position < live, chance - labels.astype(jnp.float32), 0.0)
        both = jnp.dot(halves(residual), block, preferred_element_type=jnp.float32)
        grad_ref[...] += both[:rows] + both[rows:]
        return carry

    lax.fori_loop(0, (live + 1) // 2, pair, 0)


def store_square(grad_ref, square_ref):
    gradient = grad_ref[...]
    square = jnp.sum(gradient * gradient, axis=0, keepdims=True)
    square = sum(square[:, at : at + 128] for at in range(0, square.shape[1], 128))
    square_ref[...] = jnp.broadcast_to(square, square_ref.shape)


def chip_behind(hops, loop_size):
    chips = loop_size // 2
    me = lax.axis_index("loop")
    core, row, outer = me % 2, me // 2 % 2, me // 4
    position = jnp.where(row == 0, outer, chips - 1 - outer)
    at = lax.rem(position + chips + jnp.where(core == 0, -hops, hops), chips)
    return jnp.where(at < chips // 2, 2 * at, 2 * (chips - 1 - at) + 1)


def pieces_kernel(loop_size, hops, first, last, list_ref, count_ref, *rest):
    rest = list(rest)
    given_ref, labels_ref = rest.pop(0), rest.pop(0)
    pieces = [rest.pop(0) for _ in hops]
    before_ref = None if first else rest.pop(0)
    grad_ref = rest.pop(0)
    parts_ref = rest.pop(0) if first else given_ref
    square_ref = rest.pop(0) if last else None
    tiles, slots = rest
    tile = tiles.shape[0] // CHUNK
    if first:
        parts_ref[...] = halves(given_ref[...])
        grad_ref[...] = jnp.zeros_like(grad_ref)
    else:
        grad_ref[...] = before_ref[...]
    wanted = [
        jnp.where(slot < count_ref[0], list_ref[0, slot], -1) for slot in range(list_ref.shape[1])
    ]
    live = jnp.int32(0)
    for piece, hop in zip(pieces, hops):
        chip = chip_behind(hop, loop_size)
        for core in range(2):
            found = jnp.int32(-1)
            for slot, name in enumerate(wanted):
                found = jnp.where(name == 2 * chip + core, slot, found)

            @pl.when(found >= 0)
            def _():
                into = pl.ds(pl.multiple_of(live * tile, tile), tile)
                tiles[into, :] = piece[core * tile : (core + 1) * tile, :]
                slots[live] = found

            live = live + (found >= 0).astype(jnp.int32)
    slots[live] = 0

    def labels_at(position):
        return labels_ref[:, pl.ds(pl.multiple_of(slots[position] * tile, tile), tile)]

    add_tiles(grad_ref, parts_ref, tiles, live, labels_at)
    if last:
        store_square(grad_ref, square_ref)


def add_pieces(loop_size, held, lists, given, labels, before, last):
    first = before is None
    width = given.shape[1]
    rows = given.shape[0] // (1 if first else 2)
    pieces = [piece for _, piece in held]
    tile = pieces[0].shape[0] // 2
    most = min(2 * len(pieces), CHUNK)
    out_shape = [jax.ShapeDtypeStruct((rows, width), jnp.float32)]
    if first:
        out_shape.append(jax.ShapeDtypeStruct((2 * rows, width), jnp.bfloat16))
    if last:
        out_shape.append(jax.ShapeDtypeStruct((loop_size, 128), jnp.float32))
    extra = [] if first else [before]
    return pl.pallas_call(
        functools.partial(pieces_kernel, loop_size, [hops for hops, _ in held], first, last),
        out_shape=out_shape,
        in_specs=[pl.BlockSpec(memory_space=pltpu.SMEM)] * 2
        + [pl.BlockSpec(memory_space=pltpu.VMEM)] * (2 + len(pieces) + len(extra)),
        out_specs=[pl.BlockSpec(memory_space=pltpu.VMEM)] * len(out_shape),
        scratch_shapes=[
            pltpu.VMEM((CHUNK * tile, width), jnp.bfloat16),
            pltpu.SMEM((CHUNK + 1,), jnp.int32),
        ],
        compiler_params=pltpu.CompilerParams(vmem_limit_bytes=24 * 1024 * 1024),
        cost_estimate=pl.CostEstimate(
            flops=8 * rows * width * most * tile,
            bytes_accessed=8 * rows * width,
            transcendentals=rows * most * tile,
        ),
        name="add_pieces",
    )(*lists, given, labels, *pieces, *extra)


def ring_gradient(users, items, lists, labels):
    loop_size = lax.axis_size("loop")
    far = loop_size // 4
    near = join(items, to_other_core(items, loop_size))
    ready, gradient, parts = [(0, near)], None, None
    for hop in range(1, far + 1):
        near = to_next(near, loop_size)
        if hop < 2:
            late = []
        elif gradient is None:
            gradient, parts = add_pieces(loop_size, ready, lists, users, labels, None, False)
            ready = []
        else:
            (gradient,) = add_pieces(loop_size, ready, lists, parts, labels, gradient, False)
            ready = []
        if gradient is not None:
            near, gradient = lax.optimization_barrier((near, gradient))
        ready = ready + late + [(hop, near)]
        late = []
        if hop < far:
            late = [(-hop, to_other_core(near, loop_size))]
            if hop == far - 1:
                ready, late = ready + late, []
    return add_pieces(loop_size, ready, lists, parts, labels, gradient, True)


def chunks_kernel(
    list_ref, count_ref, users_ref, labels_ref, items_ref, grad_ref, square_ref, tiles, parts_ref, sems
):
    tile = tiles.shape[0] // CHUNK
    step = pl.program_id(0)
    live = jnp.clip(count_ref[0] - step * CHUNK, 0, CHUNK)

    @pl.when(step == 0)
    def _():
        parts_ref[...] = halves(users_ref[...])
        grad_ref[...] = jnp.zeros_like(grad_ref)

    def move(slot):
        start = pl.multiple_of(list_ref[0, step * CHUNK + slot] * tile, tile)
        return pltpu.make_async_copy(
            items_ref.at[pl.ds(start, tile), :], tiles.at[pl.ds(slot * tile, tile), :], sems.at[slot]
        )

    for slot in range(CHUNK):
        pl.when(slot < live)(lambda slot=slot: move(slot).start())
    for slot in range(CHUNK):
        pl.when(slot < live)(lambda slot=slot: move(slot).wait())

    def labels_at(position):
        return labels_ref[:, pl.ds(pl.multiple_of(position * tile, tile), tile)]

    add_tiles(grad_ref, parts_ref, tiles, live, labels_at)

    @pl.when(step == pl.num_programs(0) - 1)
    def _():
        store_square(grad_ref, square_ref)


def add_chunks(loop_size, items, lists, users, labels):
    rows, width = users.shape
    slots = lists[0].shape[1]
    tile = labels.shape[1] // slots
    return pl.pallas_call(
        chunks_kernel,
        grid=(slots // CHUNK,),
        out_shape=[
            jax.ShapeDtypeStruct((rows, width), jnp.float32),
            jax.ShapeDtypeStruct((loop_size, 128), jnp.float32),
        ],
        in_specs=[
            pl.BlockSpec(memory_space=pltpu.SMEM),
            pl.BlockSpec(memory_space=pltpu.SMEM),
            pl.BlockSpec((rows, width), lambda step: (0, 0)),
            pl.BlockSpec((rows, CHUNK * tile), lambda step: (0, step)),
            pl.BlockSpec(memory_space=pl.ANY),
        ],
        out_specs=[
            pl.BlockSpec((rows, width), lambda step: (0, 0)),
            pl.BlockSpec((loop_size, 128), lambda step: (0, 0)),
        ],
        scratch_shapes=[
            pltpu.VMEM((CHUNK * tile, width), jnp.bfloat16),
            pltpu.VMEM((2 * rows, width), jnp.bfloat16),
            pltpu.SemaphoreType.DMA((CHUNK,)),
        ],
        compiler_params=pltpu.CompilerParams(vmem_limit_bytes=32 * 1024 * 1024),
        cost_estimate=pl.CostEstimate(
            flops=8 * rows * width * slots * tile,
            bytes_accessed=4 * rows * (slots * tile + 2 * width) + 2 * slots * tile * width,
            transcendentals=rows * slots * tile,
        ),
        name="add_chunks",
    )(*lists, users, labels, items)


def update_kernel(entries, users_ref, grad_ref, squares_ref, out_ref):
    total = jnp.sum(squares_ref[...], axis=0, keepdims=True)
    total = jnp.sum(total, axis=1, keepdims=True)
    scale = 0.5 / jnp.sqrt(total / entries + 1e-06)
    out_ref[...] = users_ref[...] - scale * grad_ref[...]


def local(users, items, tile_blocks, tile_count, labels):
    loop_size = lax.axis_size("loop")
    rows, width = users.shape
    slots = tile_blocks.shape[1]
    lists = (tile_blocks, tile_count)
    if loop_size <= RING_LIMIT and loop_size % 8 == 0 and slots <= CHUNK:
        gradient, square = ring_gradient(users, items, lists, labels)
    else:
        whole = lax.all_gather(items, "loop", axis=0, tiled=True)
        gradient, square = add_chunks(loop_size, whole, lists, users, labels)

    squares = lax.all_to_all(square, "loop", 0, 0, tiled=True)
    return pl.pallas_call(
        functools.partial(update_kernel, rows * loop_size * width),
        out_shape=jax.ShapeDtypeStruct((rows, width), jnp.float32),
        in_specs=[pl.BlockSpec(memory_space=pltpu.VMEM)] * 3,
        out_specs=pl.BlockSpec(memory_space=pltpu.VMEM),
        compiler_params=pltpu.CompilerParams(vmem_limit_bytes=16 * 1024 * 1024),
        cost_estimate=pl.CostEstimate(
            flops=2 * rows * width, bytes_accessed=12 * rows * width, transcendentals=0
        ),
        name="update",
    )(users, gradient, squares)


def solution(mesh):
    in_specs = (
        P(("group", "loop"), None),
        P(("group", "loop"), None),
        P(("group", "loop"), None),
        P(("group", "loop")),
        P(("group", "loop"), None),
    )
    out_specs = P(("group", "loop"), None)
    return jax.shard_map(local, mesh=mesh, in_specs=in_specs, out_specs=out_specs, check_vma=False)
```

time: 153 us -> 45.1 us (0.29); the launches traced: 151 us -> 44.9 us
  blocking collectives: 46.2 us -> 12.4 us
  waiting for transfers between devices: 45.7 us -> 12.6 us
  other arithmetic: 18.3 us -> 0 us
  between operations: 14.8 us -> 0.74 us
  loops' own time: 12.1 us -> 0 us
  starting transfers between devices: 0.01 us -> 9.29 us
  Pallas kernels: 0 us -> 7.03 us
  local copies, waits for them, and re-layouts: 9.56 us -> 2.84 us
  matrix products: 4.6 us -> 0 us
    psum x1 -> x0, blocking collectives: 46.2 us -> none  [local(): squares = lax.psum(jnp.sum(gradient * gradient), 'loop')]
    all_gather x1 -> x0, waiting for transfers between devices: 45 us -> none  [local(): piece = lax.all_gather(items, 'loop', axis=0, tiled=True)]
    convert_element_type x16 -> x0, other arithmetic: 14.9 us -> none  [take_block(): lax.dynamic_slice_in_dim(piece, index * tile_width, tile_width, 0)]
    ppermute x0 -> x8, waiting for transfers between devices: none -> 12.6 us  [the longest x4 11.4 us: to_next(): return lax.ppermute(array, 'loop', pairs)]
    all_to_all x0 -> x1, blocking collectives: none -> 12.4 us  [local(): squares = lax.all_to_all(square, 'loop', 0, 0, tiled=True)]
    another operation x17 -> x0, loops' own time: 12.1 us -> none  [the longest x1 10.5 us: local(): lax.fori_loop(0, piece.shape[0] // tile_width, sweep_blocks, zero_grad)]
    dynamic_slice x16 -> x0, local copies, waits for them, and re-layouts: 9.51 us -> none  [sweep_blocks(): own_index = own_slots[index]]
    ppermute x0 -> x8, starting transfers between devices: none -> 9.29 us  [the longest x4 8.76 us: to_next(): return lax.ppermute(array, 'loop', pairs)]
  transfers between devices with their start and end apart: 1 -> 8, of which waited for: 1 -> 4; matrix products, arithmetic and copies ran while one was open for 1% -> 0% of each run, Pallas kernels for 0% -> 8%
where the time goes in v3:
time: 45.1 us; the launch traced here: 44.9 us
  waiting for transfers between devices  12.6 us (28%)
  blocking collectives  12.4 us (27%)
  starting transfers between devices  9.29 us (21%)
  Pallas kernels  7.03 us (16%)
  local copies, waits for them, and re-layouts  2.84 us (6%)
  between operations  0.74 us (2%)
    all_to_all x1, blocking collectives, local(): squares = lax.all_to_all(square, 'loop', 0, 0, tiled=True)  12.4 us
    ppermute x4, waiting for transfers between devices, to_next(): return lax.ppermute(array, 'loop', pairs)  11.4 us
    ppermute x4, starting transfers between devices, to_next(): return lax.ppermute(array, 'loop', pairs)  8.76 us
    pallas_call x4, Pallas kernels, add_pieces(): pl.pallas_call(functools.partial(pieces_kernel, loop_size, [hops for hops...  4.36 us
    unnamed x12, local copies, waits for them, and re-layouts  2.84 us
    pallas_call x1, Pallas kernels, join(): pl.pallas_call(join_kernel, out_shape=jax.ShapeDtypeStruct((2 * tile, wid...  1.7 us
    ppermute x4, waiting for transfers between devices, to_other_core(): lax.ppermute(array, 'loop', [(at, at ^ 1) for at in range(loop_size)])  1.2 us
    pallas_call x1, Pallas kernels, local(): pl.pallas_call(functools.partial(update_kernel, rows * loop_size * width)...  0.97 us
  transfers between devices with their start and end apart: 8, of which 4 were waited for; matrix products, arithmetic and copies ran while one was open for 0% of the time, Pallas kernels for 8%

profile of v3, /device:TPU:0, one launch (start us, length us, event | category | flops | bytes accessed | tf_op | source)
XLA Modules:
  0.0 44.9 jit_solution(10784185421992752967)
XLA Ops:
  0.0 0.0 copy-start.2
  0.0 0.5 %collective-permute-start = (bf16[128,512]{1,0:T(8,128)(2,1)}, bf16[128,512]{1,0:T(8,128)(2,1)S(1)}, u32[]{:S(2)}, u32[]{:S(2)}) collective-permute-start(bf16[128,512]{1,0:T(8,128)(2,1)} %own_ref.1), channel_id=1, source_target_pairs={{0,1},{1,0},{2,3},{3,2},{4,5},{5,4},{6,7},{7,6},{8,9},{9,8},{10,11... | collective-permute-start | bytes 393224 | tf_op jit(solution)/shard_map/ppermute | solution.py:33
  0.5 1.2 %collective-permute-done.other_ref = bf16[128,512]{1,0:T(8,128)(2,1)S(1)} collective-permute-done((bf16[128,512]{1,0:T(8,128)(2,1)}, bf16[128,512]{1,0:T(8,128)(2,1)S(1)}, u32[]{:S(2)}, u32[]{:S(2)}) %collective-permute-start) | collective-permute-done | bytes 131104 | tf_op jit(solution)/shard_map/ppermute | solution.py:33
  1.7 0.0 copy-start.5
  1.7 0.7 %copy-done.5 = bf16[128,512]{1,0:T(8,128)(2,1)} copy-done((bf16[128,512]{1,0:T(8,128)(2,1)}, bf16[128,512]{1,0:T(8,128)(2,1)S(1)}, u32[]{:S(2)}) %copy-start.5) | copy-done | bytes 131096
  2.3 1.7 %join.1.rest_2_ = bf16[256,512]{1,0:T(8,128)(2,1)} custom-call(bf16[128,512]{1,0:T(8,128)(2,1)} %own_ref.1, bf16[128,512]{1,0:T(8,128)(2,1)} %copy-done.5), custom_call_target="tpu_custom_call" | custom-call | bytes 524288 | tf_op jit(solution)/shard_map/join/pallas_call | solution.py:45
  4.0 0.0 copy-start.4
  4.0 2.9 %collective-permute-start.1 = (bf16[256,512]{1,0:T(8,128)(2,1)}, bf16[256,512]{1,0:T(8,128)(2,1)S(1)}, u32[]{:S(2)}, u32[]{:S(2)}) collective-permute-start(bf16[256,512]{1,0:T(8,128)(2,1)} %join.1.rest_2_), channel_id=1, source_target_pairs={{0,4},{4,8},{8,12},{12,14},{14,10},{10,6},{6,2},{2,0},{1,3},{5,1},... | collective-permute-start | bytes 786440 | tf_op jit(solution)/shard_map/ppermute | solution.py:29
  6.9 4.5 %collective-permute-done.1.rest_3_ = bf16[256,512]{1,0:T(8,128)(2,1)S(1)} collective-permute-done((bf16[256,512]{1,0:T(8,128)(2,1)}, bf16[256,512]{1,0:T(8,128)(2,1)S(1)}, u32[]{:S(2)}, u32[]{:S(2)}) %collective-permute-start.1) | collective-permute-done | bytes 262176 | tf_op jit(solution)/shard_map/ppermute | solution.py:29
  11.4 2.1 %collective-permute-start.2 = (bf16[256,512]{1,0:T(8,128)(2,1)S(1)}, bf16[256,512]{1,0:T(8,128)(2,1)S(1)}, u32[]{:S(2)}, u32[]{:S(2)}) collective-permute-start(bf16[256,512]{1,0:T(8,128)(2,1)S(1)} %collective-permute-done.1.rest_3_), channel_id=1, source_target_pairs={{0,4},{4,8},{8,12},{12,14},{14,10},{10,6},{6,2},{2,0},{1,3},{5,1},... | collective-permute-start | bytes 786440 | tf_op jit(solution)/shard_map/ppermute | solution.py:29
  14.2 0.1 collective-permute-start.4
  14.3 0.0 copy-done.2
  14.3 0.0 copy-done.4
  14.3 0.0 copy-start
  14.3 1.2 %copy-done = s32[256,1024]{1,0:T(8,128)S(1)} copy-done((s32[256,1024]{1,0:T(8,128)S(1)}, s32[256,1024]{1,0:T(8,128)}, u32[]{:S(2)}) %copy-start) | copy-done | bytes 1048600
  15.5 0.0 copy-start.3
  15.5 0.9 %copy-done.3 = bf16[256,512]{1,0:T(8,128)(2,1)S(1)} copy-done((bf16[256,512]{1,0:T(8,128)(2,1)S(1)}, bf16[256,512]{1,0:T(8,128)(2,1)}, u32[]{:S(2)}) %copy-start.3) | copy-done | bytes 262168
  16.5 0.0 copy-start.1
  16.5 1.5 %add_pieces.4 = (f32[256,512]{1,0:T(8,128)S(1)}, bf16[512,512]{1,0:T(8,128)(2,1)S(1)}) custom-call(s32[1,8]{1,0:T(1,128)S(1)} %copy-done.4, s32[1]{0:T(128)S(6)} %copy.7.count_ref, f32[256,512]{1,0:T(8,128)S(1)} %copy-done.2, s32[256,1024]{1,0:T(8,128)S(1)} %copy-done, bf16[256,512]{1,0:T(8,128)(2,1)S(1)} %copy-done.3, ...), custom_call_target="tpu_custom_call" | custom-call | flops 536870912 | bytes 1048576 | tf_op jit(solution)/shard_map/add_pieces/pallas_call | solution.py:159
  18.0 0.0 collective-permute-done.2.rest_3_
  18.0 1.9 %collective-permute-start.3 = (bf16[256,512]{1,0:T(8,128)(2,1)S(1)}, bf16[256,512]{1,0:T(8,128)(2,1)S(1)}, u32[]{:S(2)}, u32[]{:S(2)}) collective-permute-start(bf16[256,512]{1,0:T(8,128)(2,1)S(1)} %collective-permute-done.2.rest_3_), channel_id=1, source_target_pairs={{0,4},{4,8},{8,12},{12,14},{14,10},{10,6},{6,2},{2,0},{1,3},{5,1},... | collective-permute-start | bytes 786440 | tf_op jit(solution)/shard_map/ppermute | solution.py:29
  19.9 0.0 collective-permute-start.6
  19.9 0.0 collective-permute-done.4.rest_2_
  19.9 0.0 copy-done.1
  19.9 1.5 %add_pieces.5.rest_5_ = f32[256,512]{1,0:T(8,128)S(1)} custom-call(s32[1,8]{1,0:T(1,128)S(1)} %copy-done.4, s32[1]{0:T(128)S(6)} %copy.7.count_ref, bf16[512,512]{1,0:T(8,128)(2,1)S(1)} %get-tuple-element.15.rest_0_, s32[256,1024]{1,0:T(8,128)S(1)} %copy-done.1, bf16[256,512]{1,0:T(8,128)(2,1)S(1)} %collective-permute-done.4.rest_2_, ...), custom_call_target="tpu_custom_call" | custom-call | flops 536870912 | bytes 1048576 | tf_op jit(solution)/shard_map/add_pieces/pallas_call | solution.py:159
  21.4 3.0 %collective-permute-done.3.rest_3_ = bf16[256,512]{1,0:T(8,128)(2,1)S(1)} collective-permute-done((bf16[256,512]{1,0:T(8,128)(2,1)S(1)}, bf16[256,512]{1,0:T(8,128)(2,1)S(1)}, u32[]{:S(2)}, u32[]{:S(2)}) %collective-permute-start.3) | collective-permute-done | bytes 262176 | tf_op jit(solution)/shard_map/ppermute | solution.py:29
  24.4 0.0 collective-permute-start.7
  24.4 1.8 %collective-permute-start.5 = (bf16[256,512]{1,0:T(8,128)(2,1)S(1)}, bf16[256,512]{1,0:T(8,128)(2,1)S(1)}, u32[]{:S(2)}, u32[]{:S(2)}) collective-permute-start(bf16[256,512]{1,0:T(8,128)(2,1)S(1)} %collective-permute-done.3.rest_3_), channel_id=1, source_target_pairs={{0,4},{4,8},{8,12},{12,14},{14,10},{10,6},{6,2},{2,0},{1,3},{5,1},... | collective-permute-start | bytes 786440 | tf_op jit(solution)/shard_map/ppermute | solution.py:29
  26.3 0.0 collective-permute-done.6.rest_2_
  26.3 0.0 collective-permute-done.7.rest_4_
  26.3 0.7 %add_pieces.6.rest_3_ = f32[256,512]{1,0:T(8,128)S(1)} custom-call(s32[1,8]{1,0:T(1,128)S(1)} %copy-done.4, s32[1]{0:T(128)S(6)} %copy.7.count_ref, bf16[512,512]{1,0:T(8,128)(2,1)S(1)} %get-tuple-element.15.rest_0_, s32[256,1024]{1,0:T(8,128)S(1)} %copy-done.1, bf16[256,512]{1,0:T(8,128)(2,1)S(1)} %collective-permute-done.6.rest_2_, ...), custom_call_target="tpu_custom_call" | custom-call | flops 805306368 | bytes 1048576 | tf_op jit(solution)/shard_map/add_pieces/pallas_call | solution.py:159
  27.0 3.8 %collective-permute-done.5.rest_2_ = bf16[256,512]{1,0:T(8,128)(2,1)S(1)} collective-permute-done((bf16[256,512]{1,0:T(8,128)(2,1)S(1)}, bf16[256,512]{1,0:T(8,128)(2,1)S(1)}, u32[]{:S(2)}, u32[]{:S(2)}) %collective-permute-start.5) | collective-permute-done | bytes 262176 | tf_op jit(solution)/shard_map/ppermute | solution.py:29
  30.8 0.7 %add_pieces.7 = (f32[256,512]{1,0:T(8,128)S(1)}, f32[16,128]{1,0:T(8,128)S(1)}) custom-call(s32[1,8]{1,0:T(1,128)S(1)} %copy-done.4, s32[1]{0:T(128)S(6)} %copy.7.count_ref, bf16[512,512]{1,0:T(8,128)(2,1)S(1)} %get-tuple-element.15.rest_0_, s32[256,1024]{1,0:T(8,128)S(1)} %copy-done.1, bf16[256,512]{1,0:T(8,128)(2,1)S(1)} %collective-permute-done.5.rest_2_, ...), custom_call_target="tpu_custom_call" | custom-call | flops 268435456 | bytes 1048576 | tf_op jit(solution)/shard_map/add_pieces/pallas_call | solution.py:159
  31.5 12.4 %all_to_all.11 = f32[16,1,128]{2,1,0:T(1,128)S(1)} all-to-all(f32[16,1,128]{2,1,0:T(1,128)S(1)} %bitcast.5), channel_id=1, replica_groups=mesh['group'=2,'loop'=16] {'loop'}, dimensions={0} | all-to-all | bytes 16384 | tf_op jit(solution)/shard_map/all_to_all | solution.py:293
  43.9 1.0 %update.1 = f32[256,512]{1,0:T(8,128)} custom-call(f32[256,512]{1,0:T(8,128)S(1)} %copy-done.2, f32[256,512]{1,0:T(8,128)S(1)} %get-tuple-element.23.grad_ref, f32[16,128]{1,0:T(8,128)S(1)} %bitcast.4), custom_call_target="tpu_custom_call" | custom-call | flops 262144 | bytes 1572864 | tf_op jit(solution)/shard_map/update/pallas_call | solution.py:294
Async XLA Ops:
  0.0 14.3 %copy-start.2 = (f32[256,512]{1,0:T(8,128)S(1)}, f32[256,512]{1,0:T(8,128)}, u32[]{:S(2)}) copy-start(f32[256,512]{1,0:T(8,128)} %users_ref.1) | copy-start | bytes 1572868
  0.0 1.6 %collective-permute-start = (bf16[128,512]{1,0:T(8,128)(2,1)}, bf16[128,512]{1,0:T(8,128)(2,1)S(1)}, u32[]{:S(2)}, u32[]{:S(2)}) collective-permute-start(bf16[128,512]{1,0:T(8,128)(2,1)} %own_ref.1), channel_id=1, source_target_pairs={{0,1},{1,0},{2,3},{3,2},{4,5},{5,4},{6,7},{7,6},{8,9},{9,8},{10,11... | collective-permute-start | bytes 393224 | tf_op jit(solution)/shard_map/ppermute | solution.py:33
  1.7 0.7 %copy-start.5 = (bf16[128,512]{1,0:T(8,128)(2,1)}, bf16[128,512]{1,0:T(8,128)(2,1)S(1)}, u32[]{:S(2)}) copy-start(bf16[128,512]{1,0:T(8,128)(2,1)S(1)} %collective-permute-done.other_ref) | copy-start | bytes 393220
  4.0 10.3 %copy-start.4 = (s32[1,8]{1,0:T(1,128)S(1)}, s32[1,8]{1,0:T(1,128)}, u32[]{:S(2)}) copy-start(s32[1,8]{1,0:T(1,128)} %list_ref.7) | copy-start | bytes 100
  4.0 7.4 %collective-permute-start.1 = (bf16[256,512]{1,0:T(8,128)(2,1)}, bf16[256,512]{1,0:T(8,128)(2,1)S(1)}, u32[]{:S(2)}, u32[]{:S(2)}) collective-permute-start(bf16[256,512]{1,0:T(8,128)(2,1)} %join.1.rest_2_), channel_id=1, source_target_pairs={{0,4},{4,8},{8,12},{12,14},{14,10},{10,6},{6,2},{2,0},{1,3},{5,1},... | collective-permute-start | bytes 786440 | tf_op jit(solution)/shard_map/ppermute | solution.py:29
  11.4 6.5 %collective-permute-start.2 = (bf16[256,512]{1,0:T(8,128)(2,1)S(1)}, bf16[256,512]{1,0:T(8,128)(2,1)S(1)}, u32[]{:S(2)}, u32[]{:S(2)}) collective-permute-start(bf16[256,512]{1,0:T(8,128)(2,1)S(1)} %collective-permute-done.1.rest_3_), channel_id=1, source_target_pairs={{0,4},{4,8},{8,12},{12,14},{14,10},{10,6},{6,2},{2,0},{1,3},{5,1},... | collective-permute-start | bytes 786440 | tf_op jit(solution)/shard_map/ppermute | solution.py:29
  14.2 5.7 %collective-permute-start.4 = (bf16[256,512]{1,0:T(8,128)(2,1)S(1)}, bf16[256,512]{1,0:T(8,128)(2,1)S(1)}, u32[]{:S(2)}, u32[]{:S(2)}) collective-permute-start(bf16[256,512]{1,0:T(8,128)(2,1)S(1)} %collective-permute-done.1.rest_3_), channel_id=1, source_target_pairs={{0,1},{1,0},{2,3},{3,2},{4,5},{5,4},{6,7},{7,6},{8,9},{9,8},{10,11... | collective-permute-start | bytes 786440 | tf_op jit(solution)/shard_map/ppermute | solution.py:33
  14.3 1.2 %copy-start = (s32[256,1024]{1,0:T(8,128)S(1)}, s32[256,1024]{1,0:T(8,128)}, u32[]{:S(2)}) copy-start(s32[256,1024]{1,0:T(8,128)} %rest_1_.7) | copy-start | bytes 3145732
  15.5 0.9 %copy-start.3 = (bf16[256,512]{1,0:T(8,128)(2,1)S(1)}, bf16[256,512]{1,0:T(8,128)(2,1)}, u32[]{:S(2)}) copy-start(bf16[256,512]{1,0:T(8,128)(2,1)} %join.1.rest_2_) | copy-start | bytes 786436
  16.5 3.5 %copy-start.1 = (s32[256,1024]{1,0:T(8,128)S(1)}, s32[256,1024]{1,0:T(8,128)}, u32[]{:S(2)}) copy-start(s32[256,1024]{1,0:T(8,128)} %rest_1_.7) | copy-start | bytes 3145732
  18.0 6.4 %collective-permute-start.3 = (bf16[256,512]{1,0:T(8,128)(2,1)S(1)}, bf16[256,512]{1,0:T(8,128)(2,1)S(1)}, u32[]{:S(2)}, u32[]{:S(2)}) collective-permute-start(bf16[256,512]{1,0:T(8,128)(2,1)S(1)} %collective-permute-done.2.rest_3_), channel_id=1, source_target_pairs={{0,4},{4,8},{8,12},{12,14},{14,10},{10,6},{6,2},{2,0},{1,3},{5,1},... | collective-permute-start | bytes 786440 | tf_op jit(solution)/shard_map/ppermute | solution.py:29
  19.9 6.4 %collective-permute-start.6 = (bf16[256,512]{1,0:T(8,128)(2,1)S(1)}, bf16[256,512]{1,0:T(8,128)(2,1)S(1)}, u32[]{:S(2)}, u32[]{:S(2)}) collective-permute-start(bf16[256,512]{1,0:T(8,128)(2,1)S(1)} %collective-permute-done.2.rest_3_), channel_id=1, source_target_pairs={{0,1},{1,0},{2,3},{3,2},{4,5},{5,4},{6,7},{7,6},{8,9},{9,8},{10,11... | collective-permute-start | bytes 786440 | tf_op jit(solution)/shard_map/ppermute | solution.py:33
  24.4 1.9 %collective-permute-start.7 = (bf16[256,512]{1,0:T(8,128)(2,1)S(1)}, bf16[256,512]{1,0:T(8,128)(2,1)S(1)}, u32[]{:S(2)}, u32[]{:S(2)}) collective-permute-start(bf16[256,512]{1,0:T(8,128)(2,1)S(1)} %collective-permute-done.3.rest_3_), channel_id=1, source_target_pairs={{0,1},{1,0},{2,3},{3,2},{4,5},{5,4},{6,7},{7,6},{8,9},{9,8},{10,11... | collective-permute-start | bytes 786440 | tf_op jit(solution)/shard_map/ppermute | solution.py:33
  24.4 6.4 %collective-permute-start.5 = (bf16[256,512]{1,0:T(8,128)(2,1)S(1)}, bf16[256,512]{1,0:T(8,128)(2,1)S(1)}, u32[]{:S(2)}, u32[]{:S(2)}) collective-permute-start(bf16[256,512]{1,0:T(8,128)(2,1)S(1)} %collective-permute-done.3.rest_3_), channel_id=1, source_target_pairs={{0,4},{4,8},{8,12},{12,14},{14,10},{10,6},{6,2},{2,0},{1,3},{5,1},... | collective-permute-start | bytes 786440 | tf_op jit(solution)/shard_map/ppermute | solution.py:29

commit v4 on v3

--- a/solution.py
+++ b/solution.py
@@ -22,36 +22,15 @@
     return 2 * outer, device
 
 
-def to_next(array, loop_size):
+def to_next(array, direction, loop_size):
     chips, device = ring_place(loop_size)
-    pairs = [(device(at, 0), device(at + 1, 0)) for at in range(chips)]
-    pairs += [(device(at, 1), device(at - 1, 1)) for at in range(chips)]
+    pairs = [(device(at, 0), device(at + direction, 0)) for at in range(chips)]
+    pairs += [(device(at, 1), device(at - direction, 1)) for at in range(chips)]
     return lax.ppermute(array, "loop", pairs)
 
 
 def to_other_core(array, loop_size):
     return lax.ppermute(array, "loop", [(at, at ^ 1) for at in range(loop_size)])
-
-
-def join_kernel(own_ref, other_ref, both_ref):
-    tile = own_ref.shape[0]
-    core = lax.axis_index("loop") % 2
-    both_ref[pl.ds(pl.multiple_of(core * tile, tile), tile), :] = own_ref[...]
-    both_ref[pl.ds(pl.multiple_of((1 - core) * tile, tile), tile), :] = other_ref[...]
-
-
-def join(own, other):
-    tile, width = own.shape
-    return pl.pallas_call(
-        join_kernel,
-        out_shape=jax.ShapeDtypeStruct((2 * tile, width), own.dtype),
-        in_specs=[pl.BlockSpec(memory_space=pltpu.VMEM)] * 2,
-        out_specs=pl.BlockSpec(memory_space=pltpu.VMEM),
-        cost_estimate=pl.CostEstimate(
-            flops=0, bytes_accessed=8 * tile * width, transcendentals=0
-        ),
-        name="join",
-    )(own, other)
 
 
 def halves(values):
@@ -91,19 +70,21 @@
     square_ref[...] = jnp.broadcast_to(square, square_ref.shape)
 
 
-def chip_behind(hops, loop_size):
+def origin_block(origin, loop_size):
+    hops, other = origin
     chips = loop_size // 2
     me = lax.axis_index("loop")
     core, row, outer = me % 2, me // 2 % 2, me // 4
     position = jnp.where(row == 0, outer, chips - 1 - outer)
     at = lax.rem(position + chips + jnp.where(core == 0, -hops, hops), chips)
-    return jnp.where(at < chips // 2, 2 * at, 2 * (chips - 1 - at) + 1)
-
-
-def pieces_kernel(loop_size, hops, first, last, list_ref, count_ref, *rest):
+    chip = jnp.where(at < chips // 2, 2 * at, 2 * (chips - 1 - at) + 1)
+    return 2 * chip + (1 - core if other else core)
+
+
+def pieces_kernel(loop_size, origins, first, last, list_ref, count_ref, *rest):
     rest = list(rest)
     given_ref, labels_ref = rest.pop(0), rest.pop(0)
-    pieces = [rest.pop(0) for _ in hops]
+    pieces = [rest.pop(0) for _ in origins]
     before_ref = None if first else rest.pop(0)
     grad_ref = rest.pop(0)
     parts_ref = rest.pop(0) if first else given_ref
@@ -119,20 +100,18 @@
         jnp.where(slot < count_ref[0], list_ref[0, slot], -1) for slot in range(list_ref.shape[1])
     ]
     live = jnp.int32(0)
-    for piece, hop in zip(pieces, hops):
-        chip = chip_behind(hop, loop_size)
-        for core in range(2):
-            found = jnp.int32(-1)
-            for slot, name in enumerate(wanted):
-                found = jnp.where(name == 2 * chip + core, slot, found)
-
-            @pl.when(found >= 0)
-            def _():
-                into = pl.ds(pl.multiple_of(live * tile, tile), tile)
-                tiles[into, :] = piece[core * tile : (core + 1) * tile, :]
-                slots[live] = found
-
-            live = live + (found >= 0).astype(jnp.int32)
+    for piece, origin in zip(pieces, origins):
+        block = origin_block(origin, loop_size)
+        found = jnp.int32(-1)
+        for slot, name in enumerate(wanted):
+            found = jnp.where(name == block, slot, found)
+
+        @pl.when(found >= 0)
+        def _():
+            tiles[pl.ds(pl.multiple_of(live * tile, tile), tile), :] = piece[...]
+            slots[live] = found
+
+        live = live + (found >= 0).astype(jnp.int32)
     slots[live] = 0
 
     def labels_at(position):
@@ -148,16 +127,16 @@
     width = given.shape[1]
     rows = given.shape[0] // (1 if first else 2)
     pieces = [piece for _, piece in held]
-    tile = pieces[0].shape[0] // 2
-    most = min(2 * len(pieces), CHUNK)
+    tile = pieces[0].shape[0]
+    most = min(len(pieces), CHUNK)
     out_shape = [jax.ShapeDtypeStruct((rows, width), jnp.float32)]
     if first:
         out_shape.append(jax.ShapeDtypeStruct((2 * rows, width), jnp.bfloat16))
     if last:
         out_shape.append(jax.ShapeDtypeStruct((loop_size, 128), jnp.float32))
     extra = [] if first else [before]
-    return pl.pallas_call(
-        functools.partial(pieces_kernel, loop_size, [hops for hops, _ in held], first, last),
+    results = pl.pallas_call(
+        functools.partial(pieces_kernel, loop_size, [origin for origin, _ in held], first, last),
         out_shape=out_shape,
         in_specs=[pl.BlockSpec(memory_space=pltpu.SMEM)] * 2
         + [pl.BlockSpec(memory_space=pltpu.VMEM)] * (2 + len(pieces) + len(extra)),
@@ -174,32 +153,29 @@
         ),
         name="add_pieces",
     )(*lists, given, labels, *pieces, *extra)
+    return results if first or last else (results[0], given)
 
 
 def ring_gradient(users, items, lists, labels):
     loop_size = lax.axis_size("loop")
     far = loop_size // 4
-    near = join(items, to_other_core(items, loop_size))
-    ready, gradient, parts = [(0, near)], None, None
+    held = [[((0, 0), items), ((0, 1), to_other_core(items, loop_size))]]
+    given, gradient = users, None
+    up = down = items
     for hop in range(1, far + 1):
-        near = to_next(near, loop_size)
-        if hop < 2:
-            late = []
-        elif gradient is None:
-            gradient, parts = add_pieces(loop_size, ready, lists, users, labels, None, False)
-            ready = []
-        else:
-            (gradient,) = add_pieces(loop_size, ready, lists, parts, labels, gradient, False)
-            ready = []
-        if gradient is not None:
-            near, gradient = lax.optimization_barrier((near, gradient))
-        ready = ready + late + [(hop, near)]
-        late = []
+        if hop > 2:
+            gradient, given = add_pieces(loop_size, held[hop - 3], lists, given, labels, gradient, False)
+            up, gradient = lax.optimization_barrier((up, gradient))
+        up = to_next(up, 1, loop_size)
         if hop < far:
-            late = [(-hop, to_other_core(near, loop_size))]
-            if hop == far - 1:
-                ready, late = ready + late, []
-    return add_pieces(loop_size, ready, lists, parts, labels, gradient, True)
+            down = to_next(down, -1, loop_size)
+            arrived = [((hop, 0), up), ((-hop, 0), down)]
+            arrived += [((-hop, 1), to_other_core(up, loop_size)), ((hop, 1), to_other_core(down, loop_size))]
+            held.append(arrived)
+    gradient, given = add_pieces(loop_size, held[far - 2], lists, given, labels, gradient, False)
+    up, gradient = lax.optimization_barrier((up, gradient))
+    last = held[far - 1] + [((far, 0), up), ((far, 1), to_other_core(up, loop_size))]
+    return add_pieces(loop_size, last, lists, given, labels, gradient, True)
 
 
 def chunks_kernel(

time: 45.1 us -> 42.2 us (0.936)
  waiting for transfers between devices: 12.6 us -> 7.38 us
  starting transfers between devices: 9.29 us -> 11 us
  Pallas kernels: 7.03 us -> 7.76 us
  blocking collectives: 12.4 us -> 11.8 us
    ppermute x4 -> x7, waiting for transfers between devices: 11.4 us -> 6.02 us  [to_next(): return lax.ppermute(array, 'loop', pairs)]
    ppermute x4 -> x8, starting transfers between devices: 0.53 us -> 1.44 us  [to_other_core(): lax.ppermute(array, 'loop', [(at, at ^ 1) for at in range(loop_size)])]
    ppermute x4 -> x7, starting transfers between devices: 8.76 us -> 9.54 us  [to_next(): return lax.ppermute(array, 'loop', pairs)]
    pallas_call x5 -> x4, Pallas kernels: 6.06 us -> 6.78 us  [add_pieces(): pl.pallas_call(functools.partial(pieces_kernel, loop_size, [origin for or...]
    all_to_all x1, blocking collectives: 12.4 us -> 11.8 us  [local(): squares = lax.all_to_all(square, 'loop', 0, 0, tiled=True)]
    unnamed x12 -> x10, local copies, waits for them, and re-layouts: 2.84 us -> 3.17 us
    ppermute x4 -> x8, waiting for transfers between devices: 1.2 us -> 1.35 us  [to_other_core(): lax.ppermute(array, 'loop', [(at, at ^ 1) for at in range(loop_size)])]
  transfers between devices with their start and end apart: 8 -> 15, of which waited for: 4 -> 5; matrix products, arithmetic and copies ran while one was open for 0% -> 0% of each run, Pallas kernels for 8% -> 11%
where the time goes in v4:
time: 42.2 us; the launch traced here: 41.9 us
  blocking collectives  11.8 us (28%)
  starting transfers between devices  11 us (26%)
  Pallas kernels  7.76 us (18%)
  waiting for transfers between devices  7.38 us (17%)
  local copies, waits for them, and re-layouts  3.17 us (8%)
  between operations  0.74 us (2%)
    all_to_all x1, blocking collectives, local(): squares = lax.all_to_all(square, 'loop', 0, 0, tiled=True)  11.8 us
    ppermute x7, starting transfers between devices, to_next(): return lax.ppermute(array, 'loop', pairs)  9.54 us
    pallas_call x4, Pallas kernels, add_pieces(): pl.pallas_call(functools.partial(pieces_kernel, loop_size, [origin for or...  6.78 us
    ppermute x7, waiting for transfers between devices, to_next(): return lax.ppermute(array, 'loop', pairs)  6.02 us
    unnamed x10, local copies, waits for them, and re-layouts  3.17 us
    ppermute x8, starting transfers between devices, to_other_core(): lax.ppermute(array, 'loop', [(at, at ^ 1) for at in range(loop_size)])  1.44 us
    ppermute x8, waiting for transfers between devices, to_other_core(): lax.ppermute(array, 'loop', [(at, at ^ 1) for at in range(loop_size)])  1.35 us
    pallas_call x1, Pallas kernels, local(): pl.pallas_call(functools.partial(update_kernel, rows * loop_size * width)...  0.98 us
  transfers between devices with their start and end apart: 15, of which 5 were waited for; matrix products, arithmetic and copies ran while one was open for 0% of the time, Pallas kernels for 11%

profile of v4, /device:TPU:0, one launch (start us, length us, event | category | flops | bytes accessed | tf_op | source)
XLA Modules:
  0.0 41.9 jit_solution(13802277445885907421)
XLA Ops:
  0.0 0.0 copy-start.4
  0.0 3.0 %collective-permute-start.1 = (bf16[128,512]{1,0:T(8,128)(2,1)}, bf16[128,512]{1,0:T(8,128)(2,1)S(1)}, u32[]{:S(2)}, u32[]{:S(2)}) collective-permute-start(bf16[128,512]{1,0:T(8,128)(2,1)} %rest_2_.1), channel_id=1, source_target_pairs={{0,4},{4,8},{8,12},{12,14},{14,10},{10,6},{6,2},{2,0},{1,3},{5,1},... | collective-permute-start | bytes 393224 | tf_op jit(solution)/shard_map/ppermute | solution.py:29
  3.0 0.0 collective-permute-start.4
  3.0 0.0 collective-permute-start
  3.0 3.9 %collective-permute-done.1.rest_2_ = bf16[128,512]{1,0:T(8,128)(2,1)S(1)} collective-permute-done((bf16[128,512]{1,0:T(8,128)(2,1)}, bf16[128,512]{1,0:T(8,128)(2,1)S(1)}, u32[]{:S(2)}, u32[]{:S(2)}) %collective-permute-start.1) | collective-permute-done | bytes 131104 | tf_op jit(solution)/shard_map/ppermute | solution.py:29
  7.0 1.5 %collective-permute-start.2 = (bf16[128,512]{1,0:T(8,128)(2,1)S(1)}, bf16[128,512]{1,0:T(8,128)(2,1)S(1)}, u32[]{:S(2)}, u32[]{:S(2)}) collective-permute-start(bf16[128,512]{1,0:T(8,128)(2,1)S(1)} %collective-permute-done.1.rest_2_), channel_id=1, source_target_pairs={{0,4},{4,8},{8,12},{12,14},{14,10},{10,6},{6,2},{2,0},{1,3},{5,1},... | collective-permute-start | bytes 393224 | tf_op jit(solution)/shard_map/ppermute | solution.py:29
  8.5 0.0 collective-permute-done.4.rest_3_
  8.5 0.9 %collective-permute-start.5 = (bf16[128,512]{1,0:T(8,128)(2,1)S(1)}, bf16[128,512]{1,0:T(8,128)(2,1)S(1)}, u32[]{:S(2)}, u32[]{:S(2)}) collective-permute-start(bf16[128,512]{1,0:T(8,128)(2,1)S(1)} %collective-permute-done.4.rest_3_), channel_id=1, source_target_pairs={{0,2},{4,0},{8,4},{12,8},{14,12},{10,14},{6,10},{2,6},{1,5},{5,9},... | collective-permute-start | bytes 393224 | tf_op jit(solution)/shard_map/ppermute | solution.py:29
  9.4 0.0 collective-permute-start.10
  9.4 0.5 %collective-permute-start.9 = (bf16[128,512]{1,0:T(8,128)(2,1)S(1)}, bf16[128,512]{1,0:T(8,128)(2,1)S(1)}, u32[]{:S(2)}, u32[]{:S(2)}) collective-permute-start(bf16[128,512]{1,0:T(8,128)(2,1)S(1)} %collective-permute-done.1.rest_2_), channel_id=1, source_target_pairs={{0,1},{1,0},{2,3},{3,2},{4,5},{5,4},{6,7},{7,6},{8,9},{9,8},{10,11... | collective-permute-start | bytes 393224 | tf_op jit(solution)/shard_map/ppermute | solution.py:33
  10.6 0.0 collective-permute-done.rest_3_
  10.6 0.0 copy-done.4
  10.6 0.0 copy-start
  10.6 1.2 %copy-done = s32[256,1024]{1,0:T(8,128)S(1)} copy-done((s32[256,1024]{1,0:T(8,128)S(1)}, s32[256,1024]{1,0:T(8,128)}, u32[]{:S(2)}) %copy-start) | copy-done | bytes 1048600
  11.8 0.0 copy-start.2
  11.8 1.0 %copy-done.2 = f32[256,512]{1,0:T(8,128)S(1)} copy-done((f32[256,512]{1,0:T(8,128)S(1)}, f32[256,512]{1,0:T(8,128)}, u32[]{:S(2)}) %copy-start.2) | copy-done | bytes 524312
  12.8 0.0 copy-start.3
  12.9 0.9 %copy-done.3 = bf16[128,512]{1,0:T(8,128)(2,1)S(1)} copy-done((bf16[128,512]{1,0:T(8,128)(2,1)S(1)}, bf16[128,512]{1,0:T(8,128)(2,1)}, u32[]{:S(2)}) %copy-start.3) | copy-done | bytes 131096
  13.8 0.0 copy-start.1
  13.8 1.5 %add_pieces.4 = (f32[256,512]{1,0:T(8,128)S(1)}, bf16[512,512]{1,0:T(8,128)(2,1)S(1)}) custom-call(s32[1,8]{1,0:T(1,128)S(1)} %copy-done.4, s32[1]{0:T(128)S(6)} %copy.7.count_ref, f32[256,512]{1,0:T(8,128)S(1)} %copy-done.2, s32[256,1024]{1,0:T(8,128)S(1)} %copy-done, bf16[128,512]{1,0:T(8,128)(2,1)S(1)} %copy-done.3, ...), custom_call_target="tpu_custom_call" | custom-call | flops 268435456 | bytes 1048576 | tf_op jit(solution)/shard_map/add_pieces/pallas_call | solution.py:138
  15.3 0.0 collective-permute-done.2.rest_2_
  15.3 1.2 %collective-permute-start.3 = (bf16[128,512]{1,0:T(8,128)(2,1)S(1)}, bf16[128,512]{1,0:T(8,128)(2,1)S(1)}, u32[]{:S(2)}, u32[]{:S(2)}) collective-permute-start(bf16[128,512]{1,0:T(8,128)(2,1)S(1)} %collective-permute-done.2.rest_2_), channel_id=1, source_target_pairs={{0,4},{4,8},{8,12},{12,14},{14,10},{10,6},{6,2},{2,0},{1,3},{5,1},... | collective-permute-start | bytes 393224 | tf_op jit(solution)/shard_map/ppermute | solution.py:29
  16.5 0.6 %collective-permute-start.12 = (bf16[128,512]{1,0:T(8,128)(2,1)S(1)}, bf16[128,512]{1,0:T(8,128)(2,1)S(1)}, u32[]{:S(2)}, u32[]{:S(2)}) collective-permute-start(bf16[128,512]{1,0:T(8,128)(2,1)S(1)} %collective-permute-done.2.rest_2_), channel_id=1, source_target_pairs={{0,1},{1,0},{2,3},{3,2},{4,5},{5,4},{6,7},{7,6},{8,9},{9,8},{10,11... | collective-permute-start | bytes 393224 | tf_op jit(solution)/shard_map/ppermute | solution.py:33
  17.1 0.0 collective-permute-done.5.rest_3_
  17.1 0.0 collective-permute-start.13
  17.1 0.0 collective-permute-done.10.rest_5_
  17.1 0.8 %collective-permute-start.6 = (bf16[128,512]{1,0:T(8,128)(2,1)S(1)}, bf16[128,512]{1,0:T(8,128)(2,1)S(1)}, u32[]{:S(2)}, u32[]{:S(2)}) collective-permute-start(bf16[128,512]{1,0:T(8,128)(2,1)S(1)} %collective-permute-done.5.rest_3_), channel_id=1, source_target_pairs={{0,2},{4,0},{8,4},{12,8},{14,12},{10,14},{6,10},{2,6},{1,5},{5,9},... | collective-permute-start | bytes 393224 | tf_op jit(solution)/shard_map/ppermute | solution.py:29
  17.9 0.0 collective-permute-done.9.rest_4_
  17.9 0.0 copy-done.1
  17.9 1.5 %add_pieces.5.rest_6_ = f32[256,512]{1,0:T(8,128)S(1)} custom-call(s32[1,8]{1,0:T(1,128)S(1)} %copy-done.4, s32[1]{0:T(128)S(6)} %copy.7.count_ref, bf16[512,512]{1,0:T(8,128)(2,1)S(1)} %get-tuple-element.15.rest_0_, s32[256,1024]{1,0:T(8,128)S(1)} %copy-done.1, bf16[128,512]{1,0:T(8,128)(2,1)S(1)} %collective-permute-done.1.rest_2_, ...), custom_call_target="tpu_custom_call" | custom-call | flops 536870912 | bytes 1048576 | tf_op jit(solution)/shard_map/add_pieces/pallas_call | solution.py:138
  19.4 1.0 %collective-permute-done.3.rest_2_ = bf16[128,512]{1,0:T(8,128)(2,1)S(1)} collective-permute-done((bf16[128,512]{1,0:T(8,128)(2,1)S(1)}, bf16[128,512]{1,0:T(8,128)(2,1)S(1)}, u32[]{:S(2)}, u32[]{:S(2)}) %collective-permute-start.3) | collective-permute-done | bytes 131104 | tf_op jit(solution)/shard_map/ppermute | solution.py:29
  20.4 2.1 %collective-permute-start.11 = (bf16[128,512]{1,0:T(8,128)(2,1)S(1)}, bf16[128,512]{1,0:T(8,128)(2,1)S(1)}, u32[]{:S(2)}, u32[]{:S(2)}) collective-permute-start(bf16[128,512]{1,0:T(8,128)(2,1)S(1)} %collective-permute-done.3.rest_2_), channel_id=1, source_target_pairs={{0,4},{4,8},{8,12},{12,14},{14,10},{10,6},{6,2},{2,0},{1,3},{5,1},... | collective-permute-start | bytes 393224 | tf_op jit(solution)/shard_map/ppermute | solution.py:29
  22.4 0.0 collective-permute-start.7
  22.4 0.2 collective-permute-done.6.rest_3_
  22.6 0.3 collective-permute-start.8
  22.9 0.0 collective-permute-done.12.rest_4_
  22.9 0.0 collective-permute-done.13.rest_5_
  22.9 1.5 %add_pieces.6.rest_8_ = f32[256,512]{1,0:T(8,128)S(1)} custom-call(s32[1,8]{1,0:T(1,128)S(1)} %copy-done.4, s32[1]{0:T(128)S(6)} %copy.7.count_ref, bf16[512,512]{1,0:T(8,128)(2,1)S(1)} %get-tuple-element.15.rest_0_, s32[256,1024]{1,0:T(8,128)S(1)} %copy-done.1, bf16[128,512]{1,0:T(8,128)(2,1)S(1)} %collective-permute-done.2.rest_2_, ...), custom_call_target="tpu_custom_call" | custom-call | flops 536870912 | bytes 1048576 | tf_op jit(solution)/shard_map/add_pieces/pallas_call | solution.py:138
  24.4 0.9 %collective-permute-done.11.rest_6_ = bf16[128,512]{1,0:T(8,128)(2,1)S(1)} collective-permute-done((bf16[128,512]{1,0:T(8,128)(2,1)S(1)}, bf16[128,512]{1,0:T(8,128)(2,1)S(1)}, u32[]{:S(2)}, u32[]{:S(2)}) %collective-permute-start.11) | collective-permute-done | bytes 131104 | tf_op jit(solution)/shard_map/ppermute | solution.py:29
  25.3 0.0 collective-permute-start.14
  25.3 0.0 collective-permute-done.7.rest_4_
  25.3 0.0 collective-permute-done.8.rest_5_
  25.3 1.3 %collective-permute-done.14.rest_7_ = bf16[128,512]{1,0:T(8,128)(2,1)S(1)} collective-permute-done((bf16[128,512]{1,0:T(8,128)(2,1)S(1)}, bf16[128,512]{1,0:T(8,128)(2,1)S(1)}, u32[]{:S(2)}, u32[]{:S(2)}) %collective-permute-start.14) | collective-permute-done | bytes 131104 | tf_op jit(solution)/shard_map/ppermute | solution.py:33
  26.7 2.4 %add_pieces.7 = (f32[256,512]{1,0:T(8,128)S(1)}, f32[16,128]{1,0:T(8,128)S(1)}) custom-call(s32[1,8]{1,0:T(1,128)S(1)} %copy-done.4, s32[1]{0:T(128)S(6)} %copy.7.count_ref, bf16[512,512]{1,0:T(8,128)(2,1)S(1)} %get-tuple-element.15.rest_0_, s32[256,1024]{1,0:T(8,128)S(1)} %copy-done.1, bf16[128,512]{1,0:T(8,128)(2,1)S(1)} %collective-permute-done.3.rest_2_, ...), custom_call_target="tpu_custom_call" | custom-call | flops 805306368 | bytes 1048576 | tf_op jit(solution)/shard_map/add_pieces/pallas_call | solution.py:138
  29.0 11.8 %all_to_all.11 = f32[16,1,128]{2,1,0:T(1,128)S(1)} all-to-all(f32[16,1,128]{2,1,0:T(1,128)S(1)} %bitcast.5), channel_id=1, replica_groups=mesh['group'=2,'loop'=16] {'loop'}, dimensions={0} | all-to-all | bytes 16384 | tf_op jit(solution)/shard_map/all_to_all | solution.py:269
  40.9 1.0 %update.1 = f32[256,512]{1,0:T(8,128)} custom-call(f32[256,512]{1,0:T(8,128)S(1)} %copy-done.2, f32[256,512]{1,0:T(8,128)S(1)} %get-tuple-element.23.grad_ref, f32[16,128]{1,0:T(8,128)S(1)} %bitcast.4), custom_call_target="tpu_custom_call" | custom-call | flops 262144 | bytes 1572864 | tf_op jit(solution)/shard_map/update/pallas_call | solution.py:270
Async XLA Ops:
  0.0 10.6 %copy-start.4 = (s32[1,8]{1,0:T(1,128)S(1)}, s32[1,8]{1,0:T(1,128)}, u32[]{:S(2)}) copy-start(s32[1,8]{1,0:T(1,128)} %list_ref.7) | copy-start | bytes 100
  0.0 7.0 %collective-permute-start.1 = (bf16[128,512]{1,0:T(8,128)(2,1)}, bf16[128,512]{1,0:T(8,128)(2,1)S(1)}, u32[]{:S(2)}, u32[]{:S(2)}) collective-permute-start(bf16[128,512]{1,0:T(8,128)(2,1)} %rest_2_.1), channel_id=1, source_target_pairs={{0,4},{4,8},{8,12},{12,14},{14,10},{10,6},{6,2},{2,0},{1,3},{5,1},... | collective-permute-start | bytes 393224 | tf_op jit(solution)/shard_map/ppermute | solution.py:29
  3.0 5.5 %collective-permute-start.4 = (bf16[128,512]{1,0:T(8,128)(2,1)}, bf16[128,512]{1,0:T(8,128)(2,1)S(1)}, u32[]{:S(2)}, u32[]{:S(2)}) collective-permute-start(bf16[128,512]{1,0:T(8,128)(2,1)} %rest_2_.1), channel_id=1, source_target_pairs={{0,2},{4,0},{8,4},{12,8},{14,12},{10,14},{6,10},{2,6},{1,5},{5,9},... | collective-permute-start | bytes 393224 | tf_op jit(solution)/shard_map/ppermute | solution.py:29
  3.0 7.5 %collective-permute-start = (bf16[128,512]{1,0:T(8,128)(2,1)}, bf16[128,512]{1,0:T(8,128)(2,1)S(1)}, u32[]{:S(2)}, u32[]{:S(2)}) collective-permute-start(bf16[128,512]{1,0:T(8,128)(2,1)} %rest_2_.1), channel_id=1, source_target_pairs={{0,1},{1,0},{2,3},{3,2},{4,5},{5,4},{6,7},{7,6},{8,9},{9,8},{10,11... | collective-permute-start | bytes 393224 | tf_op jit(solution)/shard_map/ppermute | solution.py:33
  7.0 8.3 %collective-permute-start.2 = (bf16[128,512]{1,0:T(8,128)(2,1)S(1)}, bf16[128,512]{1,0:T(8,128)(2,1)S(1)}, u32[]{:S(2)}, u32[]{:S(2)}) collective-permute-start(bf16[128,512]{1,0:T(8,128)(2,1)S(1)} %collective-permute-done.1.rest_2_), channel_id=1, source_target_pairs={{0,4},{4,8},{8,12},{12,14},{14,10},{10,6},{6,2},{2,0},{1,3},{5,1},... | collective-permute-start | bytes 393224 | tf_op jit(solution)/shard_map/ppermute | solution.py:29
  8.5 8.5 %collective-permute-start.5 = (bf16[128,512]{1,0:T(8,128)(2,1)S(1)}, bf16[128,512]{1,0:T(8,128)(2,1)S(1)}, u32[]{:S(2)}, u32[]{:S(2)}) collective-permute-start(bf16[128,512]{1,0:T(8,128)(2,1)S(1)} %collective-permute-done.4.rest_3_), channel_id=1, source_target_pairs={{0,2},{4,0},{8,4},{12,8},{14,12},{10,14},{6,10},{2,6},{1,5},{5,9},... | collective-permute-start | bytes 393224 | tf_op jit(solution)/shard_map/ppermute | solution.py:29
  9.4 7.7 %collective-permute-start.10 = (bf16[128,512]{1,0:T(8,128)(2,1)S(1)}, bf16[128,512]{1,0:T(8,128)(2,1)S(1)}, u32[]{:S(2)}, u32[]{:S(2)}) collective-permute-start(bf16[128,512]{1,0:T(8,128)(2,1)S(1)} %collective-permute-done.4.rest_3_), channel_id=1, source_target_pairs={{0,1},{1,0},{2,3},{3,2},{4,5},{5,4},{6,7},{7,6},{8,9},{9,8},{10,11... | collective-permute-start | bytes 393224 | tf_op jit(solution)/shard_map/ppermute | solution.py:33
  9.4 8.5 %collective-permute-start.9 = (bf16[128,512]{1,0:T(8,128)(2,1)S(1)}, bf16[128,512]{1,0:T(8,128)(2,1)S(1)}, u32[]{:S(2)}, u32[]{:S(2)}) collective-permute-start(bf16[128,512]{1,0:T(8,128)(2,1)S(1)} %collective-permute-done.1.rest_2_), channel_id=1, source_target_pairs={{0,1},{1,0},{2,3},{3,2},{4,5},{5,4},{6,7},{7,6},{8,9},{9,8},{10,11... | collective-permute-start | bytes 393224 | tf_op jit(solution)/shard_map/ppermute | solution.py:33
  10.6 1.2 %copy-start = (s32[256,1024]{1,0:T(8,128)S(1)}, s32[256,1024]{1,0:T(8,128)}, u32[]{:S(2)}) copy-start(s32[256,1024]{1,0:T(8,128)} %rest_1_.7) | copy-start | bytes 3145732
  11.8 1.0 %copy-start.2 = (f32[256,512]{1,0:T(8,128)S(1)}, f32[256,512]{1,0:T(8,128)}, u32[]{:S(2)}) copy-start(f32[256,512]{1,0:T(8,128)} %users_ref.1) | copy-start | bytes 1572868
  12.8 0.9 %copy-start.3 = (bf16[128,512]{1,0:T(8,128)(2,1)S(1)}, bf16[128,512]{1,0:T(8,128)(2,1)}, u32[]{:S(2)}) copy-start(bf16[128,512]{1,0:T(8,128)(2,1)} %rest_2_.1) | copy-start | bytes 393220
  13.8 4.2 %copy-start.1 = (s32[256,1024]{1,0:T(8,128)S(1)}, s32[256,1024]{1,0:T(8,128)}, u32[]{:S(2)}) copy-start(s32[256,1024]{1,0:T(8,128)} %rest_1_.7) | copy-start | bytes 3145732
  15.3 5.1 %collective-permute-start.3 = (bf16[128,512]{1,0:T(8,128)(2,1)S(1)}, bf16[128,512]{1,0:T(8,128)(2,1)S(1)}, u32[]{:S(2)}, u32[]{:S(2)}) collective-permute-start(bf16[128,512]{1,0:T(8,128)(2,1)S(1)} %collective-permute-done.2.rest_2_), channel_id=1, source_target_pairs={{0,4},{4,8},{8,12},{12,14},{14,10},{10,6},{6,2},{2,0},{1,3},{5,1},... | collective-permute-start | bytes 393224 | tf_op jit(solution)/shard_map/ppermute | solution.py:29
  16.5 6.5 %collective-permute-start.12 = (bf16[128,512]{1,0:T(8,128)(2,1)S(1)}, bf16[128,512]{1,0:T(8,128)(2,1)S(1)}, u32[]{:S(2)}, u32[]{:S(2)}) collective-permute-start(bf16[128,512]{1,0:T(8,128)(2,1)S(1)} %collective-permute-done.2.rest_2_), channel_id=1, source_target_pairs={{0,1},{1,0},{2,3},{3,2},{4,5},{5,4},{6,7},{7,6},{8,9},{9,8},{10,11... | collective-permute-start | bytes 393224 | tf_op jit(solution)/shard_map/ppermute | solution.py:33
  17.1 5.9 %collective-permute-start.13 = (bf16[128,512]{1,0:T(8,128)(2,1)S(1)}, bf16[128,512]{1,0:T(8,128)(2,1)S(1)}, u32[]{:S(2)}, u32[]{:S(2)}) collective-permute-start(bf16[128,512]{1,0:T(8,128)(2,1)S(1)} %collective-permute-done.5.rest_3_), channel_id=1, source_target_pairs={{0,1},{1,0},{2,3},{3,2},{4,5},{5,4},{6,7},{7,6},{8,9},{9,8},{10,11... | collective-permute-start | bytes 393224 | tf_op jit(solution)/shard_map/ppermute | solution.py:33
  17.1 5.5 %collective-permute-start.6 = (bf16[128,512]{1,0:T(8,128)(2,1)S(1)}, bf16[128,512]{1,0:T(8,128)(2,1)S(1)}, u32[]{:S(2)}, u32[]{:S(2)}) collective-permute-start(bf16[128,512]{1,0:T(8,128)(2,1)S(1)} %collective-permute-done.5.rest_3_), channel_id=1, source_target_pairs={{0,2},{4,0},{8,4},{12,8},{14,12},{10,14},{6,10},{2,6},{1,5},{5,9},... | collective-permute-start | bytes 393224 | tf_op jit(solution)/shard_map/ppermute | solution.py:29
  20.4 5.0 %collective-permute-start.11 = (bf16[128,512]{1,0:T(8,128)(2,1)S(1)}, bf16[128,512]{1,0:T(8,128)(2,1)S(1)}, u32[]{:S(2)}, u32[]{:S(2)}) collective-permute-start(bf16[128,512]{1,0:T(8,128)(2,1)S(1)} %collective-permute-done.3.rest_2_), channel_id=1, source_target_pairs={{0,4},{4,8},{8,12},{12,14},{14,10},{10,6},{6,2},{2,0},{1,3},{5,1},... | collective-permute-start | bytes 393224 | tf_op jit(solution)/shard_map/ppermute | solution.py:29
  22.4 2.9 %collective-permute-start.7 = (bf16[128,512]{1,0:T(8,128)(2,1)S(1)}, bf16[128,512]{1,0:T(8,128)(2,1)S(1)}, u32[]{:S(2)}, u32[]{:S(2)}) collective-permute-start(bf16[128,512]{1,0:T(8,128)(2,1)S(1)} %collective-permute-done.3.rest_2_), channel_id=1, source_target_pairs={{0,1},{1,0},{2,3},{3,2},{4,5},{5,4},{6,7},{7,6},{8,9},{9,8},{10,11... | collective-permute-start | bytes 393224 | tf_op jit(solution)/shard_map/ppermute | solution.py:33
  22.6 2.7 %collective-permute-start.8 = (bf16[128,512]{1,0:T(8,128)(2,1)S(1)}, bf16[128,512]{1,0:T(8,128)(2,1)S(1)}, u32[]{:S(2)}, u32[]{:S(2)}) collective-permute-start(bf16[128,512]{1,0:T(8,128)(2,1)S(1)} %collective-permute-done.6.rest_3_), channel_id=1, source_target_pairs={{0,1},{1,0},{2,3},{3,2},{4,5},{5,4},{6,7},{7,6},{8,9},{9,8},{10,11... | collective-permute-start | bytes 393224 | tf_op jit(solution)/shard_map/ppermute | solution.py:33
  25.3 1.3 %collective-permute-start.14 = (bf16[128,512]{1,0:T(8,128)(2,1)S(1)}, bf16[128,512]{1,0:T(8,128)(2,1)S(1)}, u32[]{:S(2)}, u32[]{:S(2)}) collective-permute-start(bf16[128,512]{1,0:T(8,128)(2,1)S(1)} %collective-permute-done.11.rest_6_), channel_id=1, source_target_pairs={{0,1},{1,0},{2,3},{3,2},{4,5},{5,4},{6,7},{7,6},{8,9},{9,8},{10,11... | collective-permute-start | bytes 393224 | tf_op jit(solution)/shard_map/ppermute | solution.py:33

commit v5 on v4

--- a/solution.py
+++ b/solution.py
@@ -38,8 +38,53 @@
     return jnp.concatenate([upper, (values - upper.astype(jnp.float32)).astype(jnp.bfloat16)], 0)
 
 
-def add_tiles(grad_ref, parts_ref, tiles, live, labels_at):
+def table_kernel(loop_size, origins, list_ref, count_ref, table_ref):
+    wanted = [
+        jnp.where(slot < count_ref[0], list_ref[0, slot], -1) for slot in range(list_ref.shape[1])
+    ]
+    for at, origin in enumerate(origins):
+        block = origin_block(origin, loop_size)
+        found = jnp.int32(-1)
+        for slot, name in enumerate(wanted):
+            found = jnp.where(name == block, slot, found)
+        table_ref[at] = found
+
+
+def slot_table(loop_size, origins, block_list, live_count):
+    return pl.pallas_call(
+        functools.partial(table_kernel, loop_size, origins),
+        out_shape=jax.ShapeDtypeStruct((len(origins),), jnp.int32),
+        in_specs=[pl.BlockSpec(memory_space=pltpu.SMEM)] * 2,
+        out_specs=pl.BlockSpec(memory_space=pltpu.SMEM),
+        cost_estimate=pl.CostEstimate(flops=2**32, bytes_accessed=1024, transcendentals=0),
+        name="slot_table",
+    )(block_list, live_count)
+
+
+def add_some(grad_ref, parts_ref, tiles, start, count, labels_at):
     rows = grad_ref.shape[0]
+    tile = tiles.shape[0] // CHUNK
+    block = tiles[pl.ds(pl.multiple_of(start * tile, 2 * tile), count * tile), :]
+    upper, lower = [], []
+    for at in range(0, count, 2):
+        both = lax.dot_general(
+            parts_ref[...],
+            block[at * tile : (at + 2) * tile],
+            (((1,), (1,)), ((), ())),
+            preferred_element_type=jnp.float32,
+        )
+        labels = jnp.concatenate([labels_at(start + at), labels_at(start + at + 1)], 1)
+        residual = 0.5 * jnp.tanh(both[:rows] + both[rows:]) + (0.5 - labels.astype(jnp.float32))
+        upper.append(residual.astype(jnp.bfloat16))
+        lower.append((residual - upper[-1].astype(jnp.float32)).astype(jnp.bfloat16))
+    grad_ref[...] += jnp.dot(
+        jnp.concatenate(upper + lower, 1),
+        jnp.concatenate([block, block], 0),
+        preferred_element_type=jnp.float32,
+    )
+
+
+def add_tiles(grad_ref, parts_ref, tiles, live, most, labels_at):
     tile = tiles.shape[0] // CHUNK
 
     @pl.when(live % 2 == 1)
@@ -47,20 +92,18 @@
         blank = pl.multiple_of(live * tile, tile)
         tiles[pl.ds(blank, tile), :] = jnp.zeros((tile, tiles.shape[1]), tiles.dtype)
 
-    def pair(index, carry):
-        block = tiles[pl.ds(pl.multiple_of(index * 2 * tile, 2 * tile), 2 * tile), :]
-        both = lax.dot_general(
-            parts_ref[...], block, (((1,), (1,)), ((), ())), preferred_element_type=jnp.float32
-        )
-        chance = 0.5 * jnp.tanh(0.5 * (both[:rows] + both[rows:])) + 0.5
-        labels = jnp.concatenate([labels_at(2 * index), labels_at(2 * index + 1)], 1)
-        position = 2 * index + lax.broadcasted_iota(jnp.int32, chance.shape, 1) // tile
-        residual = jnp.where(position < live, chance - labels.astype(jnp.float32), 0.0)
-        both = jnp.dot(halves(residual), block, preferred_element_type=jnp.float32)
-        grad_ref[...] += both[:rows] + both[rows:]
-        return carry
-
-    lax.fori_loop(0, (live + 1) // 2, pair, 0)
+    fours = (live + 1) // 4 if most > 2 else jnp.int32(0)
+    if most > 2:
+
+        def four(index, carry):
+            add_some(grad_ref, parts_ref, tiles, index * 4, 4, labels_at)
+            return carry
+
+        lax.fori_loop(0, fours, four, 0)
+
+    @pl.when(live > 4 * fours)
+    def _():
+        add_some(grad_ref, parts_ref, tiles, 4 * fours, 2, labels_at)
 
 
 def store_square(grad_ref, square_ref):
@@ -81,34 +124,31 @@
     return 2 * chip + (1 - core if other else core)
 
 
-def pieces_kernel(loop_size, origins, first, last, list_ref, count_ref, *rest):
+def pieces_kernel(places, sizes, packed, first, last, table_ref, given_ref, labels_ref, *rest):
     rest = list(rest)
-    given_ref, labels_ref = rest.pop(0), rest.pop(0)
-    pieces = [rest.pop(0) for _ in origins]
+    arrays = [rest.pop(0) for _ in sizes]
     before_ref = None if first else rest.pop(0)
     grad_ref = rest.pop(0)
     parts_ref = rest.pop(0) if first else given_ref
+    pack_ref = rest.pop(0) if packed else None
     square_ref = rest.pop(0) if last else None
     tiles, slots = rest
     tile = tiles.shape[0] // CHUNK
+    for at, index in enumerate(packed):
+        pack_ref[at * tile : (at + 1) * tile, :] = arrays[index][...]
     if first:
-        parts_ref[...] = halves(given_ref[...])
+        parts_ref[...] = halves(0.5 * given_ref[...])
         grad_ref[...] = jnp.zeros_like(grad_ref)
     else:
         grad_ref[...] = before_ref[...]
-    wanted = [
-        jnp.where(slot < count_ref[0], list_ref[0, slot], -1) for slot in range(list_ref.shape[1])
-    ]
     live = jnp.int32(0)
-    for piece, origin in zip(pieces, origins):
-        block = origin_block(origin, loop_size)
-        found = jnp.int32(-1)
-        for slot, name in enumerate(wanted):
-            found = jnp.where(name == block, slot, found)
+    for at, index, row in places:
+        found = table_ref[at]
 
         @pl.when(found >= 0)
         def _():
-            tiles[pl.ds(pl.multiple_of(live * tile, tile), tile), :] = piece[...]
+            into = pl.ds(pl.multiple_of(live * tile, tile), tile)
+            tiles[into, :] = arrays[index][row * tile : (row + 1) * tile, :]
             slots[live] = found
 
         live = live + (found >= 0).astype(jnp.int32)
@@ -117,29 +157,32 @@
     def labels_at(position):
         return labels_ref[:, pl.ds(pl.multiple_of(slots[position] * tile, tile), tile)]
 
-    add_tiles(grad_ref, parts_ref, tiles, live, labels_at)
+    add_tiles(grad_ref, parts_ref, tiles, live, min(len(places), CHUNK), labels_at)
     if last:
         store_square(grad_ref, square_ref)
 
 
-def add_pieces(loop_size, held, lists, given, labels, before, last):
+def add_pieces(held, packed, loop_size, table, given, labels, before, last):
     first = before is None
     width = given.shape[1]
     rows = given.shape[0] // (1 if first else 2)
-    pieces = [piece for _, piece in held]
-    tile = pieces[0].shape[0]
-    most = min(len(pieces), CHUNK)
+    arrays = [array for array, _ in held]
+    tile = arrays[0].shape[0] // len(held[0][1])
+    places = [(at, index, row) for index, (_, entries) in enumerate(held) for row, at in enumerate(entries)]
+    most = min(len(places), CHUNK)
     out_shape = [jax.ShapeDtypeStruct((rows, width), jnp.float32)]
     if first:
         out_shape.append(jax.ShapeDtypeStruct((2 * rows, width), jnp.bfloat16))
+    if packed:
+        out_shape.append(jax.ShapeDtypeStruct((len(packed) * tile, width), jnp.bfloat16))
     if last:
         out_shape.append(jax.ShapeDtypeStruct((loop_size, 128), jnp.float32))
     extra = [] if first else [before]
-    results = pl.pallas_call(
-        functools.partial(pieces_kernel, loop_size, [origin for origin, _ in held], first, last),
+    return pl.pallas_call(
+        functools.partial(pieces_kernel, places, [a.shape for a in arrays], packed, first, last),
         out_shape=out_shape,
-        in_specs=[pl.BlockSpec(memory_space=pltpu.SMEM)] * 2
-        + [pl.BlockSpec(memory_space=pltpu.VMEM)] * (2 + len(pieces) + len(extra)),
+        in_specs=[pl.BlockSpec(memory_space=pltpu.SMEM)]
+        + [pl.BlockSpec(memory_space=pltpu.VMEM)] * (2 + len(arrays) + len(extra)),
         out_specs=[pl.BlockSpec(memory_space=pltpu.VMEM)] * len(out_shape),
         scratch_shapes=[
             pltpu.VMEM((CHUNK * tile, width), jnp.bfloat16),
@@ -147,35 +190,54 @@
         ],
         compiler_params=pltpu.CompilerParams(vmem_limit_bytes=24 * 1024 * 1024),
         cost_estimate=pl.CostEstimate(
-            flops=8 * rows * width * most * tile,
+            flops=128 * rows * width * most * tile,
             bytes_accessed=8 * rows * width,
             transcendentals=rows * most * tile,
         ),
         name="add_pieces",
-    )(*lists, given, labels, *pieces, *extra)
-    return results if first or last else (results[0], given)
+    )(table, given, labels, *arrays, *extra)
 
 
 def ring_gradient(users, items, lists, labels):
     loop_size = lax.axis_size("loop")
     far = loop_size // 4
-    held = [[((0, 0), items), ((0, 1), to_other_core(items, loop_size))]]
+    origins = [(hops, 0) for hops in range(1 - far, far + 1)]
+    origins += [(-hops, 1) for hops, _ in origins]
+    table = slot_table(loop_size, origins, *lists)
+    where = {origin: at for at, origin in enumerate(origins)}
+
+    def held(hops, array):
+        return array, [where[hops, 0]]
+
+    def other(arrays, hops):
+        return to_other_core(arrays, loop_size), [where[-hop, 1] for hop in hops]
+
+    up = to_next(items, 1, loop_size)
+    down = to_next(items, -1, loop_size)
+    up, table = lax.optimization_barrier((up, table))
+    here, hops, early, late = [held(0, items), held(1, up), held(-1, down)], [0, 1, -1], [], []
     given, gradient = users, None
-    up = down = items
-    for hop in range(1, far + 1):
-        if hop > 2:
-            gradient, given = add_pieces(loop_size, held[hop - 3], lists, given, labels, gradient, False)
-            up, gradient = lax.optimization_barrier((up, gradient))
+    for hop in range(2, far + 1):
         up = to_next(up, 1, loop_size)
         if hop < far:
             down = to_next(down, -1, loop_size)
-            arrived = [((hop, 0), up), ((-hop, 0), down)]
-            arrived += [((-hop, 1), to_other_core(up, loop_size)), ((hop, 1), to_other_core(down, loop_size))]
-            held.append(arrived)
-    gradient, given = add_pieces(loop_size, held[far - 2], lists, given, labels, gradient, False)
-    up, gradient = lax.optimization_barrier((up, gradient))
-    last = held[far - 1] + [((far, 0), up), ((far, 1), to_other_core(up, loop_size))]
-    return add_pieces(loop_size, last, lists, given, labels, gradient, True)
+        if gradient is None:
+            gradient, given, pack = add_pieces(
+                here, [0, 1, 2], loop_size, table, given, labels, None, False
+            )
+        else:
+            gradient, pack = add_pieces(
+                here + early, [0, 1], loop_size, table, given, labels, gradient, False
+            )
+        up, gradient = lax.optimization_barrier((up, gradient))
+        early, late = late, [other(pack, hops)]
+        here, hops = [held(hop, up)], [hop, -hop]
+        if hop < far:
+            here.append(held(-hop, down))
+    final = other(up, [far])
+    (gradient,) = add_pieces(early, [], loop_size, table, given, labels, gradient, False)
+    final = here + late + [final]
+    return *add_pieces(final, [], loop_size, table, given, labels, gradient, True), users
 
 
 def chunks_kernel(
@@ -187,7 +249,7 @@
 
     @pl.when(step == 0)
     def _():
-        parts_ref[...] = halves(users_ref[...])
+        parts_ref[...] = halves(0.5 * users_ref[...])
         grad_ref[...] = jnp.zeros_like(grad_ref)
 
     def move(slot):
@@ -204,7 +266,7 @@
     def labels_at(position):
         return labels_ref[:, pl.ds(pl.multiple_of(position * tile, tile), tile)]
 
-    add_tiles(grad_ref, parts_ref, tiles, live, labels_at)
+    add_tiles(grad_ref, parts_ref, tiles, live, CHUNK, labels_at)
 
     @pl.when(step == pl.num_programs(0) - 1)
     def _():
@@ -261,7 +323,7 @@
     slots = tile_blocks.shape[1]
     lists = (tile_blocks, tile_count)
     if loop_size <= RING_LIMIT and loop_size % 8 == 0 and slots <= CHUNK:
-        gradient, square = ring_gradient(users, items, lists, labels)
+        gradient, square, users = ring_gradient(users, items, lists, labels)
     else:
         whole = lax.all_gather(items, "loop", axis=0, tiled=True)
         gradient, square = add_chunks(loop_size, whole, lists, users, labels)

time: 42.2 us -> 39.2 us (0.929)
  waiting for transfers between devices: 7.38 us -> 10 us
  starting transfers between devices: 11 us -> 8.4 us
  local copies, waits for them, and re-layouts: 3.17 us -> 0.67 us
  blocking collectives: 11.8 us -> 10.2 us
  Pallas kernels: 7.76 us -> 8.92 us
    ppermute x7, waiting for transfers between devices: 6.02 us -> 10 us  [to_next(): return lax.ppermute(array, 'loop', pairs)]
    unnamed x10, local copies, waits for them, and re-layouts: 3.17 us -> 0.67 us
    ppermute x7, starting transfers between devices: 9.54 us -> 7.75 us  [to_next(): return lax.ppermute(array, 'loop', pairs)]
    all_to_all x1, blocking collectives: 11.8 us -> 10.2 us  [local(): squares = lax.all_to_all(square, 'loop', 0, 0, tiled=True)]
    ppermute x8 -> x4, waiting for transfers between devices: 1.35 us -> 0.01 us  [to_other_core(): lax.ppermute(array, 'loop', [(at, at ^ 1) for at in range(loop_size)])]
    pallas_call x4 -> x6, Pallas kernels: 6.78 us -> 7.95 us  [the longest x5 6.49 us: add_pieces(): pl.pallas_call(functools.partial(pieces_kernel, places, [a.shape for a in...]
    ppermute x8 -> x4, starting transfers between devices: 1.44 us -> 0.65 us  [to_other_core(): lax.ppermute(array, 'loop', [(at, at ^ 1) for at in range(loop_size)])]
  transfers between devices with their start and end apart: 15 -> 11, of which waited for: 5 -> 4; matrix products, arithmetic and copies ran while one was open for 0% -> 0% of each run, Pallas kernels for 11% -> 17%
where the time goes in v5:
time: 39.2 us; the launch traced here: 39 us
  blocking collectives  10.2 us (26%)
  waiting for transfers between devices  10 us (26%)
  Pallas kernels  8.92 us (23%)
  starting transfers between devices  8.4 us (21%)
  between operations  0.77 us (2%)
  local copies, waits for them, and re-layouts  0.67 us (2%)
    all_to_all x1, blocking collectives, local(): squares = lax.all_to_all(square, 'loop', 0, 0, tiled=True)  10.2 us
    ppermute x7, waiting for transfers between devices, to_next(): return lax.ppermute(array, 'loop', pairs)  10 us
    ppermute x7, starting transfers between devices, to_next(): return lax.ppermute(array, 'loop', pairs)  7.75 us
    pallas_call x5, Pallas kernels, add_pieces(): pl.pallas_call(functools.partial(pieces_kernel, places, [a.shape for a in...  6.49 us
    pallas_call x1, Pallas kernels, slot_table(): pl.pallas_call(functools.partial(table_kernel, loop_size, origins), out_s...  1.46 us
    pallas_call x1, Pallas kernels, local(): pl.pallas_call(functools.partial(update_kernel, rows * loop_size * width)...  0.97 us
  transfers between devices with their start and end apart: 11, of which 4 were waited for; matrix products, arithmetic and copies ran while one was open for 0% of the time, Pallas kernels for 17%

profile of v5, /device:TPU:0, one launch (start us, length us, event | category | flops | bytes accessed | tf_op | source)
XLA Modules:
  0.0 39.0 jit_solution(13886688565707693937)
XLA Ops:
  0.0 3.0 %collective-permute-start = (bf16[128,512]{1,0:T(8,128)(2,1)}, bf16[128,512]{1,0:T(8,128)(2,1)S(1)}, u32[]{:S(2)}, u32[]{:S(2)}) collective-permute-start(bf16[128,512]{1,0:T(8,128)(2,1)} %rest_0_.1), channel_id=1, source_target_pairs={{0,4},{4,8},{8,12},{12,14},{14,10},{10,6},{6,2},{2,0},{1,3},{5,1},... | collective-permute-start | bytes 393224 | tf_op jit(solution)/shard_map/ppermute | solution.py:29
  3.0 0.0 collective-permute-start.1
  3.7 0.0 copy-start
  3.7 0.0 copy-start.1
  3.7 0.0 copy-start.2
  3.7 1.5 %slot_table.1.table_ref = s32[16]{0:T(128)} custom-call(s32[1,8]{1,0:T(1,128)} %list_ref.1, s32[1]{0:T(128)S(6)} %copy.7.count_ref), custom_call_target="tpu_custom_call" | custom-call | flops 4294967296 | bytes 1024 | tf_op jit(solution)/shard_map/slot_table/pallas_call | solution.py:54
  5.2 1.8 %collective-permute-done.rest_1_ = bf16[128,512]{1,0:T(8,128)(2,1)S(1)} collective-permute-done((bf16[128,512]{1,0:T(8,128)(2,1)}, bf16[128,512]{1,0:T(8,128)(2,1)S(1)}, u32[]{:S(2)}, u32[]{:S(2)}) %collective-permute-start) | collective-permute-done | bytes 131104 | tf_op jit(solution)/shard_map/ppermute | solution.py:29
  7.0 1.5 %collective-permute-start.2 = (bf16[128,512]{1,0:T(8,128)(2,1)S(1)}, bf16[128,512]{1,0:T(8,128)(2,1)S(1)}, u32[]{:S(2)}, u32[]{:S(2)}) collective-permute-start(bf16[128,512]{1,0:T(8,128)(2,1)S(1)} %collective-permute-done.rest_1_), channel_id=1, source_target_pairs={{0,4},{4,8},{8,12},{12,14},{14,10},{10,6},{6,2},{2,0},{1,3},{5,1},... | collective-permute-start | bytes 393224 | tf_op jit(solution)/shard_map/ppermute | solution.py:29
  8.5 0.0 collective-permute-done.1.rest_2_
  8.5 0.9 %collective-permute-start.4 = (bf16[128,512]{1,0:T(8,128)(2,1)S(1)}, bf16[128,512]{1,0:T(8,128)(2,1)S(1)}, u32[]{:S(2)}, u32[]{:S(2)}) collective-permute-start(bf16[128,512]{1,0:T(8,128)(2,1)S(1)} %collective-permute-done.1.rest_2_), channel_id=1, source_target_pairs={{0,2},{4,0},{8,4},{12,8},{14,12},{10,14},{6,10},{2,6},{1,5},{5,9},... | collective-permute-start | bytes 393224 | tf_op jit(solution)/shard_map/ppermute | solution.py:29
  9.4 0.0 copy-done
  9.4 0.0 copy-done.1
  9.4 0.0 copy-done.2
  9.4 0.0 copy-start.3
  9.4 0.6 %copy-done.3 = s32[16]{0:T(128)S(1)} copy-done((s32[16]{0:T(128)S(1)}, s32[16]{0:T(128)}, u32[]{:S(2)}) %copy-start.3) | copy-done | bytes 88
  10.1 0.8 %add_pieces.5 = (f32[256,512]{1,0:T(8,128)S(1)}, bf16[512,512]{1,0:T(8,128)(2,1)S(1)}, bf16[384,512]{1,0:T(8,128)(2,1)S(1)}) custom-call(s32[16]{0:T(128)S(1)} %copy-done.3, f32[256,512]{1,0:T(8,128)S(1)} %copy-done, s32[256,1024]{1,0:T(8,128)S(1)} %copy-done.1, bf16[128,512]{1,0:T(8,128)(2,1)S(1)} %copy-done.2, ...), custom_call_target="tpu_custom_call" | custom-call | flops 6442450944 | bytes 1048576 | tf_op jit(solution)/shard_map/add_pieces/pallas_call | solution.py:181
  10.8 0.1 collective-permute-start.7
  10.9 2.2 %collective-permute-done.2.rest_0_ = bf16[128,512]{1,0:T(8,128)(2,1)S(1)} collective-permute-done((bf16[128,512]{1,0:T(8,128)(2,1)S(1)}, bf16[128,512]{1,0:T(8,128)(2,1)S(1)}, u32[]{:S(2)}, u32[]{:S(2)}) %collective-permute-start.2) | collective-permute-done | bytes 131104 | tf_op jit(solution)/shard_map/ppermute | solution.py:29
  13.2 0.0 copy-start.4
  13.2 0.3 collective-permute-start.3
  13.5 0.0 collective-permute-done.4.rest_1_
  13.5 1.7 %collective-permute-start.6 = (bf16[128,512]{1,0:T(8,128)(2,1)S(1)}, bf16[128,512]{1,0:T(8,128)(2,1)S(1)}, u32[]{:S(2)}, u32[]{:S(2)}) collective-permute-start(bf16[128,512]{1,0:T(8,128)(2,1)S(1)} %collective-permute-done.4.rest_1_), channel_id=1, source_target_pairs={{0,2},{4,0},{8,4},{12,8},{14,12},{10,14},{6,10},{2,6},{1,5},{5,9},... | collective-permute-start | bytes 393224 | tf_op jit(solution)/shard_map/ppermute | solution.py:29
  15.2 0.0 copy-done.4
  15.2 1.4 %add_pieces.6 = (f32[256,512]{1,0:T(8,128)S(1)}, bf16[256,512]{1,0:T(8,128)(2,1)S(1)}) custom-call(s32[16]{0:T(128)S(1)} %copy-done.4, bf16[512,512]{1,0:T(8,128)(2,1)S(1)} %get-tuple-element.24.given_ref, s32[256,1024]{1,0:T(8,128)S(1)} %copy-done.1, bf16[128,512]{1,0:T(8,128)(2,1)S(1)} %collective-permute-done.2.rest_0_, ...), custom_call_target="tpu_custom_call" | custom-call | flops 4294967296 | bytes 1048576 | tf_op jit(solution)/shard_map/add_pieces/pallas_call | solution.py:181
  16.6 0.1 collective-permute-start.10
  16.7 2.7 %collective-permute-done.3.rest_0_ = bf16[128,512]{1,0:T(8,128)(2,1)S(1)} collective-permute-done((bf16[128,512]{1,0:T(8,128)(2,1)S(1)}, bf16[128,512]{1,0:T(8,128)(2,1)S(1)}, u32[]{:S(2)}, u32[]{:S(2)}) %collective-permute-start.3) | collective-permute-done | bytes 131104 | tf_op jit(solution)/shard_map/ppermute | solution.py:29
  19.4 0.3 collective-permute-start.5
  19.7 0.0 collective-permute-done.6.rest_1_
  19.7 0.0 collective-permute-done.7.rest_2_
  19.7 1.4 %add_pieces.7 = (f32[256,512]{1,0:T(8,128)S(1)}, bf16[256,512]{1,0:T(8,128)(2,1)S(1)}) custom-call(s32[16]{0:T(128)S(1)} %copy-done.4, bf16[512,512]{1,0:T(8,128)(2,1)S(1)} %get-tuple-element.24.given_ref, s32[256,1024]{1,0:T(8,128)S(1)} %copy-done.1, bf16[128,512]{1,0:T(8,128)(2,1)S(1)} %collective-permute-done.3.rest_0_, ...), custom_call_target="tpu_custom_call" | custom-call | flops 10737418240 | bytes 1048576 | tf_op jit(solution)/shard_map/add_pieces/pallas_call | solution.py:181
  21.2 3.2 %collective-permute-done.5.rest_0_ = bf16[128,512]{1,0:T(8,128)(2,1)S(1)} collective-permute-done((bf16[128,512]{1,0:T(8,128)(2,1)S(1)}, bf16[128,512]{1,0:T(8,128)(2,1)S(1)}, u32[]{:S(2)}, u32[]{:S(2)}) %collective-permute-start.5) | collective-permute-done | bytes 131104 | tf_op jit(solution)/shard_map/ppermute | solution.py:29
  24.4 0.0 collective-permute-start.8
  24.4 0.5 %collective-permute-start.9 = (bf16[128,512]{1,0:T(8,128)(2,1)S(1)}, bf16[128,512]{1,0:T(8,128)(2,1)S(1)}, u32[]{:S(2)}, u32[]{:S(2)}) collective-permute-start(bf16[128,512]{1,0:T(8,128)(2,1)S(1)} %collective-permute-done.5.rest_0_), channel_id=1, source_target_pairs={{0,1},{1,0},{2,3},{3,2},{4,5},{5,4},{6,7},{7,6},{8,9},{9,8},{10,11... | collective-permute-start | bytes 393224 | tf_op jit(solution)/shard_map/ppermute | solution.py:33
  24.9 0.0 collective-permute-done.10.rest_0_
  24.9 1.4 %add_pieces.8.rest_3_ = f32[256,512]{1,0:T(8,128)S(1)} custom-call(s32[16]{0:T(128)S(1)} %copy-done.4, bf16[512,512]{1,0:T(8,128)(2,1)S(1)} %get-tuple-element.24.given_ref, s32[256,1024]{1,0:T(8,128)S(1)} %copy-done.1, bf16[256,512]{1,0:T(8,128)(2,1)S(1)} %collective-permute-done.10.rest_0_, f32[256,512]{1,0:T(8,128)S(1)} %get-tuple-element.36.rest_1_), custom_call_target="tpu_custom_call" | custom-call | flops 4294967296 | bytes 1048576 | tf_op jit(solution)/shard_map/add_pieces/pallas_call | solution.py:181
  26.3 0.0 collective-permute-done.9.rest_2_
  26.3 0.0 collective-permute-done.8.rest_1_
  26.3 1.5 %add_pieces.9 = (f32[256,512]{1,0:T(8,128)S(1)}, f32[16,128]{1,0:T(8,128)S(1)}) custom-call(s32[16]{0:T(128)S(1)} %copy-done.4, bf16[512,512]{1,0:T(8,128)(2,1)S(1)} %get-tuple-element.24.given_ref, s32[256,1024]{1,0:T(8,128)S(1)} %copy-done.1, bf16[128,512]{1,0:T(8,128)(2,1)S(1)} %collective-permute-done.5.rest_0_, ...), custom_call_target="tpu_custom_call" | custom-call | flops 8589934592 | bytes 1048576 | tf_op jit(solution)/shard_map/add_pieces/pallas_call | solution.py:181
  27.8 10.2 %all_to_all.11 = f32[16,1,128]{2,1,0:T(1,128)S(1)} all-to-all(f32[16,1,128]{2,1,0:T(1,128)S(1)} %bitcast.5), channel_id=1, replica_groups=mesh['group'=2,'loop'=16] {'loop'}, dimensions={0} | all-to-all | bytes 16384 | tf_op jit(solution)/shard_map/all_to_all | solution.py:331
  38.0 1.0 %update.1 = f32[256,512]{1,0:T(8,128)} custom-call(f32[256,512]{1,0:T(8,128)S(1)} %copy-done, f32[256,512]{1,0:T(8,128)S(1)} %get-tuple-element.37.grad_ref, f32[16,128]{1,0:T(8,128)S(1)} %bitcast.4), custom_call_target="tpu_custom_call" | custom-call | flops 262144 | bytes 1572864 | tf_op jit(solution)/shard_map/update/pallas_call | solution.py:332
Async XLA Ops:
  0.0 7.0 %collective-permute-start = (bf16[128,512]{1,0:T(8,128)(2,1)}, bf16[128,512]{1,0:T(8,128)(2,1)S(1)}, u32[]{:S(2)}, u32[]{:S(2)}) collective-permute-start(bf16[128,512]{1,0:T(8,128)(2,1)} %rest_0_.1), channel_id=1, source_target_pairs={{0,4},{4,8},{8,12},{12,14},{14,10},{10,6},{6,2},{2,0},{1,3},{5,1},... | collective-permute-start | bytes 393224 | tf_op jit(solution)/shard_map/ppermute | solution.py:29
  3.0 5.5 %collective-permute-start.1 = (bf16[128,512]{1,0:T(8,128)(2,1)}, bf16[128,512]{1,0:T(8,128)(2,1)S(1)}, u32[]{:S(2)}, u32[]{:S(2)}) collective-permute-start(bf16[128,512]{1,0:T(8,128)(2,1)} %rest_0_.1), channel_id=1, source_target_pairs={{0,2},{4,0},{8,4},{12,8},{14,12},{10,14},{6,10},{2,6},{1,5},{5,9},... | collective-permute-start | bytes 393224 | tf_op jit(solution)/shard_map/ppermute | solution.py:29
  3.7 5.7 %copy-start = (f32[256,512]{1,0:T(8,128)S(1)}, f32[256,512]{1,0:T(8,128)}, u32[]{:S(2)}) copy-start(f32[256,512]{1,0:T(8,128)} %users_ref.1) | copy-start | bytes 1572868
  3.7 5.7 %copy-start.1 = (s32[256,1024]{1,0:T(8,128)S(1)}, s32[256,1024]{1,0:T(8,128)}, u32[]{:S(2)}) copy-start(s32[256,1024]{1,0:T(8,128)} %labels_ref.9) | copy-start | bytes 3145732
  3.7 5.7 %copy-start.2 = (bf16[128,512]{1,0:T(8,128)(2,1)S(1)}, bf16[128,512]{1,0:T(8,128)(2,1)}, u32[]{:S(2)}) copy-start(bf16[128,512]{1,0:T(8,128)(2,1)} %rest_0_.1) | copy-start | bytes 393220
  7.0 6.2 %collective-permute-start.2 = (bf16[128,512]{1,0:T(8,128)(2,1)S(1)}, bf16[128,512]{1,0:T(8,128)(2,1)S(1)}, u32[]{:S(2)}, u32[]{:S(2)}) collective-permute-start(bf16[128,512]{1,0:T(8,128)(2,1)S(1)} %collective-permute-done.rest_1_), channel_id=1, source_target_pairs={{0,4},{4,8},{8,12},{12,14},{14,10},{10,6},{6,2},{2,0},{1,3},{5,1},... | collective-permute-start | bytes 393224 | tf_op jit(solution)/shard_map/ppermute | solution.py:29
  8.5 5.0 %collective-permute-start.4 = (bf16[128,512]{1,0:T(8,128)(2,1)S(1)}, bf16[128,512]{1,0:T(8,128)(2,1)S(1)}, u32[]{:S(2)}, u32[]{:S(2)}) collective-permute-start(bf16[128,512]{1,0:T(8,128)(2,1)S(1)} %collective-permute-done.1.rest_2_), channel_id=1, source_target_pairs={{0,2},{4,0},{8,4},{12,8},{14,12},{10,14},{6,10},{2,6},{1,5},{5,9},... | collective-permute-start | bytes 393224 | tf_op jit(solution)/shard_map/ppermute | solution.py:29
  9.4 0.7 %copy-start.3 = (s32[16]{0:T(128)S(1)}, s32[16]{0:T(128)}, u32[]{:S(2)}) copy-start(s32[16]{0:T(128)} %slot_table.1.table_ref) | copy-start | bytes 196
  10.8 8.9 %collective-permute-start.7 = (bf16[384,512]{1,0:T(8,128)(2,1)S(1)}, bf16[384,512]{1,0:T(8,128)(2,1)S(1)}, u32[]{:S(2)}, u32[]{:S(2)}) collective-permute-start(bf16[384,512]{1,0:T(8,128)(2,1)S(1)} %get-tuple-element.30), channel_id=1, source_target_pairs={{0,1},{1,0},{2,3},{3,2},{4,5},{5,4},{6,7},{7,6},{8,9},{9,8},{10,11... | collective-permute-start | bytes 1179656 | tf_op jit(solution)/shard_map/ppermute | solution.py:33
  13.2 2.0 %copy-start.4 = (s32[16]{0:T(128)S(1)}, s32[16]{0:T(128)}, u32[]{:S(2)}) copy-start(s32[16]{0:T(128)} %slot_table.1.table_ref) | copy-start | bytes 196
  13.2 6.3 %collective-permute-start.3 = (bf16[128,512]{1,0:T(8,128)(2,1)S(1)}, bf16[128,512]{1,0:T(8,128)(2,1)S(1)}, u32[]{:S(2)}, u32[]{:S(2)}) collective-permute-start(bf16[128,512]{1,0:T(8,128)(2,1)S(1)} %collective-permute-done.2.rest_0_), channel_id=1, source_target_pairs={{0,4},{4,8},{8,12},{12,14},{14,10},{10,6},{6,2},{2,0},{1,3},{5,1},... | collective-permute-start | bytes 393224 | tf_op jit(solution)/shard_map/ppermute | solution.py:29
  13.5 6.2 %collective-permute-start.6 = (bf16[128,512]{1,0:T(8,128)(2,1)S(1)}, bf16[128,512]{1,0:T(8,128)(2,1)S(1)}, u32[]{:S(2)}, u32[]{:S(2)}) collective-permute-start(bf16[128,512]{1,0:T(8,128)(2,1)S(1)} %collective-permute-done.4.rest_1_), channel_id=1, source_target_pairs={{0,2},{4,0},{8,4},{12,8},{14,12},{10,14},{6,10},{2,6},{1,5},{5,9},... | collective-permute-start | bytes 393224 | tf_op jit(solution)/shard_map/ppermute | solution.py:29
  16.6 8.3 %collective-permute-start.10 = (bf16[256,512]{1,0:T(8,128)(2,1)S(1)}, bf16[256,512]{1,0:T(8,128)(2,1)S(1)}, u32[]{:S(2)}, u32[]{:S(2)}) collective-permute-start(bf16[256,512]{1,0:T(8,128)(2,1)S(1)} %get-tuple-element.35), channel_id=1, source_target_pairs={{0,1},{1,0},{2,3},{3,2},{4,5},{5,4},{6,7},{7,6},{8,9},{9,8},{10,11... | collective-permute-start | bytes 786440 | tf_op jit(solution)/shard_map/ppermute | solution.py:33
  19.4 5.0 %collective-permute-start.5 = (bf16[128,512]{1,0:T(8,128)(2,1)S(1)}, bf16[128,512]{1,0:T(8,128)(2,1)S(1)}, u32[]{:S(2)}, u32[]{:S(2)}) collective-permute-start(bf16[128,512]{1,0:T(8,128)(2,1)S(1)} %collective-permute-done.3.rest_0_), channel_id=1, source_target_pairs={{0,4},{4,8},{8,12},{12,14},{14,10},{10,6},{6,2},{2,0},{1,3},{5,1},... | collective-permute-start | bytes 393224 | tf_op jit(solution)/shard_map/ppermute | solution.py:29
  24.4 1.9 %collective-permute-start.8 = (bf16[256,512]{1,0:T(8,128)(2,1)S(1)}, bf16[256,512]{1,0:T(8,128)(2,1)S(1)}, u32[]{:S(2)}, u32[]{:S(2)}) collective-permute-start(bf16[256,512]{1,0:T(8,128)(2,1)S(1)} %get-tuple-element.34), channel_id=1, source_target_pairs={{0,1},{1,0},{2,3},{3,2},{4,5},{5,4},{6,7},{7,6},{8,9},{9,8},{10,11... | collective-permute-start | bytes 786440 | tf_op jit(solution)/shard_map/ppermute | solution.py:33
  24.4 1.9 %collective-permute-start.9 = (bf16[128,512]{1,0:T(8,128)(2,1)S(1)}, bf16[128,512]{1,0:T(8,128)(2,1)S(1)}, u32[]{:S(2)}, u32[]{:S(2)}) collective-permute-start(bf16[128,512]{1,0:T(8,128)(2,1)S(1)} %collective-permute-done.5.rest_0_), channel_id=1, source_target_pairs={{0,1},{1,0},{2,3},{3,2},{4,5},{5,4},{6,7},{7,6},{8,9},{9,8},{10,11... | collective-permute-start | bytes 393224 | tf_op jit(solution)/shard_map/ppermute | solution.py:33

commit v6 on v5

--- a/solution.py
+++ b/solution.py
@@ -8,7 +8,7 @@
 from jax.sharding import PartitionSpec as P
 
 CHUNK = 8
-RING_LIMIT = 16
+RING = 16
 
 
 def ring_place(loop_size):
@@ -26,6 +26,16 @@
     chips, device = ring_place(loop_size)
     pairs = [(device(at, 0), device(at + direction, 0)) for at in range(chips)]
     pairs += [(device(at, 1), device(at - direction, 1)) for at in range(chips)]
+    return lax.ppermute(array, "loop", pairs)
+
+
+def across(array, loop_size):
+    chips, device = ring_place(loop_size)
+    pairs = [
+        (device(at, core), device(at + (3 if at % 2 == 0 else -3), core))
+        for at in range(chips)
+        for core in range(2)
+    ]
     return lax.ppermute(array, "loop", pairs)
 
 
@@ -113,23 +123,29 @@
     square_ref[...] = jnp.broadcast_to(square, square_ref.shape)
 
 
+def core_and_position(loop_size):
+    me = lax.axis_index("loop")
+    core, row, outer = me % 2, me // 2 % 2, me // 4
+    return core, jnp.where(row == 0, outer, loop_size // 2 - 1 - outer)
+
+
 def origin_block(origin, loop_size):
     hops, other = origin
     chips = loop_size // 2
-    me = lax.axis_index("loop")
-    core, row, outer = me % 2, me // 2 % 2, me // 4
-    position = jnp.where(row == 0, outer, chips - 1 - outer)
+    core, position = core_and_position(loop_size)
     at = lax.rem(position + chips + jnp.where(core == 0, -hops, hops), chips)
     chip = jnp.where(at < chips // 2, 2 * at, 2 * (chips - 1 - at) + 1)
     return 2 * chip + (1 - core if other else core)
 
 
-def pieces_kernel(places, sizes, packed, first, last, table_ref, given_ref, labels_ref, *rest):
+def pieces_kernel(places, count, packed, loop_size, first, last, table_ref, given_ref, labels_ref, *rest):
     rest = list(rest)
-    arrays = [rest.pop(0) for _ in sizes]
-    before_ref = None if first else rest.pop(0)
+    arrays = [rest.pop(0) for _ in range(count)]
+    if not first:
+        rest.pop(0)
     grad_ref = rest.pop(0)
     parts_ref = rest.pop(0) if first else given_ref
+    across_ref = rest.pop(0) if first else None
     pack_ref = rest.pop(0) if packed else None
     square_ref = rest.pop(0) if last else None
     tiles, slots = rest
@@ -137,10 +153,15 @@
     for at, index in enumerate(packed):
         pack_ref[at * tile : (at + 1) * tile, :] = arrays[index][...]
     if first:
+        core, position = core_and_position(loop_size)
+        for at in range(2):
+
+            @pl.when((core + position) % 2 == at)
+            def _():
+                across_ref[...] = arrays[1 + at][...]
+
         parts_ref[...] = halves(0.5 * given_ref[...])
         grad_ref[...] = jnp.zeros_like(grad_ref)
-    else:
-        grad_ref[...] = before_ref[...]
     live = jnp.int32(0)
     for at, index, row in places:
         found = table_ref[at]
@@ -167,23 +188,25 @@
     width = given.shape[1]
     rows = given.shape[0] // (1 if first else 2)
     arrays = [array for array, _ in held]
-    tile = arrays[0].shape[0] // len(held[0][1])
+    tile = labels.shape[1] // CHUNK
     places = [(at, index, row) for index, (_, entries) in enumerate(held) for row, at in enumerate(entries)]
     most = min(len(places), CHUNK)
     out_shape = [jax.ShapeDtypeStruct((rows, width), jnp.float32)]
     if first:
         out_shape.append(jax.ShapeDtypeStruct((2 * rows, width), jnp.bfloat16))
+        out_shape.append(jax.ShapeDtypeStruct((tile, width), jnp.bfloat16))
     if packed:
         out_shape.append(jax.ShapeDtypeStruct((len(packed) * tile, width), jnp.bfloat16))
     if last:
         out_shape.append(jax.ShapeDtypeStruct((loop_size, 128), jnp.float32))
     extra = [] if first else [before]
     return pl.pallas_call(
-        functools.partial(pieces_kernel, places, [a.shape for a in arrays], packed, first, last),
+        functools.partial(pieces_kernel, places, len(arrays), packed, loop_size, first, last),
         out_shape=out_shape,
         in_specs=[pl.BlockSpec(memory_space=pltpu.SMEM)]
         + [pl.BlockSpec(memory_space=pltpu.VMEM)] * (2 + len(arrays) + len(extra)),
         out_specs=[pl.BlockSpec(memory_space=pltpu.VMEM)] * len(out_shape),
+        input_output_aliases={} if first else {3 + len(arrays): 0},
         scratch_shapes=[
             pltpu.VMEM((CHUNK * tile, width), jnp.bfloat16),
             pltpu.SMEM((CHUNK + 1,), jnp.int32),
@@ -215,29 +238,21 @@
     up = to_next(items, 1, loop_size)
     down = to_next(items, -1, loop_size)
     up, table = lax.optimization_barrier((up, table))
-    here, hops, early, late = [held(0, items), held(1, up), held(-1, down)], [0, 1, -1], [], []
-    given, gradient = users, None
-    for hop in range(2, far + 1):
-        up = to_next(up, 1, loop_size)
-        if hop < far:
-            down = to_next(down, -1, loop_size)
-        if gradient is None:
-            gradient, given, pack = add_pieces(
-                here, [0, 1, 2], loop_size, table, given, labels, None, False
-            )
-        else:
-            gradient, pack = add_pieces(
-                here + early, [0, 1], loop_size, table, given, labels, gradient, False
-            )
-        up, gradient = lax.optimization_barrier((up, gradient))
-        early, late = late, [other(pack, hops)]
-        here, hops = [held(hop, up)], [hop, -hop]
-        if hop < far:
-            here.append(held(-hop, down))
-    final = other(up, [far])
-    (gradient,) = add_pieces(early, [], loop_size, table, given, labels, gradient, False)
-    final = here + late + [final]
-    return *add_pieces(final, [], loop_size, table, given, labels, gradient, True), users
+    first = [held(0, items), held(1, up), held(-1, down)]
+    second = [held(2, to_next(up, 1, loop_size)), held(-2, to_next(down, -1, loop_size))]
+    gradient, parts, opposite, pack = add_pieces(
+        first, [0, 1, 2], loop_size, table, users, labels, None, False
+    )
+    opposite = across(opposite, loop_size)
+    first = other(pack, [0, 1, -1])
+    third = [held(3, to_next(second[0][0], 1, loop_size)), held(-3, to_next(second[1][0], -1, loop_size))]
+    gradient, pack = add_pieces(second, [0, 1], loop_size, table, parts, labels, gradient, False)
+    second = other(pack, [2, -2])
+    third.append(held(4, opposite))
+    gradient, pack = add_pieces(third, [0, 1, 2], loop_size, table, parts, labels, gradient, False)
+    third = other(pack, [3, -3, 4])
+    (gradient,) = add_pieces([first, second], [], loop_size, table, parts, labels, gradient, False)
+    return *add_pieces([third], [], loop_size, table, parts, labels, gradient, True), users
 
 
 def chunks_kernel(
@@ -322,7 +337,7 @@
     rows, width = users.shape
     slots = tile_blocks.shape[1]
     lists = (tile_blocks, tile_count)
-    if loop_size <= RING_LIMIT and loop_size % 8 == 0 and slots <= CHUNK:
+    if loop_size == RING and slots == CHUNK:
         gradient, square, users = ring_gradient(users, items, lists, labels)
     else:
         whole = lax.all_gather(items, "loop", axis=0, tiled=True)

time: 39.2 us -> 37.4 us (0.954)
  waiting for transfers between devices: 10 us -> 4.81 us
  starting transfers between devices: 8.4 us -> 13.1 us
  Pallas kernels: 8.92 us -> 6.45 us
  blocking collectives: 10.2 us -> 11.8 us
    ppermute x7 -> x6, waiting for transfers between devices: 10 us -> 4.33 us  [to_next(): return lax.ppermute(array, 'loop', pairs)]
    ppermute x0 -> x1, starting transfers between devices: none -> 3.37 us  [across(): return lax.ppermute(array, 'loop', pairs)]
    pallas_call x5, Pallas kernels: 6.49 us -> 4.02 us  [add_pieces(): pl.pallas_call(functools.partial(pieces_kernel, places, len(arrays), pack...]
    all_to_all x1, blocking collectives: 10.2 us -> 11.8 us  [local(): squares = lax.all_to_all(square, 'loop', 0, 0, tiled=True)]
    ppermute x4 -> x3, starting transfers between devices: 0.65 us -> 1.87 us  [to_other_core(): lax.ppermute(array, 'loop', [(at, at ^ 1) for at in range(loop_size)])]
    ppermute x0 -> x1, waiting for transfers between devices: none -> 0.47 us  [across(): return lax.ppermute(array, 'loop', pairs)]
    ppermute x7 -> x6, starting transfers between devices: 7.75 us -> 7.88 us  [to_next(): return lax.ppermute(array, 'loop', pairs)]
  transfers between devices with their start and end apart: 11 -> 10, of which waited for: 4 -> 4; matrix products, arithmetic and copies ran while one was open for 0% -> 0% of each run, Pallas kernels for 17% -> 13%
where the time goes in v6:
time: 37.4 us; the launch traced here: 37.5 us
  starting transfers between devices  13.1 us (35%)
  blocking collectives  11.8 us (32%)
  Pallas kernels  6.45 us (17%)
  waiting for transfers between devices  4.81 us (13%)
  between operations  0.75 us (2%)
  local copies, waits for them, and re-layouts  0.66 us (2%)
    all_to_all x1, blocking collectives, local(): squares = lax.all_to_all(square, 'loop', 0, 0, tiled=True)  11.8 us
    ppermute x6, starting transfers between devices, to_next(): return lax.ppermute(array, 'loop', pairs)  7.88 us
    ppermute x6, waiting for transfers between devices, to_next(): return lax.ppermute(array, 'loop', pairs)  4.33 us
    pallas_call x5, Pallas kernels, add_pieces(): pl.pallas_call(functools.partial(pieces_kernel, places, len(arrays), pack...  4.02 us
    ppermute x1, starting transfers between devices, across(): return lax.ppermute(array, 'loop', pairs)  3.37 us
    ppermute x3, starting transfers between devices, to_other_core(): lax.ppermute(array, 'loop', [(at, at ^ 1) for at in range(loop_size)])  1.87 us
    pallas_call x1, Pallas kernels, slot_table(): pl.pallas_call(functools.partial(table_kernel, loop_size, origins), out_s...  1.46 us
    pallas_call x1, Pallas kernels, local(): pl.pallas_call(functools.partial(update_kernel, rows * loop_size * width)...  0.97 us
  transfers between devices with their start and end apart: 10, of which 4 were waited for; matrix products, arithmetic and copies ran while one was open for 0% of the time, Pallas kernels for 13%

profile of v6, /device:TPU:0, one launch (start us, length us, event | category | flops | bytes accessed | tf_op | source)
XLA Modules:
  0.0 37.5 jit_solution(11360500059781800964)
XLA Ops:
  0.0 3.0 %collective-permute-start = (bf16[128,512]{1,0:T(8,128)(2,1)}, bf16[128,512]{1,0:T(8,128)(2,1)S(1)}, u32[]{:S(2)}, u32[]{:S(2)}) collective-permute-start(bf16[128,512]{1,0:T(8,128)(2,1)} %rest_0_.1), channel_id=1, source_target_pairs={{0,4},{4,8},{8,12},{12,14},{14,10},{10,6},{6,2},{2,0},{1,3},{5,1},... | collective-permute-start | bytes 393224 | tf_op jit(solution)/shard_map/ppermute | solution.py:29
  3.0 0.0 collective-permute-start.1
  3.7 0.0 copy-start
  3.7 0.0 copy-start.1
  3.7 0.0 copy-start.2
  3.7 1.5 %slot_table.1.table_ref = s32[16]{0:T(128)} custom-call(s32[1,8]{1,0:T(1,128)} %list_ref.1, s32[1]{0:T(128)S(6)} %copy.15.count_ref), custom_call_target="tpu_custom_call" | custom-call | flops 4294967296 | bytes 1024 | tf_op jit(solution)/shard_map/slot_table/pallas_call | solution.py:64
  5.2 1.8 %collective-permute-done.rest_1_ = bf16[128,512]{1,0:T(8,128)(2,1)S(1)} collective-permute-done((bf16[128,512]{1,0:T(8,128)(2,1)}, bf16[128,512]{1,0:T(8,128)(2,1)S(1)}, u32[]{:S(2)}, u32[]{:S(2)}) %collective-permute-start) | collective-permute-done | bytes 131104 | tf_op jit(solution)/shard_map/ppermute | solution.py:29
  7.0 1.5 %collective-permute-start.2 = (bf16[128,512]{1,0:T(8,128)(2,1)S(1)}, bf16[128,512]{1,0:T(8,128)(2,1)S(1)}, u32[]{:S(2)}, u32[]{:S(2)}) collective-permute-start(bf16[128,512]{1,0:T(8,128)(2,1)S(1)} %collective-permute-done.rest_1_), channel_id=1, source_target_pairs={{0,4},{4,8},{8,12},{12,14},{14,10},{10,6},{6,2},{2,0},{1,3},{5,1},... | collective-permute-start | bytes 393224 | tf_op jit(solution)/shard_map/ppermute | solution.py:29
  8.5 0.0 collective-permute-done.1.rest_2_
  8.5 0.9 %collective-permute-start.4 = (bf16[128,512]{1,0:T(8,128)(2,1)S(1)}, bf16[128,512]{1,0:T(8,128)(2,1)S(1)}, u32[]{:S(2)}, u32[]{:S(2)}) collective-permute-start(bf16[128,512]{1,0:T(8,128)(2,1)S(1)} %collective-permute-done.1.rest_2_), channel_id=1, source_target_pairs={{0,2},{4,0},{8,4},{12,8},{14,12},{10,14},{6,10},{2,6},{1,5},{5,9},... | collective-permute-start | bytes 393224 | tf_op jit(solution)/shard_map/ppermute | solution.py:29
  9.4 0.0 copy-done
  9.4 0.0 copy-done.1
  9.4 0.0 copy-done.2
  9.4 0.0 copy-start.3
  9.4 0.6 %copy-done.3 = s32[16]{0:T(128)S(1)} copy-done((s32[16]{0:T(128)S(1)}, s32[16]{0:T(128)}, u32[]{:S(2)}) %copy-start.3) | copy-done | bytes 88
  10.1 0.8 %add_pieces.5 = (f32[256,512]{1,0:T(8,128)S(1)}, bf16[512,512]{1,0:T(8,128)(2,1)S(1)}, bf16[128,512]{1,0:T(8,128)(2,1)S(1)}, bf16[384,512]{1,0:T(8,128)(2,1)S(1)}) custom-call(s32[16]{0:T(128)S(1)} %copy-done.3, f32[256,512]{1,0:T(8,128)S(1)} %copy-done, s32[256,1024]{1,0:T(8,128)S(1)} %copy-done.1, bf16[128,512]{1,0:T(8,128)(2,1)S(1)} %copy-done.2, ...), custom_call_target="tpu_custom_call" | custom-call | flops 6442450944 | bytes 1048576 | tf_op jit(solution)/shard_map/add_pieces/pallas_call | solution.py:203
  10.9 3.4 %collective-permute-start.6 = (bf16[128,512]{1,0:T(8,128)(2,1)S(1)}, bf16[128,512]{1,0:T(8,128)(2,1)S(1)}, u32[]{:S(2)}, u32[]{:S(2)}) collective-permute-start(bf16[128,512]{1,0:T(8,128)(2,1)S(1)} %get-tuple-element.20), channel_id=1, source_target_pairs={{0,12},{1,13},{4,6},{5,7},{8,10},{9,11},{12,0},{13,1},{14,2},{15,3... | collective-permute-start | bytes 393224 | tf_op jit(solution)/shard_map/ppermute | solution.py:39
  14.2 0.0 collective-permute-start.8
  14.2 0.0 collective-permute-done.2.rest_0_
  14.2 0.3 collective-permute-start.3
  14.5 0.0 collective-permute-done.4.rest_1_
  14.5 2.1 %collective-permute-start.5 = (bf16[128,512]{1,0:T(8,128)(2,1)S(1)}, bf16[128,512]{1,0:T(8,128)(2,1)S(1)}, u32[]{:S(2)}, u32[]{:S(2)}) collective-permute-start(bf16[128,512]{1,0:T(8,128)(2,1)S(1)} %collective-permute-done.4.rest_1_), channel_id=1, source_target_pairs={{0,2},{4,0},{8,4},{12,8},{14,12},{10,14},{6,10},{2,6},{1,5},{5,9},... | collective-permute-start | bytes 393224 | tf_op jit(solution)/shard_map/ppermute | solution.py:29
  16.7 0.6 %add_pieces.6 = (f32[256,512]{1,0:T(8,128)S(1)}, bf16[256,512]{1,0:T(8,128)(2,1)S(1)}) custom-call(s32[16]{0:T(128)S(1)} %copy-done.3, bf16[512,512]{1,0:T(8,128)(2,1)S(1)} %get-tuple-element.19.given_ref, s32[256,1024]{1,0:T(8,128)S(1)} %copy-done.1, bf16[128,512]{1,0:T(8,128)(2,1)S(1)} %collective-permute-done.2.rest_0_, ...), custom_call_target="tpu_custom_call", output_to_operand_aliasing={{0}: (5, {})} | custom-call | flops 4294967296 | bytes 1048576 | tf_op jit(solution)/shard_map/add_pieces/pallas_call | solution.py:203
  17.3 1.0 %collective-permute-start.9 = (bf16[256,512]{1,0:T(8,128)(2,1)S(1)}, bf16[256,512]{1,0:T(8,128)(2,1)S(1)}, u32[]{:S(2)}, u32[]{:S(2)}) collective-permute-start(bf16[256,512]{1,0:T(8,128)(2,1)S(1)} %get-tuple-element.25), channel_id=1, source_target_pairs={{0,1},{1,0},{2,3},{3,2},{4,5},{5,4},{6,7},{7,6},{8,9},{9,8},{10,11... | collective-permute-start | bytes 786440 | tf_op jit(solution)/shard_map/ppermute | solution.py:43
  18.3 0.5 %collective-permute-done.6.rest_2_ = bf16[128,512]{1,0:T(8,128)(2,1)S(1)} collective-permute-done((bf16[128,512]{1,0:T(8,128)(2,1)S(1)}, bf16[128,512]{1,0:T(8,128)(2,1)S(1)}, u32[]{:S(2)}, u32[]{:S(2)}) %collective-permute-start.6) | collective-permute-done | bytes 131104 | tf_op jit(solution)/shard_map/ppermute | solution.py:39
  18.8 0.9 %collective-permute-done.3.rest_0_ = bf16[128,512]{1,0:T(8,128)(2,1)S(1)} collective-permute-done((bf16[128,512]{1,0:T(8,128)(2,1)S(1)}, bf16[128,512]{1,0:T(8,128)(2,1)S(1)}, u32[]{:S(2)}, u32[]{:S(2)}) %collective-permute-start.3) | collective-permute-done | bytes 131104 | tf_op jit(solution)/shard_map/ppermute | solution.py:29
  19.6 1.7 %collective-permute-done.5.rest_1_ = bf16[128,512]{1,0:T(8,128)(2,1)S(1)} collective-permute-done((bf16[128,512]{1,0:T(8,128)(2,1)S(1)}, bf16[128,512]{1,0:T(8,128)(2,1)S(1)}, u32[]{:S(2)}, u32[]{:S(2)}) %collective-permute-start.5) | collective-permute-done | bytes 131104 | tf_op jit(solution)/shard_map/ppermute | solution.py:29
  21.3 0.6 %add_pieces.7 = (f32[256,512]{1,0:T(8,128)S(1)}, bf16[384,512]{1,0:T(8,128)(2,1)S(1)}) custom-call(s32[16]{0:T(128)S(1)} %copy-done.3, bf16[512,512]{1,0:T(8,128)(2,1)S(1)} %get-tuple-element.19.given_ref, s32[256,1024]{1,0:T(8,128)S(1)} %copy-done.1, bf16[128,512]{1,0:T(8,128)(2,1)S(1)} %collective-permute-done.3.rest_0_, ...), custom_call_target="tpu_custom_call", output_to_operand_aliasing={{0}: (6, {})} | custom-call | flops 6442450944 | bytes 1048576 | tf_op jit(solution)/shard_map/add_pieces/pallas_call | solution.py:203
  21.9 0.9 %collective-permute-start.7 = (bf16[384,512]{1,0:T(8,128)(2,1)S(1)}, bf16[384,512]{1,0:T(8,128)(2,1)S(1)}, u32[]{:S(2)}, u32[]{:S(2)}) collective-permute-start(bf16[384,512]{1,0:T(8,128)(2,1)S(1)} %get-tuple-element.23), channel_id=1, source_target_pairs={{0,1},{1,0},{2,3},{3,2},{4,5},{5,4},{6,7},{7,6},{8,9},{9,8},{10,11... | collective-permute-start | bytes 1179656 | tf_op jit(solution)/shard_map/ppermute | solution.py:43
  22.7 0.0 collective-permute-done.8.rest_0_
  22.7 0.0 collective-permute-done.9.rest_1_
  22.8 1.4 %add_pieces.8.rest_1_ = f32[256,512]{1,0:T(8,128)S(1)} custom-call(s32[16]{0:T(128)S(1)} %copy-done.3, bf16[512,512]{1,0:T(8,128)(2,1)S(1)} %get-tuple-element.19.given_ref, s32[256,1024]{1,0:T(8,128)S(1)} %copy-done.1, bf16[384,512]{1,0:T(8,128)(2,1)S(1)} %collective-permute-done.8.rest_0_, ...), custom_call_target="tpu_custom_call", output_to_operand_aliasing={{}: (5, {})} | custom-call | flops 10737418240 | bytes 1048576 | tf_op jit(solution)/shard_map/add_pieces/pallas_call | solution.py:203
  24.2 0.0 collective-permute-done.7.rest_0_
  24.2 0.7 %add_pieces.9 = (f32[256,512]{1,0:T(8,128)S(1)}, f32[16,128]{1,0:T(8,128)S(1)}) custom-call(s32[16]{0:T(128)S(1)} %copy-done.3, bf16[512,512]{1,0:T(8,128)(2,1)S(1)} %get-tuple-element.19.given_ref, s32[256,1024]{1,0:T(8,128)S(1)} %copy-done.1, bf16[384,512]{1,0:T(8,128)(2,1)S(1)} %collective-permute-done.7.rest_0_, ...), custom_call_target="tpu_custom_call", output_to_operand_aliasing={{0}: (4, {})} | custom-call | flops 6442450944 | bytes 1048576 | tf_op jit(solution)/shard_map/add_pieces/pallas_call | solution.py:203
  24.8 11.8 %all_to_all.11 = f32[16,1,128]{2,1,0:T(1,128)S(1)} all-to-all(f32[16,1,128]{2,1,0:T(1,128)S(1)} %bitcast.5), channel_id=1, replica_groups=mesh['group'=2,'loop'=16] {'loop'}, dimensions={0} | all-to-all | bytes 16384 | tf_op jit(solution)/shard_map/all_to_all | solution.py:346
  36.6 1.0 %update.1 = f32[256,512]{1,0:T(8,128)} custom-call(f32[256,512]{1,0:T(8,128)S(1)} %copy-done, f32[256,512]{1,0:T(8,128)S(1)} %get-tuple-element.27.grad_ref, f32[16,128]{1,0:T(8,128)S(1)} %bitcast.4), custom_call_target="tpu_custom_call" | custom-call | flops 262144 | bytes 1572864 | tf_op jit(solution)/shard_map/update/pallas_call | solution.py:347
Async XLA Ops:
  0.0 7.0 %collective-permute-start = (bf16[128,512]{1,0:T(8,128)(2,1)}, bf16[128,512]{1,0:T(8,128)(2,1)S(1)}, u32[]{:S(2)}, u32[]{:S(2)}) collective-permute-start(bf16[128,512]{1,0:T(8,128)(2,1)} %rest_0_.1), channel_id=1, source_target_pairs={{0,4},{4,8},{8,12},{12,14},{14,10},{10,6},{6,2},{2,0},{1,3},{5,1},... | collective-permute-start | bytes 393224 | tf_op jit(solution)/shard_map/ppermute | solution.py:29
  3.0 5.5 %collective-permute-start.1 = (bf16[128,512]{1,0:T(8,128)(2,1)}, bf16[128,512]{1,0:T(8,128)(2,1)S(1)}, u32[]{:S(2)}, u32[]{:S(2)}) collective-permute-start(bf16[128,512]{1,0:T(8,128)(2,1)} %rest_0_.1), channel_id=1, source_target_pairs={{0,2},{4,0},{8,4},{12,8},{14,12},{10,14},{6,10},{2,6},{1,5},{5,9},... | collective-permute-start | bytes 393224 | tf_op jit(solution)/shard_map/ppermute | solution.py:29
  3.7 5.7 %copy-start = (f32[256,512]{1,0:T(8,128)S(1)}, f32[256,512]{1,0:T(8,128)}, u32[]{:S(2)}) copy-start(f32[256,512]{1,0:T(8,128)} %users_ref.1) | copy-start | bytes 1572868
  3.7 5.7 %copy-start.1 = (s32[256,1024]{1,0:T(8,128)S(1)}, s32[256,1024]{1,0:T(8,128)}, u32[]{:S(2)}) copy-start(s32[256,1024]{1,0:T(8,128)} %labels_ref.9) | copy-start | bytes 3145732
  3.7 5.7 %copy-start.2 = (bf16[128,512]{1,0:T(8,128)(2,1)S(1)}, bf16[128,512]{1,0:T(8,128)(2,1)}, u32[]{:S(2)}) copy-start(bf16[128,512]{1,0:T(8,128)(2,1)} %rest_0_.1) | copy-start | bytes 393220
  7.0 7.3 %collective-permute-start.2 = (bf16[128,512]{1,0:T(8,128)(2,1)S(1)}, bf16[128,512]{1,0:T(8,128)(2,1)S(1)}, u32[]{:S(2)}, u32[]{:S(2)}) collective-permute-start(bf16[128,512]{1,0:T(8,128)(2,1)S(1)} %collective-permute-done.rest_1_), channel_id=1, source_target_pairs={{0,4},{4,8},{8,12},{12,14},{14,10},{10,6},{6,2},{2,0},{1,3},{5,1},... | collective-permute-start | bytes 393224 | tf_op jit(solution)/shard_map/ppermute | solution.py:29
  8.5 6.0 %collective-permute-start.4 = (bf16[128,512]{1,0:T(8,128)(2,1)S(1)}, bf16[128,512]{1,0:T(8,128)(2,1)S(1)}, u32[]{:S(2)}, u32[]{:S(2)}) collective-permute-start(bf16[128,512]{1,0:T(8,128)(2,1)S(1)} %collective-permute-done.1.rest_2_), channel_id=1, source_target_pairs={{0,2},{4,0},{8,4},{12,8},{14,12},{10,14},{6,10},{2,6},{1,5},{5,9},... | collective-permute-start | bytes 393224 | tf_op jit(solution)/shard_map/ppermute | solution.py:29
  9.4 0.7 %copy-start.3 = (s32[16]{0:T(128)S(1)}, s32[16]{0:T(128)}, u32[]{:S(2)}) copy-start(s32[16]{0:T(128)} %slot_table.1.table_ref) | copy-start | bytes 196
  10.9 7.9 %collective-permute-start.6 = (bf16[128,512]{1,0:T(8,128)(2,1)S(1)}, bf16[128,512]{1,0:T(8,128)(2,1)S(1)}, u32[]{:S(2)}, u32[]{:S(2)}) collective-permute-start(bf16[128,512]{1,0:T(8,128)(2,1)S(1)} %get-tuple-element.20), channel_id=1, source_target_pairs={{0,12},{1,13},{4,6},{5,7},{8,10},{9,11},{12,0},{13,1},{14,2},{15,3... | collective-permute-start | bytes 393224 | tf_op jit(solution)/shard_map/ppermute | solution.py:39
  14.2 8.5 %collective-permute-start.8 = (bf16[384,512]{1,0:T(8,128)(2,1)S(1)}, bf16[384,512]{1,0:T(8,128)(2,1)S(1)}, u32[]{:S(2)}, u32[]{:S(2)}) collective-permute-start(bf16[384,512]{1,0:T(8,128)(2,1)S(1)} %get-tuple-element.24), channel_id=1, source_target_pairs={{0,1},{1,0},{2,3},{3,2},{4,5},{5,4},{6,7},{7,6},{8,9},{9,8},{10,11... | collective-permute-start | bytes 1179656 | tf_op jit(solution)/shard_map/ppermute | solution.py:43
  14.2 5.4 %collective-permute-start.3 = (bf16[128,512]{1,0:T(8,128)(2,1)S(1)}, bf16[128,512]{1,0:T(8,128)(2,1)S(1)}, u32[]{:S(2)}, u32[]{:S(2)}) collective-permute-start(bf16[128,512]{1,0:T(8,128)(2,1)S(1)} %collective-permute-done.2.rest_0_), channel_id=1, source_target_pairs={{0,4},{4,8},{8,12},{12,14},{14,10},{10,6},{6,2},{2,0},{1,3},{5,1},... | collective-permute-start | bytes 393224 | tf_op jit(solution)/shard_map/ppermute | solution.py:29
  14.5 6.7 %collective-permute-start.5 = (bf16[128,512]{1,0:T(8,128)(2,1)S(1)}, bf16[128,512]{1,0:T(8,128)(2,1)S(1)}, u32[]{:S(2)}, u32[]{:S(2)}) collective-permute-start(bf16[128,512]{1,0:T(8,128)(2,1)S(1)} %collective-permute-done.4.rest_1_), channel_id=1, source_target_pairs={{0,2},{4,0},{8,4},{12,8},{14,12},{10,14},{6,10},{2,6},{1,5},{5,9},... | collective-permute-start | bytes 393224 | tf_op jit(solution)/shard_map/ppermute | solution.py:29
  17.3 5.5 %collective-permute-start.9 = (bf16[256,512]{1,0:T(8,128)(2,1)S(1)}, bf16[256,512]{1,0:T(8,128)(2,1)S(1)}, u32[]{:S(2)}, u32[]{:S(2)}) collective-permute-start(bf16[256,512]{1,0:T(8,128)(2,1)S(1)} %get-tuple-element.25), channel_id=1, source_target_pairs={{0,1},{1,0},{2,3},{3,2},{4,5},{5,4},{6,7},{7,6},{8,9},{9,8},{10,11... | collective-permute-start | bytes 786440 | tf_op jit(solution)/shard_map/ppermute | solution.py:43
  21.9 2.3 %collective-permute-start.7 = (bf16[384,512]{1,0:T(8,128)(2,1)S(1)}, bf16[384,512]{1,0:T(8,128)(2,1)S(1)}, u32[]{:S(2)}, u32[]{:S(2)}) collective-permute-start(bf16[384,512]{1,0:T(8,128)(2,1)S(1)} %get-tuple-element.23), channel_id=1, source_target_pairs={{0,1},{1,0},{2,3},{3,2},{4,5},{5,4},{6,7},{7,6},{8,9},{9,8},{10,11... | collective-permute-start | bytes 1179656 | tf_op jit(solution)/shard_map/ppermute | solution.py:43

commit v7 on v6

--- a/solution.py
+++ b/solution.py
@@ -138,14 +138,47 @@
     return 2 * chip + (1 - core if other else core)
 
 
-def pieces_kernel(places, count, packed, loop_size, first, last, table_ref, given_ref, labels_ref, *rest):
+def pack_kernel(*refs):
+    tile = refs[0].shape[0]
+    for at, ref in enumerate(refs[:-1]):
+        refs[-1][at * tile : (at + 1) * tile, :] = ref[...]
+
+
+def pick_kernel(loop_size, ahead_ref, behind_ref, picked_ref):
+    core, position = core_and_position(loop_size)
+    for at, ref in enumerate((ahead_ref, behind_ref)):
+
+        @pl.when((core + position) % 2 == at)
+        def _():
+            picked_ref[...] = ref[...]
+
+
+def copies(kernel, name, rows, *arrays):
+    width = arrays[0].shape[1]
+    return pl.pallas_call(
+        kernel,
+        out_shape=jax.ShapeDtypeStruct((rows, width), arrays[0].dtype),
+        in_specs=[pl.BlockSpec(memory_space=pltpu.VMEM)] * len(arrays),
+        out_specs=pl.BlockSpec(memory_space=pltpu.VMEM),
+        compiler_params=pltpu.CompilerParams(vmem_limit_bytes=16 * 1024 * 1024),
+        cost_estimate=pl.CostEstimate(
+            flops=2**34, bytes_accessed=4 * rows * width, transcendentals=0
+        ),
+        name=name,
+    )(*arrays)
+
+
+def pack(arrays):
+    return copies(pack_kernel, "pack", sum(array.shape[0] for array in arrays), *arrays)
+
+
+def pieces_kernel(places, count, packed, first, last, table_ref, given_ref, labels_ref, *rest):
     rest = list(rest)
     arrays = [rest.pop(0) for _ in range(count)]
     if not first:
         rest.pop(0)
     grad_ref = rest.pop(0)
     parts_ref = rest.pop(0) if first else given_ref
-    across_ref = rest.pop(0) if first else None
     pack_ref = rest.pop(0) if packed else None
     square_ref = rest.pop(0) if last else None
     tiles, slots = rest
@@ -153,13 +186,6 @@
     for at, index in enumerate(packed):
         pack_ref[at * tile : (at + 1) * tile, :] = arrays[index][...]
     if first:
-        core, position = core_and_position(loop_size)
-        for at in range(2):
-
-            @pl.when((core + position) % 2 == at)
-            def _():
-                across_ref[...] = arrays[1 + at][...]
-
         parts_ref[...] = halves(0.5 * given_ref[...])
         grad_ref[...] = jnp.zeros_like(grad_ref)
     live = jnp.int32(0)
@@ -194,14 +220,13 @@
     out_shape = [jax.ShapeDtypeStruct((rows, width), jnp.float32)]
     if first:
         out_shape.append(jax.ShapeDtypeStruct((2 * rows, width), jnp.bfloat16))
-        out_shape.append(jax.ShapeDtypeStruct((tile, width), jnp.bfloat16))
     if packed:
         out_shape.append(jax.ShapeDtypeStruct((len(packed) * tile, width), jnp.bfloat16))
     if last:
         out_shape.append(jax.ShapeDtypeStruct((loop_size, 128), jnp.float32))
     extra = [] if first else [before]
     return pl.pallas_call(
-        functools.partial(pieces_kernel, places, len(arrays), packed, loop_size, first, last),
+        functools.partial(pieces_kernel, places, len(arrays), packed, first, last),
         out_shape=out_shape,
         in_specs=[pl.BlockSpec(memory_space=pltpu.SMEM)]
         + [pl.BlockSpec(memory_space=pltpu.VMEM)] * (2 + len(arrays) + len(extra)),
@@ -239,20 +264,19 @@
     down = to_next(items, -1, loop_size)
     up, table = lax.optimization_barrier((up, table))
     first = [held(0, items), held(1, up), held(-1, down)]
-    second = [held(2, to_next(up, 1, loop_size)), held(-2, to_next(down, -1, loop_size))]
-    gradient, parts, opposite, pack = add_pieces(
-        first, [0, 1, 2], loop_size, table, users, labels, None, False
+    opposite = copies(functools.partial(pick_kernel, loop_size), "pick", up.shape[0], up, down)
+    opposite = across(opposite, loop_size)
+    first += [held(2, to_next(up, 1, loop_size)), held(-2, to_next(down, -1, loop_size))]
+    then = [held(3, to_next(first[3][0], 1, loop_size)), held(-3, to_next(first[4][0], -1, loop_size))]
+    then.append(held(4, opposite))
+    gradient, parts, packed = add_pieces(
+        first, [0, 1, 2, 3, 4], loop_size, table, users, labels, None, False
     )
-    opposite = across(opposite, loop_size)
-    first = other(pack, [0, 1, -1])
-    third = [held(3, to_next(second[0][0], 1, loop_size)), held(-3, to_next(second[1][0], -1, loop_size))]
-    gradient, pack = add_pieces(second, [0, 1], loop_size, table, parts, labels, gradient, False)
-    second = other(pack, [2, -2])
-    third.append(held(4, opposite))
-    gradient, pack = add_pieces(third, [0, 1, 2], loop_size, table, parts, labels, gradient, False)
-    third = other(pack, [3, -3, 4])
-    (gradient,) = add_pieces([first, second], [], loop_size, table, parts, labels, gradient, False)
-    return *add_pieces([third], [], loop_size, table, parts, labels, gradient, True), users
+    given = other(packed, [0, 1, -1, 2, -2])
+    arrived, gradient = lax.optimization_barrier(([array for array, _ in then], gradient))
+    last = other(pack(arrived), [3, -3, 4])
+    (gradient,) = add_pieces(then + [given], [], loop_size, table, parts, labels, gradient, False)
+    return *add_pieces([last], [], loop_size, table, parts, labels, gradient, True), users
 
 
 def chunks_kernel(

time: 37.4 us -> 38.9 us (1.040)
  waiting for transfers between devices: 4.81 us -> 9.17 us
  starting transfers between devices: 13.1 us -> 9.25 us
  blocking collectives: 11.8 us -> 14.3 us
  Pallas kernels: 6.45 us -> 5.23 us
  local copies, waits for them, and re-layouts: 0.66 us -> 0.03 us
    ppermute x6, waiting for transfers between devices: 4.33 us -> 7.54 us  [to_next(): return lax.ppermute(array, 'loop', pairs)]
    all_to_all x1, blocking collectives: 11.8 us -> 14.3 us  [local(): squares = lax.all_to_all(square, 'loop', 0, 0, tiled=True)]
    ppermute x6, starting transfers between devices: 7.88 us -> 5.74 us  [to_next(): return lax.ppermute(array, 'loop', pairs)]
    ppermute x3 -> x2, starting transfers between devices: 1.87 us -> 0.14 us  [to_other_core(): lax.ppermute(array, 'loop', [(at, at ^ 1) for at in range(loop_size)])]
    pallas_call x5 -> x3, Pallas kernels: 4.02 us -> 2.88 us  [add_pieces(): pl.pallas_call(functools.partial(pieces_kernel, places, len(arrays), pack...]
    ppermute x3 -> x2, waiting for transfers between devices: 0.01 us -> 1.06 us  [to_other_core(): lax.ppermute(array, 'loop', [(at, at ^ 1) for at in range(loop_size)])]
    unnamed x8, local copies, waits for them, and re-layouts: 0.66 us -> 0.03 us
  transfers between devices with their start and end apart: 10 -> 9, of which waited for: 4 -> 6; matrix products, arithmetic and copies ran while one was open for 0% -> 0% of each run, Pallas kernels for 13% -> 9%
where the time goes in v7:
time: 38.9 us; the launch traced here: 38.7 us
  blocking collectives  14.3 us (37%)
  starting transfers between devices  9.25 us (24%)
  waiting for transfers between devices  9.17 us (24%)
  Pallas kernels  5.23 us (13%)
  between operations  0.78 us (2%)
    all_to_all x1, blocking collectives, local(): squares = lax.all_to_all(square, 'loop', 0, 0, tiled=True)  14.3 us
    ppermute x6, waiting for transfers between devices, to_next(): return lax.ppermute(array, 'loop', pairs)  7.54 us
    ppermute x6, starting transfers between devices, to_next(): return lax.ppermute(array, 'loop', pairs)  5.74 us
    ppermute x1, starting transfers between devices, across(): return lax.ppermute(array, 'loop', pairs)  3.36 us
    pallas_call x3, Pallas kernels, add_pieces(): pl.pallas_call(functools.partial(pieces_kernel, places, len(arrays), pack...  2.88 us
    pallas_call x1, Pallas kernels, slot_table(): pl.pallas_call(functools.partial(table_kernel, loop_size, origins), out_s...  1.33 us
    ppermute x2, waiting for transfers between devices, to_other_core(): lax.ppermute(array, 'loop', [(at, at ^ 1) for at in range(loop_size)])  1.06 us
    pallas_call x1, Pallas kernels, local(): pl.pallas_call(functools.partial(update_kernel, rows * loop_size * width)...  0.98 us
  transfers between devices with their start and end apart: 9, of which 6 were waited for; matrix products, arithmetic and copies ran while one was open for 0% of the time, Pallas kernels for 9%

profile of v7, /device:TPU:0, one launch (start us, length us, event | category | flops | bytes accessed | tf_op | source)
XLA Modules:
  0.0 38.7 jit_solution(1278392143656949116)
XLA Ops:
  0.0 3.0 %collective-permute-start = (bf16[128,512]{1,0:T(8,128)(2,1)}, bf16[128,512]{1,0:T(8,128)(2,1)S(1)}, u32[]{:S(2)}, u32[]{:S(2)}) collective-permute-start(bf16[128,512]{1,0:T(8,128)(2,1)} %rest_0_.1), channel_id=1, source_target_pairs={{0,4},{4,8},{8,12},{12,14},{14,10},{10,6},{6,2},{2,0},{1,3},{5,1},... | collective-permute-start | bytes 393224 | tf_op jit(solution)/shard_map/ppermute | solution.py:29
  3.0 0.0 collective-permute-start.1
  3.7 1.3 %slot_table.1.table_ref = s32[16]{0:T(128)} custom-call(s32[1,8]{1,0:T(1,128)} %list_ref.1, s32[1]{0:T(128)S(6)} %copy.11.count_ref), custom_call_target="tpu_custom_call" | custom-call | flops 4294967296 | bytes 1024 | tf_op jit(solution)/shard_map/slot_table/pallas_call | solution.py:64
  5.0 0.0 copy-start
  5.0 0.0 copy-start.1
  5.0 0.0 copy-start.2
  5.1 0.0 copy-start.3
  5.1 1.9 %collective-permute-done.rest_1_.ahead_ref = bf16[128,512]{1,0:T(8,128)(2,1)S(1)} collective-permute-done((bf16[128,512]{1,0:T(8,128)(2,1)}, bf16[128,512]{1,0:T(8,128)(2,1)S(1)}, u32[]{:S(2)}, u32[]{:S(2)}) %collective-permute-start) | collective-permute-done | bytes 131104 | tf_op jit(solution)/shard_map/ppermute | solution.py:29
  7.0 1.5 %collective-permute-start.2 = (bf16[128,512]{1,0:T(8,128)(2,1)S(1)}, bf16[128,512]{1,0:T(8,128)(2,1)S(1)}, u32[]{:S(2)}, u32[]{:S(2)}) collective-permute-start(bf16[128,512]{1,0:T(8,128)(2,1)S(1)} %collective-permute-done.rest_1_.ahead_ref), channel_id=1, source_target_pairs={{0,4},{4,8},{8,12},{12,14},{14,10},{10,6},{6,2},{2,0},{1,3},{5,1},... | collective-permute-start | bytes 393224 | tf_op jit(solution)/shard_map/ppermute | solution.py:29
  8.5 0.0 collective-permute-done.1.rest_2_.behind_ref
  8.5 0.9 %collective-permute-start.3 = (bf16[128,512]{1,0:T(8,128)(2,1)S(1)}, bf16[128,512]{1,0:T(8,128)(2,1)S(1)}, u32[]{:S(2)}, u32[]{:S(2)}) collective-permute-start(bf16[128,512]{1,0:T(8,128)(2,1)S(1)} %collective-permute-done.1.rest_2_.behind_ref), channel_id=1, source_target_pairs={{0,2},{4,0},{8,4},{12,8},{14,12},{10,14},{6,10},{2,6},{1,5},{5,9},... | collective-permute-start | bytes 393224 | tf_op jit(solution)/shard_map/ppermute | solution.py:29
  9.4 3.4 %collective-permute-start.6 = (bf16[128,512]{1,0:T(8,128)(2,1)S(1)}, bf16[128,512]{1,0:T(8,128)(2,1)S(1)}, u32[]{:S(2)}, u32[]{:S(2)}) collective-permute-start(bf16[128,512]{1,0:T(8,128)(2,1)S(1)} %pick.1), channel_id=1, source_target_pairs={{0,12},{1,13},{4,6},{5,7},{8,10},{9,11},{12,0},{13,1},{14,2},{15,3... | collective-permute-start | bytes 393224 | tf_op jit(solution)/shard_map/ppermute | solution.py:39
  12.8 0.4 collective-permute-done.2.rest_3_
  13.2 0.3 collective-permute-start.4
  13.5 2.6 %collective-permute-done.3.rest_4_ = bf16[128,512]{1,0:T(8,128)(2,1)S(1)} collective-permute-done((bf16[128,512]{1,0:T(8,128)(2,1)S(1)}, bf16[128,512]{1,0:T(8,128)(2,1)S(1)}, u32[]{:S(2)}, u32[]{:S(2)}) %collective-permute-start.3) | collective-permute-done | bytes 131104 | tf_op jit(solution)/shard_map/ppermute | solution.py:29
  16.0 0.0 collective-permute-start.5
  16.0 0.0 copy-done
  16.0 0.0 copy-done.1
  16.0 0.0 copy-done.2
  16.0 0.0 copy-done.3
  16.1 1.6 %add_pieces.3 = (f32[256,512]{1,0:T(8,128)S(1)}, bf16[512,512]{1,0:T(8,128)(2,1)S(1)}, bf16[640,512]{1,0:T(8,128)(2,1)S(1)}) custom-call(s32[16]{0:T(128)S(1)} %copy-done.3, f32[256,512]{1,0:T(8,128)S(1)} %copy-done, s32[256,1024]{1,0:T(8,128)S(1)} %copy-done.1, bf16[128,512]{1,0:T(8,128)(2,1)S(1)} %copy-done.2, ...), custom_call_target="tpu_custom_call" | custom-call | flops 10737418240 | bytes 1048576 | tf_op jit(solution)/shard_map/add_pieces/pallas_call | solution.py:228
  17.7 0.1 collective-permute-start.8
  17.7 0.6 %collective-permute-done.6.refs_2_.rest_2_ = bf16[128,512]{1,0:T(8,128)(2,1)S(1)} collective-permute-done((bf16[128,512]{1,0:T(8,128)(2,1)S(1)}, bf16[128,512]{1,0:T(8,128)(2,1)S(1)}, u32[]{:S(2)}, u32[]{:S(2)}) %collective-permute-start.6) | collective-permute-done | bytes 131104 | tf_op jit(solution)/shard_map/ppermute | solution.py:39
  18.3 0.0 collective-permute-done.4.refs_0_.rest_0_
  18.3 2.7 %collective-permute-done.5.refs_1_.rest_1_ = bf16[128,512]{1,0:T(8,128)(2,1)S(1)} collective-permute-done((bf16[128,512]{1,0:T(8,128)(2,1)S(1)}, bf16[128,512]{1,0:T(8,128)(2,1)S(1)}, u32[]{:S(2)}, u32[]{:S(2)}) %collective-permute-start.5) | collective-permute-done | bytes 131104 | tf_op jit(solution)/shard_map/ppermute | solution.py:29
  21.0 0.1 collective-permute-start.7
  21.1 0.0 collective-permute-done.8.rest_3_
  21.1 0.6 %add_pieces.4.rest_1_ = f32[256,512]{1,0:T(8,128)S(1)} custom-call(s32[16]{0:T(128)S(1)} %copy-done.3, bf16[512,512]{1,0:T(8,128)(2,1)S(1)} %get-tuple-element.18.given_ref, s32[256,1024]{1,0:T(8,128)S(1)} %copy-done.1, bf16[128,512]{1,0:T(8,128)(2,1)S(1)} %collective-permute-done.4.refs_0_.rest_0_, ...), custom_call_target="tpu_custom_call", output_to_operand_aliasing={{}: (7, {})} | custom-call | flops 17179869184 | bytes 1048576 | tf_op jit(solution)/shard_map/add_pieces/pallas_call | solution.py:228
  21.8 1.1 %collective-permute-done.7.rest_0_ = bf16[384,512]{1,0:T(8,128)(2,1)S(1)} collective-permute-done((bf16[384,512]{1,0:T(8,128)(2,1)S(1)}, bf16[384,512]{1,0:T(8,128)(2,1)S(1)}, u32[]{:S(2)}, u32[]{:S(2)}) %collective-permute-start.7) | collective-permute-done | bytes 393248 | tf_op jit(solution)/shard_map/ppermute | solution.py:43
  22.8 0.6 %add_pieces.5 = (f32[256,512]{1,0:T(8,128)S(1)}, f32[16,128]{1,0:T(8,128)S(1)}) custom-call(s32[16]{0:T(128)S(1)} %copy-done.3, bf16[512,512]{1,0:T(8,128)(2,1)S(1)} %get-tuple-element.18.given_ref, s32[256,1024]{1,0:T(8,128)S(1)} %copy-done.1, bf16[384,512]{1,0:T(8,128)(2,1)S(1)} %collective-permute-done.7.rest_0_, ...), custom_call_target="tpu_custom_call", output_to_operand_aliasing={{0}: (4, {})} | custom-call | flops 6442450944 | bytes 1048576 | tf_op jit(solution)/shard_map/add_pieces/pallas_call | solution.py:228
  23.5 14.3 %all_to_all.11 = f32[16,1,128]{2,1,0:T(1,128)S(1)} all-to-all(f32[16,1,128]{2,1,0:T(1,128)S(1)} %bitcast.5), channel_id=1, replica_groups=mesh['group'=2,'loop'=16] {'loop'}, dimensions={0} | all-to-all | bytes 16384 | tf_op jit(solution)/shard_map/all_to_all | solution.py:370
  37.7 1.0 %update.1 = f32[256,512]{1,0:T(8,128)} custom-call(f32[256,512]{1,0:T(8,128)S(1)} %copy-done, f32[256,512]{1,0:T(8,128)S(1)} %get-tuple-element.25.grad_ref, f32[16,128]{1,0:T(8,128)S(1)} %bitcast.4), custom_call_target="tpu_custom_call" | custom-call | flops 262144 | bytes 1572864 | tf_op jit(solution)/shard_map/update/pallas_call | solution.py:371
  (2 shorter events, 0.0 us)
Async XLA Ops:
  0.0 7.0 %collective-permute-start = (bf16[128,512]{1,0:T(8,128)(2,1)}, bf16[128,512]{1,0:T(8,128)(2,1)S(1)}, u32[]{:S(2)}, u32[]{:S(2)}) collective-permute-start(bf16[128,512]{1,0:T(8,128)(2,1)} %rest_0_.1), channel_id=1, source_target_pairs={{0,4},{4,8},{8,12},{12,14},{14,10},{10,6},{6,2},{2,0},{1,3},{5,1},... | collective-permute-start | bytes 393224 | tf_op jit(solution)/shard_map/ppermute | solution.py:29
  3.0 5.5 %collective-permute-start.1 = (bf16[128,512]{1,0:T(8,128)(2,1)}, bf16[128,512]{1,0:T(8,128)(2,1)S(1)}, u32[]{:S(2)}, u32[]{:S(2)}) collective-permute-start(bf16[128,512]{1,0:T(8,128)(2,1)} %rest_0_.1), channel_id=1, source_target_pairs={{0,2},{4,0},{8,4},{12,8},{14,12},{10,14},{6,10},{2,6},{1,5},{5,9},... | collective-permute-start | bytes 393224 | tf_op jit(solution)/shard_map/ppermute | solution.py:29
  5.0 11.0 %copy-start = (f32[256,512]{1,0:T(8,128)S(1)}, f32[256,512]{1,0:T(8,128)}, u32[]{:S(2)}) copy-start(f32[256,512]{1,0:T(8,128)} %users_ref.1) | copy-start | bytes 1572868
  5.0 11.0 %copy-start.1 = (s32[256,1024]{1,0:T(8,128)S(1)}, s32[256,1024]{1,0:T(8,128)}, u32[]{:S(2)}) copy-start(s32[256,1024]{1,0:T(8,128)} %labels_ref.5) | copy-start | bytes 3145732
  5.0 11.0 %copy-start.2 = (bf16[128,512]{1,0:T(8,128)(2,1)S(1)}, bf16[128,512]{1,0:T(8,128)(2,1)}, u32[]{:S(2)}) copy-start(bf16[128,512]{1,0:T(8,128)(2,1)} %rest_0_.1) | copy-start | bytes 393220
  5.1 11.0 %copy-start.3 = (s32[16]{0:T(128)S(1)}, s32[16]{0:T(128)}, u32[]{:S(2)}) copy-start(s32[16]{0:T(128)} %slot_table.1.table_ref) | copy-start | bytes 196
  7.0 6.2 %collective-permute-start.2 = (bf16[128,512]{1,0:T(8,128)(2,1)S(1)}, bf16[128,512]{1,0:T(8,128)(2,1)S(1)}, u32[]{:S(2)}, u32[]{:S(2)}) collective-permute-start(bf16[128,512]{1,0:T(8,128)(2,1)S(1)} %collective-permute-done.rest_1_.ahead_ref), channel_id=1, source_target_pairs={{0,4},{4,8},{8,12},{12,14},{14,10},{10,6},{6,2},{2,0},{1,3},{5,1},... | collective-permute-start | bytes 393224 | tf_op jit(solution)/shard_map/ppermute | solution.py:29
  8.5 7.5 %collective-permute-start.3 = (bf16[128,512]{1,0:T(8,128)(2,1)S(1)}, bf16[128,512]{1,0:T(8,128)(2,1)S(1)}, u32[]{:S(2)}, u32[]{:S(2)}) collective-permute-start(bf16[128,512]{1,0:T(8,128)(2,1)S(1)} %collective-permute-done.1.rest_2_.behind_ref), channel_id=1, source_target_pairs={{0,2},{4,0},{8,4},{12,8},{14,12},{10,14},{6,10},{2,6},{1,5},{5,9},... | collective-permute-start | bytes 393224 | tf_op jit(solution)/shard_map/ppermute | solution.py:29
  9.4 8.9 %collective-permute-start.6 = (bf16[128,512]{1,0:T(8,128)(2,1)S(1)}, bf16[128,512]{1,0:T(8,128)(2,1)S(1)}, u32[]{:S(2)}, u32[]{:S(2)}) collective-permute-start(bf16[128,512]{1,0:T(8,128)(2,1)S(1)} %pick.1), channel_id=1, source_target_pairs={{0,12},{1,13},{4,6},{5,7},{8,10},{9,11},{12,0},{13,1},{14,2},{15,3... | collective-permute-start | bytes 393224 | tf_op jit(solution)/shard_map/ppermute | solution.py:39
  13.2 5.2 %collective-permute-start.4 = (bf16[128,512]{1,0:T(8,128)(2,1)S(1)}, bf16[128,512]{1,0:T(8,128)(2,1)S(1)}, u32[]{:S(2)}, u32[]{:S(2)}) collective-permute-start(bf16[128,512]{1,0:T(8,128)(2,1)S(1)} %collective-permute-done.2.rest_3_), channel_id=1, source_target_pairs={{0,4},{4,8},{8,12},{12,14},{14,10},{10,6},{6,2},{2,0},{1,3},{5,1},... | collective-permute-start | bytes 393224 | tf_op jit(solution)/shard_map/ppermute | solution.py:29
  16.0 5.0 %collective-permute-start.5 = (bf16[128,512]{1,0:T(8,128)(2,1)S(1)}, bf16[128,512]{1,0:T(8,128)(2,1)S(1)}, u32[]{:S(2)}, u32[]{:S(2)}) collective-permute-start(bf16[128,512]{1,0:T(8,128)(2,1)S(1)} %collective-permute-done.3.rest_4_), channel_id=1, source_target_pairs={{0,2},{4,0},{8,4},{12,8},{14,12},{10,14},{6,10},{2,6},{1,5},{5,9},... | collective-permute-start | bytes 393224 | tf_op jit(solution)/shard_map/ppermute | solution.py:29
  17.7 3.4 %collective-permute-start.8 = (bf16[640,512]{1,0:T(8,128)(2,1)S(1)}, bf16[640,512]{1,0:T(8,128)(2,1)S(1)}, u32[]{:S(2)}, u32[]{:S(2)}) collective-permute-start(bf16[640,512]{1,0:T(8,128)(2,1)S(1)} %get-tuple-element.23), channel_id=1, source_target_pairs={{0,1},{1,0},{2,3},{3,2},{4,5},{5,4},{6,7},{7,6},{8,9},{9,8},{10,11... | collective-permute-start | bytes 1966088 | tf_op jit(solution)/shard_map/ppermute | solution.py:43
  21.0 1.8 %collective-permute-start.7 = (bf16[384,512]{1,0:T(8,128)(2,1)S(1)}, bf16[384,512]{1,0:T(8,128)(2,1)S(1)}, u32[]{:S(2)}, u32[]{:S(2)}) collective-permute-start(bf16[384,512]{1,0:T(8,128)(2,1)S(1)} %pack.1), channel_id=1, source_target_pairs={{0,1},{1,0},{2,3},{3,2},{4,5},{5,4},{6,7},{7,6},{8,9},{9,8},{10,11... | collective-permute-start | bytes 1179656 | tf_op jit(solution)/shard_map/ppermute | solution.py:43

commit v8 on v6

--- a/solution.py
+++ b/solution.py
@@ -49,26 +49,32 @@
 
 
 def table_kernel(loop_size, origins, list_ref, count_ref, table_ref):
-    wanted = [
-        jnp.where(slot < count_ref[0], list_ref[0, slot], -1) for slot in range(list_ref.shape[1])
-    ]
+    chips = loop_size // 2
+    lane = lax.broadcasted_iota(jnp.int32, table_ref.shape, 1)
+    core, position = core_and_position(loop_size)
+    hops, other = jnp.zeros_like(lane), jnp.zeros_like(lane)
     for at, origin in enumerate(origins):
-        block = origin_block(origin, loop_size)
-        found = jnp.int32(-1)
-        for slot, name in enumerate(wanted):
-            found = jnp.where(name == block, slot, found)
-        table_ref[at] = found
+        hops = jnp.where(lane == at, origin[0], hops)
+        other = jnp.where(lane == at, origin[1], other)
+    at = (position + chips + jnp.where(core == 0, -hops, hops)) & (chips - 1)
+    chip = jnp.where(at < chips // 2, 2 * at, 2 * (chips - 1 - at) + 1)
+    block = 2 * chip + jnp.where(other == 1, 1 - core, core)
+    found = jnp.full_like(lane, -1)
+    for slot in range(list_ref.shape[1]):
+        name = jnp.where(slot < count_ref[...], list_ref[:, slot : slot + 1], -1)
+        found = jnp.where(name == block, slot, found)
+    table_ref[...] = jnp.where(lane < len(origins), found, -1)
 
 
 def slot_table(loop_size, origins, block_list, live_count):
     return pl.pallas_call(
         functools.partial(table_kernel, loop_size, origins),
-        out_shape=jax.ShapeDtypeStruct((len(origins),), jnp.int32),
-        in_specs=[pl.BlockSpec(memory_space=pltpu.SMEM)] * 2,
-        out_specs=pl.BlockSpec(memory_space=pltpu.SMEM),
+        out_shape=jax.ShapeDtypeStruct((1, 128), jnp.int32),
+        in_specs=[pl.BlockSpec(memory_space=pltpu.VMEM)] * 2,
+        out_specs=pl.BlockSpec(memory_space=pltpu.VMEM),
         cost_estimate=pl.CostEstimate(flops=2**32, bytes_accessed=1024, transcendentals=0),
         name="slot_table",
-    )(block_list, live_count)
+    )(block_list, live_count.reshape(1, 1))
 
 
 def add_some(grad_ref, parts_ref, tiles, start, count, labels_at):
@@ -129,6 +135,93 @@
     return core, jnp.where(row == 0, outer, loop_size // 2 - 1 - outer)
 
 
+def table_kernel(loop_size, origins, list_ref, count_ref, table_ref):
+    chips = loop_size // 2
+    lane = lax.broadcasted_iota(jnp.int32, table_ref.shape, 1)
+    core, position = core_and_position(loop_size)
+    hops, other = jnp.zeros_like(lane), jnp.zeros_like(lane)
+    for at, origin in enumerate(origins):
+        hops = jnp.where(lane == at, origin[0], hops)
+        other = jnp.where(lane == at, origin[1], other)
+    at = (position + chips + jnp.where(core == 0, -hops, hops)) & (chips - 1)
+    chip = jnp.where(at < chips // 2, 2 * at, 2 * (chips - 1 - at) + 1)
+    block = 2 * chip + jnp.where(other == 1, 1 - core, core)
+    found = jnp.full_like(lane, -1)
+    for slot in range(list_ref.shape[1]):
+        name = jnp.where(slot < count_ref[...], list_ref[:, slot : slot + 1], -1)
+        found = jnp.where(name == block, slot, found)
+    table_ref[...] = jnp.where(lane < len(origins), found, -1)
+
+
+def slot_table(loop_size, origins, block_list, live_count):
+    return pl.pallas_call(
+        functools.partial(table_kernel, loop_size, origins),
+        out_shape=jax.ShapeDtypeStruct((1, 128), jnp.int32),
+        in_specs=[pl.BlockSpec(memory_space=pltpu.VMEM)] * 2,
+        out_specs=pl.BlockSpec(memory_space=pltpu.VMEM),
+        cost_estimate=pl.CostEstimate(flops=2**32, bytes_accessed=1024, transcendentals=0),
+        name="slot_table",
+    )(block_list, live_count.reshape(1, 1))
+
+
+def add_some(grad_ref, parts_ref, tiles, start, count, labels_at):
+    rows = grad_ref.shape[0]
+    tile = tiles.shape[0] // CHUNK
+    block = tiles[pl.ds(pl.multiple_of(start * tile, 2 * tile), count * tile), :]
+    upper, lower = [], []
+    for at in range(0, count, 2):
+        both = lax.dot_general(
+            parts_ref[...],
+            block[at * tile : (at + 2) * tile],
+            (((1,), (1,)), ((), ())),
+            preferred_element_type=jnp.float32,
+        )
+        labels = jnp.concatenate([labels_at(start + at), labels_at(start + at + 1)], 1)
+        residual = 0.5 * jnp.tanh(both[:rows] + both[rows:]) + (0.5 - labels.astype(jnp.float32))
+        upper.append(residual.astype(jnp.bfloat16))
+        lower.append((residual - upper[-1].astype(jnp.float32)).astype(jnp.bfloat16))
+    grad_ref[...] += jnp.dot(
+        jnp.concatenate(upper + lower, 1),
+        jnp.concatenate([block, block], 0),
+        preferred_element_type=jnp.float32,
+    )
+
+
+def add_tiles(grad_ref, parts_ref, tiles, live, most, labels_at):
+    tile = tiles.shape[0] // CHUNK
+
+    @pl.when(live % 2 == 1)
+    def _():
+        blank = pl.multiple_of(live * tile, tile)
+        tiles[pl.ds(blank, tile), :] = jnp.zeros((tile, tiles.shape[1]), tiles.dtype)
+
+    fours = (live + 1) // 4 if most > 2 else jnp.int32(0)
+    if most > 2:
+
+        def four(index, carry):
+            add_some(grad_ref, parts_ref, tiles, index * 4, 4, labels_at)
+            return carry
+
+        lax.fori_loop(0, fours, four, 0)
+
+    @pl.when(live > 4 * fours)
+    def _():
+        add_some(grad_ref, parts_ref, tiles, 4 * fours, 2, labels_at)
+
+
+def store_square(grad_ref, square_ref):
+    gradient = grad_ref[...]
+    square = jnp.sum(gradient * gradient, axis=0, keepdims=True)
+    square = sum(square[:, at : at + 128] for at in range(0, square.shape[1], 128))
+    square_ref[...] = jnp.broadcast_to(square, square_ref.shape)
+
+
+def core_and_position(loop_size):
+    me = lax.axis_index("loop")
+    core, row, outer = me % 2, me // 2 % 2, me // 4
+    return core, jnp.where(row == 0, outer, loop_size // 2 - 1 - outer)
+
+
 def origin_block(origin, loop_size):
     hops, other = origin
     chips = loop_size // 2
@@ -163,8 +256,9 @@
         parts_ref[...] = halves(0.5 * given_ref[...])
         grad_ref[...] = jnp.zeros_like(grad_ref)
     live = jnp.int32(0)
-    for at, index, row in places:
-        found = table_ref[at]
+    table = table_ref[...]
+    entries = [table[0, at] for at, _, _ in places]
+    for found, (_, index, row) in zip(entries, places):
 
         @pl.when(found >= 0)
         def _():
@@ -203,8 +297,7 @@
     return pl.pallas_call(
         functools.partial(pieces_kernel, places, len(arrays), packed, loop_size, first, last),
         out_shape=out_shape,
-        in_specs=[pl.BlockSpec(memory_space=pltpu.SMEM)]
-        + [pl.BlockSpec(memory_space=pltpu.VMEM)] * (2 + len(arrays) + len(extra)),
+        in_specs=[pl.BlockSpec(memory_space=pltpu.VMEM)] * (3 + len(arrays) + len(extra)),
         out_specs=[pl.BlockSpec(memory_space=pltpu.VMEM)] * len(out_shape),
         input_output_aliases={} if first else {3 + len(arrays): 0},
         scratch_shapes=[

time: 37.4 us -> 36.6 us (0.979); the launches traced: 37.5 us -> 36 us
  waiting for transfers between devices: 4.81 us -> 8.46 us
  starting transfers between devices: 13.1 us -> 10.1 us
  Pallas kernels: 6.45 us -> 4.07 us
    pallas_call x5, Pallas kernels: 4.02 us -> 1.69 us  [add_pieces(): pl.pallas_call(functools.partial(pieces_kernel, places, len(arrays), pack...]
    ppermute x3, starting transfers between devices: 1.87 us -> 0.14 us  [to_other_core(): lax.ppermute(array, 'loop', [(at, at ^ 1) for at in range(loop_size)])]
    ppermute x3, waiting for transfers between devices: 0.01 us -> 1.53 us  [to_other_core(): lax.ppermute(array, 'loop', [(at, at ^ 1) for at in range(loop_size)])]
    ppermute x6, starting transfers between devices: 7.88 us -> 6.55 us  [to_next(): return lax.ppermute(array, 'loop', pairs)]
    ppermute x6, waiting for transfers between devices: 4.33 us -> 5.49 us  [to_next(): return lax.ppermute(array, 'loop', pairs)]
    ppermute x1, waiting for transfers between devices: 0.47 us -> 1.44 us  [across(): return lax.ppermute(array, 'loop', pairs)]
  transfers between devices with their start and end apart: 10 -> 10, of which waited for: 4 -> 6; matrix products, arithmetic and copies ran while one was open for 0% -> 0% of each run, Pallas kernels for 13% -> 8%
where the time goes in v8:
time: 36.6 us; the launch traced here: 36 us
  blocking collectives  12.1 us (33%)
  starting transfers between devices  10.1 us (28%)
  waiting for transfers between devices  8.46 us (23%)
  Pallas kernels  4.07 us (11%)
  between operations  0.76 us (2%)
  local copies, waits for them, and re-layouts  0.58 us (2%)
    all_to_all x1, blocking collectives, local(): squares = lax.all_to_all(square, 'loop', 0, 0, tiled=True)  12.1 us
    ppermute x6, starting transfers between devices, to_next(): return lax.ppermute(array, 'loop', pairs)  6.55 us
    ppermute x6, waiting for transfers between devices, to_next(): return lax.ppermute(array, 'loop', pairs)  5.49 us
    ppermute x1, starting transfers between devices, across(): return lax.ppermute(array, 'loop', pairs)  3.37 us
    pallas_call x5, Pallas kernels, add_pieces(): pl.pallas_call(functools.partial(pieces_kernel, places, len(arrays), pack...  1.69 us
    ppermute x3, waiting for transfers between devices, to_other_core(): lax.ppermute(array, 'loop', [(at, at ^ 1) for at in range(loop_size)])  1.53 us
    ppermute x1, waiting for transfers between devices, across(): return lax.ppermute(array, 'loop', pairs)  1.44 us
    pallas_call x1, Pallas kernels, slot_table(): pl.pallas_call(functools.partial(table_kernel, loop_size, origins), out_s...  1.41 us
  transfers between devices with their start and end apart: 10, of which 6 were waited for; matrix products, arithmetic and copies ran while one was open for 0% of the time, Pallas kernels for 8%

profile of v8, /device:TPU:0, one launch (start us, length us, event | category | flops | bytes accessed | tf_op | source)
XLA Modules:
  0.0 36.0 jit_solution(15514521845804017689)
XLA Ops:
  0.0 3.0 %collective-permute-start = (bf16[128,512]{1,0:T(8,128)(2,1)}, bf16[128,512]{1,0:T(8,128)(2,1)S(1)}, u32[]{:S(2)}, u32[]{:S(2)}) collective-permute-start(bf16[128,512]{1,0:T(8,128)(2,1)} %rest_0_.1), channel_id=1, source_target_pairs={{0,4},{4,8},{8,12},{12,14},{14,10},{10,6},{6,2},{2,0},{1,3},{5,1},... | collective-permute-start | bytes 393224 | tf_op jit(solution)/shard_map/ppermute | solution.py:29
  3.0 0.0 collective-permute-start.1
  3.7 0.0 copy-start
  3.7 0.0 copy-start.1
  3.7 0.0 copy-start.2
  3.7 1.4 %slot_table.1.table_ref = s32[1,128]{1,0:T(1,128)} custom-call(s32[1,8]{1,0:T(1,128)} %list_ref.1, s32[1,1]{1,0:T(1,128)} %bitcast.5.count_ref), custom_call_target="tpu_custom_call" | custom-call | flops 4294967296 | bytes 1024 | tf_op jit(solution)/shard_map/slot_table/pallas_call | solution.py:157
  5.1 1.9 %collective-permute-done.rest_1_ = bf16[128,512]{1,0:T(8,128)(2,1)S(1)} collective-permute-done((bf16[128,512]{1,0:T(8,128)(2,1)}, bf16[128,512]{1,0:T(8,128)(2,1)S(1)}, u32[]{:S(2)}, u32[]{:S(2)}) %collective-permute-start) | collective-permute-done | bytes 131104 | tf_op jit(solution)/shard_map/ppermute | solution.py:29
  7.0 1.5 %collective-permute-start.2 = (bf16[128,512]{1,0:T(8,128)(2,1)S(1)}, bf16[128,512]{1,0:T(8,128)(2,1)S(1)}, u32[]{:S(2)}, u32[]{:S(2)}) collective-permute-start(bf16[128,512]{1,0:T(8,128)(2,1)S(1)} %collective-permute-done.rest_1_), channel_id=1, source_target_pairs={{0,4},{4,8},{8,12},{12,14},{14,10},{10,6},{6,2},{2,0},{1,3},{5,1},... | collective-permute-start | bytes 393224 | tf_op jit(solution)/shard_map/ppermute | solution.py:29
  8.5 0.0 collective-permute-done.1.rest_2_
  8.5 0.9 %collective-permute-start.4 = (bf16[128,512]{1,0:T(8,128)(2,1)S(1)}, bf16[128,512]{1,0:T(8,128)(2,1)S(1)}, u32[]{:S(2)}, u32[]{:S(2)}) collective-permute-start(bf16[128,512]{1,0:T(8,128)(2,1)S(1)} %collective-permute-done.1.rest_2_), channel_id=1, source_target_pairs={{0,2},{4,0},{8,4},{12,8},{14,12},{10,14},{6,10},{2,6},{1,5},{5,9},... | collective-permute-start | bytes 393224 | tf_op jit(solution)/shard_map/ppermute | solution.py:29
  9.4 0.0 copy-done
  9.4 0.0 copy-done.1
  9.4 0.0 copy-done.2
  9.4 0.0 copy-start.3
  9.4 0.6 %copy-done.3 = s32[1,128]{1,0:T(1,128)S(1)} copy-done((s32[1,128]{1,0:T(1,128)S(1)}, s32[1,128]{1,0:T(1,128)}, u32[]{:S(2)}) %copy-start.3) | copy-done | bytes 536
  10.0 0.3 add_pieces.5
  10.3 3.4 %collective-permute-start.6 = (bf16[128,512]{1,0:T(8,128)(2,1)S(1)}, bf16[128,512]{1,0:T(8,128)(2,1)S(1)}, u32[]{:S(2)}, u32[]{:S(2)}) collective-permute-start(bf16[128,512]{1,0:T(8,128)(2,1)S(1)} %get-tuple-element.20), channel_id=1, source_target_pairs={{0,12},{1,13},{4,6},{5,7},{8,10},{9,11},{12,0},{13,1},{14,2},{15,3... | collective-permute-start | bytes 393224 | tf_op jit(solution)/shard_map/ppermute | solution.py:39
  13.6 0.0 collective-permute-start.8
  13.6 0.0 collective-permute-done.2.rest_0_
  13.6 0.3 collective-permute-start.3
  13.9 0.9 %collective-permute-done.4.rest_1_ = bf16[128,512]{1,0:T(8,128)(2,1)S(1)} collective-permute-done((bf16[128,512]{1,0:T(8,128)(2,1)S(1)}, bf16[128,512]{1,0:T(8,128)(2,1)S(1)}, u32[]{:S(2)}, u32[]{:S(2)}) %collective-permute-start.4) | collective-permute-done | bytes 131104 | tf_op jit(solution)/shard_map/ppermute | solution.py:29
  14.9 0.8 %collective-permute-start.5 = (bf16[128,512]{1,0:T(8,128)(2,1)S(1)}, bf16[128,512]{1,0:T(8,128)(2,1)S(1)}, u32[]{:S(2)}, u32[]{:S(2)}) collective-permute-start(bf16[128,512]{1,0:T(8,128)(2,1)S(1)} %collective-permute-done.4.rest_1_), channel_id=1, source_target_pairs={{0,2},{4,0},{8,4},{12,8},{14,12},{10,14},{6,10},{2,6},{1,5},{5,9},... | collective-permute-start | bytes 393224 | tf_op jit(solution)/shard_map/ppermute | solution.py:29
  15.7 0.1 add_pieces.6
  15.8 0.1 collective-permute-start.9
  15.9 1.4 %collective-permute-done.6.rest_2_ = bf16[128,512]{1,0:T(8,128)(2,1)S(1)} collective-permute-done((bf16[128,512]{1,0:T(8,128)(2,1)S(1)}, bf16[128,512]{1,0:T(8,128)(2,1)S(1)}, u32[]{:S(2)}, u32[]{:S(2)}) %collective-permute-start.6) | collective-permute-done | bytes 131104 | tf_op jit(solution)/shard_map/ppermute | solution.py:39
  17.3 1.9 %collective-permute-done.3.rest_0_ = bf16[128,512]{1,0:T(8,128)(2,1)S(1)} collective-permute-done((bf16[128,512]{1,0:T(8,128)(2,1)S(1)}, bf16[128,512]{1,0:T(8,128)(2,1)S(1)}, u32[]{:S(2)}, u32[]{:S(2)}) %collective-permute-start.3) | collective-permute-done | bytes 131104 | tf_op jit(solution)/shard_map/ppermute | solution.py:29
  19.2 0.8 %collective-permute-done.5.rest_1_ = bf16[128,512]{1,0:T(8,128)(2,1)S(1)} collective-permute-done((bf16[128,512]{1,0:T(8,128)(2,1)S(1)}, bf16[128,512]{1,0:T(8,128)(2,1)S(1)}, u32[]{:S(2)}, u32[]{:S(2)}) %collective-permute-start.5) | collective-permute-done | bytes 131104 | tf_op jit(solution)/shard_map/ppermute | solution.py:29
  20.0 0.9 %add_pieces.7 = (f32[256,512]{1,0:T(8,128)S(1)}, bf16[384,512]{1,0:T(8,128)(2,1)S(1)}) custom-call(s32[1,128]{1,0:T(1,128)S(1)} %copy-done.3, bf16[512,512]{1,0:T(8,128)(2,1)S(1)} %get-tuple-element.19.given_ref, s32[256,1024]{1,0:T(8,128)S(1)} %copy-done.1, bf16[128,512]{1,0:T(8,128)(2,1)S(1)} %collective-permute-done.3.rest_0_, ...), custom_call_target="tpu_custom_call", output_to_operand_aliasing={{0}: (6, {})} | custom-call | flops 6442450944 | bytes 1048576 | tf_op jit(solution)/shard_map/add_pieces/pallas_call | solution.py:297
  21.0 0.1 collective-permute-start.7
  21.0 0.0 collective-permute-done.8.rest_0_
  21.1 0.0 collective-permute-done.9.rest_1_
  21.1 0.2 add_pieces.8.rest_1_
  21.2 1.5 %collective-permute-done.7.rest_0_ = bf16[384,512]{1,0:T(8,128)(2,1)S(1)} collective-permute-done((bf16[384,512]{1,0:T(8,128)(2,1)S(1)}, bf16[384,512]{1,0:T(8,128)(2,1)S(1)}, u32[]{:S(2)}, u32[]{:S(2)}) %collective-permute-start.7) | collective-permute-done | bytes 393248 | tf_op jit(solution)/shard_map/ppermute | solution.py:43
  22.8 0.2 add_pieces.9
  23.0 12.1 %all_to_all.11 = f32[16,1,128]{2,1,0:T(1,128)S(1)} all-to-all(f32[16,1,128]{2,1,0:T(1,128)S(1)} %bitcast.7), channel_id=1, replica_groups=mesh['group'=2,'loop'=16] {'loop'}, dimensions={0} | all-to-all | bytes 16384 | tf_op jit(solution)/shard_map/all_to_all | solution.py:439
  35.0 1.0 %update.1 = f32[256,512]{1,0:T(8,128)} custom-call(f32[256,512]{1,0:T(8,128)S(1)} %copy-done, f32[256,512]{1,0:T(8,128)S(1)} %get-tuple-element.27.grad_ref, f32[16,128]{1,0:T(8,128)S(1)} %bitcast.6), custom_call_target="tpu_custom_call" | custom-call | flops 262144 | bytes 1572864 | tf_op jit(solution)/shard_map/update/pallas_call | solution.py:440
Async XLA Ops:
  0.0 7.0 %collective-permute-start = (bf16[128,512]{1,0:T(8,128)(2,1)}, bf16[128,512]{1,0:T(8,128)(2,1)S(1)}, u32[]{:S(2)}, u32[]{:S(2)}) collective-permute-start(bf16[128,512]{1,0:T(8,128)(2,1)} %rest_0_.1), channel_id=1, source_target_pairs={{0,4},{4,8},{8,12},{12,14},{14,10},{10,6},{6,2},{2,0},{1,3},{5,1},... | collective-permute-start | bytes 393224 | tf_op jit(solution)/shard_map/ppermute | solution.py:29
  3.0 5.5 %collective-permute-start.1 = (bf16[128,512]{1,0:T(8,128)(2,1)}, bf16[128,512]{1,0:T(8,128)(2,1)S(1)}, u32[]{:S(2)}, u32[]{:S(2)}) collective-permute-start(bf16[128,512]{1,0:T(8,128)(2,1)} %rest_0_.1), channel_id=1, source_target_pairs={{0,2},{4,0},{8,4},{12,8},{14,12},{10,14},{6,10},{2,6},{1,5},{5,9},... | collective-permute-start | bytes 393224 | tf_op jit(solution)/shard_map/ppermute | solution.py:29
  3.7 5.7 %copy-start = (f32[256,512]{1,0:T(8,128)S(1)}, f32[256,512]{1,0:T(8,128)}, u32[]{:S(2)}) copy-start(f32[256,512]{1,0:T(8,128)} %users_ref.1) | copy-start | bytes 1572868
  3.7 5.7 %copy-start.1 = (s32[256,1024]{1,0:T(8,128)S(1)}, s32[256,1024]{1,0:T(8,128)}, u32[]{:S(2)}) copy-start(s32[256,1024]{1,0:T(8,128)} %labels_ref.9) | copy-start | bytes 3145732
  3.7 5.7 %copy-start.2 = (bf16[128,512]{1,0:T(8,128)(2,1)S(1)}, bf16[128,512]{1,0:T(8,128)(2,1)}, u32[]{:S(2)}) copy-start(bf16[128,512]{1,0:T(8,128)(2,1)} %rest_0_.1) | copy-start | bytes 393220
  7.0 6.7 %collective-permute-start.2 = (bf16[128,512]{1,0:T(8,128)(2,1)S(1)}, bf16[128,512]{1,0:T(8,128)(2,1)S(1)}, u32[]{:S(2)}, u32[]{:S(2)}) collective-permute-start(bf16[128,512]{1,0:T(8,128)(2,1)S(1)} %collective-permute-done.rest_1_), channel_id=1, source_target_pairs={{0,4},{4,8},{8,12},{12,14},{14,10},{10,6},{6,2},{2,0},{1,3},{5,1},... | collective-permute-start | bytes 393224 | tf_op jit(solution)/shard_map/ppermute | solution.py:29
  8.5 6.4 %collective-permute-start.4 = (bf16[128,512]{1,0:T(8,128)(2,1)S(1)}, bf16[128,512]{1,0:T(8,128)(2,1)S(1)}, u32[]{:S(2)}, u32[]{:S(2)}) collective-permute-start(bf16[128,512]{1,0:T(8,128)(2,1)S(1)} %collective-permute-done.1.rest_2_), channel_id=1, source_target_pairs={{0,2},{4,0},{8,4},{12,8},{14,12},{10,14},{6,10},{2,6},{1,5},{5,9},... | collective-permute-start | bytes 393224 | tf_op jit(solution)/shard_map/ppermute | solution.py:29
  9.4 0.6 %copy-start.3 = (s32[1,128]{1,0:T(1,128)S(1)}, s32[1,128]{1,0:T(1,128)}, u32[]{:S(2)}) copy-start(s32[1,128]{1,0:T(1,128)} %slot_table.1.table_ref) | copy-start | bytes 1540
  10.3 7.1 %collective-permute-start.6 = (bf16[128,512]{1,0:T(8,128)(2,1)S(1)}, bf16[128,512]{1,0:T(8,128)(2,1)S(1)}, u32[]{:S(2)}, u32[]{:S(2)}) collective-permute-start(bf16[128,512]{1,0:T(8,128)(2,1)S(1)} %get-tuple-element.20), channel_id=1, source_target_pairs={{0,12},{1,13},{4,6},{5,7},{8,10},{9,11},{12,0},{13,1},{14,2},{15,3... | collective-permute-start | bytes 393224 | tf_op jit(solution)/shard_map/ppermute | solution.py:39
  13.6 7.4 %collective-permute-start.8 = (bf16[384,512]{1,0:T(8,128)(2,1)S(1)}, bf16[384,512]{1,0:T(8,128)(2,1)S(1)}, u32[]{:S(2)}, u32[]{:S(2)}) collective-permute-start(bf16[384,512]{1,0:T(8,128)(2,1)S(1)} %get-tuple-element.24), channel_id=1, source_target_pairs={{0,1},{1,0},{2,3},{3,2},{4,5},{5,4},{6,7},{7,6},{8,9},{9,8},{10,11... | collective-permute-start | bytes 1179656 | tf_op jit(solution)/shard_map/ppermute | solution.py:43
  13.6 5.6 %collective-permute-start.3 = (bf16[128,512]{1,0:T(8,128)(2,1)S(1)}, bf16[128,512]{1,0:T(8,128)(2,1)S(1)}, u32[]{:S(2)}, u32[]{:S(2)}) collective-permute-start(bf16[128,512]{1,0:T(8,128)(2,1)S(1)} %collective-permute-done.2.rest_0_), channel_id=1, source_target_pairs={{0,4},{4,8},{8,12},{12,14},{14,10},{10,6},{6,2},{2,0},{1,3},{5,1},... | collective-permute-start | bytes 393224 | tf_op jit(solution)/shard_map/ppermute | solution.py:29
  14.9 5.2 %collective-permute-start.5 = (bf16[128,512]{1,0:T(8,128)(2,1)S(1)}, bf16[128,512]{1,0:T(8,128)(2,1)S(1)}, u32[]{:S(2)}, u32[]{:S(2)}) collective-permute-start(bf16[128,512]{1,0:T(8,128)(2,1)S(1)} %collective-permute-done.4.rest_1_), channel_id=1, source_target_pairs={{0,2},{4,0},{8,4},{12,8},{14,12},{10,14},{6,10},{2,6},{1,5},{5,9},... | collective-permute-start | bytes 393224 | tf_op jit(solution)/shard_map/ppermute | solution.py:29
  15.8 5.2 %collective-permute-start.9 = (bf16[256,512]{1,0:T(8,128)(2,1)S(1)}, bf16[256,512]{1,0:T(8,128)(2,1)S(1)}, u32[]{:S(2)}, u32[]{:S(2)}) collective-permute-start(bf16[256,512]{1,0:T(8,128)(2,1)S(1)} %get-tuple-element.25), channel_id=1, source_target_pairs={{0,1},{1,0},{2,3},{3,2},{4,5},{5,4},{6,7},{7,6},{8,9},{9,8},{10,11... | collective-permute-start | bytes 786440 | tf_op jit(solution)/shard_map/ppermute | solution.py:43
  21.0 1.8 %collective-permute-start.7 = (bf16[384,512]{1,0:T(8,128)(2,1)S(1)}, bf16[384,512]{1,0:T(8,128)(2,1)S(1)}, u32[]{:S(2)}, u32[]{:S(2)}) collective-permute-start(bf16[384,512]{1,0:T(8,128)(2,1)S(1)} %get-tuple-element.23), channel_id=1, source_target_pairs={{0,1},{1,0},{2,3},{3,2},{4,5},{5,4},{6,7},{7,6},{8,9},{9,8},{10,11... | collective-permute-start | bytes 1179656 | tf_op jit(solution)/shard_map/ppermute | solution.py:43

commit v9 on v8

--- a/solution.py
+++ b/solution.py
@@ -72,6 +72,7 @@
         out_shape=jax.ShapeDtypeStruct((1, 128), jnp.int32),
         in_specs=[pl.BlockSpec(memory_space=pltpu.VMEM)] * 2,
         out_specs=pl.BlockSpec(memory_space=pltpu.VMEM),
+        compiler_params=pltpu.CompilerParams(vmem_limit_bytes=16 * 1024 * 1024),
         cost_estimate=pl.CostEstimate(flops=2**32, bytes_accessed=1024, transcendentals=0),
         name="slot_table",
     )(block_list, live_count.reshape(1, 1))
@@ -159,6 +160,7 @@
         out_shape=jax.ShapeDtypeStruct((1, 128), jnp.int32),
         in_specs=[pl.BlockSpec(memory_space=pltpu.VMEM)] * 2,
         out_specs=pl.BlockSpec(memory_space=pltpu.VMEM),
+        compiler_params=pltpu.CompilerParams(vmem_limit_bytes=16 * 1024 * 1024),
         cost_estimate=pl.CostEstimate(flops=2**32, bytes_accessed=1024, transcendentals=0),
         name="slot_table",
     )(block_list, live_count.reshape(1, 1))
@@ -292,7 +294,7 @@
     if packed:
         out_shape.append(jax.ShapeDtypeStruct((len(packed) * tile, width), jnp.bfloat16))
     if last:
-        out_shape.append(jax.ShapeDtypeStruct((loop_size, 128), jnp.float32))
+        out_shape.append(jax.ShapeDtypeStruct((len(sum_groups(loop_size)[0][0]), 128), jnp.float32))
     extra = [] if first else [before]
     return pl.pallas_call(
         functools.partial(pieces_kernel, places, len(arrays), packed, loop_size, first, last),
@@ -385,12 +387,13 @@
     rows, width = users.shape
     slots = lists[0].shape[1]
     tile = labels.shape[1] // slots
+    near = len(sum_groups(loop_size)[0][0])
     return pl.pallas_call(
         chunks_kernel,
         grid=(slots // CHUNK,),
         out_shape=[
             jax.ShapeDtypeStruct((rows, width), jnp.float32),
-            jax.ShapeDtypeStruct((loop_size, 128), jnp.float32),
+            jax.ShapeDtypeStruct((near, 128), jnp.float32),
         ],
         in_specs=[
             pl.BlockSpec(memory_space=pltpu.SMEM),
@@ -401,7 +404,7 @@
         ],
         out_specs=[
             pl.BlockSpec((rows, width), lambda step: (0, 0)),
-            pl.BlockSpec((loop_size, 128), lambda step: (0, 0)),
+            pl.BlockSpec((near, 128), lambda step: (0, 0)),
         ],
         scratch_shapes=[
             pltpu.VMEM((CHUNK * tile, width), jnp.bfloat16),
@@ -418,6 +421,31 @@
     )(*lists, users, labels, items)
 
 
+def sum_groups(loop_size):
+    near = 4 if loop_size % 4 == 0 else 1
+    starts = range(0, loop_size, near)
+    return [
+        [[start + at for at in range(near)] for start in starts],
+        [[start + at for start in starts] for at in range(near)],
+    ]
+
+
+def spread_kernel(squares_ref, sums_ref):
+    total = jnp.sum(squares_ref[...], axis=0, keepdims=True)
+    sums_ref[...] = jnp.broadcast_to(total, sums_ref.shape)
+
+
+def spread_sum(squares, copies):
+    return pl.pallas_call(
+        spread_kernel,
+        out_shape=jax.ShapeDtypeStruct((copies, squares.shape[1]), jnp.float32),
+        in_specs=[pl.BlockSpec(memory_space=pltpu.VMEM)],
+        out_specs=pl.BlockSpec(memory_space=pltpu.VMEM),
+        compiler_params=pltpu.CompilerParams(vmem_limit_bytes=16 * 1024 * 1024),
+        name="spread_sum",
+    )(squares)
+
+
 def update_kernel(entries, users_ref, grad_ref, squares_ref, out_ref):
     total = jnp.sum(squares_ref[...], axis=0, keepdims=True)
     total = jnp.sum(total, axis=1, keepdims=True)
@@ -436,7 +464,10 @@
         whole = lax.all_gather(items, "loop", axis=0, tiled=True)
         gradient, square = add_chunks(loop_size, whole, lists, users, labels)
 
-    squares = lax.all_to_all(square, "loop", 0, 0, tiled=True)
+    near, far = sum_groups(loop_size)
+    square = lax.all_to_all(square, "loop", 0, 0, axis_index_groups=near, tiled=True)
+    square = spread_sum(square, len(far[0]))
+    squares = lax.all_to_all(square, "loop", 0, 0, axis_index_groups=far, tiled=True)
     return pl.pallas_call(
         functools.partial(update_kernel, rows * loop_size * width),
         out_shape=jax.ShapeDtypeStruct((rows, width), jnp.float32),

time: 36.6 us -> 40.7 us (1.11); the launches traced: 36 us -> 40.7 us
  blocking collectives: 12.1 us -> 16.9 us
  Pallas kernels: 4.07 us -> 2.84 us
  starting transfers between devices: 10.1 us -> 10.9 us
    all_to_all x1 -> x2, blocking collectives: 12.1 us -> 16.9 us  [the longest x1 8.82 us: local(): lax.all_to_all(square, 'loop', 0, 0, axis_index_groups=far, tiled=True)]
    pallas_call x1, Pallas kernels: 1.41 us -> 0.15 us  [slot_table(): pl.pallas_call(functools.partial(table_kernel, loop_size, origins), out_s...]
    ppermute x3, starting transfers between devices: 0.14 us -> 1.05 us  [to_other_core(): lax.ppermute(array, 'loop', [(at, at ^ 1) for at in range(loop_size)])]
    ppermute x6, waiting for transfers between devices: 5.49 us -> 6.18 us  [to_next(): return lax.ppermute(array, 'loop', pairs)]
  transfers between devices with their start and end apart: 10 -> 10, of which waited for: 6 -> 6; matrix products, arithmetic and copies ran while one was open for 0% -> 0% of each run, Pallas kernels for 8% -> 4%
where the time goes in v9:
time: 40.7 us
  blocking collectives  16.9 us (42%)
  starting transfers between devices  10.9 us (27%)
  waiting for transfers between devices  8.72 us (21%)
  Pallas kernels  2.84 us (7%)
  between operations  0.73 us (2%)
  local copies, waits for them, and re-layouts  0.66 us (2%)
    all_to_all x1, blocking collectives, local(): lax.all_to_all(square, 'loop', 0, 0, axis_index_groups=far, tiled=True)  8.82 us
    all_to_all x1, blocking collectives, local(): lax.all_to_all(square, 'loop', 0, 0, axis_index_groups=near, tiled=True)  8.05 us
    ppermute x6, starting transfers between devices, to_next(): return lax.ppermute(array, 'loop', pairs)  6.48 us
    ppermute x6, waiting for transfers between devices, to_next(): return lax.ppermute(array, 'loop', pairs)  6.18 us
    ppermute x1, starting transfers between devices, across(): return lax.ppermute(array, 'loop', pairs)  3.37 us
    pallas_call x5, Pallas kernels, add_pieces(): pl.pallas_call(functools.partial(pieces_kernel, places, len(arrays), pack...  1.7 us
    ppermute x1, waiting for transfers between devices, across(): return lax.ppermute(array, 'loop', pairs)  1.36 us
    ppermute x3, waiting for transfers between devices, to_other_core(): lax.ppermute(array, 'loop', [(at, at ^ 1) for at in range(loop_size)])  1.19 us
  transfers between devices with their start and end apart: 10, of which 6 were waited for; matrix products, arithmetic and copies ran while one was open for 0% of the time, Pallas kernels for 4%

profile of v9, /device:TPU:0, one launch (start us, length us, event | category | flops | bytes accessed | tf_op | source)
XLA Modules:
  0.0 40.7 jit_solution(13759817093514921584)
XLA Ops:
  0.0 3.0 %collective-permute-start = (bf16[128,512]{1,0:T(8,128)(2,1)}, bf16[128,512]{1,0:T(8,128)(2,1)S(1)}, u32[]{:S(2)}, u32[]{:S(2)}) collective-permute-start(bf16[128,512]{1,0:T(8,128)(2,1)} %rest_0_.1), channel_id=1, source_target_pairs={{0,4},{4,8},{8,12},{12,14},{14,10},{10,6},{6,2},{2,0},{1,3},{5,1},... | collective-permute-start | bytes 393224 | tf_op jit(solution)/shard_map/ppermute | solution.py:29
  3.0 0.0 collective-permute-start.1
  3.7 0.0 copy-start.3
  3.7 0.6 %copy-done.3 = s32[1,8]{1,0:T(1,128)S(1)} copy-done((s32[1,8]{1,0:T(1,128)S(1)}, s32[1,8]{1,0:T(1,128)}, u32[]{:S(2)}) %copy-start.3) | copy-done | bytes 56
  4.3 0.0 copy-start
  4.3 0.0 copy-start.1
  4.3 0.0 copy-start.2
  4.3 0.1 slot_table.1.table_ref
  4.5 2.5 %collective-permute-done.rest_1_ = bf16[128,512]{1,0:T(8,128)(2,1)S(1)} collective-permute-done((bf16[128,512]{1,0:T(8,128)(2,1)}, bf16[128,512]{1,0:T(8,128)(2,1)S(1)}, u32[]{:S(2)}, u32[]{:S(2)}) %collective-permute-start) | collective-permute-done | bytes 131104 | tf_op jit(solution)/shard_map/ppermute | solution.py:29
  7.0 1.5 %collective-permute-start.2 = (bf16[128,512]{1,0:T(8,128)(2,1)S(1)}, bf16[128,512]{1,0:T(8,128)(2,1)S(1)}, u32[]{:S(2)}, u32[]{:S(2)}) collective-permute-start(bf16[128,512]{1,0:T(8,128)(2,1)S(1)} %collective-permute-done.rest_1_), channel_id=1, source_target_pairs={{0,4},{4,8},{8,12},{12,14},{14,10},{10,6},{6,2},{2,0},{1,3},{5,1},... | collective-permute-start | bytes 393224 | tf_op jit(solution)/shard_map/ppermute | solution.py:29
  8.5 0.0 collective-permute-done.1.rest_2_
  8.5 0.9 %collective-permute-start.4 = (bf16[128,512]{1,0:T(8,128)(2,1)S(1)}, bf16[128,512]{1,0:T(8,128)(2,1)S(1)}, u32[]{:S(2)}, u32[]{:S(2)}) collective-permute-start(bf16[128,512]{1,0:T(8,128)(2,1)S(1)} %collective-permute-done.1.rest_2_), channel_id=1, source_target_pairs={{0,2},{4,0},{8,4},{12,8},{14,12},{10,14},{6,10},{2,6},{1,5},{5,9},... | collective-permute-start | bytes 393224 | tf_op jit(solution)/shard_map/ppermute | solution.py:29
  9.4 0.0 copy-done
  9.4 0.0 copy-done.1
  9.4 0.0 copy-done.2
  9.4 1.1 %add_pieces.5 = (f32[256,512]{1,0:T(8,128)S(1)}, bf16[512,512]{1,0:T(8,128)(2,1)S(1)}, bf16[128,512]{1,0:T(8,128)(2,1)S(1)}, bf16[384,512]{1,0:T(8,128)(2,1)S(1)}) custom-call(s32[1,128]{1,0:T(1,128)S(1)} %slot_table.1.table_ref, f32[256,512]{1,0:T(8,128)S(1)} %copy-done, s32[256,1024]{1,0:T(8,128)S(1)} %copy-done.1, bf16[128,512]{1,0:T(8,128)(2,1)S(1)} %copy-done.2, ...), custom_call_target="tpu_custom_call" | custom-call | flops 6442450944 | bytes 1048576 | tf_op jit(solution)/shard_map/add_pieces/pallas_call | solution.py:299
  10.5 3.4 %collective-permute-start.6 = (bf16[128,512]{1,0:T(8,128)(2,1)S(1)}, bf16[128,512]{1,0:T(8,128)(2,1)S(1)}, u32[]{:S(2)}, u32[]{:S(2)}) collective-permute-start(bf16[128,512]{1,0:T(8,128)(2,1)S(1)} %get-tuple-element.20), channel_id=1, source_target_pairs={{0,12},{1,13},{4,6},{5,7},{8,10},{9,11},{12,0},{13,1},{14,2},{15,3... | collective-permute-start | bytes 393224 | tf_op jit(solution)/shard_map/ppermute | solution.py:39
  13.9 0.0 collective-permute-start.8
  13.9 0.0 collective-permute-done.2.rest_0_
  13.9 0.0 collective-permute-start.3
  13.9 1.0 %collective-permute-done.4.rest_1_ = bf16[128,512]{1,0:T(8,128)(2,1)S(1)} collective-permute-done((bf16[128,512]{1,0:T(8,128)(2,1)S(1)}, bf16[128,512]{1,0:T(8,128)(2,1)S(1)}, u32[]{:S(2)}, u32[]{:S(2)}) %collective-permute-start.4) | collective-permute-done | bytes 131104 | tf_op jit(solution)/shard_map/ppermute | solution.py:29
  14.9 1.0 %collective-permute-start.5 = (bf16[128,512]{1,0:T(8,128)(2,1)S(1)}, bf16[128,512]{1,0:T(8,128)(2,1)S(1)}, u32[]{:S(2)}, u32[]{:S(2)}) collective-permute-start(bf16[128,512]{1,0:T(8,128)(2,1)S(1)} %collective-permute-done.4.rest_1_), channel_id=1, source_target_pairs={{0,2},{4,0},{8,4},{12,8},{14,12},{10,14},{6,10},{2,6},{1,5},{5,9},... | collective-permute-start | bytes 393224 | tf_op jit(solution)/shard_map/ppermute | solution.py:29
  15.9 0.1 add_pieces.6
  16.0 0.1 collective-permute-start.9
  16.1 1.4 %collective-permute-done.6.rest_2_ = bf16[128,512]{1,0:T(8,128)(2,1)S(1)} collective-permute-done((bf16[128,512]{1,0:T(8,128)(2,1)S(1)}, bf16[128,512]{1,0:T(8,128)(2,1)S(1)}, u32[]{:S(2)}, u32[]{:S(2)}) %collective-permute-start.6) | collective-permute-done | bytes 131104 | tf_op jit(solution)/shard_map/ppermute | solution.py:39
  17.5 2.0 %collective-permute-done.3.rest_0_ = bf16[128,512]{1,0:T(8,128)(2,1)S(1)} collective-permute-done((bf16[128,512]{1,0:T(8,128)(2,1)S(1)}, bf16[128,512]{1,0:T(8,128)(2,1)S(1)}, u32[]{:S(2)}, u32[]{:S(2)}) %collective-permute-start.3) | collective-permute-done | bytes 131104 | tf_op jit(solution)/shard_map/ppermute | solution.py:29
  19.4 0.7 %collective-permute-done.5.rest_1_ = bf16[128,512]{1,0:T(8,128)(2,1)S(1)} collective-permute-done((bf16[128,512]{1,0:T(8,128)(2,1)S(1)}, bf16[128,512]{1,0:T(8,128)(2,1)S(1)}, u32[]{:S(2)}, u32[]{:S(2)}) %collective-permute-start.5) | collective-permute-done | bytes 131104 | tf_op jit(solution)/shard_map/ppermute | solution.py:29
  20.2 0.1 add_pieces.7
  20.3 1.0 %collective-permute-start.7 = (bf16[384,512]{1,0:T(8,128)(2,1)S(1)}, bf16[384,512]{1,0:T(8,128)(2,1)S(1)}, u32[]{:S(2)}, u32[]{:S(2)}) collective-permute-start(bf16[384,512]{1,0:T(8,128)(2,1)S(1)} %get-tuple-element.23), channel_id=1, source_target_pairs={{0,1},{1,0},{2,3},{3,2},{4,5},{5,4},{6,7},{7,6},{8,9},{9,8},{10,11... | collective-permute-start | bytes 1179656 | tf_op jit(solution)/shard_map/ppermute | solution.py:43
  21.3 0.0 collective-permute-done.8.rest_0_
  21.3 0.0 collective-permute-done.9.rest_1_
  21.3 0.2 add_pieces.8.rest_1_
  21.5 1.2 %collective-permute-done.7.rest_0_ = bf16[384,512]{1,0:T(8,128)(2,1)S(1)} collective-permute-done((bf16[384,512]{1,0:T(8,128)(2,1)S(1)}, bf16[384,512]{1,0:T(8,128)(2,1)S(1)}, u32[]{:S(2)}, u32[]{:S(2)}) %collective-permute-start.7) | collective-permute-done | bytes 393248 | tf_op jit(solution)/shard_map/ppermute | solution.py:43
  22.6 0.2 add_pieces.9
  22.8 8.0 %all_to_all.22 = f32[4,1,128]{2,1,0:T(1,128)S(1)} all-to-all(f32[4,1,128]{2,1,0:T(1,128)S(1)} %bitcast.13), channel_id=1, replica_groups={{0,1,2,3},{4,5,6,7},{8,9,10,11},{12,13,14,15},{16,17,18,19},{20,21,22,2..., dimensions={0} | all-to-all | bytes 4096 | tf_op jit(solution)/shard_map/all_to_all | solution.py:468
  30.9 8.8 %all_to_all.23 = f32[4,1,128]{2,1,0:T(1,128)S(1)} all-to-all(f32[4,1,128]{2,1,0:T(1,128)S(1)} %bitcast.12), channel_id=1, replica_groups={{0,4,8,12},{1,5,9,13},{2,6,10,14},{3,7,11,15},{16,20,24,28},{17,21,25,2..., dimensions={0} | all-to-all | bytes 4096 | tf_op jit(solution)/shard_map/all_to_all | solution.py:470
  39.7 1.0 %update.1 = f32[256,512]{1,0:T(8,128)} custom-call(f32[256,512]{1,0:T(8,128)S(1)} %copy-done, f32[256,512]{1,0:T(8,128)S(1)} %get-tuple-element.27.grad_ref, f32[4,128]{1,0:T(4,128)S(1)} %bitcast.10), custom_call_target="tpu_custom_call" | custom-call | flops 262144 | bytes 1572864 | tf_op jit(solution)/shard_map/update/pallas_call | solution.py:471
  (1 shorter events, 0.0 us)
Async XLA Ops:
  0.0 7.0 %collective-permute-start = (bf16[128,512]{1,0:T(8,128)(2,1)}, bf16[128,512]{1,0:T(8,128)(2,1)S(1)}, u32[]{:S(2)}, u32[]{:S(2)}) collective-permute-start(bf16[128,512]{1,0:T(8,128)(2,1)} %rest_0_.1), channel_id=1, source_target_pairs={{0,4},{4,8},{8,12},{12,14},{14,10},{10,6},{6,2},{2,0},{1,3},{5,1},... | collective-permute-start | bytes 393224 | tf_op jit(solution)/shard_map/ppermute | solution.py:29
  3.0 5.5 %collective-permute-start.1 = (bf16[128,512]{1,0:T(8,128)(2,1)}, bf16[128,512]{1,0:T(8,128)(2,1)S(1)}, u32[]{:S(2)}, u32[]{:S(2)}) collective-permute-start(bf16[128,512]{1,0:T(8,128)(2,1)} %rest_0_.1), channel_id=1, source_target_pairs={{0,2},{4,0},{8,4},{12,8},{14,12},{10,14},{6,10},{2,6},{1,5},{5,9},... | collective-permute-start | bytes 393224 | tf_op jit(solution)/shard_map/ppermute | solution.py:29
  3.7 0.7 %copy-start.3 = (s32[1,8]{1,0:T(1,128)S(1)}, s32[1,8]{1,0:T(1,128)}, u32[]{:S(2)}) copy-start(s32[1,8]{1,0:T(1,128)} %list_ref.1) | copy-start | bytes 100
  4.3 5.1 %copy-start = (f32[256,512]{1,0:T(8,128)S(1)}, f32[256,512]{1,0:T(8,128)}, u32[]{:S(2)}) copy-start(f32[256,512]{1,0:T(8,128)} %users_ref.1) | copy-start | bytes 1572868
  4.3 5.1 %copy-start.1 = (s32[256,1024]{1,0:T(8,128)S(1)}, s32[256,1024]{1,0:T(8,128)}, u32[]{:S(2)}) copy-start(s32[256,1024]{1,0:T(8,128)} %labels_ref.9) | copy-start | bytes 3145732
  4.3 5.1 %copy-start.2 = (bf16[128,512]{1,0:T(8,128)(2,1)S(1)}, bf16[128,512]{1,0:T(8,128)(2,1)}, u32[]{:S(2)}) copy-start(bf16[128,512]{1,0:T(8,128)(2,1)} %rest_0_.1) | copy-start | bytes 393220
  7.0 6.9 %collective-permute-start.2 = (bf16[128,512]{1,0:T(8,128)(2,1)S(1)}, bf16[128,512]{1,0:T(8,128)(2,1)S(1)}, u32[]{:S(2)}, u32[]{:S(2)}) collective-permute-start(bf16[128,512]{1,0:T(8,128)(2,1)S(1)} %collective-permute-done.rest_1_), channel_id=1, source_target_pairs={{0,4},{4,8},{8,12},{12,14},{14,10},{10,6},{6,2},{2,0},{1,3},{5,1},... | collective-permute-start | bytes 393224 | tf_op jit(solution)/shard_map/ppermute | solution.py:29
  8.5 6.4 %collective-permute-start.4 = (bf16[128,512]{1,0:T(8,128)(2,1)S(1)}, bf16[128,512]{1,0:T(8,128)(2,1)S(1)}, u32[]{:S(2)}, u32[]{:S(2)}) collective-permute-start(bf16[128,512]{1,0:T(8,128)(2,1)S(1)} %collective-permute-done.1.rest_2_), channel_id=1, source_target_pairs={{0,2},{4,0},{8,4},{12,8},{14,12},{10,14},{6,10},{2,6},{1,5},{5,9},... | collective-permute-start | bytes 393224 | tf_op jit(solution)/shard_map/ppermute | solution.py:29
  10.5 7.0 %collective-permute-start.6 = (bf16[128,512]{1,0:T(8,128)(2,1)S(1)}, bf16[128,512]{1,0:T(8,128)(2,1)S(1)}, u32[]{:S(2)}, u32[]{:S(2)}) collective-permute-start(bf16[128,512]{1,0:T(8,128)(2,1)S(1)} %get-tuple-element.20), channel_id=1, source_target_pairs={{0,12},{1,13},{4,6},{5,7},{8,10},{9,11},{12,0},{13,1},{14,2},{15,3... | collective-permute-start | bytes 393224 | tf_op jit(solution)/shard_map/ppermute | solution.py:39
  13.9 7.4 %collective-permute-start.8 = (bf16[384,512]{1,0:T(8,128)(2,1)S(1)}, bf16[384,512]{1,0:T(8,128)(2,1)S(1)}, u32[]{:S(2)}, u32[]{:S(2)}) collective-permute-start(bf16[384,512]{1,0:T(8,128)(2,1)S(1)} %get-tuple-element.24), channel_id=1, source_target_pairs={{0,1},{1,0},{2,3},{3,2},{4,5},{5,4},{6,7},{7,6},{8,9},{9,8},{10,11... | collective-permute-start | bytes 1179656 | tf_op jit(solution)/shard_map/ppermute | solution.py:43
  13.9 5.6 %collective-permute-start.3 = (bf16[128,512]{1,0:T(8,128)(2,1)S(1)}, bf16[128,512]{1,0:T(8,128)(2,1)S(1)}, u32[]{:S(2)}, u32[]{:S(2)}) collective-permute-start(bf16[128,512]{1,0:T(8,128)(2,1)S(1)} %collective-permute-done.2.rest_0_), channel_id=1, source_target_pairs={{0,4},{4,8},{8,12},{12,14},{14,10},{10,6},{6,2},{2,0},{1,3},{5,1},... | collective-permute-start | bytes 393224 | tf_op jit(solution)/shard_map/ppermute | solution.py:29
  14.9 5.3 %collective-permute-start.5 = (bf16[128,512]{1,0:T(8,128)(2,1)S(1)}, bf16[128,512]{1,0:T(8,128)(2,1)S(1)}, u32[]{:S(2)}, u32[]{:S(2)}) collective-permute-start(bf16[128,512]{1,0:T(8,128)(2,1)S(1)} %collective-permute-done.4.rest_1_), channel_id=1, source_target_pairs={{0,2},{4,0},{8,4},{12,8},{14,12},{10,14},{6,10},{2,6},{1,5},{5,9},... | collective-permute-start | bytes 393224 | tf_op jit(solution)/shard_map/ppermute | solution.py:29
  16.0 5.3 %collective-permute-start.9 = (bf16[256,512]{1,0:T(8,128)(2,1)S(1)}, bf16[256,512]{1,0:T(8,128)(2,1)S(1)}, u32[]{:S(2)}, u32[]{:S(2)}) collective-permute-start(bf16[256,512]{1,0:T(8,128)(2,1)S(1)} %get-tuple-element.25), channel_id=1, source_target_pairs={{0,1},{1,0},{2,3},{3,2},{4,5},{5,4},{6,7},{7,6},{8,9},{9,8},{10,11... | collective-permute-start | bytes 786440 | tf_op jit(solution)/shard_map/ppermute | solution.py:43
  20.3 2.3 %collective-permute-start.7 = (bf16[384,512]{1,0:T(8,128)(2,1)S(1)}, bf16[384,512]{1,0:T(8,128)(2,1)S(1)}, u32[]{:S(2)}, u32[]{:S(2)}) collective-permute-start(bf16[384,512]{1,0:T(8,128)(2,1)S(1)} %get-tuple-element.23), channel_id=1, source_target_pairs={{0,1},{1,0},{2,3},{3,2},{4,5},{5,4},{6,7},{7,6},{8,9},{9,8},{10,11... | collective-permute-start | bytes 1179656 | tf_op jit(solution)/shard_map/ppermute | solution.py:43

commit v10 on v8

--- a/solution.py
+++ b/solution.py
@@ -72,6 +72,7 @@
         out_shape=jax.ShapeDtypeStruct((1, 128), jnp.int32),
         in_specs=[pl.BlockSpec(memory_space=pltpu.VMEM)] * 2,
         out_specs=pl.BlockSpec(memory_space=pltpu.VMEM),
+        compiler_params=pltpu.CompilerParams(vmem_limit_bytes=16 * 1024 * 1024),
         cost_estimate=pl.CostEstimate(flops=2**32, bytes_accessed=1024, transcendentals=0),
         name="slot_table",
     )(block_list, live_count.reshape(1, 1))
@@ -159,6 +160,7 @@
         out_shape=jax.ShapeDtypeStruct((1, 128), jnp.int32),
         in_specs=[pl.BlockSpec(memory_space=pltpu.VMEM)] * 2,
         out_specs=pl.BlockSpec(memory_space=pltpu.VMEM),
+        compiler_params=pltpu.CompilerParams(vmem_limit_bytes=16 * 1024 * 1024),
         cost_estimate=pl.CostEstimate(flops=2**32, bytes_accessed=1024, transcendentals=0),
         name="slot_table",
     )(block_list, live_count.reshape(1, 1))
@@ -231,6 +233,27 @@
     return 2 * chip + (1 - core if other else core)
 
 
+def pack_kernel(*refs):
+    tile = refs[0].shape[0]
+    for at, ref in enumerate(refs[:-1]):
+        refs[-1][at * tile : (at + 1) * tile, :] = ref[...]
+
+
+def pack(arrays):
+    tile, width = arrays[0].shape
+    return pl.pallas_call(
+        pack_kernel,
+        out_shape=jax.ShapeDtypeStruct((len(arrays) * tile, width), arrays[0].dtype),
+        in_specs=[pl.BlockSpec(memory_space=pltpu.VMEM)] * len(arrays),
+        out_specs=pl.BlockSpec(memory_space=pltpu.VMEM),
+        compiler_params=pltpu.CompilerParams(vmem_limit_bytes=16 * 1024 * 1024),
+        cost_estimate=pl.CostEstimate(
+            flops=2**34, bytes_accessed=4 * len(arrays) * tile * width, transcendentals=0
+        ),
+        name="pack",
+    )(*arrays)
+
+
 def pieces_kernel(places, count, packed, loop_size, first, last, table_ref, given_ref, labels_ref, *rest):
     rest = list(rest)
     arrays = [rest.pop(0) for _ in range(count)]
@@ -333,19 +356,21 @@
     up, table = lax.optimization_barrier((up, table))
     first = [held(0, items), held(1, up), held(-1, down)]
     second = [held(2, to_next(up, 1, loop_size)), held(-2, to_next(down, -1, loop_size))]
-    gradient, parts, opposite, pack = add_pieces(
+    gradient, parts, opposite, packed = add_pieces(
         first, [0, 1, 2], loop_size, table, users, labels, None, False
     )
     opposite = across(opposite, loop_size)
-    first = other(pack, [0, 1, -1])
+    first = other(packed, [0, 1, -1])
     third = [held(3, to_next(second[0][0], 1, loop_size)), held(-3, to_next(second[1][0], -1, loop_size))]
-    gradient, pack = add_pieces(second, [0, 1], loop_size, table, parts, labels, gradient, False)
-    second = other(pack, [2, -2])
+    gradient, packed = add_pieces(second, [0, 1], loop_size, table, parts, labels, gradient, False)
+    second = other(packed, [2, -2])
     third.append(held(4, opposite))
-    gradient, pack = add_pieces(third, [0, 1, 2], loop_size, table, parts, labels, gradient, False)
-    third = other(pack, [3, -3, 4])
-    (gradient,) = add_pieces([first, second], [], loop_size, table, parts, labels, gradient, False)
-    return *add_pieces([third], [], loop_size, table, parts, labels, gradient, True), users
+    arrived, gradient = lax.optimization_barrier(([array for array, _ in third], gradient))
+    last = other(pack(arrived), [3, -3, 4])
+    (gradient,) = add_pieces(
+        third + [first, second], [], loop_size, table, parts, labels, gradient, False
+    )
+    return *add_pieces([last], [], loop_size, table, parts, labels, gradient, True), users
 
 
 def chunks_kernel(

time: 36.6 us -> 36 us (0.984); the launches traced: 36 us -> 35.8 us
  waiting for transfers between devices: 8.46 us -> 6.41 us
  starting transfers between devices: 10.1 us -> 11.3 us
  Pallas kernels: 4.07 us -> 5.19 us
  blocking collectives: 12.1 us -> 11.5 us
    pallas_call x5 -> x4, Pallas kernels: 1.69 us -> 4.04 us  [add_pieces(): pl.pallas_call(functools.partial(pieces_kernel, places, len(arrays), pack...]
    ppermute x3, waiting for transfers between devices: 1.53 us -> 0.01 us  [to_other_core(): lax.ppermute(array, 'loop', [(at, at ^ 1) for at in range(loop_size)])]
    pallas_call x1, Pallas kernels: 1.41 us -> 0.15 us  [slot_table(): pl.pallas_call(functools.partial(table_kernel, loop_size, origins), out_s...]
    ppermute x1, starting transfers between devices: 3.37 us -> 4.16 us  [across(): return lax.ppermute(array, 'loop', pairs)]
    ppermute x1, waiting for transfers between devices: 1.44 us -> 0.65 us  [across(): return lax.ppermute(array, 'loop', pairs)]
    all_to_all x1, blocking collectives: 12.1 us -> 11.5 us  [local(): squares = lax.all_to_all(square, 'loop', 0, 0, tiled=True)]
  transfers between devices with their start and end apart: 10 -> 10, of which waited for: 6 -> 5; matrix products, arithmetic and copies ran while one was open for 0% -> 0% of each run, Pallas kernels for 8% -> 9%
where the time goes in v10:
time: 36 us; the launch traced here: 35.8 us
  blocking collectives  11.5 us (32%)
  starting transfers between devices  11.3 us (31%)
  waiting for transfers between devices  6.41 us (18%)
  Pallas kernels  5.19 us (14%)
  between operations  0.73 us (2%)
  local copies, waits for them, and re-layouts  0.66 us (2%)
    all_to_all x1, blocking collectives, local(): squares = lax.all_to_all(square, 'loop', 0, 0, tiled=True)  11.5 us
    ppermute x6, starting transfers between devices, to_next(): return lax.ppermute(array, 'loop', pairs)  6.91 us
    ppermute x6, waiting for transfers between devices, to_next(): return lax.ppermute(array, 'loop', pairs)  5.75 us
    ppermute x1, starting transfers between devices, across(): return lax.ppermute(array, 'loop', pairs)  4.16 us
    pallas_call x4, Pallas kernels, add_pieces(): pl.pallas_call(functools.partial(pieces_kernel, places, len(arrays), pack...  4.04 us
    pallas_call x1, Pallas kernels, local(): pl.pallas_call(functools.partial(update_kernel, rows * loop_size * width)...  0.98 us
  transfers between devices with their start and end apart: 10, of which 5 were waited for; matrix products, arithmetic and copies ran while one was open for 0% of the time, Pallas kernels for 9%

profile of v10, /device:TPU:0, one launch (start us, length us, event | category | flops | bytes accessed | tf_op | source)
XLA Modules:
  0.0 35.8 jit_solution(101898649232961129)
XLA Ops:
  0.0 3.0 %collective-permute-start = (bf16[128,512]{1,0:T(8,128)(2,1)}, bf16[128,512]{1,0:T(8,128)(2,1)S(1)}, u32[]{:S(2)}, u32[]{:S(2)}) collective-permute-start(bf16[128,512]{1,0:T(8,128)(2,1)} %rest_0_.1), channel_id=1, source_target_pairs={{0,4},{4,8},{8,12},{12,14},{14,10},{10,6},{6,2},{2,0},{1,3},{5,1},... | collective-permute-start | bytes 393224 | tf_op jit(solution)/shard_map/ppermute | solution.py:29
  3.0 0.0 collective-permute-start.1
  3.7 0.0 copy-start.3
  3.7 0.6 %copy-done.3 = s32[1,8]{1,0:T(1,128)S(1)} copy-done((s32[1,8]{1,0:T(1,128)S(1)}, s32[1,8]{1,0:T(1,128)}, u32[]{:S(2)}) %copy-start.3) | copy-done | bytes 56
  4.3 0.0 copy-start
  4.3 0.0 copy-start.1
  4.3 0.0 copy-start.2
  4.3 0.1 slot_table.1.table_ref
  4.5 2.5 %collective-permute-done.rest_1_ = bf16[128,512]{1,0:T(8,128)(2,1)S(1)} collective-permute-done((bf16[128,512]{1,0:T(8,128)(2,1)}, bf16[128,512]{1,0:T(8,128)(2,1)S(1)}, u32[]{:S(2)}, u32[]{:S(2)}) %collective-permute-start) | collective-permute-done | bytes 131104 | tf_op jit(solution)/shard_map/ppermute | solution.py:29
  7.0 1.5 %collective-permute-start.2 = (bf16[128,512]{1,0:T(8,128)(2,1)S(1)}, bf16[128,512]{1,0:T(8,128)(2,1)S(1)}, u32[]{:S(2)}, u32[]{:S(2)}) collective-permute-start(bf16[128,512]{1,0:T(8,128)(2,1)S(1)} %collective-permute-done.rest_1_), channel_id=1, source_target_pairs={{0,4},{4,8},{8,12},{12,14},{14,10},{10,6},{6,2},{2,0},{1,3},{5,1},... | collective-permute-start | bytes 393224 | tf_op jit(solution)/shard_map/ppermute | solution.py:29
  8.5 0.0 collective-permute-done.1.rest_2_
  8.5 0.9 %collective-permute-start.4 = (bf16[128,512]{1,0:T(8,128)(2,1)S(1)}, bf16[128,512]{1,0:T(8,128)(2,1)S(1)}, u32[]{:S(2)}, u32[]{:S(2)}) collective-permute-start(bf16[128,512]{1,0:T(8,128)(2,1)S(1)} %collective-permute-done.1.rest_2_), channel_id=1, source_target_pairs={{0,2},{4,0},{8,4},{12,8},{14,12},{10,14},{6,10},{2,6},{1,5},{5,9},... | collective-permute-start | bytes 393224 | tf_op jit(solution)/shard_map/ppermute | solution.py:29
  9.4 0.0 copy-done
  9.4 0.0 copy-done.1
  9.4 0.0 copy-done.2
  9.4 0.3 add_pieces.4
  9.7 4.2 %collective-permute-start.6 = (bf16[128,512]{1,0:T(8,128)(2,1)S(1)}, bf16[128,512]{1,0:T(8,128)(2,1)S(1)}, u32[]{:S(2)}, u32[]{:S(2)}) collective-permute-start(bf16[128,512]{1,0:T(8,128)(2,1)S(1)} %get-tuple-element.22), channel_id=1, source_target_pairs={{0,12},{1,13},{4,6},{5,7},{8,10},{9,11},{12,0},{13,1},{14,2},{15,3... | collective-permute-start | bytes 393224 | tf_op jit(solution)/shard_map/ppermute | solution.py:39
  13.9 0.0 collective-permute-start.8
  13.9 0.0 collective-permute-done.2.rest_0_
  13.9 0.3 collective-permute-start.3
  14.2 0.6 %collective-permute-done.4.rest_1_ = bf16[128,512]{1,0:T(8,128)(2,1)S(1)} collective-permute-done((bf16[128,512]{1,0:T(8,128)(2,1)S(1)}, bf16[128,512]{1,0:T(8,128)(2,1)S(1)}, u32[]{:S(2)}, u32[]{:S(2)}) %collective-permute-start.4) | collective-permute-done | bytes 131104 | tf_op jit(solution)/shard_map/ppermute | solution.py:29
  14.7 1.2 %collective-permute-start.5 = (bf16[128,512]{1,0:T(8,128)(2,1)S(1)}, bf16[128,512]{1,0:T(8,128)(2,1)S(1)}, u32[]{:S(2)}, u32[]{:S(2)}) collective-permute-start(bf16[128,512]{1,0:T(8,128)(2,1)S(1)} %collective-permute-done.4.rest_1_), channel_id=1, source_target_pairs={{0,2},{4,0},{8,4},{12,8},{14,12},{10,14},{6,10},{2,6},{1,5},{5,9},... | collective-permute-start | bytes 393224 | tf_op jit(solution)/shard_map/ppermute | solution.py:29
  15.9 0.9 %add_pieces.5 = (f32[256,512]{1,0:T(8,128)S(1)}, bf16[256,512]{1,0:T(8,128)(2,1)S(1)}) custom-call(s32[1,128]{1,0:T(1,128)S(1)} %slot_table.1.table_ref, bf16[512,512]{1,0:T(8,128)(2,1)S(1)} %get-tuple-element.21.given_ref, s32[256,1024]{1,0:T(8,128)S(1)} %copy-done.1, ...), custom_call_target="tpu_custom_call", output_to_operand_aliasing={{0}: (5, {})} | custom-call | flops 4294967296 | bytes 1048576 | tf_op jit(solution)/shard_map/add_pieces/pallas_call | solution.py:320
  16.8 0.1 collective-permute-start.9
  16.9 0.7 %collective-permute-done.6.refs_2_.rest_2_ = bf16[128,512]{1,0:T(8,128)(2,1)S(1)} collective-permute-done((bf16[128,512]{1,0:T(8,128)(2,1)S(1)}, bf16[128,512]{1,0:T(8,128)(2,1)S(1)}, u32[]{:S(2)}, u32[]{:S(2)}) %collective-permute-start.6) | collective-permute-done | bytes 131104 | tf_op jit(solution)/shard_map/ppermute | solution.py:39
  17.6 2.6 %collective-permute-done.3.refs_0_.rest_0_ = bf16[128,512]{1,0:T(8,128)(2,1)S(1)} collective-permute-done((bf16[128,512]{1,0:T(8,128)(2,1)S(1)}, bf16[128,512]{1,0:T(8,128)(2,1)S(1)}, u32[]{:S(2)}, u32[]{:S(2)}) %collective-permute-start.3) | collective-permute-done | bytes 131104 | tf_op jit(solution)/shard_map/ppermute | solution.py:29
  20.2 0.1 collective-permute-done.5.refs_1_.rest_1_
  20.3 0.2 collective-permute-start.7
  20.4 0.0 collective-permute-done.9.rest_4_
  20.5 0.0 collective-permute-done.8.rest_3_
  20.5 1.8 %add_pieces.6.rest_1_ = f32[256,512]{1,0:T(8,128)S(1)} custom-call(s32[1,128]{1,0:T(1,128)S(1)} %slot_table.1.table_ref, bf16[512,512]{1,0:T(8,128)(2,1)S(1)} %get-tuple-element.21.given_ref, s32[256,1024]{1,0:T(8,128)S(1)} %copy-done.1, bf16[128,512]{1,0:T(8,128)(2,1)S(1)} %collective-permute-done.3.refs_0_.rest_0_, ...), custom_call_target="tpu_custom_call", output_to_operand_aliasing={{}: (8, {})} | custom-call | flops 17179869184 | bytes 1048576 | tf_op jit(solution)/shard_map/add_pieces/pallas_call | solution.py:320
  22.3 0.0 collective-permute-done.7.rest_0_
  22.3 1.0 %add_pieces.7 = (f32[256,512]{1,0:T(8,128)S(1)}, f32[16,128]{1,0:T(8,128)S(1)}) custom-call(s32[1,128]{1,0:T(1,128)S(1)} %slot_table.1.table_ref, bf16[512,512]{1,0:T(8,128)(2,1)S(1)} %get-tuple-element.21.given_ref, s32[256,1024]{1,0:T(8,128)S(1)} %copy-done.1, ...), custom_call_target="tpu_custom_call", output_to_operand_aliasing={{0}: (4, {})} | custom-call | flops 6442450944 | bytes 1048576 | tf_op jit(solution)/shard_map/add_pieces/pallas_call | solution.py:320
  23.3 11.5 %all_to_all.11 = f32[16,1,128]{2,1,0:T(1,128)S(1)} all-to-all(f32[16,1,128]{2,1,0:T(1,128)S(1)} %bitcast.7), channel_id=1, replica_groups=mesh['group'=2,'loop'=16] {'loop'}, dimensions={0} | all-to-all | bytes 16384 | tf_op jit(solution)/shard_map/all_to_all | solution.py:464
  34.9 1.0 %update.1 = f32[256,512]{1,0:T(8,128)} custom-call(f32[256,512]{1,0:T(8,128)S(1)} %copy-done, f32[256,512]{1,0:T(8,128)S(1)} %get-tuple-element.31.grad_ref, f32[16,128]{1,0:T(8,128)S(1)} %bitcast.6), custom_call_target="tpu_custom_call" | custom-call | flops 262144 | bytes 1572864 | tf_op jit(solution)/shard_map/update/pallas_call | solution.py:465
  (1 shorter events, 0.0 us)
Async XLA Ops:
  0.0 7.0 %collective-permute-start = (bf16[128,512]{1,0:T(8,128)(2,1)}, bf16[128,512]{1,0:T(8,128)(2,1)S(1)}, u32[]{:S(2)}, u32[]{:S(2)}) collective-permute-start(bf16[128,512]{1,0:T(8,128)(2,1)} %rest_0_.1), channel_id=1, source_target_pairs={{0,4},{4,8},{8,12},{12,14},{14,10},{10,6},{6,2},{2,0},{1,3},{5,1},... | collective-permute-start | bytes 393224 | tf_op jit(solution)/shard_map/ppermute | solution.py:29
  3.0 5.5 %collective-permute-start.1 = (bf16[128,512]{1,0:T(8,128)(2,1)}, bf16[128,512]{1,0:T(8,128)(2,1)S(1)}, u32[]{:S(2)}, u32[]{:S(2)}) collective-permute-start(bf16[128,512]{1,0:T(8,128)(2,1)} %rest_0_.1), channel_id=1, source_target_pairs={{0,2},{4,0},{8,4},{12,8},{14,12},{10,14},{6,10},{2,6},{1,5},{5,9},... | collective-permute-start | bytes 393224 | tf_op jit(solution)/shard_map/ppermute | solution.py:29
  3.7 0.7 %copy-start.3 = (s32[1,8]{1,0:T(1,128)S(1)}, s32[1,8]{1,0:T(1,128)}, u32[]{:S(2)}) copy-start(s32[1,8]{1,0:T(1,128)} %list_ref.1) | copy-start | bytes 100
  4.3 5.1 %copy-start = (f32[256,512]{1,0:T(8,128)S(1)}, f32[256,512]{1,0:T(8,128)}, u32[]{:S(2)}) copy-start(f32[256,512]{1,0:T(8,128)} %users_ref.1) | copy-start | bytes 1572868
  4.3 5.1 %copy-start.1 = (s32[256,1024]{1,0:T(8,128)S(1)}, s32[256,1024]{1,0:T(8,128)}, u32[]{:S(2)}) copy-start(s32[256,1024]{1,0:T(8,128)} %labels_ref.7) | copy-start | bytes 3145732
  4.3 5.1 %copy-start.2 = (bf16[128,512]{1,0:T(8,128)(2,1)S(1)}, bf16[128,512]{1,0:T(8,128)(2,1)}, u32[]{:S(2)}) copy-start(bf16[128,512]{1,0:T(8,128)(2,1)} %rest_0_.1) | copy-start | bytes 393220
  7.0 6.9 %collective-permute-start.2 = (bf16[128,512]{1,0:T(8,128)(2,1)S(1)}, bf16[128,512]{1,0:T(8,128)(2,1)S(1)}, u32[]{:S(2)}, u32[]{:S(2)}) collective-permute-start(bf16[128,512]{1,0:T(8,128)(2,1)S(1)} %collective-permute-done.rest_1_), channel_id=1, source_target_pairs={{0,4},{4,8},{8,12},{12,14},{14,10},{10,6},{6,2},{2,0},{1,3},{5,1},... | collective-permute-start | bytes 393224 | tf_op jit(solution)/shard_map/ppermute | solution.py:29
  8.5 6.2 %collective-permute-start.4 = (bf16[128,512]{1,0:T(8,128)(2,1)S(1)}, bf16[128,512]{1,0:T(8,128)(2,1)S(1)}, u32[]{:S(2)}, u32[]{:S(2)}) collective-permute-start(bf16[128,512]{1,0:T(8,128)(2,1)S(1)} %collective-permute-done.1.rest_2_), channel_id=1, source_target_pairs={{0,2},{4,0},{8,4},{12,8},{14,12},{10,14},{6,10},{2,6},{1,5},{5,9},... | collective-permute-start | bytes 393224 | tf_op jit(solution)/shard_map/ppermute | solution.py:29
  9.7 7.9 %collective-permute-start.6 = (bf16[128,512]{1,0:T(8,128)(2,1)S(1)}, bf16[128,512]{1,0:T(8,128)(2,1)S(1)}, u32[]{:S(2)}, u32[]{:S(2)}) collective-permute-start(bf16[128,512]{1,0:T(8,128)(2,1)S(1)} %get-tuple-element.22), channel_id=1, source_target_pairs={{0,12},{1,13},{4,6},{5,7},{8,10},{9,11},{12,0},{13,1},{14,2},{15,3... | collective-permute-start | bytes 393224 | tf_op jit(solution)/shard_map/ppermute | solution.py:39
  13.9 6.6 %collective-permute-start.8 = (bf16[384,512]{1,0:T(8,128)(2,1)S(1)}, bf16[384,512]{1,0:T(8,128)(2,1)S(1)}, u32[]{:S(2)}, u32[]{:S(2)}) collective-permute-start(bf16[384,512]{1,0:T(8,128)(2,1)S(1)} %get-tuple-element.28), channel_id=1, source_target_pairs={{0,1},{1,0},{2,3},{3,2},{4,5},{5,4},{6,7},{7,6},{8,9},{9,8},{10,11... | collective-permute-start | bytes 1179656 | tf_op jit(solution)/shard_map/ppermute | solution.py:43
  13.9 6.3 %collective-permute-start.3 = (bf16[128,512]{1,0:T(8,128)(2,1)S(1)}, bf16[128,512]{1,0:T(8,128)(2,1)S(1)}, u32[]{:S(2)}, u32[]{:S(2)}) collective-permute-start(bf16[128,512]{1,0:T(8,128)(2,1)S(1)} %collective-permute-done.2.rest_0_), channel_id=1, source_target_pairs={{0,4},{4,8},{8,12},{12,14},{14,10},{10,6},{6,2},{2,0},{1,3},{5,1},... | collective-permute-start | bytes 393224 | tf_op jit(solution)/shard_map/ppermute | solution.py:29
  14.7 5.5 %collective-permute-start.5 = (bf16[128,512]{1,0:T(8,128)(2,1)S(1)}, bf16[128,512]{1,0:T(8,128)(2,1)S(1)}, u32[]{:S(2)}, u32[]{:S(2)}) collective-permute-start(bf16[128,512]{1,0:T(8,128)(2,1)S(1)} %collective-permute-done.4.rest_1_), channel_id=1, source_target_pairs={{0,2},{4,0},{8,4},{12,8},{14,12},{10,14},{6,10},{2,6},{1,5},{5,9},... | collective-permute-start | bytes 393224 | tf_op jit(solution)/shard_map/ppermute | solution.py:29
  16.8 3.6 %collective-permute-start.9 = (bf16[256,512]{1,0:T(8,128)(2,1)S(1)}, bf16[256,512]{1,0:T(8,128)(2,1)S(1)}, u32[]{:S(2)}, u32[]{:S(2)}) collective-permute-start(bf16[256,512]{1,0:T(8,128)(2,1)S(1)} %get-tuple-element.29), channel_id=1, source_target_pairs={{0,1},{1,0},{2,3},{3,2},{4,5},{5,4},{6,7},{7,6},{8,9},{9,8},{10,11... | collective-permute-start | bytes 786440 | tf_op jit(solution)/shard_map/ppermute | solution.py:43
  20.3 2.0 %collective-permute-start.7 = (bf16[384,512]{1,0:T(8,128)(2,1)S(1)}, bf16[384,512]{1,0:T(8,128)(2,1)S(1)}, u32[]{:S(2)}, u32[]{:S(2)}) collective-permute-start(bf16[384,512]{1,0:T(8,128)(2,1)S(1)} %pack.1), channel_id=1, source_target_pairs={{0,1},{1,0},{2,3},{3,2},{4,5},{5,4},{6,7},{7,6},{8,9},{9,8},{10,11... | collective-permute-start | bytes 1179656 | tf_op jit(solution)/shard_map/ppermute | solution.py:43

commit v11 on v10

--- a/solution.py
+++ b/solution.py
@@ -29,13 +29,9 @@
     return lax.ppermute(array, "loop", pairs)
 
 
-def across(array, loop_size):
+def to_opposite(array, loop_size):
     chips, device = ring_place(loop_size)
-    pairs = [
-        (device(at, core), device(at + (3 if at % 2 == 0 else -3), core))
-        for at in range(chips)
-        for core in range(2)
-    ]
+    pairs = [(device(at, core), device(at + chips // 2, core)) for at in range(chips) for core in range(2)]
     return lax.ppermute(array, "loop", pairs)
 
 
@@ -254,14 +250,13 @@
     )(*arrays)
 
 
-def pieces_kernel(places, count, packed, loop_size, first, last, table_ref, given_ref, labels_ref, *rest):
+def pieces_kernel(places, count, packed, first, last, table_ref, given_ref, labels_ref, *rest):
     rest = list(rest)
     arrays = [rest.pop(0) for _ in range(count)]
     if not first:
         rest.pop(0)
     grad_ref = rest.pop(0)
     parts_ref = rest.pop(0) if first else given_ref
-    across_ref = rest.pop(0) if first else None
     pack_ref = rest.pop(0) if packed else None
     square_ref = rest.pop(0) if last else None
     tiles, slots = rest
@@ -269,13 +264,6 @@
     for at, index in enumerate(packed):
         pack_ref[at * tile : (at + 1) * tile, :] = arrays[index][...]
     if first:
-        core, position = core_and_position(loop_size)
-        for at in range(2):
-
-            @pl.when((core + position) % 2 == at)
-            def _():
-                across_ref[...] = arrays[1 + at][...]
-
         parts_ref[...] = halves(0.5 * given_ref[...])
         grad_ref[...] = jnp.zeros_like(grad_ref)
     live = jnp.int32(0)
@@ -300,25 +288,25 @@
         store_square(grad_ref, square_ref)
 
 
-def add_pieces(held, packed, loop_size, table, given, labels, before, last):
+def add_pieces(held, packed, loop_size, table, given, labels, before, last, worked=None):
     first = before is None
     width = given.shape[1]
     rows = given.shape[0] // (1 if first else 2)
     arrays = [array for array, _ in held]
     tile = labels.shape[1] // CHUNK
     places = [(at, index, row) for index, (_, entries) in enumerate(held) for row, at in enumerate(entries)]
+    places = places[:worked]
     most = min(len(places), CHUNK)
     out_shape = [jax.ShapeDtypeStruct((rows, width), jnp.float32)]
     if first:
         out_shape.append(jax.ShapeDtypeStruct((2 * rows, width), jnp.bfloat16))
-        out_shape.append(jax.ShapeDtypeStruct((tile, width), jnp.bfloat16))
     if packed:
         out_shape.append(jax.ShapeDtypeStruct((len(packed) * tile, width), jnp.bfloat16))
     if last:
         out_shape.append(jax.ShapeDtypeStruct((loop_size, 128), jnp.float32))
     extra = [] if first else [before]
     return pl.pallas_call(
-        functools.partial(pieces_kernel, places, len(arrays), packed, loop_size, first, last),
+        functools.partial(pieces_kernel, places, len(arrays), packed, first, last),
         out_shape=out_shape,
         in_specs=[pl.BlockSpec(memory_space=pltpu.VMEM)] * (3 + len(arrays) + len(extra)),
         out_specs=[pl.BlockSpec(memory_space=pltpu.VMEM)] * len(out_shape),
@@ -354,21 +342,19 @@
     up = to_next(items, 1, loop_size)
     down = to_next(items, -1, loop_size)
     up, table = lax.optimization_barrier((up, table))
-    first = [held(0, items), held(1, up), held(-1, down)]
+    opposite = to_opposite(items, loop_size)
+    first = [held(0, items), held(1, up), held(-1, down), held(4, opposite)]
     second = [held(2, to_next(up, 1, loop_size)), held(-2, to_next(down, -1, loop_size))]
-    gradient, parts, opposite, packed = add_pieces(
-        first, [0, 1, 2], loop_size, table, users, labels, None, False
+    third = [held(3, to_next(second[0][0], 1, loop_size)), held(-3, to_next(second[1][0], -1, loop_size))]
+    gradient, parts = add_pieces(first, [], loop_size, table, users, labels, None, False)
+    gradient, packed = add_pieces(
+        second + first, [0, 1, 2, 3, 4, 5], loop_size, table, parts, labels, gradient, False, 2
     )
-    opposite = across(opposite, loop_size)
-    first = other(packed, [0, 1, -1])
-    third = [held(3, to_next(second[0][0], 1, loop_size)), held(-3, to_next(second[1][0], -1, loop_size))]
-    gradient, packed = add_pieces(second, [0, 1], loop_size, table, parts, labels, gradient, False)
-    second = other(packed, [2, -2])
-    third.append(held(4, opposite))
+    first = other(packed, [2, -2, 0, 1, -1, 4])
     arrived, gradient = lax.optimization_barrier(([array for array, _ in third], gradient))
-    last = other(pack(arrived), [3, -3, 4])
+    last = other(pack(arrived), [3, -3])
     (gradient,) = add_pieces(
-        third + [first, second], [], loop_size, table, parts, labels, gradient, False
+        third + [first], [], loop_size, table, parts, labels, gradient, False
     )
     return *add_pieces([last], [], loop_size, table, parts, labels, gradient, True), users
 

time: 36 us -> 36.4 us (1.011)
  blocking collectives: 11.5 us -> 10.1 us
  starting transfers between devices: 11.3 us -> 12.3 us
  waiting for transfers between devices: 6.41 us -> 7.24 us
    ppermute x1, waiting for transfers between devices: 0.65 us -> 2.33 us  [to_opposite(): return lax.ppermute(array, 'loop', pairs)]
    all_to_all x1, blocking collectives: 11.5 us -> 10.1 us  [local(): squares = lax.all_to_all(square, 'loop', 0, 0, tiled=True)]
    ppermute x6, waiting for transfers between devices: 5.75 us -> 4.9 us  [to_next(): return lax.ppermute(array, 'loop', pairs)]
    ppermute x1, starting transfers between devices: 4.16 us -> 5 us  [to_opposite(): return lax.ppermute(array, 'loop', pairs)]
  transfers between devices with their start and end apart: 10 -> 9, of which waited for: 5 -> 3; matrix products, arithmetic and copies ran while one was open for 0% -> 0% of each run, Pallas kernels for 9% -> 9%
where the time goes in v11:
time: 36.4 us; the launch traced here: 36.2 us
  starting transfers between devices  12.3 us (34%)
  blocking collectives  10.1 us (28%)
  waiting for transfers between devices  7.24 us (20%)
  Pallas kernels  5.13 us (14%)
  between operations  0.76 us (2%)
  local copies, waits for them, and re-layouts  0.66 us (2%)
    all_to_all x1, blocking collectives, local(): squares = lax.all_to_all(square, 'loop', 0, 0, tiled=True)  10.1 us
    ppermute x6, starting transfers between devices, to_next(): return lax.ppermute(array, 'loop', pairs)  7.12 us
    ppermute x1, starting transfers between devices, to_opposite(): return lax.ppermute(array, 'loop', pairs)  5 us
    ppermute x6, waiting for transfers between devices, to_next(): return lax.ppermute(array, 'loop', pairs)  4.9 us
    pallas_call x4, Pallas kernels, add_pieces(): pl.pallas_call(functools.partial(pieces_kernel, places, len(arrays), pack...  3.99 us
    ppermute x1, waiting for transfers between devices, to_opposite(): return lax.ppermute(array, 'loop', pairs)  2.33 us
    pallas_call x1, Pallas kernels, local(): pl.pallas_call(functools.partial(update_kernel, rows * loop_size * width)...  0.98 us
  transfers between devices with their start and end apart: 9, of which 3 were waited for; matrix products, arithmetic and copies ran while one was open for 0% of the time, Pallas kernels for 9%

profile of v11, /device:TPU:0, one launch (start us, length us, event | category | flops | bytes accessed | tf_op | source)
XLA Modules:
  0.0 36.2 jit_solution(1387482813101114020)
XLA Ops:
  0.0 3.0 %collective-permute-start = (bf16[128,512]{1,0:T(8,128)(2,1)}, bf16[128,512]{1,0:T(8,128)(2,1)S(1)}, u32[]{:S(2)}, u32[]{:S(2)}) collective-permute-start(bf16[128,512]{1,0:T(8,128)(2,1)} %rest_2_.1), channel_id=1, source_target_pairs={{0,4},{4,8},{8,12},{12,14},{14,10},{10,6},{6,2},{2,0},{1,3},{5,1},... | collective-permute-start | bytes 393224 | tf_op jit(solution)/shard_map/ppermute | solution.py:29
  3.0 0.0 collective-permute-start.1
  3.0 5.0 %collective-permute-start.2 = (bf16[128,512]{1,0:T(8,128)(2,1)}, bf16[128,512]{1,0:T(8,128)(2,1)S(1)}, u32[]{:S(2)}, u32[]{:S(2)}) collective-permute-start(bf16[128,512]{1,0:T(8,128)(2,1)} %rest_2_.1), channel_id=1, source_target_pairs={{0,14},{1,15},{4,10},{5,11},{8,6},{9,7},{12,2},{13,3},{14,0},{15,1... | collective-permute-start | bytes 393224 | tf_op jit(solution)/shard_map/ppermute | solution.py:35
  8.7 0.0 copy-start.3
  8.7 0.6 %copy-done.3 = s32[1,8]{1,0:T(1,128)S(1)} copy-done((s32[1,8]{1,0:T(1,128)S(1)}, s32[1,8]{1,0:T(1,128)}, u32[]{:S(2)}) %copy-start.3) | copy-done | bytes 56
  9.3 0.0 copy-start
  9.3 0.0 copy-start.1
  9.3 0.0 copy-start.2
  9.3 0.1 slot_table.1.table_ref
  9.5 0.0 collective-permute-done.rest_1_.rest_3_
  9.5 0.1 collective-permute-start.3
  9.6 0.0 collective-permute-done.1.rest_2_.rest_4_
  9.6 2.0 %collective-permute-start.5 = (bf16[128,512]{1,0:T(8,128)(2,1)S(1)}, bf16[128,512]{1,0:T(8,128)(2,1)S(1)}, u32[]{:S(2)}, u32[]{:S(2)}) collective-permute-start(bf16[128,512]{1,0:T(8,128)(2,1)S(1)} %collective-permute-done.1.rest_2_.rest_4_), channel_id=1, source_target_pairs={{0,2},{4,0},{8,4},{12,8},{14,12},{10,14},{6,10},{2,6},{1,5},{5,9},... | collective-permute-start | bytes 393224 | tf_op jit(solution)/shard_map/ppermute | solution.py:29
  11.6 2.3 %collective-permute-done.2.rest_3_.rest_5_ = bf16[128,512]{1,0:T(8,128)(2,1)S(1)} collective-permute-done((bf16[128,512]{1,0:T(8,128)(2,1)}, bf16[128,512]{1,0:T(8,128)(2,1)S(1)}, u32[]{:S(2)}, u32[]{:S(2)}) %collective-permute-start.2) | collective-permute-done | bytes 131104 | tf_op jit(solution)/shard_map/ppermute | solution.py:35
  13.9 0.0 copy-done
  13.9 0.0 copy-done.1
  13.9 0.0 copy-done.2
  13.9 1.0 %add_pieces.4 = (f32[256,512]{1,0:T(8,128)S(1)}, bf16[512,512]{1,0:T(8,128)(2,1)S(1)}) custom-call(s32[1,128]{1,0:T(1,128)S(1)} %slot_table.1.table_ref, f32[256,512]{1,0:T(8,128)S(1)} %copy-done, s32[256,1024]{1,0:T(8,128)S(1)} %copy-done.1, bf16[128,512]{1,0:T(8,128)(2,1)S(1)} %copy-done.2, bf16[128,512]{1,0:T(8,128)(2,1)S(1)} %collective-permute-done.rest_1_.rest_3_, ...), custom_call_target="tpu_custom_call" | custom-call | flops 8589934592 | bytes 1048576 | tf_op jit(solution)/shard_map/add_pieces/pallas_call | solution.py:308
  15.0 1.8 %collective-permute-done.3.rest_0_ = bf16[128,512]{1,0:T(8,128)(2,1)S(1)} collective-permute-done((bf16[128,512]{1,0:T(8,128)(2,1)S(1)}, bf16[128,512]{1,0:T(8,128)(2,1)S(1)}, u32[]{:S(2)}, u32[]{:S(2)}) %collective-permute-start.3) | collective-permute-done | bytes 131104 | tf_op jit(solution)/shard_map/ppermute | solution.py:29
  16.7 0.4 %collective-permute-start.4 = (bf16[128,512]{1,0:T(8,128)(2,1)S(1)}, bf16[128,512]{1,0:T(8,128)(2,1)S(1)}, u32[]{:S(2)}, u32[]{:S(2)}) collective-permute-start(bf16[128,512]{1,0:T(8,128)(2,1)S(1)} %collective-permute-done.3.rest_0_), channel_id=1, source_target_pairs={{0,4},{4,8},{8,12},{12,14},{14,10},{10,6},{6,2},{2,0},{1,3},{5,1},... | collective-permute-start | bytes 393224 | tf_op jit(solution)/shard_map/ppermute | solution.py:29
  17.1 0.0 collective-permute-done.5.rest_1_
  17.1 1.6 %collective-permute-start.6 = (bf16[128,512]{1,0:T(8,128)(2,1)S(1)}, bf16[128,512]{1,0:T(8,128)(2,1)S(1)}, u32[]{:S(2)}, u32[]{:S(2)}) collective-permute-start(bf16[128,512]{1,0:T(8,128)(2,1)S(1)} %collective-permute-done.5.rest_1_), channel_id=1, source_target_pairs={{0,2},{4,0},{8,4},{12,8},{14,12},{10,14},{6,10},{2,6},{1,5},{5,9},... | collective-permute-start | bytes 393224 | tf_op jit(solution)/shard_map/ppermute | solution.py:29
  18.8 0.1 add_pieces.5
  18.9 0.1 collective-permute-start.8
  19.0 3.1 %collective-permute-done.4.refs_0_.rest_0_ = bf16[128,512]{1,0:T(8,128)(2,1)S(1)} collective-permute-done((bf16[128,512]{1,0:T(8,128)(2,1)S(1)}, bf16[128,512]{1,0:T(8,128)(2,1)S(1)}, u32[]{:S(2)}, u32[]{:S(2)}) %collective-permute-start.4) | collective-permute-done | bytes 131104 | tf_op jit(solution)/shard_map/ppermute | solution.py:29
  22.1 0.0 collective-permute-done.6.refs_1_.rest_1_
  22.1 0.1 collective-permute-start.7
  22.2 0.0 collective-permute-done.8.rest_2_
  22.2 1.8 %add_pieces.6.rest_1_ = f32[256,512]{1,0:T(8,128)S(1)} custom-call(s32[1,128]{1,0:T(1,128)S(1)} %slot_table.1.table_ref, bf16[512,512]{1,0:T(8,128)(2,1)S(1)} %get-tuple-element.18.given_ref, s32[256,1024]{1,0:T(8,128)S(1)} %copy-done.1, bf16[128,512]{1,0:T(8,128)(2,1)S(1)} %collective-permute-done.4.refs_0_.rest_0_, ...), custom_call_target="tpu_custom_call", output_to_operand_aliasing={{}: (6, {})} | custom-call | flops 17179869184 | bytes 1048576 | tf_op jit(solution)/shard_map/add_pieces/pallas_call | solution.py:308
  24.1 0.0 collective-permute-done.7.rest_0_
  24.1 1.0 %add_pieces.7 = (f32[256,512]{1,0:T(8,128)S(1)}, f32[16,128]{1,0:T(8,128)S(1)}) custom-call(s32[1,128]{1,0:T(1,128)S(1)} %slot_table.1.table_ref, bf16[512,512]{1,0:T(8,128)(2,1)S(1)} %get-tuple-element.18.given_ref, s32[256,1024]{1,0:T(8,128)S(1)} %copy-done.1, ...), custom_call_target="tpu_custom_call", output_to_operand_aliasing={{0}: (4, {})} | custom-call | flops 4294967296 | bytes 1048576 | tf_op jit(solution)/shard_map/add_pieces/pallas_call | solution.py:308
  25.1 10.1 %all_to_all.11 = f32[16,1,128]{2,1,0:T(1,128)S(1)} all-to-all(f32[16,1,128]{2,1,0:T(1,128)S(1)} %bitcast.7), channel_id=1, replica_groups=mesh['group'=2,'loop'=16] {'loop'}, dimensions={0} | all-to-all | bytes 16384 | tf_op jit(solution)/shard_map/all_to_all | solution.py:450
  35.2 1.0 %update.1 = f32[256,512]{1,0:T(8,128)} custom-call(f32[256,512]{1,0:T(8,128)S(1)} %copy-done, f32[256,512]{1,0:T(8,128)S(1)} %get-tuple-element.25.grad_ref, f32[16,128]{1,0:T(8,128)S(1)} %bitcast.6), custom_call_target="tpu_custom_call" | custom-call | flops 262144 | bytes 1572864 | tf_op jit(solution)/shard_map/update/pallas_call | solution.py:451
  (1 shorter events, 0.0 us)
Async XLA Ops:
  0.0 9.5 %collective-permute-start = (bf16[128,512]{1,0:T(8,128)(2,1)}, bf16[128,512]{1,0:T(8,128)(2,1)S(1)}, u32[]{:S(2)}, u32[]{:S(2)}) collective-permute-start(bf16[128,512]{1,0:T(8,128)(2,1)} %rest_2_.1), channel_id=1, source_target_pairs={{0,4},{4,8},{8,12},{12,14},{14,10},{10,6},{6,2},{2,0},{1,3},{5,1},... | collective-permute-start | bytes 393224 | tf_op jit(solution)/shard_map/ppermute | solution.py:29
  3.0 6.5 %collective-permute-start.1 = (bf16[128,512]{1,0:T(8,128)(2,1)}, bf16[128,512]{1,0:T(8,128)(2,1)S(1)}, u32[]{:S(2)}, u32[]{:S(2)}) collective-permute-start(bf16[128,512]{1,0:T(8,128)(2,1)} %rest_2_.1), channel_id=1, source_target_pairs={{0,2},{4,0},{8,4},{12,8},{14,12},{10,14},{6,10},{2,6},{1,5},{5,9},... | collective-permute-start | bytes 393224 | tf_op jit(solution)/shard_map/ppermute | solution.py:29
  3.0 10.9 %collective-permute-start.2 = (bf16[128,512]{1,0:T(8,128)(2,1)}, bf16[128,512]{1,0:T(8,128)(2,1)S(1)}, u32[]{:S(2)}, u32[]{:S(2)}) collective-permute-start(bf16[128,512]{1,0:T(8,128)(2,1)} %rest_2_.1), channel_id=1, source_target_pairs={{0,14},{1,15},{4,10},{5,11},{8,6},{9,7},{12,2},{13,3},{14,0},{15,1... | collective-permute-start | bytes 393224 | tf_op jit(solution)/shard_map/ppermute | solution.py:35
  8.7 0.7 %copy-start.3 = (s32[1,8]{1,0:T(1,128)S(1)}, s32[1,8]{1,0:T(1,128)}, u32[]{:S(2)}) copy-start(s32[1,8]{1,0:T(1,128)} %list_ref.1) | copy-start | bytes 100
  9.3 4.6 %copy-start = (f32[256,512]{1,0:T(8,128)S(1)}, f32[256,512]{1,0:T(8,128)}, u32[]{:S(2)}) copy-start(f32[256,512]{1,0:T(8,128)} %users_ref.1) | copy-start | bytes 1572868
  9.3 4.6 %copy-start.1 = (s32[256,1024]{1,0:T(8,128)S(1)}, s32[256,1024]{1,0:T(8,128)}, u32[]{:S(2)}) copy-start(s32[256,1024]{1,0:T(8,128)} %labels_ref.7) | copy-start | bytes 3145732
  9.3 4.6 %copy-start.2 = (bf16[128,512]{1,0:T(8,128)(2,1)S(1)}, bf16[128,512]{1,0:T(8,128)(2,1)}, u32[]{:S(2)}) copy-start(bf16[128,512]{1,0:T(8,128)(2,1)} %rest_2_.1) | copy-start | bytes 393220
  9.5 7.2 %collective-permute-start.3 = (bf16[128,512]{1,0:T(8,128)(2,1)S(1)}, bf16[128,512]{1,0:T(8,128)(2,1)S(1)}, u32[]{:S(2)}, u32[]{:S(2)}) collective-permute-start(bf16[128,512]{1,0:T(8,128)(2,1)S(1)} %collective-permute-done.rest_1_.rest_3_), channel_id=1, source_target_pairs={{0,4},{4,8},{8,12},{12,14},{14,10},{10,6},{6,2},{2,0},{1,3},{5,1},... | collective-permute-start | bytes 393224 | tf_op jit(solution)/shard_map/ppermute | solution.py:29
  9.6 7.6 %collective-permute-start.5 = (bf16[128,512]{1,0:T(8,128)(2,1)S(1)}, bf16[128,512]{1,0:T(8,128)(2,1)S(1)}, u32[]{:S(2)}, u32[]{:S(2)}) collective-permute-start(bf16[128,512]{1,0:T(8,128)(2,1)S(1)} %collective-permute-done.1.rest_2_.rest_4_), channel_id=1, source_target_pairs={{0,2},{4,0},{8,4},{12,8},{14,12},{10,14},{6,10},{2,6},{1,5},{5,9},... | collective-permute-start | bytes 393224 | tf_op jit(solution)/shard_map/ppermute | solution.py:29
  16.7 5.4 %collective-permute-start.4 = (bf16[128,512]{1,0:T(8,128)(2,1)S(1)}, bf16[128,512]{1,0:T(8,128)(2,1)S(1)}, u32[]{:S(2)}, u32[]{:S(2)}) collective-permute-start(bf16[128,512]{1,0:T(8,128)(2,1)S(1)} %collective-permute-done.3.rest_0_), channel_id=1, source_target_pairs={{0,4},{4,8},{8,12},{12,14},{14,10},{10,6},{6,2},{2,0},{1,3},{5,1},... | collective-permute-start | bytes 393224 | tf_op jit(solution)/shard_map/ppermute | solution.py:29
  17.1 5.0 %collective-permute-start.6 = (bf16[128,512]{1,0:T(8,128)(2,1)S(1)}, bf16[128,512]{1,0:T(8,128)(2,1)S(1)}, u32[]{:S(2)}, u32[]{:S(2)}) collective-permute-start(bf16[128,512]{1,0:T(8,128)(2,1)S(1)} %collective-permute-done.5.rest_1_), channel_id=1, source_target_pairs={{0,2},{4,0},{8,4},{12,8},{14,12},{10,14},{6,10},{2,6},{1,5},{5,9},... | collective-permute-start | bytes 393224 | tf_op jit(solution)/shard_map/ppermute | solution.py:29
  18.9 3.3 %collective-permute-start.8 = (bf16[768,512]{1,0:T(8,128)(2,1)S(1)}, bf16[768,512]{1,0:T(8,128)(2,1)S(1)}, u32[]{:S(2)}, u32[]{:S(2)}) collective-permute-start(bf16[768,512]{1,0:T(8,128)(2,1)S(1)} %get-tuple-element.23), channel_id=1, source_target_pairs={{0,1},{1,0},{2,3},{3,2},{4,5},{5,4},{6,7},{7,6},{8,9},{9,8},{10,11... | collective-permute-start | bytes 2359304 | tf_op jit(solution)/shard_map/ppermute | solution.py:39
  22.1 1.9 %collective-permute-start.7 = (bf16[256,512]{1,0:T(8,128)(2,1)S(1)}, bf16[256,512]{1,0:T(8,128)(2,1)S(1)}, u32[]{:S(2)}, u32[]{:S(2)}) collective-permute-start(bf16[256,512]{1,0:T(8,128)(2,1)S(1)} %pack.1), channel_id=1, source_target_pairs={{0,1},{1,0},{2,3},{3,2},{4,5},{5,4},{6,7},{7,6},{8,9},{9,8},{10,11... | collective-permute-start | bytes 786440 | tf_op jit(solution)/shard_map/ppermute | solution.py:39

commit v12 on v10

--- a/solution.py
+++ b/solution.py
@@ -352,8 +352,9 @@
         return to_other_core(arrays, loop_size), [where[-hop, 1] for hop in hops]
 
     up = to_next(items, 1, loop_size)
-    down = to_next(items, -1, loop_size)
-    up, table = lax.optimization_barrier((up, table))
+    later, table = lax.optimization_barrier((items, table))
+    down = to_next(later, -1, loop_size)
+    down, up = down, lax.optimization_barrier((up, table))[0]
     first = [held(0, items), held(1, up), held(-1, down)]
     second = [held(2, to_next(up, 1, loop_size)), held(-2, to_next(down, -1, loop_size))]
     gradient, parts, opposite, packed = add_pieces(

time: 36 us -> 38 us (1.056)
  waiting for transfers between devices: 6.41 us -> 9.4 us
  Pallas kernels: 5.19 us -> 3.53 us
  local copies, waits for them, and re-layouts: 0.66 us -> 1.41 us
  blocking collectives: 11.5 us -> 11.9 us
    pallas_call x4, Pallas kernels: 4.04 us -> 2.37 us  [add_pieces(): pl.pallas_call(functools.partial(pieces_kernel, places, len(arrays), pack...]
    ppermute x6, waiting for transfers between devices: 5.75 us -> 7.29 us  [to_next(): return lax.ppermute(array, 'loop', pairs)]
    ppermute x3, waiting for transfers between devices: 0.01 us -> 1.49 us  [to_other_core(): lax.ppermute(array, 'loop', [(at, at ^ 1) for at in range(loop_size)])]
    unnamed x8, local copies, waits for them, and re-layouts: 0.66 us -> 1.41 us
    ppermute x6, starting transfers between devices: 6.91 us -> 6.51 us  [to_next(): return lax.ppermute(array, 'loop', pairs)]
  transfers between devices with their start and end apart: 10 -> 10, of which waited for: 5 -> 7; matrix products, arithmetic and copies ran while one was open for 0% -> 0% of each run, Pallas kernels for 9% -> 4%
where the time goes in v12:
time: 38 us; the launch traced here: 37.9 us
  blocking collectives  11.9 us (31%)
  starting transfers between devices  11 us (29%)
  waiting for transfers between devices  9.4 us (25%)
  Pallas kernels  3.53 us (9%)
  local copies, waits for them, and re-layouts  1.41 us (4%)
  between operations  0.72 us (2%)
    all_to_all x1, blocking collectives, local(): squares = lax.all_to_all(square, 'loop', 0, 0, tiled=True)  11.9 us
    ppermute x6, waiting for transfers between devices, to_next(): return lax.ppermute(array, 'loop', pairs)  7.29 us
    ppermute x6, starting transfers between devices, to_next(): return lax.ppermute(array, 'loop', pairs)  6.51 us
    ppermute x1, starting transfers between devices, across(): return lax.ppermute(array, 'loop', pairs)  4.27 us
    pallas_call x4, Pallas kernels, add_pieces(): pl.pallas_call(functools.partial(pieces_kernel, places, len(arrays), pack...  2.37 us
    ppermute x3, waiting for transfers between devices, to_other_core(): lax.ppermute(array, 'loop', [(at, at ^ 1) for at in range(loop_size)])  1.49 us
    unnamed x8, local copies, waits for them, and re-layouts  1.41 us
    pallas_call x1, Pallas kernels, local(): pl.pallas_call(functools.partial(update_kernel, rows * loop_size * width)...  0.98 us
  transfers between devices with their start and end apart: 10, of which 7 were waited for; matrix products, arithmetic and copies ran while one was open for 0% of the time, Pallas kernels for 4%

profile of v12, /device:TPU:0, one launch (start us, length us, event | category | flops | bytes accessed | tf_op | source)
XLA Modules:
  0.0 37.9 jit_solution(639613726416470524)
XLA Ops:
  0.0 3.0 %collective-permute-start = (bf16[128,512]{1,0:T(8,128)(2,1)}, bf16[128,512]{1,0:T(8,128)(2,1)S(1)}, u32[]{:S(2)}, u32[]{:S(2)}) collective-permute-start(bf16[128,512]{1,0:T(8,128)(2,1)} %rest_0_.1), channel_id=1, source_target_pairs={{0,4},{4,8},{8,12},{12,14},{14,10},{10,6},{6,2},{2,0},{1,3},{5,1},... | collective-permute-start | bytes 393224 | tf_op jit(solution)/shard_map/ppermute | solution.py:29
  3.7 0.0 copy-start.3
  3.7 0.6 %copy-done.3 = s32[1,8]{1,0:T(1,128)S(1)} copy-done((s32[1,8]{1,0:T(1,128)S(1)}, s32[1,8]{1,0:T(1,128)}, u32[]{:S(2)}) %copy-start.3) | copy-done | bytes 56
  4.3 0.0 copy-start.2
  4.3 0.0 copy-start
  4.3 0.0 copy-start.1
  4.3 0.1 slot_table.1.table_ref
  4.5 0.7 %copy-done.2 = bf16[128,512]{1,0:T(8,128)(2,1)S(1)} copy-done((bf16[128,512]{1,0:T(8,128)(2,1)S(1)}, bf16[128,512]{1,0:T(8,128)(2,1)}, u32[]{:S(2)}) %copy-start.2) | copy-done | bytes 131096
  5.2 0.0 collective-permute-start.1
  5.2 1.1 %collective-permute-done.rest_1_ = bf16[128,512]{1,0:T(8,128)(2,1)S(1)} collective-permute-done((bf16[128,512]{1,0:T(8,128)(2,1)}, bf16[128,512]{1,0:T(8,128)(2,1)S(1)}, u32[]{:S(2)}, u32[]{:S(2)}) %collective-permute-start) | collective-permute-done | bytes 131104 | tf_op jit(solution)/shard_map/ppermute | solution.py:29
  6.4 2.4 %collective-permute-start.2 = (bf16[128,512]{1,0:T(8,128)(2,1)S(1)}, bf16[128,512]{1,0:T(8,128)(2,1)S(1)}, u32[]{:S(2)}, u32[]{:S(2)}) collective-permute-start(bf16[128,512]{1,0:T(8,128)(2,1)S(1)} %collective-permute-done.rest_1_), channel_id=1, source_target_pairs={{0,4},{4,8},{8,12},{12,14},{14,10},{10,6},{6,2},{2,0},{1,3},{5,1},... | collective-permute-start | bytes 393224 | tf_op jit(solution)/shard_map/ppermute | solution.py:29
  8.8 2.1 %collective-permute-done.1.rest_2_ = bf16[128,512]{1,0:T(8,128)(2,1)S(1)} collective-permute-done((bf16[128,512]{1,0:T(8,128)(2,1)S(1)}, bf16[128,512]{1,0:T(8,128)(2,1)S(1)}, u32[]{:S(2)}, u32[]{:S(2)}) %collective-permute-start.1) | collective-permute-done | bytes 131104 | tf_op jit(solution)/shard_map/ppermute | solution.py:29
  10.8 0.0 collective-permute-start.4
  10.8 0.0 copy-done
  10.8 0.0 copy-done.1
  10.9 0.3 add_pieces.4
  11.2 4.3 %collective-permute-start.6 = (bf16[128,512]{1,0:T(8,128)(2,1)S(1)}, bf16[128,512]{1,0:T(8,128)(2,1)S(1)}, u32[]{:S(2)}, u32[]{:S(2)}) collective-permute-start(bf16[128,512]{1,0:T(8,128)(2,1)S(1)} %get-tuple-element.24), channel_id=1, source_target_pairs={{0,12},{1,13},{4,6},{5,7},{8,10},{9,11},{12,0},{13,1},{14,2},{15,3... | collective-permute-start | bytes 393224 | tf_op jit(solution)/shard_map/ppermute | solution.py:39
  15.4 0.0 collective-permute-start.8
  15.4 0.0 collective-permute-done.2.rest_0_
  15.4 0.4 %collective-permute-start.3 = (bf16[128,512]{1,0:T(8,128)(2,1)S(1)}, bf16[128,512]{1,0:T(8,128)(2,1)S(1)}, u32[]{:S(2)}, u32[]{:S(2)}) collective-permute-start(bf16[128,512]{1,0:T(8,128)(2,1)S(1)} %collective-permute-done.2.rest_0_), channel_id=1, source_target_pairs={{0,4},{4,8},{8,12},{12,14},{14,10},{10,6},{6,2},{2,0},{1,3},{5,1},... | collective-permute-start | bytes 393224 | tf_op jit(solution)/shard_map/ppermute | solution.py:29
  15.9 1.3 %collective-permute-done.4.rest_1_ = bf16[128,512]{1,0:T(8,128)(2,1)S(1)} collective-permute-done((bf16[128,512]{1,0:T(8,128)(2,1)S(1)}, bf16[128,512]{1,0:T(8,128)(2,1)S(1)}, u32[]{:S(2)}, u32[]{:S(2)}) %collective-permute-start.4) | collective-permute-done | bytes 131104 | tf_op jit(solution)/shard_map/ppermute | solution.py:29
  17.2 0.7 %collective-permute-start.5 = (bf16[128,512]{1,0:T(8,128)(2,1)S(1)}, bf16[128,512]{1,0:T(8,128)(2,1)S(1)}, u32[]{:S(2)}, u32[]{:S(2)}) collective-permute-start(bf16[128,512]{1,0:T(8,128)(2,1)S(1)} %collective-permute-done.4.rest_1_), channel_id=1, source_target_pairs={{0,2},{4,0},{8,4},{12,8},{14,12},{10,14},{6,10},{2,6},{1,5},{5,9},... | collective-permute-start | bytes 393224 | tf_op jit(solution)/shard_map/ppermute | solution.py:29
  17.9 0.9 %add_pieces.5 = (f32[256,512]{1,0:T(8,128)S(1)}, bf16[256,512]{1,0:T(8,128)(2,1)S(1)}) custom-call(s32[1,128]{1,0:T(1,128)S(1)} %slot_table.1.table_ref, bf16[512,512]{1,0:T(8,128)(2,1)S(1)} %get-tuple-element.23.given_ref, s32[256,1024]{1,0:T(8,128)S(1)} %copy-done.1, ...), custom_call_target="tpu_custom_call", output_to_operand_aliasing={{0}: (5, {})} | custom-call | flops 4294967296 | bytes 1048576 | tf_op jit(solution)/shard_map/add_pieces/pallas_call | solution.py:320
  18.8 0.1 collective-permute-start.9
  18.9 0.6 %collective-permute-done.6.refs_2_.rest_2_ = bf16[128,512]{1,0:T(8,128)(2,1)S(1)} collective-permute-done((bf16[128,512]{1,0:T(8,128)(2,1)S(1)}, bf16[128,512]{1,0:T(8,128)(2,1)S(1)}, u32[]{:S(2)}, u32[]{:S(2)}) %collective-permute-start.6) | collective-permute-done | bytes 131104 | tf_op jit(solution)/shard_map/ppermute | solution.py:39
  19.5 1.3 %collective-permute-done.3.refs_0_.rest_0_ = bf16[128,512]{1,0:T(8,128)(2,1)S(1)} collective-permute-done((bf16[128,512]{1,0:T(8,128)(2,1)S(1)}, bf16[128,512]{1,0:T(8,128)(2,1)S(1)}, u32[]{:S(2)}, u32[]{:S(2)}) %collective-permute-start.3) | collective-permute-done | bytes 131104 | tf_op jit(solution)/shard_map/ppermute | solution.py:29
  20.8 1.4 %collective-permute-done.5.refs_1_.rest_1_ = bf16[128,512]{1,0:T(8,128)(2,1)S(1)} collective-permute-done((bf16[128,512]{1,0:T(8,128)(2,1)S(1)}, bf16[128,512]{1,0:T(8,128)(2,1)S(1)}, u32[]{:S(2)}, u32[]{:S(2)}) %collective-permute-start.5) | collective-permute-done | bytes 131104 | tf_op jit(solution)/shard_map/ppermute | solution.py:29
  22.3 0.1 collective-permute-start.7
  22.4 0.0 collective-permute-done.9.rest_4_
  22.4 0.0 collective-permute-done.8.rest_3_
  22.4 0.2 add_pieces.6.rest_1_
  22.6 1.5 %collective-permute-done.7.rest_0_ = bf16[384,512]{1,0:T(8,128)(2,1)S(1)} collective-permute-done((bf16[384,512]{1,0:T(8,128)(2,1)S(1)}, bf16[384,512]{1,0:T(8,128)(2,1)S(1)}, u32[]{:S(2)}, u32[]{:S(2)}) %collective-permute-start.7) | collective-permute-done | bytes 393248 | tf_op jit(solution)/shard_map/ppermute | solution.py:43
  24.0 1.0 %add_pieces.7 = (f32[256,512]{1,0:T(8,128)S(1)}, f32[16,128]{1,0:T(8,128)S(1)}) custom-call(s32[1,128]{1,0:T(1,128)S(1)} %slot_table.1.table_ref, bf16[512,512]{1,0:T(8,128)(2,1)S(1)} %get-tuple-element.23.given_ref, s32[256,1024]{1,0:T(8,128)S(1)} %copy-done.1, ...), custom_call_target="tpu_custom_call", output_to_operand_aliasing={{0}: (4, {})} | custom-call | flops 6442450944 | bytes 1048576 | tf_op jit(solution)/shard_map/add_pieces/pallas_call | solution.py:320
  25.0 11.9 %all_to_all.11 = f32[16,1,128]{2,1,0:T(1,128)S(1)} all-to-all(f32[16,1,128]{2,1,0:T(1,128)S(1)} %bitcast.7), channel_id=1, replica_groups=mesh['group'=2,'loop'=16] {'loop'}, dimensions={0} | all-to-all | bytes 16384 | tf_op jit(solution)/shard_map/all_to_all | solution.py:465
  37.0 1.0 %update.1 = f32[256,512]{1,0:T(8,128)} custom-call(f32[256,512]{1,0:T(8,128)S(1)} %copy-done, f32[256,512]{1,0:T(8,128)S(1)} %get-tuple-element.33.grad_ref, f32[16,128]{1,0:T(8,128)S(1)} %bitcast.6), custom_call_target="tpu_custom_call" | custom-call | flops 262144 | bytes 1572864 | tf_op jit(solution)/shard_map/update/pallas_call | solution.py:466
  (1 shorter events, 0.0 us)
Async XLA Ops:
  0.0 6.4 %collective-permute-start = (bf16[128,512]{1,0:T(8,128)(2,1)}, bf16[128,512]{1,0:T(8,128)(2,1)S(1)}, u32[]{:S(2)}, u32[]{:S(2)}) collective-permute-start(bf16[128,512]{1,0:T(8,128)(2,1)} %rest_0_.1), channel_id=1, source_target_pairs={{0,4},{4,8},{8,12},{12,14},{14,10},{10,6},{6,2},{2,0},{1,3},{5,1},... | collective-permute-start | bytes 393224 | tf_op jit(solution)/shard_map/ppermute | solution.py:29
  3.7 0.7 %copy-start.3 = (s32[1,8]{1,0:T(1,128)S(1)}, s32[1,8]{1,0:T(1,128)}, u32[]{:S(2)}) copy-start(s32[1,8]{1,0:T(1,128)} %list_ref.1) | copy-start | bytes 100
  4.3 0.9 %copy-start.2 = (bf16[128,512]{1,0:T(8,128)(2,1)S(1)}, bf16[128,512]{1,0:T(8,128)(2,1)}, u32[]{:S(2)}) copy-start(bf16[128,512]{1,0:T(8,128)(2,1)} %rest_0_.1) | copy-start | bytes 393220
  4.3 6.5 %copy-start = (f32[256,512]{1,0:T(8,128)S(1)}, f32[256,512]{1,0:T(8,128)}, u32[]{:S(2)}) copy-start(f32[256,512]{1,0:T(8,128)} %users_ref.1) | copy-start | bytes 1572868
  4.3 6.5 %copy-start.1 = (s32[256,1024]{1,0:T(8,128)S(1)}, s32[256,1024]{1,0:T(8,128)}, u32[]{:S(2)}) copy-start(s32[256,1024]{1,0:T(8,128)} %labels_ref.7) | copy-start | bytes 3145732
  5.2 5.6 %collective-permute-start.1 = (bf16[128,512]{1,0:T(8,128)(2,1)S(1)}, bf16[128,512]{1,0:T(8,128)(2,1)S(1)}, u32[]{:S(2)}, u32[]{:S(2)}) collective-permute-start(bf16[128,512]{1,0:T(8,128)(2,1)S(1)} %copy-done.2), channel_id=1, source_target_pairs={{0,2},{4,0},{8,4},{12,8},{14,12},{10,14},{6,10},{2,6},{1,5},{5,9},... | collective-permute-start | bytes 393224 | tf_op jit(solution)/shard_map/ppermute | solution.py:29
  6.4 9.0 %collective-permute-start.2 = (bf16[128,512]{1,0:T(8,128)(2,1)S(1)}, bf16[128,512]{1,0:T(8,128)(2,1)S(1)}, u32[]{:S(2)}, u32[]{:S(2)}) collective-permute-start(bf16[128,512]{1,0:T(8,128)(2,1)S(1)} %collective-permute-done.rest_1_), channel_id=1, source_target_pairs={{0,4},{4,8},{8,12},{12,14},{14,10},{10,6},{6,2},{2,0},{1,3},{5,1},... | collective-permute-start | bytes 393224 | tf_op jit(solution)/shard_map/ppermute | solution.py:29
  10.8 6.4 %collective-permute-start.4 = (bf16[128,512]{1,0:T(8,128)(2,1)S(1)}, bf16[128,512]{1,0:T(8,128)(2,1)S(1)}, u32[]{:S(2)}, u32[]{:S(2)}) collective-permute-start(bf16[128,512]{1,0:T(8,128)(2,1)S(1)} %collective-permute-done.1.rest_2_), channel_id=1, source_target_pairs={{0,2},{4,0},{8,4},{12,8},{14,12},{10,14},{6,10},{2,6},{1,5},{5,9},... | collective-permute-start | bytes 393224 | tf_op jit(solution)/shard_map/ppermute | solution.py:29
  11.2 8.4 %collective-permute-start.6 = (bf16[128,512]{1,0:T(8,128)(2,1)S(1)}, bf16[128,512]{1,0:T(8,128)(2,1)S(1)}, u32[]{:S(2)}, u32[]{:S(2)}) collective-permute-start(bf16[128,512]{1,0:T(8,128)(2,1)S(1)} %get-tuple-element.24), channel_id=1, source_target_pairs={{0,12},{1,13},{4,6},{5,7},{8,10},{9,11},{12,0},{13,1},{14,2},{15,3... | collective-permute-start | bytes 393224 | tf_op jit(solution)/shard_map/ppermute | solution.py:39
  15.4 7.0 %collective-permute-start.8 = (bf16[384,512]{1,0:T(8,128)(2,1)S(1)}, bf16[384,512]{1,0:T(8,128)(2,1)S(1)}, u32[]{:S(2)}, u32[]{:S(2)}) collective-permute-start(bf16[384,512]{1,0:T(8,128)(2,1)S(1)} %get-tuple-element.30), channel_id=1, source_target_pairs={{0,1},{1,0},{2,3},{3,2},{4,5},{5,4},{6,7},{7,6},{8,9},{9,8},{10,11... | collective-permute-start | bytes 1179656 | tf_op jit(solution)/shard_map/ppermute | solution.py:43
  15.4 5.4 %collective-permute-start.3 = (bf16[128,512]{1,0:T(8,128)(2,1)S(1)}, bf16[128,512]{1,0:T(8,128)(2,1)S(1)}, u32[]{:S(2)}, u32[]{:S(2)}) collective-permute-start(bf16[128,512]{1,0:T(8,128)(2,1)S(1)} %collective-permute-done.2.rest_0_), channel_id=1, source_target_pairs={{0,4},{4,8},{8,12},{12,14},{14,10},{10,6},{6,2},{2,0},{1,3},{5,1},... | collective-permute-start | bytes 393224 | tf_op jit(solution)/shard_map/ppermute | solution.py:29
  17.2 5.0 %collective-permute-start.5 = (bf16[128,512]{1,0:T(8,128)(2,1)S(1)}, bf16[128,512]{1,0:T(8,128)(2,1)S(1)}, u32[]{:S(2)}, u32[]{:S(2)}) collective-permute-start(bf16[128,512]{1,0:T(8,128)(2,1)S(1)} %collective-permute-done.4.rest_1_), channel_id=1, source_target_pairs={{0,2},{4,0},{8,4},{12,8},{14,12},{10,14},{6,10},{2,6},{1,5},{5,9},... | collective-permute-start | bytes 393224 | tf_op jit(solution)/shard_map/ppermute | solution.py:29
  18.8 3.6 %collective-permute-start.9 = (bf16[256,512]{1,0:T(8,128)(2,1)S(1)}, bf16[256,512]{1,0:T(8,128)(2,1)S(1)}, u32[]{:S(2)}, u32[]{:S(2)}) collective-permute-start(bf16[256,512]{1,0:T(8,128)(2,1)S(1)} %get-tuple-element.31), channel_id=1, source_target_pairs={{0,1},{1,0},{2,3},{3,2},{4,5},{5,4},{6,7},{7,6},{8,9},{9,8},{10,11... | collective-permute-start | bytes 786440 | tf_op jit(solution)/shard_map/ppermute | solution.py:43
  22.3 1.8 %collective-permute-start.7 = (bf16[384,512]{1,0:T(8,128)(2,1)S(1)}, bf16[384,512]{1,0:T(8,128)(2,1)S(1)}, u32[]{:S(2)}, u32[]{:S(2)}) collective-permute-start(bf16[384,512]{1,0:T(8,128)(2,1)S(1)} %pack.1), channel_id=1, source_target_pairs={{0,1},{1,0},{2,3},{3,2},{4,5},{5,4},{6,7},{7,6},{8,9},{9,8},{10,11... | collective-permute-start | bytes 1179656 | tf_op jit(solution)/shard_map/ppermute | solution.py:43

commit v13 on v10

--- a/solution.py
+++ b/solution.py
@@ -81,16 +81,18 @@
 def add_some(grad_ref, parts_ref, tiles, start, count, labels_at):
     rows = grad_ref.shape[0]
     tile = tiles.shape[0] // CHUNK
-    block = tiles[pl.ds(pl.multiple_of(start * tile, 2 * tile), count * tile), :]
+    block = tiles[pl.ds(pl.multiple_of(start * tile, tile), count * tile), :]
     upper, lower = [], []
     for at in range(0, count, 2):
+        few = min(2, count)
         both = lax.dot_general(
             parts_ref[...],
-            block[at * tile : (at + 2) * tile],
+            block[at * tile : (at + few) * tile],
             (((1,), (1,)), ((), ())),
             preferred_element_type=jnp.float32,
         )
-        labels = jnp.concatenate([labels_at(start + at), labels_at(start + at + 1)], 1)
+        labels = [labels_at(start + at + more) for more in range(few)]
+        labels = labels[0] if few == 1 else jnp.concatenate(labels, 1)
         residual = 0.5 * jnp.tanh(both[:rows] + both[rows:]) + (0.5 - labels.astype(jnp.float32))
         upper.append(residual.astype(jnp.bfloat16))
         lower.append((residual - upper[-1].astype(jnp.float32)).astype(jnp.bfloat16))
@@ -103,14 +105,14 @@
 
 def add_tiles(grad_ref, parts_ref, tiles, live, most, labels_at):
     tile = tiles.shape[0] // CHUNK
-
-    @pl.when(live % 2 == 1)
-    def _():
-        blank = pl.multiple_of(live * tile, tile)
-        tiles[pl.ds(blank, tile), :] = jnp.zeros((tile, tiles.shape[1]), tiles.dtype)
-
-    fours = (live + 1) // 4 if most > 2 else jnp.int32(0)
-    if most > 2:
+    fours = jnp.int32(0)
+    if most > 3:
+        fours = (live + 1) // 4
+
+        @pl.when(live % 4 == 3)
+        def _():
+            blank = pl.multiple_of(live * tile, tile)
+            tiles[pl.ds(blank, tile), :] = jnp.zeros((tile, tiles.shape[1]), tiles.dtype)
 
         def four(index, carry):
             add_some(grad_ref, parts_ref, tiles, index * 4, 4, labels_at)
@@ -118,9 +120,11 @@
 
         lax.fori_loop(0, fours, four, 0)
 
-    @pl.when(live > 4 * fours)
-    def _():
-        add_some(grad_ref, parts_ref, tiles, 4 * fours, 2, labels_at)
+    def one(index, carry):
+        add_some(grad_ref, parts_ref, tiles, index, 1, labels_at)
+        return carry
+
+    lax.fori_loop(4 * fours, jnp.maximum(live, 4 * fours), one, 0)
 
 
 def store_square(grad_ref, square_ref):
@@ -366,11 +370,11 @@
     second = other(packed, [2, -2])
     third.append(held(4, opposite))
     arrived, gradient = lax.optimization_barrier(([array for array, _ in third], gradient))
-    last = other(pack(arrived), [3, -3, 4])
+    final = other(pack(arrived), [3, -3, 4])
     (gradient,) = add_pieces(
         third + [first, second], [], loop_size, table, parts, labels, gradient, False
     )
-    return *add_pieces([last], [], loop_size, table, parts, labels, gradient, True), users
+    return *add_pieces([final], [], loop_size, table, parts, labels, gradient, True), users
 
 
 def chunks_kernel(
@@ -443,11 +447,19 @@
     )(*lists, users, labels, items)
 
 
-def update_kernel(entries, users_ref, grad_ref, squares_ref, out_ref):
+def update_kernel(entries, users_ref, grad_ref, squares_ref, out_ref, result, sems):
     total = jnp.sum(squares_ref[...], axis=0, keepdims=True)
     total = jnp.sum(total, axis=1, keepdims=True)
     scale = 0.5 / jnp.sqrt(total / entries + 1e-06)
-    out_ref[...] = users_ref[...] - scale * grad_ref[...]
+    rows = users_ref.shape[0] // sems.shape[0]
+    copies = []
+    for at in range(sems.shape[0]):
+        part = pl.ds(at * rows, rows)
+        result[part, :] = users_ref[part, :] - scale * grad_ref[part, :]
+        copies.append(pltpu.make_async_copy(result.at[part, :], out_ref.at[part, :], sems.at[at]))
+        copies[-1].start()
+    for copy in copies:
+        copy.wait()
 
 
 def local(users, items, tile_blocks, tile_count, labels):
@@ -466,7 +478,8 @@
         functools.partial(update_kernel, rows * loop_size * width),
         out_shape=jax.ShapeDtypeStruct((rows, width), jnp.float32),
         in_specs=[pl.BlockSpec(memory_space=pltpu.VMEM)] * 3,
-        out_specs=pl.BlockSpec(memory_space=pltpu.VMEM),
+        out_specs=pl.BlockSpec(memory_space=pl.ANY),
+        scratch_shapes=[pltpu.VMEM((rows, width), jnp.float32), pltpu.SemaphoreType.DMA((4,))],
         compiler_params=pltpu.CompilerParams(vmem_limit_bytes=16 * 1024 * 1024),
         cost_estimate=pl.CostEstimate(
             flops=2 * rows * width, bytes_accessed=12 * rows * width, transcendentals=0

time: 36 us -> 35.5 us (0.986)
  waiting for transfers between devices: 6.41 us -> 8.71 us
  Pallas kernels: 5.19 us -> 3.47 us
  starting transfers between devices: 11.3 us -> 10.4 us
    ppermute x1, waiting for transfers between devices: 0.65 us -> 2.43 us  [across(): return lax.ppermute(array, 'loop', pairs)]
    pallas_call x4, Pallas kernels: 4.04 us -> 2.36 us  [add_pieces(): pl.pallas_call(functools.partial(pieces_kernel, places, len(arrays), pack...]
    ppermute x1, starting transfers between devices: 4.16 us -> 3.37 us  [across(): return lax.ppermute(array, 'loop', pairs)]
    ppermute x3, waiting for transfers between devices: 0.01 us -> 0.72 us  [to_other_core(): lax.ppermute(array, 'loop', [(at, at ^ 1) for at in range(loop_size)])]
  transfers between devices with their start and end apart: 10 -> 10, of which waited for: 5 -> 7; matrix products, arithmetic and copies ran while one was open for 0% -> 0% of each run, Pallas kernels for 9% -> 4%
where the time goes in v13:
time: 35.5 us; the launch traced here: 35.3 us
  blocking collectives  11.4 us (32%)
  starting transfers between devices  10.4 us (29%)
  waiting for transfers between devices  8.71 us (25%)
  Pallas kernels  3.47 us (10%)
  between operations  0.74 us (2%)
  local copies, waits for them, and re-layouts  0.66 us (2%)
    all_to_all x1, blocking collectives, local(): squares = lax.all_to_all(square, 'loop', 0, 0, tiled=True)  11.4 us
    ppermute x6, starting transfers between devices, to_next(): return lax.ppermute(array, 'loop', pairs)  6.88 us
    ppermute x6, waiting for transfers between devices, to_next(): return lax.ppermute(array, 'loop', pairs)  5.55 us
    ppermute x1, starting transfers between devices, across(): return lax.ppermute(array, 'loop', pairs)  3.37 us
    ppermute x1, waiting for transfers between devices, across(): return lax.ppermute(array, 'loop', pairs)  2.43 us
    pallas_call x4, Pallas kernels, add_pieces(): pl.pallas_call(functools.partial(pieces_kernel, places, len(arrays), pack...  2.36 us
    pallas_call x1, Pallas kernels, local(): pl.pallas_call(functools.partial(update_kernel, rows * loop_size * width)...  0.93 us
    ppermute x3, waiting for transfers between devices, to_other_core(): lax.ppermute(array, 'loop', [(at, at ^ 1) for at in range(loop_size)])  0.72 us
  transfers between devices with their start and end apart: 10, of which 7 were waited for; matrix products, arithmetic and copies ran while one was open for 0% of the time, Pallas kernels for 4%

profile of v13, /device:TPU:0, one launch (start us, length us, event | category | flops | bytes accessed | tf_op | source)
XLA Modules:
  0.0 35.3 jit_solution(3402602554996695882)
XLA Ops:
  0.0 3.0 %collective-permute-start = (bf16[128,512]{1,0:T(8,128)(2,1)}, bf16[128,512]{1,0:T(8,128)(2,1)S(1)}, u32[]{:S(2)}, u32[]{:S(2)}) collective-permute-start(bf16[128,512]{1,0:T(8,128)(2,1)} %rest_0_.1), channel_id=1, source_target_pairs={{0,4},{4,8},{8,12},{12,14},{14,10},{10,6},{6,2},{2,0},{1,3},{5,1},... | collective-permute-start | bytes 393224 | tf_op jit(solution)/shard_map/ppermute | solution.py:29
  3.0 0.0 collective-permute-start.1
  3.7 0.0 copy-start.3
  3.7 0.6 %copy-done.3 = s32[1,8]{1,0:T(1,128)S(1)} copy-done((s32[1,8]{1,0:T(1,128)S(1)}, s32[1,8]{1,0:T(1,128)}, u32[]{:S(2)}) %copy-start.3) | copy-done | bytes 56
  4.3 0.0 copy-start
  4.3 0.0 copy-start.1
  4.3 0.0 copy-start.2
  4.3 0.1 slot_table.1.table_ref
  4.5 2.5 %collective-permute-done.rest_1_ = bf16[128,512]{1,0:T(8,128)(2,1)S(1)} collective-permute-done((bf16[128,512]{1,0:T(8,128)(2,1)}, bf16[128,512]{1,0:T(8,128)(2,1)S(1)}, u32[]{:S(2)}, u32[]{:S(2)}) %collective-permute-start) | collective-permute-done | bytes 131104 | tf_op jit(solution)/shard_map/ppermute | solution.py:29
  7.0 1.5 %collective-permute-start.2 = (bf16[128,512]{1,0:T(8,128)(2,1)S(1)}, bf16[128,512]{1,0:T(8,128)(2,1)S(1)}, u32[]{:S(2)}, u32[]{:S(2)}) collective-permute-start(bf16[128,512]{1,0:T(8,128)(2,1)S(1)} %collective-permute-done.rest_1_), channel_id=1, source_target_pairs={{0,4},{4,8},{8,12},{12,14},{14,10},{10,6},{6,2},{2,0},{1,3},{5,1},... | collective-permute-start | bytes 393224 | tf_op jit(solution)/shard_map/ppermute | solution.py:29
  8.5 0.0 collective-permute-done.1.rest_2_
  8.5 0.9 %collective-permute-start.4 = (bf16[128,512]{1,0:T(8,128)(2,1)S(1)}, bf16[128,512]{1,0:T(8,128)(2,1)S(1)}, u32[]{:S(2)}, u32[]{:S(2)}) collective-permute-start(bf16[128,512]{1,0:T(8,128)(2,1)S(1)} %collective-permute-done.1.rest_2_), channel_id=1, source_target_pairs={{0,2},{4,0},{8,4},{12,8},{14,12},{10,14},{6,10},{2,6},{1,5},{5,9},... | collective-permute-start | bytes 393224 | tf_op jit(solution)/shard_map/ppermute | solution.py:29
  9.4 0.0 copy-done
  9.4 0.0 copy-done.1
  9.4 0.0 copy-done.2
  9.4 0.3 add_pieces.4
  9.7 3.4 %collective-permute-start.6 = (bf16[128,512]{1,0:T(8,128)(2,1)S(1)}, bf16[128,512]{1,0:T(8,128)(2,1)S(1)}, u32[]{:S(2)}, u32[]{:S(2)}) collective-permute-start(bf16[128,512]{1,0:T(8,128)(2,1)S(1)} %get-tuple-element.22), channel_id=1, source_target_pairs={{0,12},{1,13},{4,6},{5,7},{8,10},{9,11},{12,0},{13,1},{14,2},{15,3... | collective-permute-start | bytes 393224 | tf_op jit(solution)/shard_map/ppermute | solution.py:39
  13.1 0.0 collective-permute-start.8
  13.1 0.1 collective-permute-done.2.rest_0_
  13.2 1.0 %collective-permute-start.3 = (bf16[128,512]{1,0:T(8,128)(2,1)S(1)}, bf16[128,512]{1,0:T(8,128)(2,1)S(1)}, u32[]{:S(2)}, u32[]{:S(2)}) collective-permute-start(bf16[128,512]{1,0:T(8,128)(2,1)S(1)} %collective-permute-done.2.rest_0_), channel_id=1, source_target_pairs={{0,4},{4,8},{8,12},{12,14},{14,10},{10,6},{6,2},{2,0},{1,3},{5,1},... | collective-permute-start | bytes 393224 | tf_op jit(solution)/shard_map/ppermute | solution.py:29
  14.2 0.6 %collective-permute-done.4.rest_1_ = bf16[128,512]{1,0:T(8,128)(2,1)S(1)} collective-permute-done((bf16[128,512]{1,0:T(8,128)(2,1)S(1)}, bf16[128,512]{1,0:T(8,128)(2,1)S(1)}, u32[]{:S(2)}, u32[]{:S(2)}) %collective-permute-start.4) | collective-permute-done | bytes 131104 | tf_op jit(solution)/shard_map/ppermute | solution.py:29
  14.8 0.4 %collective-permute-start.5 = (bf16[128,512]{1,0:T(8,128)(2,1)S(1)}, bf16[128,512]{1,0:T(8,128)(2,1)S(1)}, u32[]{:S(2)}, u32[]{:S(2)}) collective-permute-start(bf16[128,512]{1,0:T(8,128)(2,1)S(1)} %collective-permute-done.4.rest_1_), channel_id=1, source_target_pairs={{0,2},{4,0},{8,4},{12,8},{14,12},{10,14},{6,10},{2,6},{1,5},{5,9},... | collective-permute-start | bytes 393224 | tf_op jit(solution)/shard_map/ppermute | solution.py:29
  15.2 0.1 add_pieces.5
  15.3 0.1 collective-permute-start.9
  15.4 2.4 %collective-permute-done.6.refs_2_.rest_2_ = bf16[128,512]{1,0:T(8,128)(2,1)S(1)} collective-permute-done((bf16[128,512]{1,0:T(8,128)(2,1)S(1)}, bf16[128,512]{1,0:T(8,128)(2,1)S(1)}, u32[]{:S(2)}, u32[]{:S(2)}) %collective-permute-start.6) | collective-permute-done | bytes 131104 | tf_op jit(solution)/shard_map/ppermute | solution.py:39
  17.8 1.0 %collective-permute-done.3.refs_0_.rest_0_ = bf16[128,512]{1,0:T(8,128)(2,1)S(1)} collective-permute-done((bf16[128,512]{1,0:T(8,128)(2,1)S(1)}, bf16[128,512]{1,0:T(8,128)(2,1)S(1)}, u32[]{:S(2)}, u32[]{:S(2)}) %collective-permute-start.3) | collective-permute-done | bytes 131104 | tf_op jit(solution)/shard_map/ppermute | solution.py:29
  18.8 1.4 %collective-permute-done.5.refs_1_.rest_1_ = bf16[128,512]{1,0:T(8,128)(2,1)S(1)} collective-permute-done((bf16[128,512]{1,0:T(8,128)(2,1)S(1)}, bf16[128,512]{1,0:T(8,128)(2,1)S(1)}, u32[]{:S(2)}, u32[]{:S(2)}) %collective-permute-start.5) | collective-permute-done | bytes 131104 | tf_op jit(solution)/shard_map/ppermute | solution.py:29
  20.3 0.1 collective-permute-start.7
  20.3 0.0 collective-permute-done.9.rest_4_
  20.3 0.0 collective-permute-done.8.rest_3_
  20.4 1.0 %add_pieces.6.rest_1_ = f32[256,512]{1,0:T(8,128)S(1)} custom-call(s32[1,128]{1,0:T(1,128)S(1)} %slot_table.1.table_ref, bf16[512,512]{1,0:T(8,128)(2,1)S(1)} %get-tuple-element.21.given_ref, s32[256,1024]{1,0:T(8,128)S(1)} %copy-done.1, bf16[128,512]{1,0:T(8,128)(2,1)S(1)} %collective-permute-done.3.refs_0_.rest_0_, ...), custom_call_target="tpu_custom_call", output_to_operand_aliasing={{}: (8, {})} | custom-call | flops 17179869184 | bytes 1048576 | tf_op jit(solution)/shard_map/add_pieces/pallas_call | solution.py:324
  21.3 0.7 %collective-permute-done.7.rest_0_ = bf16[384,512]{1,0:T(8,128)(2,1)S(1)} collective-permute-done((bf16[384,512]{1,0:T(8,128)(2,1)S(1)}, bf16[384,512]{1,0:T(8,128)(2,1)S(1)}, u32[]{:S(2)}, u32[]{:S(2)}) %collective-permute-start.7) | collective-permute-done | bytes 393248 | tf_op jit(solution)/shard_map/ppermute | solution.py:43
  22.0 1.0 %add_pieces.7 = (f32[256,512]{1,0:T(8,128)S(1)}, f32[16,128]{1,0:T(8,128)S(1)}) custom-call(s32[1,128]{1,0:T(1,128)S(1)} %slot_table.1.table_ref, bf16[512,512]{1,0:T(8,128)(2,1)S(1)} %get-tuple-element.21.given_ref, s32[256,1024]{1,0:T(8,128)S(1)} %copy-done.1, ...), custom_call_target="tpu_custom_call", output_to_operand_aliasing={{0}: (4, {})} | custom-call | flops 6442450944 | bytes 1048576 | tf_op jit(solution)/shard_map/add_pieces/pallas_call | solution.py:324
  23.0 11.4 %all_to_all.11 = f32[16,1,128]{2,1,0:T(1,128)S(1)} all-to-all(f32[16,1,128]{2,1,0:T(1,128)S(1)} %bitcast.7), channel_id=1, replica_groups=mesh['group'=2,'loop'=16] {'loop'}, dimensions={0} | all-to-all | bytes 16384 | tf_op jit(solution)/shard_map/all_to_all | solution.py:476
  34.4 0.9 %update.1 = f32[256,512]{1,0:T(8,128)} custom-call(f32[256,512]{1,0:T(8,128)S(1)} %copy-done, f32[256,512]{1,0:T(8,128)S(1)} %get-tuple-element.31.grad_ref, f32[16,128]{1,0:T(8,128)S(1)} %bitcast.6), custom_call_target="tpu_custom_call" | custom-call | flops 262144 | bytes 1572864 | tf_op jit(solution)/shard_map/update/pallas_call | solution.py:477
  (1 shorter events, 0.0 us)
Async XLA Ops:
  0.0 7.0 %collective-permute-start = (bf16[128,512]{1,0:T(8,128)(2,1)}, bf16[128,512]{1,0:T(8,128)(2,1)S(1)}, u32[]{:S(2)}, u32[]{:S(2)}) collective-permute-start(bf16[128,512]{1,0:T(8,128)(2,1)} %rest_0_.1), channel_id=1, source_target_pairs={{0,4},{4,8},{8,12},{12,14},{14,10},{10,6},{6,2},{2,0},{1,3},{5,1},... | collective-permute-start | bytes 393224 | tf_op jit(solution)/shard_map/ppermute | solution.py:29
  3.0 5.5 %collective-permute-start.1 = (bf16[128,512]{1,0:T(8,128)(2,1)}, bf16[128,512]{1,0:T(8,128)(2,1)S(1)}, u32[]{:S(2)}, u32[]{:S(2)}) collective-permute-start(bf16[128,512]{1,0:T(8,128)(2,1)} %rest_0_.1), channel_id=1, source_target_pairs={{0,2},{4,0},{8,4},{12,8},{14,12},{10,14},{6,10},{2,6},{1,5},{5,9},... | collective-permute-start | bytes 393224 | tf_op jit(solution)/shard_map/ppermute | solution.py:29
  3.7 0.7 %copy-start.3 = (s32[1,8]{1,0:T(1,128)S(1)}, s32[1,8]{1,0:T(1,128)}, u32[]{:S(2)}) copy-start(s32[1,8]{1,0:T(1,128)} %list_ref.1) | copy-start | bytes 100
  4.3 5.1 %copy-start = (f32[256,512]{1,0:T(8,128)S(1)}, f32[256,512]{1,0:T(8,128)}, u32[]{:S(2)}) copy-start(f32[256,512]{1,0:T(8,128)} %users_ref.1) | copy-start | bytes 1572868
  4.3 5.1 %copy-start.1 = (s32[256,1024]{1,0:T(8,128)S(1)}, s32[256,1024]{1,0:T(8,128)}, u32[]{:S(2)}) copy-start(s32[256,1024]{1,0:T(8,128)} %labels_ref.7) | copy-start | bytes 3145732
  4.3 5.1 %copy-start.2 = (bf16[128,512]{1,0:T(8,128)(2,1)S(1)}, bf16[128,512]{1,0:T(8,128)(2,1)}, u32[]{:S(2)}) copy-start(bf16[128,512]{1,0:T(8,128)(2,1)} %rest_0_.1) | copy-start | bytes 393220
  7.0 6.2 %collective-permute-start.2 = (bf16[128,512]{1,0:T(8,128)(2,1)S(1)}, bf16[128,512]{1,0:T(8,128)(2,1)S(1)}, u32[]{:S(2)}, u32[]{:S(2)}) collective-permute-start(bf16[128,512]{1,0:T(8,128)(2,1)S(1)} %collective-permute-done.rest_1_), channel_id=1, source_target_pairs={{0,4},{4,8},{8,12},{12,14},{14,10},{10,6},{6,2},{2,0},{1,3},{5,1},... | collective-permute-start | bytes 393224 | tf_op jit(solution)/shard_map/ppermute | solution.py:29
  8.5 6.3 %collective-permute-start.4 = (bf16[128,512]{1,0:T(8,128)(2,1)S(1)}, bf16[128,512]{1,0:T(8,128)(2,1)S(1)}, u32[]{:S(2)}, u32[]{:S(2)}) collective-permute-start(bf16[128,512]{1,0:T(8,128)(2,1)S(1)} %collective-permute-done.1.rest_2_), channel_id=1, source_target_pairs={{0,2},{4,0},{8,4},{12,8},{14,12},{10,14},{6,10},{2,6},{1,5},{5,9},... | collective-permute-start | bytes 393224 | tf_op jit(solution)/shard_map/ppermute | solution.py:29
  9.7 8.1 %collective-permute-start.6 = (bf16[128,512]{1,0:T(8,128)(2,1)S(1)}, bf16[128,512]{1,0:T(8,128)(2,1)S(1)}, u32[]{:S(2)}, u32[]{:S(2)}) collective-permute-start(bf16[128,512]{1,0:T(8,128)(2,1)S(1)} %get-tuple-element.22), channel_id=1, source_target_pairs={{0,12},{1,13},{4,6},{5,7},{8,10},{9,11},{12,0},{13,1},{14,2},{15,3... | collective-permute-start | bytes 393224 | tf_op jit(solution)/shard_map/ppermute | solution.py:39
  13.1 7.3 %collective-permute-start.8 = (bf16[384,512]{1,0:T(8,128)(2,1)S(1)}, bf16[384,512]{1,0:T(8,128)(2,1)S(1)}, u32[]{:S(2)}, u32[]{:S(2)}) collective-permute-start(bf16[384,512]{1,0:T(8,128)(2,1)S(1)} %get-tuple-element.28), channel_id=1, source_target_pairs={{0,1},{1,0},{2,3},{3,2},{4,5},{5,4},{6,7},{7,6},{8,9},{9,8},{10,11... | collective-permute-start | bytes 1179656 | tf_op jit(solution)/shard_map/ppermute | solution.py:43
  13.2 5.7 %collective-permute-start.3 = (bf16[128,512]{1,0:T(8,128)(2,1)S(1)}, bf16[128,512]{1,0:T(8,128)(2,1)S(1)}, u32[]{:S(2)}, u32[]{:S(2)}) collective-permute-start(bf16[128,512]{1,0:T(8,128)(2,1)S(1)} %collective-permute-done.2.rest_0_), channel_id=1, source_target_pairs={{0,4},{4,8},{8,12},{12,14},{14,10},{10,6},{6,2},{2,0},{1,3},{5,1},... | collective-permute-start | bytes 393224 | tf_op jit(solution)/shard_map/ppermute | solution.py:29
  14.8 5.5 %collective-permute-start.5 = (bf16[128,512]{1,0:T(8,128)(2,1)S(1)}, bf16[128,512]{1,0:T(8,128)(2,1)S(1)}, u32[]{:S(2)}, u32[]{:S(2)}) collective-permute-start(bf16[128,512]{1,0:T(8,128)(2,1)S(1)} %collective-permute-done.4.rest_1_), channel_id=1, source_target_pairs={{0,2},{4,0},{8,4},{12,8},{14,12},{10,14},{6,10},{2,6},{1,5},{5,9},... | collective-permute-start | bytes 393224 | tf_op jit(solution)/shard_map/ppermute | solution.py:29
  15.3 5.0 %collective-permute-start.9 = (bf16[256,512]{1,0:T(8,128)(2,1)S(1)}, bf16[256,512]{1,0:T(8,128)(2,1)S(1)}, u32[]{:S(2)}, u32[]{:S(2)}) collective-permute-start(bf16[256,512]{1,0:T(8,128)(2,1)S(1)} %get-tuple-element.29), channel_id=1, source_target_pairs={{0,1},{1,0},{2,3},{3,2},{4,5},{5,4},{6,7},{7,6},{8,9},{9,8},{10,11... | collective-permute-start | bytes 786440 | tf_op jit(solution)/shard_map/ppermute | solution.py:43
  20.3 1.8 %collective-permute-start.7 = (bf16[384,512]{1,0:T(8,128)(2,1)S(1)}, bf16[384,512]{1,0:T(8,128)(2,1)S(1)}, u32[]{:S(2)}, u32[]{:S(2)}) collective-permute-start(bf16[384,512]{1,0:T(8,128)(2,1)S(1)} %pack.1), channel_id=1, source_target_pairs={{0,1},{1,0},{2,3},{3,2},{4,5},{5,4},{6,7},{7,6},{8,9},{9,8},{10,11... | collective-permute-start | bytes 1179656 | tf_op jit(solution)/shard_map/ppermute | solution.py:43

commit v14 on v13

--- a/solution.py
+++ b/solution.py
@@ -9,6 +9,7 @@
 
 CHUNK = 8
 RING = 16
+FEW = 3
 
 
 def ring_place(loop_size):
@@ -78,22 +79,19 @@
     )(block_list, live_count.reshape(1, 1))
 
 
-def add_some(grad_ref, parts_ref, tiles, start, count, labels_at):
+def add_block(grad_ref, parts_ref, block, labels):
     rows = grad_ref.shape[0]
-    tile = tiles.shape[0] // CHUNK
-    block = tiles[pl.ds(pl.multiple_of(start * tile, tile), count * tile), :]
+    tile = labels[0].shape[1]
     upper, lower = [], []
-    for at in range(0, count, 2):
-        few = min(2, count)
+    for at in range(0, len(labels), 2):
+        some = jnp.concatenate(labels[at : at + 2], 1)
         both = lax.dot_general(
             parts_ref[...],
-            block[at * tile : (at + few) * tile],
+            block[at * tile : at * tile + some.shape[1]],
             (((1,), (1,)), ((), ())),
             preferred_element_type=jnp.float32,
         )
-        labels = [labels_at(start + at + more) for more in range(few)]
-        labels = labels[0] if few == 1 else jnp.concatenate(labels, 1)
-        residual = 0.5 * jnp.tanh(both[:rows] + both[rows:]) + (0.5 - labels.astype(jnp.float32))
+        residual = 0.5 * jnp.tanh(both[:rows] + both[rows:]) + (0.5 - some.astype(jnp.float32))
         upper.append(residual.astype(jnp.bfloat16))
         lower.append((residual - upper[-1].astype(jnp.float32)).astype(jnp.bfloat16))
     grad_ref[...] += jnp.dot(
@@ -103,28 +101,23 @@
     )
 
 
-def add_tiles(grad_ref, parts_ref, tiles, live, most, labels_at):
+def add_tiles(grad_ref, parts_ref, tiles, live, labels_at):
     tile = tiles.shape[0] // CHUNK
-    fours = jnp.int32(0)
-    if most > 3:
-        fours = (live + 1) // 4
-
-        @pl.when(live % 4 == 3)
-        def _():
-            blank = pl.multiple_of(live * tile, tile)
-            tiles[pl.ds(blank, tile), :] = jnp.zeros((tile, tiles.shape[1]), tiles.dtype)
-
-        def four(index, carry):
-            add_some(grad_ref, parts_ref, tiles, index * 4, 4, labels_at)
-            return carry
-
-        lax.fori_loop(0, fours, four, 0)
-
-    def one(index, carry):
-        add_some(grad_ref, parts_ref, tiles, index, 1, labels_at)
+    fours = (live + 1) // 4
+
+    @pl.when(live % 4 == 3)
+    def _():
+        blank = pl.multiple_of(live * tile, tile)
+        tiles[pl.ds(blank, tile), :] = jnp.zeros((tile, tiles.shape[1]), tiles.dtype)
+
+    def add(count, index, carry):
+        start = index * count
+        block = tiles[pl.ds(pl.multiple_of(start * tile, tile), count * tile), :]
+        add_block(grad_ref, parts_ref, block, [labels_at(start + at) for at in range(count)])
         return carry
 
-    lax.fori_loop(4 * fours, jnp.maximum(live, 4 * fours), one, 0)
+    lax.fori_loop(0, fours, functools.partial(add, 4), 0)
+    lax.fori_loop(4 * fours, jnp.maximum(live, 4 * fours), functools.partial(add, 1), 0)
 
 
 def store_square(grad_ref, square_ref):
@@ -138,103 +131,6 @@
     me = lax.axis_index("loop")
     core, row, outer = me % 2, me // 2 % 2, me // 4
     return core, jnp.where(row == 0, outer, loop_size // 2 - 1 - outer)
-
-
-def table_kernel(loop_size, origins, list_ref, count_ref, table_ref):
-    chips = loop_size // 2
-    lane = lax.broadcasted_iota(jnp.int32, table_ref.shape, 1)
-    core, position = core_and_position(loop_size)
-    hops, other = jnp.zeros_like(lane), jnp.zeros_like(lane)
-    for at, origin in enumerate(origins):
-        hops = jnp.where(lane == at, origin[0], hops)
-        other = jnp.where(lane == at, origin[1], other)
-    at = (position + chips + jnp.where(core == 0, -hops, hops)) & (chips - 1)
-    chip = jnp.where(at < chips // 2, 2 * at, 2 * (chips - 1 - at) + 1)
-    block = 2 * chip + jnp.where(other == 1, 1 - core, core)
-    found = jnp.full_like(lane, -1)
-    for slot in range(list_ref.shape[1]):
-        name = jnp.where(slot < count_ref[...], list_ref[:, slot : slot + 1], -1)
-        found = jnp.where(name == block, slot, found)
-    table_ref[...] = jnp.where(lane < len(origins), found, -1)
-
-
-def slot_table(loop_size, origins, block_list, live_count):
-    return pl.pallas_call(
-        functools.partial(table_kernel, loop_size, origins),
-        out_shape=jax.ShapeDtypeStruct((1, 128), jnp.int32),
-        in_specs=[pl.BlockSpec(memory_space=pltpu.VMEM)] * 2,
-        out_specs=pl.BlockSpec(memory_space=pltpu.VMEM),
-        compiler_params=pltpu.CompilerParams(vmem_limit_bytes=16 * 1024 * 1024),
-        cost_estimate=pl.CostEstimate(flops=2**32, bytes_accessed=1024, transcendentals=0),
-        name="slot_table",
-    )(block_list, live_count.reshape(1, 1))
-
-
-def add_some(grad_ref, parts_ref, tiles, start, count, labels_at):
-    rows = grad_ref.shape[0]
-    tile = tiles.shape[0] // CHUNK
-    block = tiles[pl.ds(pl.multiple_of(start * tile, 2 * tile), count * tile), :]
-    upper, lower = [], []
-    for at in range(0, count, 2):
-        both = lax.dot_general(
-            parts_ref[...],
-            block[at * tile : (at + 2) * tile],
-            (((1,), (1,)), ((), ())),
-            preferred_element_type=jnp.float32,
-        )
-        labels = jnp.concatenate([labels_at(start + at), labels_at(start + at + 1)], 1)
-        residual = 0.5 * jnp.tanh(both[:rows] + both[rows:]) + (0.5 - labels.astype(jnp.float32))
-        upper.append(residual.astype(jnp.bfloat16))
-        lower.append((residual - upper[-1].astype(jnp.float32)).astype(jnp.bfloat16))
-    grad_ref[...] += jnp.dot(
-        jnp.concatenate(upper + lower, 1),
-        jnp.concatenate([block, block], 0),
-        preferred_element_type=jnp.float32,
-    )
-
-
-def add_tiles(grad_ref, parts_ref, tiles, live, most, labels_at):
-    tile = tiles.shape[0] // CHUNK
-
-    @pl.when(live % 2 == 1)
-    def _():
-        blank = pl.multiple_of(live * tile, tile)
-        tiles[pl.ds(blank, tile), :] = jnp.zeros((tile, tiles.shape[1]), tiles.dtype)
-
-    fours = (live + 1) // 4 if most > 2 else jnp.int32(0)
-    if most > 2:
-
-        def four(index, carry):
-            add_some(grad_ref, parts_ref, tiles, index * 4, 4, labels_at)
-            return carry
-
-        lax.fori_loop(0, fours, four, 0)
-
-    @pl.when(live > 4 * fours)
-    def _():
-        add_some(grad_ref, parts_ref, tiles, 4 * fours, 2, labels_at)
-
-
-def store_square(grad_ref, square_ref):
-    gradient = grad_ref[...]
-    square = jnp.sum(gradient * gradient, axis=0, keepdims=True)
-    square = sum(square[:, at : at + 128] for at in range(0, square.shape[1], 128))
-    square_ref[...] = jnp.broadcast_to(square, square_ref.shape)
-
-
-def core_and_position(loop_size):
-    me = lax.axis_index("loop")
-    core, row, outer = me % 2, me // 2 % 2, me // 4
-    return core, jnp.where(row == 0, outer, loop_size // 2 - 1 - outer)
-
-
-def origin_block(origin, loop_size):
-    hops, other = origin
-    chips = loop_size // 2
-    core, position = core_and_position(loop_size)
-    at = lax.rem(position + chips + jnp.where(core == 0, -hops, hops), chips)
-    chip = jnp.where(at < chips // 2, 2 * at, 2 * (chips - 1 - at) + 1)
-    return 2 * chip + (1 - core if other else core)
 
 
 def pack_kernel(*refs):
@@ -282,24 +178,33 @@
 
         parts_ref[...] = halves(0.5 * given_ref[...])
         grad_ref[...] = jnp.zeros_like(grad_ref)
-    live = jnp.int32(0)
     table = table_ref[...]
     entries = [table[0, at] for at, _, _ in places]
-    for found, (_, index, row) in zip(entries, places):
-
-        @pl.when(found >= 0)
-        def _():
-            into = pl.ds(pl.multiple_of(live * tile, tile), tile)
-            tiles[into, :] = arrays[index][row * tile : (row + 1) * tile, :]
-            slots[live] = found
-
-        live = live + (found >= 0).astype(jnp.int32)
-    slots[live] = 0
-
-    def labels_at(position):
-        return labels_ref[:, pl.ds(pl.multiple_of(slots[position] * tile, tile), tile)]
-
-    add_tiles(grad_ref, parts_ref, tiles, live, min(len(places), CHUNK), labels_at)
+
+    def labels_of(slot):
+        return labels_ref[:, pl.ds(pl.multiple_of(slot * tile, tile), tile)]
+
+    if len(places) <= FEW:
+        for found, (_, index, row) in zip(entries, places):
+
+            @pl.when(found >= 0)
+            def _():
+                block = arrays[index][row * tile : (row + 1) * tile, :]
+                add_block(grad_ref, parts_ref, block, [labels_of(found)])
+
+    else:
+        live = jnp.int32(0)
+        for found, (_, index, row) in zip(entries, places):
+
+            @pl.when(found >= 0)
+            def _():
+                into = pl.ds(pl.multiple_of(live * tile, tile), tile)
+                tiles[into, :] = arrays[index][row * tile : (row + 1) * tile, :]
+                slots[live] = found
+
+            live = live + (found >= 0).astype(jnp.int32)
+        slots[live] = 0
+        add_tiles(grad_ref, parts_ref, tiles, live, lambda position: labels_of(slots[position]))
     if last:
         store_square(grad_ref, square_ref)
 
@@ -403,7 +308,7 @@
     def labels_at(position):
         return labels_ref[:, pl.ds(pl.multiple_of(position * tile, tile), tile)]
 
-    add_tiles(grad_ref, parts_ref, tiles, live, CHUNK, labels_at)
+    add_tiles(grad_ref, parts_ref, tiles, live, labels_at)
 
     @pl.when(step == pl.num_programs(0) - 1)
     def _():

time: 35.5 us -> 36.3 us (1.023)
  waiting for transfers between devices: 8.71 us -> 6.12 us
  blocking collectives: 11.4 us -> 13.5 us
  Pallas kernels: 3.47 us -> 4.95 us
    all_to_all x1, blocking collectives: 11.4 us -> 13.5 us  [local(): squares = lax.all_to_all(square, 'loop', 0, 0, tiled=True)]
    ppermute x1, waiting for transfers between devices: 2.43 us -> 0.7 us  [across(): return lax.ppermute(array, 'loop', pairs)]
    pallas_call x4, Pallas kernels: 2.36 us -> 3.84 us  [add_pieces(): pl.pallas_call(functools.partial(pieces_kernel, places, len(arrays), pack...]
    ppermute x3, waiting for transfers between devices: 0.72 us -> 0.06 us  [to_other_core(): lax.ppermute(array, 'loop', [(at, at ^ 1) for at in range(loop_size)])]
    ppermute x6, starting transfers between devices: 6.88 us -> 7.47 us  [to_next(): return lax.ppermute(array, 'loop', pairs)]
    ppermute x1, starting transfers between devices: 3.37 us -> 2.82 us  [across(): return lax.ppermute(array, 'loop', pairs)]
  transfers between devices with their start and end apart: 10 -> 10, of which waited for: 7 -> 6; matrix products, arithmetic and copies ran while one was open for 0% -> 0% of each run, Pallas kernels for 4% -> 11%
where the time goes in v14:
time: 36.3 us; the launch traced here: 36.4 us
  blocking collectives  13.5 us (37%)
  starting transfers between devices  10.4 us (29%)
  waiting for transfers between devices  6.12 us (17%)
  Pallas kernels  4.95 us (14%)
  between operations  0.74 us (2%)
  local copies, waits for them, and re-layouts  0.66 us (2%)
    all_to_all x1, blocking collectives, local(): squares = lax.all_to_all(square, 'loop', 0, 0, tiled=True)  13.5 us
    ppermute x6, starting transfers between devices, to_next(): return lax.ppermute(array, 'loop', pairs)  7.47 us
    ppermute x6, waiting for transfers between devices, to_next(): return lax.ppermute(array, 'loop', pairs)  5.37 us
    pallas_call x4, Pallas kernels, add_pieces(): pl.pallas_call(functools.partial(pieces_kernel, places, len(arrays), pack...  3.84 us
    ppermute x1, starting transfers between devices, across(): return lax.ppermute(array, 'loop', pairs)  2.82 us
    pallas_call x1, Pallas kernels, local(): pl.pallas_call(functools.partial(update_kernel, rows * loop_size * width)...  0.93 us
  transfers between devices with their start and end apart: 10, of which 6 were waited for; matrix products, arithmetic and copies ran while one was open for 0% of the time, Pallas kernels for 11%

profile of v14, /device:TPU:0, one launch (start us, length us, event | category | flops | bytes accessed | tf_op | source)
XLA Modules:
  0.0 36.4 jit_solution(11874659941400475672)
XLA Ops:
  0.0 3.0 %collective-permute-start = (bf16[128,512]{1,0:T(8,128)(2,1)}, bf16[128,512]{1,0:T(8,128)(2,1)S(1)}, u32[]{:S(2)}, u32[]{:S(2)}) collective-permute-start(bf16[128,512]{1,0:T(8,128)(2,1)} %rest_0_.1), channel_id=1, source_target_pairs={{0,4},{4,8},{8,12},{12,14},{14,10},{10,6},{6,2},{2,0},{1,3},{5,1},... | collective-permute-start | bytes 393224 | tf_op jit(solution)/shard_map/ppermute | solution.py:30
  3.0 0.0 collective-permute-start.1
  3.7 0.0 copy-start.3
  3.7 0.6 %copy-done.3 = s32[1,8]{1,0:T(1,128)S(1)} copy-done((s32[1,8]{1,0:T(1,128)S(1)}, s32[1,8]{1,0:T(1,128)}, u32[]{:S(2)}) %copy-start.3) | copy-done | bytes 56
  4.3 0.0 copy-start
  4.3 0.0 copy-start.1
  4.3 0.0 copy-start.2
  4.3 0.1 slot_table.1.table_ref
  4.5 2.5 %collective-permute-done.rest_1_ = bf16[128,512]{1,0:T(8,128)(2,1)S(1)} collective-permute-done((bf16[128,512]{1,0:T(8,128)(2,1)}, bf16[128,512]{1,0:T(8,128)(2,1)S(1)}, u32[]{:S(2)}, u32[]{:S(2)}) %collective-permute-start) | collective-permute-done | bytes 131104 | tf_op jit(solution)/shard_map/ppermute | solution.py:30
  7.0 1.5 %collective-permute-start.2 = (bf16[128,512]{1,0:T(8,128)(2,1)S(1)}, bf16[128,512]{1,0:T(8,128)(2,1)S(1)}, u32[]{:S(2)}, u32[]{:S(2)}) collective-permute-start(bf16[128,512]{1,0:T(8,128)(2,1)S(1)} %collective-permute-done.rest_1_), channel_id=1, source_target_pairs={{0,4},{4,8},{8,12},{12,14},{14,10},{10,6},{6,2},{2,0},{1,3},{5,1},... | collective-permute-start | bytes 393224 | tf_op jit(solution)/shard_map/ppermute | solution.py:30
  8.5 0.0 collective-permute-done.1.rest_2_
  8.5 0.9 %collective-permute-start.4 = (bf16[128,512]{1,0:T(8,128)(2,1)S(1)}, bf16[128,512]{1,0:T(8,128)(2,1)S(1)}, u32[]{:S(2)}, u32[]{:S(2)}) collective-permute-start(bf16[128,512]{1,0:T(8,128)(2,1)S(1)} %collective-permute-done.1.rest_2_), channel_id=1, source_target_pairs={{0,2},{4,0},{8,4},{12,8},{14,12},{10,14},{6,10},{2,6},{1,5},{5,9},... | collective-permute-start | bytes 393224 | tf_op jit(solution)/shard_map/ppermute | solution.py:30
  9.4 0.0 copy-done
  9.4 0.0 copy-done.1
  9.4 0.0 copy-done.2
  9.4 0.8 %add_pieces.4 = (f32[256,512]{1,0:T(8,128)S(1)}, bf16[512,512]{1,0:T(8,128)(2,1)S(1)}, bf16[128,512]{1,0:T(8,128)(2,1)S(1)}, bf16[384,512]{1,0:T(8,128)(2,1)S(1)}) custom-call(s32[1,128]{1,0:T(1,128)S(1)} %slot_table.1.table_ref, f32[256,512]{1,0:T(8,128)S(1)} %copy-done, s32[256,1024]{1,0:T(8,128)S(1)} %copy-done.1, bf16[128,512]{1,0:T(8,128)(2,1)S(1)} %copy-done.2, ...), custom_call_target="tpu_custom_call" | custom-call | flops 6442450944 | bytes 1048576 | tf_op jit(solution)/shard_map/add_pieces/pallas_call | solution.py:229
  10.2 2.8 %collective-permute-start.6 = (bf16[128,512]{1,0:T(8,128)(2,1)S(1)}, bf16[128,512]{1,0:T(8,128)(2,1)S(1)}, u32[]{:S(2)}, u32[]{:S(2)}) collective-permute-start(bf16[128,512]{1,0:T(8,128)(2,1)S(1)} %get-tuple-element.22), channel_id=1, source_target_pairs={{0,12},{1,13},{4,6},{5,7},{8,10},{9,11},{12,0},{13,1},{14,2},{15,3... | collective-permute-start | bytes 393224 | tf_op jit(solution)/shard_map/ppermute | solution.py:40
  13.0 0.0 collective-permute-start.8
  13.0 0.1 collective-permute-done.2.rest_0_
  13.2 1.8 %collective-permute-start.3 = (bf16[128,512]{1,0:T(8,128)(2,1)S(1)}, bf16[128,512]{1,0:T(8,128)(2,1)S(1)}, u32[]{:S(2)}, u32[]{:S(2)}) collective-permute-start(bf16[128,512]{1,0:T(8,128)(2,1)S(1)} %collective-permute-done.2.rest_0_), channel_id=1, source_target_pairs={{0,4},{4,8},{8,12},{12,14},{14,10},{10,6},{6,2},{2,0},{1,3},{5,1},... | collective-permute-start | bytes 393224 | tf_op jit(solution)/shard_map/ppermute | solution.py:30
  15.0 0.0 collective-permute-done.4.rest_1_
  15.0 0.2 collective-permute-start.5
  15.2 1.2 %add_pieces.5 = (f32[256,512]{1,0:T(8,128)S(1)}, bf16[256,512]{1,0:T(8,128)(2,1)S(1)}) custom-call(s32[1,128]{1,0:T(1,128)S(1)} %slot_table.1.table_ref, bf16[512,512]{1,0:T(8,128)(2,1)S(1)} %get-tuple-element.21.given_ref, s32[256,1024]{1,0:T(8,128)S(1)} %copy-done.1, ...), custom_call_target="tpu_custom_call", output_to_operand_aliasing={{0}: (5, {})} | custom-call | flops 4294967296 | bytes 1048576 | tf_op jit(solution)/shard_map/add_pieces/pallas_call | solution.py:229
  16.4 0.1 collective-permute-start.9
  16.5 0.7 %collective-permute-done.6.refs_2_.rest_2_ = bf16[128,512]{1,0:T(8,128)(2,1)S(1)} collective-permute-done((bf16[128,512]{1,0:T(8,128)(2,1)S(1)}, bf16[128,512]{1,0:T(8,128)(2,1)S(1)}, u32[]{:S(2)}, u32[]{:S(2)}) %collective-permute-start.6) | collective-permute-done | bytes 131104 | tf_op jit(solution)/shard_map/ppermute | solution.py:40
  17.2 1.6 %collective-permute-done.3.refs_0_.rest_0_ = bf16[128,512]{1,0:T(8,128)(2,1)S(1)} collective-permute-done((bf16[128,512]{1,0:T(8,128)(2,1)S(1)}, bf16[128,512]{1,0:T(8,128)(2,1)S(1)}, u32[]{:S(2)}, u32[]{:S(2)}) %collective-permute-start.3) | collective-permute-done | bytes 131104 | tf_op jit(solution)/shard_map/ppermute | solution.py:30
  18.8 1.1 %collective-permute-done.5.refs_1_.rest_1_ = bf16[128,512]{1,0:T(8,128)(2,1)S(1)} collective-permute-done((bf16[128,512]{1,0:T(8,128)(2,1)S(1)}, bf16[128,512]{1,0:T(8,128)(2,1)S(1)}, u32[]{:S(2)}, u32[]{:S(2)}) %collective-permute-start.5) | collective-permute-done | bytes 131104 | tf_op jit(solution)/shard_map/ppermute | solution.py:30
  20.0 0.1 collective-permute-start.7
  20.1 0.0 collective-permute-done.9.rest_4_
  20.1 0.0 collective-permute-done.8.rest_3_
  20.1 1.6 %add_pieces.6.rest_1_ = f32[256,512]{1,0:T(8,128)S(1)} custom-call(s32[1,128]{1,0:T(1,128)S(1)} %slot_table.1.table_ref, bf16[512,512]{1,0:T(8,128)(2,1)S(1)} %get-tuple-element.21.given_ref, s32[256,1024]{1,0:T(8,128)S(1)} %copy-done.1, bf16[128,512]{1,0:T(8,128)(2,1)S(1)} %collective-permute-done.3.refs_0_.rest_0_, ...), custom_call_target="tpu_custom_call", output_to_operand_aliasing={{}: (8, {})} | custom-call | flops 17179869184 | bytes 1048576 | tf_op jit(solution)/shard_map/add_pieces/pallas_call | solution.py:229
  21.7 0.1 collective-permute-done.7.rest_0_
  21.8 0.2 add_pieces.7
  22.0 13.5 %all_to_all.11 = f32[16,1,128]{2,1,0:T(1,128)S(1)} all-to-all(f32[16,1,128]{2,1,0:T(1,128)S(1)} %bitcast.7), channel_id=1, replica_groups=mesh['group'=2,'loop'=16] {'loop'}, dimensions={0} | all-to-all | bytes 16384 | tf_op jit(solution)/shard_map/all_to_all | solution.py:381
  35.4 0.9 %update.1 = f32[256,512]{1,0:T(8,128)} custom-call(f32[256,512]{1,0:T(8,128)S(1)} %copy-done, f32[256,512]{1,0:T(8,128)S(1)} %get-tuple-element.31.grad_ref, f32[16,128]{1,0:T(8,128)S(1)} %bitcast.6), custom_call_target="tpu_custom_call" | custom-call | flops 262144 | bytes 1572864 | tf_op jit(solution)/shard_map/update/pallas_call | solution.py:382
  (1 shorter events, 0.0 us)
Async XLA Ops:
  0.0 7.0 %collective-permute-start = (bf16[128,512]{1,0:T(8,128)(2,1)}, bf16[128,512]{1,0:T(8,128)(2,1)S(1)}, u32[]{:S(2)}, u32[]{:S(2)}) collective-permute-start(bf16[128,512]{1,0:T(8,128)(2,1)} %rest_0_.1), channel_id=1, source_target_pairs={{0,4},{4,8},{8,12},{12,14},{14,10},{10,6},{6,2},{2,0},{1,3},{5,1},... | collective-permute-start | bytes 393224 | tf_op jit(solution)/shard_map/ppermute | solution.py:30
  3.0 5.5 %collective-permute-start.1 = (bf16[128,512]{1,0:T(8,128)(2,1)}, bf16[128,512]{1,0:T(8,128)(2,1)S(1)}, u32[]{:S(2)}, u32[]{:S(2)}) collective-permute-start(bf16[128,512]{1,0:T(8,128)(2,1)} %rest_0_.1), channel_id=1, source_target_pairs={{0,2},{4,0},{8,4},{12,8},{14,12},{10,14},{6,10},{2,6},{1,5},{5,9},... | collective-permute-start | bytes 393224 | tf_op jit(solution)/shard_map/ppermute | solution.py:30
  3.7 0.7 %copy-start.3 = (s32[1,8]{1,0:T(1,128)S(1)}, s32[1,8]{1,0:T(1,128)}, u32[]{:S(2)}) copy-start(s32[1,8]{1,0:T(1,128)} %list_ref.1) | copy-start | bytes 100
  4.3 5.1 %copy-start = (f32[256,512]{1,0:T(8,128)S(1)}, f32[256,512]{1,0:T(8,128)}, u32[]{:S(2)}) copy-start(f32[256,512]{1,0:T(8,128)} %users_ref.1) | copy-start | bytes 1572868
  4.3 5.1 %copy-start.1 = (s32[256,1024]{1,0:T(8,128)S(1)}, s32[256,1024]{1,0:T(8,128)}, u32[]{:S(2)}) copy-start(s32[256,1024]{1,0:T(8,128)} %labels_ref.7) | copy-start | bytes 3145732
  4.3 5.1 %copy-start.2 = (bf16[128,512]{1,0:T(8,128)(2,1)S(1)}, bf16[128,512]{1,0:T(8,128)(2,1)}, u32[]{:S(2)}) copy-start(bf16[128,512]{1,0:T(8,128)(2,1)} %rest_0_.1) | copy-start | bytes 393220
  7.0 6.2 %collective-permute-start.2 = (bf16[128,512]{1,0:T(8,128)(2,1)S(1)}, bf16[128,512]{1,0:T(8,128)(2,1)S(1)}, u32[]{:S(2)}, u32[]{:S(2)}) collective-permute-start(bf16[128,512]{1,0:T(8,128)(2,1)S(1)} %collective-permute-done.rest_1_), channel_id=1, source_target_pairs={{0,4},{4,8},{8,12},{12,14},{14,10},{10,6},{6,2},{2,0},{1,3},{5,1},... | collective-permute-start | bytes 393224 | tf_op jit(solution)/shard_map/ppermute | solution.py:30
  8.5 6.5 %collective-permute-start.4 = (bf16[128,512]{1,0:T(8,128)(2,1)S(1)}, bf16[128,512]{1,0:T(8,128)(2,1)S(1)}, u32[]{:S(2)}, u32[]{:S(2)}) collective-permute-start(bf16[128,512]{1,0:T(8,128)(2,1)S(1)} %collective-permute-done.1.rest_2_), channel_id=1, source_target_pairs={{0,2},{4,0},{8,4},{12,8},{14,12},{10,14},{6,10},{2,6},{1,5},{5,9},... | collective-permute-start | bytes 393224 | tf_op jit(solution)/shard_map/ppermute | solution.py:30
  10.2 7.0 %collective-permute-start.6 = (bf16[128,512]{1,0:T(8,128)(2,1)S(1)}, bf16[128,512]{1,0:T(8,128)(2,1)S(1)}, u32[]{:S(2)}, u32[]{:S(2)}) collective-permute-start(bf16[128,512]{1,0:T(8,128)(2,1)S(1)} %get-tuple-element.22), channel_id=1, source_target_pairs={{0,12},{1,13},{4,6},{5,7},{8,10},{9,11},{12,0},{13,1},{14,2},{15,3... | collective-permute-start | bytes 393224 | tf_op jit(solution)/shard_map/ppermute | solution.py:40
  13.0 7.1 %collective-permute-start.8 = (bf16[384,512]{1,0:T(8,128)(2,1)S(1)}, bf16[384,512]{1,0:T(8,128)(2,1)S(1)}, u32[]{:S(2)}, u32[]{:S(2)}) collective-permute-start(bf16[384,512]{1,0:T(8,128)(2,1)S(1)} %get-tuple-element.28), channel_id=1, source_target_pairs={{0,1},{1,0},{2,3},{3,2},{4,5},{5,4},{6,7},{7,6},{8,9},{9,8},{10,11... | collective-permute-start | bytes 1179656 | tf_op jit(solution)/shard_map/ppermute | solution.py:44
  13.2 5.7 %collective-permute-start.3 = (bf16[128,512]{1,0:T(8,128)(2,1)S(1)}, bf16[128,512]{1,0:T(8,128)(2,1)S(1)}, u32[]{:S(2)}, u32[]{:S(2)}) collective-permute-start(bf16[128,512]{1,0:T(8,128)(2,1)S(1)} %collective-permute-done.2.rest_0_), channel_id=1, source_target_pairs={{0,4},{4,8},{8,12},{12,14},{14,10},{10,6},{6,2},{2,0},{1,3},{5,1},... | collective-permute-start | bytes 393224 | tf_op jit(solution)/shard_map/ppermute | solution.py:30
  15.0 5.0 %collective-permute-start.5 = (bf16[128,512]{1,0:T(8,128)(2,1)S(1)}, bf16[128,512]{1,0:T(8,128)(2,1)S(1)}, u32[]{:S(2)}, u32[]{:S(2)}) collective-permute-start(bf16[128,512]{1,0:T(8,128)(2,1)S(1)} %collective-permute-done.4.rest_1_), channel_id=1, source_target_pairs={{0,2},{4,0},{8,4},{12,8},{14,12},{10,14},{6,10},{2,6},{1,5},{5,9},... | collective-permute-start | bytes 393224 | tf_op jit(solution)/shard_map/ppermute | solution.py:30
  16.4 3.7 %collective-permute-start.9 = (bf16[256,512]{1,0:T(8,128)(2,1)S(1)}, bf16[256,512]{1,0:T(8,128)(2,1)S(1)}, u32[]{:S(2)}, u32[]{:S(2)}) collective-permute-start(bf16[256,512]{1,0:T(8,128)(2,1)S(1)} %get-tuple-element.29), channel_id=1, source_target_pairs={{0,1},{1,0},{2,3},{3,2},{4,5},{5,4},{6,7},{7,6},{8,9},{9,8},{10,11... | collective-permute-start | bytes 786440 | tf_op jit(solution)/shard_map/ppermute | solution.py:44
  20.0 1.8 %collective-permute-start.7 = (bf16[384,512]{1,0:T(8,128)(2,1)S(1)}, bf16[384,512]{1,0:T(8,128)(2,1)S(1)}, u32[]{:S(2)}, u32[]{:S(2)}) collective-permute-start(bf16[384,512]{1,0:T(8,128)(2,1)S(1)} %pack.1), channel_id=1, source_target_pairs={{0,1},{1,0},{2,3},{3,2},{4,5},{5,4},{6,7},{7,6},{8,9},{9,8},{10,11... | collective-permute-start | bytes 1179656 | tf_op jit(solution)/shard_map/ppermute | solution.py:44

commit v15 on v14

--- a/solution.py
+++ b/solution.py
@@ -117,7 +117,8 @@
         return carry
 
     lax.fori_loop(0, fours, functools.partial(add, 4), 0)
-    lax.fori_loop(4 * fours, jnp.maximum(live, 4 * fours), functools.partial(add, 1), 0)
+    pl.when(live - 4 * fours == 2)(lambda: add(2, 2 * fours, None))
+    pl.when(live - 4 * fours == 1)(lambda: add(1, 4 * fours, None))
 
 
 def store_square(grad_ref, square_ref):
@@ -224,7 +225,7 @@
     if packed:
         out_shape.append(jax.ShapeDtypeStruct((len(packed) * tile, width), jnp.bfloat16))
     if last:
-        out_shape.append(jax.ShapeDtypeStruct((loop_size, 128), jnp.float32))
+        out_shape.append(jax.ShapeDtypeStruct((8, 128), jnp.float32))
     extra = [] if first else [before]
     return pl.pallas_call(
         functools.partial(pieces_kernel, places, len(arrays), packed, loop_size, first, last),
@@ -324,7 +325,7 @@
         grid=(slots // CHUNK,),
         out_shape=[
             jax.ShapeDtypeStruct((rows, width), jnp.float32),
-            jax.ShapeDtypeStruct((loop_size, 128), jnp.float32),
+            jax.ShapeDtypeStruct((8, 128), jnp.float32),
         ],
         in_specs=[
             pl.BlockSpec(memory_space=pltpu.SMEM),
@@ -335,7 +336,7 @@
         ],
         out_specs=[
             pl.BlockSpec((rows, width), lambda step: (0, 0)),
-            pl.BlockSpec((loop_size, 128), lambda step: (0, 0)),
+            pl.BlockSpec((8, 128), lambda step: (0, 0)),
         ],
         scratch_shapes=[
             pltpu.VMEM((CHUNK * tile, width), jnp.bfloat16),
@@ -353,7 +354,7 @@
 
 
 def update_kernel(entries, users_ref, grad_ref, squares_ref, out_ref, result, sems):
-    total = jnp.sum(squares_ref[...], axis=0, keepdims=True)
+    total = jnp.sum(squares_ref[...], axis=0, keepdims=True) / 8
     total = jnp.sum(total, axis=1, keepdims=True)
     scale = 0.5 / jnp.sqrt(total / entries + 1e-06)
     rows = users_ref.shape[0] // sems.shape[0]
@@ -378,7 +379,7 @@
         whole = lax.all_gather(items, "loop", axis=0, tiled=True)
         gradient, square = add_chunks(loop_size, whole, lists, users, labels)
 
-    squares = lax.all_to_all(square, "loop", 0, 0, tiled=True)
+    squares = lax.all_gather(square, "loop", axis=0, tiled=True)
     return pl.pallas_call(
         functools.partial(update_kernel, rows * loop_size * width),
         out_shape=jax.ShapeDtypeStruct((rows, width), jnp.float32),

time: 36.3 us -> 45.2 us (1.25)
  blocking collectives: 13.5 us -> 20.9 us
  waiting for transfers between devices: 6.12 us -> 8.39 us
  Pallas kernels: 4.95 us -> 4.07 us
    all_gather x0 -> x1, blocking collectives: none -> 20.9 us  [local(): squares = lax.all_gather(square, 'loop', axis=0, tiled=True)]
    all_to_all x1 -> x0, blocking collectives: 13.5 us -> none  [local(): squares = lax.all_to_all(square, 'loop', 0, 0, tiled=True)]
    ppermute x1, waiting for transfers between devices: 0.7 us -> 3.2 us  [across(): return lax.ppermute(array, 'loop', pairs)]
    ppermute x6, waiting for transfers between devices: 5.37 us -> 3.68 us  [to_next(): return lax.ppermute(array, 'loop', pairs)]
    ppermute x3, waiting for transfers between devices: 0.06 us -> 1.51 us  [to_other_core(): lax.ppermute(array, 'loop', [(at, at ^ 1) for at in range(loop_size)])]
    pallas_call x4, Pallas kernels: 3.84 us -> 2.95 us  [add_pieces(): pl.pallas_call(functools.partial(pieces_kernel, places, len(arrays), pack...]
    ppermute x1, starting transfers between devices: 2.82 us -> 2.25 us  [across(): return lax.ppermute(array, 'loop', pairs)]
  transfers between devices with their start and end apart: 10 -> 10, of which waited for: 6 -> 5; matrix products, arithmetic and copies ran while one was open for 0% -> 0% of each run, Pallas kernels for 11% -> 5%
where the time goes in v15:
time: 45.2 us; the launch traced here: 45 us
  blocking collectives  20.9 us (46%)
  starting transfers between devices  10.3 us (23%)
  waiting for transfers between devices  8.39 us (19%)
  Pallas kernels  4.07 us (9%)
  between operations  0.73 us (2%)
  local copies, waits for them, and re-layouts  0.66 us (1%)
    all_gather x1, blocking collectives, local(): squares = lax.all_gather(square, 'loop', axis=0, tiled=True)  20.9 us
    ppermute x6, starting transfers between devices, to_next(): return lax.ppermute(array, 'loop', pairs)  7.47 us
    ppermute x6, waiting for transfers between devices, to_next(): return lax.ppermute(array, 'loop', pairs)  3.68 us
    ppermute x1, waiting for transfers between devices, across(): return lax.ppermute(array, 'loop', pairs)  3.2 us
    pallas_call x4, Pallas kernels, add_pieces(): pl.pallas_call(functools.partial(pieces_kernel, places, len(arrays), pack...  2.95 us
    ppermute x1, starting transfers between devices, across(): return lax.ppermute(array, 'loop', pairs)  2.25 us
    ppermute x3, waiting for transfers between devices, to_other_core(): lax.ppermute(array, 'loop', [(at, at ^ 1) for at in range(loop_size)])  1.51 us
    pallas_call x1, Pallas kernels, local(): pl.pallas_call(functools.partial(update_kernel, rows * loop_size * width)...  0.95 us
  transfers between devices with their start and end apart: 10, of which 5 were waited for; matrix products, arithmetic and copies ran while one was open for 0% of the time, Pallas kernels for 5%

profile of v15, /device:TPU:0, one launch (start us, length us, event | category | flops | bytes accessed | tf_op | source)
XLA Modules:
  0.0 45.0 jit_solution(5895862630332083267)
XLA Ops:
  0.0 3.0 %collective-permute-start = (bf16[128,512]{1,0:T(8,128)(2,1)}, bf16[128,512]{1,0:T(8,128)(2,1)S(1)}, u32[]{:S(2)}, u32[]{:S(2)}) collective-permute-start(bf16[128,512]{1,0:T(8,128)(2,1)} %rest_0_.1), channel_id=1, source_target_pairs={{0,4},{4,8},{8,12},{12,14},{14,10},{10,6},{6,2},{2,0},{1,3},{5,1},... | collective-permute-start | bytes 393224 | tf_op jit(solution)/shard_map/ppermute | solution.py:30
  3.0 0.0 collective-permute-start.1
  3.7 0.0 copy-start.3
  3.7 0.6 %copy-done.3 = s32[1,8]{1,0:T(1,128)S(1)} copy-done((s32[1,8]{1,0:T(1,128)S(1)}, s32[1,8]{1,0:T(1,128)}, u32[]{:S(2)}) %copy-start.3) | copy-done | bytes 56
  4.3 0.0 copy-start
  4.3 0.0 copy-start.1
  4.3 0.0 copy-start.2
  4.3 0.1 slot_table.1.table_ref
  4.5 2.5 %collective-permute-done.rest_1_ = bf16[128,512]{1,0:T(8,128)(2,1)S(1)} collective-permute-done((bf16[128,512]{1,0:T(8,128)(2,1)}, bf16[128,512]{1,0:T(8,128)(2,1)S(1)}, u32[]{:S(2)}, u32[]{:S(2)}) %collective-permute-start) | collective-permute-done | bytes 131104 | tf_op jit(solution)/shard_map/ppermute | solution.py:30
  7.0 1.5 %collective-permute-start.2 = (bf16[128,512]{1,0:T(8,128)(2,1)S(1)}, bf16[128,512]{1,0:T(8,128)(2,1)S(1)}, u32[]{:S(2)}, u32[]{:S(2)}) collective-permute-start(bf16[128,512]{1,0:T(8,128)(2,1)S(1)} %collective-permute-done.rest_1_), channel_id=1, source_target_pairs={{0,4},{4,8},{8,12},{12,14},{14,10},{10,6},{6,2},{2,0},{1,3},{5,1},... | collective-permute-start | bytes 393224 | tf_op jit(solution)/shard_map/ppermute | solution.py:30
  8.5 0.0 collective-permute-done.1.rest_2_
  8.5 0.9 %collective-permute-start.4 = (bf16[128,512]{1,0:T(8,128)(2,1)S(1)}, bf16[128,512]{1,0:T(8,128)(2,1)S(1)}, u32[]{:S(2)}, u32[]{:S(2)}) collective-permute-start(bf16[128,512]{1,0:T(8,128)(2,1)S(1)} %collective-permute-done.1.rest_2_), channel_id=1, source_target_pairs={{0,2},{4,0},{8,4},{12,8},{14,12},{10,14},{6,10},{2,6},{1,5},{5,9},... | collective-permute-start | bytes 393224 | tf_op jit(solution)/shard_map/ppermute | solution.py:30
  9.4 0.0 copy-done
  9.4 0.0 copy-done.1
  9.4 0.0 copy-done.2
  9.4 1.4 %add_pieces.4 = (f32[256,512]{1,0:T(8,128)S(1)}, bf16[512,512]{1,0:T(8,128)(2,1)S(1)}, bf16[128,512]{1,0:T(8,128)(2,1)S(1)}, bf16[384,512]{1,0:T(8,128)(2,1)S(1)}) custom-call(s32[1,128]{1,0:T(1,128)S(1)} %slot_table.1.table_ref, f32[256,512]{1,0:T(8,128)S(1)} %copy-done, s32[256,1024]{1,0:T(8,128)S(1)} %copy-done.1, bf16[128,512]{1,0:T(8,128)(2,1)S(1)} %copy-done.2, ...), custom_call_target="tpu_custom_call" | custom-call | flops 6442450944 | bytes 1048576 | tf_op jit(solution)/shard_map/add_pieces/pallas_call | solution.py:230
  10.8 2.3 %collective-permute-start.6 = (bf16[128,512]{1,0:T(8,128)(2,1)S(1)}, bf16[128,512]{1,0:T(8,128)(2,1)S(1)}, u32[]{:S(2)}, u32[]{:S(2)}) collective-permute-start(bf16[128,512]{1,0:T(8,128)(2,1)S(1)} %get-tuple-element.22), channel_id=1, source_target_pairs={{0,12},{1,13},{4,6},{5,7},{8,10},{9,11},{12,0},{13,1},{14,2},{15,3... | collective-permute-start | bytes 393224 | tf_op jit(solution)/shard_map/ppermute | solution.py:40
  13.0 0.0 collective-permute-start.8
  13.0 0.1 collective-permute-done.2.rest_0_
  13.2 0.3 collective-permute-start.3
  13.5 0.0 collective-permute-done.4.rest_1_
  13.5 1.7 %collective-permute-start.5 = (bf16[128,512]{1,0:T(8,128)(2,1)S(1)}, bf16[128,512]{1,0:T(8,128)(2,1)S(1)}, u32[]{:S(2)}, u32[]{:S(2)}) collective-permute-start(bf16[128,512]{1,0:T(8,128)(2,1)S(1)} %collective-permute-done.4.rest_1_), channel_id=1, source_target_pairs={{0,2},{4,0},{8,4},{12,8},{14,12},{10,14},{6,10},{2,6},{1,5},{5,9},... | collective-permute-start | bytes 393224 | tf_op jit(solution)/shard_map/ppermute | solution.py:30
  15.2 0.7 %add_pieces.5 = (f32[256,512]{1,0:T(8,128)S(1)}, bf16[256,512]{1,0:T(8,128)(2,1)S(1)}) custom-call(s32[1,128]{1,0:T(1,128)S(1)} %slot_table.1.table_ref, bf16[512,512]{1,0:T(8,128)(2,1)S(1)} %get-tuple-element.21.given_ref, s32[256,1024]{1,0:T(8,128)S(1)} %copy-done.1, ...), custom_call_target="tpu_custom_call", output_to_operand_aliasing={{0}: (5, {})} | custom-call | flops 4294967296 | bytes 1048576 | tf_op jit(solution)/shard_map/add_pieces/pallas_call | solution.py:230
  15.9 0.5 %collective-permute-start.9 = (bf16[256,512]{1,0:T(8,128)(2,1)S(1)}, bf16[256,512]{1,0:T(8,128)(2,1)S(1)}, u32[]{:S(2)}, u32[]{:S(2)}) collective-permute-start(bf16[256,512]{1,0:T(8,128)(2,1)S(1)} %get-tuple-element.29), channel_id=1, source_target_pairs={{0,1},{1,0},{2,3},{3,2},{4,5},{5,4},{6,7},{7,6},{8,9},{9,8},{10,11... | collective-permute-start | bytes 786440 | tf_op jit(solution)/shard_map/ppermute | solution.py:44
  16.3 3.2 %collective-permute-done.6.refs_2_.rest_2_ = bf16[128,512]{1,0:T(8,128)(2,1)S(1)} collective-permute-done((bf16[128,512]{1,0:T(8,128)(2,1)S(1)}, bf16[128,512]{1,0:T(8,128)(2,1)S(1)}, u32[]{:S(2)}, u32[]{:S(2)}) %collective-permute-start.6) | collective-permute-done | bytes 131104 | tf_op jit(solution)/shard_map/ppermute | solution.py:40
  19.5 0.0 collective-permute-done.3.refs_0_.rest_0_
  19.5 1.1 %collective-permute-done.5.refs_1_.rest_1_ = bf16[128,512]{1,0:T(8,128)(2,1)S(1)} collective-permute-done((bf16[128,512]{1,0:T(8,128)(2,1)S(1)}, bf16[128,512]{1,0:T(8,128)(2,1)S(1)}, u32[]{:S(2)}, u32[]{:S(2)}) %collective-permute-start.5) | collective-permute-done | bytes 131104 | tf_op jit(solution)/shard_map/ppermute | solution.py:30
  20.6 0.1 collective-permute-start.7
  20.7 0.0 collective-permute-done.9.rest_4_
  20.7 0.0 collective-permute-done.8.rest_3_
  20.7 0.2 add_pieces.6.rest_1_
  20.9 1.5 %collective-permute-done.7.rest_0_ = bf16[384,512]{1,0:T(8,128)(2,1)S(1)} collective-permute-done((bf16[384,512]{1,0:T(8,128)(2,1)S(1)}, bf16[384,512]{1,0:T(8,128)(2,1)S(1)}, u32[]{:S(2)}, u32[]{:S(2)}) %collective-permute-start.7) | collective-permute-done | bytes 393248 | tf_op jit(solution)/shard_map/ppermute | solution.py:44
  22.4 0.7 %add_pieces.7 = (f32[256,512]{1,0:T(8,128)S(1)}, f32[8,128]{1,0:T(8,128)S(1)}) custom-call(s32[1,128]{1,0:T(1,128)S(1)} %slot_table.1.table_ref, bf16[512,512]{1,0:T(8,128)(2,1)S(1)} %get-tuple-element.21.given_ref, s32[256,1024]{1,0:T(8,128)S(1)} %copy-done.1, bf16[384,512]{1,0:T(8,128)(2,1)S(1)} %collective-permute-done.7.rest_0_, ...), custom_call_target="tpu_custom_call", output_to_operand_aliasing={{0}: (4, {})} | custom-call | flops 6442450944 | bytes 1048576 | tf_op jit(solution)/shard_map/add_pieces/pallas_call | solution.py:230
  23.2 20.9 %all_gather.3.squares_ref = f32[128,128]{1,0:T(8,128)S(1)} all-gather(f32[8,128]{1,0:T(8,128)S(1)} %get-tuple-element.32), channel_id=1, replica_groups=mesh['group'=2,'loop'=16] {'loop'}, dimensions={0}, use_global_device_ids=true | all-gather | bytes 69632 | tf_op jit(solution)/shard_map/all_gather | solution.py:382
  44.1 0.9 %update.1 = f32[256,512]{1,0:T(8,128)} custom-call(f32[256,512]{1,0:T(8,128)S(1)} %copy-done, f32[256,512]{1,0:T(8,128)S(1)} %get-tuple-element.31.grad_ref, f32[128,128]{1,0:T(8,128)S(1)} %all_gather.3.squares_ref), custom_call_target="tpu_custom_call" | custom-call | flops 262144 | bytes 1572864 | tf_op jit(solution)/shard_map/update/pallas_call | solution.py:383
  (1 shorter events, 0.0 us)
Async XLA Ops:
  0.0 7.0 %collective-permute-start = (bf16[128,512]{1,0:T(8,128)(2,1)}, bf16[128,512]{1,0:T(8,128)(2,1)S(1)}, u32[]{:S(2)}, u32[]{:S(2)}) collective-permute-start(bf16[128,512]{1,0:T(8,128)(2,1)} %rest_0_.1), channel_id=1, source_target_pairs={{0,4},{4,8},{8,12},{12,14},{14,10},{10,6},{6,2},{2,0},{1,3},{5,1},... | collective-permute-start | bytes 393224 | tf_op jit(solution)/shard_map/ppermute | solution.py:30
  3.0 5.5 %collective-permute-start.1 = (bf16[128,512]{1,0:T(8,128)(2,1)}, bf16[128,512]{1,0:T(8,128)(2,1)S(1)}, u32[]{:S(2)}, u32[]{:S(2)}) collective-permute-start(bf16[128,512]{1,0:T(8,128)(2,1)} %rest_0_.1), channel_id=1, source_target_pairs={{0,2},{4,0},{8,4},{12,8},{14,12},{10,14},{6,10},{2,6},{1,5},{5,9},... | collective-permute-start | bytes 393224 | tf_op jit(solution)/shard_map/ppermute | solution.py:30
  3.7 0.7 %copy-start.3 = (s32[1,8]{1,0:T(1,128)S(1)}, s32[1,8]{1,0:T(1,128)}, u32[]{:S(2)}) copy-start(s32[1,8]{1,0:T(1,128)} %list_ref.1) | copy-start | bytes 100
  4.3 5.1 %copy-start = (f32[256,512]{1,0:T(8,128)S(1)}, f32[256,512]{1,0:T(8,128)}, u32[]{:S(2)}) copy-start(f32[256,512]{1,0:T(8,128)} %users_ref.1) | copy-start | bytes 1572868
  4.3 5.1 %copy-start.1 = (s32[256,1024]{1,0:T(8,128)S(1)}, s32[256,1024]{1,0:T(8,128)}, u32[]{:S(2)}) copy-start(s32[256,1024]{1,0:T(8,128)} %labels_ref.7) | copy-start | bytes 3145732
  4.3 5.1 %copy-start.2 = (bf16[128,512]{1,0:T(8,128)(2,1)S(1)}, bf16[128,512]{1,0:T(8,128)(2,1)}, u32[]{:S(2)}) copy-start(bf16[128,512]{1,0:T(8,128)(2,1)} %rest_0_.1) | copy-start | bytes 393220
  7.0 6.2 %collective-permute-start.2 = (bf16[128,512]{1,0:T(8,128)(2,1)S(1)}, bf16[128,512]{1,0:T(8,128)(2,1)S(1)}, u32[]{:S(2)}, u32[]{:S(2)}) collective-permute-start(bf16[128,512]{1,0:T(8,128)(2,1)S(1)} %collective-permute-done.rest_1_), channel_id=1, source_target_pairs={{0,4},{4,8},{8,12},{12,14},{14,10},{10,6},{6,2},{2,0},{1,3},{5,1},... | collective-permute-start | bytes 393224 | tf_op jit(solution)/shard_map/ppermute | solution.py:30
  8.5 5.0 %collective-permute-start.4 = (bf16[128,512]{1,0:T(8,128)(2,1)S(1)}, bf16[128,512]{1,0:T(8,128)(2,1)S(1)}, u32[]{:S(2)}, u32[]{:S(2)}) collective-permute-start(bf16[128,512]{1,0:T(8,128)(2,1)S(1)} %collective-permute-done.1.rest_2_), channel_id=1, source_target_pairs={{0,2},{4,0},{8,4},{12,8},{14,12},{10,14},{6,10},{2,6},{1,5},{5,9},... | collective-permute-start | bytes 393224 | tf_op jit(solution)/shard_map/ppermute | solution.py:30
  10.8 8.7 %collective-permute-start.6 = (bf16[128,512]{1,0:T(8,128)(2,1)S(1)}, bf16[128,512]{1,0:T(8,128)(2,1)S(1)}, u32[]{:S(2)}, u32[]{:S(2)}) collective-permute-start(bf16[128,512]{1,0:T(8,128)(2,1)S(1)} %get-tuple-element.22), channel_id=1, source_target_pairs={{0,12},{1,13},{4,6},{5,7},{8,10},{9,11},{12,0},{13,1},{14,2},{15,3... | collective-permute-start | bytes 393224 | tf_op jit(solution)/shard_map/ppermute | solution.py:40
  13.0 7.7 %collective-permute-start.8 = (bf16[384,512]{1,0:T(8,128)(2,1)S(1)}, bf16[384,512]{1,0:T(8,128)(2,1)S(1)}, u32[]{:S(2)}, u32[]{:S(2)}) collective-permute-start(bf16[384,512]{1,0:T(8,128)(2,1)S(1)} %get-tuple-element.28), channel_id=1, source_target_pairs={{0,1},{1,0},{2,3},{3,2},{4,5},{5,4},{6,7},{7,6},{8,9},{9,8},{10,11... | collective-permute-start | bytes 1179656 | tf_op jit(solution)/shard_map/ppermute | solution.py:44
  13.2 6.4 %collective-permute-start.3 = (bf16[128,512]{1,0:T(8,128)(2,1)S(1)}, bf16[128,512]{1,0:T(8,128)(2,1)S(1)}, u32[]{:S(2)}, u32[]{:S(2)}) collective-permute-start(bf16[128,512]{1,0:T(8,128)(2,1)S(1)} %collective-permute-done.2.rest_0_), channel_id=1, source_target_pairs={{0,4},{4,8},{8,12},{12,14},{14,10},{10,6},{6,2},{2,0},{1,3},{5,1},... | collective-permute-start | bytes 393224 | tf_op jit(solution)/shard_map/ppermute | solution.py:30
  13.5 7.1 %collective-permute-start.5 = (bf16[128,512]{1,0:T(8,128)(2,1)S(1)}, bf16[128,512]{1,0:T(8,128)(2,1)S(1)}, u32[]{:S(2)}, u32[]{:S(2)}) collective-permute-start(bf16[128,512]{1,0:T(8,128)(2,1)S(1)} %collective-permute-done.4.rest_1_), channel_id=1, source_target_pairs={{0,2},{4,0},{8,4},{12,8},{14,12},{10,14},{6,10},{2,6},{1,5},{5,9},... | collective-permute-start | bytes 393224 | tf_op jit(solution)/shard_map/ppermute | solution.py:30
  15.9 4.9 %collective-permute-start.9 = (bf16[256,512]{1,0:T(8,128)(2,1)S(1)}, bf16[256,512]{1,0:T(8,128)(2,1)S(1)}, u32[]{:S(2)}, u32[]{:S(2)}) collective-permute-start(bf16[256,512]{1,0:T(8,128)(2,1)S(1)} %get-tuple-element.29), channel_id=1, source_target_pairs={{0,1},{1,0},{2,3},{3,2},{4,5},{5,4},{6,7},{7,6},{8,9},{9,8},{10,11... | collective-permute-start | bytes 786440 | tf_op jit(solution)/shard_map/ppermute | solution.py:44
  20.6 1.8 %collective-permute-start.7 = (bf16[384,512]{1,0:T(8,128)(2,1)S(1)}, bf16[384,512]{1,0:T(8,128)(2,1)S(1)}, u32[]{:S(2)}, u32[]{:S(2)}) collective-permute-start(bf16[384,512]{1,0:T(8,128)(2,1)S(1)} %pack.1), channel_id=1, source_target_pairs={{0,1},{1,0},{2,3},{3,2},{4,5},{5,4},{6,7},{7,6},{8,9},{9,8},{10,11... | collective-permute-start | bytes 1179656 | tf_op jit(solution)/shard_map/ppermute | solution.py:44

commit v16 on v14

--- a/solution.py
+++ b/solution.py
@@ -9,7 +9,6 @@
 
 CHUNK = 8
 RING = 16
-FEW = 3
 
 
 def ring_place(loop_size):
@@ -117,7 +116,8 @@
         return carry
 
     lax.fori_loop(0, fours, functools.partial(add, 4), 0)
-    lax.fori_loop(4 * fours, jnp.maximum(live, 4 * fours), functools.partial(add, 1), 0)
+    pl.when(live - 4 * fours == 2)(lambda: add(2, 2 * fours, None))
+    pl.when(live - 4 * fours == 1)(lambda: add(1, 4 * fours, None))
 
 
 def store_square(grad_ref, square_ref):
@@ -184,27 +184,18 @@
     def labels_of(slot):
         return labels_ref[:, pl.ds(pl.multiple_of(slot * tile, tile), tile)]
 
-    if len(places) <= FEW:
-        for found, (_, index, row) in zip(entries, places):
-
-            @pl.when(found >= 0)
-            def _():
-                block = arrays[index][row * tile : (row + 1) * tile, :]
-                add_block(grad_ref, parts_ref, block, [labels_of(found)])
-
-    else:
-        live = jnp.int32(0)
-        for found, (_, index, row) in zip(entries, places):
-
-            @pl.when(found >= 0)
-            def _():
-                into = pl.ds(pl.multiple_of(live * tile, tile), tile)
-                tiles[into, :] = arrays[index][row * tile : (row + 1) * tile, :]
-                slots[live] = found
-
-            live = live + (found >= 0).astype(jnp.int32)
-        slots[live] = 0
-        add_tiles(grad_ref, parts_ref, tiles, live, lambda position: labels_of(slots[position]))
+    live = jnp.int32(0)
+    for found, (_, index, row) in zip(entries, places):
+
+        @pl.when(found >= 0)
+        def _():
+            into = pl.ds(pl.multiple_of(live * tile, tile), tile)
+            tiles[into, :] = arrays[index][row * tile : (row + 1) * tile, :]
+            slots[live] = found
+
+        live = live + (found >= 0).astype(jnp.int32)
+    slots[live] = 0
+    add_tiles(grad_ref, parts_ref, tiles, live, lambda position: labels_of(slots[position]))
     if last:
         store_square(grad_ref, square_ref)
 

time: 36.3 us -> 35.4 us (0.975); the launches traced: 36.4 us -> 35.1 us
  blocking collectives: 13.5 us -> 11.1 us
  waiting for transfers between devices: 6.12 us -> 8.33 us
  starting transfers between devices: 10.4 us -> 9.29 us
    all_to_all x1, blocking collectives: 13.5 us -> 11.1 us  [local(): squares = lax.all_to_all(square, 'loop', 0, 0, tiled=True)]
    ppermute x6, starting transfers between devices: 7.47 us -> 6.66 us  [to_next(): return lax.ppermute(array, 'loop', pairs)]
    ppermute x6, waiting for transfers between devices: 5.37 us -> 6.16 us  [to_next(): return lax.ppermute(array, 'loop', pairs)]
    ppermute x1, waiting for transfers between devices: 0.7 us -> 1.45 us  [across(): return lax.ppermute(array, 'loop', pairs)]
    ppermute x3, waiting for transfers between devices: 0.06 us -> 0.72 us  [to_other_core(): lax.ppermute(array, 'loop', [(at, at ^ 1) for at in range(loop_size)])]
  transfers between devices with their start and end apart: 10 -> 10, of which waited for: 6 -> 7; matrix products, arithmetic and copies ran while one was open for 0% -> 0% of each run, Pallas kernels for 11% -> 9%
where the time goes in v16:
time: 35.4 us; the launch traced here: 35.1 us
  blocking collectives  11.1 us (31%)
  starting transfers between devices  9.29 us (26%)
  waiting for transfers between devices  8.33 us (24%)
  Pallas kernels  4.96 us (14%)
  between operations  0.74 us (2%)
  local copies, waits for them, and re-layouts  0.66 us (2%)
    all_to_all x1, blocking collectives, local(): squares = lax.all_to_all(square, 'loop', 0, 0, tiled=True)  11.1 us
    ppermute x6, starting transfers between devices, to_next(): return lax.ppermute(array, 'loop', pairs)  6.66 us
    ppermute x6, waiting for transfers between devices, to_next(): return lax.ppermute(array, 'loop', pairs)  6.16 us
    pallas_call x4, Pallas kernels, add_pieces(): pl.pallas_call(functools.partial(pieces_kernel, places, len(arrays), pack...  3.85 us
    ppermute x1, starting transfers between devices, across(): return lax.ppermute(array, 'loop', pairs)  2.48 us
    ppermute x1, waiting for transfers between devices, across(): return lax.ppermute(array, 'loop', pairs)  1.45 us
    pallas_call x1, Pallas kernels, local(): pl.pallas_call(functools.partial(update_kernel, rows * loop_size * width)...  0.93 us
    ppermute x3, waiting for transfers between devices, to_other_core(): lax.ppermute(array, 'loop', [(at, at ^ 1) for at in range(loop_size)])  0.72 us
  transfers between devices with their start and end apart: 10, of which 7 were waited for; matrix products, arithmetic and copies ran while one was open for 0% of the time, Pallas kernels for 9%

profile of v16, /device:TPU:0, one launch (start us, length us, event | category | flops | bytes accessed | tf_op | source)
XLA Modules:
  0.0 35.1 jit_solution(10357653697908032475)
XLA Ops:
  0.0 3.0 %collective-permute-start = (bf16[128,512]{1,0:T(8,128)(2,1)}, bf16[128,512]{1,0:T(8,128)(2,1)S(1)}, u32[]{:S(2)}, u32[]{:S(2)}) collective-permute-start(bf16[128,512]{1,0:T(8,128)(2,1)} %rest_0_.1), channel_id=1, source_target_pairs={{0,4},{4,8},{8,12},{12,14},{14,10},{10,6},{6,2},{2,0},{1,3},{5,1},... | collective-permute-start | bytes 393224 | tf_op jit(solution)/shard_map/ppermute | solution.py:29
  3.0 0.0 collective-permute-start.1
  3.7 0.0 copy-start.3
  3.7 0.6 %copy-done.3 = s32[1,8]{1,0:T(1,128)S(1)} copy-done((s32[1,8]{1,0:T(1,128)S(1)}, s32[1,8]{1,0:T(1,128)}, u32[]{:S(2)}) %copy-start.3) | copy-done | bytes 56
  4.3 0.0 copy-start
  4.3 0.0 copy-start.1
  4.3 0.0 copy-start.2
  4.3 0.1 slot_table.1.table_ref
  4.5 2.5 %collective-permute-done.rest_1_ = bf16[128,512]{1,0:T(8,128)(2,1)S(1)} collective-permute-done((bf16[128,512]{1,0:T(8,128)(2,1)}, bf16[128,512]{1,0:T(8,128)(2,1)S(1)}, u32[]{:S(2)}, u32[]{:S(2)}) %collective-permute-start) | collective-permute-done | bytes 131104 | tf_op jit(solution)/shard_map/ppermute | solution.py:29
  7.0 1.5 %collective-permute-start.2 = (bf16[128,512]{1,0:T(8,128)(2,1)S(1)}, bf16[128,512]{1,0:T(8,128)(2,1)S(1)}, u32[]{:S(2)}, u32[]{:S(2)}) collective-permute-start(bf16[128,512]{1,0:T(8,128)(2,1)S(1)} %collective-permute-done.rest_1_), channel_id=1, source_target_pairs={{0,4},{4,8},{8,12},{12,14},{14,10},{10,6},{6,2},{2,0},{1,3},{5,1},... | collective-permute-start | bytes 393224 | tf_op jit(solution)/shard_map/ppermute | solution.py:29
  8.5 0.0 collective-permute-done.1.rest_2_
  8.5 0.9 %collective-permute-start.4 = (bf16[128,512]{1,0:T(8,128)(2,1)S(1)}, bf16[128,512]{1,0:T(8,128)(2,1)S(1)}, u32[]{:S(2)}, u32[]{:S(2)}) collective-permute-start(bf16[128,512]{1,0:T(8,128)(2,1)S(1)} %collective-permute-done.1.rest_2_), channel_id=1, source_target_pairs={{0,2},{4,0},{8,4},{12,8},{14,12},{10,14},{6,10},{2,6},{1,5},{5,9},... | collective-permute-start | bytes 393224 | tf_op jit(solution)/shard_map/ppermute | solution.py:29
  9.4 0.0 copy-done
  9.4 0.0 copy-done.1
  9.4 0.0 copy-done.2
  9.4 1.2 %add_pieces.4 = (f32[256,512]{1,0:T(8,128)S(1)}, bf16[512,512]{1,0:T(8,128)(2,1)S(1)}, bf16[128,512]{1,0:T(8,128)(2,1)S(1)}, bf16[384,512]{1,0:T(8,128)(2,1)S(1)}) custom-call(s32[1,128]{1,0:T(1,128)S(1)} %slot_table.1.table_ref, f32[256,512]{1,0:T(8,128)S(1)} %copy-done, s32[256,1024]{1,0:T(8,128)S(1)} %copy-done.1, bf16[128,512]{1,0:T(8,128)(2,1)S(1)} %copy-done.2, ...), custom_call_target="tpu_custom_call" | custom-call | flops 6442450944 | bytes 1048576 | tf_op jit(solution)/shard_map/add_pieces/pallas_call | solution.py:220
  10.6 2.5 %collective-permute-start.6 = (bf16[128,512]{1,0:T(8,128)(2,1)S(1)}, bf16[128,512]{1,0:T(8,128)(2,1)S(1)}, u32[]{:S(2)}, u32[]{:S(2)}) collective-permute-start(bf16[128,512]{1,0:T(8,128)(2,1)S(1)} %get-tuple-element.22), channel_id=1, source_target_pairs={{0,12},{1,13},{4,6},{5,7},{8,10},{9,11},{12,0},{13,1},{14,2},{15,3... | collective-permute-start | bytes 393224 | tf_op jit(solution)/shard_map/ppermute | solution.py:39
  13.1 0.0 collective-permute-start.8
  13.1 0.1 collective-permute-done.2.rest_0_
  13.2 0.8 %collective-permute-start.3 = (bf16[128,512]{1,0:T(8,128)(2,1)S(1)}, bf16[128,512]{1,0:T(8,128)(2,1)S(1)}, u32[]{:S(2)}, u32[]{:S(2)}) collective-permute-start(bf16[128,512]{1,0:T(8,128)(2,1)S(1)} %collective-permute-done.2.rest_0_), channel_id=1, source_target_pairs={{0,4},{4,8},{8,12},{12,14},{14,10},{10,6},{6,2},{2,0},{1,3},{5,1},... | collective-permute-start | bytes 393224 | tf_op jit(solution)/shard_map/ppermute | solution.py:29
  13.9 0.9 %collective-permute-done.4.rest_1_ = bf16[128,512]{1,0:T(8,128)(2,1)S(1)} collective-permute-done((bf16[128,512]{1,0:T(8,128)(2,1)S(1)}, bf16[128,512]{1,0:T(8,128)(2,1)S(1)}, u32[]{:S(2)}, u32[]{:S(2)}) %collective-permute-start.4) | collective-permute-done | bytes 131104 | tf_op jit(solution)/shard_map/ppermute | solution.py:29
  14.9 0.4 %collective-permute-start.5 = (bf16[128,512]{1,0:T(8,128)(2,1)S(1)}, bf16[128,512]{1,0:T(8,128)(2,1)S(1)}, u32[]{:S(2)}, u32[]{:S(2)}) collective-permute-start(bf16[128,512]{1,0:T(8,128)(2,1)S(1)} %collective-permute-done.4.rest_1_), channel_id=1, source_target_pairs={{0,2},{4,0},{8,4},{12,8},{14,12},{10,14},{6,10},{2,6},{1,5},{5,9},... | collective-permute-start | bytes 393224 | tf_op jit(solution)/shard_map/ppermute | solution.py:29
  15.3 0.7 %add_pieces.5 = (f32[256,512]{1,0:T(8,128)S(1)}, bf16[256,512]{1,0:T(8,128)(2,1)S(1)}) custom-call(s32[1,128]{1,0:T(1,128)S(1)} %slot_table.1.table_ref, bf16[512,512]{1,0:T(8,128)(2,1)S(1)} %get-tuple-element.21.given_ref, s32[256,1024]{1,0:T(8,128)S(1)} %copy-done.1, ...), custom_call_target="tpu_custom_call", output_to_operand_aliasing={{0}: (5, {})} | custom-call | flops 4294967296 | bytes 1048576 | tf_op jit(solution)/shard_map/add_pieces/pallas_call | solution.py:220
  16.0 0.1 collective-permute-start.9
  16.1 1.5 %collective-permute-done.6.refs_2_.rest_2_ = bf16[128,512]{1,0:T(8,128)(2,1)S(1)} collective-permute-done((bf16[128,512]{1,0:T(8,128)(2,1)S(1)}, bf16[128,512]{1,0:T(8,128)(2,1)S(1)}, u32[]{:S(2)}, u32[]{:S(2)}) %collective-permute-start.6) | collective-permute-done | bytes 131104 | tf_op jit(solution)/shard_map/ppermute | solution.py:39
  17.6 0.7 %collective-permute-done.3.refs_0_.rest_0_ = bf16[128,512]{1,0:T(8,128)(2,1)S(1)} collective-permute-done((bf16[128,512]{1,0:T(8,128)(2,1)S(1)}, bf16[128,512]{1,0:T(8,128)(2,1)S(1)}, u32[]{:S(2)}, u32[]{:S(2)}) %collective-permute-start.3) | collective-permute-done | bytes 131104 | tf_op jit(solution)/shard_map/ppermute | solution.py:29
  18.3 2.0 %collective-permute-done.5.refs_1_.rest_1_ = bf16[128,512]{1,0:T(8,128)(2,1)S(1)} collective-permute-done((bf16[128,512]{1,0:T(8,128)(2,1)S(1)}, bf16[128,512]{1,0:T(8,128)(2,1)S(1)}, u32[]{:S(2)}, u32[]{:S(2)}) %collective-permute-start.5) | collective-permute-done | bytes 131104 | tf_op jit(solution)/shard_map/ppermute | solution.py:29
  20.3 0.1 collective-permute-start.7
  20.3 0.0 collective-permute-done.9.rest_4_
  20.3 0.0 collective-permute-done.8.rest_3_
  20.4 1.0 %add_pieces.6.rest_1_ = f32[256,512]{1,0:T(8,128)S(1)} custom-call(s32[1,128]{1,0:T(1,128)S(1)} %slot_table.1.table_ref, bf16[512,512]{1,0:T(8,128)(2,1)S(1)} %get-tuple-element.21.given_ref, s32[256,1024]{1,0:T(8,128)S(1)} %copy-done.1, bf16[128,512]{1,0:T(8,128)(2,1)S(1)} %collective-permute-done.3.refs_0_.rest_0_, ...), custom_call_target="tpu_custom_call", output_to_operand_aliasing={{}: (8, {})} | custom-call | flops 17179869184 | bytes 1048576 | tf_op jit(solution)/shard_map/add_pieces/pallas_call | solution.py:220
  21.3 0.7 %collective-permute-done.7.rest_0_ = bf16[384,512]{1,0:T(8,128)(2,1)S(1)} collective-permute-done((bf16[384,512]{1,0:T(8,128)(2,1)S(1)}, bf16[384,512]{1,0:T(8,128)(2,1)S(1)}, u32[]{:S(2)}, u32[]{:S(2)}) %collective-permute-start.7) | collective-permute-done | bytes 393248 | tf_op jit(solution)/shard_map/ppermute | solution.py:43
  22.0 1.0 %add_pieces.7 = (f32[256,512]{1,0:T(8,128)S(1)}, f32[16,128]{1,0:T(8,128)S(1)}) custom-call(s32[1,128]{1,0:T(1,128)S(1)} %slot_table.1.table_ref, bf16[512,512]{1,0:T(8,128)(2,1)S(1)} %get-tuple-element.21.given_ref, s32[256,1024]{1,0:T(8,128)S(1)} %copy-done.1, ...), custom_call_target="tpu_custom_call", output_to_operand_aliasing={{0}: (4, {})} | custom-call | flops 6442450944 | bytes 1048576 | tf_op jit(solution)/shard_map/add_pieces/pallas_call | solution.py:220
  23.0 11.1 %all_to_all.11 = f32[16,1,128]{2,1,0:T(1,128)S(1)} all-to-all(f32[16,1,128]{2,1,0:T(1,128)S(1)} %bitcast.7), channel_id=1, replica_groups=mesh['group'=2,'loop'=16] {'loop'}, dimensions={0} | all-to-all | bytes 16384 | tf_op jit(solution)/shard_map/all_to_all | solution.py:372
  34.1 0.9 %update.1 = f32[256,512]{1,0:T(8,128)} custom-call(f32[256,512]{1,0:T(8,128)S(1)} %copy-done, f32[256,512]{1,0:T(8,128)S(1)} %get-tuple-element.31.grad_ref, f32[16,128]{1,0:T(8,128)S(1)} %bitcast.6), custom_call_target="tpu_custom_call" | custom-call | flops 262144 | bytes 1572864 | tf_op jit(solution)/shard_map/update/pallas_call | solution.py:373
  (1 shorter events, 0.0 us)
Async XLA Ops:
  0.0 7.0 %collective-permute-start = (bf16[128,512]{1,0:T(8,128)(2,1)}, bf16[128,512]{1,0:T(8,128)(2,1)S(1)}, u32[]{:S(2)}, u32[]{:S(2)}) collective-permute-start(bf16[128,512]{1,0:T(8,128)(2,1)} %rest_0_.1), channel_id=1, source_target_pairs={{0,4},{4,8},{8,12},{12,14},{14,10},{10,6},{6,2},{2,0},{1,3},{5,1},... | collective-permute-start | bytes 393224 | tf_op jit(solution)/shard_map/ppermute | solution.py:29
  3.0 5.5 %collective-permute-start.1 = (bf16[128,512]{1,0:T(8,128)(2,1)}, bf16[128,512]{1,0:T(8,128)(2,1)S(1)}, u32[]{:S(2)}, u32[]{:S(2)}) collective-permute-start(bf16[128,512]{1,0:T(8,128)(2,1)} %rest_0_.1), channel_id=1, source_target_pairs={{0,2},{4,0},{8,4},{12,8},{14,12},{10,14},{6,10},{2,6},{1,5},{5,9},... | collective-permute-start | bytes 393224 | tf_op jit(solution)/shard_map/ppermute | solution.py:29
  3.7 0.7 %copy-start.3 = (s32[1,8]{1,0:T(1,128)S(1)}, s32[1,8]{1,0:T(1,128)}, u32[]{:S(2)}) copy-start(s32[1,8]{1,0:T(1,128)} %list_ref.1) | copy-start | bytes 100
  4.3 5.1 %copy-start = (f32[256,512]{1,0:T(8,128)S(1)}, f32[256,512]{1,0:T(8,128)}, u32[]{:S(2)}) copy-start(f32[256,512]{1,0:T(8,128)} %users_ref.1) | copy-start | bytes 1572868
  4.3 5.1 %copy-start.1 = (s32[256,1024]{1,0:T(8,128)S(1)}, s32[256,1024]{1,0:T(8,128)}, u32[]{:S(2)}) copy-start(s32[256,1024]{1,0:T(8,128)} %labels_ref.7) | copy-start | bytes 3145732
  4.3 5.1 %copy-start.2 = (bf16[128,512]{1,0:T(8,128)(2,1)S(1)}, bf16[128,512]{1,0:T(8,128)(2,1)}, u32[]{:S(2)}) copy-start(bf16[128,512]{1,0:T(8,128)(2,1)} %rest_0_.1) | copy-start | bytes 393220
  7.0 6.2 %collective-permute-start.2 = (bf16[128,512]{1,0:T(8,128)(2,1)S(1)}, bf16[128,512]{1,0:T(8,128)(2,1)S(1)}, u32[]{:S(2)}, u32[]{:S(2)}) collective-permute-start(bf16[128,512]{1,0:T(8,128)(2,1)S(1)} %collective-permute-done.rest_1_), channel_id=1, source_target_pairs={{0,4},{4,8},{8,12},{12,14},{14,10},{10,6},{6,2},{2,0},{1,3},{5,1},... | collective-permute-start | bytes 393224 | tf_op jit(solution)/shard_map/ppermute | solution.py:29
  8.5 6.4 %collective-permute-start.4 = (bf16[128,512]{1,0:T(8,128)(2,1)S(1)}, bf16[128,512]{1,0:T(8,128)(2,1)S(1)}, u32[]{:S(2)}, u32[]{:S(2)}) collective-permute-start(bf16[128,512]{1,0:T(8,128)(2,1)S(1)} %collective-permute-done.1.rest_2_), channel_id=1, source_target_pairs={{0,2},{4,0},{8,4},{12,8},{14,12},{10,14},{6,10},{2,6},{1,5},{5,9},... | collective-permute-start | bytes 393224 | tf_op jit(solution)/shard_map/ppermute | solution.py:29
  10.6 7.0 %collective-permute-start.6 = (bf16[128,512]{1,0:T(8,128)(2,1)S(1)}, bf16[128,512]{1,0:T(8,128)(2,1)S(1)}, u32[]{:S(2)}, u32[]{:S(2)}) collective-permute-start(bf16[128,512]{1,0:T(8,128)(2,1)S(1)} %get-tuple-element.22), channel_id=1, source_target_pairs={{0,12},{1,13},{4,6},{5,7},{8,10},{9,11},{12,0},{13,1},{14,2},{15,3... | collective-permute-start | bytes 393224 | tf_op jit(solution)/shard_map/ppermute | solution.py:39
  13.1 7.3 %collective-permute-start.8 = (bf16[384,512]{1,0:T(8,128)(2,1)S(1)}, bf16[384,512]{1,0:T(8,128)(2,1)S(1)}, u32[]{:S(2)}, u32[]{:S(2)}) collective-permute-start(bf16[384,512]{1,0:T(8,128)(2,1)S(1)} %get-tuple-element.28), channel_id=1, source_target_pairs={{0,1},{1,0},{2,3},{3,2},{4,5},{5,4},{6,7},{7,6},{8,9},{9,8},{10,11... | collective-permute-start | bytes 1179656 | tf_op jit(solution)/shard_map/ppermute | solution.py:43
  13.2 5.1 %collective-permute-start.3 = (bf16[128,512]{1,0:T(8,128)(2,1)S(1)}, bf16[128,512]{1,0:T(8,128)(2,1)S(1)}, u32[]{:S(2)}, u32[]{:S(2)}) collective-permute-start(bf16[128,512]{1,0:T(8,128)(2,1)S(1)} %collective-permute-done.2.rest_0_), channel_id=1, source_target_pairs={{0,4},{4,8},{8,12},{12,14},{14,10},{10,6},{6,2},{2,0},{1,3},{5,1},... | collective-permute-start | bytes 393224 | tf_op jit(solution)/shard_map/ppermute | solution.py:29
  14.9 5.4 %collective-permute-start.5 = (bf16[128,512]{1,0:T(8,128)(2,1)S(1)}, bf16[128,512]{1,0:T(8,128)(2,1)S(1)}, u32[]{:S(2)}, u32[]{:S(2)}) collective-permute-start(bf16[128,512]{1,0:T(8,128)(2,1)S(1)} %collective-permute-done.4.rest_1_), channel_id=1, source_target_pairs={{0,2},{4,0},{8,4},{12,8},{14,12},{10,14},{6,10},{2,6},{1,5},{5,9},... | collective-permute-start | bytes 393224 | tf_op jit(solution)/shard_map/ppermute | solution.py:29
  16.0 4.3 %collective-permute-start.9 = (bf16[256,512]{1,0:T(8,128)(2,1)S(1)}, bf16[256,512]{1,0:T(8,128)(2,1)S(1)}, u32[]{:S(2)}, u32[]{:S(2)}) collective-permute-start(bf16[256,512]{1,0:T(8,128)(2,1)S(1)} %get-tuple-element.29), channel_id=1, source_target_pairs={{0,1},{1,0},{2,3},{3,2},{4,5},{5,4},{6,7},{7,6},{8,9},{9,8},{10,11... | collective-permute-start | bytes 786440 | tf_op jit(solution)/shard_map/ppermute | solution.py:43
  20.3 1.8 %collective-permute-start.7 = (bf16[384,512]{1,0:T(8,128)(2,1)S(1)}, bf16[384,512]{1,0:T(8,128)(2,1)S(1)}, u32[]{:S(2)}, u32[]{:S(2)}) collective-permute-start(bf16[384,512]{1,0:T(8,128)(2,1)S(1)} %pack.1), channel_id=1, source_target_pairs={{0,1},{1,0},{2,3},{3,2},{4,5},{5,4},{6,7},{7,6},{8,9},{9,8},{10,11... | collective-permute-start | bytes 1179656 | tf_op jit(solution)/shard_map/ppermute | solution.py:43

commit v17 on v16

--- a/solution.py
+++ b/solution.py
@@ -133,35 +133,46 @@
     return core, jnp.where(row == 0, outer, loop_size // 2 - 1 - outer)
 
 
-def pack_kernel(*refs):
+def pack_kernel(loop_size, *refs):
+    count = len(refs) - (1 if loop_size is None else 2)
     tile = refs[0].shape[0]
-    for at, ref in enumerate(refs[:-1]):
-        refs[-1][at * tile : (at + 1) * tile, :] = ref[...]
-
-
-def pack(arrays):
+    if loop_size is not None:
+        core, position = core_and_position(loop_size)
+        for at in range(2):
+
+            @pl.when((core + position) % 2 == at)
+            def _():
+                refs[-1][...] = refs[1 + at][...]
+
+    for at in range(count):
+        refs[count][at * tile : (at + 1) * tile, :] = refs[at][...]
+
+
+def pack(arrays, loop_size=None):
     tile, width = arrays[0].shape
-    return pl.pallas_call(
-        pack_kernel,
-        out_shape=jax.ShapeDtypeStruct((len(arrays) * tile, width), arrays[0].dtype),
+    shapes = [(len(arrays) * tile, width)] + ([] if loop_size is None else [(tile, width)])
+    return pl.pallas_call(
+        functools.partial(pack_kernel, loop_size),
+        out_shape=[jax.ShapeDtypeStruct(shape, arrays[0].dtype) for shape in shapes],
         in_specs=[pl.BlockSpec(memory_space=pltpu.VMEM)] * len(arrays),
-        out_specs=pl.BlockSpec(memory_space=pltpu.VMEM),
+        out_specs=[pl.BlockSpec(memory_space=pltpu.VMEM)] * len(shapes),
         compiler_params=pltpu.CompilerParams(vmem_limit_bytes=16 * 1024 * 1024),
         cost_estimate=pl.CostEstimate(
-            flops=2**34, bytes_accessed=4 * len(arrays) * tile * width, transcendentals=0
+            flops=2**34 if loop_size is None else 2**32,
+            bytes_accessed=4 * len(arrays) * tile * width,
+            transcendentals=0,
         ),
         name="pack",
     )(*arrays)
 
 
-def pieces_kernel(places, count, packed, loop_size, first, last, table_ref, given_ref, labels_ref, *rest):
+def pieces_kernel(places, count, packed, first, last, table_ref, given_ref, labels_ref, *rest):
     rest = list(rest)
     arrays = [rest.pop(0) for _ in range(count)]
     if not first:
         rest.pop(0)
     grad_ref = rest.pop(0)
     parts_ref = rest.pop(0) if first else given_ref
-    across_ref = rest.pop(0) if first else None
     pack_ref = rest.pop(0) if packed else None
     square_ref = rest.pop(0) if last else None
     tiles, slots = rest
@@ -169,13 +180,6 @@
     for at, index in enumerate(packed):
         pack_ref[at * tile : (at + 1) * tile, :] = arrays[index][...]
     if first:
-        core, position = core_and_position(loop_size)
-        for at in range(2):
-
-            @pl.when((core + position) % 2 == at)
-            def _():
-                across_ref[...] = arrays[1 + at][...]
-
         parts_ref[...] = halves(0.5 * given_ref[...])
         grad_ref[...] = jnp.zeros_like(grad_ref)
     table = table_ref[...]
@@ -211,14 +215,13 @@
     out_shape = [jax.ShapeDtypeStruct((rows, width), jnp.float32)]
     if first:
         out_shape.append(jax.ShapeDtypeStruct((2 * rows, width), jnp.bfloat16))
-        out_shape.append(jax.ShapeDtypeStruct((tile, width), jnp.bfloat16))
     if packed:
         out_shape.append(jax.ShapeDtypeStruct((len(packed) * tile, width), jnp.bfloat16))
     if last:
         out_shape.append(jax.ShapeDtypeStruct((loop_size, 128), jnp.float32))
     extra = [] if first else [before]
     return pl.pallas_call(
-        functools.partial(pieces_kernel, places, len(arrays), packed, loop_size, first, last),
+        functools.partial(pieces_kernel, places, len(arrays), packed, first, last),
         out_shape=out_shape,
         in_specs=[pl.BlockSpec(memory_space=pltpu.VMEM)] * (3 + len(arrays) + len(extra)),
         out_specs=[pl.BlockSpec(memory_space=pltpu.VMEM)] * len(out_shape),
@@ -229,7 +232,7 @@
         ],
         compiler_params=pltpu.CompilerParams(vmem_limit_bytes=24 * 1024 * 1024),
         cost_estimate=pl.CostEstimate(
-            flops=128 * rows * width * most * tile,
+            flops=(8 if first else 128) * rows * width * most * tile,
             bytes_accessed=8 * rows * width,
             transcendentals=rows * most * tile,
         ),
@@ -256,17 +259,16 @@
     up, table = lax.optimization_barrier((up, table))
     first = [held(0, items), held(1, up), held(-1, down)]
     second = [held(2, to_next(up, 1, loop_size)), held(-2, to_next(down, -1, loop_size))]
-    gradient, parts, opposite, packed = add_pieces(
-        first, [0, 1, 2], loop_size, table, users, labels, None, False
-    )
+    packed, opposite = pack([items, up, down], loop_size)
     opposite = across(opposite, loop_size)
+    gradient, parts = add_pieces(first, [], loop_size, table, users, labels, None, False)
     first = other(packed, [0, 1, -1])
     third = [held(3, to_next(second[0][0], 1, loop_size)), held(-3, to_next(second[1][0], -1, loop_size))]
     gradient, packed = add_pieces(second, [0, 1], loop_size, table, parts, labels, gradient, False)
     second = other(packed, [2, -2])
     third.append(held(4, opposite))
     arrived, gradient = lax.optimization_barrier(([array for array, _ in third], gradient))
-    final = other(pack(arrived), [3, -3, 4])
+    final = other(pack(arrived)[0], [3, -3, 4])
     (gradient,) = add_pieces(
         third + [first, second], [], loop_size, table, parts, labels, gradient, False
     )

time: 35.4 us -> 35.9 us (1.014)
  blocking collectives: 11.1 us -> 12.9 us
  Pallas kernels: 4.96 us -> 3.36 us
  starting transfers between devices: 9.29 us -> 9.99 us
    all_to_all x1, blocking collectives: 11.1 us -> 12.9 us  [local(): squares = lax.all_to_all(square, 'loop', 0, 0, tiled=True)]
    pallas_call x4, Pallas kernels: 3.85 us -> 2.21 us  [add_pieces(): pl.pallas_call(functools.partial(pieces_kernel, places, len(arrays), pack...]
    ppermute x1, starting transfers between devices: 2.48 us -> 3.36 us  [across(): return lax.ppermute(array, 'loop', pairs)]
  transfers between devices with their start and end apart: 10 -> 10, of which waited for: 7 -> 6; matrix products, arithmetic and copies ran while one was open for 0% -> 0% of each run, Pallas kernels for 9% -> 6%
where the time goes in v17:
time: 35.9 us; the launch traced here: 35.8 us
  blocking collectives  12.9 us (36%)
  starting transfers between devices  9.99 us (28%)
  waiting for transfers between devices  8.07 us (22%)
  Pallas kernels  3.36 us (9%)
  between operations  0.75 us (2%)
  local copies, waits for them, and re-layouts  0.66 us (2%)
    all_to_all x1, blocking collectives, local(): squares = lax.all_to_all(square, 'loop', 0, 0, tiled=True)  12.9 us
    ppermute x6, waiting for transfers between devices, to_next(): return lax.ppermute(array, 'loop', pairs)  6.4 us
    ppermute x6, starting transfers between devices, to_next(): return lax.ppermute(array, 'loop', pairs)  6.37 us
    ppermute x1, starting transfers between devices, across(): return lax.ppermute(array, 'loop', pairs)  3.36 us
    pallas_call x4, Pallas kernels, add_pieces(): pl.pallas_call(functools.partial(pieces_kernel, places, len(arrays), pack...  2.21 us
    ppermute x1, waiting for transfers between devices, across(): return lax.ppermute(array, 'loop', pairs)  1.12 us
    pallas_call x1, Pallas kernels, local(): pl.pallas_call(functools.partial(update_kernel, rows * loop_size * width)...  0.93 us
  transfers between devices with their start and end apart: 10, of which 6 were waited for; matrix products, arithmetic and copies ran while one was open for 0% of the time, Pallas kernels for 6%

profile of v17, /device:TPU:0, one launch (start us, length us, event | category | flops | bytes accessed | tf_op | source)
XLA Modules:
  0.0 35.8 jit_solution(11848108585999141991)
XLA Ops:
  0.0 3.0 %collective-permute-start = (bf16[128,512]{1,0:T(8,128)(2,1)}, bf16[128,512]{1,0:T(8,128)(2,1)S(1)}, u32[]{:S(2)}, u32[]{:S(2)}) collective-permute-start(bf16[128,512]{1,0:T(8,128)(2,1)} %refs_0_.1), channel_id=1, source_target_pairs={{0,4},{4,8},{8,12},{12,14},{14,10},{10,6},{6,2},{2,0},{1,3},{5,1},... | collective-permute-start | bytes 393224 | tf_op jit(solution)/shard_map/ppermute | solution.py:29
  3.0 0.0 collective-permute-start.1
  3.7 0.0 copy-start.3
  3.7 0.6 %copy-done.3 = s32[1,8]{1,0:T(1,128)S(1)} copy-done((s32[1,8]{1,0:T(1,128)S(1)}, s32[1,8]{1,0:T(1,128)}, u32[]{:S(2)}) %copy-start.3) | copy-done | bytes 56
  4.3 0.0 copy-start.2
  4.3 0.1 slot_table.1.table_ref
  4.5 0.0 copy-start
  4.5 0.0 copy-start.1
  4.5 2.5 %collective-permute-done.rest_1_.refs_1_ = bf16[128,512]{1,0:T(8,128)(2,1)S(1)} collective-permute-done((bf16[128,512]{1,0:T(8,128)(2,1)}, bf16[128,512]{1,0:T(8,128)(2,1)S(1)}, u32[]{:S(2)}, u32[]{:S(2)}) %collective-permute-start) | collective-permute-done | bytes 131104 | tf_op jit(solution)/shard_map/ppermute | solution.py:29
  7.0 1.5 %collective-permute-start.2 = (bf16[128,512]{1,0:T(8,128)(2,1)S(1)}, bf16[128,512]{1,0:T(8,128)(2,1)S(1)}, u32[]{:S(2)}, u32[]{:S(2)}) collective-permute-start(bf16[128,512]{1,0:T(8,128)(2,1)S(1)} %collective-permute-done.rest_1_.refs_1_), channel_id=1, source_target_pairs={{0,4},{4,8},{8,12},{12,14},{14,10},{10,6},{6,2},{2,0},{1,3},{5,1},... | collective-permute-start | bytes 393224 | tf_op jit(solution)/shard_map/ppermute | solution.py:29
  8.5 0.0 collective-permute-done.1.rest_2_.refs_2_
  8.5 0.9 %collective-permute-start.4 = (bf16[128,512]{1,0:T(8,128)(2,1)S(1)}, bf16[128,512]{1,0:T(8,128)(2,1)S(1)}, u32[]{:S(2)}, u32[]{:S(2)}) collective-permute-start(bf16[128,512]{1,0:T(8,128)(2,1)S(1)} %collective-permute-done.1.rest_2_.refs_2_), channel_id=1, source_target_pairs={{0,2},{4,0},{8,4},{12,8},{14,12},{10,14},{6,10},{2,6},{1,5},{5,9},... | collective-permute-start | bytes 393224 | tf_op jit(solution)/shard_map/ppermute | solution.py:29
  9.4 0.0 copy-done.2
  9.4 3.4 %collective-permute-start.6 = (bf16[128,512]{1,0:T(8,128)(2,1)S(1)}, bf16[128,512]{1,0:T(8,128)(2,1)S(1)}, u32[]{:S(2)}, u32[]{:S(2)}) collective-permute-start(bf16[128,512]{1,0:T(8,128)(2,1)S(1)} %get-tuple-element.22), channel_id=1, source_target_pairs={{0,12},{1,13},{4,6},{5,7},{8,10},{9,11},{12,0},{13,1},{14,2},{15,3... | collective-permute-start | bytes 393224 | tf_op jit(solution)/shard_map/ppermute | solution.py:39
  12.8 0.0 collective-permute-start.8
  12.8 0.0 copy-done
  12.8 0.0 copy-done.1
  12.8 0.8 %add_pieces.4 = (f32[256,512]{1,0:T(8,128)S(1)}, bf16[512,512]{1,0:T(8,128)(2,1)S(1)}) custom-call(s32[1,128]{1,0:T(1,128)S(1)} %slot_table.1.table_ref, f32[256,512]{1,0:T(8,128)S(1)} %copy-done, s32[256,1024]{1,0:T(8,128)S(1)} %copy-done.1, bf16[128,512]{1,0:T(8,128)(2,1)S(1)} %copy-done.2, bf16[128,512]{1,0:T(8,128)(2,1)S(1)} %collective-permute-done.rest_1_.refs_1_, ...), custom_call_target="tpu_custom_call" | custom-call | flops 402653184 | bytes 1048576 | tf_op jit(solution)/shard_map/add_pieces/pallas_call | solution.py:223
  13.6 0.0 collective-permute-done.2.rest_0_
  13.7 0.1 collective-permute-start.3
  13.7 1.1 %collective-permute-done.4.rest_1_ = bf16[128,512]{1,0:T(8,128)(2,1)S(1)} collective-permute-done((bf16[128,512]{1,0:T(8,128)(2,1)S(1)}, bf16[128,512]{1,0:T(8,128)(2,1)S(1)}, u32[]{:S(2)}, u32[]{:S(2)}) %collective-permute-start.4) | collective-permute-done | bytes 131104 | tf_op jit(solution)/shard_map/ppermute | solution.py:29
  14.9 0.9 %collective-permute-start.5 = (bf16[128,512]{1,0:T(8,128)(2,1)S(1)}, bf16[128,512]{1,0:T(8,128)(2,1)S(1)}, u32[]{:S(2)}, u32[]{:S(2)}) collective-permute-start(bf16[128,512]{1,0:T(8,128)(2,1)S(1)} %collective-permute-done.4.rest_1_), channel_id=1, source_target_pairs={{0,2},{4,0},{8,4},{12,8},{14,12},{10,14},{6,10},{2,6},{1,5},{5,9},... | collective-permute-start | bytes 393224 | tf_op jit(solution)/shard_map/ppermute | solution.py:29
  15.7 0.1 add_pieces.5
  15.9 0.1 collective-permute-start.9
  16.0 1.1 %collective-permute-done.6.refs_2_.rest_2_ = bf16[128,512]{1,0:T(8,128)(2,1)S(1)} collective-permute-done((bf16[128,512]{1,0:T(8,128)(2,1)S(1)}, bf16[128,512]{1,0:T(8,128)(2,1)S(1)}, u32[]{:S(2)}, u32[]{:S(2)}) %collective-permute-start.6) | collective-permute-done | bytes 131104 | tf_op jit(solution)/shard_map/ppermute | solution.py:39
  17.1 2.2 %collective-permute-done.3.refs_0_.rest_0_ = bf16[128,512]{1,0:T(8,128)(2,1)S(1)} collective-permute-done((bf16[128,512]{1,0:T(8,128)(2,1)S(1)}, bf16[128,512]{1,0:T(8,128)(2,1)S(1)}, u32[]{:S(2)}, u32[]{:S(2)}) %collective-permute-start.3) | collective-permute-done | bytes 131104 | tf_op jit(solution)/shard_map/ppermute | solution.py:29
  19.3 0.6 %collective-permute-done.5.refs_1_.rest_1_ = bf16[128,512]{1,0:T(8,128)(2,1)S(1)} collective-permute-done((bf16[128,512]{1,0:T(8,128)(2,1)S(1)}, bf16[128,512]{1,0:T(8,128)(2,1)S(1)}, u32[]{:S(2)}, u32[]{:S(2)}) %collective-permute-start.5) | collective-permute-done | bytes 131104 | tf_op jit(solution)/shard_map/ppermute | solution.py:29
  19.9 0.2 collective-permute-start.7
  20.1 0.0 collective-permute-done.9.rest_4_
  20.1 0.0 collective-permute-done.8.rest_3_
  20.1 1.1 %add_pieces.6.rest_1_ = f32[256,512]{1,0:T(8,128)S(1)} custom-call(s32[1,128]{1,0:T(1,128)S(1)} %slot_table.1.table_ref, bf16[512,512]{1,0:T(8,128)(2,1)S(1)} %get-tuple-element.21.given_ref, s32[256,1024]{1,0:T(8,128)S(1)} %copy-done.1, bf16[128,512]{1,0:T(8,128)(2,1)S(1)} %collective-permute-done.3.refs_0_.rest_0_, ...), custom_call_target="tpu_custom_call", output_to_operand_aliasing={{}: (8, {})} | custom-call | flops 17179869184 | bytes 1048576 | tf_op jit(solution)/shard_map/add_pieces/pallas_call | solution.py:223
  21.1 0.5 %collective-permute-done.7.rest_0_ = bf16[384,512]{1,0:T(8,128)(2,1)S(1)} collective-permute-done((bf16[384,512]{1,0:T(8,128)(2,1)S(1)}, bf16[384,512]{1,0:T(8,128)(2,1)S(1)}, u32[]{:S(2)}, u32[]{:S(2)}) %collective-permute-start.7) | collective-permute-done | bytes 393248 | tf_op jit(solution)/shard_map/ppermute | solution.py:43
  21.7 0.2 add_pieces.7
  21.9 12.9 %all_to_all.11 = f32[16,1,128]{2,1,0:T(1,128)S(1)} all-to-all(f32[16,1,128]{2,1,0:T(1,128)S(1)} %bitcast.7), channel_id=1, replica_groups=mesh['group'=2,'loop'=16] {'loop'}, dimensions={0} | all-to-all | bytes 16384 | tf_op jit(solution)/shard_map/all_to_all | solution.py:374
  34.8 0.9 %update.1 = f32[256,512]{1,0:T(8,128)} custom-call(f32[256,512]{1,0:T(8,128)S(1)} %copy-done, f32[256,512]{1,0:T(8,128)S(1)} %get-tuple-element.31.grad_ref, f32[16,128]{1,0:T(8,128)S(1)} %bitcast.6), custom_call_target="tpu_custom_call" | custom-call | flops 262144 | bytes 1572864 | tf_op jit(solution)/shard_map/update/pallas_call | solution.py:375
  (2 shorter events, 0.1 us)
Async XLA Ops:
  0.0 7.0 %collective-permute-start = (bf16[128,512]{1,0:T(8,128)(2,1)}, bf16[128,512]{1,0:T(8,128)(2,1)S(1)}, u32[]{:S(2)}, u32[]{:S(2)}) collective-permute-start(bf16[128,512]{1,0:T(8,128)(2,1)} %refs_0_.1), channel_id=1, source_target_pairs={{0,4},{4,8},{8,12},{12,14},{14,10},{10,6},{6,2},{2,0},{1,3},{5,1},... | collective-permute-start | bytes 393224 | tf_op jit(solution)/shard_map/ppermute | solution.py:29
  3.0 5.5 %collective-permute-start.1 = (bf16[128,512]{1,0:T(8,128)(2,1)}, bf16[128,512]{1,0:T(8,128)(2,1)S(1)}, u32[]{:S(2)}, u32[]{:S(2)}) collective-permute-start(bf16[128,512]{1,0:T(8,128)(2,1)} %refs_0_.1), channel_id=1, source_target_pairs={{0,2},{4,0},{8,4},{12,8},{14,12},{10,14},{6,10},{2,6},{1,5},{5,9},... | collective-permute-start | bytes 393224 | tf_op jit(solution)/shard_map/ppermute | solution.py:29
  3.7 0.7 %copy-start.3 = (s32[1,8]{1,0:T(1,128)S(1)}, s32[1,8]{1,0:T(1,128)}, u32[]{:S(2)}) copy-start(s32[1,8]{1,0:T(1,128)} %list_ref.1) | copy-start | bytes 100
  4.3 5.1 %copy-start.2 = (bf16[128,512]{1,0:T(8,128)(2,1)S(1)}, bf16[128,512]{1,0:T(8,128)(2,1)}, u32[]{:S(2)}) copy-start(bf16[128,512]{1,0:T(8,128)(2,1)} %refs_0_.1) | copy-start | bytes 393220
  4.5 8.3 %copy-start = (f32[256,512]{1,0:T(8,128)S(1)}, f32[256,512]{1,0:T(8,128)}, u32[]{:S(2)}) copy-start(f32[256,512]{1,0:T(8,128)} %users_ref.1) | copy-start | bytes 1572868
  4.5 8.3 %copy-start.1 = (s32[256,1024]{1,0:T(8,128)S(1)}, s32[256,1024]{1,0:T(8,128)}, u32[]{:S(2)}) copy-start(s32[256,1024]{1,0:T(8,128)} %labels_ref.7) | copy-start | bytes 3145732
  7.0 6.7 %collective-permute-start.2 = (bf16[128,512]{1,0:T(8,128)(2,1)S(1)}, bf16[128,512]{1,0:T(8,128)(2,1)S(1)}, u32[]{:S(2)}, u32[]{:S(2)}) collective-permute-start(bf16[128,512]{1,0:T(8,128)(2,1)S(1)} %collective-permute-done.rest_1_.refs_1_), channel_id=1, source_target_pairs={{0,4},{4,8},{8,12},{12,14},{14,10},{10,6},{6,2},{2,0},{1,3},{5,1},... | collective-permute-start | bytes 393224 | tf_op jit(solution)/shard_map/ppermute | solution.py:29
  8.5 6.4 %collective-permute-start.4 = (bf16[128,512]{1,0:T(8,128)(2,1)S(1)}, bf16[128,512]{1,0:T(8,128)(2,1)S(1)}, u32[]{:S(2)}, u32[]{:S(2)}) collective-permute-start(bf16[128,512]{1,0:T(8,128)(2,1)S(1)} %collective-permute-done.1.rest_2_.refs_2_), channel_id=1, source_target_pairs={{0,2},{4,0},{8,4},{12,8},{14,12},{10,14},{6,10},{2,6},{1,5},{5,9},... | collective-permute-start | bytes 393224 | tf_op jit(solution)/shard_map/ppermute | solution.py:29
  9.4 7.6 %collective-permute-start.6 = (bf16[128,512]{1,0:T(8,128)(2,1)S(1)}, bf16[128,512]{1,0:T(8,128)(2,1)S(1)}, u32[]{:S(2)}, u32[]{:S(2)}) collective-permute-start(bf16[128,512]{1,0:T(8,128)(2,1)S(1)} %get-tuple-element.22), channel_id=1, source_target_pairs={{0,12},{1,13},{4,6},{5,7},{8,10},{9,11},{12,0},{13,1},{14,2},{15,3... | collective-permute-start | bytes 393224 | tf_op jit(solution)/shard_map/ppermute | solution.py:39
  12.8 7.3 %collective-permute-start.8 = (bf16[384,512]{1,0:T(8,128)(2,1)S(1)}, bf16[384,512]{1,0:T(8,128)(2,1)S(1)}, u32[]{:S(2)}, u32[]{:S(2)}) collective-permute-start(bf16[384,512]{1,0:T(8,128)(2,1)S(1)} %get-tuple-element.28), channel_id=1, source_target_pairs={{0,1},{1,0},{2,3},{3,2},{4,5},{5,4},{6,7},{7,6},{8,9},{9,8},{10,11... | collective-permute-start | bytes 1179656 | tf_op jit(solution)/shard_map/ppermute | solution.py:43
  13.7 5.6 %collective-permute-start.3 = (bf16[128,512]{1,0:T(8,128)(2,1)S(1)}, bf16[128,512]{1,0:T(8,128)(2,1)S(1)}, u32[]{:S(2)}, u32[]{:S(2)}) collective-permute-start(bf16[128,512]{1,0:T(8,128)(2,1)S(1)} %collective-permute-done.2.rest_0_), channel_id=1, source_target_pairs={{0,4},{4,8},{8,12},{12,14},{14,10},{10,6},{6,2},{2,0},{1,3},{5,1},... | collective-permute-start | bytes 393224 | tf_op jit(solution)/shard_map/ppermute | solution.py:29
  14.9 5.0 %collective-permute-start.5 = (bf16[128,512]{1,0:T(8,128)(2,1)S(1)}, bf16[128,512]{1,0:T(8,128)(2,1)S(1)}, u32[]{:S(2)}, u32[]{:S(2)}) collective-permute-start(bf16[128,512]{1,0:T(8,128)(2,1)S(1)} %collective-permute-done.4.rest_1_), channel_id=1, source_target_pairs={{0,2},{4,0},{8,4},{12,8},{14,12},{10,14},{6,10},{2,6},{1,5},{5,9},... | collective-permute-start | bytes 393224 | tf_op jit(solution)/shard_map/ppermute | solution.py:29
  15.9 4.2 %collective-permute-start.9 = (bf16[256,512]{1,0:T(8,128)(2,1)S(1)}, bf16[256,512]{1,0:T(8,128)(2,1)S(1)}, u32[]{:S(2)}, u32[]{:S(2)}) collective-permute-start(bf16[256,512]{1,0:T(8,128)(2,1)S(1)} %get-tuple-element.29), channel_id=1, source_target_pairs={{0,1},{1,0},{2,3},{3,2},{4,5},{5,4},{6,7},{7,6},{8,9},{9,8},{10,11... | collective-permute-start | bytes 786440 | tf_op jit(solution)/shard_map/ppermute | solution.py:43
  19.9 1.8 %collective-permute-start.7 = (bf16[384,512]{1,0:T(8,128)(2,1)S(1)}, bf16[384,512]{1,0:T(8,128)(2,1)S(1)}, u32[]{:S(2)}, u32[]{:S(2)}) collective-permute-start(bf16[384,512]{1,0:T(8,128)(2,1)S(1)} %pack.3), channel_id=1, source_target_pairs={{0,1},{1,0},{2,3},{3,2},{4,5},{5,4},{6,7},{7,6},{8,9},{9,8},{10,11... | collective-permute-start | bytes 1179656 | tf_op jit(solution)/shard_map/ppermute | solution.py:43

commit v18 on v17

--- a/solution.py
+++ b/solution.py
@@ -134,8 +134,9 @@
 
 
 def pack_kernel(loop_size, *refs):
-    count = len(refs) - (1 if loop_size is None else 2)
     tile = refs[0].shape[0]
+    sources = refs[:-1] if loop_size is None else (refs[0], refs[2])
+    packed_ref = refs[-1] if loop_size is None else refs[-2]
     if loop_size is not None:
         core, position = core_and_position(loop_size)
         for at in range(2):
@@ -144,13 +145,13 @@
             def _():
                 refs[-1][...] = refs[1 + at][...]
 
-    for at in range(count):
-        refs[count][at * tile : (at + 1) * tile, :] = refs[at][...]
+    for at, ref in enumerate(sources):
+        packed_ref[at * tile : (at + 1) * tile, :] = ref[...]
 
 
 def pack(arrays, loop_size=None):
     tile, width = arrays[0].shape
-    shapes = [(len(arrays) * tile, width)] + ([] if loop_size is None else [(tile, width)])
+    shapes = [(len(arrays) * tile, width)] if loop_size is None else [(2 * tile, width), (tile, width)]
     return pl.pallas_call(
         functools.partial(pack_kernel, loop_size),
         out_shape=[jax.ShapeDtypeStruct(shape, arrays[0].dtype) for shape in shapes],
@@ -259,10 +260,11 @@
     up, table = lax.optimization_barrier((up, table))
     first = [held(0, items), held(1, up), held(-1, down)]
     second = [held(2, to_next(up, 1, loop_size)), held(-2, to_next(down, -1, loop_size))]
+    first.append(other(up, [1]))
     packed, opposite = pack([items, up, down], loop_size)
     opposite = across(opposite, loop_size)
     gradient, parts = add_pieces(first, [], loop_size, table, users, labels, None, False)
-    first = other(packed, [0, 1, -1])
+    first = other(packed, [0, -1])
     third = [held(3, to_next(second[0][0], 1, loop_size)), held(-3, to_next(second[1][0], -1, loop_size))]
     gradient, packed = add_pieces(second, [0, 1], loop_size, table, parts, labels, gradient, False)
     second = other(packed, [2, -2])

time: 35.9 us -> 35.4 us (0.986)
  blocking collectives: 12.9 us -> 11.1 us
  waiting for transfers between devices: 8.07 us -> 6.57 us
  starting transfers between devices: 9.99 us -> 11.4 us
  Pallas kernels: 3.36 us -> 4.7 us
    ppermute x6, waiting for transfers between devices: 6.4 us -> 3.2 us  [to_next(): return lax.ppermute(array, 'loop', pairs)]
    all_to_all x1, blocking collectives: 12.9 us -> 11.1 us  [local(): squares = lax.all_to_all(square, 'loop', 0, 0, tiled=True)]
    ppermute x6, starting transfers between devices: 6.37 us -> 7.99 us  [to_next(): return lax.ppermute(array, 'loop', pairs)]
    ppermute x1, waiting for transfers between devices: 1.12 us -> 2.72 us  [across(): return lax.ppermute(array, 'loop', pairs)]
    pallas_call x4, Pallas kernels: 2.21 us -> 3.57 us  [add_pieces(): pl.pallas_call(functools.partial(pieces_kernel, places, len(arrays), pack...]
  transfers between devices with their start and end apart: 10 -> 11, of which waited for: 6 -> 4; matrix products, arithmetic and copies ran while one was open for 0% -> 0% of each run, Pallas kernels for 6% -> 9%
where the time goes in v18:
time: 35.4 us; the launch traced here: 35.2 us
  starting transfers between devices  11.4 us (32%)
  blocking collectives  11.1 us (31%)
  waiting for transfers between devices  6.57 us (19%)
  Pallas kernels  4.7 us (13%)
  between operations  0.76 us (2%)
  local copies, waits for them, and re-layouts  0.66 us (2%)
    all_to_all x1, blocking collectives, local(): squares = lax.all_to_all(square, 'loop', 0, 0, tiled=True)  11.1 us
    ppermute x6, starting transfers between devices, to_next(): return lax.ppermute(array, 'loop', pairs)  7.99 us
    pallas_call x4, Pallas kernels, add_pieces(): pl.pallas_call(functools.partial(pieces_kernel, places, len(arrays), pack...  3.57 us
    ppermute x1, starting transfers between devices, across(): return lax.ppermute(array, 'loop', pairs)  3.31 us
    ppermute x6, waiting for transfers between devices, to_next(): return lax.ppermute(array, 'loop', pairs)  3.2 us
    ppermute x1, waiting for transfers between devices, across(): return lax.ppermute(array, 'loop', pairs)  2.72 us
    pallas_call x1, Pallas kernels, local(): pl.pallas_call(functools.partial(update_kernel, rows * loop_size * width)...  0.93 us
  transfers between devices with their start and end apart: 11, of which 4 were waited for; matrix products, arithmetic and copies ran while one was open for 0% of the time, Pallas kernels for 9%

profile of v18, /device:TPU:0, one launch (start us, length us, event | category | flops | bytes accessed | tf_op | source)
XLA Modules:
  0.0 35.2 jit_solution(12626320947145831079)
XLA Ops:
  0.0 3.0 %collective-permute-start = (bf16[128,512]{1,0:T(8,128)(2,1)}, bf16[128,512]{1,0:T(8,128)(2,1)S(1)}, u32[]{:S(2)}, u32[]{:S(2)}) collective-permute-start(bf16[128,512]{1,0:T(8,128)(2,1)} %refs_0_.1), channel_id=1, source_target_pairs={{0,4},{4,8},{8,12},{12,14},{14,10},{10,6},{6,2},{2,0},{1,3},{5,1},... | collective-permute-start | bytes 393224 | tf_op jit(solution)/shard_map/ppermute | solution.py:29
  3.0 0.0 collective-permute-start.1
  3.7 0.0 copy-start.3
  3.7 0.6 %copy-done.3 = s32[1,8]{1,0:T(1,128)S(1)} copy-done((s32[1,8]{1,0:T(1,128)S(1)}, s32[1,8]{1,0:T(1,128)}, u32[]{:S(2)}) %copy-start.3) | copy-done | bytes 56
  4.3 0.0 copy-start.2
  4.3 0.1 slot_table.1.table_ref
  4.5 0.0 copy-start
  4.5 0.0 copy-start.1
  4.5 2.5 %collective-permute-done.rest_1_.refs_1_ = bf16[128,512]{1,0:T(8,128)(2,1)S(1)} collective-permute-done((bf16[128,512]{1,0:T(8,128)(2,1)}, bf16[128,512]{1,0:T(8,128)(2,1)S(1)}, u32[]{:S(2)}, u32[]{:S(2)}) %collective-permute-start) | collective-permute-done | bytes 131104 | tf_op jit(solution)/shard_map/ppermute | solution.py:29
  7.0 0.0 collective-permute-start.2
  7.0 1.5 %collective-permute-start.3 = (bf16[128,512]{1,0:T(8,128)(2,1)S(1)}, bf16[128,512]{1,0:T(8,128)(2,1)S(1)}, u32[]{:S(2)}, u32[]{:S(2)}) collective-permute-start(bf16[128,512]{1,0:T(8,128)(2,1)S(1)} %collective-permute-done.rest_1_.refs_1_), channel_id=1, source_target_pairs={{0,4},{4,8},{8,12},{12,14},{14,10},{10,6},{6,2},{2,0},{1,3},{5,1},... | collective-permute-start | bytes 393224 | tf_op jit(solution)/shard_map/ppermute | solution.py:29
  8.5 0.0 collective-permute-done.1.rest_2_.refs_2_
  8.5 1.0 %collective-permute-start.5 = (bf16[128,512]{1,0:T(8,128)(2,1)S(1)}, bf16[128,512]{1,0:T(8,128)(2,1)S(1)}, u32[]{:S(2)}, u32[]{:S(2)}) collective-permute-start(bf16[128,512]{1,0:T(8,128)(2,1)S(1)} %collective-permute-done.1.rest_2_.refs_2_), channel_id=1, source_target_pairs={{0,2},{4,0},{8,4},{12,8},{14,12},{10,14},{6,10},{2,6},{1,5},{5,9},... | collective-permute-start | bytes 393224 | tf_op jit(solution)/shard_map/ppermute | solution.py:29
  9.5 0.0 copy-done.2
  9.5 3.3 %collective-permute-start.7 = (bf16[128,512]{1,0:T(8,128)(2,1)S(1)}, bf16[128,512]{1,0:T(8,128)(2,1)S(1)}, u32[]{:S(2)}, u32[]{:S(2)}) collective-permute-start(bf16[128,512]{1,0:T(8,128)(2,1)S(1)} %get-tuple-element.22), channel_id=1, source_target_pairs={{0,12},{1,13},{4,6},{5,7},{8,10},{9,11},{12,0},{13,1},{14,2},{15,3... | collective-permute-start | bytes 393224 | tf_op jit(solution)/shard_map/ppermute | solution.py:39
  12.8 0.0 collective-permute-start.9
  12.8 0.0 collective-permute-done.3.rest_0_
  12.8 1.7 %collective-permute-start.4 = (bf16[128,512]{1,0:T(8,128)(2,1)S(1)}, bf16[128,512]{1,0:T(8,128)(2,1)S(1)}, u32[]{:S(2)}, u32[]{:S(2)}) collective-permute-start(bf16[128,512]{1,0:T(8,128)(2,1)S(1)} %collective-permute-done.3.rest_0_), channel_id=1, source_target_pairs={{0,4},{4,8},{8,12},{12,14},{14,10},{10,6},{6,2},{2,0},{1,3},{5,1},... | collective-permute-start | bytes 393224 | tf_op jit(solution)/shard_map/ppermute | solution.py:29
  14.5 0.0 collective-permute-done.5.rest_1_
  14.5 0.8 %collective-permute-start.6 = (bf16[128,512]{1,0:T(8,128)(2,1)S(1)}, bf16[128,512]{1,0:T(8,128)(2,1)S(1)}, u32[]{:S(2)}, u32[]{:S(2)}) collective-permute-start(bf16[128,512]{1,0:T(8,128)(2,1)S(1)} %collective-permute-done.5.rest_1_), channel_id=1, source_target_pairs={{0,2},{4,0},{8,4},{12,8},{14,12},{10,14},{6,10},{2,6},{1,5},{5,9},... | collective-permute-start | bytes 393224 | tf_op jit(solution)/shard_map/ppermute | solution.py:29
  15.3 0.0 collective-permute-done.2.rest_3_
  15.3 0.0 copy-done
  15.3 0.0 copy-done.1
  15.3 1.0 %add_pieces.4 = (f32[256,512]{1,0:T(8,128)S(1)}, bf16[512,512]{1,0:T(8,128)(2,1)S(1)}) custom-call(s32[1,128]{1,0:T(1,128)S(1)} %slot_table.1.table_ref, f32[256,512]{1,0:T(8,128)S(1)} %copy-done, s32[256,1024]{1,0:T(8,128)S(1)} %copy-done.1, bf16[128,512]{1,0:T(8,128)(2,1)S(1)} %copy-done.2, bf16[128,512]{1,0:T(8,128)(2,1)S(1)} %collective-permute-done.rest_1_.refs_1_, ...), custom_call_target="tpu_custom_call" | custom-call | flops 536870912 | bytes 1048576 | tf_op jit(solution)/shard_map/add_pieces/pallas_call | solution.py:224
  16.4 0.7 %add_pieces.5 = (f32[256,512]{1,0:T(8,128)S(1)}, bf16[256,512]{1,0:T(8,128)(2,1)S(1)}) custom-call(s32[1,128]{1,0:T(1,128)S(1)} %slot_table.1.table_ref, bf16[512,512]{1,0:T(8,128)(2,1)S(1)} %get-tuple-element.21.given_ref, s32[256,1024]{1,0:T(8,128)S(1)} %copy-done.1, ...), custom_call_target="tpu_custom_call", output_to_operand_aliasing={{0}: (5, {})} | custom-call | flops 4294967296 | bytes 1048576 | tf_op jit(solution)/shard_map/add_pieces/pallas_call | solution.py:224
  17.1 0.1 collective-permute-start.10
  17.2 2.7 %collective-permute-done.7.refs_2_.rest_2_ = bf16[128,512]{1,0:T(8,128)(2,1)S(1)} collective-permute-done((bf16[128,512]{1,0:T(8,128)(2,1)S(1)}, bf16[128,512]{1,0:T(8,128)(2,1)S(1)}, u32[]{:S(2)}, u32[]{:S(2)}) %collective-permute-start.7) | collective-permute-done | bytes 131104 | tf_op jit(solution)/shard_map/ppermute | solution.py:39
  19.9 0.0 collective-permute-done.4.refs_0_.rest_0_
  19.9 0.7 %collective-permute-done.6.refs_1_.rest_1_ = bf16[128,512]{1,0:T(8,128)(2,1)S(1)} collective-permute-done((bf16[128,512]{1,0:T(8,128)(2,1)S(1)}, bf16[128,512]{1,0:T(8,128)(2,1)S(1)}, u32[]{:S(2)}, u32[]{:S(2)}) %collective-permute-start.6) | collective-permute-done | bytes 131104 | tf_op jit(solution)/shard_map/ppermute | solution.py:29
  20.6 0.1 collective-permute-start.8
  20.7 0.0 collective-permute-done.9.rest_3_
  20.7 0.0 collective-permute-done.10.rest_4_
  20.7 1.0 %add_pieces.6.rest_1_ = f32[256,512]{1,0:T(8,128)S(1)} custom-call(s32[1,128]{1,0:T(1,128)S(1)} %slot_table.1.table_ref, bf16[512,512]{1,0:T(8,128)(2,1)S(1)} %get-tuple-element.21.given_ref, s32[256,1024]{1,0:T(8,128)S(1)} %copy-done.1, bf16[128,512]{1,0:T(8,128)(2,1)S(1)} %collective-permute-done.4.refs_0_.rest_0_, ...), custom_call_target="tpu_custom_call", output_to_operand_aliasing={{}: (8, {})} | custom-call | flops 15032385536 | bytes 1048576 | tf_op jit(solution)/shard_map/add_pieces/pallas_call | solution.py:224
  21.8 0.6 %collective-permute-done.8.rest_0_ = bf16[384,512]{1,0:T(8,128)(2,1)S(1)} collective-permute-done((bf16[384,512]{1,0:T(8,128)(2,1)S(1)}, bf16[384,512]{1,0:T(8,128)(2,1)S(1)}, u32[]{:S(2)}, u32[]{:S(2)}) %collective-permute-start.8) | collective-permute-done | bytes 393248 | tf_op jit(solution)/shard_map/ppermute | solution.py:43
  22.4 0.8 %add_pieces.7 = (f32[256,512]{1,0:T(8,128)S(1)}, f32[16,128]{1,0:T(8,128)S(1)}) custom-call(s32[1,128]{1,0:T(1,128)S(1)} %slot_table.1.table_ref, bf16[512,512]{1,0:T(8,128)(2,1)S(1)} %get-tuple-element.21.given_ref, s32[256,1024]{1,0:T(8,128)S(1)} %copy-done.1, ...), custom_call_target="tpu_custom_call", output_to_operand_aliasing={{0}: (4, {})} | custom-call | flops 6442450944 | bytes 1048576 | tf_op jit(solution)/shard_map/add_pieces/pallas_call | solution.py:224
  23.2 11.1 %all_to_all.11 = f32[16,1,128]{2,1,0:T(1,128)S(1)} all-to-all(f32[16,1,128]{2,1,0:T(1,128)S(1)} %bitcast.7), channel_id=1, replica_groups=mesh['group'=2,'loop'=16] {'loop'}, dimensions={0} | all-to-all | bytes 16384 | tf_op jit(solution)/shard_map/all_to_all | solution.py:376
  34.3 0.9 %update.1 = f32[256,512]{1,0:T(8,128)} custom-call(f32[256,512]{1,0:T(8,128)S(1)} %copy-done, f32[256,512]{1,0:T(8,128)S(1)} %get-tuple-element.31.grad_ref, f32[16,128]{1,0:T(8,128)S(1)} %bitcast.6), custom_call_target="tpu_custom_call" | custom-call | flops 262144 | bytes 1572864 | tf_op jit(solution)/shard_map/update/pallas_call | solution.py:377
  (2 shorter events, 0.1 us)
Async XLA Ops:
  0.0 7.0 %collective-permute-start = (bf16[128,512]{1,0:T(8,128)(2,1)}, bf16[128,512]{1,0:T(8,128)(2,1)S(1)}, u32[]{:S(2)}, u32[]{:S(2)}) collective-permute-start(bf16[128,512]{1,0:T(8,128)(2,1)} %refs_0_.1), channel_id=1, source_target_pairs={{0,4},{4,8},{8,12},{12,14},{14,10},{10,6},{6,2},{2,0},{1,3},{5,1},... | collective-permute-start | bytes 393224 | tf_op jit(solution)/shard_map/ppermute | solution.py:29
  3.0 5.5 %collective-permute-start.1 = (bf16[128,512]{1,0:T(8,128)(2,1)}, bf16[128,512]{1,0:T(8,128)(2,1)S(1)}, u32[]{:S(2)}, u32[]{:S(2)}) collective-permute-start(bf16[128,512]{1,0:T(8,128)(2,1)} %refs_0_.1), channel_id=1, source_target_pairs={{0,2},{4,0},{8,4},{12,8},{14,12},{10,14},{6,10},{2,6},{1,5},{5,9},... | collective-permute-start | bytes 393224 | tf_op jit(solution)/shard_map/ppermute | solution.py:29
  3.7 0.7 %copy-start.3 = (s32[1,8]{1,0:T(1,128)S(1)}, s32[1,8]{1,0:T(1,128)}, u32[]{:S(2)}) copy-start(s32[1,8]{1,0:T(1,128)} %list_ref.1) | copy-start | bytes 100
  4.3 5.1 %copy-start.2 = (bf16[128,512]{1,0:T(8,128)(2,1)S(1)}, bf16[128,512]{1,0:T(8,128)(2,1)}, u32[]{:S(2)}) copy-start(bf16[128,512]{1,0:T(8,128)(2,1)} %refs_0_.1) | copy-start | bytes 393220
  4.5 10.8 %copy-start = (f32[256,512]{1,0:T(8,128)S(1)}, f32[256,512]{1,0:T(8,128)}, u32[]{:S(2)}) copy-start(f32[256,512]{1,0:T(8,128)} %users_ref.1) | copy-start | bytes 1572868
  4.5 10.8 %copy-start.1 = (s32[256,1024]{1,0:T(8,128)S(1)}, s32[256,1024]{1,0:T(8,128)}, u32[]{:S(2)}) copy-start(s32[256,1024]{1,0:T(8,128)} %labels_ref.7) | copy-start | bytes 3145732
  7.0 8.3 %collective-permute-start.2 = (bf16[128,512]{1,0:T(8,128)(2,1)S(1)}, bf16[128,512]{1,0:T(8,128)(2,1)S(1)}, u32[]{:S(2)}, u32[]{:S(2)}) collective-permute-start(bf16[128,512]{1,0:T(8,128)(2,1)S(1)} %collective-permute-done.rest_1_.refs_1_), channel_id=1, source_target_pairs={{0,1},{1,0},{2,3},{3,2},{4,5},{5,4},{6,7},{7,6},{8,9},{9,8},{10,11... | collective-permute-start | bytes 393224 | tf_op jit(solution)/shard_map/ppermute | solution.py:43
  7.0 5.8 %collective-permute-start.3 = (bf16[128,512]{1,0:T(8,128)(2,1)S(1)}, bf16[128,512]{1,0:T(8,128)(2,1)S(1)}, u32[]{:S(2)}, u32[]{:S(2)}) collective-permute-start(bf16[128,512]{1,0:T(8,128)(2,1)S(1)} %collective-permute-done.rest_1_.refs_1_), channel_id=1, source_target_pairs={{0,4},{4,8},{8,12},{12,14},{14,10},{10,6},{6,2},{2,0},{1,3},{5,1},... | collective-permute-start | bytes 393224 | tf_op jit(solution)/shard_map/ppermute | solution.py:29
  8.5 6.0 %collective-permute-start.5 = (bf16[128,512]{1,0:T(8,128)(2,1)S(1)}, bf16[128,512]{1,0:T(8,128)(2,1)S(1)}, u32[]{:S(2)}, u32[]{:S(2)}) collective-permute-start(bf16[128,512]{1,0:T(8,128)(2,1)S(1)} %collective-permute-done.1.rest_2_.refs_2_), channel_id=1, source_target_pairs={{0,2},{4,0},{8,4},{12,8},{14,12},{10,14},{6,10},{2,6},{1,5},{5,9},... | collective-permute-start | bytes 393224 | tf_op jit(solution)/shard_map/ppermute | solution.py:29
  9.5 10.4 %collective-permute-start.7 = (bf16[128,512]{1,0:T(8,128)(2,1)S(1)}, bf16[128,512]{1,0:T(8,128)(2,1)S(1)}, u32[]{:S(2)}, u32[]{:S(2)}) collective-permute-start(bf16[128,512]{1,0:T(8,128)(2,1)S(1)} %get-tuple-element.22), channel_id=1, source_target_pairs={{0,12},{1,13},{4,6},{5,7},{8,10},{9,11},{12,0},{13,1},{14,2},{15,3... | collective-permute-start | bytes 393224 | tf_op jit(solution)/shard_map/ppermute | solution.py:39
  12.8 7.9 %collective-permute-start.9 = (bf16[256,512]{1,0:T(8,128)(2,1)S(1)}, bf16[256,512]{1,0:T(8,128)(2,1)S(1)}, u32[]{:S(2)}, u32[]{:S(2)}) collective-permute-start(bf16[256,512]{1,0:T(8,128)(2,1)S(1)} %get-tuple-element.28), channel_id=1, source_target_pairs={{0,1},{1,0},{2,3},{3,2},{4,5},{5,4},{6,7},{7,6},{8,9},{9,8},{10,11... | collective-permute-start | bytes 786440 | tf_op jit(solution)/shard_map/ppermute | solution.py:43
  12.8 7.1 %collective-permute-start.4 = (bf16[128,512]{1,0:T(8,128)(2,1)S(1)}, bf16[128,512]{1,0:T(8,128)(2,1)S(1)}, u32[]{:S(2)}, u32[]{:S(2)}) collective-permute-start(bf16[128,512]{1,0:T(8,128)(2,1)S(1)} %collective-permute-done.3.rest_0_), channel_id=1, source_target_pairs={{0,4},{4,8},{8,12},{12,14},{14,10},{10,6},{6,2},{2,0},{1,3},{5,1},... | collective-permute-start | bytes 393224 | tf_op jit(solution)/shard_map/ppermute | solution.py:29
  14.5 6.1 %collective-permute-start.6 = (bf16[128,512]{1,0:T(8,128)(2,1)S(1)}, bf16[128,512]{1,0:T(8,128)(2,1)S(1)}, u32[]{:S(2)}, u32[]{:S(2)}) collective-permute-start(bf16[128,512]{1,0:T(8,128)(2,1)S(1)} %collective-permute-done.5.rest_1_), channel_id=1, source_target_pairs={{0,2},{4,0},{8,4},{12,8},{14,12},{10,14},{6,10},{2,6},{1,5},{5,9},... | collective-permute-start | bytes 393224 | tf_op jit(solution)/shard_map/ppermute | solution.py:29
  17.1 3.6 %collective-permute-start.10 = (bf16[256,512]{1,0:T(8,128)(2,1)S(1)}, bf16[256,512]{1,0:T(8,128)(2,1)S(1)}, u32[]{:S(2)}, u32[]{:S(2)}) collective-permute-start(bf16[256,512]{1,0:T(8,128)(2,1)S(1)} %get-tuple-element.29), channel_id=1, source_target_pairs={{0,1},{1,0},{2,3},{3,2},{4,5},{5,4},{6,7},{7,6},{8,9},{9,8},{10,11... | collective-permute-start | bytes 786440 | tf_op jit(solution)/shard_map/ppermute | solution.py:43
  20.6 1.8 %collective-permute-start.8 = (bf16[384,512]{1,0:T(8,128)(2,1)S(1)}, bf16[384,512]{1,0:T(8,128)(2,1)S(1)}, u32[]{:S(2)}, u32[]{:S(2)}) collective-permute-start(bf16[384,512]{1,0:T(8,128)(2,1)S(1)} %pack.3), channel_id=1, source_target_pairs={{0,1},{1,0},{2,3},{3,2},{4,5},{5,4},{6,7},{7,6},{8,9},{9,8},{10,11... | collective-permute-start | bytes 1179656 | tf_op jit(solution)/shard_map/ppermute | solution.py:43

commit v19 on v16

--- a/solution.py
+++ b/solution.py
@@ -16,7 +16,7 @@
 
     def device(position, core):
         position = position % (2 * outer)
-        chip = 2 * position if position < outer else 2 * (2 * outer - 1 - position) + 1
+        chip = 2 * (outer - 1 - position) if position < outer else 2 * (position - outer) + 1
         return 2 * chip + core
 
     return 2 * outer, device
@@ -57,7 +57,7 @@
         hops = jnp.where(lane == at, origin[0], hops)
         other = jnp.where(lane == at, origin[1], other)
     at = (position + chips + jnp.where(core == 0, -hops, hops)) & (chips - 1)
-    chip = jnp.where(at < chips // 2, 2 * at, 2 * (chips - 1 - at) + 1)
+    chip = jnp.where(at < chips // 2, chips - 2 - 2 * at, 2 * at - chips + 1)
     block = 2 * chip + jnp.where(other == 1, 1 - core, core)
     found = jnp.full_like(lane, -1)
     for slot in range(list_ref.shape[1]):
@@ -130,7 +130,7 @@
 def core_and_position(loop_size):
     me = lax.axis_index("loop")
     core, row, outer = me % 2, me // 2 % 2, me // 4
-    return core, jnp.where(row == 0, outer, loop_size // 2 - 1 - outer)
+    return core, loop_size // 4 + jnp.where(row == 0, -1 - outer, outer)
 
 
 def pack_kernel(*refs):

time: 35.4 us -> 35.2 us (level)
  starting transfers between devices: 9.29 us -> 11.1 us
  blocking collectives: 11.1 us -> 10.4 us
  Pallas kernels: 4.96 us -> 4.38 us
    ppermute x6, waiting for transfers between devices: 6.16 us -> 4.59 us  [to_next(): return lax.ppermute(array, 'loop', pairs)]
    ppermute x1, waiting for transfers between devices: 1.45 us -> 2.85 us  [across(): return lax.ppermute(array, 'loop', pairs)]
    ppermute x1, starting transfers between devices: 2.48 us -> 3.37 us  [across(): return lax.ppermute(array, 'loop', pairs)]
    ppermute x6, starting transfers between devices: 6.66 us -> 7.47 us  [to_next(): return lax.ppermute(array, 'loop', pairs)]
    all_to_all x1, blocking collectives: 11.1 us -> 10.4 us  [local(): squares = lax.all_to_all(square, 'loop', 0, 0, tiled=True)]
    pallas_call x4, Pallas kernels: 3.85 us -> 3.27 us  [add_pieces(): pl.pallas_call(functools.partial(pieces_kernel, places, len(arrays), pack...]
  transfers between devices with their start and end apart: 10 -> 10, of which waited for: 7 -> 4; matrix products, arithmetic and copies ran while one was open for 0% -> 0% of each run, Pallas kernels for 9% -> 7%
where the time goes in v19:
time: 35.2 us
  starting transfers between devices  11.1 us (32%)
  blocking collectives  10.4 us (30%)
  waiting for transfers between devices  8.04 us (23%)
  Pallas kernels  4.38 us (12%)
  between operations  0.72 us (2%)
  local copies, waits for them, and re-layouts  0.66 us (2%)
    all_to_all x1, blocking collectives, local(): squares = lax.all_to_all(square, 'loop', 0, 0, tiled=True)  10.4 us
    ppermute x6, starting transfers between devices, to_next(): return lax.ppermute(array, 'loop', pairs)  7.47 us
    ppermute x6, waiting for transfers between devices, to_next(): return lax.ppermute(array, 'loop', pairs)  4.59 us
    ppermute x1, starting transfers between devices, across(): return lax.ppermute(array, 'loop', pairs)  3.37 us
    pallas_call x4, Pallas kernels, add_pieces(): pl.pallas_call(functools.partial(pieces_kernel, places, len(arrays), pack...  3.27 us
    ppermute x1, waiting for transfers between devices, across(): return lax.ppermute(array, 'loop', pairs)  2.85 us
    pallas_call x1, Pallas kernels, local(): pl.pallas_call(functools.partial(update_kernel, rows * loop_size * width)...  0.93 us
  transfers between devices with their start and end apart: 10, of which 4 were waited for; matrix products, arithmetic and copies ran while one was open for 0% of the time, Pallas kernels for 7%

profile of v19, /device:TPU:0, one launch (start us, length us, event | category | flops | bytes accessed | tf_op | source)
XLA Modules:
  0.0 35.2 jit_solution(8367653435225080291)
XLA Ops:
  0.0 3.0 %collective-permute-start = (bf16[128,512]{1,0:T(8,128)(2,1)}, bf16[128,512]{1,0:T(8,128)(2,1)S(1)}, u32[]{:S(2)}, u32[]{:S(2)}) collective-permute-start(bf16[128,512]{1,0:T(8,128)(2,1)} %rest_0_.1), channel_id=1, source_target_pairs={{12,8},{8,4},{4,0},{0,2},{2,6},{6,10},{10,14},{14,12},{13,15},{9,1... | collective-permute-start | bytes 393224 | tf_op jit(solution)/shard_map/ppermute | solution.py:29
  3.0 0.1 collective-permute-start.1
  3.7 0.0 copy-start.3
  3.7 0.6 %copy-done.3 = s32[1,8]{1,0:T(1,128)S(1)} copy-done((s32[1,8]{1,0:T(1,128)S(1)}, s32[1,8]{1,0:T(1,128)}, u32[]{:S(2)}) %copy-start.3) | copy-done | bytes 56
  4.3 0.0 copy-start
  4.3 0.0 copy-start.1
  4.3 0.0 copy-start.2
  4.3 0.1 slot_table.1.table_ref
  4.5 2.5 %collective-permute-done.rest_1_ = bf16[128,512]{1,0:T(8,128)(2,1)S(1)} collective-permute-done((bf16[128,512]{1,0:T(8,128)(2,1)}, bf16[128,512]{1,0:T(8,128)(2,1)S(1)}, u32[]{:S(2)}, u32[]{:S(2)}) %collective-permute-start) | collective-permute-done | bytes 131104 | tf_op jit(solution)/shard_map/ppermute | solution.py:29
  7.0 1.5 %collective-permute-start.2 = (bf16[128,512]{1,0:T(8,128)(2,1)S(1)}, bf16[128,512]{1,0:T(8,128)(2,1)S(1)}, u32[]{:S(2)}, u32[]{:S(2)}) collective-permute-start(bf16[128,512]{1,0:T(8,128)(2,1)S(1)} %collective-permute-done.rest_1_), channel_id=1, source_target_pairs={{12,8},{8,4},{4,0},{0,2},{2,6},{6,10},{10,14},{14,12},{13,15},{9,1... | collective-permute-start | bytes 393224 | tf_op jit(solution)/shard_map/ppermute | solution.py:29
  8.5 0.0 collective-permute-done.1.rest_2_
  8.5 0.9 %collective-permute-start.4 = (bf16[128,512]{1,0:T(8,128)(2,1)S(1)}, bf16[128,512]{1,0:T(8,128)(2,1)S(1)}, u32[]{:S(2)}, u32[]{:S(2)}) collective-permute-start(bf16[128,512]{1,0:T(8,128)(2,1)S(1)} %collective-permute-done.1.rest_2_), channel_id=1, source_target_pairs={{12,14},{8,12},{4,8},{0,4},{2,0},{6,2},{10,6},{14,10},{13,9},{9,5}... | collective-permute-start | bytes 393224 | tf_op jit(solution)/shard_map/ppermute | solution.py:29
  9.5 0.0 copy-done
  9.5 0.0 copy-done.1
  9.5 0.0 copy-done.2
  9.5 1.1 %add_pieces.4 = (f32[256,512]{1,0:T(8,128)S(1)}, bf16[512,512]{1,0:T(8,128)(2,1)S(1)}, bf16[128,512]{1,0:T(8,128)(2,1)S(1)}, bf16[384,512]{1,0:T(8,128)(2,1)S(1)}) custom-call(s32[1,128]{1,0:T(1,128)S(1)} %slot_table.1.table_ref, f32[256,512]{1,0:T(8,128)S(1)} %copy-done, s32[256,1024]{1,0:T(8,128)S(1)} %copy-done.1, bf16[128,512]{1,0:T(8,128)(2,1)S(1)} %copy-done.2, ...), custom_call_target="tpu_custom_call" | custom-call | flops 6442450944 | bytes 1048576 | tf_op jit(solution)/shard_map/add_pieces/pallas_call | solution.py:220
  10.6 3.4 %collective-permute-start.6 = (bf16[128,512]{1,0:T(8,128)(2,1)S(1)}, bf16[128,512]{1,0:T(8,128)(2,1)S(1)}, u32[]{:S(2)}, u32[]{:S(2)}) collective-permute-start(bf16[128,512]{1,0:T(8,128)(2,1)S(1)} %get-tuple-element.22), channel_id=1, source_target_pairs={{12,0},{13,1},{8,10},{9,11},{4,6},{5,7},{0,12},{1,13},{2,14},{3,15... | collective-permute-start | bytes 393224 | tf_op jit(solution)/shard_map/ppermute | solution.py:39
  13.9 0.0 collective-permute-start.8
  13.9 0.0 collective-permute-done.2.rest_0_
  13.9 0.7 %collective-permute-start.3 = (bf16[128,512]{1,0:T(8,128)(2,1)S(1)}, bf16[128,512]{1,0:T(8,128)(2,1)S(1)}, u32[]{:S(2)}, u32[]{:S(2)}) collective-permute-start(bf16[128,512]{1,0:T(8,128)(2,1)S(1)} %collective-permute-done.2.rest_0_), channel_id=1, source_target_pairs={{12,8},{8,4},{4,0},{0,2},{2,6},{6,10},{10,14},{14,12},{13,15},{9,1... | collective-permute-start | bytes 393224 | tf_op jit(solution)/shard_map/ppermute | solution.py:29
  14.6 0.0 collective-permute-done.4.rest_1_
  14.6 1.4 %collective-permute-start.5 = (bf16[128,512]{1,0:T(8,128)(2,1)S(1)}, bf16[128,512]{1,0:T(8,128)(2,1)S(1)}, u32[]{:S(2)}, u32[]{:S(2)}) collective-permute-start(bf16[128,512]{1,0:T(8,128)(2,1)S(1)} %collective-permute-done.4.rest_1_), channel_id=1, source_target_pairs={{12,14},{8,12},{4,8},{0,4},{2,0},{6,2},{10,6},{14,10},{13,9},{9,5}... | collective-permute-start | bytes 393224 | tf_op jit(solution)/shard_map/ppermute | solution.py:29
  16.0 0.1 add_pieces.5
  16.1 0.1 collective-permute-start.9
  16.2 2.9 %collective-permute-done.6.refs_2_.rest_2_ = bf16[128,512]{1,0:T(8,128)(2,1)S(1)} collective-permute-done((bf16[128,512]{1,0:T(8,128)(2,1)S(1)}, bf16[128,512]{1,0:T(8,128)(2,1)S(1)}, u32[]{:S(2)}, u32[]{:S(2)}) %collective-permute-start.6) | collective-permute-done | bytes 131104 | tf_op jit(solution)/shard_map/ppermute | solution.py:39
  19.0 2.0 %collective-permute-done.3.refs_0_.rest_0_ = bf16[128,512]{1,0:T(8,128)(2,1)S(1)} collective-permute-done((bf16[128,512]{1,0:T(8,128)(2,1)S(1)}, bf16[128,512]{1,0:T(8,128)(2,1)S(1)}, u32[]{:S(2)}, u32[]{:S(2)}) %collective-permute-start.3) | collective-permute-done | bytes 131104 | tf_op jit(solution)/shard_map/ppermute | solution.py:29
  21.1 0.0 collective-permute-done.5.refs_1_.rest_1_
  21.1 0.1 collective-permute-start.7
  21.3 0.0 collective-permute-done.9.rest_4_
  21.3 0.0 collective-permute-done.8.rest_3_
  21.3 1.1 %add_pieces.6.rest_1_ = f32[256,512]{1,0:T(8,128)S(1)} custom-call(s32[1,128]{1,0:T(1,128)S(1)} %slot_table.1.table_ref, bf16[512,512]{1,0:T(8,128)(2,1)S(1)} %get-tuple-element.21.given_ref, s32[256,1024]{1,0:T(8,128)S(1)} %copy-done.1, bf16[128,512]{1,0:T(8,128)(2,1)S(1)} %collective-permute-done.3.refs_0_.rest_0_, ...), custom_call_target="tpu_custom_call", output_to_operand_aliasing={{}: (8, {})} | custom-call | flops 17179869184 | bytes 1048576 | tf_op jit(solution)/shard_map/add_pieces/pallas_call | solution.py:220
  22.3 0.6 %collective-permute-done.7.rest_0_ = bf16[384,512]{1,0:T(8,128)(2,1)S(1)} collective-permute-done((bf16[384,512]{1,0:T(8,128)(2,1)S(1)}, bf16[384,512]{1,0:T(8,128)(2,1)S(1)}, u32[]{:S(2)}, u32[]{:S(2)}) %collective-permute-start.7) | collective-permute-done | bytes 393248 | tf_op jit(solution)/shard_map/ppermute | solution.py:43
  22.9 1.0 %add_pieces.7 = (f32[256,512]{1,0:T(8,128)S(1)}, f32[16,128]{1,0:T(8,128)S(1)}) custom-call(s32[1,128]{1,0:T(1,128)S(1)} %slot_table.1.table_ref, bf16[512,512]{1,0:T(8,128)(2,1)S(1)} %get-tuple-element.21.given_ref, s32[256,1024]{1,0:T(8,128)S(1)} %copy-done.1, ...), custom_call_target="tpu_custom_call", output_to_operand_aliasing={{0}: (4, {})} | custom-call | flops 6442450944 | bytes 1048576 | tf_op jit(solution)/shard_map/add_pieces/pallas_call | solution.py:220
  23.9 10.4 %all_to_all.11 = f32[16,1,128]{2,1,0:T(1,128)S(1)} all-to-all(f32[16,1,128]{2,1,0:T(1,128)S(1)} %bitcast.7), channel_id=1, replica_groups=mesh['group'=2,'loop'=16] {'loop'}, dimensions={0} | all-to-all | bytes 16384 | tf_op jit(solution)/shard_map/all_to_all | solution.py:372
  34.3 0.9 %update.1 = f32[256,512]{1,0:T(8,128)} custom-call(f32[256,512]{1,0:T(8,128)S(1)} %copy-done, f32[256,512]{1,0:T(8,128)S(1)} %get-tuple-element.31.grad_ref, f32[16,128]{1,0:T(8,128)S(1)} %bitcast.6), custom_call_target="tpu_custom_call" | custom-call | flops 262144 | bytes 1572864 | tf_op jit(solution)/shard_map/update/pallas_call | solution.py:373
  (1 shorter events, 0.0 us)
Async XLA Ops:
  0.0 7.0 %collective-permute-start = (bf16[128,512]{1,0:T(8,128)(2,1)}, bf16[128,512]{1,0:T(8,128)(2,1)S(1)}, u32[]{:S(2)}, u32[]{:S(2)}) collective-permute-start(bf16[128,512]{1,0:T(8,128)(2,1)} %rest_0_.1), channel_id=1, source_target_pairs={{12,8},{8,4},{4,0},{0,2},{2,6},{6,10},{10,14},{14,12},{13,15},{9,1... | collective-permute-start | bytes 393224 | tf_op jit(solution)/shard_map/ppermute | solution.py:29
  3.0 5.5 %collective-permute-start.1 = (bf16[128,512]{1,0:T(8,128)(2,1)}, bf16[128,512]{1,0:T(8,128)(2,1)S(1)}, u32[]{:S(2)}, u32[]{:S(2)}) collective-permute-start(bf16[128,512]{1,0:T(8,128)(2,1)} %rest_0_.1), channel_id=1, source_target_pairs={{12,14},{8,12},{4,8},{0,4},{2,0},{6,2},{10,6},{14,10},{13,9},{9,5}... | collective-permute-start | bytes 393224 | tf_op jit(solution)/shard_map/ppermute | solution.py:29
  3.7 0.7 %copy-start.3 = (s32[1,8]{1,0:T(1,128)S(1)}, s32[1,8]{1,0:T(1,128)}, u32[]{:S(2)}) copy-start(s32[1,8]{1,0:T(1,128)} %list_ref.1) | copy-start | bytes 100
  4.3 5.1 %copy-start = (f32[256,512]{1,0:T(8,128)S(1)}, f32[256,512]{1,0:T(8,128)}, u32[]{:S(2)}) copy-start(f32[256,512]{1,0:T(8,128)} %users_ref.1) | copy-start | bytes 1572868
  4.3 5.1 %copy-start.1 = (s32[256,1024]{1,0:T(8,128)S(1)}, s32[256,1024]{1,0:T(8,128)}, u32[]{:S(2)}) copy-start(s32[256,1024]{1,0:T(8,128)} %labels_ref.7) | copy-start | bytes 3145732
  4.3 5.1 %copy-start.2 = (bf16[128,512]{1,0:T(8,128)(2,1)S(1)}, bf16[128,512]{1,0:T(8,128)(2,1)}, u32[]{:S(2)}) copy-start(bf16[128,512]{1,0:T(8,128)(2,1)} %rest_0_.1) | copy-start | bytes 393220
  7.0 6.9 %collective-permute-start.2 = (bf16[128,512]{1,0:T(8,128)(2,1)S(1)}, bf16[128,512]{1,0:T(8,128)(2,1)S(1)}, u32[]{:S(2)}, u32[]{:S(2)}) collective-permute-start(bf16[128,512]{1,0:T(8,128)(2,1)S(1)} %collective-permute-done.rest_1_), channel_id=1, source_target_pairs={{12,8},{8,4},{4,0},{0,2},{2,6},{6,10},{10,14},{14,12},{13,15},{9,1... | collective-permute-start | bytes 393224 | tf_op jit(solution)/shard_map/ppermute | solution.py:29
  8.5 6.1 %collective-permute-start.4 = (bf16[128,512]{1,0:T(8,128)(2,1)S(1)}, bf16[128,512]{1,0:T(8,128)(2,1)S(1)}, u32[]{:S(2)}, u32[]{:S(2)}) collective-permute-start(bf16[128,512]{1,0:T(8,128)(2,1)S(1)} %collective-permute-done.1.rest_2_), channel_id=1, source_target_pairs={{12,14},{8,12},{4,8},{0,4},{2,0},{6,2},{10,6},{14,10},{13,9},{9,5}... | collective-permute-start | bytes 393224 | tf_op jit(solution)/shard_map/ppermute | solution.py:29
  10.6 8.5 %collective-permute-start.6 = (bf16[128,512]{1,0:T(8,128)(2,1)S(1)}, bf16[128,512]{1,0:T(8,128)(2,1)S(1)}, u32[]{:S(2)}, u32[]{:S(2)}) collective-permute-start(bf16[128,512]{1,0:T(8,128)(2,1)S(1)} %get-tuple-element.22), channel_id=1, source_target_pairs={{12,0},{13,1},{8,10},{9,11},{4,6},{5,7},{0,12},{1,13},{2,14},{3,15... | collective-permute-start | bytes 393224 | tf_op jit(solution)/shard_map/ppermute | solution.py:39
  13.9 7.3 %collective-permute-start.8 = (bf16[384,512]{1,0:T(8,128)(2,1)S(1)}, bf16[384,512]{1,0:T(8,128)(2,1)S(1)}, u32[]{:S(2)}, u32[]{:S(2)}) collective-permute-start(bf16[384,512]{1,0:T(8,128)(2,1)S(1)} %get-tuple-element.28), channel_id=1, source_target_pairs={{0,1},{1,0},{2,3},{3,2},{4,5},{5,4},{6,7},{7,6},{8,9},{9,8},{10,11... | collective-permute-start | bytes 1179656 | tf_op jit(solution)/shard_map/ppermute | solution.py:43
  13.9 7.2 %collective-permute-start.3 = (bf16[128,512]{1,0:T(8,128)(2,1)S(1)}, bf16[128,512]{1,0:T(8,128)(2,1)S(1)}, u32[]{:S(2)}, u32[]{:S(2)}) collective-permute-start(bf16[128,512]{1,0:T(8,128)(2,1)S(1)} %collective-permute-done.2.rest_0_), channel_id=1, source_target_pairs={{12,8},{8,4},{4,0},{0,2},{2,6},{6,10},{10,14},{14,12},{13,15},{9,1... | collective-permute-start | bytes 393224 | tf_op jit(solution)/shard_map/ppermute | solution.py:29
  14.6 6.5 %collective-permute-start.5 = (bf16[128,512]{1,0:T(8,128)(2,1)S(1)}, bf16[128,512]{1,0:T(8,128)(2,1)S(1)}, u32[]{:S(2)}, u32[]{:S(2)}) collective-permute-start(bf16[128,512]{1,0:T(8,128)(2,1)S(1)} %collective-permute-done.4.rest_1_), channel_id=1, source_target_pairs={{12,14},{8,12},{4,8},{0,4},{2,0},{6,2},{10,6},{14,10},{13,9},{9,5}... | collective-permute-start | bytes 393224 | tf_op jit(solution)/shard_map/ppermute | solution.py:29
  16.1 5.2 %collective-permute-start.9 = (bf16[256,512]{1,0:T(8,128)(2,1)S(1)}, bf16[256,512]{1,0:T(8,128)(2,1)S(1)}, u32[]{:S(2)}, u32[]{:S(2)}) collective-permute-start(bf16[256,512]{1,0:T(8,128)(2,1)S(1)} %get-tuple-element.29), channel_id=1, source_target_pairs={{0,1},{1,0},{2,3},{3,2},{4,5},{5,4},{6,7},{7,6},{8,9},{9,8},{10,11... | collective-permute-start | bytes 786440 | tf_op jit(solution)/shard_map/ppermute | solution.py:43
  21.1 1.8 %collective-permute-start.7 = (bf16[384,512]{1,0:T(8,128)(2,1)S(1)}, bf16[384,512]{1,0:T(8,128)(2,1)S(1)}, u32[]{:S(2)}, u32[]{:S(2)}) collective-permute-start(bf16[384,512]{1,0:T(8,128)(2,1)S(1)} %pack.1), channel_id=1, source_target_pairs={{0,1},{1,0},{2,3},{3,2},{4,5},{5,4},{6,7},{7,6},{8,9},{9,8},{10,11... | collective-permute-start | bytes 1179656 | tf_op jit(solution)/shard_map/ppermute | solution.py:43

commit v20 on v16

--- a/solution.py
+++ b/solution.py
@@ -31,12 +31,13 @@
 
 def across(array, loop_size):
     chips, device = ring_place(loop_size)
-    pairs = [
-        (device(at, core), device(at + (3 if at % 2 == 0 else -3), core))
-        for at in range(chips)
-        for core in range(2)
-    ]
+    pairs = [(device(at, 0), device(at + (3 if at % 2 == 0 else -3), 0)) for at in range(chips)]
     return lax.ppermute(array, "loop", pairs)
+
+
+def to_opposite(array, loop_size):
+    chips, device = ring_place(loop_size)
+    return lax.ppermute(array, "loop", [(device(at, 1), device(at + chips // 2, 1)) for at in range(chips)])
 
 
 def to_other_core(array, loop_size):
@@ -52,10 +53,11 @@
     chips = loop_size // 2
     lane = lax.broadcasted_iota(jnp.int32, table_ref.shape, 1)
     core, position = core_and_position(loop_size)
-    hops, other = jnp.zeros_like(lane), jnp.zeros_like(lane)
+    hops, other, missing = jnp.zeros_like(lane), jnp.zeros_like(lane), jnp.full_like(lane, 2)
     for at, origin in enumerate(origins):
         hops = jnp.where(lane == at, origin[0], hops)
         other = jnp.where(lane == at, origin[1], other)
+        missing = jnp.where(lane == at, origin[2], missing)
     at = (position + chips + jnp.where(core == 0, -hops, hops)) & (chips - 1)
     chip = jnp.where(at < chips // 2, 2 * at, 2 * (chips - 1 - at) + 1)
     block = 2 * chip + jnp.where(other == 1, 1 - core, core)
@@ -63,7 +65,7 @@
     for slot in range(list_ref.shape[1]):
         name = jnp.where(slot < count_ref[...], list_ref[:, slot : slot + 1], -1)
         found = jnp.where(name == block, slot, found)
-    table_ref[...] = jnp.where(lane < len(origins), found, -1)
+    table_ref[...] = jnp.where((lane < len(origins)) & (missing != core), found, -1)
 
 
 def slot_table(loop_size, origins, block_list, live_count):
@@ -135,15 +137,21 @@
 
 def pack_kernel(*refs):
     tile = refs[0].shape[0]
-    for at, ref in enumerate(refs[:-1]):
-        refs[-1][at * tile : (at + 1) * tile, :] = ref[...]
+    packed_ref = refs[-1]
+    for at, ref in enumerate(refs[:-3]):
+        packed_ref[at * tile : (at + 1) * tile, :] = ref[...]
+    for core, ref in enumerate(refs[-3:-1]):
+
+        @pl.when(lax.axis_index("loop") % 2 == core)
+        def _():
+            packed_ref[(len(refs) - 3) * tile :, :] = ref[...]
 
 
 def pack(arrays):
     tile, width = arrays[0].shape
     return pl.pallas_call(
         pack_kernel,
-        out_shape=jax.ShapeDtypeStruct((len(arrays) * tile, width), arrays[0].dtype),
+        out_shape=jax.ShapeDtypeStruct(((len(arrays) - 1) * tile, width), arrays[0].dtype),
         in_specs=[pl.BlockSpec(memory_space=pltpu.VMEM)] * len(arrays),
         out_specs=pl.BlockSpec(memory_space=pltpu.VMEM),
         compiler_params=pltpu.CompilerParams(vmem_limit_bytes=16 * 1024 * 1024),
@@ -240,21 +248,22 @@
 def ring_gradient(users, items, lists, labels):
     loop_size = lax.axis_size("loop")
     far = loop_size // 4
-    origins = [(hops, 0) for hops in range(1 - far, far + 1)]
-    origins += [(-hops, 1) for hops, _ in origins]
+    origins = [(hops, 0, 2) for hops in range(1 - far, far)] + [(far, 0, 1), (far, 0, 0)]
+    origins += [(-hops, 1, 2) for hops in range(1 - far, far + 1)]
     table = slot_table(loop_size, origins, *lists)
     where = {origin: at for at, origin in enumerate(origins)}
 
-    def held(hops, array):
-        return array, [where[hops, 0]]
+    def held(hops, array, missing=2):
+        return array, [where[hops, 0, missing]]
 
     def other(arrays, hops):
-        return to_other_core(arrays, loop_size), [where[-hop, 1] for hop in hops]
+        return to_other_core(arrays, loop_size), [where[-hop, 1, 2] for hop in hops]
 
     up = to_next(items, 1, loop_size)
     down = to_next(items, -1, loop_size)
     up, table = lax.optimization_barrier((up, table))
-    first = [held(0, items), held(1, up), held(-1, down)]
+    straight = held(far, to_opposite(items, loop_size), 0)
+    first = [held(0, items), held(1, up), held(-1, down), straight]
     second = [held(2, to_next(up, 1, loop_size)), held(-2, to_next(down, -1, loop_size))]
     gradient, parts, opposite, packed = add_pieces(
         first, [0, 1, 2], loop_size, table, users, labels, None, False
@@ -264,9 +273,9 @@
     third = [held(3, to_next(second[0][0], 1, loop_size)), held(-3, to_next(second[1][0], -1, loop_size))]
     gradient, packed = add_pieces(second, [0, 1], loop_size, table, parts, labels, gradient, False)
     second = other(packed, [2, -2])
-    third.append(held(4, opposite))
+    third.append(held(far, opposite, 1))
     arrived, gradient = lax.optimization_barrier(([array for array, _ in third], gradient))
-    final = other(pack(arrived), [3, -3, 4])
+    final = other(pack([*arrived, straight[0]]), [3, -3, far])
     (gradient,) = add_pieces(
         third + [first, second], [], loop_size, table, parts, labels, gradient, False
     )

time: 35.4 us -> 36.8 us (1.040)
  starting transfers between devices: 9.29 us -> 14.3 us
  Pallas kernels: 4.96 us -> 2.5 us
  waiting for transfers between devices: 8.33 us -> 6.6 us
  blocking collectives: 11.1 us -> 11.5 us
    ppermute x1, starting transfers between devices: 2.48 us -> 5.78 us  [across(): return lax.ppermute(array, 'loop', pairs)]
    pallas_call x4, Pallas kernels: 3.85 us -> 1.39 us  [add_pieces(): pl.pallas_call(functools.partial(pieces_kernel, places, len(arrays), pack...]
    ppermute x1, waiting for transfers between devices: 1.45 us -> 0.01 us  [across(): return lax.ppermute(array, 'loop', pairs)]
    ppermute x6, waiting for transfers between devices: 6.16 us -> 5.17 us  [to_next(): return lax.ppermute(array, 'loop', pairs)]
    ppermute x6, starting transfers between devices: 6.66 us -> 7.52 us  [to_next(): return lax.ppermute(array, 'loop', pairs)]
    ppermute x3, waiting for transfers between devices: 0.72 us -> 1.43 us  [to_other_core(): lax.ppermute(array, 'loop', [(at, at ^ 1) for at in range(loop_size)])]
    ppermute x0 -> x1, starting transfers between devices: none -> 0.66 us  [to_opposite(): lax.ppermute(array, 'loop', [(device(at, 1), device(at + chips // 2, 1))...]
    all_to_all x1, blocking collectives: 11.1 us -> 11.5 us  [local(): squares = lax.all_to_all(square, 'loop', 0, 0, tiled=True)]
  transfers between devices with their start and end apart: 10 -> 11, of which waited for: 7 -> 3; matrix products, arithmetic and copies ran while one was open for 0% -> 0% of each run, Pallas kernels for 9% -> 4%
where the time goes in v20:
time: 36.8 us; the launch traced here: 36.3 us
  starting transfers between devices  14.3 us (39%)
  blocking collectives  11.5 us (31%)
  waiting for transfers between devices  6.6 us (18%)
  Pallas kernels  2.5 us (7%)
  between operations  0.76 us (2%)
  local copies, waits for them, and re-layouts  0.66 us (2%)
    all_to_all x1, blocking collectives, local(): squares = lax.all_to_all(square, 'loop', 0, 0, tiled=True)  11.5 us
    ppermute x6, starting transfers between devices, to_next(): return lax.ppermute(array, 'loop', pairs)  7.52 us
    ppermute x1, starting transfers between devices, across(): return lax.ppermute(array, 'loop', pairs)  5.78 us
    ppermute x6, waiting for transfers between devices, to_next(): return lax.ppermute(array, 'loop', pairs)  5.17 us
    ppermute x3, waiting for transfers between devices, to_other_core(): lax.ppermute(array, 'loop', [(at, at ^ 1) for at in range(loop_size)])  1.43 us
    pallas_call x4, Pallas kernels, add_pieces(): pl.pallas_call(functools.partial(pieces_kernel, places, len(arrays), pack...  1.39 us
    pallas_call x1, Pallas kernels, local(): pl.pallas_call(functools.partial(update_kernel, rows * loop_size * width)...  0.93 us
  transfers between devices with their start and end apart: 11, of which 3 were waited for; matrix products, arithmetic and copies ran while one was open for 0% of the time, Pallas kernels for 4%

profile of v20, /device:TPU:0, one launch (start us, length us, event | category | flops | bytes accessed | tf_op | source)
XLA Modules:
  0.0 36.3 jit_solution(7129683375931057396)
XLA Ops:
  0.0 3.0 %collective-permute-start = (bf16[128,512]{1,0:T(8,128)(2,1)}, bf16[128,512]{1,0:T(8,128)(2,1)S(1)}, u32[]{:S(2)}, u32[]{:S(2)}) collective-permute-start(bf16[128,512]{1,0:T(8,128)(2,1)} %rest_0_.1), channel_id=1, source_target_pairs={{0,4},{4,8},{8,12},{12,14},{14,10},{10,6},{6,2},{2,0},{1,3},{5,1},... | collective-permute-start | bytes 393224 | tf_op jit(solution)/shard_map/ppermute | solution.py:29
  3.0 0.0 collective-permute-start.1
  3.0 0.7 %collective-permute-start.2 = (bf16[128,512]{1,0:T(8,128)(2,1)}, bf16[128,512]{1,0:T(8,128)(2,1)S(1)}, u32[]{:S(2)}, u32[]{:S(2)}) collective-permute-start(bf16[128,512]{1,0:T(8,128)(2,1)} %rest_0_.1), channel_id=1, source_target_pairs={{1,15},{5,11},{9,7},{13,3},{15,1},{11,5},{7,9},{3,13},{17,31},{21,... | collective-permute-start | bytes 393224 | tf_op jit(solution)/shard_map/ppermute | solution.py:40
  4.3 0.0 copy-start.3
  4.3 0.6 %copy-done.3 = s32[1,8]{1,0:T(1,128)S(1)} copy-done((s32[1,8]{1,0:T(1,128)S(1)}, s32[1,8]{1,0:T(1,128)}, u32[]{:S(2)}) %copy-start.3) | copy-done | bytes 56
  5.0 0.0 copy-start
  5.0 0.0 copy-start.1
  5.0 0.0 copy-start.2
  5.0 0.1 slot_table.1.table_ref
  5.2 1.8 %collective-permute-done.rest_1_ = bf16[128,512]{1,0:T(8,128)(2,1)S(1)} collective-permute-done((bf16[128,512]{1,0:T(8,128)(2,1)}, bf16[128,512]{1,0:T(8,128)(2,1)S(1)}, u32[]{:S(2)}, u32[]{:S(2)}) %collective-permute-start) | collective-permute-done | bytes 131104 | tf_op jit(solution)/shard_map/ppermute | solution.py:29
  7.0 1.5 %collective-permute-start.3 = (bf16[128,512]{1,0:T(8,128)(2,1)S(1)}, bf16[128,512]{1,0:T(8,128)(2,1)S(1)}, u32[]{:S(2)}, u32[]{:S(2)}) collective-permute-start(bf16[128,512]{1,0:T(8,128)(2,1)S(1)} %collective-permute-done.rest_1_), channel_id=1, source_target_pairs={{0,4},{4,8},{8,12},{12,14},{14,10},{10,6},{6,2},{2,0},{1,3},{5,1},... | collective-permute-start | bytes 393224 | tf_op jit(solution)/shard_map/ppermute | solution.py:29
  8.5 0.0 collective-permute-done.1.rest_2_
  8.5 0.9 %collective-permute-start.5 = (bf16[128,512]{1,0:T(8,128)(2,1)S(1)}, bf16[128,512]{1,0:T(8,128)(2,1)S(1)}, u32[]{:S(2)}, u32[]{:S(2)}) collective-permute-start(bf16[128,512]{1,0:T(8,128)(2,1)S(1)} %collective-permute-done.1.rest_2_), channel_id=1, source_target_pairs={{0,2},{4,0},{8,4},{12,8},{14,12},{10,14},{6,10},{2,6},{1,5},{5,9},... | collective-permute-start | bytes 393224 | tf_op jit(solution)/shard_map/ppermute | solution.py:29
  9.4 0.0 collective-permute-done.2.rest_3_.refs_3_
  9.4 0.0 copy-done
  9.4 0.0 copy-done.1
  9.4 0.0 copy-done.2
  9.4 0.3 add_pieces.4
  9.7 5.8 %collective-permute-start.7 = (bf16[128,512]{1,0:T(8,128)(2,1)S(1)}, bf16[128,512]{1,0:T(8,128)(2,1)S(1)}, u32[]{:S(2)}, u32[]{:S(2)}) collective-permute-start(bf16[128,512]{1,0:T(8,128)(2,1)S(1)} %get-tuple-element.22), channel_id=1, source_target_pairs={{0,12},{4,6},{8,10},{12,0},{14,2},{10,8},{6,4},{2,14},{16,28},{20,... | collective-permute-start | bytes 393224 | tf_op jit(solution)/shard_map/ppermute | solution.py:35
  15.5 0.1 collective-permute-start.9
  15.6 0.0 collective-permute-done.3.rest_0_
  15.6 0.3 collective-permute-start.4
  16.0 0.0 collective-permute-done.5.rest_1_
  16.0 1.7 %collective-permute-start.6 = (bf16[128,512]{1,0:T(8,128)(2,1)S(1)}, bf16[128,512]{1,0:T(8,128)(2,1)S(1)}, u32[]{:S(2)}, u32[]{:S(2)}) collective-permute-start(bf16[128,512]{1,0:T(8,128)(2,1)S(1)} %collective-permute-done.5.rest_1_), channel_id=1, source_target_pairs={{0,2},{4,0},{8,4},{12,8},{14,12},{10,14},{6,10},{2,6},{1,5},{5,9},... | collective-permute-start | bytes 393224 | tf_op jit(solution)/shard_map/ppermute | solution.py:29
  17.7 0.7 %add_pieces.5 = (f32[256,512]{1,0:T(8,128)S(1)}, bf16[256,512]{1,0:T(8,128)(2,1)S(1)}) custom-call(s32[1,128]{1,0:T(1,128)S(1)} %slot_table.1.table_ref, bf16[512,512]{1,0:T(8,128)(2,1)S(1)} %get-tuple-element.21.given_ref, s32[256,1024]{1,0:T(8,128)S(1)} %copy-done.1, ...), custom_call_target="tpu_custom_call", output_to_operand_aliasing={{0}: (5, {})} | custom-call | flops 4294967296 | bytes 1048576 | tf_op jit(solution)/shard_map/add_pieces/pallas_call | solution.py:228
  18.4 0.1 collective-permute-start.10
  18.5 0.0 collective-permute-done.7.refs_2_.rest_2_
  18.5 3.3 %collective-permute-done.4.refs_0_.rest_0_ = bf16[128,512]{1,0:T(8,128)(2,1)S(1)} collective-permute-done((bf16[128,512]{1,0:T(8,128)(2,1)S(1)}, bf16[128,512]{1,0:T(8,128)(2,1)S(1)}, u32[]{:S(2)}, u32[]{:S(2)}) %collective-permute-start.4) | collective-permute-done | bytes 131104 | tf_op jit(solution)/shard_map/ppermute | solution.py:29
  21.8 0.0 collective-permute-done.6.refs_1_.rest_1_
  21.9 0.2 collective-permute-start.8
  22.0 0.0 collective-permute-done.10.rest_4_
  22.1 0.0 collective-permute-done.9.rest_3_
  22.1 0.2 add_pieces.6.rest_1_
  22.2 1.4 %collective-permute-done.8.rest_0_ = bf16[384,512]{1,0:T(8,128)(2,1)S(1)} collective-permute-done((bf16[384,512]{1,0:T(8,128)(2,1)S(1)}, bf16[384,512]{1,0:T(8,128)(2,1)S(1)}, u32[]{:S(2)}, u32[]{:S(2)}) %collective-permute-start.8) | collective-permute-done | bytes 393248 | tf_op jit(solution)/shard_map/ppermute | solution.py:44
  23.7 0.2 add_pieces.7
  23.9 11.5 %all_to_all.11 = f32[16,1,128]{2,1,0:T(1,128)S(1)} all-to-all(f32[16,1,128]{2,1,0:T(1,128)S(1)} %bitcast.7), channel_id=1, replica_groups=mesh['group'=2,'loop'=16] {'loop'}, dimensions={0} | all-to-all | bytes 16384 | tf_op jit(solution)/shard_map/all_to_all | solution.py:381
  35.4 0.9 %update.1 = f32[256,512]{1,0:T(8,128)} custom-call(f32[256,512]{1,0:T(8,128)S(1)} %copy-done, f32[256,512]{1,0:T(8,128)S(1)} %get-tuple-element.31.grad_ref, f32[16,128]{1,0:T(8,128)S(1)} %bitcast.6), custom_call_target="tpu_custom_call" | custom-call | flops 262144 | bytes 1572864 | tf_op jit(solution)/shard_map/update/pallas_call | solution.py:382
  (1 shorter events, 0.0 us)
Async XLA Ops:
  0.0 7.0 %collective-permute-start = (bf16[128,512]{1,0:T(8,128)(2,1)}, bf16[128,512]{1,0:T(8,128)(2,1)S(1)}, u32[]{:S(2)}, u32[]{:S(2)}) collective-permute-start(bf16[128,512]{1,0:T(8,128)(2,1)} %rest_0_.1), channel_id=1, source_target_pairs={{0,4},{4,8},{8,12},{12,14},{14,10},{10,6},{6,2},{2,0},{1,3},{5,1},... | collective-permute-start | bytes 393224 | tf_op jit(solution)/shard_map/ppermute | solution.py:29
  3.0 5.5 %collective-permute-start.1 = (bf16[128,512]{1,0:T(8,128)(2,1)}, bf16[128,512]{1,0:T(8,128)(2,1)S(1)}, u32[]{:S(2)}, u32[]{:S(2)}) collective-permute-start(bf16[128,512]{1,0:T(8,128)(2,1)} %rest_0_.1), channel_id=1, source_target_pairs={{0,2},{4,0},{8,4},{12,8},{14,12},{10,14},{6,10},{2,6},{1,5},{5,9},... | collective-permute-start | bytes 393224 | tf_op jit(solution)/shard_map/ppermute | solution.py:29
  3.0 6.4 %collective-permute-start.2 = (bf16[128,512]{1,0:T(8,128)(2,1)}, bf16[128,512]{1,0:T(8,128)(2,1)S(1)}, u32[]{:S(2)}, u32[]{:S(2)}) collective-permute-start(bf16[128,512]{1,0:T(8,128)(2,1)} %rest_0_.1), channel_id=1, source_target_pairs={{1,15},{5,11},{9,7},{13,3},{15,1},{11,5},{7,9},{3,13},{17,31},{21,... | collective-permute-start | bytes 393224 | tf_op jit(solution)/shard_map/ppermute | solution.py:40
  4.3 0.7 %copy-start.3 = (s32[1,8]{1,0:T(1,128)S(1)}, s32[1,8]{1,0:T(1,128)}, u32[]{:S(2)}) copy-start(s32[1,8]{1,0:T(1,128)} %list_ref.1) | copy-start | bytes 100
  5.0 4.4 %copy-start = (f32[256,512]{1,0:T(8,128)S(1)}, f32[256,512]{1,0:T(8,128)}, u32[]{:S(2)}) copy-start(f32[256,512]{1,0:T(8,128)} %users_ref.1) | copy-start | bytes 1572868
  5.0 4.4 %copy-start.1 = (s32[256,1024]{1,0:T(8,128)S(1)}, s32[256,1024]{1,0:T(8,128)}, u32[]{:S(2)}) copy-start(s32[256,1024]{1,0:T(8,128)} %labels_ref.7) | copy-start | bytes 3145732
  5.0 4.4 %copy-start.2 = (bf16[128,512]{1,0:T(8,128)(2,1)S(1)}, bf16[128,512]{1,0:T(8,128)(2,1)}, u32[]{:S(2)}) copy-start(bf16[128,512]{1,0:T(8,128)(2,1)} %rest_0_.1) | copy-start | bytes 393220
  7.0 8.6 %collective-permute-start.3 = (bf16[128,512]{1,0:T(8,128)(2,1)S(1)}, bf16[128,512]{1,0:T(8,128)(2,1)S(1)}, u32[]{:S(2)}, u32[]{:S(2)}) collective-permute-start(bf16[128,512]{1,0:T(8,128)(2,1)S(1)} %collective-permute-done.rest_1_), channel_id=1, source_target_pairs={{0,4},{4,8},{8,12},{12,14},{14,10},{10,6},{6,2},{2,0},{1,3},{5,1},... | collective-permute-start | bytes 393224 | tf_op jit(solution)/shard_map/ppermute | solution.py:29
  8.5 7.5 %collective-permute-start.5 = (bf16[128,512]{1,0:T(8,128)(2,1)S(1)}, bf16[128,512]{1,0:T(8,128)(2,1)S(1)}, u32[]{:S(2)}, u32[]{:S(2)}) collective-permute-start(bf16[128,512]{1,0:T(8,128)(2,1)S(1)} %collective-permute-done.1.rest_2_), channel_id=1, source_target_pairs={{0,2},{4,0},{8,4},{12,8},{14,12},{10,14},{6,10},{2,6},{1,5},{5,9},... | collective-permute-start | bytes 393224 | tf_op jit(solution)/shard_map/ppermute | solution.py:29
  9.7 8.8 %collective-permute-start.7 = (bf16[128,512]{1,0:T(8,128)(2,1)S(1)}, bf16[128,512]{1,0:T(8,128)(2,1)S(1)}, u32[]{:S(2)}, u32[]{:S(2)}) collective-permute-start(bf16[128,512]{1,0:T(8,128)(2,1)S(1)} %get-tuple-element.22), channel_id=1, source_target_pairs={{0,12},{4,6},{8,10},{12,0},{14,2},{10,8},{6,4},{2,14},{16,28},{20,... | collective-permute-start | bytes 393224 | tf_op jit(solution)/shard_map/ppermute | solution.py:35
  15.5 6.5 %collective-permute-start.9 = (bf16[384,512]{1,0:T(8,128)(2,1)S(1)}, bf16[384,512]{1,0:T(8,128)(2,1)S(1)}, u32[]{:S(2)}, u32[]{:S(2)}) collective-permute-start(bf16[384,512]{1,0:T(8,128)(2,1)S(1)} %get-tuple-element.28), channel_id=1, source_target_pairs={{0,1},{1,0},{2,3},{3,2},{4,5},{5,4},{6,7},{7,6},{8,9},{9,8},{10,11... | collective-permute-start | bytes 1179656 | tf_op jit(solution)/shard_map/ppermute | solution.py:44
  15.6 6.2 %collective-permute-start.4 = (bf16[128,512]{1,0:T(8,128)(2,1)S(1)}, bf16[128,512]{1,0:T(8,128)(2,1)S(1)}, u32[]{:S(2)}, u32[]{:S(2)}) collective-permute-start(bf16[128,512]{1,0:T(8,128)(2,1)S(1)} %collective-permute-done.3.rest_0_), channel_id=1, source_target_pairs={{0,4},{4,8},{8,12},{12,14},{14,10},{10,6},{6,2},{2,0},{1,3},{5,1},... | collective-permute-start | bytes 393224 | tf_op jit(solution)/shard_map/ppermute | solution.py:29
  16.0 5.9 %collective-permute-start.6 = (bf16[128,512]{1,0:T(8,128)(2,1)S(1)}, bf16[128,512]{1,0:T(8,128)(2,1)S(1)}, u32[]{:S(2)}, u32[]{:S(2)}) collective-permute-start(bf16[128,512]{1,0:T(8,128)(2,1)S(1)} %collective-permute-done.5.rest_1_), channel_id=1, source_target_pairs={{0,2},{4,0},{8,4},{12,8},{14,12},{10,14},{6,10},{2,6},{1,5},{5,9},... | collective-permute-start | bytes 393224 | tf_op jit(solution)/shard_map/ppermute | solution.py:29
  18.4 3.6 %collective-permute-start.10 = (bf16[256,512]{1,0:T(8,128)(2,1)S(1)}, bf16[256,512]{1,0:T(8,128)(2,1)S(1)}, u32[]{:S(2)}, u32[]{:S(2)}) collective-permute-start(bf16[256,512]{1,0:T(8,128)(2,1)S(1)} %get-tuple-element.29), channel_id=1, source_target_pairs={{0,1},{1,0},{2,3},{3,2},{4,5},{5,4},{6,7},{7,6},{8,9},{9,8},{10,11... | collective-permute-start | bytes 786440 | tf_op jit(solution)/shard_map/ppermute | solution.py:44
  21.9 1.8 %collective-permute-start.8 = (bf16[384,512]{1,0:T(8,128)(2,1)S(1)}, bf16[384,512]{1,0:T(8,128)(2,1)S(1)}, u32[]{:S(2)}, u32[]{:S(2)}) collective-permute-start(bf16[384,512]{1,0:T(8,128)(2,1)S(1)} %pack.1), channel_id=1, source_target_pairs={{0,1},{1,0},{2,3},{3,2},{4,5},{5,4},{6,7},{7,6},{8,9},{9,8},{10,11... | collective-permute-start | bytes 1179656 | tf_op jit(solution)/shard_map/ppermute | solution.py:44

commit v21 on v16

--- a/solution.py
+++ b/solution.py
@@ -39,6 +39,16 @@
     return lax.ppermute(array, "loop", pairs)
 
 
+def to_pair(array, loop_size):
+    chips, device = ring_place(loop_size)
+    pairs = [
+        (device(at, core), device(at + (1 if at % 2 else -1), core))
+        for at in range(chips)
+        for core in range(2)
+    ]
+    return lax.ppermute(array, "loop", pairs)
+
+
 def to_other_core(array, loop_size):
     return lax.ppermute(array, "loop", [(at, at ^ 1) for at in range(loop_size)])
 
@@ -52,11 +62,13 @@
     chips = loop_size // 2
     lane = lax.broadcasted_iota(jnp.int32, table_ref.shape, 1)
     core, position = core_and_position(loop_size)
-    hops, other = jnp.zeros_like(lane), jnp.zeros_like(lane)
+    hops, skips, other = jnp.zeros_like(lane), jnp.zeros_like(lane), jnp.zeros_like(lane)
     for at, origin in enumerate(origins):
         hops = jnp.where(lane == at, origin[0], hops)
-        other = jnp.where(lane == at, origin[1], other)
-    at = (position + chips + jnp.where(core == 0, -hops, hops)) & (chips - 1)
+        skips = jnp.where(lane == at, origin[1], skips)
+        other = jnp.where(lane == at, origin[2], other)
+    hops = jnp.where(core == 0, -hops, hops) + jnp.where(position % 2 == 0, skips, -skips)
+    at = (position + chips + hops) & (chips - 1)
     chip = jnp.where(at < chips // 2, 2 * at, 2 * (chips - 1 - at) + 1)
     block = 2 * chip + jnp.where(other == 1, 1 - core, core)
     found = jnp.full_like(lane, -1)
@@ -133,6 +145,29 @@
     return core, jnp.where(row == 0, outer, loop_size // 2 - 1 - outer)
 
 
+def pick_kernel(loop_size, upper_ref, lower_ref, picked_ref):
+    core, position = core_and_position(loop_size)
+    for at, ref in enumerate((lower_ref, upper_ref)):
+
+        @pl.when((core + position) % 2 == at)
+        def _():
+            picked_ref[...] = ref[...]
+
+
+def pick(upper, lower, loop_size):
+    return pl.pallas_call(
+        functools.partial(pick_kernel, loop_size),
+        out_shape=jax.ShapeDtypeStruct(upper.shape, upper.dtype),
+        in_specs=[pl.BlockSpec(memory_space=pltpu.VMEM)] * 2,
+        out_specs=pl.BlockSpec(memory_space=pltpu.VMEM),
+        compiler_params=pltpu.CompilerParams(vmem_limit_bytes=16 * 1024 * 1024),
+        cost_estimate=pl.CostEstimate(
+            flops=0, bytes_accessed=4 * upper.size, transcendentals=0
+        ),
+        name="pick",
+    )(upper, lower)
+
+
 def pack_kernel(*refs):
     tile = refs[0].shape[0]
     for at, ref in enumerate(refs[:-1]):
@@ -239,34 +274,33 @@
 
 def ring_gradient(users, items, lists, labels):
     loop_size = lax.axis_size("loop")
-    far = loop_size // 4
-    origins = [(hops, 0) for hops in range(1 - far, far + 1)]
-    origins += [(-hops, 1) for hops, _ in origins]
+    near = [(0, 0), (1, 0), (-1, 0), (0, 3), (2, 0), (-2, 0), (0, -3), (4, 0)]
+    origins = [(hops, skips, 0) for hops, skips in near] + [(-hops, skips, 1) for hops, skips in near]
     table = slot_table(loop_size, origins, *lists)
-    where = {origin: at for at, origin in enumerate(origins)}
-
-    def held(hops, array):
-        return array, [where[hops, 0]]
-
-    def other(arrays, hops):
-        return to_other_core(arrays, loop_size), [where[-hop, 1] for hop in hops]
+
+    def held(array, origin):
+        return array, [near.index(origin)]
+
+    def other(array, some):
+        return to_other_core(array, loop_size), [len(near) + near.index(origin) for origin in some]
 
     up = to_next(items, 1, loop_size)
     down = to_next(items, -1, loop_size)
     up, table = lax.optimization_barrier((up, table))
-    first = [held(0, items), held(1, up), held(-1, down)]
-    second = [held(2, to_next(up, 1, loop_size)), held(-2, to_next(down, -1, loop_size))]
+    first = [held(items, (0, 0)), held(up, (1, 0)), held(down, (-1, 0))]
+    first.append(held(across(items, loop_size), (0, 3)))
+    up, down = to_next(up, 1, loop_size), to_next(down, -1, loop_size)
+    second = [held(up, (2, 0)), held(down, (-2, 0))]
     gradient, parts, opposite, packed = add_pieces(
-        first, [0, 1, 2], loop_size, table, users, labels, None, False
+        first, [0, 1, 2, 3], loop_size, table, users, labels, None, False
     )
-    opposite = across(opposite, loop_size)
-    first = other(packed, [0, 1, -1])
-    third = [held(3, to_next(second[0][0], 1, loop_size)), held(-3, to_next(second[1][0], -1, loop_size))]
+    third = [held(across(opposite, loop_size), (4, 0))]
+    first = other(packed, near[:4])
+    third.append(held(to_pair(pick(up, down, loop_size), loop_size), (0, -3)))
     gradient, packed = add_pieces(second, [0, 1], loop_size, table, parts, labels, gradient, False)
-    second = other(packed, [2, -2])
-    third.append(held(4, opposite))
+    second = other(packed, near[4:6])
     arrived, gradient = lax.optimization_barrier(([array for array, _ in third], gradient))
-    final = other(pack(arrived), [3, -3, 4])
+    final = other(pack(arrived), [(4, 0), (0, -3)])
     (gradient,) = add_pieces(
         third + [first, second], [], loop_size, table, parts, labels, gradient, False
     )

time: 35.4 us -> 36.2 us (1.023)
  waiting for transfers between devices: 8.33 us -> 9.71 us
  blocking collectives: 11.1 us -> 10.7 us
    ppermute x1 -> x2, waiting for transfers between devices: 1.45 us -> 5.51 us  [across(): return lax.ppermute(array, 'loop', pairs)]
    ppermute x6 -> x4, waiting for transfers between devices: 6.16 us -> 2.69 us  [to_next(): return lax.ppermute(array, 'loop', pairs)]
    ppermute x1 -> x2, starting transfers between devices: 2.48 us -> 5.21 us  [across(): return lax.ppermute(array, 'loop', pairs)]
    ppermute x6 -> x4, starting transfers between devices: 6.66 us -> 4.1 us  [to_next(): return lax.ppermute(array, 'loop', pairs)]
    ppermute x0 -> x1, waiting for transfers between devices: none -> 1.07 us  [to_pair(): return lax.ppermute(array, 'loop', pairs)]
    all_to_all x1, blocking collectives: 11.1 us -> 10.7 us  [local(): squares = lax.all_to_all(square, 'loop', 0, 0, tiled=True)]
  transfers between devices with their start and end apart: 10 -> 10, of which waited for: 7 -> 6; matrix products, arithmetic and copies ran while one was open for 0% -> 0% of each run, Pallas kernels for 9% -> 8%
where the time goes in v21:
time: 36.2 us
  blocking collectives  10.7 us (30%)
  waiting for transfers between devices  9.71 us (27%)
  starting transfers between devices  9.61 us (27%)
  Pallas kernels  4.75 us (13%)
  between operations  0.76 us (2%)
  local copies, waits for them, and re-layouts  0.66 us (2%)
    all_to_all x1, blocking collectives, local(): squares = lax.all_to_all(square, 'loop', 0, 0, tiled=True)  10.7 us
    ppermute x2, waiting for transfers between devices, across(): return lax.ppermute(array, 'loop', pairs)  5.51 us
    ppermute x2, starting transfers between devices, across(): return lax.ppermute(array, 'loop', pairs)  5.21 us
    ppermute x4, starting transfers between devices, to_next(): return lax.ppermute(array, 'loop', pairs)  4.1 us
    pallas_call x4, Pallas kernels, add_pieces(): pl.pallas_call(functools.partial(pieces_kernel, places, len(arrays), pack...  3.64 us
    ppermute x4, waiting for transfers between devices, to_next(): return lax.ppermute(array, 'loop', pairs)  2.69 us
    ppermute x1, waiting for transfers between devices, to_pair(): return lax.ppermute(array, 'loop', pairs)  1.07 us
    pallas_call x1, Pallas kernels, local(): pl.pallas_call(functools.partial(update_kernel, rows * loop_size * width)...  0.93 us
  transfers between devices with their start and end apart: 10, of which 6 were waited for; matrix products, arithmetic and copies ran while one was open for 0% of the time, Pallas kernels for 8%

profile of v21, /device:TPU:0, one launch (start us, length us, event | category | flops | bytes accessed | tf_op | source)
XLA Modules:
  0.0 36.2 jit_solution(3097602595971580253)
XLA Ops:
  0.0 3.0 %collective-permute-start = (bf16[128,512]{1,0:T(8,128)(2,1)}, bf16[128,512]{1,0:T(8,128)(2,1)S(1)}, u32[]{:S(2)}, u32[]{:S(2)}) collective-permute-start(bf16[128,512]{1,0:T(8,128)(2,1)} %rest_0_.1), channel_id=1, source_target_pairs={{0,4},{4,8},{8,12},{12,14},{14,10},{10,6},{6,2},{2,0},{1,3},{5,1},... | collective-permute-start | bytes 393224 | tf_op jit(solution)/shard_map/ppermute | solution.py:29
  3.0 0.0 collective-permute-start.1
  3.0 4.0 %collective-permute-start.2 = (bf16[128,512]{1,0:T(8,128)(2,1)}, bf16[128,512]{1,0:T(8,128)(2,1)S(1)}, u32[]{:S(2)}, u32[]{:S(2)}) collective-permute-start(bf16[128,512]{1,0:T(8,128)(2,1)} %rest_0_.1), channel_id=1, source_target_pairs={{0,12},{1,13},{4,6},{5,7},{8,10},{9,11},{12,0},{13,1},{14,2},{15,3... | collective-permute-start | bytes 393224 | tf_op jit(solution)/shard_map/ppermute | solution.py:39
  7.7 0.0 copy-start.3
  7.7 0.6 %copy-done.3 = s32[1,8]{1,0:T(1,128)S(1)} copy-done((s32[1,8]{1,0:T(1,128)S(1)}, s32[1,8]{1,0:T(1,128)}, u32[]{:S(2)}) %copy-start.3) | copy-done | bytes 56
  8.4 0.0 copy-start
  8.4 0.0 copy-start.1
  8.4 0.0 copy-start.2
  8.4 0.1 slot_table.1.table_ref
  8.5 0.0 collective-permute-done.rest_1_
  8.5 0.1 collective-permute-start.4
  8.6 1.0 %collective-permute-done.1.rest_2_ = bf16[128,512]{1,0:T(8,128)(2,1)S(1)} collective-permute-done((bf16[128,512]{1,0:T(8,128)(2,1)}, bf16[128,512]{1,0:T(8,128)(2,1)S(1)}, u32[]{:S(2)}, u32[]{:S(2)}) %collective-permute-start.1) | collective-permute-done | bytes 131104 | tf_op jit(solution)/shard_map/ppermute | solution.py:29
  9.6 1.0 %collective-permute-start.5 = (bf16[128,512]{1,0:T(8,128)(2,1)S(1)}, bf16[128,512]{1,0:T(8,128)(2,1)S(1)}, u32[]{:S(2)}, u32[]{:S(2)}) collective-permute-start(bf16[128,512]{1,0:T(8,128)(2,1)S(1)} %collective-permute-done.1.rest_2_), channel_id=1, source_target_pairs={{0,2},{4,0},{8,4},{12,8},{14,12},{10,14},{6,10},{2,6},{1,5},{5,9},... | collective-permute-start | bytes 393224 | tf_op jit(solution)/shard_map/ppermute | solution.py:29
  10.6 2.5 %collective-permute-done.2.rest_3_ = bf16[128,512]{1,0:T(8,128)(2,1)S(1)} collective-permute-done((bf16[128,512]{1,0:T(8,128)(2,1)}, bf16[128,512]{1,0:T(8,128)(2,1)S(1)}, u32[]{:S(2)}, u32[]{:S(2)}) %collective-permute-start.2) | collective-permute-done | bytes 131104 | tf_op jit(solution)/shard_map/ppermute | solution.py:39
  13.1 0.0 copy-done
  13.1 0.0 copy-done.1
  13.1 0.0 copy-done.2
  13.1 1.1 %add_pieces.4 = (f32[256,512]{1,0:T(8,128)S(1)}, bf16[512,512]{1,0:T(8,128)(2,1)S(1)}, bf16[128,512]{1,0:T(8,128)(2,1)S(1)}, bf16[512,512]{1,0:T(8,128)(2,1)S(1)}) custom-call(s32[1,128]{1,0:T(1,128)S(1)} %slot_table.1.table_ref, f32[256,512]{1,0:T(8,128)S(1)} %copy-done, s32[256,1024]{1,0:T(8,128)S(1)} %copy-done.1, bf16[128,512]{1,0:T(8,128)(2,1)S(1)} %copy-done.2, ...), custom_call_target="tpu_custom_call" | custom-call | flops 8589934592 | bytes 1048576 | tf_op jit(solution)/shard_map/add_pieces/pallas_call | solution.py:255
  14.3 1.2 %collective-permute-start.3 = (bf16[128,512]{1,0:T(8,128)(2,1)S(1)}, bf16[128,512]{1,0:T(8,128)(2,1)S(1)}, u32[]{:S(2)}, u32[]{:S(2)}) collective-permute-start(bf16[128,512]{1,0:T(8,128)(2,1)S(1)} %get-tuple-element.21), channel_id=1, source_target_pairs={{0,12},{1,13},{4,6},{5,7},{8,10},{9,11},{12,0},{13,1},{14,2},{15,3... | collective-permute-start | bytes 393224 | tf_op jit(solution)/shard_map/ppermute | solution.py:39
  15.4 0.0 collective-permute-start.8
  15.4 0.0 collective-permute-done.4.upper_ref.rest_0_
  15.4 1.7 %collective-permute-done.5.lower_ref.rest_1_ = bf16[128,512]{1,0:T(8,128)(2,1)S(1)} collective-permute-done((bf16[128,512]{1,0:T(8,128)(2,1)S(1)}, bf16[128,512]{1,0:T(8,128)(2,1)S(1)}, u32[]{:S(2)}, u32[]{:S(2)}) %collective-permute-start.5) | collective-permute-done | bytes 131104 | tf_op jit(solution)/shard_map/ppermute | solution.py:29
  17.1 0.2 collective-permute-start.6
  17.3 0.7 %add_pieces.5 = (f32[256,512]{1,0:T(8,128)S(1)}, bf16[256,512]{1,0:T(8,128)(2,1)S(1)}) custom-call(s32[1,128]{1,0:T(1,128)S(1)} %slot_table.1.table_ref, bf16[512,512]{1,0:T(8,128)(2,1)S(1)} %get-tuple-element.20.given_ref, s32[256,1024]{1,0:T(8,128)S(1)} %copy-done.1, ...), custom_call_target="tpu_custom_call", output_to_operand_aliasing={{0}: (5, {})} | custom-call | flops 4294967296 | bytes 1048576 | tf_op jit(solution)/shard_map/add_pieces/pallas_call | solution.py:255
  18.0 0.1 collective-permute-start.9
  18.1 3.0 %collective-permute-done.3.refs_0_.rest_0_ = bf16[128,512]{1,0:T(8,128)(2,1)S(1)} collective-permute-done((bf16[128,512]{1,0:T(8,128)(2,1)S(1)}, bf16[128,512]{1,0:T(8,128)(2,1)S(1)}, u32[]{:S(2)}, u32[]{:S(2)}) %collective-permute-start.3) | collective-permute-done | bytes 131104 | tf_op jit(solution)/shard_map/ppermute | solution.py:39
  21.1 1.1 %collective-permute-done.6.refs_1_.rest_1_ = bf16[128,512]{1,0:T(8,128)(2,1)S(1)} collective-permute-done((bf16[128,512]{1,0:T(8,128)(2,1)S(1)}, bf16[128,512]{1,0:T(8,128)(2,1)S(1)}, u32[]{:S(2)}, u32[]{:S(2)}) %collective-permute-start.6) | collective-permute-done | bytes 131104 | tf_op jit(solution)/shard_map/ppermute | solution.py:49
  22.2 0.1 collective-permute-start.7
  22.3 0.0 collective-permute-done.9.rest_3_
  22.3 0.0 collective-permute-done.8.rest_2_
  22.3 1.1 %add_pieces.6.rest_1_ = f32[256,512]{1,0:T(8,128)S(1)} custom-call(s32[1,128]{1,0:T(1,128)S(1)} %slot_table.1.table_ref, bf16[512,512]{1,0:T(8,128)(2,1)S(1)} %get-tuple-element.20.given_ref, s32[256,1024]{1,0:T(8,128)S(1)} %copy-done.1, bf16[128,512]{1,0:T(8,128)(2,1)S(1)} %collective-permute-done.3.refs_0_.rest_0_, ...), custom_call_target="tpu_custom_call", output_to_operand_aliasing={{}: (7, {})} | custom-call | flops 17179869184 | bytes 1048576 | tf_op jit(solution)/shard_map/add_pieces/pallas_call | solution.py:255
  23.3 0.4 %collective-permute-done.7.rest_0_ = bf16[256,512]{1,0:T(8,128)(2,1)S(1)} collective-permute-done((bf16[256,512]{1,0:T(8,128)(2,1)S(1)}, bf16[256,512]{1,0:T(8,128)(2,1)S(1)}, u32[]{:S(2)}, u32[]{:S(2)}) %collective-permute-start.7) | collective-permute-done | bytes 262176 | tf_op jit(solution)/shard_map/ppermute | solution.py:53
  23.8 0.8 %add_pieces.7 = (f32[256,512]{1,0:T(8,128)S(1)}, f32[16,128]{1,0:T(8,128)S(1)}) custom-call(s32[1,128]{1,0:T(1,128)S(1)} %slot_table.1.table_ref, bf16[512,512]{1,0:T(8,128)(2,1)S(1)} %get-tuple-element.20.given_ref, s32[256,1024]{1,0:T(8,128)S(1)} %copy-done.1, ...), custom_call_target="tpu_custom_call", output_to_operand_aliasing={{0}: (4, {})} | custom-call | flops 4294967296 | bytes 1048576 | tf_op jit(solution)/shard_map/add_pieces/pallas_call | solution.py:255
  24.6 10.7 %all_to_all.11 = f32[16,1,128]{2,1,0:T(1,128)S(1)} all-to-all(f32[16,1,128]{2,1,0:T(1,128)S(1)} %bitcast.7), channel_id=1, replica_groups=mesh['group'=2,'loop'=16] {'loop'}, dimensions={0} | all-to-all | bytes 16384 | tf_op jit(solution)/shard_map/all_to_all | solution.py:406
  35.3 0.9 %update.1 = f32[256,512]{1,0:T(8,128)} custom-call(f32[256,512]{1,0:T(8,128)S(1)} %copy-done, f32[256,512]{1,0:T(8,128)S(1)} %get-tuple-element.29.grad_ref, f32[16,128]{1,0:T(8,128)S(1)} %bitcast.6), custom_call_target="tpu_custom_call" | custom-call | flops 262144 | bytes 1572864 | tf_op jit(solution)/shard_map/update/pallas_call | solution.py:407
  (2 shorter events, 0.0 us)
Async XLA Ops:
  0.0 8.5 %collective-permute-start = (bf16[128,512]{1,0:T(8,128)(2,1)}, bf16[128,512]{1,0:T(8,128)(2,1)S(1)}, u32[]{:S(2)}, u32[]{:S(2)}) collective-permute-start(bf16[128,512]{1,0:T(8,128)(2,1)} %rest_0_.1), channel_id=1, source_target_pairs={{0,4},{4,8},{8,12},{12,14},{14,10},{10,6},{6,2},{2,0},{1,3},{5,1},... | collective-permute-start | bytes 393224 | tf_op jit(solution)/shard_map/ppermute | solution.py:29
  3.0 6.6 %collective-permute-start.1 = (bf16[128,512]{1,0:T(8,128)(2,1)}, bf16[128,512]{1,0:T(8,128)(2,1)S(1)}, u32[]{:S(2)}, u32[]{:S(2)}) collective-permute-start(bf16[128,512]{1,0:T(8,128)(2,1)} %rest_0_.1), channel_id=1, source_target_pairs={{0,2},{4,0},{8,4},{12,8},{14,12},{10,14},{6,10},{2,6},{1,5},{5,9},... | collective-permute-start | bytes 393224 | tf_op jit(solution)/shard_map/ppermute | solution.py:29
  3.0 10.1 %collective-permute-start.2 = (bf16[128,512]{1,0:T(8,128)(2,1)}, bf16[128,512]{1,0:T(8,128)(2,1)S(1)}, u32[]{:S(2)}, u32[]{:S(2)}) collective-permute-start(bf16[128,512]{1,0:T(8,128)(2,1)} %rest_0_.1), channel_id=1, source_target_pairs={{0,12},{1,13},{4,6},{5,7},{8,10},{9,11},{12,0},{13,1},{14,2},{15,3... | collective-permute-start | bytes 393224 | tf_op jit(solution)/shard_map/ppermute | solution.py:39
  7.7 0.7 %copy-start.3 = (s32[1,8]{1,0:T(1,128)S(1)}, s32[1,8]{1,0:T(1,128)}, u32[]{:S(2)}) copy-start(s32[1,8]{1,0:T(1,128)} %list_ref.1) | copy-start | bytes 100
  8.4 4.8 %copy-start = (f32[256,512]{1,0:T(8,128)S(1)}, f32[256,512]{1,0:T(8,128)}, u32[]{:S(2)}) copy-start(f32[256,512]{1,0:T(8,128)} %users_ref.1) | copy-start | bytes 1572868
  8.4 4.8 %copy-start.1 = (s32[256,1024]{1,0:T(8,128)S(1)}, s32[256,1024]{1,0:T(8,128)}, u32[]{:S(2)}) copy-start(s32[256,1024]{1,0:T(8,128)} %labels_ref.7) | copy-start | bytes 3145732
  8.4 4.8 %copy-start.2 = (bf16[128,512]{1,0:T(8,128)(2,1)S(1)}, bf16[128,512]{1,0:T(8,128)(2,1)}, u32[]{:S(2)}) copy-start(bf16[128,512]{1,0:T(8,128)(2,1)} %rest_0_.1) | copy-start | bytes 393220
  8.5 6.9 %collective-permute-start.4 = (bf16[128,512]{1,0:T(8,128)(2,1)S(1)}, bf16[128,512]{1,0:T(8,128)(2,1)S(1)}, u32[]{:S(2)}, u32[]{:S(2)}) collective-permute-start(bf16[128,512]{1,0:T(8,128)(2,1)S(1)} %collective-permute-done.rest_1_), channel_id=1, source_target_pairs={{0,4},{4,8},{8,12},{12,14},{14,10},{10,6},{6,2},{2,0},{1,3},{5,1},... | collective-permute-start | bytes 393224 | tf_op jit(solution)/shard_map/ppermute | solution.py:29
  9.6 7.5 %collective-permute-start.5 = (bf16[128,512]{1,0:T(8,128)(2,1)S(1)}, bf16[128,512]{1,0:T(8,128)(2,1)S(1)}, u32[]{:S(2)}, u32[]{:S(2)}) collective-permute-start(bf16[128,512]{1,0:T(8,128)(2,1)S(1)} %collective-permute-done.1.rest_2_), channel_id=1, source_target_pairs={{0,2},{4,0},{8,4},{12,8},{14,12},{10,14},{6,10},{2,6},{1,5},{5,9},... | collective-permute-start | bytes 393224 | tf_op jit(solution)/shard_map/ppermute | solution.py:29
  14.3 6.8 %collective-permute-start.3 = (bf16[128,512]{1,0:T(8,128)(2,1)S(1)}, bf16[128,512]{1,0:T(8,128)(2,1)S(1)}, u32[]{:S(2)}, u32[]{:S(2)}) collective-permute-start(bf16[128,512]{1,0:T(8,128)(2,1)S(1)} %get-tuple-element.21), channel_id=1, source_target_pairs={{0,12},{1,13},{4,6},{5,7},{8,10},{9,11},{12,0},{13,1},{14,2},{15,3... | collective-permute-start | bytes 393224 | tf_op jit(solution)/shard_map/ppermute | solution.py:39
  15.4 6.9 %collective-permute-start.8 = (bf16[512,512]{1,0:T(8,128)(2,1)S(1)}, bf16[512,512]{1,0:T(8,128)(2,1)S(1)}, u32[]{:S(2)}, u32[]{:S(2)}) collective-permute-start(bf16[512,512]{1,0:T(8,128)(2,1)S(1)} %get-tuple-element.26), channel_id=1, source_target_pairs={{0,1},{1,0},{2,3},{3,2},{4,5},{5,4},{6,7},{7,6},{8,9},{9,8},{10,11... | collective-permute-start | bytes 1572872 | tf_op jit(solution)/shard_map/ppermute | solution.py:53
  17.1 5.0 %collective-permute-start.6 = (bf16[128,512]{1,0:T(8,128)(2,1)S(1)}, bf16[128,512]{1,0:T(8,128)(2,1)S(1)}, u32[]{:S(2)}, u32[]{:S(2)}) collective-permute-start(bf16[128,512]{1,0:T(8,128)(2,1)S(1)} %pick.1), channel_id=1, source_target_pairs={{0,2},{1,3},{4,8},{5,9},{8,4},{9,5},{12,14},{13,15},{14,12},{15,13... | collective-permute-start | bytes 393224 | tf_op jit(solution)/shard_map/ppermute | solution.py:49
  18.0 4.3 %collective-permute-start.9 = (bf16[256,512]{1,0:T(8,128)(2,1)S(1)}, bf16[256,512]{1,0:T(8,128)(2,1)S(1)}, u32[]{:S(2)}, u32[]{:S(2)}) collective-permute-start(bf16[256,512]{1,0:T(8,128)(2,1)S(1)} %get-tuple-element.27), channel_id=1, source_target_pairs={{0,1},{1,0},{2,3},{3,2},{4,5},{5,4},{6,7},{7,6},{8,9},{9,8},{10,11... | collective-permute-start | bytes 786440 | tf_op jit(solution)/shard_map/ppermute | solution.py:53
  22.2 1.6 %collective-permute-start.7 = (bf16[256,512]{1,0:T(8,128)(2,1)S(1)}, bf16[256,512]{1,0:T(8,128)(2,1)S(1)}, u32[]{:S(2)}, u32[]{:S(2)}) collective-permute-start(bf16[256,512]{1,0:T(8,128)(2,1)S(1)} %pack.1), channel_id=1, source_target_pairs={{0,1},{1,0},{2,3},{3,2},{4,5},{5,4},{6,7},{7,6},{8,9},{9,8},{10,11... | collective-permute-start | bytes 786440 | tf_op jit(solution)/shard_map/ppermute | solution.py:53

commit v22 on v21

--- a/solution.py
+++ b/solution.py
@@ -288,17 +288,17 @@
     down = to_next(items, -1, loop_size)
     up, table = lax.optimization_barrier((up, table))
     first = [held(items, (0, 0)), held(up, (1, 0)), held(down, (-1, 0))]
-    first.append(held(across(items, loop_size), (0, 3)))
+    skipped = held(across(items, loop_size), (0, 3))
     up, down = to_next(up, 1, loop_size), to_next(down, -1, loop_size)
-    second = [held(up, (2, 0)), held(down, (-2, 0))]
+    second = [held(up, (2, 0)), held(down, (-2, 0)), skipped]
     gradient, parts, opposite, packed = add_pieces(
-        first, [0, 1, 2, 3], loop_size, table, users, labels, None, False
+        first, [0, 1, 2], loop_size, table, users, labels, None, False
     )
     third = [held(across(opposite, loop_size), (4, 0))]
-    first = other(packed, near[:4])
+    first = other(packed, near[:3])
     third.append(held(to_pair(pick(up, down, loop_size), loop_size), (0, -3)))
-    gradient, packed = add_pieces(second, [0, 1], loop_size, table, parts, labels, gradient, False)
-    second = other(packed, near[4:6])
+    gradient, packed = add_pieces(second, [0, 1, 2], loop_size, table, parts, labels, gradient, False)
+    second = other(packed, [(2, 0), (-2, 0), (0, 3)])
     arrived, gradient = lax.optimization_barrier(([array for array, _ in third], gradient))
     final = other(pack(arrived), [(4, 0), (0, -3)])
     (gradient,) = add_pieces(

time: 36.2 us -> 36.2 us (level)
  waiting for transfers between devices: 9.71 us -> 7.35 us
  starting transfers between devices: 9.61 us -> 11.3 us
  blocking collectives: 10.7 us -> 11.1 us
    ppermute x2, waiting for transfers between devices: 5.51 us -> 0.01 us  [across(): return lax.ppermute(array, 'loop', pairs)]
    ppermute x1, waiting for transfers between devices: 1.07 us -> 3.19 us  [to_pair(): return lax.ppermute(array, 'loop', pairs)]
    ppermute x4, waiting for transfers between devices: 2.69 us -> 4.15 us  [to_next(): return lax.ppermute(array, 'loop', pairs)]
    ppermute x1, starting transfers between devices: 0.15 us -> 1.02 us  [to_pair(): return lax.ppermute(array, 'loop', pairs)]
    ppermute x2, starting transfers between devices: 5.21 us -> 6.03 us  [across(): return lax.ppermute(array, 'loop', pairs)]
    ppermute x3, waiting for transfers between devices: 0.44 us -> 0.01 us  [to_other_core(): lax.ppermute(array, 'loop', [(at, at ^ 1) for at in range(loop_size)])]
    all_to_all x1, blocking collectives: 10.7 us -> 11.1 us  [local(): squares = lax.all_to_all(square, 'loop', 0, 0, tiled=True)]
  transfers between devices with their start and end apart: 10 -> 10, of which waited for: 6 -> 4; matrix products, arithmetic and copies ran while one was open for 0% -> 0% of each run, Pallas kernels for 8% -> 10%
where the time goes in v22:
time: 36.2 us; the launch traced here: 35.9 us
  starting transfers between devices  11.3 us (31%)
  blocking collectives  11.1 us (31%)
  waiting for transfers between devices  7.35 us (20%)
  Pallas kernels  4.73 us (13%)
  between operations  0.77 us (2%)
  local copies, waits for them, and re-layouts  0.66 us (2%)
    all_to_all x1, blocking collectives, local(): squares = lax.all_to_all(square, 'loop', 0, 0, tiled=True)  11.1 us
    ppermute x2, starting transfers between devices, across(): return lax.ppermute(array, 'loop', pairs)  6.03 us
    ppermute x4, waiting for transfers between devices, to_next(): return lax.ppermute(array, 'loop', pairs)  4.15 us
    ppermute x4, starting transfers between devices, to_next(): return lax.ppermute(array, 'loop', pairs)  4.1 us
    pallas_call x4, Pallas kernels, add_pieces(): pl.pallas_call(functools.partial(pieces_kernel, places, len(arrays), pack...  3.62 us
    ppermute x1, waiting for transfers between devices, to_pair(): return lax.ppermute(array, 'loop', pairs)  3.19 us
    ppermute x1, starting transfers between devices, to_pair(): return lax.ppermute(array, 'loop', pairs)  1.02 us
    pallas_call x1, Pallas kernels, local(): pl.pallas_call(functools.partial(update_kernel, rows * loop_size * width)...  0.93 us
  transfers between devices with their start and end apart: 10, of which 4 were waited for; matrix products, arithmetic and copies ran while one was open for 0% of the time, Pallas kernels for 10%

profile of v22, /device:TPU:0, one launch (start us, length us, event | category | flops | bytes accessed | tf_op | source)
XLA Modules:
  0.0 35.9 jit_solution(17297108500096767772)
XLA Ops:
  0.0 3.0 %collective-permute-start = (bf16[128,512]{1,0:T(8,128)(2,1)}, bf16[128,512]{1,0:T(8,128)(2,1)S(1)}, u32[]{:S(2)}, u32[]{:S(2)}) collective-permute-start(bf16[128,512]{1,0:T(8,128)(2,1)} %rest_0_.1), channel_id=1, source_target_pairs={{0,4},{4,8},{8,12},{12,14},{14,10},{10,6},{6,2},{2,0},{1,3},{5,1},... | collective-permute-start | bytes 393224 | tf_op jit(solution)/shard_map/ppermute | solution.py:29
  3.0 0.0 collective-permute-start.1
  3.0 4.0 %collective-permute-start.6 = (bf16[128,512]{1,0:T(8,128)(2,1)}, bf16[128,512]{1,0:T(8,128)(2,1)S(1)}, u32[]{:S(2)}, u32[]{:S(2)}) collective-permute-start(bf16[128,512]{1,0:T(8,128)(2,1)} %rest_0_.1), channel_id=1, source_target_pairs={{0,12},{1,13},{4,6},{5,7},{8,10},{9,11},{12,0},{13,1},{14,2},{15,3... | collective-permute-start | bytes 393224 | tf_op jit(solution)/shard_map/ppermute | solution.py:39
  7.7 0.0 copy-start.3
  7.7 0.6 %copy-done.3 = s32[1,8]{1,0:T(1,128)S(1)} copy-done((s32[1,8]{1,0:T(1,128)S(1)}, s32[1,8]{1,0:T(1,128)}, u32[]{:S(2)}) %copy-start.3) | copy-done | bytes 56
  8.4 0.0 copy-start
  8.4 0.0 copy-start.1
  8.4 0.0 copy-start.2
  8.4 0.1 slot_table.1.table_ref
  8.5 0.0 collective-permute-done.rest_1_
  8.5 0.1 collective-permute-start.3
  8.6 1.0 %collective-permute-done.1.rest_2_ = bf16[128,512]{1,0:T(8,128)(2,1)S(1)} collective-permute-done((bf16[128,512]{1,0:T(8,128)(2,1)}, bf16[128,512]{1,0:T(8,128)(2,1)S(1)}, u32[]{:S(2)}, u32[]{:S(2)}) %collective-permute-start.1) | collective-permute-done | bytes 131104 | tf_op jit(solution)/shard_map/ppermute | solution.py:29
  9.6 1.0 %collective-permute-start.4 = (bf16[128,512]{1,0:T(8,128)(2,1)S(1)}, bf16[128,512]{1,0:T(8,128)(2,1)S(1)}, u32[]{:S(2)}, u32[]{:S(2)}) collective-permute-start(bf16[128,512]{1,0:T(8,128)(2,1)S(1)} %collective-permute-done.1.rest_2_), channel_id=1, source_target_pairs={{0,2},{4,0},{8,4},{12,8},{14,12},{10,14},{6,10},{2,6},{1,5},{5,9},... | collective-permute-start | bytes 393224 | tf_op jit(solution)/shard_map/ppermute | solution.py:29
  10.6 0.0 copy-done
  10.6 0.0 copy-done.1
  10.6 0.0 copy-done.2
  10.6 0.9 %add_pieces.4 = (f32[256,512]{1,0:T(8,128)S(1)}, bf16[512,512]{1,0:T(8,128)(2,1)S(1)}, bf16[128,512]{1,0:T(8,128)(2,1)S(1)}, bf16[384,512]{1,0:T(8,128)(2,1)S(1)}) custom-call(s32[1,128]{1,0:T(1,128)S(1)} %slot_table.1.table_ref, f32[256,512]{1,0:T(8,128)S(1)} %copy-done, s32[256,1024]{1,0:T(8,128)S(1)} %copy-done.1, bf16[128,512]{1,0:T(8,128)(2,1)S(1)} %copy-done.2, ...), custom_call_target="tpu_custom_call" | custom-call | flops 6442450944 | bytes 1048576 | tf_op jit(solution)/shard_map/add_pieces/pallas_call | solution.py:255
  11.5 2.0 %collective-permute-start.2 = (bf16[128,512]{1,0:T(8,128)(2,1)S(1)}, bf16[128,512]{1,0:T(8,128)(2,1)S(1)}, u32[]{:S(2)}, u32[]{:S(2)}) collective-permute-start(bf16[128,512]{1,0:T(8,128)(2,1)S(1)} %get-tuple-element.21), channel_id=1, source_target_pairs={{0,12},{1,13},{4,6},{5,7},{8,10},{9,11},{12,0},{13,1},{14,2},{15,3... | collective-permute-start | bytes 393224 | tf_op jit(solution)/shard_map/ppermute | solution.py:39
  13.5 0.0 collective-permute-start.8
  13.5 0.7 %collective-permute-done.3.upper_ref.rest_0_ = bf16[128,512]{1,0:T(8,128)(2,1)S(1)} collective-permute-done((bf16[128,512]{1,0:T(8,128)(2,1)S(1)}, bf16[128,512]{1,0:T(8,128)(2,1)S(1)}, u32[]{:S(2)}, u32[]{:S(2)}) %collective-permute-start.3) | collective-permute-done | bytes 131104 | tf_op jit(solution)/shard_map/ppermute | solution.py:29
  14.2 2.4 %collective-permute-done.4.lower_ref.rest_1_ = bf16[128,512]{1,0:T(8,128)(2,1)S(1)} collective-permute-done((bf16[128,512]{1,0:T(8,128)(2,1)S(1)}, bf16[128,512]{1,0:T(8,128)(2,1)S(1)}, u32[]{:S(2)}, u32[]{:S(2)}) %collective-permute-start.4) | collective-permute-done | bytes 131104 | tf_op jit(solution)/shard_map/ppermute | solution.py:29
  16.7 1.0 %collective-permute-start.5 = (bf16[128,512]{1,0:T(8,128)(2,1)S(1)}, bf16[128,512]{1,0:T(8,128)(2,1)S(1)}, u32[]{:S(2)}, u32[]{:S(2)}) collective-permute-start(bf16[128,512]{1,0:T(8,128)(2,1)S(1)} %pick.1), channel_id=1, source_target_pairs={{0,2},{1,3},{4,8},{5,9},{8,4},{9,5},{12,14},{13,15},{14,12},{15,13... | collective-permute-start | bytes 393224 | tf_op jit(solution)/shard_map/ppermute | solution.py:49
  17.7 0.0 collective-permute-done.6.rest_2_
  17.7 0.7 %add_pieces.5 = (f32[256,512]{1,0:T(8,128)S(1)}, bf16[384,512]{1,0:T(8,128)(2,1)S(1)}) custom-call(s32[1,128]{1,0:T(1,128)S(1)} %slot_table.1.table_ref, bf16[512,512]{1,0:T(8,128)(2,1)S(1)} %get-tuple-element.20.given_ref, s32[256,1024]{1,0:T(8,128)S(1)} %copy-done.1, ...), custom_call_target="tpu_custom_call", output_to_operand_aliasing={{0}: (6, {})} | custom-call | flops 6442450944 | bytes 1048576 | tf_op jit(solution)/shard_map/add_pieces/pallas_call | solution.py:255
  18.4 0.1 collective-permute-start.9
  18.5 0.0 collective-permute-done.2.refs_0_.rest_0_
  18.5 3.2 %collective-permute-done.5.refs_1_.rest_1_ = bf16[128,512]{1,0:T(8,128)(2,1)S(1)} collective-permute-done((bf16[128,512]{1,0:T(8,128)(2,1)S(1)}, bf16[128,512]{1,0:T(8,128)(2,1)S(1)}, u32[]{:S(2)}, u32[]{:S(2)}) %collective-permute-start.5) | collective-permute-done | bytes 131104 | tf_op jit(solution)/shard_map/ppermute | solution.py:49
  21.7 0.1 collective-permute-start.7
  21.8 0.0 collective-permute-done.8.rest_2_
  21.8 0.0 collective-permute-done.9.rest_3_
  21.8 1.8 %add_pieces.6.rest_1_ = f32[256,512]{1,0:T(8,128)S(1)} custom-call(s32[1,128]{1,0:T(1,128)S(1)} %slot_table.1.table_ref, bf16[512,512]{1,0:T(8,128)(2,1)S(1)} %get-tuple-element.20.given_ref, s32[256,1024]{1,0:T(8,128)S(1)} %copy-done.1, bf16[128,512]{1,0:T(8,128)(2,1)S(1)} %collective-permute-done.2.refs_0_.rest_0_, ...), custom_call_target="tpu_custom_call", output_to_operand_aliasing={{}: (7, {})} | custom-call | flops 17179869184 | bytes 1048576 | tf_op jit(solution)/shard_map/add_pieces/pallas_call | solution.py:255
  23.7 0.0 collective-permute-done.7.rest_0_
  23.7 0.2 add_pieces.7
  23.9 11.1 %all_to_all.11 = f32[16,1,128]{2,1,0:T(1,128)S(1)} all-to-all(f32[16,1,128]{2,1,0:T(1,128)S(1)} %bitcast.7), channel_id=1, replica_groups=mesh['group'=2,'loop'=16] {'loop'}, dimensions={0} | all-to-all | bytes 16384 | tf_op jit(solution)/shard_map/all_to_all | solution.py:406
  34.9 0.9 %update.1 = f32[256,512]{1,0:T(8,128)} custom-call(f32[256,512]{1,0:T(8,128)S(1)} %copy-done, f32[256,512]{1,0:T(8,128)S(1)} %get-tuple-element.29.grad_ref, f32[16,128]{1,0:T(8,128)S(1)} %bitcast.6), custom_call_target="tpu_custom_call" | custom-call | flops 262144 | bytes 1572864 | tf_op jit(solution)/shard_map/update/pallas_call | solution.py:407
  (2 shorter events, 0.0 us)
Async XLA Ops:
  0.0 8.5 %collective-permute-start = (bf16[128,512]{1,0:T(8,128)(2,1)}, bf16[128,512]{1,0:T(8,128)(2,1)S(1)}, u32[]{:S(2)}, u32[]{:S(2)}) collective-permute-start(bf16[128,512]{1,0:T(8,128)(2,1)} %rest_0_.1), channel_id=1, source_target_pairs={{0,4},{4,8},{8,12},{12,14},{14,10},{10,6},{6,2},{2,0},{1,3},{5,1},... | collective-permute-start | bytes 393224 | tf_op jit(solution)/shard_map/ppermute | solution.py:29
  3.0 6.6 %collective-permute-start.1 = (bf16[128,512]{1,0:T(8,128)(2,1)}, bf16[128,512]{1,0:T(8,128)(2,1)S(1)}, u32[]{:S(2)}, u32[]{:S(2)}) collective-permute-start(bf16[128,512]{1,0:T(8,128)(2,1)} %rest_0_.1), channel_id=1, source_target_pairs={{0,2},{4,0},{8,4},{12,8},{14,12},{10,14},{6,10},{2,6},{1,5},{5,9},... | collective-permute-start | bytes 393224 | tf_op jit(solution)/shard_map/ppermute | solution.py:29
  3.0 14.7 %collective-permute-start.6 = (bf16[128,512]{1,0:T(8,128)(2,1)}, bf16[128,512]{1,0:T(8,128)(2,1)S(1)}, u32[]{:S(2)}, u32[]{:S(2)}) collective-permute-start(bf16[128,512]{1,0:T(8,128)(2,1)} %rest_0_.1), channel_id=1, source_target_pairs={{0,12},{1,13},{4,6},{5,7},{8,10},{9,11},{12,0},{13,1},{14,2},{15,3... | collective-permute-start | bytes 393224 | tf_op jit(solution)/shard_map/ppermute | solution.py:39
  7.7 0.7 %copy-start.3 = (s32[1,8]{1,0:T(1,128)S(1)}, s32[1,8]{1,0:T(1,128)}, u32[]{:S(2)}) copy-start(s32[1,8]{1,0:T(1,128)} %list_ref.1) | copy-start | bytes 100
  8.4 2.2 %copy-start = (f32[256,512]{1,0:T(8,128)S(1)}, f32[256,512]{1,0:T(8,128)}, u32[]{:S(2)}) copy-start(f32[256,512]{1,0:T(8,128)} %users_ref.1) | copy-start | bytes 1572868
  8.4 2.2 %copy-start.1 = (s32[256,1024]{1,0:T(8,128)S(1)}, s32[256,1024]{1,0:T(8,128)}, u32[]{:S(2)}) copy-start(s32[256,1024]{1,0:T(8,128)} %labels_ref.7) | copy-start | bytes 3145732
  8.4 2.2 %copy-start.2 = (bf16[128,512]{1,0:T(8,128)(2,1)S(1)}, bf16[128,512]{1,0:T(8,128)(2,1)}, u32[]{:S(2)}) copy-start(bf16[128,512]{1,0:T(8,128)(2,1)} %rest_0_.1) | copy-start | bytes 393220
  8.5 5.7 %collective-permute-start.3 = (bf16[128,512]{1,0:T(8,128)(2,1)S(1)}, bf16[128,512]{1,0:T(8,128)(2,1)S(1)}, u32[]{:S(2)}, u32[]{:S(2)}) collective-permute-start(bf16[128,512]{1,0:T(8,128)(2,1)S(1)} %collective-permute-done.rest_1_), channel_id=1, source_target_pairs={{0,4},{4,8},{8,12},{12,14},{14,10},{10,6},{6,2},{2,0},{1,3},{5,1},... | collective-permute-start | bytes 393224 | tf_op jit(solution)/shard_map/ppermute | solution.py:29
  9.6 7.0 %collective-permute-start.4 = (bf16[128,512]{1,0:T(8,128)(2,1)S(1)}, bf16[128,512]{1,0:T(8,128)(2,1)S(1)}, u32[]{:S(2)}, u32[]{:S(2)}) collective-permute-start(bf16[128,512]{1,0:T(8,128)(2,1)S(1)} %collective-permute-done.1.rest_2_), channel_id=1, source_target_pairs={{0,2},{4,0},{8,4},{12,8},{14,12},{10,14},{6,10},{2,6},{1,5},{5,9},... | collective-permute-start | bytes 393224 | tf_op jit(solution)/shard_map/ppermute | solution.py:29
  11.5 7.0 %collective-permute-start.2 = (bf16[128,512]{1,0:T(8,128)(2,1)S(1)}, bf16[128,512]{1,0:T(8,128)(2,1)S(1)}, u32[]{:S(2)}, u32[]{:S(2)}) collective-permute-start(bf16[128,512]{1,0:T(8,128)(2,1)S(1)} %get-tuple-element.21), channel_id=1, source_target_pairs={{0,12},{1,13},{4,6},{5,7},{8,10},{9,11},{12,0},{13,1},{14,2},{15,3... | collective-permute-start | bytes 393224 | tf_op jit(solution)/shard_map/ppermute | solution.py:39
  13.5 8.3 %collective-permute-start.8 = (bf16[384,512]{1,0:T(8,128)(2,1)S(1)}, bf16[384,512]{1,0:T(8,128)(2,1)S(1)}, u32[]{:S(2)}, u32[]{:S(2)}) collective-permute-start(bf16[384,512]{1,0:T(8,128)(2,1)S(1)} %get-tuple-element.26), channel_id=1, source_target_pairs={{0,1},{1,0},{2,3},{3,2},{4,5},{5,4},{6,7},{7,6},{8,9},{9,8},{10,11... | collective-permute-start | bytes 1179656 | tf_op jit(solution)/shard_map/ppermute | solution.py:53
  16.7 5.0 %collective-permute-start.5 = (bf16[128,512]{1,0:T(8,128)(2,1)S(1)}, bf16[128,512]{1,0:T(8,128)(2,1)S(1)}, u32[]{:S(2)}, u32[]{:S(2)}) collective-permute-start(bf16[128,512]{1,0:T(8,128)(2,1)S(1)} %pick.1), channel_id=1, source_target_pairs={{0,2},{1,3},{4,8},{5,9},{8,4},{9,5},{12,14},{13,15},{14,12},{15,13... | collective-permute-start | bytes 393224 | tf_op jit(solution)/shard_map/ppermute | solution.py:49
  18.4 3.4 %collective-permute-start.9 = (bf16[384,512]{1,0:T(8,128)(2,1)S(1)}, bf16[384,512]{1,0:T(8,128)(2,1)S(1)}, u32[]{:S(2)}, u32[]{:S(2)}) collective-permute-start(bf16[384,512]{1,0:T(8,128)(2,1)S(1)} %get-tuple-element.27), channel_id=1, source_target_pairs={{0,1},{1,0},{2,3},{3,2},{4,5},{5,4},{6,7},{7,6},{8,9},{9,8},{10,11... | collective-permute-start | bytes 1179656 | tf_op jit(solution)/shard_map/ppermute | solution.py:53
  21.7 2.0 %collective-permute-start.7 = (bf16[256,512]{1,0:T(8,128)(2,1)S(1)}, bf16[256,512]{1,0:T(8,128)(2,1)S(1)}, u32[]{:S(2)}, u32[]{:S(2)}) collective-permute-start(bf16[256,512]{1,0:T(8,128)(2,1)S(1)} %pack.1), channel_id=1, source_target_pairs={{0,1},{1,0},{2,3},{3,2},{4,5},{5,4},{6,7},{7,6},{8,9},{9,8},{10,11... | collective-permute-start | bytes 786440 | tf_op jit(solution)/shard_map/ppermute | solution.py:53

commit v23 on v22

--- a/solution.py
+++ b/solution.py
@@ -39,14 +39,8 @@
     return lax.ppermute(array, "loop", pairs)
 
 
-def to_pair(array, loop_size):
-    chips, device = ring_place(loop_size)
-    pairs = [
-        (device(at, core), device(at + (1 if at % 2 else -1), core))
-        for at in range(chips)
-        for core in range(2)
-    ]
-    return lax.ppermute(array, "loop", pairs)
+def to_other_row(array, loop_size):
+    return lax.ppermute(array, "loop", [(at, at ^ 2) for at in range(loop_size)])
 
 
 def to_other_core(array, loop_size):
@@ -147,9 +141,10 @@
 
 def pick_kernel(loop_size, upper_ref, lower_ref, picked_ref):
     core, position = core_and_position(loop_size)
+    middle = (position + 1) // 2
     for at, ref in enumerate((lower_ref, upper_ref)):
 
-        @pl.when((core + position) % 2 == at)
+        @pl.when((core + position + middle) % 2 == at)
         def _():
             picked_ref[...] = ref[...]
 
@@ -296,7 +291,7 @@
     )
     third = [held(across(opposite, loop_size), (4, 0))]
     first = other(packed, near[:3])
-    third.append(held(to_pair(pick(up, down, loop_size), loop_size), (0, -3)))
+    third.append(held(to_other_row(pick(up, down, loop_size), loop_size), (0, -3)))
     gradient, packed = add_pieces(second, [0, 1, 2], loop_size, table, parts, labels, gradient, False)
     second = other(packed, [(2, 0), (-2, 0), (0, 3)])
     arrived, gradient = lax.optimization_barrier(([array for array, _ in third], gradient))

time: 36.2 us -> 35.6 us (0.983); the launches traced: 35.9 us -> 36 us
  waiting for transfers between devices: 7.35 us -> 9.13 us
  blocking collectives: 11.1 us -> 10.2 us
  starting transfers between devices: 11.3 us -> 10.5 us
    all_to_all x1, blocking collectives: 11.1 us -> 10.2 us  [local(): squares = lax.all_to_all(square, 'loop', 0, 0, tiled=True)]
    ppermute x4, waiting for transfers between devices: 4.15 us -> 4.92 us  [to_next(): return lax.ppermute(array, 'loop', pairs)]
    ppermute x1, starting transfers between devices: 1.02 us -> 0.25 us  [to_other_row(): lax.ppermute(array, 'loop', [(at, at ^ 2) for at in range(loop_size)])]
    ppermute x3, waiting for transfers between devices: 0.01 us -> 0.45 us  [to_other_core(): lax.ppermute(array, 'loop', [(at, at ^ 1) for at in range(loop_size)])]
  transfers between devices with their start and end apart: 10 -> 10, of which waited for: 4 -> 6; matrix products, arithmetic and copies ran while one was open for 0% -> 0% of each run, Pallas kernels for 10% -> 8%
where the time goes in v23:
time: 35.6 us; the launch traced here: 36 us
  starting transfers between devices  10.5 us (29%)
  blocking collectives  10.2 us (29%)
  waiting for transfers between devices  9.13 us (26%)
  Pallas kernels  4.72 us (13%)
  between operations  0.75 us (2%)
  local copies, waits for them, and re-layouts  0.66 us (2%)
    all_to_all x1, blocking collectives, local(): squares = lax.all_to_all(square, 'loop', 0, 0, tiled=True)  10.2 us
    ppermute x2, starting transfers between devices, across(): return lax.ppermute(array, 'loop', pairs)  6.03 us
    ppermute x4, waiting for transfers between devices, to_next(): return lax.ppermute(array, 'loop', pairs)  4.92 us
    ppermute x4, starting transfers between devices, to_next(): return lax.ppermute(array, 'loop', pairs)  4.1 us
    pallas_call x4, Pallas kernels, add_pieces(): pl.pallas_call(functools.partial(pieces_kernel, places, len(arrays), pack...  3.61 us
    ppermute x1, waiting for transfers between devices, to_other_row(): lax.ppermute(array, 'loop', [(at, at ^ 2) for at in range(loop_size)])  3.52 us
    pallas_call x1, Pallas kernels, local(): pl.pallas_call(functools.partial(update_kernel, rows * loop_size * width)...  0.93 us
  transfers between devices with their start and end apart: 10, of which 6 were waited for; matrix products, arithmetic and copies ran while one was open for 0% of the time, Pallas kernels for 8%

profile of v23, /device:TPU:0, one launch (start us, length us, event | category | flops | bytes accessed | tf_op | source)
XLA Modules:
  0.0 36.0 jit_solution(10243363633364799824)
XLA Ops:
  0.0 3.0 %collective-permute-start = (bf16[128,512]{1,0:T(8,128)(2,1)}, bf16[128,512]{1,0:T(8,128)(2,1)S(1)}, u32[]{:S(2)}, u32[]{:S(2)}) collective-permute-start(bf16[128,512]{1,0:T(8,128)(2,1)} %rest_0_.1), channel_id=1, source_target_pairs={{0,4},{4,8},{8,12},{12,14},{14,10},{10,6},{6,2},{2,0},{1,3},{5,1},... | collective-permute-start | bytes 393224 | tf_op jit(solution)/shard_map/ppermute | solution.py:29
  3.0 0.0 collective-permute-start.1
  3.0 4.0 %collective-permute-start.6 = (bf16[128,512]{1,0:T(8,128)(2,1)}, bf16[128,512]{1,0:T(8,128)(2,1)S(1)}, u32[]{:S(2)}, u32[]{:S(2)}) collective-permute-start(bf16[128,512]{1,0:T(8,128)(2,1)} %rest_0_.1), channel_id=1, source_target_pairs={{0,12},{1,13},{4,6},{5,7},{8,10},{9,11},{12,0},{13,1},{14,2},{15,3... | collective-permute-start | bytes 393224 | tf_op jit(solution)/shard_map/ppermute | solution.py:39
  7.7 0.0 copy-start.3
  7.7 0.6 %copy-done.3 = s32[1,8]{1,0:T(1,128)S(1)} copy-done((s32[1,8]{1,0:T(1,128)S(1)}, s32[1,8]{1,0:T(1,128)}, u32[]{:S(2)}) %copy-start.3) | copy-done | bytes 56
  8.4 0.0 copy-start
  8.4 0.0 copy-start.1
  8.4 0.0 copy-start.2
  8.4 0.1 slot_table.1.table_ref
  8.5 0.0 collective-permute-done.rest_1_
  8.5 0.1 collective-permute-start.3
  8.6 1.0 %collective-permute-done.1.rest_2_ = bf16[128,512]{1,0:T(8,128)(2,1)S(1)} collective-permute-done((bf16[128,512]{1,0:T(8,128)(2,1)}, bf16[128,512]{1,0:T(8,128)(2,1)S(1)}, u32[]{:S(2)}, u32[]{:S(2)}) %collective-permute-start.1) | collective-permute-done | bytes 131104 | tf_op jit(solution)/shard_map/ppermute | solution.py:29
  9.6 1.0 %collective-permute-start.4 = (bf16[128,512]{1,0:T(8,128)(2,1)S(1)}, bf16[128,512]{1,0:T(8,128)(2,1)S(1)}, u32[]{:S(2)}, u32[]{:S(2)}) collective-permute-start(bf16[128,512]{1,0:T(8,128)(2,1)S(1)} %collective-permute-done.1.rest_2_), channel_id=1, source_target_pairs={{0,2},{4,0},{8,4},{12,8},{14,12},{10,14},{6,10},{2,6},{1,5},{5,9},... | collective-permute-start | bytes 393224 | tf_op jit(solution)/shard_map/ppermute | solution.py:29
  10.6 0.0 copy-done
  10.6 0.0 copy-done.1
  10.6 0.0 copy-done.2
  10.6 0.9 %add_pieces.4 = (f32[256,512]{1,0:T(8,128)S(1)}, bf16[512,512]{1,0:T(8,128)(2,1)S(1)}, bf16[128,512]{1,0:T(8,128)(2,1)S(1)}, bf16[384,512]{1,0:T(8,128)(2,1)S(1)}) custom-call(s32[1,128]{1,0:T(1,128)S(1)} %slot_table.1.table_ref, f32[256,512]{1,0:T(8,128)S(1)} %copy-done, s32[256,1024]{1,0:T(8,128)S(1)} %copy-done.1, bf16[128,512]{1,0:T(8,128)(2,1)S(1)} %copy-done.2, ...), custom_call_target="tpu_custom_call" | custom-call | flops 6442450944 | bytes 1048576 | tf_op jit(solution)/shard_map/add_pieces/pallas_call | solution.py:250
  11.5 2.0 %collective-permute-start.2 = (bf16[128,512]{1,0:T(8,128)(2,1)S(1)}, bf16[128,512]{1,0:T(8,128)(2,1)S(1)}, u32[]{:S(2)}, u32[]{:S(2)}) collective-permute-start(bf16[128,512]{1,0:T(8,128)(2,1)S(1)} %get-tuple-element.21), channel_id=1, source_target_pairs={{0,12},{1,13},{4,6},{5,7},{8,10},{9,11},{12,0},{13,1},{14,2},{15,3... | collective-permute-start | bytes 393224 | tf_op jit(solution)/shard_map/ppermute | solution.py:39
  13.5 0.0 collective-permute-start.8
  13.5 0.7 %collective-permute-done.3.upper_ref.rest_0_ = bf16[128,512]{1,0:T(8,128)(2,1)S(1)} collective-permute-done((bf16[128,512]{1,0:T(8,128)(2,1)S(1)}, bf16[128,512]{1,0:T(8,128)(2,1)S(1)}, u32[]{:S(2)}, u32[]{:S(2)}) %collective-permute-start.3) | collective-permute-done | bytes 131104 | tf_op jit(solution)/shard_map/ppermute | solution.py:29
  14.2 3.2 %collective-permute-done.4.lower_ref.rest_1_ = bf16[128,512]{1,0:T(8,128)(2,1)S(1)} collective-permute-done((bf16[128,512]{1,0:T(8,128)(2,1)S(1)}, bf16[128,512]{1,0:T(8,128)(2,1)S(1)}, u32[]{:S(2)}, u32[]{:S(2)}) %collective-permute-start.4) | collective-permute-done | bytes 131104 | tf_op jit(solution)/shard_map/ppermute | solution.py:29
  17.4 0.3 collective-permute-start.5
  17.7 0.0 collective-permute-done.6.rest_2_
  17.7 0.9 %add_pieces.5 = (f32[256,512]{1,0:T(8,128)S(1)}, bf16[384,512]{1,0:T(8,128)(2,1)S(1)}) custom-call(s32[1,128]{1,0:T(1,128)S(1)} %slot_table.1.table_ref, bf16[512,512]{1,0:T(8,128)(2,1)S(1)} %get-tuple-element.20.given_ref, s32[256,1024]{1,0:T(8,128)S(1)} %copy-done.1, ...), custom_call_target="tpu_custom_call", output_to_operand_aliasing={{0}: (6, {})} | custom-call | flops 6442450944 | bytes 1048576 | tf_op jit(solution)/shard_map/add_pieces/pallas_call | solution.py:250
  18.6 0.1 collective-permute-start.9
  18.7 0.2 collective-permute-done.2.refs_0_.rest_0_
  18.9 3.5 %collective-permute-done.5.refs_1_.rest_1_ = bf16[128,512]{1,0:T(8,128)(2,1)S(1)} collective-permute-done((bf16[128,512]{1,0:T(8,128)(2,1)S(1)}, bf16[128,512]{1,0:T(8,128)(2,1)S(1)}, u32[]{:S(2)}, u32[]{:S(2)}) %collective-permute-start.5) | collective-permute-done | bytes 131104 | tf_op jit(solution)/shard_map/ppermute | solution.py:43
  22.5 0.1 collective-permute-start.7
  22.6 0.0 collective-permute-done.8.rest_2_
  22.6 0.0 collective-permute-done.9.rest_3_
  22.6 1.0 %add_pieces.6.rest_1_ = f32[256,512]{1,0:T(8,128)S(1)} custom-call(s32[1,128]{1,0:T(1,128)S(1)} %slot_table.1.table_ref, bf16[512,512]{1,0:T(8,128)(2,1)S(1)} %get-tuple-element.20.given_ref, s32[256,1024]{1,0:T(8,128)S(1)} %copy-done.1, bf16[128,512]{1,0:T(8,128)(2,1)S(1)} %collective-permute-done.2.refs_0_.rest_0_, ...), custom_call_target="tpu_custom_call", output_to_operand_aliasing={{}: (7, {})} | custom-call | flops 17179869184 | bytes 1048576 | tf_op jit(solution)/shard_map/add_pieces/pallas_call | solution.py:250
  23.6 0.4 %collective-permute-done.7.rest_0_ = bf16[256,512]{1,0:T(8,128)(2,1)S(1)} collective-permute-done((bf16[256,512]{1,0:T(8,128)(2,1)S(1)}, bf16[256,512]{1,0:T(8,128)(2,1)S(1)}, u32[]{:S(2)}, u32[]{:S(2)}) %collective-permute-start.7) | collective-permute-done | bytes 262176 | tf_op jit(solution)/shard_map/ppermute | solution.py:47
  24.1 0.8 %add_pieces.7 = (f32[256,512]{1,0:T(8,128)S(1)}, f32[16,128]{1,0:T(8,128)S(1)}) custom-call(s32[1,128]{1,0:T(1,128)S(1)} %slot_table.1.table_ref, bf16[512,512]{1,0:T(8,128)(2,1)S(1)} %get-tuple-element.20.given_ref, s32[256,1024]{1,0:T(8,128)S(1)} %copy-done.1, ...), custom_call_target="tpu_custom_call", output_to_operand_aliasing={{0}: (4, {})} | custom-call | flops 4294967296 | bytes 1048576 | tf_op jit(solution)/shard_map/add_pieces/pallas_call | solution.py:250
  24.9 10.2 %all_to_all.11 = f32[16,1,128]{2,1,0:T(1,128)S(1)} all-to-all(f32[16,1,128]{2,1,0:T(1,128)S(1)} %bitcast.7), channel_id=1, replica_groups=mesh['group'=2,'loop'=16] {'loop'}, dimensions={0} | all-to-all | bytes 16384 | tf_op jit(solution)/shard_map/all_to_all | solution.py:401
  35.1 0.9 %update.1 = f32[256,512]{1,0:T(8,128)} custom-call(f32[256,512]{1,0:T(8,128)S(1)} %copy-done, f32[256,512]{1,0:T(8,128)S(1)} %get-tuple-element.29.grad_ref, f32[16,128]{1,0:T(8,128)S(1)} %bitcast.6), custom_call_target="tpu_custom_call" | custom-call | flops 262144 | bytes 1572864 | tf_op jit(solution)/shard_map/update/pallas_call | solution.py:402
  (2 shorter events, 0.0 us)
Async XLA Ops:
  0.0 8.5 %collective-permute-start = (bf16[128,512]{1,0:T(8,128)(2,1)}, bf16[128,512]{1,0:T(8,128)(2,1)S(1)}, u32[]{:S(2)}, u32[]{:S(2)}) collective-permute-start(bf16[128,512]{1,0:T(8,128)(2,1)} %rest_0_.1), channel_id=1, source_target_pairs={{0,4},{4,8},{8,12},{12,14},{14,10},{10,6},{6,2},{2,0},{1,3},{5,1},... | collective-permute-start | bytes 393224 | tf_op jit(solution)/shard_map/ppermute | solution.py:29
  3.0 6.6 %collective-permute-start.1 = (bf16[128,512]{1,0:T(8,128)(2,1)}, bf16[128,512]{1,0:T(8,128)(2,1)S(1)}, u32[]{:S(2)}, u32[]{:S(2)}) collective-permute-start(bf16[128,512]{1,0:T(8,128)(2,1)} %rest_0_.1), channel_id=1, source_target_pairs={{0,2},{4,0},{8,4},{12,8},{14,12},{10,14},{6,10},{2,6},{1,5},{5,9},... | collective-permute-start | bytes 393224 | tf_op jit(solution)/shard_map/ppermute | solution.py:29
  3.0 14.7 %collective-permute-start.6 = (bf16[128,512]{1,0:T(8,128)(2,1)}, bf16[128,512]{1,0:T(8,128)(2,1)S(1)}, u32[]{:S(2)}, u32[]{:S(2)}) collective-permute-start(bf16[128,512]{1,0:T(8,128)(2,1)} %rest_0_.1), channel_id=1, source_target_pairs={{0,12},{1,13},{4,6},{5,7},{8,10},{9,11},{12,0},{13,1},{14,2},{15,3... | collective-permute-start | bytes 393224 | tf_op jit(solution)/shard_map/ppermute | solution.py:39
  7.7 0.7 %copy-start.3 = (s32[1,8]{1,0:T(1,128)S(1)}, s32[1,8]{1,0:T(1,128)}, u32[]{:S(2)}) copy-start(s32[1,8]{1,0:T(1,128)} %list_ref.1) | copy-start | bytes 100
  8.4 2.2 %copy-start = (f32[256,512]{1,0:T(8,128)S(1)}, f32[256,512]{1,0:T(8,128)}, u32[]{:S(2)}) copy-start(f32[256,512]{1,0:T(8,128)} %users_ref.1) | copy-start | bytes 1572868
  8.4 2.2 %copy-start.1 = (s32[256,1024]{1,0:T(8,128)S(1)}, s32[256,1024]{1,0:T(8,128)}, u32[]{:S(2)}) copy-start(s32[256,1024]{1,0:T(8,128)} %labels_ref.7) | copy-start | bytes 3145732
  8.4 2.2 %copy-start.2 = (bf16[128,512]{1,0:T(8,128)(2,1)S(1)}, bf16[128,512]{1,0:T(8,128)(2,1)}, u32[]{:S(2)}) copy-start(bf16[128,512]{1,0:T(8,128)(2,1)} %rest_0_.1) | copy-start | bytes 393220
  8.5 5.7 %collective-permute-start.3 = (bf16[128,512]{1,0:T(8,128)(2,1)S(1)}, bf16[128,512]{1,0:T(8,128)(2,1)S(1)}, u32[]{:S(2)}, u32[]{:S(2)}) collective-permute-start(bf16[128,512]{1,0:T(8,128)(2,1)S(1)} %collective-permute-done.rest_1_), channel_id=1, source_target_pairs={{0,4},{4,8},{8,12},{12,14},{14,10},{10,6},{6,2},{2,0},{1,3},{5,1},... | collective-permute-start | bytes 393224 | tf_op jit(solution)/shard_map/ppermute | solution.py:29
  9.6 7.8 %collective-permute-start.4 = (bf16[128,512]{1,0:T(8,128)(2,1)S(1)}, bf16[128,512]{1,0:T(8,128)(2,1)S(1)}, u32[]{:S(2)}, u32[]{:S(2)}) collective-permute-start(bf16[128,512]{1,0:T(8,128)(2,1)S(1)} %collective-permute-done.1.rest_2_), channel_id=1, source_target_pairs={{0,2},{4,0},{8,4},{12,8},{14,12},{10,14},{6,10},{2,6},{1,5},{5,9},... | collective-permute-start | bytes 393224 | tf_op jit(solution)/shard_map/ppermute | solution.py:29
  11.5 7.4 %collective-permute-start.2 = (bf16[128,512]{1,0:T(8,128)(2,1)S(1)}, bf16[128,512]{1,0:T(8,128)(2,1)S(1)}, u32[]{:S(2)}, u32[]{:S(2)}) collective-permute-start(bf16[128,512]{1,0:T(8,128)(2,1)S(1)} %get-tuple-element.21), channel_id=1, source_target_pairs={{0,12},{1,13},{4,6},{5,7},{8,10},{9,11},{12,0},{13,1},{14,2},{15,3... | collective-permute-start | bytes 393224 | tf_op jit(solution)/shard_map/ppermute | solution.py:39
  13.5 9.1 %collective-permute-start.8 = (bf16[384,512]{1,0:T(8,128)(2,1)S(1)}, bf16[384,512]{1,0:T(8,128)(2,1)S(1)}, u32[]{:S(2)}, u32[]{:S(2)}) collective-permute-start(bf16[384,512]{1,0:T(8,128)(2,1)S(1)} %get-tuple-element.26), channel_id=1, source_target_pairs={{0,1},{1,0},{2,3},{3,2},{4,5},{5,4},{6,7},{7,6},{8,9},{9,8},{10,11... | collective-permute-start | bytes 1179656 | tf_op jit(solution)/shard_map/ppermute | solution.py:47
  17.4 5.0 %collective-permute-start.5 = (bf16[128,512]{1,0:T(8,128)(2,1)S(1)}, bf16[128,512]{1,0:T(8,128)(2,1)S(1)}, u32[]{:S(2)}, u32[]{:S(2)}) collective-permute-start(bf16[128,512]{1,0:T(8,128)(2,1)S(1)} %pick.1), channel_id=1, source_target_pairs={{0,2},{1,3},{2,0},{3,1},{4,6},{5,7},{6,4},{7,5},{8,10},{9,11},{10,... | collective-permute-start | bytes 393224 | tf_op jit(solution)/shard_map/ppermute | solution.py:43
  18.6 4.0 %collective-permute-start.9 = (bf16[384,512]{1,0:T(8,128)(2,1)S(1)}, bf16[384,512]{1,0:T(8,128)(2,1)S(1)}, u32[]{:S(2)}, u32[]{:S(2)}) collective-permute-start(bf16[384,512]{1,0:T(8,128)(2,1)S(1)} %get-tuple-element.27), channel_id=1, source_target_pairs={{0,1},{1,0},{2,3},{3,2},{4,5},{5,4},{6,7},{7,6},{8,9},{9,8},{10,11... | collective-permute-start | bytes 1179656 | tf_op jit(solution)/shard_map/ppermute | solution.py:47
  22.5 1.6 %collective-permute-start.7 = (bf16[256,512]{1,0:T(8,128)(2,1)S(1)}, bf16[256,512]{1,0:T(8,128)(2,1)S(1)}, u32[]{:S(2)}, u32[]{:S(2)}) collective-permute-start(bf16[256,512]{1,0:T(8,128)(2,1)S(1)} %pack.1), channel_id=1, source_target_pairs={{0,1},{1,0},{2,3},{3,2},{4,5},{5,4},{6,7},{7,6},{8,9},{9,8},{10,11... | collective-permute-start | bytes 786440 | tf_op jit(solution)/shard_map/ppermute | solution.py:47

commit v24 on v18

--- a/solution.py
+++ b/solution.py
@@ -135,7 +135,7 @@
 
 def pack_kernel(loop_size, *refs):
     tile = refs[0].shape[0]
-    sources = refs[:-1] if loop_size is None else (refs[0], refs[2])
+    sources = refs[:-1] if loop_size is None else refs[:2]
     packed_ref = refs[-1] if loop_size is None else refs[-2]
     if loop_size is not None:
         core, position = core_and_position(loop_size)
@@ -260,11 +260,11 @@
     up, table = lax.optimization_barrier((up, table))
     first = [held(0, items), held(1, up), held(-1, down)]
     second = [held(2, to_next(up, 1, loop_size)), held(-2, to_next(down, -1, loop_size))]
-    first.append(other(up, [1]))
+    first.append(other(down, [-1]))
     packed, opposite = pack([items, up, down], loop_size)
     opposite = across(opposite, loop_size)
     gradient, parts = add_pieces(first, [], loop_size, table, users, labels, None, False)
-    first = other(packed, [0, -1])
+    first = other(packed, [0, 1])
     third = [held(3, to_next(second[0][0], 1, loop_size)), held(-3, to_next(second[1][0], -1, loop_size))]
     gradient, packed = add_pieces(second, [0, 1], loop_size, table, parts, labels, gradient, False)
     second = other(packed, [2, -2])

time: 35.4 us -> 35.3 us (level)
  blocking collectives: 11.1 us -> 10.6 us
    ppermute x6, waiting for transfers between devices: 3.2 us -> 4.35 us  [to_next(): return lax.ppermute(array, 'loop', pairs)]
    ppermute x1, waiting for transfers between devices: 2.72 us -> 2.01 us  [across(): return lax.ppermute(array, 'loop', pairs)]
    ppermute x4, starting transfers between devices: 0.15 us -> 0.84 us  [to_other_core(): lax.ppermute(array, 'loop', [(at, at ^ 1) for at in range(loop_size)])]
    ppermute x4, waiting for transfers between devices: 0.64 us -> 0.01 us  [to_other_core(): lax.ppermute(array, 'loop', [(at, at ^ 1) for at in range(loop_size)])]
    all_to_all x1, blocking collectives: 11.1 us -> 10.6 us  [local(): squares = lax.all_to_all(square, 'loop', 0, 0, tiled=True)]
  transfers between devices with their start and end apart: 11 -> 11, of which waited for: 4 -> 4; matrix products, arithmetic and copies ran while one was open for 0% -> 0% of each run, Pallas kernels for 9% -> 10%
where the time goes in v24:
time: 35.3 us; the launch traced here: 34.8 us
  starting transfers between devices  11.7 us (33%)
  blocking collectives  10.6 us (30%)
  waiting for transfers between devices  6.37 us (18%)
  Pallas kernels  4.72 us (13%)
  between operations  0.77 us (2%)
  local copies, waits for them, and re-layouts  0.66 us (2%)
    all_to_all x1, blocking collectives, local(): squares = lax.all_to_all(square, 'loop', 0, 0, tiled=True)  10.6 us
    ppermute x6, starting transfers between devices, to_next(): return lax.ppermute(array, 'loop', pairs)  7.64 us
    ppermute x6, waiting for transfers between devices, to_next(): return lax.ppermute(array, 'loop', pairs)  4.35 us
    pallas_call x4, Pallas kernels, add_pieces(): pl.pallas_call(functools.partial(pieces_kernel, places, len(arrays), pack...  3.59 us
    ppermute x1, starting transfers between devices, across(): return lax.ppermute(array, 'loop', pairs)  3.26 us
    ppermute x1, waiting for transfers between devices, across(): return lax.ppermute(array, 'loop', pairs)  2.01 us
    pallas_call x1, Pallas kernels, local(): pl.pallas_call(functools.partial(update_kernel, rows * loop_size * width)...  0.93 us
    ppermute x4, starting transfers between devices, to_other_core(): lax.ppermute(array, 'loop', [(at, at ^ 1) for at in range(loop_size)])  0.84 us
  transfers between devices with their start and end apart: 11, of which 4 were waited for; matrix products, arithmetic and copies ran while one was open for 0% of the time, Pallas kernels for 10%

profile of v24, /device:TPU:0, one launch (start us, length us, event | category | flops | bytes accessed | tf_op | source)
XLA Modules:
  0.0 34.8 jit_solution(3358888405364942107)
XLA Ops:
  0.0 3.0 %collective-permute-start = (bf16[128,512]{1,0:T(8,128)(2,1)}, bf16[128,512]{1,0:T(8,128)(2,1)S(1)}, u32[]{:S(2)}, u32[]{:S(2)}) collective-permute-start(bf16[128,512]{1,0:T(8,128)(2,1)} %refs_0_.1), channel_id=1, source_target_pairs={{0,4},{4,8},{8,12},{12,14},{14,10},{10,6},{6,2},{2,0},{1,3},{5,1},... | collective-permute-start | bytes 393224 | tf_op jit(solution)/shard_map/ppermute | solution.py:29
  3.0 0.0 collective-permute-start.1
  3.7 0.0 copy-start.3
  3.7 0.6 %copy-done.3 = s32[1,8]{1,0:T(1,128)S(1)} copy-done((s32[1,8]{1,0:T(1,128)S(1)}, s32[1,8]{1,0:T(1,128)}, u32[]{:S(2)}) %copy-start.3) | copy-done | bytes 56
  4.3 0.0 copy-start.2
  4.3 0.1 slot_table.1.table_ref
  4.5 0.0 copy-start
  4.5 0.0 copy-start.1
  4.5 2.5 %collective-permute-done.rest_1_.refs_1_ = bf16[128,512]{1,0:T(8,128)(2,1)S(1)} collective-permute-done((bf16[128,512]{1,0:T(8,128)(2,1)}, bf16[128,512]{1,0:T(8,128)(2,1)S(1)}, u32[]{:S(2)}, u32[]{:S(2)}) %collective-permute-start) | collective-permute-done | bytes 131104 | tf_op jit(solution)/shard_map/ppermute | solution.py:29
  7.0 1.5 %collective-permute-start.3 = (bf16[128,512]{1,0:T(8,128)(2,1)S(1)}, bf16[128,512]{1,0:T(8,128)(2,1)S(1)}, u32[]{:S(2)}, u32[]{:S(2)}) collective-permute-start(bf16[128,512]{1,0:T(8,128)(2,1)S(1)} %collective-permute-done.rest_1_.refs_1_), channel_id=1, source_target_pairs={{0,4},{4,8},{8,12},{12,14},{14,10},{10,6},{6,2},{2,0},{1,3},{5,1},... | collective-permute-start | bytes 393224 | tf_op jit(solution)/shard_map/ppermute | solution.py:29
  8.5 0.0 collective-permute-done.1.rest_2_.refs_2_
  8.5 0.0 collective-permute-start.2
  8.5 1.0 %collective-permute-start.5 = (bf16[128,512]{1,0:T(8,128)(2,1)S(1)}, bf16[128,512]{1,0:T(8,128)(2,1)S(1)}, u32[]{:S(2)}, u32[]{:S(2)}) collective-permute-start(bf16[128,512]{1,0:T(8,128)(2,1)S(1)} %collective-permute-done.1.rest_2_.refs_2_), channel_id=1, source_target_pairs={{0,2},{4,0},{8,4},{12,8},{14,12},{10,14},{6,10},{2,6},{1,5},{5,9},... | collective-permute-start | bytes 393224 | tf_op jit(solution)/shard_map/ppermute | solution.py:29
  9.5 0.0 copy-done.2
  9.5 3.3 %collective-permute-start.7 = (bf16[128,512]{1,0:T(8,128)(2,1)S(1)}, bf16[128,512]{1,0:T(8,128)(2,1)S(1)}, u32[]{:S(2)}, u32[]{:S(2)}) collective-permute-start(bf16[128,512]{1,0:T(8,128)(2,1)S(1)} %get-tuple-element.22), channel_id=1, source_target_pairs={{0,12},{1,13},{4,6},{5,7},{8,10},{9,11},{12,0},{13,1},{14,2},{15,3... | collective-permute-start | bytes 393224 | tf_op jit(solution)/shard_map/ppermute | solution.py:39
  12.8 0.7 %collective-permute-start.9 = (bf16[256,512]{1,0:T(8,128)(2,1)S(1)}, bf16[256,512]{1,0:T(8,128)(2,1)S(1)}, u32[]{:S(2)}, u32[]{:S(2)}) collective-permute-start(bf16[256,512]{1,0:T(8,128)(2,1)S(1)} %get-tuple-element.28), channel_id=1, source_target_pairs={{0,1},{1,0},{2,3},{3,2},{4,5},{5,4},{6,7},{7,6},{8,9},{9,8},{10,11... | collective-permute-start | bytes 786440 | tf_op jit(solution)/shard_map/ppermute | solution.py:43
  13.5 0.0 collective-permute-done.3.rest_0_
  13.5 0.0 collective-permute-start.4
  13.5 0.0 collective-permute-done.5.rest_1_
  13.5 2.0 %collective-permute-start.6 = (bf16[128,512]{1,0:T(8,128)(2,1)S(1)}, bf16[128,512]{1,0:T(8,128)(2,1)S(1)}, u32[]{:S(2)}, u32[]{:S(2)}) collective-permute-start(bf16[128,512]{1,0:T(8,128)(2,1)S(1)} %collective-permute-done.5.rest_1_), channel_id=1, source_target_pairs={{0,2},{4,0},{8,4},{12,8},{14,12},{10,14},{6,10},{2,6},{1,5},{5,9},... | collective-permute-start | bytes 393224 | tf_op jit(solution)/shard_map/ppermute | solution.py:29
  15.6 0.0 collective-permute-done.2.rest_3_
  15.6 0.0 copy-done
  15.6 0.0 copy-done.1
  15.6 0.8 %add_pieces.4 = (f32[256,512]{1,0:T(8,128)S(1)}, bf16[512,512]{1,0:T(8,128)(2,1)S(1)}) custom-call(s32[1,128]{1,0:T(1,128)S(1)} %slot_table.1.table_ref, f32[256,512]{1,0:T(8,128)S(1)} %copy-done, s32[256,1024]{1,0:T(8,128)S(1)} %copy-done.1, bf16[128,512]{1,0:T(8,128)(2,1)S(1)} %copy-done.2, bf16[128,512]{1,0:T(8,128)(2,1)S(1)} %collective-permute-done.rest_1_.refs_1_, ...), custom_call_target="tpu_custom_call" | custom-call | flops 536870912 | bytes 1048576 | tf_op jit(solution)/shard_map/add_pieces/pallas_call | solution.py:224
  16.4 0.7 %add_pieces.5 = (f32[256,512]{1,0:T(8,128)S(1)}, bf16[256,512]{1,0:T(8,128)(2,1)S(1)}) custom-call(s32[1,128]{1,0:T(1,128)S(1)} %slot_table.1.table_ref, bf16[512,512]{1,0:T(8,128)(2,1)S(1)} %get-tuple-element.21.given_ref, s32[256,1024]{1,0:T(8,128)S(1)} %copy-done.1, ...), custom_call_target="tpu_custom_call", output_to_operand_aliasing={{0}: (5, {})} | custom-call | flops 4294967296 | bytes 1048576 | tf_op jit(solution)/shard_map/add_pieces/pallas_call | solution.py:224
  17.2 0.1 collective-permute-start.10
  17.2 2.0 %collective-permute-done.7.refs_2_.rest_2_ = bf16[128,512]{1,0:T(8,128)(2,1)S(1)} collective-permute-done((bf16[128,512]{1,0:T(8,128)(2,1)S(1)}, bf16[128,512]{1,0:T(8,128)(2,1)S(1)}, u32[]{:S(2)}, u32[]{:S(2)}) %collective-permute-start.7) | collective-permute-done | bytes 131104 | tf_op jit(solution)/shard_map/ppermute | solution.py:39
  19.2 0.6 %collective-permute-done.4.refs_0_.rest_0_ = bf16[128,512]{1,0:T(8,128)(2,1)S(1)} collective-permute-done((bf16[128,512]{1,0:T(8,128)(2,1)S(1)}, bf16[128,512]{1,0:T(8,128)(2,1)S(1)}, u32[]{:S(2)}, u32[]{:S(2)}) %collective-permute-start.4) | collective-permute-done | bytes 131104 | tf_op jit(solution)/shard_map/ppermute | solution.py:29
  19.8 1.3 %collective-permute-done.6.refs_1_.rest_1_ = bf16[128,512]{1,0:T(8,128)(2,1)S(1)} collective-permute-done((bf16[128,512]{1,0:T(8,128)(2,1)S(1)}, bf16[128,512]{1,0:T(8,128)(2,1)S(1)}, u32[]{:S(2)}, u32[]{:S(2)}) %collective-permute-start.6) | collective-permute-done | bytes 131104 | tf_op jit(solution)/shard_map/ppermute | solution.py:29
  21.1 0.1 collective-permute-start.8
  21.2 0.0 collective-permute-done.9.rest_3_
  21.2 0.0 collective-permute-done.10.rest_4_
  21.2 1.8 %add_pieces.6.rest_1_ = f32[256,512]{1,0:T(8,128)S(1)} custom-call(s32[1,128]{1,0:T(1,128)S(1)} %slot_table.1.table_ref, bf16[512,512]{1,0:T(8,128)(2,1)S(1)} %get-tuple-element.21.given_ref, s32[256,1024]{1,0:T(8,128)S(1)} %copy-done.1, bf16[128,512]{1,0:T(8,128)(2,1)S(1)} %collective-permute-done.4.refs_0_.rest_0_, ...), custom_call_target="tpu_custom_call", output_to_operand_aliasing={{}: (8, {})} | custom-call | flops 15032385536 | bytes 1048576 | tf_op jit(solution)/shard_map/add_pieces/pallas_call | solution.py:224
  23.1 0.0 collective-permute-done.8.rest_0_
  23.1 0.2 add_pieces.7
  23.3 10.6 %all_to_all.11 = f32[16,1,128]{2,1,0:T(1,128)S(1)} all-to-all(f32[16,1,128]{2,1,0:T(1,128)S(1)} %bitcast.7), channel_id=1, replica_groups=mesh['group'=2,'loop'=16] {'loop'}, dimensions={0} | all-to-all | bytes 16384 | tf_op jit(solution)/shard_map/all_to_all | solution.py:376
  33.9 0.9 %update.1 = f32[256,512]{1,0:T(8,128)} custom-call(f32[256,512]{1,0:T(8,128)S(1)} %copy-done, f32[256,512]{1,0:T(8,128)S(1)} %get-tuple-element.31.grad_ref, f32[16,128]{1,0:T(8,128)S(1)} %bitcast.6), custom_call_target="tpu_custom_call" | custom-call | flops 262144 | bytes 1572864 | tf_op jit(solution)/shard_map/update/pallas_call | solution.py:377
  (2 shorter events, 0.1 us)
Async XLA Ops:
  0.0 7.0 %collective-permute-start = (bf16[128,512]{1,0:T(8,128)(2,1)}, bf16[128,512]{1,0:T(8,128)(2,1)S(1)}, u32[]{:S(2)}, u32[]{:S(2)}) collective-permute-start(bf16[128,512]{1,0:T(8,128)(2,1)} %refs_0_.1), channel_id=1, source_target_pairs={{0,4},{4,8},{8,12},{12,14},{14,10},{10,6},{6,2},{2,0},{1,3},{5,1},... | collective-permute-start | bytes 393224 | tf_op jit(solution)/shard_map/ppermute | solution.py:29
  3.0 5.5 %collective-permute-start.1 = (bf16[128,512]{1,0:T(8,128)(2,1)}, bf16[128,512]{1,0:T(8,128)(2,1)S(1)}, u32[]{:S(2)}, u32[]{:S(2)}) collective-permute-start(bf16[128,512]{1,0:T(8,128)(2,1)} %refs_0_.1), channel_id=1, source_target_pairs={{0,2},{4,0},{8,4},{12,8},{14,12},{10,14},{6,10},{2,6},{1,5},{5,9},... | collective-permute-start | bytes 393224 | tf_op jit(solution)/shard_map/ppermute | solution.py:29
  3.7 0.7 %copy-start.3 = (s32[1,8]{1,0:T(1,128)S(1)}, s32[1,8]{1,0:T(1,128)}, u32[]{:S(2)}) copy-start(s32[1,8]{1,0:T(1,128)} %list_ref.1) | copy-start | bytes 100
  4.3 5.2 %copy-start.2 = (bf16[128,512]{1,0:T(8,128)(2,1)S(1)}, bf16[128,512]{1,0:T(8,128)(2,1)}, u32[]{:S(2)}) copy-start(bf16[128,512]{1,0:T(8,128)(2,1)} %refs_0_.1) | copy-start | bytes 393220
  4.5 11.1 %copy-start = (f32[256,512]{1,0:T(8,128)S(1)}, f32[256,512]{1,0:T(8,128)}, u32[]{:S(2)}) copy-start(f32[256,512]{1,0:T(8,128)} %users_ref.1) | copy-start | bytes 1572868
  4.5 11.1 %copy-start.1 = (s32[256,1024]{1,0:T(8,128)S(1)}, s32[256,1024]{1,0:T(8,128)}, u32[]{:S(2)}) copy-start(s32[256,1024]{1,0:T(8,128)} %labels_ref.7) | copy-start | bytes 3145732
  7.0 6.5 %collective-permute-start.3 = (bf16[128,512]{1,0:T(8,128)(2,1)S(1)}, bf16[128,512]{1,0:T(8,128)(2,1)S(1)}, u32[]{:S(2)}, u32[]{:S(2)}) collective-permute-start(bf16[128,512]{1,0:T(8,128)(2,1)S(1)} %collective-permute-done.rest_1_.refs_1_), channel_id=1, source_target_pairs={{0,4},{4,8},{8,12},{12,14},{14,10},{10,6},{6,2},{2,0},{1,3},{5,1},... | collective-permute-start | bytes 393224 | tf_op jit(solution)/shard_map/ppermute | solution.py:29
  8.5 7.1 %collective-permute-start.2 = (bf16[128,512]{1,0:T(8,128)(2,1)S(1)}, bf16[128,512]{1,0:T(8,128)(2,1)S(1)}, u32[]{:S(2)}, u32[]{:S(2)}) collective-permute-start(bf16[128,512]{1,0:T(8,128)(2,1)S(1)} %collective-permute-done.1.rest_2_.refs_2_), channel_id=1, source_target_pairs={{0,1},{1,0},{2,3},{3,2},{4,5},{5,4},{6,7},{7,6},{8,9},{9,8},{10,11... | collective-permute-start | bytes 393224 | tf_op jit(solution)/shard_map/ppermute | solution.py:43
  8.5 5.1 %collective-permute-start.5 = (bf16[128,512]{1,0:T(8,128)(2,1)S(1)}, bf16[128,512]{1,0:T(8,128)(2,1)S(1)}, u32[]{:S(2)}, u32[]{:S(2)}) collective-permute-start(bf16[128,512]{1,0:T(8,128)(2,1)S(1)} %collective-permute-done.1.rest_2_.refs_2_), channel_id=1, source_target_pairs={{0,2},{4,0},{8,4},{12,8},{14,12},{10,14},{6,10},{2,6},{1,5},{5,9},... | collective-permute-start | bytes 393224 | tf_op jit(solution)/shard_map/ppermute | solution.py:29
  9.5 9.7 %collective-permute-start.7 = (bf16[128,512]{1,0:T(8,128)(2,1)S(1)}, bf16[128,512]{1,0:T(8,128)(2,1)S(1)}, u32[]{:S(2)}, u32[]{:S(2)}) collective-permute-start(bf16[128,512]{1,0:T(8,128)(2,1)S(1)} %get-tuple-element.22), channel_id=1, source_target_pairs={{0,12},{1,13},{4,6},{5,7},{8,10},{9,11},{12,0},{13,1},{14,2},{15,3... | collective-permute-start | bytes 393224 | tf_op jit(solution)/shard_map/ppermute | solution.py:39
  12.8 8.4 %collective-permute-start.9 = (bf16[256,512]{1,0:T(8,128)(2,1)S(1)}, bf16[256,512]{1,0:T(8,128)(2,1)S(1)}, u32[]{:S(2)}, u32[]{:S(2)}) collective-permute-start(bf16[256,512]{1,0:T(8,128)(2,1)S(1)} %get-tuple-element.28), channel_id=1, source_target_pairs={{0,1},{1,0},{2,3},{3,2},{4,5},{5,4},{6,7},{7,6},{8,9},{9,8},{10,11... | collective-permute-start | bytes 786440 | tf_op jit(solution)/shard_map/ppermute | solution.py:43
  13.5 6.3 %collective-permute-start.4 = (bf16[128,512]{1,0:T(8,128)(2,1)S(1)}, bf16[128,512]{1,0:T(8,128)(2,1)S(1)}, u32[]{:S(2)}, u32[]{:S(2)}) collective-permute-start(bf16[128,512]{1,0:T(8,128)(2,1)S(1)} %collective-permute-done.3.rest_0_), channel_id=1, source_target_pairs={{0,4},{4,8},{8,12},{12,14},{14,10},{10,6},{6,2},{2,0},{1,3},{5,1},... | collective-permute-start | bytes 393224 | tf_op jit(solution)/shard_map/ppermute | solution.py:29
  13.5 7.6 %collective-permute-start.6 = (bf16[128,512]{1,0:T(8,128)(2,1)S(1)}, bf16[128,512]{1,0:T(8,128)(2,1)S(1)}, u32[]{:S(2)}, u32[]{:S(2)}) collective-permute-start(bf16[128,512]{1,0:T(8,128)(2,1)S(1)} %collective-permute-done.5.rest_1_), channel_id=1, source_target_pairs={{0,2},{4,0},{8,4},{12,8},{14,12},{10,14},{6,10},{2,6},{1,5},{5,9},... | collective-permute-start | bytes 393224 | tf_op jit(solution)/shard_map/ppermute | solution.py:29
  17.2 4.1 %collective-permute-start.10 = (bf16[256,512]{1,0:T(8,128)(2,1)S(1)}, bf16[256,512]{1,0:T(8,128)(2,1)S(1)}, u32[]{:S(2)}, u32[]{:S(2)}) collective-permute-start(bf16[256,512]{1,0:T(8,128)(2,1)S(1)} %get-tuple-element.29), channel_id=1, source_target_pairs={{0,1},{1,0},{2,3},{3,2},{4,5},{5,4},{6,7},{7,6},{8,9},{9,8},{10,11... | collective-permute-start | bytes 786440 | tf_op jit(solution)/shard_map/ppermute | solution.py:43
  21.1 2.0 %collective-permute-start.8 = (bf16[384,512]{1,0:T(8,128)(2,1)S(1)}, bf16[384,512]{1,0:T(8,128)(2,1)S(1)}, u32[]{:S(2)}, u32[]{:S(2)}) collective-permute-start(bf16[384,512]{1,0:T(8,128)(2,1)S(1)} %pack.3), channel_id=1, source_target_pairs={{0,1},{1,0},{2,3},{3,2},{4,5},{5,4},{6,7},{7,6},{8,9},{9,8},{10,11... | collective-permute-start | bytes 1179656 | tf_op jit(solution)/shard_map/ppermute | solution.py:43

commit v25 on v16

--- a/solution.py
+++ b/solution.py
@@ -262,11 +262,13 @@
     opposite = across(opposite, loop_size)
     first = other(packed, [0, 1, -1])
     third = [held(3, to_next(second[0][0], 1, loop_size)), held(-3, to_next(second[1][0], -1, loop_size))]
-    gradient, packed = add_pieces(second, [0, 1], loop_size, table, parts, labels, gradient, False)
-    second = other(packed, [2, -2])
-    third.append(held(4, opposite))
+    second.append(held(4, opposite))
+    gradient, packed = add_pieces(
+        second, [0, 1, 2], loop_size, table, parts, labels, gradient, False
+    )
+    second = other(packed, [2, -2, 4])
     arrived, gradient = lax.optimization_barrier(([array for array, _ in third], gradient))
-    final = other(pack(arrived), [3, -3, 4])
+    final = other(pack(arrived), [3, -3])
     (gradient,) = add_pieces(
         third + [first, second], [], loop_size, table, parts, labels, gradient, False
     )

time: 35.4 us -> 35.5 us (level); the launches traced: 35.1 us -> 35.8 us
  blocking collectives: 11.1 us -> 13.2 us
  Pallas kernels: 4.96 us -> 3.05 us
  starting transfers between devices: 9.29 us -> 11 us
  waiting for transfers between devices: 8.33 us -> 7.21 us
    all_to_all x1, blocking collectives: 11.1 us -> 13.2 us  [local(): squares = lax.all_to_all(square, 'loop', 0, 0, tiled=True)]
    pallas_call x4, Pallas kernels: 3.85 us -> 1.95 us  [add_pieces(): pl.pallas_call(functools.partial(pieces_kernel, places, len(arrays), pack...]
    ppermute x1, starting transfers between devices: 2.48 us -> 3.94 us  [across(): return lax.ppermute(array, 'loop', pairs)]
    ppermute x6, waiting for transfers between devices: 6.16 us -> 5.13 us  [to_next(): return lax.ppermute(array, 'loop', pairs)]
  transfers between devices with their start and end apart: 10 -> 10, of which waited for: 7 -> 6; matrix products, arithmetic and copies ran while one was open for 0% -> 0% of each run, Pallas kernels for 9% -> 5%
where the time goes in v25:
time: 35.5 us; the launch traced here: 35.8 us
  blocking collectives  13.2 us (37%)
  starting transfers between devices  11 us (31%)
  waiting for transfers between devices  7.21 us (20%)
  Pallas kernels  3.05 us (9%)
  between operations  0.72 us (2%)
  local copies, waits for them, and re-layouts  0.66 us (2%)
    all_to_all x1, blocking collectives, local(): squares = lax.all_to_all(square, 'loop', 0, 0, tiled=True)  13.2 us
    ppermute x6, starting transfers between devices, to_next(): return lax.ppermute(array, 'loop', pairs)  6.78 us
    ppermute x6, waiting for transfers between devices, to_next(): return lax.ppermute(array, 'loop', pairs)  5.13 us
    ppermute x1, starting transfers between devices, across(): return lax.ppermute(array, 'loop', pairs)  3.94 us
    pallas_call x4, Pallas kernels, add_pieces(): pl.pallas_call(functools.partial(pieces_kernel, places, len(arrays), pack...  1.95 us
    ppermute x1, waiting for transfers between devices, across(): return lax.ppermute(array, 'loop', pairs)  1.42 us
    pallas_call x1, Pallas kernels, local(): pl.pallas_call(functools.partial(update_kernel, rows * loop_size * width)...  0.93 us
  transfers between devices with their start and end apart: 10, of which 6 were waited for; matrix products, arithmetic and copies ran while one was open for 0% of the time, Pallas kernels for 5%

profile of v25, /device:TPU:0, one launch (start us, length us, event | category | flops | bytes accessed | tf_op | source)
XLA Modules:
  0.0 35.8 jit_solution(14708713667259609613)
XLA Ops:
  0.0 3.0 %collective-permute-start = (bf16[128,512]{1,0:T(8,128)(2,1)}, bf16[128,512]{1,0:T(8,128)(2,1)S(1)}, u32[]{:S(2)}, u32[]{:S(2)}) collective-permute-start(bf16[128,512]{1,0:T(8,128)(2,1)} %rest_0_.1), channel_id=1, source_target_pairs={{0,4},{4,8},{8,12},{12,14},{14,10},{10,6},{6,2},{2,0},{1,3},{5,1},... | collective-permute-start | bytes 393224 | tf_op jit(solution)/shard_map/ppermute | solution.py:29
  3.0 0.0 collective-permute-start.1
  3.7 0.0 copy-start.3
  3.7 0.6 %copy-done.3 = s32[1,8]{1,0:T(1,128)S(1)} copy-done((s32[1,8]{1,0:T(1,128)S(1)}, s32[1,8]{1,0:T(1,128)}, u32[]{:S(2)}) %copy-start.3) | copy-done | bytes 56
  4.3 0.0 copy-start
  4.3 0.0 copy-start.1
  4.3 0.0 copy-start.2
  4.3 0.1 slot_table.1.table_ref
  4.5 2.5 %collective-permute-done.rest_1_ = bf16[128,512]{1,0:T(8,128)(2,1)S(1)} collective-permute-done((bf16[128,512]{1,0:T(8,128)(2,1)}, bf16[128,512]{1,0:T(8,128)(2,1)S(1)}, u32[]{:S(2)}, u32[]{:S(2)}) %collective-permute-start) | collective-permute-done | bytes 131104 | tf_op jit(solution)/shard_map/ppermute | solution.py:29
  7.0 1.5 %collective-permute-start.2 = (bf16[128,512]{1,0:T(8,128)(2,1)S(1)}, bf16[128,512]{1,0:T(8,128)(2,1)S(1)}, u32[]{:S(2)}, u32[]{:S(2)}) collective-permute-start(bf16[128,512]{1,0:T(8,128)(2,1)S(1)} %collective-permute-done.rest_1_), channel_id=1, source_target_pairs={{0,4},{4,8},{8,12},{12,14},{14,10},{10,6},{6,2},{2,0},{1,3},{5,1},... | collective-permute-start | bytes 393224 | tf_op jit(solution)/shard_map/ppermute | solution.py:29
  8.5 0.0 collective-permute-done.1.rest_2_
  8.5 0.9 %collective-permute-start.4 = (bf16[128,512]{1,0:T(8,128)(2,1)S(1)}, bf16[128,512]{1,0:T(8,128)(2,1)S(1)}, u32[]{:S(2)}, u32[]{:S(2)}) collective-permute-start(bf16[128,512]{1,0:T(8,128)(2,1)S(1)} %collective-permute-done.1.rest_2_), channel_id=1, source_target_pairs={{0,2},{4,0},{8,4},{12,8},{14,12},{10,14},{6,10},{2,6},{1,5},{5,9},... | collective-permute-start | bytes 393224 | tf_op jit(solution)/shard_map/ppermute | solution.py:29
  9.4 0.0 copy-done
  9.4 0.0 copy-done.1
  9.4 0.0 copy-done.2
  9.4 0.3 add_pieces.4
  9.7 3.9 %collective-permute-start.6 = (bf16[128,512]{1,0:T(8,128)(2,1)S(1)}, bf16[128,512]{1,0:T(8,128)(2,1)S(1)}, u32[]{:S(2)}, u32[]{:S(2)}) collective-permute-start(bf16[128,512]{1,0:T(8,128)(2,1)S(1)} %get-tuple-element.21), channel_id=1, source_target_pairs={{0,12},{1,13},{4,6},{5,7},{8,10},{9,11},{12,0},{13,1},{14,2},{15,3... | collective-permute-start | bytes 393224 | tf_op jit(solution)/shard_map/ppermute | solution.py:39
  13.6 0.0 collective-permute-start.8
  13.6 0.0 collective-permute-done.2.rest_0_
  13.7 0.5 %collective-permute-start.3 = (bf16[128,512]{1,0:T(8,128)(2,1)S(1)}, bf16[128,512]{1,0:T(8,128)(2,1)S(1)}, u32[]{:S(2)}, u32[]{:S(2)}) collective-permute-start(bf16[128,512]{1,0:T(8,128)(2,1)S(1)} %collective-permute-done.2.rest_0_), channel_id=1, source_target_pairs={{0,4},{4,8},{8,12},{12,14},{14,10},{10,6},{6,2},{2,0},{1,3},{5,1},... | collective-permute-start | bytes 393224 | tf_op jit(solution)/shard_map/ppermute | solution.py:29
  14.2 0.7 %collective-permute-done.4.rest_1_ = bf16[128,512]{1,0:T(8,128)(2,1)S(1)} collective-permute-done((bf16[128,512]{1,0:T(8,128)(2,1)S(1)}, bf16[128,512]{1,0:T(8,128)(2,1)S(1)}, u32[]{:S(2)}, u32[]{:S(2)}) %collective-permute-start.4) | collective-permute-done | bytes 131104 | tf_op jit(solution)/shard_map/ppermute | solution.py:29
  14.9 0.8 %collective-permute-start.5 = (bf16[128,512]{1,0:T(8,128)(2,1)S(1)}, bf16[128,512]{1,0:T(8,128)(2,1)S(1)}, u32[]{:S(2)}, u32[]{:S(2)}) collective-permute-start(bf16[128,512]{1,0:T(8,128)(2,1)S(1)} %collective-permute-done.4.rest_1_), channel_id=1, source_target_pairs={{0,2},{4,0},{8,4},{12,8},{14,12},{10,14},{6,10},{2,6},{1,5},{5,9},... | collective-permute-start | bytes 393224 | tf_op jit(solution)/shard_map/ppermute | solution.py:29
  15.7 1.4 %collective-permute-done.6.rest_2_ = bf16[128,512]{1,0:T(8,128)(2,1)S(1)} collective-permute-done((bf16[128,512]{1,0:T(8,128)(2,1)S(1)}, bf16[128,512]{1,0:T(8,128)(2,1)S(1)}, u32[]{:S(2)}, u32[]{:S(2)}) %collective-permute-start.6) | collective-permute-done | bytes 131104 | tf_op jit(solution)/shard_map/ppermute | solution.py:39
  17.1 0.7 %add_pieces.5 = (f32[256,512]{1,0:T(8,128)S(1)}, bf16[384,512]{1,0:T(8,128)(2,1)S(1)}) custom-call(s32[1,128]{1,0:T(1,128)S(1)} %slot_table.1.table_ref, bf16[512,512]{1,0:T(8,128)(2,1)S(1)} %get-tuple-element.20.given_ref, s32[256,1024]{1,0:T(8,128)S(1)} %copy-done.1, ...), custom_call_target="tpu_custom_call", output_to_operand_aliasing={{0}: (6, {})} | custom-call | flops 6442450944 | bytes 1048576 | tf_op jit(solution)/shard_map/add_pieces/pallas_call | solution.py:220
  17.8 0.1 collective-permute-start.9
  17.9 1.3 %collective-permute-done.3.refs_0_.rest_0_ = bf16[128,512]{1,0:T(8,128)(2,1)S(1)} collective-permute-done((bf16[128,512]{1,0:T(8,128)(2,1)S(1)}, bf16[128,512]{1,0:T(8,128)(2,1)S(1)}, u32[]{:S(2)}, u32[]{:S(2)}) %collective-permute-start.3) | collective-permute-done | bytes 131104 | tf_op jit(solution)/shard_map/ppermute | solution.py:29
  19.2 0.6 %collective-permute-done.5.refs_1_.rest_1_ = bf16[128,512]{1,0:T(8,128)(2,1)S(1)} collective-permute-done((bf16[128,512]{1,0:T(8,128)(2,1)S(1)}, bf16[128,512]{1,0:T(8,128)(2,1)S(1)}, u32[]{:S(2)}, u32[]{:S(2)}) %collective-permute-start.5) | collective-permute-done | bytes 131104 | tf_op jit(solution)/shard_map/ppermute | solution.py:29
  19.9 0.2 collective-permute-start.7
  20.1 0.0 collective-permute-done.8.rest_2_
  20.1 0.0 collective-permute-done.9.rest_3_
  20.1 0.7 %add_pieces.6.rest_1_ = f32[256,512]{1,0:T(8,128)S(1)} custom-call(s32[1,128]{1,0:T(1,128)S(1)} %slot_table.1.table_ref, bf16[512,512]{1,0:T(8,128)(2,1)S(1)} %get-tuple-element.20.given_ref, s32[256,1024]{1,0:T(8,128)S(1)} %copy-done.1, bf16[128,512]{1,0:T(8,128)(2,1)S(1)} %collective-permute-done.3.refs_0_.rest_0_, ...), custom_call_target="tpu_custom_call", output_to_operand_aliasing={{}: (7, {})} | custom-call | flops 17179869184 | bytes 1048576 | tf_op jit(solution)/shard_map/add_pieces/pallas_call | solution.py:220
  20.8 0.7 %collective-permute-done.7.rest_0_ = bf16[256,512]{1,0:T(8,128)(2,1)S(1)} collective-permute-done((bf16[256,512]{1,0:T(8,128)(2,1)S(1)}, bf16[256,512]{1,0:T(8,128)(2,1)S(1)}, u32[]{:S(2)}, u32[]{:S(2)}) %collective-permute-start.7) | collective-permute-done | bytes 262176 | tf_op jit(solution)/shard_map/ppermute | solution.py:43
  21.5 0.2 add_pieces.7
  21.7 13.2 %all_to_all.11 = f32[16,1,128]{2,1,0:T(1,128)S(1)} all-to-all(f32[16,1,128]{2,1,0:T(1,128)S(1)} %bitcast.7), channel_id=1, replica_groups=mesh['group'=2,'loop'=16] {'loop'}, dimensions={0} | all-to-all | bytes 16384 | tf_op jit(solution)/shard_map/all_to_all | solution.py:374
  34.8 0.9 %update.1 = f32[256,512]{1,0:T(8,128)} custom-call(f32[256,512]{1,0:T(8,128)S(1)} %copy-done, f32[256,512]{1,0:T(8,128)S(1)} %get-tuple-element.29.grad_ref, f32[16,128]{1,0:T(8,128)S(1)} %bitcast.6), custom_call_target="tpu_custom_call" | custom-call | flops 262144 | bytes 1572864 | tf_op jit(solution)/shard_map/update/pallas_call | solution.py:375
  (1 shorter events, 0.0 us)
Async XLA Ops:
  0.0 7.0 %collective-permute-start = (bf16[128,512]{1,0:T(8,128)(2,1)}, bf16[128,512]{1,0:T(8,128)(2,1)S(1)}, u32[]{:S(2)}, u32[]{:S(2)}) collective-permute-start(bf16[128,512]{1,0:T(8,128)(2,1)} %rest_0_.1), channel_id=1, source_target_pairs={{0,4},{4,8},{8,12},{12,14},{14,10},{10,6},{6,2},{2,0},{1,3},{5,1},... | collective-permute-start | bytes 393224 | tf_op jit(solution)/shard_map/ppermute | solution.py:29
  3.0 5.5 %collective-permute-start.1 = (bf16[128,512]{1,0:T(8,128)(2,1)}, bf16[128,512]{1,0:T(8,128)(2,1)S(1)}, u32[]{:S(2)}, u32[]{:S(2)}) collective-permute-start(bf16[128,512]{1,0:T(8,128)(2,1)} %rest_0_.1), channel_id=1, source_target_pairs={{0,2},{4,0},{8,4},{12,8},{14,12},{10,14},{6,10},{2,6},{1,5},{5,9},... | collective-permute-start | bytes 393224 | tf_op jit(solution)/shard_map/ppermute | solution.py:29
  3.7 0.7 %copy-start.3 = (s32[1,8]{1,0:T(1,128)S(1)}, s32[1,8]{1,0:T(1,128)}, u32[]{:S(2)}) copy-start(s32[1,8]{1,0:T(1,128)} %list_ref.1) | copy-start | bytes 100
  4.3 5.1 %copy-start = (f32[256,512]{1,0:T(8,128)S(1)}, f32[256,512]{1,0:T(8,128)}, u32[]{:S(2)}) copy-start(f32[256,512]{1,0:T(8,128)} %users_ref.1) | copy-start | bytes 1572868
  4.3 5.1 %copy-start.1 = (s32[256,1024]{1,0:T(8,128)S(1)}, s32[256,1024]{1,0:T(8,128)}, u32[]{:S(2)}) copy-start(s32[256,1024]{1,0:T(8,128)} %labels_ref.7) | copy-start | bytes 3145732
  4.3 5.1 %copy-start.2 = (bf16[128,512]{1,0:T(8,128)(2,1)S(1)}, bf16[128,512]{1,0:T(8,128)(2,1)}, u32[]{:S(2)}) copy-start(bf16[128,512]{1,0:T(8,128)(2,1)} %rest_0_.1) | copy-start | bytes 393220
  7.0 6.7 %collective-permute-start.2 = (bf16[128,512]{1,0:T(8,128)(2,1)S(1)}, bf16[128,512]{1,0:T(8,128)(2,1)S(1)}, u32[]{:S(2)}, u32[]{:S(2)}) collective-permute-start(bf16[128,512]{1,0:T(8,128)(2,1)S(1)} %collective-permute-done.rest_1_), channel_id=1, source_target_pairs={{0,4},{4,8},{8,12},{12,14},{14,10},{10,6},{6,2},{2,0},{1,3},{5,1},... | collective-permute-start | bytes 393224 | tf_op jit(solution)/shard_map/ppermute | solution.py:29
  8.5 6.4 %collective-permute-start.4 = (bf16[128,512]{1,0:T(8,128)(2,1)S(1)}, bf16[128,512]{1,0:T(8,128)(2,1)S(1)}, u32[]{:S(2)}, u32[]{:S(2)}) collective-permute-start(bf16[128,512]{1,0:T(8,128)(2,1)S(1)} %collective-permute-done.1.rest_2_), channel_id=1, source_target_pairs={{0,2},{4,0},{8,4},{12,8},{14,12},{10,14},{6,10},{2,6},{1,5},{5,9},... | collective-permute-start | bytes 393224 | tf_op jit(solution)/shard_map/ppermute | solution.py:29
  9.7 7.4 %collective-permute-start.6 = (bf16[128,512]{1,0:T(8,128)(2,1)S(1)}, bf16[128,512]{1,0:T(8,128)(2,1)S(1)}, u32[]{:S(2)}, u32[]{:S(2)}) collective-permute-start(bf16[128,512]{1,0:T(8,128)(2,1)S(1)} %get-tuple-element.21), channel_id=1, source_target_pairs={{0,12},{1,13},{4,6},{5,7},{8,10},{9,11},{12,0},{13,1},{14,2},{15,3... | collective-permute-start | bytes 393224 | tf_op jit(solution)/shard_map/ppermute | solution.py:39
  13.6 6.4 %collective-permute-start.8 = (bf16[384,512]{1,0:T(8,128)(2,1)S(1)}, bf16[384,512]{1,0:T(8,128)(2,1)S(1)}, u32[]{:S(2)}, u32[]{:S(2)}) collective-permute-start(bf16[384,512]{1,0:T(8,128)(2,1)S(1)} %get-tuple-element.26), channel_id=1, source_target_pairs={{0,1},{1,0},{2,3},{3,2},{4,5},{5,4},{6,7},{7,6},{8,9},{9,8},{10,11... | collective-permute-start | bytes 1179656 | tf_op jit(solution)/shard_map/ppermute | solution.py:43
  13.7 5.6 %collective-permute-start.3 = (bf16[128,512]{1,0:T(8,128)(2,1)S(1)}, bf16[128,512]{1,0:T(8,128)(2,1)S(1)}, u32[]{:S(2)}, u32[]{:S(2)}) collective-permute-start(bf16[128,512]{1,0:T(8,128)(2,1)S(1)} %collective-permute-done.2.rest_0_), channel_id=1, source_target_pairs={{0,4},{4,8},{8,12},{12,14},{14,10},{10,6},{6,2},{2,0},{1,3},{5,1},... | collective-permute-start | bytes 393224 | tf_op jit(solution)/shard_map/ppermute | solution.py:29
  14.9 5.0 %collective-permute-start.5 = (bf16[128,512]{1,0:T(8,128)(2,1)S(1)}, bf16[128,512]{1,0:T(8,128)(2,1)S(1)}, u32[]{:S(2)}, u32[]{:S(2)}) collective-permute-start(bf16[128,512]{1,0:T(8,128)(2,1)S(1)} %collective-permute-done.4.rest_1_), channel_id=1, source_target_pairs={{0,2},{4,0},{8,4},{12,8},{14,12},{10,14},{6,10},{2,6},{1,5},{5,9},... | collective-permute-start | bytes 393224 | tf_op jit(solution)/shard_map/ppermute | solution.py:29
  17.8 2.2 %collective-permute-start.9 = (bf16[384,512]{1,0:T(8,128)(2,1)S(1)}, bf16[384,512]{1,0:T(8,128)(2,1)S(1)}, u32[]{:S(2)}, u32[]{:S(2)}) collective-permute-start(bf16[384,512]{1,0:T(8,128)(2,1)S(1)} %get-tuple-element.27), channel_id=1, source_target_pairs={{0,1},{1,0},{2,3},{3,2},{4,5},{5,4},{6,7},{7,6},{8,9},{9,8},{10,11... | collective-permute-start | bytes 1179656 | tf_op jit(solution)/shard_map/ppermute | solution.py:43
  19.9 1.6 %collective-permute-start.7 = (bf16[256,512]{1,0:T(8,128)(2,1)S(1)}, bf16[256,512]{1,0:T(8,128)(2,1)S(1)}, u32[]{:S(2)}, u32[]{:S(2)}) collective-permute-start(bf16[256,512]{1,0:T(8,128)(2,1)S(1)} %pack.1), channel_id=1, source_target_pairs={{0,1},{1,0},{2,3},{3,2},{4,5},{5,4},{6,7},{7,6},{8,9},{9,8},{10,11... | collective-permute-start | bytes 786440 | tf_op jit(solution)/shard_map/ppermute | solution.py:43

commit v26 on v16

--- a/solution.py
+++ b/solution.py
@@ -215,7 +215,7 @@
     if packed:
         out_shape.append(jax.ShapeDtypeStruct((len(packed) * tile, width), jnp.bfloat16))
     if last:
-        out_shape.append(jax.ShapeDtypeStruct((loop_size, 128), jnp.float32))
+        out_shape.append(jax.ShapeDtypeStruct((8 * loop_size, 128), jnp.float32))
     extra = [] if first else [before]
     return pl.pallas_call(
         functools.partial(pieces_kernel, places, len(arrays), packed, loop_size, first, last),
@@ -315,7 +315,7 @@
         grid=(slots // CHUNK,),
         out_shape=[
             jax.ShapeDtypeStruct((rows, width), jnp.float32),
-            jax.ShapeDtypeStruct((loop_size, 128), jnp.float32),
+            jax.ShapeDtypeStruct((8 * loop_size, 128), jnp.float32),
         ],
         in_specs=[
             pl.BlockSpec(memory_space=pltpu.SMEM),
@@ -326,7 +326,7 @@
         ],
         out_specs=[
             pl.BlockSpec((rows, width), lambda step: (0, 0)),
-            pl.BlockSpec((loop_size, 128), lambda step: (0, 0)),
+            pl.BlockSpec((8 * loop_size, 128), lambda step: (0, 0)),
         ],
         scratch_shapes=[
             pltpu.VMEM((CHUNK * tile, width), jnp.bfloat16),
@@ -344,7 +344,7 @@
 
 
 def update_kernel(entries, users_ref, grad_ref, squares_ref, out_ref, result, sems):
-    total = jnp.sum(squares_ref[...], axis=0, keepdims=True)
+    total = jnp.sum(squares_ref[...], axis=0, keepdims=True) / 8
     total = jnp.sum(total, axis=1, keepdims=True)
     scale = 0.5 / jnp.sqrt(total / entries + 1e-06)
     rows = users_ref.shape[0] // sems.shape[0]

time: 35.4 us -> 35.6 us (level)
  Pallas kernels: 4.96 us -> 2.5 us
  starting transfers between devices: 9.29 us -> 11 us
  blocking collectives: 11.1 us -> 12.5 us
    pallas_call x4, Pallas kernels: 3.85 us -> 1.38 us  [add_pieces(): pl.pallas_call(functools.partial(pieces_kernel, places, len(arrays), pack...]
    ppermute x1, starting transfers between devices: 2.48 us -> 4.16 us  [across(): return lax.ppermute(array, 'loop', pairs)]
    all_to_all x1, blocking collectives: 11.1 us -> 12.5 us  [local(): squares = lax.all_to_all(square, 'loop', 0, 0, tiled=True)]
    ppermute x1, waiting for transfers between devices: 1.45 us -> 0.5 us  [across(): return lax.ppermute(array, 'loop', pairs)]
    ppermute x3, waiting for transfers between devices: 0.72 us -> 1.37 us  [to_other_core(): lax.ppermute(array, 'loop', [(at, at ^ 1) for at in range(loop_size)])]
  transfers between devices with their start and end apart: 10 -> 10, of which waited for: 7 -> 6; matrix products, arithmetic and copies ran while one was open for 0% -> 0% of each run, Pallas kernels for 9% -> 4%
where the time goes in v26:
time: 35.6 us; the launch traced here: 35.4 us
  blocking collectives  12.5 us (35%)
  starting transfers between devices  11 us (31%)
  waiting for transfers between devices  8.04 us (23%)
  Pallas kernels  2.5 us (7%)
  between operations  0.72 us (2%)
  local copies, waits for them, and re-layouts  0.66 us (2%)
    all_to_all x1, blocking collectives, local(): squares = lax.all_to_all(square, 'loop', 0, 0, tiled=True)  12.5 us
    ppermute x6, starting transfers between devices, to_next(): return lax.ppermute(array, 'loop', pairs)  6.48 us
    ppermute x6, waiting for transfers between devices, to_next(): return lax.ppermute(array, 'loop', pairs)  6.17 us
    ppermute x1, starting transfers between devices, across(): return lax.ppermute(array, 'loop', pairs)  4.16 us
    pallas_call x4, Pallas kernels, add_pieces(): pl.pallas_call(functools.partial(pieces_kernel, places, len(arrays), pack...  1.38 us
    ppermute x3, waiting for transfers between devices, to_other_core(): lax.ppermute(array, 'loop', [(at, at ^ 1) for at in range(loop_size)])  1.37 us
    pallas_call x1, Pallas kernels, local(): pl.pallas_call(functools.partial(update_kernel, rows * loop_size * width)...  0.95 us
  transfers between devices with their start and end apart: 10, of which 6 were waited for; matrix products, arithmetic and copies ran while one was open for 0% of the time, Pallas kernels for 4%

profile of v26, /device:TPU:0, one launch (start us, length us, event | category | flops | bytes accessed | tf_op | source)
XLA Modules:
  0.0 35.4 jit_solution(12751401898895858806)
XLA Ops:
  0.0 3.0 %collective-permute-start = (bf16[128,512]{1,0:T(8,128)(2,1)}, bf16[128,512]{1,0:T(8,128)(2,1)S(1)}, u32[]{:S(2)}, u32[]{:S(2)}) collective-permute-start(bf16[128,512]{1,0:T(8,128)(2,1)} %rest_0_.1), channel_id=1, source_target_pairs={{0,4},{4,8},{8,12},{12,14},{14,10},{10,6},{6,2},{2,0},{1,3},{5,1},... | collective-permute-start | bytes 393224 | tf_op jit(solution)/shard_map/ppermute | solution.py:29
  3.0 0.0 collective-permute-start.1
  3.7 0.0 copy-start.3
  3.7 0.6 %copy-done.3 = s32[1,8]{1,0:T(1,128)S(1)} copy-done((s32[1,8]{1,0:T(1,128)S(1)}, s32[1,8]{1,0:T(1,128)}, u32[]{:S(2)}) %copy-start.3) | copy-done | bytes 56
  4.3 0.0 copy-start
  4.3 0.0 copy-start.1
  4.3 0.0 copy-start.2
  4.3 0.1 slot_table.1.table_ref
  4.5 2.5 %collective-permute-done.rest_1_ = bf16[128,512]{1,0:T(8,128)(2,1)S(1)} collective-permute-done((bf16[128,512]{1,0:T(8,128)(2,1)}, bf16[128,512]{1,0:T(8,128)(2,1)S(1)}, u32[]{:S(2)}, u32[]{:S(2)}) %collective-permute-start) | collective-permute-done | bytes 131104 | tf_op jit(solution)/shard_map/ppermute | solution.py:29
  7.0 1.5 %collective-permute-start.2 = (bf16[128,512]{1,0:T(8,128)(2,1)S(1)}, bf16[128,512]{1,0:T(8,128)(2,1)S(1)}, u32[]{:S(2)}, u32[]{:S(2)}) collective-permute-start(bf16[128,512]{1,0:T(8,128)(2,1)S(1)} %collective-permute-done.rest_1_), channel_id=1, source_target_pairs={{0,4},{4,8},{8,12},{12,14},{14,10},{10,6},{6,2},{2,0},{1,3},{5,1},... | collective-permute-start | bytes 393224 | tf_op jit(solution)/shard_map/ppermute | solution.py:29
  8.5 0.0 collective-permute-done.1.rest_2_
  8.5 0.9 %collective-permute-start.4 = (bf16[128,512]{1,0:T(8,128)(2,1)S(1)}, bf16[128,512]{1,0:T(8,128)(2,1)S(1)}, u32[]{:S(2)}, u32[]{:S(2)}) collective-permute-start(bf16[128,512]{1,0:T(8,128)(2,1)S(1)} %collective-permute-done.1.rest_2_), channel_id=1, source_target_pairs={{0,2},{4,0},{8,4},{12,8},{14,12},{10,14},{6,10},{2,6},{1,5},{5,9},... | collective-permute-start | bytes 393224 | tf_op jit(solution)/shard_map/ppermute | solution.py:29
  9.4 0.0 copy-done
  9.4 0.0 copy-done.1
  9.4 0.0 copy-done.2
  9.4 0.3 add_pieces.4
  9.7 4.2 %collective-permute-start.6 = (bf16[128,512]{1,0:T(8,128)(2,1)S(1)}, bf16[128,512]{1,0:T(8,128)(2,1)S(1)}, u32[]{:S(2)}, u32[]{:S(2)}) collective-permute-start(bf16[128,512]{1,0:T(8,128)(2,1)S(1)} %get-tuple-element.22), channel_id=1, source_target_pairs={{0,12},{1,13},{4,6},{5,7},{8,10},{9,11},{12,0},{13,1},{14,2},{15,3... | collective-permute-start | bytes 393224 | tf_op jit(solution)/shard_map/ppermute | solution.py:39
  13.9 0.0 collective-permute-start.8
  13.9 0.0 collective-permute-done.2.rest_0_
  13.9 0.0 collective-permute-start.3
  13.9 1.0 %collective-permute-done.4.rest_1_ = bf16[128,512]{1,0:T(8,128)(2,1)S(1)} collective-permute-done((bf16[128,512]{1,0:T(8,128)(2,1)S(1)}, bf16[128,512]{1,0:T(8,128)(2,1)S(1)}, u32[]{:S(2)}, u32[]{:S(2)}) %collective-permute-start.4) | collective-permute-done | bytes 131104 | tf_op jit(solution)/shard_map/ppermute | solution.py:29
  14.9 1.0 %collective-permute-start.5 = (bf16[128,512]{1,0:T(8,128)(2,1)S(1)}, bf16[128,512]{1,0:T(8,128)(2,1)S(1)}, u32[]{:S(2)}, u32[]{:S(2)}) collective-permute-start(bf16[128,512]{1,0:T(8,128)(2,1)S(1)} %collective-permute-done.4.rest_1_), channel_id=1, source_target_pairs={{0,2},{4,0},{8,4},{12,8},{14,12},{10,14},{6,10},{2,6},{1,5},{5,9},... | collective-permute-start | bytes 393224 | tf_op jit(solution)/shard_map/ppermute | solution.py:29
  15.9 0.7 %add_pieces.5 = (f32[256,512]{1,0:T(8,128)S(1)}, bf16[256,512]{1,0:T(8,128)(2,1)S(1)}) custom-call(s32[1,128]{1,0:T(1,128)S(1)} %slot_table.1.table_ref, bf16[512,512]{1,0:T(8,128)(2,1)S(1)} %get-tuple-element.21.given_ref, s32[256,1024]{1,0:T(8,128)S(1)} %copy-done.1, ...), custom_call_target="tpu_custom_call", output_to_operand_aliasing={{0}: (5, {})} | custom-call | flops 4294967296 | bytes 1048576 | tf_op jit(solution)/shard_map/add_pieces/pallas_call | solution.py:220
  16.6 0.1 collective-permute-start.9
  16.7 0.5 %collective-permute-done.6.refs_2_.rest_2_ = bf16[128,512]{1,0:T(8,128)(2,1)S(1)} collective-permute-done((bf16[128,512]{1,0:T(8,128)(2,1)S(1)}, bf16[128,512]{1,0:T(8,128)(2,1)S(1)}, u32[]{:S(2)}, u32[]{:S(2)}) %collective-permute-start.6) | collective-permute-done | bytes 131104 | tf_op jit(solution)/shard_map/ppermute | solution.py:39
  17.2 2.2 %collective-permute-done.3.refs_0_.rest_0_ = bf16[128,512]{1,0:T(8,128)(2,1)S(1)} collective-permute-done((bf16[128,512]{1,0:T(8,128)(2,1)S(1)}, bf16[128,512]{1,0:T(8,128)(2,1)S(1)}, u32[]{:S(2)}, u32[]{:S(2)}) %collective-permute-start.3) | collective-permute-done | bytes 131104 | tf_op jit(solution)/shard_map/ppermute | solution.py:29
  19.4 0.5 %collective-permute-done.5.refs_1_.rest_1_ = bf16[128,512]{1,0:T(8,128)(2,1)S(1)} collective-permute-done((bf16[128,512]{1,0:T(8,128)(2,1)S(1)}, bf16[128,512]{1,0:T(8,128)(2,1)S(1)}, u32[]{:S(2)}, u32[]{:S(2)}) %collective-permute-start.5) | collective-permute-done | bytes 131104 | tf_op jit(solution)/shard_map/ppermute | solution.py:29
  19.9 0.2 collective-permute-start.7
  20.2 0.0 collective-permute-done.9.rest_4_
  20.2 0.0 collective-permute-done.8.rest_3_
  20.2 0.2 add_pieces.6.rest_1_
  20.3 1.4 %collective-permute-done.7.rest_0_ = bf16[384,512]{1,0:T(8,128)(2,1)S(1)} collective-permute-done((bf16[384,512]{1,0:T(8,128)(2,1)S(1)}, bf16[384,512]{1,0:T(8,128)(2,1)S(1)}, u32[]{:S(2)}, u32[]{:S(2)}) %collective-permute-start.7) | collective-permute-done | bytes 393248 | tf_op jit(solution)/shard_map/ppermute | solution.py:43
  21.7 0.2 add_pieces.7
  21.9 12.5 %all_to_all.11 = f32[16,8,128]{2,1,0:T(8,128)S(1)} all-to-all(f32[16,8,128]{2,1,0:T(8,128)S(1)} %bitcast.5), channel_id=1, replica_groups=mesh['group'=2,'loop'=16] {'loop'}, dimensions={0} | all-to-all | bytes 131072 | tf_op jit(solution)/shard_map/all_to_all | solution.py:372
  34.5 0.9 %update.1 = f32[256,512]{1,0:T(8,128)} custom-call(f32[256,512]{1,0:T(8,128)S(1)} %copy-done, f32[256,512]{1,0:T(8,128)S(1)} %get-tuple-element.31.grad_ref, f32[128,128]{1,0:T(8,128)S(1)} %bitcast.4), custom_call_target="tpu_custom_call" | custom-call | flops 262144 | bytes 1572864 | tf_op jit(solution)/shard_map/update/pallas_call | solution.py:373
  (1 shorter events, 0.0 us)
Async XLA Ops:
  0.0 7.0 %collective-permute-start = (bf16[128,512]{1,0:T(8,128)(2,1)}, bf16[128,512]{1,0:T(8,128)(2,1)S(1)}, u32[]{:S(2)}, u32[]{:S(2)}) collective-permute-start(bf16[128,512]{1,0:T(8,128)(2,1)} %rest_0_.1), channel_id=1, source_target_pairs={{0,4},{4,8},{8,12},{12,14},{14,10},{10,6},{6,2},{2,0},{1,3},{5,1},... | collective-permute-start | bytes 393224 | tf_op jit(solution)/shard_map/ppermute | solution.py:29
  3.0 5.5 %collective-permute-start.1 = (bf16[128,512]{1,0:T(8,128)(2,1)}, bf16[128,512]{1,0:T(8,128)(2,1)S(1)}, u32[]{:S(2)}, u32[]{:S(2)}) collective-permute-start(bf16[128,512]{1,0:T(8,128)(2,1)} %rest_0_.1), channel_id=1, source_target_pairs={{0,2},{4,0},{8,4},{12,8},{14,12},{10,14},{6,10},{2,6},{1,5},{5,9},... | collective-permute-start | bytes 393224 | tf_op jit(solution)/shard_map/ppermute | solution.py:29
  3.7 0.7 %copy-start.3 = (s32[1,8]{1,0:T(1,128)S(1)}, s32[1,8]{1,0:T(1,128)}, u32[]{:S(2)}) copy-start(s32[1,8]{1,0:T(1,128)} %list_ref.1) | copy-start | bytes 100
  4.3 5.1 %copy-start = (f32[256,512]{1,0:T(8,128)S(1)}, f32[256,512]{1,0:T(8,128)}, u32[]{:S(2)}) copy-start(f32[256,512]{1,0:T(8,128)} %users_ref.1) | copy-start | bytes 1572868
  4.3 5.1 %copy-start.1 = (s32[256,1024]{1,0:T(8,128)S(1)}, s32[256,1024]{1,0:T(8,128)}, u32[]{:S(2)}) copy-start(s32[256,1024]{1,0:T(8,128)} %labels_ref.7) | copy-start | bytes 3145732
  4.3 5.1 %copy-start.2 = (bf16[128,512]{1,0:T(8,128)(2,1)S(1)}, bf16[128,512]{1,0:T(8,128)(2,1)}, u32[]{:S(2)}) copy-start(bf16[128,512]{1,0:T(8,128)(2,1)} %rest_0_.1) | copy-start | bytes 393220
  7.0 6.9 %collective-permute-start.2 = (bf16[128,512]{1,0:T(8,128)(2,1)S(1)}, bf16[128,512]{1,0:T(8,128)(2,1)S(1)}, u32[]{:S(2)}, u32[]{:S(2)}) collective-permute-start(bf16[128,512]{1,0:T(8,128)(2,1)S(1)} %collective-permute-done.rest_1_), channel_id=1, source_target_pairs={{0,4},{4,8},{8,12},{12,14},{14,10},{10,6},{6,2},{2,0},{1,3},{5,1},... | collective-permute-start | bytes 393224 | tf_op jit(solution)/shard_map/ppermute | solution.py:29
  8.5 6.4 %collective-permute-start.4 = (bf16[128,512]{1,0:T(8,128)(2,1)S(1)}, bf16[128,512]{1,0:T(8,128)(2,1)S(1)}, u32[]{:S(2)}, u32[]{:S(2)}) collective-permute-start(bf16[128,512]{1,0:T(8,128)(2,1)S(1)} %collective-permute-done.1.rest_2_), channel_id=1, source_target_pairs={{0,2},{4,0},{8,4},{12,8},{14,12},{10,14},{6,10},{2,6},{1,5},{5,9},... | collective-permute-start | bytes 393224 | tf_op jit(solution)/shard_map/ppermute | solution.py:29
  9.7 7.5 %collective-permute-start.6 = (bf16[128,512]{1,0:T(8,128)(2,1)S(1)}, bf16[128,512]{1,0:T(8,128)(2,1)S(1)}, u32[]{:S(2)}, u32[]{:S(2)}) collective-permute-start(bf16[128,512]{1,0:T(8,128)(2,1)S(1)} %get-tuple-element.22), channel_id=1, source_target_pairs={{0,12},{1,13},{4,6},{5,7},{8,10},{9,11},{12,0},{13,1},{14,2},{15,3... | collective-permute-start | bytes 393224 | tf_op jit(solution)/shard_map/ppermute | solution.py:39
  13.9 6.3 %collective-permute-start.8 = (bf16[384,512]{1,0:T(8,128)(2,1)S(1)}, bf16[384,512]{1,0:T(8,128)(2,1)S(1)}, u32[]{:S(2)}, u32[]{:S(2)}) collective-permute-start(bf16[384,512]{1,0:T(8,128)(2,1)S(1)} %get-tuple-element.28), channel_id=1, source_target_pairs={{0,1},{1,0},{2,3},{3,2},{4,5},{5,4},{6,7},{7,6},{8,9},{9,8},{10,11... | collective-permute-start | bytes 1179656 | tf_op jit(solution)/shard_map/ppermute | solution.py:43
  13.9 5.6 %collective-permute-start.3 = (bf16[128,512]{1,0:T(8,128)(2,1)S(1)}, bf16[128,512]{1,0:T(8,128)(2,1)S(1)}, u32[]{:S(2)}, u32[]{:S(2)}) collective-permute-start(bf16[128,512]{1,0:T(8,128)(2,1)S(1)} %collective-permute-done.2.rest_0_), channel_id=1, source_target_pairs={{0,4},{4,8},{8,12},{12,14},{14,10},{10,6},{6,2},{2,0},{1,3},{5,1},... | collective-permute-start | bytes 393224 | tf_op jit(solution)/shard_map/ppermute | solution.py:29
  14.9 5.0 %collective-permute-start.5 = (bf16[128,512]{1,0:T(8,128)(2,1)S(1)}, bf16[128,512]{1,0:T(8,128)(2,1)S(1)}, u32[]{:S(2)}, u32[]{:S(2)}) collective-permute-start(bf16[128,512]{1,0:T(8,128)(2,1)S(1)} %collective-permute-done.4.rest_1_), channel_id=1, source_target_pairs={{0,2},{4,0},{8,4},{12,8},{14,12},{10,14},{6,10},{2,6},{1,5},{5,9},... | collective-permute-start | bytes 393224 | tf_op jit(solution)/shard_map/ppermute | solution.py:29
  16.6 3.5 %collective-permute-start.9 = (bf16[256,512]{1,0:T(8,128)(2,1)S(1)}, bf16[256,512]{1,0:T(8,128)(2,1)S(1)}, u32[]{:S(2)}, u32[]{:S(2)}) collective-permute-start(bf16[256,512]{1,0:T(8,128)(2,1)S(1)} %get-tuple-element.29), channel_id=1, source_target_pairs={{0,1},{1,0},{2,3},{3,2},{4,5},{5,4},{6,7},{7,6},{8,9},{9,8},{10,11... | collective-permute-start | bytes 786440 | tf_op jit(solution)/shard_map/ppermute | solution.py:43
  19.9 1.8 %collective-permute-start.7 = (bf16[384,512]{1,0:T(8,128)(2,1)S(1)}, bf16[384,512]{1,0:T(8,128)(2,1)S(1)}, u32[]{:S(2)}, u32[]{:S(2)}) collective-permute-start(bf16[384,512]{1,0:T(8,128)(2,1)S(1)} %pack.1), channel_id=1, source_target_pairs={{0,1},{1,0},{2,3},{3,2},{4,5},{5,4},{6,7},{7,6},{8,9},{9,8},{10,11... | collective-permute-start | bytes 1179656 | tf_op jit(solution)/shard_map/ppermute | solution.py:43

commit v27 on v18

--- a/solution.py
+++ b/solution.py
@@ -16,7 +16,7 @@
 
     def device(position, core):
         position = position % (2 * outer)
-        chip = 2 * position if position < outer else 2 * (2 * outer - 1 - position) + 1
+        chip = 2 * (outer - 1 - position) if position < outer else 2 * (position - outer) + 1
         return 2 * chip + core
 
     return 2 * outer, device
@@ -57,7 +57,7 @@
         hops = jnp.where(lane == at, origin[0], hops)
         other = jnp.where(lane == at, origin[1], other)
     at = (position + chips + jnp.where(core == 0, -hops, hops)) & (chips - 1)
-    chip = jnp.where(at < chips // 2, 2 * at, 2 * (chips - 1 - at) + 1)
+    chip = jnp.where(at < chips // 2, chips - 2 - 2 * at, 2 * at - chips + 1)
     block = 2 * chip + jnp.where(other == 1, 1 - core, core)
     found = jnp.full_like(lane, -1)
     for slot in range(list_ref.shape[1]):
@@ -130,7 +130,7 @@
 def core_and_position(loop_size):
     me = lax.axis_index("loop")
     core, row, outer = me % 2, me // 2 % 2, me // 4
-    return core, jnp.where(row == 0, outer, loop_size // 2 - 1 - outer)
+    return core, loop_size // 4 + jnp.where(row == 0, -1 - outer, outer)
 
 
 def pack_kernel(loop_size, *refs):

time: 35.4 us -> 35.4 us (level)
  Pallas kernels: 4.7 us -> 2.47 us
  waiting for transfers between devices: 6.57 us -> 8.37 us
  starting transfers between devices: 11.4 us -> 12.6 us
  blocking collectives: 11.1 us -> 10.5 us
    ppermute x6, waiting for transfers between devices: 3.2 us -> 6.12 us  [to_next(): return lax.ppermute(array, 'loop', pairs)]
    pallas_call x4, Pallas kernels: 3.57 us -> 1.34 us  [add_pieces(): pl.pallas_call(functools.partial(pieces_kernel, places, len(arrays), pack...]
    ppermute x1, waiting for transfers between devices: 2.72 us -> 0.81 us  [across(): return lax.ppermute(array, 'loop', pairs)]
    ppermute x4, starting transfers between devices: 0.15 us -> 0.98 us  [to_other_core(): lax.ppermute(array, 'loop', [(at, at ^ 1) for at in range(loop_size)])]
    ppermute x1, starting transfers between devices: 3.31 us -> 4.12 us  [across(): return lax.ppermute(array, 'loop', pairs)]
    ppermute x4, waiting for transfers between devices: 0.64 us -> 1.44 us  [to_other_core(): lax.ppermute(array, 'loop', [(at, at ^ 1) for at in range(loop_size)])]
    all_to_all x1, blocking collectives: 11.1 us -> 10.5 us  [local(): squares = lax.all_to_all(square, 'loop', 0, 0, tiled=True)]
    ppermute x6, starting transfers between devices: 7.99 us -> 7.52 us  [to_next(): return lax.ppermute(array, 'loop', pairs)]
  transfers between devices with their start and end apart: 11 -> 11, of which waited for: 4 -> 4; matrix products, arithmetic and copies ran while one was open for 0% -> 0% of each run, Pallas kernels for 9% -> 4%
where the time goes in v27:
time: 35.4 us
  starting transfers between devices  12.6 us (36%)
  blocking collectives  10.5 us (30%)
  waiting for transfers between devices  8.37 us (24%)
  Pallas kernels  2.47 us (7%)
  between operations  0.73 us (2%)
  local copies, waits for them, and re-layouts  0.66 us (2%)
    all_to_all x1, blocking collectives, local(): squares = lax.all_to_all(square, 'loop', 0, 0, tiled=True)  10.5 us
    ppermute x6, starting transfers between devices, to_next(): return lax.ppermute(array, 'loop', pairs)  7.52 us
    ppermute x6, waiting for transfers between devices, to_next(): return lax.ppermute(array, 'loop', pairs)  6.12 us
    ppermute x1, starting transfers between devices, across(): return lax.ppermute(array, 'loop', pairs)  4.12 us
    ppermute x4, waiting for transfers between devices, to_other_core(): lax.ppermute(array, 'loop', [(at, at ^ 1) for at in range(loop_size)])  1.44 us
    pallas_call x4, Pallas kernels, add_pieces(): pl.pallas_call(functools.partial(pieces_kernel, places, len(arrays), pack...  1.34 us
    ppermute x4, starting transfers between devices, to_other_core(): lax.ppermute(array, 'loop', [(at, at ^ 1) for at in range(loop_size)])  0.98 us
    pallas_call x1, Pallas kernels, local(): pl.pallas_call(functools.partial(update_kernel, rows * loop_size * width)...  0.93 us
  transfers between devices with their start and end apart: 11, of which 4 were waited for; matrix products, arithmetic and copies ran while one was open for 0% of the time, Pallas kernels for 4%

profile of v27, /device:TPU:0, one launch (start us, length us, event | category | flops | bytes accessed | tf_op | source)
XLA Modules:
  0.0 35.4 jit_solution(4860908057032835694)
XLA Ops:
  0.0 3.0 %collective-permute-start = (bf16[128,512]{1,0:T(8,128)(2,1)}, bf16[128,512]{1,0:T(8,128)(2,1)S(1)}, u32[]{:S(2)}, u32[]{:S(2)}) collective-permute-start(bf16[128,512]{1,0:T(8,128)(2,1)} %refs_0_.1), channel_id=1, source_target_pairs={{12,8},{8,4},{4,0},{0,2},{2,6},{6,10},{10,14},{14,12},{13,15},{9,1... | collective-permute-start | bytes 393224 | tf_op jit(solution)/shard_map/ppermute | solution.py:29
  3.0 0.1 collective-permute-start.1
  3.7 0.0 copy-start.3
  3.7 0.6 %copy-done.3 = s32[1,8]{1,0:T(1,128)S(1)} copy-done((s32[1,8]{1,0:T(1,128)S(1)}, s32[1,8]{1,0:T(1,128)}, u32[]{:S(2)}) %copy-start.3) | copy-done | bytes 56
  4.3 0.0 copy-start.2
  4.3 0.1 slot_table.1.table_ref
  4.5 0.0 copy-start
  4.5 0.0 copy-start.1
  4.5 2.5 %collective-permute-done.rest_1_.refs_1_ = bf16[128,512]{1,0:T(8,128)(2,1)S(1)} collective-permute-done((bf16[128,512]{1,0:T(8,128)(2,1)}, bf16[128,512]{1,0:T(8,128)(2,1)S(1)}, u32[]{:S(2)}, u32[]{:S(2)}) %collective-permute-start) | collective-permute-done | bytes 131104 | tf_op jit(solution)/shard_map/ppermute | solution.py:29
  7.0 0.0 collective-permute-start.2
  7.0 1.5 %collective-permute-start.3 = (bf16[128,512]{1,0:T(8,128)(2,1)S(1)}, bf16[128,512]{1,0:T(8,128)(2,1)S(1)}, u32[]{:S(2)}, u32[]{:S(2)}) collective-permute-start(bf16[128,512]{1,0:T(8,128)(2,1)S(1)} %collective-permute-done.rest_1_.refs_1_), channel_id=1, source_target_pairs={{12,8},{8,4},{4,0},{0,2},{2,6},{6,10},{10,14},{14,12},{13,15},{9,1... | collective-permute-start | bytes 393224 | tf_op jit(solution)/shard_map/ppermute | solution.py:29
  8.5 0.0 collective-permute-done.1.rest_2_.refs_2_
  8.5 1.0 %collective-permute-start.5 = (bf16[128,512]{1,0:T(8,128)(2,1)S(1)}, bf16[128,512]{1,0:T(8,128)(2,1)S(1)}, u32[]{:S(2)}, u32[]{:S(2)}) collective-permute-start(bf16[128,512]{1,0:T(8,128)(2,1)S(1)} %collective-permute-done.1.rest_2_.refs_2_), channel_id=1, source_target_pairs={{12,14},{8,12},{4,8},{0,4},{2,0},{6,2},{10,6},{14,10},{13,9},{9,5}... | collective-permute-start | bytes 393224 | tf_op jit(solution)/shard_map/ppermute | solution.py:29
  9.5 0.0 copy-done.2
  9.5 4.1 %collective-permute-start.7 = (bf16[128,512]{1,0:T(8,128)(2,1)S(1)}, bf16[128,512]{1,0:T(8,128)(2,1)S(1)}, u32[]{:S(2)}, u32[]{:S(2)}) collective-permute-start(bf16[128,512]{1,0:T(8,128)(2,1)S(1)} %get-tuple-element.22), channel_id=1, source_target_pairs={{12,0},{13,1},{8,10},{9,11},{4,6},{5,7},{0,12},{1,13},{2,14},{3,15... | collective-permute-start | bytes 393224 | tf_op jit(solution)/shard_map/ppermute | solution.py:39
  13.7 0.0 collective-permute-start.9
  13.7 0.0 collective-permute-done.3.rest_0_
  13.7 0.8 %collective-permute-start.4 = (bf16[128,512]{1,0:T(8,128)(2,1)S(1)}, bf16[128,512]{1,0:T(8,128)(2,1)S(1)}, u32[]{:S(2)}, u32[]{:S(2)}) collective-permute-start(bf16[128,512]{1,0:T(8,128)(2,1)S(1)} %collective-permute-done.3.rest_0_), channel_id=1, source_target_pairs={{12,8},{8,4},{4,0},{0,2},{2,6},{6,10},{10,14},{14,12},{13,15},{9,1... | collective-permute-start | bytes 393224 | tf_op jit(solution)/shard_map/ppermute | solution.py:29
  14.5 0.0 collective-permute-done.5.rest_1_
  14.5 1.2 %collective-permute-start.6 = (bf16[128,512]{1,0:T(8,128)(2,1)S(1)}, bf16[128,512]{1,0:T(8,128)(2,1)S(1)}, u32[]{:S(2)}, u32[]{:S(2)}) collective-permute-start(bf16[128,512]{1,0:T(8,128)(2,1)S(1)} %collective-permute-done.5.rest_1_), channel_id=1, source_target_pairs={{12,14},{8,12},{4,8},{0,4},{2,0},{6,2},{10,6},{14,10},{13,9},{9,5}... | collective-permute-start | bytes 393224 | tf_op jit(solution)/shard_map/ppermute | solution.py:29
  15.7 0.0 collective-permute-done.2.rest_3_
  15.7 0.0 copy-done
  15.7 0.0 copy-done.1
  15.7 0.8 %add_pieces.4 = (f32[256,512]{1,0:T(8,128)S(1)}, bf16[512,512]{1,0:T(8,128)(2,1)S(1)}) custom-call(s32[1,128]{1,0:T(1,128)S(1)} %slot_table.1.table_ref, f32[256,512]{1,0:T(8,128)S(1)} %copy-done, s32[256,1024]{1,0:T(8,128)S(1)} %copy-done.1, bf16[128,512]{1,0:T(8,128)(2,1)S(1)} %copy-done.2, bf16[128,512]{1,0:T(8,128)(2,1)S(1)} %collective-permute-done.rest_1_.refs_1_, ...), custom_call_target="tpu_custom_call" | custom-call | flops 536870912 | bytes 1048576 | tf_op jit(solution)/shard_map/add_pieces/pallas_call | solution.py:224
  16.5 0.1 add_pieces.5
  16.7 0.8 %collective-permute-start.10 = (bf16[256,512]{1,0:T(8,128)(2,1)S(1)}, bf16[256,512]{1,0:T(8,128)(2,1)S(1)}, u32[]{:S(2)}, u32[]{:S(2)}) collective-permute-start(bf16[256,512]{1,0:T(8,128)(2,1)S(1)} %get-tuple-element.29), channel_id=1, source_target_pairs={{0,1},{1,0},{2,3},{3,2},{4,5},{5,4},{6,7},{7,6},{8,9},{9,8},{10,11... | collective-permute-start | bytes 786440 | tf_op jit(solution)/shard_map/ppermute | solution.py:43
  17.5 0.8 %collective-permute-done.7.refs_2_.rest_2_ = bf16[128,512]{1,0:T(8,128)(2,1)S(1)} collective-permute-done((bf16[128,512]{1,0:T(8,128)(2,1)S(1)}, bf16[128,512]{1,0:T(8,128)(2,1)S(1)}, u32[]{:S(2)}, u32[]{:S(2)}) %collective-permute-start.7) | collective-permute-done | bytes 131104 | tf_op jit(solution)/shard_map/ppermute | solution.py:39
  18.3 3.6 %collective-permute-done.4.refs_0_.rest_0_ = bf16[128,512]{1,0:T(8,128)(2,1)S(1)} collective-permute-done((bf16[128,512]{1,0:T(8,128)(2,1)S(1)}, bf16[128,512]{1,0:T(8,128)(2,1)S(1)}, u32[]{:S(2)}, u32[]{:S(2)}) %collective-permute-start.4) | collective-permute-done | bytes 131104 | tf_op jit(solution)/shard_map/ppermute | solution.py:29
  21.9 0.0 collective-permute-done.6.refs_1_.rest_1_
  21.9 0.2 collective-permute-start.8
  22.1 0.0 collective-permute-done.9.rest_3_
  22.1 0.0 collective-permute-done.10.rest_4_
  22.1 0.2 add_pieces.6.rest_1_
  22.3 1.4 %collective-permute-done.8.rest_0_ = bf16[384,512]{1,0:T(8,128)(2,1)S(1)} collective-permute-done((bf16[384,512]{1,0:T(8,128)(2,1)S(1)}, bf16[384,512]{1,0:T(8,128)(2,1)S(1)}, u32[]{:S(2)}, u32[]{:S(2)}) %collective-permute-start.8) | collective-permute-done | bytes 393248 | tf_op jit(solution)/shard_map/ppermute | solution.py:43
  23.7 0.2 add_pieces.7
  23.9 10.5 %all_to_all.11 = f32[16,1,128]{2,1,0:T(1,128)S(1)} all-to-all(f32[16,1,128]{2,1,0:T(1,128)S(1)} %bitcast.7), channel_id=1, replica_groups=mesh['group'=2,'loop'=16] {'loop'}, dimensions={0} | all-to-all | bytes 16384 | tf_op jit(solution)/shard_map/all_to_all | solution.py:376
  34.5 0.9 %update.1 = f32[256,512]{1,0:T(8,128)} custom-call(f32[256,512]{1,0:T(8,128)S(1)} %copy-done, f32[256,512]{1,0:T(8,128)S(1)} %get-tuple-element.31.grad_ref, f32[16,128]{1,0:T(8,128)S(1)} %bitcast.6), custom_call_target="tpu_custom_call" | custom-call | flops 262144 | bytes 1572864 | tf_op jit(solution)/shard_map/update/pallas_call | solution.py:377
  (2 shorter events, 0.1 us)
Async XLA Ops:
  0.0 7.0 %collective-permute-start = (bf16[128,512]{1,0:T(8,128)(2,1)}, bf16[128,512]{1,0:T(8,128)(2,1)S(1)}, u32[]{:S(2)}, u32[]{:S(2)}) collective-permute-start(bf16[128,512]{1,0:T(8,128)(2,1)} %refs_0_.1), channel_id=1, source_target_pairs={{12,8},{8,4},{4,0},{0,2},{2,6},{6,10},{10,14},{14,12},{13,15},{9,1... | collective-permute-start | bytes 393224 | tf_op jit(solution)/shard_map/ppermute | solution.py:29
  3.0 5.5 %collective-permute-start.1 = (bf16[128,512]{1,0:T(8,128)(2,1)}, bf16[128,512]{1,0:T(8,128)(2,1)S(1)}, u32[]{:S(2)}, u32[]{:S(2)}) collective-permute-start(bf16[128,512]{1,0:T(8,128)(2,1)} %refs_0_.1), channel_id=1, source_target_pairs={{12,14},{8,12},{4,8},{0,4},{2,0},{6,2},{10,6},{14,10},{13,9},{9,5}... | collective-permute-start | bytes 393224 | tf_op jit(solution)/shard_map/ppermute | solution.py:29
  3.7 0.7 %copy-start.3 = (s32[1,8]{1,0:T(1,128)S(1)}, s32[1,8]{1,0:T(1,128)}, u32[]{:S(2)}) copy-start(s32[1,8]{1,0:T(1,128)} %list_ref.1) | copy-start | bytes 100
  4.3 5.2 %copy-start.2 = (bf16[128,512]{1,0:T(8,128)(2,1)S(1)}, bf16[128,512]{1,0:T(8,128)(2,1)}, u32[]{:S(2)}) copy-start(bf16[128,512]{1,0:T(8,128)(2,1)} %refs_0_.1) | copy-start | bytes 393220
  4.5 11.2 %copy-start = (f32[256,512]{1,0:T(8,128)S(1)}, f32[256,512]{1,0:T(8,128)}, u32[]{:S(2)}) copy-start(f32[256,512]{1,0:T(8,128)} %users_ref.1) | copy-start | bytes 1572868
  4.5 11.2 %copy-start.1 = (s32[256,1024]{1,0:T(8,128)S(1)}, s32[256,1024]{1,0:T(8,128)}, u32[]{:S(2)}) copy-start(s32[256,1024]{1,0:T(8,128)} %labels_ref.7) | copy-start | bytes 3145732
  7.0 8.7 %collective-permute-start.2 = (bf16[128,512]{1,0:T(8,128)(2,1)S(1)}, bf16[128,512]{1,0:T(8,128)(2,1)S(1)}, u32[]{:S(2)}, u32[]{:S(2)}) collective-permute-start(bf16[128,512]{1,0:T(8,128)(2,1)S(1)} %collective-permute-done.rest_1_.refs_1_), channel_id=1, source_target_pairs={{0,1},{1,0},{2,3},{3,2},{4,5},{5,4},{6,7},{7,6},{8,9},{9,8},{10,11... | collective-permute-start | bytes 393224 | tf_op jit(solution)/shard_map/ppermute | solution.py:43
  7.0 6.6 %collective-permute-start.3 = (bf16[128,512]{1,0:T(8,128)(2,1)S(1)}, bf16[128,512]{1,0:T(8,128)(2,1)S(1)}, u32[]{:S(2)}, u32[]{:S(2)}) collective-permute-start(bf16[128,512]{1,0:T(8,128)(2,1)S(1)} %collective-permute-done.rest_1_.refs_1_), channel_id=1, source_target_pairs={{12,8},{8,4},{4,0},{0,2},{2,6},{6,10},{10,14},{14,12},{13,15},{9,1... | collective-permute-start | bytes 393224 | tf_op jit(solution)/shard_map/ppermute | solution.py:29
  8.5 6.0 %collective-permute-start.5 = (bf16[128,512]{1,0:T(8,128)(2,1)S(1)}, bf16[128,512]{1,0:T(8,128)(2,1)S(1)}, u32[]{:S(2)}, u32[]{:S(2)}) collective-permute-start(bf16[128,512]{1,0:T(8,128)(2,1)S(1)} %collective-permute-done.1.rest_2_.refs_2_), channel_id=1, source_target_pairs={{12,14},{8,12},{4,8},{0,4},{2,0},{6,2},{10,6},{14,10},{13,9},{9,5}... | collective-permute-start | bytes 393224 | tf_op jit(solution)/shard_map/ppermute | solution.py:29
  9.5 8.8 %collective-permute-start.7 = (bf16[128,512]{1,0:T(8,128)(2,1)S(1)}, bf16[128,512]{1,0:T(8,128)(2,1)S(1)}, u32[]{:S(2)}, u32[]{:S(2)}) collective-permute-start(bf16[128,512]{1,0:T(8,128)(2,1)S(1)} %get-tuple-element.22), channel_id=1, source_target_pairs={{12,0},{13,1},{8,10},{9,11},{4,6},{5,7},{0,12},{1,13},{2,14},{3,15... | collective-permute-start | bytes 393224 | tf_op jit(solution)/shard_map/ppermute | solution.py:39
  13.7 8.4 %collective-permute-start.9 = (bf16[256,512]{1,0:T(8,128)(2,1)S(1)}, bf16[256,512]{1,0:T(8,128)(2,1)S(1)}, u32[]{:S(2)}, u32[]{:S(2)}) collective-permute-start(bf16[256,512]{1,0:T(8,128)(2,1)S(1)} %get-tuple-element.28), channel_id=1, source_target_pairs={{0,1},{1,0},{2,3},{3,2},{4,5},{5,4},{6,7},{7,6},{8,9},{9,8},{10,11... | collective-permute-start | bytes 786440 | tf_op jit(solution)/shard_map/ppermute | solution.py:43
  13.7 8.2 %collective-permute-start.4 = (bf16[128,512]{1,0:T(8,128)(2,1)S(1)}, bf16[128,512]{1,0:T(8,128)(2,1)S(1)}, u32[]{:S(2)}, u32[]{:S(2)}) collective-permute-start(bf16[128,512]{1,0:T(8,128)(2,1)S(1)} %collective-permute-done.3.rest_0_), channel_id=1, source_target_pairs={{12,8},{8,4},{4,0},{0,2},{2,6},{6,10},{10,14},{14,12},{13,15},{9,1... | collective-permute-start | bytes 393224 | tf_op jit(solution)/shard_map/ppermute | solution.py:29
  14.5 7.4 %collective-permute-start.6 = (bf16[128,512]{1,0:T(8,128)(2,1)S(1)}, bf16[128,512]{1,0:T(8,128)(2,1)S(1)}, u32[]{:S(2)}, u32[]{:S(2)}) collective-permute-start(bf16[128,512]{1,0:T(8,128)(2,1)S(1)} %collective-permute-done.5.rest_1_), channel_id=1, source_target_pairs={{12,14},{8,12},{4,8},{0,4},{2,0},{6,2},{10,6},{14,10},{13,9},{9,5}... | collective-permute-start | bytes 393224 | tf_op jit(solution)/shard_map/ppermute | solution.py:29
  16.7 5.4 %collective-permute-start.10 = (bf16[256,512]{1,0:T(8,128)(2,1)S(1)}, bf16[256,512]{1,0:T(8,128)(2,1)S(1)}, u32[]{:S(2)}, u32[]{:S(2)}) collective-permute-start(bf16[256,512]{1,0:T(8,128)(2,1)S(1)} %get-tuple-element.29), channel_id=1, source_target_pairs={{0,1},{1,0},{2,3},{3,2},{4,5},{5,4},{6,7},{7,6},{8,9},{9,8},{10,11... | collective-permute-start | bytes 786440 | tf_op jit(solution)/shard_map/ppermute | solution.py:43
  21.9 1.8 %collective-permute-start.8 = (bf16[384,512]{1,0:T(8,128)(2,1)S(1)}, bf16[384,512]{1,0:T(8,128)(2,1)S(1)}, u32[]{:S(2)}, u32[]{:S(2)}) collective-permute-start(bf16[384,512]{1,0:T(8,128)(2,1)S(1)} %pack.3), channel_id=1, source_target_pairs={{0,1},{1,0},{2,3},{3,2},{4,5},{5,4},{6,7},{7,6},{8,9},{9,8},{10,11... | collective-permute-start | bytes 1179656 | tf_op jit(solution)/shard_map/ppermute | solution.py:43

commit v28 on v18

--- a/solution.py
+++ b/solution.py
@@ -80,24 +80,29 @@
 
 def add_block(grad_ref, parts_ref, block, labels):
     rows = grad_ref.shape[0]
+    half = rows // 2
     tile = labels[0].shape[1]
-    upper, lower = [], []
-    for at in range(0, len(labels), 2):
-        some = jnp.concatenate(labels[at : at + 2], 1)
-        both = lax.dot_general(
-            parts_ref[...],
-            block[at * tile : at * tile + some.shape[1]],
-            (((1,), (1,)), ((), ())),
+    for start in range(0, rows, half):
+        both_parts = jnp.concatenate(
+            [parts_ref[start : start + half, :], parts_ref[rows + start : rows + start + half, :]], 0
+        )
+        upper, lower = [], []
+        for at in range(0, len(labels), 2):
+            some = jnp.concatenate([each[start : start + half] for each in labels[at : at + 2]], 1)
+            both = lax.dot_general(
+                both_parts,
+                block[at * tile : at * tile + some.shape[1]],
+                (((1,), (1,)), ((), ())),
+                preferred_element_type=jnp.float32,
+            )
+            residual = 0.5 * jnp.tanh(both[:half] + both[half:]) + (0.5 - some.astype(jnp.float32))
+            upper.append(residual.astype(jnp.bfloat16))
+            lower.append((residual - upper[-1].astype(jnp.float32)).astype(jnp.bfloat16))
+        grad_ref[start : start + half, :] += jnp.dot(
+            jnp.concatenate(upper + lower, 1),
+            jnp.concatenate([block, block], 0),
             preferred_element_type=jnp.float32,
         )
-        residual = 0.5 * jnp.tanh(both[:rows] + both[rows:]) + (0.5 - some.astype(jnp.float32))
-        upper.append(residual.astype(jnp.bfloat16))
-        lower.append((residual - upper[-1].astype(jnp.float32)).astype(jnp.bfloat16))
-    grad_ref[...] += jnp.dot(
-        jnp.concatenate(upper + lower, 1),
-        jnp.concatenate([block, block], 0),
-        preferred_element_type=jnp.float32,
-    )
 
 
 def add_tiles(grad_ref, parts_ref, tiles, live, labels_at):

time: 35.4 us -> 35.3 us (level)
  waiting for transfers between devices: 6.57 us -> 7.69 us
  Pallas kernels: 4.7 us -> 3.76 us
    ppermute x1, waiting for transfers between devices: 2.72 us -> 4.07 us  [across(): return lax.ppermute(array, 'loop', pairs)]
    pallas_call x4, Pallas kernels: 3.57 us -> 2.62 us  [add_pieces(): pl.pallas_call(functools.partial(pieces_kernel, places, len(arrays), pack...]
  transfers between devices with their start and end apart: 11 -> 11, of which waited for: 4 -> 4; matrix products, arithmetic and copies ran while one was open for 0% -> 0% of each run, Pallas kernels for 9% -> 5%
where the time goes in v28:
time: 35.3 us; the launch traced here: 35.4 us
  starting transfers between devices  11.4 us (32%)
  blocking collectives  11.1 us (31%)
  waiting for transfers between devices  7.69 us (22%)
  Pallas kernels  3.76 us (11%)
  between operations  0.76 us (2%)
  local copies, waits for them, and re-layouts  0.66 us (2%)
    all_to_all x1, blocking collectives, local(): squares = lax.all_to_all(square, 'loop', 0, 0, tiled=True)  11.1 us
    ppermute x6, starting transfers between devices, to_next(): return lax.ppermute(array, 'loop', pairs)  7.99 us
    ppermute x1, waiting for transfers between devices, across(): return lax.ppermute(array, 'loop', pairs)  4.07 us
    ppermute x1, starting transfers between devices, across(): return lax.ppermute(array, 'loop', pairs)  3.31 us
    ppermute x6, waiting for transfers between devices, to_next(): return lax.ppermute(array, 'loop', pairs)  3.2 us
    pallas_call x4, Pallas kernels, add_pieces(): pl.pallas_call(functools.partial(pieces_kernel, places, len(arrays), pack...  2.62 us
    pallas_call x1, Pallas kernels, local(): pl.pallas_call(functools.partial(update_kernel, rows * loop_size * width)...  0.93 us
  transfers between devices with their start and end apart: 11, of which 4 were waited for; matrix products, arithmetic and copies ran while one was open for 0% of the time, Pallas kernels for 5%

profile of v28, /device:TPU:0, one launch (start us, length us, event | category | flops | bytes accessed | tf_op | source)
XLA Modules:
  0.0 35.4 jit_solution(7236866804031646943)
XLA Ops:
  0.0 3.0 %collective-permute-start = (bf16[128,512]{1,0:T(8,128)(2,1)}, bf16[128,512]{1,0:T(8,128)(2,1)S(1)}, u32[]{:S(2)}, u32[]{:S(2)}) collective-permute-start(bf16[128,512]{1,0:T(8,128)(2,1)} %refs_0_.1), channel_id=1, source_target_pairs={{0,4},{4,8},{8,12},{12,14},{14,10},{10,6},{6,2},{2,0},{1,3},{5,1},... | collective-permute-start | bytes 393224 | tf_op jit(solution)/shard_map/ppermute | solution.py:29
  3.0 0.0 collective-permute-start.1
  3.7 0.0 copy-start.3
  3.7 0.6 %copy-done.3 = s32[1,8]{1,0:T(1,128)S(1)} copy-done((s32[1,8]{1,0:T(1,128)S(1)}, s32[1,8]{1,0:T(1,128)}, u32[]{:S(2)}) %copy-start.3) | copy-done | bytes 56
  4.3 0.0 copy-start.2
  4.3 0.1 slot_table.1.table_ref
  4.5 0.0 copy-start
  4.5 0.0 copy-start.1
  4.5 2.5 %collective-permute-done.rest_1_.refs_1_ = bf16[128,512]{1,0:T(8,128)(2,1)S(1)} collective-permute-done((bf16[128,512]{1,0:T(8,128)(2,1)}, bf16[128,512]{1,0:T(8,128)(2,1)S(1)}, u32[]{:S(2)}, u32[]{:S(2)}) %collective-permute-start) | collective-permute-done | bytes 131104 | tf_op jit(solution)/shard_map/ppermute | solution.py:29
  7.0 0.0 collective-permute-start.2
  7.0 1.5 %collective-permute-start.3 = (bf16[128,512]{1,0:T(8,128)(2,1)S(1)}, bf16[128,512]{1,0:T(8,128)(2,1)S(1)}, u32[]{:S(2)}, u32[]{:S(2)}) collective-permute-start(bf16[128,512]{1,0:T(8,128)(2,1)S(1)} %collective-permute-done.rest_1_.refs_1_), channel_id=1, source_target_pairs={{0,4},{4,8},{8,12},{12,14},{14,10},{10,6},{6,2},{2,0},{1,3},{5,1},... | collective-permute-start | bytes 393224 | tf_op jit(solution)/shard_map/ppermute | solution.py:29
  8.5 0.0 collective-permute-done.1.rest_2_.refs_2_
  8.5 1.0 %collective-permute-start.5 = (bf16[128,512]{1,0:T(8,128)(2,1)S(1)}, bf16[128,512]{1,0:T(8,128)(2,1)S(1)}, u32[]{:S(2)}, u32[]{:S(2)}) collective-permute-start(bf16[128,512]{1,0:T(8,128)(2,1)S(1)} %collective-permute-done.1.rest_2_.refs_2_), channel_id=1, source_target_pairs={{0,2},{4,0},{8,4},{12,8},{14,12},{10,14},{6,10},{2,6},{1,5},{5,9},... | collective-permute-start | bytes 393224 | tf_op jit(solution)/shard_map/ppermute | solution.py:29
  9.5 0.0 copy-done.2
  9.5 3.3 %collective-permute-start.7 = (bf16[128,512]{1,0:T(8,128)(2,1)S(1)}, bf16[128,512]{1,0:T(8,128)(2,1)S(1)}, u32[]{:S(2)}, u32[]{:S(2)}) collective-permute-start(bf16[128,512]{1,0:T(8,128)(2,1)S(1)} %get-tuple-element.22), channel_id=1, source_target_pairs={{0,12},{1,13},{4,6},{5,7},{8,10},{9,11},{12,0},{13,1},{14,2},{15,3... | collective-permute-start | bytes 393224 | tf_op jit(solution)/shard_map/ppermute | solution.py:39
  12.8 0.0 collective-permute-start.9
  12.8 0.0 collective-permute-done.3.rest_0_
  12.8 1.7 %collective-permute-start.4 = (bf16[128,512]{1,0:T(8,128)(2,1)S(1)}, bf16[128,512]{1,0:T(8,128)(2,1)S(1)}, u32[]{:S(2)}, u32[]{:S(2)}) collective-permute-start(bf16[128,512]{1,0:T(8,128)(2,1)S(1)} %collective-permute-done.3.rest_0_), channel_id=1, source_target_pairs={{0,4},{4,8},{8,12},{12,14},{14,10},{10,6},{6,2},{2,0},{1,3},{5,1},... | collective-permute-start | bytes 393224 | tf_op jit(solution)/shard_map/ppermute | solution.py:29
  14.5 0.0 collective-permute-done.5.rest_1_
  14.5 0.8 %collective-permute-start.6 = (bf16[128,512]{1,0:T(8,128)(2,1)S(1)}, bf16[128,512]{1,0:T(8,128)(2,1)S(1)}, u32[]{:S(2)}, u32[]{:S(2)}) collective-permute-start(bf16[128,512]{1,0:T(8,128)(2,1)S(1)} %collective-permute-done.5.rest_1_), channel_id=1, source_target_pairs={{0,2},{4,0},{8,4},{12,8},{14,12},{10,14},{6,10},{2,6},{1,5},{5,9},... | collective-permute-start | bytes 393224 | tf_op jit(solution)/shard_map/ppermute | solution.py:29
  15.3 0.0 collective-permute-done.2.rest_3_
  15.3 0.0 copy-done
  15.3 0.0 copy-done.1
  15.3 0.3 add_pieces.4
  15.6 0.1 add_pieces.5
  15.7 0.1 collective-permute-start.10
  15.8 4.1 %collective-permute-done.7.refs_2_.rest_2_ = bf16[128,512]{1,0:T(8,128)(2,1)S(1)} collective-permute-done((bf16[128,512]{1,0:T(8,128)(2,1)S(1)}, bf16[128,512]{1,0:T(8,128)(2,1)S(1)}, u32[]{:S(2)}, u32[]{:S(2)}) %collective-permute-start.7) | collective-permute-done | bytes 131104 | tf_op jit(solution)/shard_map/ppermute | solution.py:39
  19.9 0.0 collective-permute-done.4.refs_0_.rest_0_
  19.9 0.7 %collective-permute-done.6.refs_1_.rest_1_ = bf16[128,512]{1,0:T(8,128)(2,1)S(1)} collective-permute-done((bf16[128,512]{1,0:T(8,128)(2,1)S(1)}, bf16[128,512]{1,0:T(8,128)(2,1)S(1)}, u32[]{:S(2)}, u32[]{:S(2)}) %collective-permute-start.6) | collective-permute-done | bytes 131104 | tf_op jit(solution)/shard_map/ppermute | solution.py:29
  20.6 0.1 collective-permute-start.8
  20.7 0.0 collective-permute-done.9.rest_3_
  20.7 0.0 collective-permute-done.10.rest_4_
  20.7 1.3 %add_pieces.6.rest_1_ = f32[256,512]{1,0:T(8,128)S(1)} custom-call(s32[1,128]{1,0:T(1,128)S(1)} %slot_table.1.table_ref, bf16[512,512]{1,0:T(8,128)(2,1)S(1)} %get-tuple-element.21.given_ref, s32[256,1024]{1,0:T(8,128)S(1)} %copy-done.1, bf16[128,512]{1,0:T(8,128)(2,1)S(1)} %collective-permute-done.4.refs_0_.rest_0_, ...), custom_call_target="tpu_custom_call", output_to_operand_aliasing={{}: (8, {})} | custom-call | flops 15032385536 | bytes 1048576 | tf_op jit(solution)/shard_map/add_pieces/pallas_call | solution.py:229
  22.0 0.4 %collective-permute-done.8.rest_0_ = bf16[384,512]{1,0:T(8,128)(2,1)S(1)} collective-permute-done((bf16[384,512]{1,0:T(8,128)(2,1)S(1)}, bf16[384,512]{1,0:T(8,128)(2,1)S(1)}, u32[]{:S(2)}, u32[]{:S(2)}) %collective-permute-start.8) | collective-permute-done | bytes 393248 | tf_op jit(solution)/shard_map/ppermute | solution.py:43
  22.4 1.0 %add_pieces.7 = (f32[256,512]{1,0:T(8,128)S(1)}, f32[16,128]{1,0:T(8,128)S(1)}) custom-call(s32[1,128]{1,0:T(1,128)S(1)} %slot_table.1.table_ref, bf16[512,512]{1,0:T(8,128)(2,1)S(1)} %get-tuple-element.21.given_ref, s32[256,1024]{1,0:T(8,128)S(1)} %copy-done.1, ...), custom_call_target="tpu_custom_call", output_to_operand_aliasing={{0}: (4, {})} | custom-call | flops 6442450944 | bytes 1048576 | tf_op jit(solution)/shard_map/add_pieces/pallas_call | solution.py:229
  23.4 11.1 %all_to_all.11 = f32[16,1,128]{2,1,0:T(1,128)S(1)} all-to-all(f32[16,1,128]{2,1,0:T(1,128)S(1)} %bitcast.7), channel_id=1, replica_groups=mesh['group'=2,'loop'=16] {'loop'}, dimensions={0} | all-to-all | bytes 16384 | tf_op jit(solution)/shard_map/all_to_all | solution.py:381
  34.5 0.9 %update.1 = f32[256,512]{1,0:T(8,128)} custom-call(f32[256,512]{1,0:T(8,128)S(1)} %copy-done, f32[256,512]{1,0:T(8,128)S(1)} %get-tuple-element.31.grad_ref, f32[16,128]{1,0:T(8,128)S(1)} %bitcast.6), custom_call_target="tpu_custom_call" | custom-call | flops 262144 | bytes 1572864 | tf_op jit(solution)/shard_map/update/pallas_call | solution.py:382
  (2 shorter events, 0.1 us)
Async XLA Ops:
  0.0 7.0 %collective-permute-start = (bf16[128,512]{1,0:T(8,128)(2,1)}, bf16[128,512]{1,0:T(8,128)(2,1)S(1)}, u32[]{:S(2)}, u32[]{:S(2)}) collective-permute-start(bf16[128,512]{1,0:T(8,128)(2,1)} %refs_0_.1), channel_id=1, source_target_pairs={{0,4},{4,8},{8,12},{12,14},{14,10},{10,6},{6,2},{2,0},{1,3},{5,1},... | collective-permute-start | bytes 393224 | tf_op jit(solution)/shard_map/ppermute | solution.py:29
  3.0 5.5 %collective-permute-start.1 = (bf16[128,512]{1,0:T(8,128)(2,1)}, bf16[128,512]{1,0:T(8,128)(2,1)S(1)}, u32[]{:S(2)}, u32[]{:S(2)}) collective-permute-start(bf16[128,512]{1,0:T(8,128)(2,1)} %refs_0_.1), channel_id=1, source_target_pairs={{0,2},{4,0},{8,4},{12,8},{14,12},{10,14},{6,10},{2,6},{1,5},{5,9},... | collective-permute-start | bytes 393224 | tf_op jit(solution)/shard_map/ppermute | solution.py:29
  3.7 0.7 %copy-start.3 = (s32[1,8]{1,0:T(1,128)S(1)}, s32[1,8]{1,0:T(1,128)}, u32[]{:S(2)}) copy-start(s32[1,8]{1,0:T(1,128)} %list_ref.1) | copy-start | bytes 100
  4.3 5.1 %copy-start.2 = (bf16[128,512]{1,0:T(8,128)(2,1)S(1)}, bf16[128,512]{1,0:T(8,128)(2,1)}, u32[]{:S(2)}) copy-start(bf16[128,512]{1,0:T(8,128)(2,1)} %refs_0_.1) | copy-start | bytes 393220
  4.5 10.8 %copy-start = (f32[256,512]{1,0:T(8,128)S(1)}, f32[256,512]{1,0:T(8,128)}, u32[]{:S(2)}) copy-start(f32[256,512]{1,0:T(8,128)} %users_ref.1) | copy-start | bytes 1572868
  4.5 10.8 %copy-start.1 = (s32[256,1024]{1,0:T(8,128)S(1)}, s32[256,1024]{1,0:T(8,128)}, u32[]{:S(2)}) copy-start(s32[256,1024]{1,0:T(8,128)} %labels_ref.7) | copy-start | bytes 3145732
  7.0 8.3 %collective-permute-start.2 = (bf16[128,512]{1,0:T(8,128)(2,1)S(1)}, bf16[128,512]{1,0:T(8,128)(2,1)S(1)}, u32[]{:S(2)}, u32[]{:S(2)}) collective-permute-start(bf16[128,512]{1,0:T(8,128)(2,1)S(1)} %collective-permute-done.rest_1_.refs_1_), channel_id=1, source_target_pairs={{0,1},{1,0},{2,3},{3,2},{4,5},{5,4},{6,7},{7,6},{8,9},{9,8},{10,11... | collective-permute-start | bytes 393224 | tf_op jit(solution)/shard_map/ppermute | solution.py:43
  7.0 5.8 %collective-permute-start.3 = (bf16[128,512]{1,0:T(8,128)(2,1)S(1)}, bf16[128,512]{1,0:T(8,128)(2,1)S(1)}, u32[]{:S(2)}, u32[]{:S(2)}) collective-permute-start(bf16[128,512]{1,0:T(8,128)(2,1)S(1)} %collective-permute-done.rest_1_.refs_1_), channel_id=1, source_target_pairs={{0,4},{4,8},{8,12},{12,14},{14,10},{10,6},{6,2},{2,0},{1,3},{5,1},... | collective-permute-start | bytes 393224 | tf_op jit(solution)/shard_map/ppermute | solution.py:29
  8.5 6.0 %collective-permute-start.5 = (bf16[128,512]{1,0:T(8,128)(2,1)S(1)}, bf16[128,512]{1,0:T(8,128)(2,1)S(1)}, u32[]{:S(2)}, u32[]{:S(2)}) collective-permute-start(bf16[128,512]{1,0:T(8,128)(2,1)S(1)} %collective-permute-done.1.rest_2_.refs_2_), channel_id=1, source_target_pairs={{0,2},{4,0},{8,4},{12,8},{14,12},{10,14},{6,10},{2,6},{1,5},{5,9},... | collective-permute-start | bytes 393224 | tf_op jit(solution)/shard_map/ppermute | solution.py:29
  9.5 10.4 %collective-permute-start.7 = (bf16[128,512]{1,0:T(8,128)(2,1)S(1)}, bf16[128,512]{1,0:T(8,128)(2,1)S(1)}, u32[]{:S(2)}, u32[]{:S(2)}) collective-permute-start(bf16[128,512]{1,0:T(8,128)(2,1)S(1)} %get-tuple-element.22), channel_id=1, source_target_pairs={{0,12},{1,13},{4,6},{5,7},{8,10},{9,11},{12,0},{13,1},{14,2},{15,3... | collective-permute-start | bytes 393224 | tf_op jit(solution)/shard_map/ppermute | solution.py:39
  12.8 7.9 %collective-permute-start.9 = (bf16[256,512]{1,0:T(8,128)(2,1)S(1)}, bf16[256,512]{1,0:T(8,128)(2,1)S(1)}, u32[]{:S(2)}, u32[]{:S(2)}) collective-permute-start(bf16[256,512]{1,0:T(8,128)(2,1)S(1)} %get-tuple-element.28), channel_id=1, source_target_pairs={{0,1},{1,0},{2,3},{3,2},{4,5},{5,4},{6,7},{7,6},{8,9},{9,8},{10,11... | collective-permute-start | bytes 786440 | tf_op jit(solution)/shard_map/ppermute | solution.py:43
  12.8 7.1 %collective-permute-start.4 = (bf16[128,512]{1,0:T(8,128)(2,1)S(1)}, bf16[128,512]{1,0:T(8,128)(2,1)S(1)}, u32[]{:S(2)}, u32[]{:S(2)}) collective-permute-start(bf16[128,512]{1,0:T(8,128)(2,1)S(1)} %collective-permute-done.3.rest_0_), channel_id=1, source_target_pairs={{0,4},{4,8},{8,12},{12,14},{14,10},{10,6},{6,2},{2,0},{1,3},{5,1},... | collective-permute-start | bytes 393224 | tf_op jit(solution)/shard_map/ppermute | solution.py:29
  14.5 6.1 %collective-permute-start.6 = (bf16[128,512]{1,0:T(8,128)(2,1)S(1)}, bf16[128,512]{1,0:T(8,128)(2,1)S(1)}, u32[]{:S(2)}, u32[]{:S(2)}) collective-permute-start(bf16[128,512]{1,0:T(8,128)(2,1)S(1)} %collective-permute-done.5.rest_1_), channel_id=1, source_target_pairs={{0,2},{4,0},{8,4},{12,8},{14,12},{10,14},{6,10},{2,6},{1,5},{5,9},... | collective-permute-start | bytes 393224 | tf_op jit(solution)/shard_map/ppermute | solution.py:29
  15.7 5.0 %collective-permute-start.10 = (bf16[256,512]{1,0:T(8,128)(2,1)S(1)}, bf16[256,512]{1,0:T(8,128)(2,1)S(1)}, u32[]{:S(2)}, u32[]{:S(2)}) collective-permute-start(bf16[256,512]{1,0:T(8,128)(2,1)S(1)} %get-tuple-element.29), channel_id=1, source_target_pairs={{0,1},{1,0},{2,3},{3,2},{4,5},{5,4},{6,7},{7,6},{8,9},{9,8},{10,11... | collective-permute-start | bytes 786440 | tf_op jit(solution)/shard_map/ppermute | solution.py:43
  20.6 1.8 %collective-permute-start.8 = (bf16[384,512]{1,0:T(8,128)(2,1)S(1)}, bf16[384,512]{1,0:T(8,128)(2,1)S(1)}, u32[]{:S(2)}, u32[]{:S(2)}) collective-permute-start(bf16[384,512]{1,0:T(8,128)(2,1)S(1)} %pack.3), channel_id=1, source_target_pairs={{0,1},{1,0},{2,3},{3,2},{4,5},{5,4},{6,7},{7,6},{8,9},{9,8},{10,11... | collective-permute-start | bytes 1179656 | tf_op jit(solution)/shard_map/ppermute | solution.py:43

commit v29 on v18

--- a/solution.py
+++ b/solution.py
@@ -45,7 +45,7 @@
 
 def halves(values):
     upper = values.astype(jnp.bfloat16)
-    return jnp.concatenate([upper, (values - upper.astype(jnp.float32)).astype(jnp.bfloat16)], 0)
+    return jnp.concatenate([upper, (values - upper.astype(jnp.float32)).astype(jnp.bfloat16)], 1)
 
 
 def table_kernel(loop_size, origins, list_ref, count_ref, table_ref):
@@ -79,18 +79,18 @@
 
 
 def add_block(grad_ref, parts_ref, block, labels):
-    rows = grad_ref.shape[0]
     tile = labels[0].shape[1]
     upper, lower = [], []
     for at in range(0, len(labels), 2):
         some = jnp.concatenate(labels[at : at + 2], 1)
-        both = lax.dot_general(
+        items = block[at * tile : at * tile + some.shape[1]]
+        half_scores = lax.dot_general(
             parts_ref[...],
-            block[at * tile : at * tile + some.shape[1]],
+            jnp.concatenate([items, items], 1),
             (((1,), (1,)), ((), ())),
             preferred_element_type=jnp.float32,
         )
-        residual = 0.5 * jnp.tanh(both[:rows] + both[rows:]) + (0.5 - some.astype(jnp.float32))
+        residual = 0.5 * jnp.tanh(half_scores) + (0.5 - some.astype(jnp.float32))
         upper.append(residual.astype(jnp.bfloat16))
         lower.append((residual - upper[-1].astype(jnp.float32)).astype(jnp.bfloat16))
     grad_ref[...] += jnp.dot(
@@ -207,15 +207,15 @@
 
 def add_pieces(held, packed, loop_size, table, given, labels, before, last):
     first = before is None
-    width = given.shape[1]
-    rows = given.shape[0] // (1 if first else 2)
+    width = given.shape[1] // (1 if first else 2)
+    rows = given.shape[0]
     arrays = [array for array, _ in held]
     tile = labels.shape[1] // CHUNK
     places = [(at, index, row) for index, (_, entries) in enumerate(held) for row, at in enumerate(entries)]
     most = min(len(places), CHUNK)
     out_shape = [jax.ShapeDtypeStruct((rows, width), jnp.float32)]
     if first:
-        out_shape.append(jax.ShapeDtypeStruct((2 * rows, width), jnp.bfloat16))
+        out_shape.append(jax.ShapeDtypeStruct((rows, 2 * width), jnp.bfloat16))
     if packed:
         out_shape.append(jax.ShapeDtypeStruct((len(packed) * tile, width), jnp.bfloat16))
     if last:
@@ -334,7 +334,7 @@
         ],
         scratch_shapes=[
             pltpu.VMEM((CHUNK * tile, width), jnp.bfloat16),
-            pltpu.VMEM((2 * rows, width), jnp.bfloat16),
+            pltpu.VMEM((rows, 2 * width), jnp.bfloat16),
             pltpu.SemaphoreType.DMA((CHUNK,)),
         ],
         compiler_params=pltpu.CompilerParams(vmem_limit_bytes=32 * 1024 * 1024),

time: 35.4 us -> 35.2 us (level)
  Pallas kernels: 4.7 us -> 3.8 us
  blocking collectives: 11.1 us -> 11.6 us
    pallas_call x4, Pallas kernels: 3.57 us -> 2.67 us  [add_pieces(): pl.pallas_call(functools.partial(pieces_kernel, places, len(arrays), pack...]
    all_to_all x1, blocking collectives: 11.1 us -> 11.6 us  [local(): squares = lax.all_to_all(square, 'loop', 0, 0, tiled=True)]
  transfers between devices with their start and end apart: 11 -> 11, of which waited for: 4 -> 4; matrix products, arithmetic and copies ran while one was open for 0% -> 0% of each run, Pallas kernels for 9% -> 8%
where the time goes in v29:
time: 35.2 us
  blocking collectives  11.6 us (33%)
  starting transfers between devices  11.4 us (32%)
  waiting for transfers between devices  6.9 us (20%)
  Pallas kernels  3.8 us (11%)
  between operations  0.76 us (2%)
  local copies, waits for them, and re-layouts  0.66 us (2%)
    all_to_all x1, blocking collectives, local(): squares = lax.all_to_all(square, 'loop', 0, 0, tiled=True)  11.6 us
    ppermute x6, starting transfers between devices, to_next(): return lax.ppermute(array, 'loop', pairs)  7.99 us
    ppermute x1, starting transfers between devices, across(): return lax.ppermute(array, 'loop', pairs)  3.31 us
    ppermute x6, waiting for transfers between devices, to_next(): return lax.ppermute(array, 'loop', pairs)  3.2 us
    ppermute x1, waiting for transfers between devices, across(): return lax.ppermute(array, 'loop', pairs)  2.73 us
    pallas_call x4, Pallas kernels, add_pieces(): pl.pallas_call(functools.partial(pieces_kernel, places, len(arrays), pack...  2.67 us
    ppermute x4, waiting for transfers between devices, to_other_core(): lax.ppermute(array, 'loop', [(at, at ^ 1) for at in range(loop_size)])  0.96 us
    pallas_call x1, Pallas kernels, local(): pl.pallas_call(functools.partial(update_kernel, rows * loop_size * width)...  0.93 us
  transfers between devices with their start and end apart: 11, of which 4 were waited for; matrix products, arithmetic and copies ran while one was open for 0% of the time, Pallas kernels for 8%

profile of v29, /device:TPU:0, one launch (start us, length us, event | category | flops | bytes accessed | tf_op | source)
XLA Modules:
  0.0 35.2 jit_solution(9884929347225905227)
XLA Ops:
  0.0 3.0 %collective-permute-start = (bf16[128,512]{1,0:T(8,128)(2,1)}, bf16[128,512]{1,0:T(8,128)(2,1)S(1)}, u32[]{:S(2)}, u32[]{:S(2)}) collective-permute-start(bf16[128,512]{1,0:T(8,128)(2,1)} %refs_0_.1), channel_id=1, source_target_pairs={{0,4},{4,8},{8,12},{12,14},{14,10},{10,6},{6,2},{2,0},{1,3},{5,1},... | collective-permute-start | bytes 393224 | tf_op jit(solution)/shard_map/ppermute | solution.py:29
  3.0 0.0 collective-permute-start.1
  3.7 0.0 copy-start.3
  3.7 0.6 %copy-done.3 = s32[1,8]{1,0:T(1,128)S(1)} copy-done((s32[1,8]{1,0:T(1,128)S(1)}, s32[1,8]{1,0:T(1,128)}, u32[]{:S(2)}) %copy-start.3) | copy-done | bytes 56
  4.3 0.0 copy-start.2
  4.3 0.1 slot_table.1.table_ref
  4.5 0.0 copy-start
  4.5 0.0 copy-start.1
  4.5 2.5 %collective-permute-done.rest_1_.refs_1_ = bf16[128,512]{1,0:T(8,128)(2,1)S(1)} collective-permute-done((bf16[128,512]{1,0:T(8,128)(2,1)}, bf16[128,512]{1,0:T(8,128)(2,1)S(1)}, u32[]{:S(2)}, u32[]{:S(2)}) %collective-permute-start) | collective-permute-done | bytes 131104 | tf_op jit(solution)/shard_map/ppermute | solution.py:29
  7.0 0.0 collective-permute-start.2
  7.0 1.5 %collective-permute-start.3 = (bf16[128,512]{1,0:T(8,128)(2,1)S(1)}, bf16[128,512]{1,0:T(8,128)(2,1)S(1)}, u32[]{:S(2)}, u32[]{:S(2)}) collective-permute-start(bf16[128,512]{1,0:T(8,128)(2,1)S(1)} %collective-permute-done.rest_1_.refs_1_), channel_id=1, source_target_pairs={{0,4},{4,8},{8,12},{12,14},{14,10},{10,6},{6,2},{2,0},{1,3},{5,1},... | collective-permute-start | bytes 393224 | tf_op jit(solution)/shard_map/ppermute | solution.py:29
  8.5 0.0 collective-permute-done.1.rest_2_.refs_2_
  8.5 1.0 %collective-permute-start.5 = (bf16[128,512]{1,0:T(8,128)(2,1)S(1)}, bf16[128,512]{1,0:T(8,128)(2,1)S(1)}, u32[]{:S(2)}, u32[]{:S(2)}) collective-permute-start(bf16[128,512]{1,0:T(8,128)(2,1)S(1)} %collective-permute-done.1.rest_2_.refs_2_), channel_id=1, source_target_pairs={{0,2},{4,0},{8,4},{12,8},{14,12},{10,14},{6,10},{2,6},{1,5},{5,9},... | collective-permute-start | bytes 393224 | tf_op jit(solution)/shard_map/ppermute | solution.py:29
  9.5 0.0 copy-done.2
  9.5 3.3 %collective-permute-start.7 = (bf16[128,512]{1,0:T(8,128)(2,1)S(1)}, bf16[128,512]{1,0:T(8,128)(2,1)S(1)}, u32[]{:S(2)}, u32[]{:S(2)}) collective-permute-start(bf16[128,512]{1,0:T(8,128)(2,1)S(1)} %get-tuple-element.22), channel_id=1, source_target_pairs={{0,12},{1,13},{4,6},{5,7},{8,10},{9,11},{12,0},{13,1},{14,2},{15,3... | collective-permute-start | bytes 393224 | tf_op jit(solution)/shard_map/ppermute | solution.py:39
  12.8 0.0 collective-permute-start.9
  12.8 0.0 collective-permute-done.3.rest_0_
  12.8 1.7 %collective-permute-start.4 = (bf16[128,512]{1,0:T(8,128)(2,1)S(1)}, bf16[128,512]{1,0:T(8,128)(2,1)S(1)}, u32[]{:S(2)}, u32[]{:S(2)}) collective-permute-start(bf16[128,512]{1,0:T(8,128)(2,1)S(1)} %collective-permute-done.3.rest_0_), channel_id=1, source_target_pairs={{0,4},{4,8},{8,12},{12,14},{14,10},{10,6},{6,2},{2,0},{1,3},{5,1},... | collective-permute-start | bytes 393224 | tf_op jit(solution)/shard_map/ppermute | solution.py:29
  14.5 0.0 collective-permute-done.5.rest_1_
  14.5 0.8 %collective-permute-start.6 = (bf16[128,512]{1,0:T(8,128)(2,1)S(1)}, bf16[128,512]{1,0:T(8,128)(2,1)S(1)}, u32[]{:S(2)}, u32[]{:S(2)}) collective-permute-start(bf16[128,512]{1,0:T(8,128)(2,1)S(1)} %collective-permute-done.5.rest_1_), channel_id=1, source_target_pairs={{0,2},{4,0},{8,4},{12,8},{14,12},{10,14},{6,10},{2,6},{1,5},{5,9},... | collective-permute-start | bytes 393224 | tf_op jit(solution)/shard_map/ppermute | solution.py:29
  15.3 0.0 collective-permute-done.2.rest_3_
  15.3 0.0 copy-done
  15.3 0.0 copy-done.1
  15.3 1.0 %add_pieces.4 = (f32[256,512]{1,0:T(8,128)S(1)}, bf16[256,1024]{1,0:T(8,128)(2,1)S(1)}) custom-call(s32[1,128]{1,0:T(1,128)S(1)} %slot_table.1.table_ref, f32[256,512]{1,0:T(8,128)S(1)} %copy-done, s32[256,1024]{1,0:T(8,128)S(1)} %copy-done.1, bf16[128,512]{1,0:T(8,128)(2,1)S(1)} %copy-done.2, bf16[128,512]{1,0:T(8,128)(2,1)S(1)} %collective-permute-done.rest_1_.refs_1_, ...), custom_call_target="tpu_custom_call" | custom-call | flops 536870912 | bytes 1048576 | tf_op jit(solution)/shard_map/add_pieces/pallas_call | solution.py:224
  16.4 0.7 %add_pieces.5 = (f32[256,512]{1,0:T(8,128)S(1)}, bf16[256,512]{1,0:T(8,128)(2,1)S(1)}) custom-call(s32[1,128]{1,0:T(1,128)S(1)} %slot_table.1.table_ref, bf16[256,1024]{1,0:T(8,128)(2,1)S(1)} %get-tuple-element.21.given_ref, s32[256,1024]{1,0:T(8,128)S(1)} %copy-done.1, ...), custom_call_target="tpu_custom_call", output_to_operand_aliasing={{0}: (5, {})} | custom-call | flops 4294967296 | bytes 1048576 | tf_op jit(solution)/shard_map/add_pieces/pallas_call | solution.py:224
  17.1 0.1 collective-permute-start.10
  17.1 2.7 %collective-permute-done.7.refs_2_.rest_2_ = bf16[128,512]{1,0:T(8,128)(2,1)S(1)} collective-permute-done((bf16[128,512]{1,0:T(8,128)(2,1)S(1)}, bf16[128,512]{1,0:T(8,128)(2,1)S(1)}, u32[]{:S(2)}, u32[]{:S(2)}) %collective-permute-start.7) | collective-permute-done | bytes 131104 | tf_op jit(solution)/shard_map/ppermute | solution.py:39
  19.9 0.0 collective-permute-done.4.refs_0_.rest_0_
  19.9 0.7 %collective-permute-done.6.refs_1_.rest_1_ = bf16[128,512]{1,0:T(8,128)(2,1)S(1)} collective-permute-done((bf16[128,512]{1,0:T(8,128)(2,1)S(1)}, bf16[128,512]{1,0:T(8,128)(2,1)S(1)}, u32[]{:S(2)}, u32[]{:S(2)}) %collective-permute-start.6) | collective-permute-done | bytes 131104 | tf_op jit(solution)/shard_map/ppermute | solution.py:29
  20.6 0.1 collective-permute-start.8
  20.7 0.0 collective-permute-done.9.rest_3_
  20.7 0.0 collective-permute-done.10.rest_4_
  20.7 0.7 %add_pieces.6.rest_1_ = f32[256,512]{1,0:T(8,128)S(1)} custom-call(s32[1,128]{1,0:T(1,128)S(1)} %slot_table.1.table_ref, bf16[256,1024]{1,0:T(8,128)(2,1)S(1)} %get-tuple-element.21.given_ref, s32[256,1024]{1,0:T(8,128)S(1)} %copy-done.1, bf16[128,512]{1,0:T(8,128)(2,1)S(1)} %collective-permute-done.4.refs_0_.rest_0_, ...), custom_call_target="tpu_custom_call", output_to_operand_aliasing={{}: (8, {})} | custom-call | flops 15032385536 | bytes 1048576 | tf_op jit(solution)/shard_map/add_pieces/pallas_call | solution.py:224
  21.5 1.0 %collective-permute-done.8.rest_0_ = bf16[384,512]{1,0:T(8,128)(2,1)S(1)} collective-permute-done((bf16[384,512]{1,0:T(8,128)(2,1)S(1)}, bf16[384,512]{1,0:T(8,128)(2,1)S(1)}, u32[]{:S(2)}, u32[]{:S(2)}) %collective-permute-start.8) | collective-permute-done | bytes 393248 | tf_op jit(solution)/shard_map/ppermute | solution.py:43
  22.4 0.2 add_pieces.7
  22.6 11.6 %all_to_all.11 = f32[16,1,128]{2,1,0:T(1,128)S(1)} all-to-all(f32[16,1,128]{2,1,0:T(1,128)S(1)} %bitcast.7), channel_id=1, replica_groups=mesh['group'=2,'loop'=16] {'loop'}, dimensions={0} | all-to-all | bytes 16384 | tf_op jit(solution)/shard_map/all_to_all | solution.py:376
  34.3 0.9 %update.1 = f32[256,512]{1,0:T(8,128)} custom-call(f32[256,512]{1,0:T(8,128)S(1)} %copy-done, f32[256,512]{1,0:T(8,128)S(1)} %get-tuple-element.31.grad_ref, f32[16,128]{1,0:T(8,128)S(1)} %bitcast.6), custom_call_target="tpu_custom_call" | custom-call | flops 262144 | bytes 1572864 | tf_op jit(solution)/shard_map/update/pallas_call | solution.py:377
  (2 shorter events, 0.1 us)
Async XLA Ops:
  0.0 7.0 %collective-permute-start = (bf16[128,512]{1,0:T(8,128)(2,1)}, bf16[128,512]{1,0:T(8,128)(2,1)S(1)}, u32[]{:S(2)}, u32[]{:S(2)}) collective-permute-start(bf16[128,512]{1,0:T(8,128)(2,1)} %refs_0_.1), channel_id=1, source_target_pairs={{0,4},{4,8},{8,12},{12,14},{14,10},{10,6},{6,2},{2,0},{1,3},{5,1},... | collective-permute-start | bytes 393224 | tf_op jit(solution)/shard_map/ppermute | solution.py:29
  3.0 5.5 %collective-permute-start.1 = (bf16[128,512]{1,0:T(8,128)(2,1)}, bf16[128,512]{1,0:T(8,128)(2,1)S(1)}, u32[]{:S(2)}, u32[]{:S(2)}) collective-permute-start(bf16[128,512]{1,0:T(8,128)(2,1)} %refs_0_.1), channel_id=1, source_target_pairs={{0,2},{4,0},{8,4},{12,8},{14,12},{10,14},{6,10},{2,6},{1,5},{5,9},... | collective-permute-start | bytes 393224 | tf_op jit(solution)/shard_map/ppermute | solution.py:29
  3.7 0.7 %copy-start.3 = (s32[1,8]{1,0:T(1,128)S(1)}, s32[1,8]{1,0:T(1,128)}, u32[]{:S(2)}) copy-start(s32[1,8]{1,0:T(1,128)} %list_ref.1) | copy-start | bytes 100
  4.3 5.1 %copy-start.2 = (bf16[128,512]{1,0:T(8,128)(2,1)S(1)}, bf16[128,512]{1,0:T(8,128)(2,1)}, u32[]{:S(2)}) copy-start(bf16[128,512]{1,0:T(8,128)(2,1)} %refs_0_.1) | copy-start | bytes 393220
  4.5 10.8 %copy-start = (f32[256,512]{1,0:T(8,128)S(1)}, f32[256,512]{1,0:T(8,128)}, u32[]{:S(2)}) copy-start(f32[256,512]{1,0:T(8,128)} %users_ref.1) | copy-start | bytes 1572868
  4.5 10.8 %copy-start.1 = (s32[256,1024]{1,0:T(8,128)S(1)}, s32[256,1024]{1,0:T(8,128)}, u32[]{:S(2)}) copy-start(s32[256,1024]{1,0:T(8,128)} %labels_ref.7) | copy-start | bytes 3145732
  7.0 8.3 %collective-permute-start.2 = (bf16[128,512]{1,0:T(8,128)(2,1)S(1)}, bf16[128,512]{1,0:T(8,128)(2,1)S(1)}, u32[]{:S(2)}, u32[]{:S(2)}) collective-permute-start(bf16[128,512]{1,0:T(8,128)(2,1)S(1)} %collective-permute-done.rest_1_.refs_1_), channel_id=1, source_target_pairs={{0,1},{1,0},{2,3},{3,2},{4,5},{5,4},{6,7},{7,6},{8,9},{9,8},{10,11... | collective-permute-start | bytes 393224 | tf_op jit(solution)/shard_map/ppermute | solution.py:43
  7.0 5.8 %collective-permute-start.3 = (bf16[128,512]{1,0:T(8,128)(2,1)S(1)}, bf16[128,512]{1,0:T(8,128)(2,1)S(1)}, u32[]{:S(2)}, u32[]{:S(2)}) collective-permute-start(bf16[128,512]{1,0:T(8,128)(2,1)S(1)} %collective-permute-done.rest_1_.refs_1_), channel_id=1, source_target_pairs={{0,4},{4,8},{8,12},{12,14},{14,10},{10,6},{6,2},{2,0},{1,3},{5,1},... | collective-permute-start | bytes 393224 | tf_op jit(solution)/shard_map/ppermute | solution.py:29
  8.5 6.0 %collective-permute-start.5 = (bf16[128,512]{1,0:T(8,128)(2,1)S(1)}, bf16[128,512]{1,0:T(8,128)(2,1)S(1)}, u32[]{:S(2)}, u32[]{:S(2)}) collective-permute-start(bf16[128,512]{1,0:T(8,128)(2,1)S(1)} %collective-permute-done.1.rest_2_.refs_2_), channel_id=1, source_target_pairs={{0,2},{4,0},{8,4},{12,8},{14,12},{10,14},{6,10},{2,6},{1,5},{5,9},... | collective-permute-start | bytes 393224 | tf_op jit(solution)/shard_map/ppermute | solution.py:29
  9.5 10.4 %collective-permute-start.7 = (bf16[128,512]{1,0:T(8,128)(2,1)S(1)}, bf16[128,512]{1,0:T(8,128)(2,1)S(1)}, u32[]{:S(2)}, u32[]{:S(2)}) collective-permute-start(bf16[128,512]{1,0:T(8,128)(2,1)S(1)} %get-tuple-element.22), channel_id=1, source_target_pairs={{0,12},{1,13},{4,6},{5,7},{8,10},{9,11},{12,0},{13,1},{14,2},{15,3... | collective-permute-start | bytes 393224 | tf_op jit(solution)/shard_map/ppermute | solution.py:39
  12.8 7.9 %collective-permute-start.9 = (bf16[256,512]{1,0:T(8,128)(2,1)S(1)}, bf16[256,512]{1,0:T(8,128)(2,1)S(1)}, u32[]{:S(2)}, u32[]{:S(2)}) collective-permute-start(bf16[256,512]{1,0:T(8,128)(2,1)S(1)} %get-tuple-element.28), channel_id=1, source_target_pairs={{0,1},{1,0},{2,3},{3,2},{4,5},{5,4},{6,7},{7,6},{8,9},{9,8},{10,11... | collective-permute-start | bytes 786440 | tf_op jit(solution)/shard_map/ppermute | solution.py:43
  12.8 7.1 %collective-permute-start.4 = (bf16[128,512]{1,0:T(8,128)(2,1)S(1)}, bf16[128,512]{1,0:T(8,128)(2,1)S(1)}, u32[]{:S(2)}, u32[]{:S(2)}) collective-permute-start(bf16[128,512]{1,0:T(8,128)(2,1)S(1)} %collective-permute-done.3.rest_0_), channel_id=1, source_target_pairs={{0,4},{4,8},{8,12},{12,14},{14,10},{10,6},{6,2},{2,0},{1,3},{5,1},... | collective-permute-start | bytes 393224 | tf_op jit(solution)/shard_map/ppermute | solution.py:29
  14.5 6.1 %collective-permute-start.6 = (bf16[128,512]{1,0:T(8,128)(2,1)S(1)}, bf16[128,512]{1,0:T(8,128)(2,1)S(1)}, u32[]{:S(2)}, u32[]{:S(2)}) collective-permute-start(bf16[128,512]{1,0:T(8,128)(2,1)S(1)} %collective-permute-done.5.rest_1_), channel_id=1, source_target_pairs={{0,2},{4,0},{8,4},{12,8},{14,12},{10,14},{6,10},{2,6},{1,5},{5,9},... | collective-permute-start | bytes 393224 | tf_op jit(solution)/shard_map/ppermute | solution.py:29
  17.1 3.7 %collective-permute-start.10 = (bf16[256,512]{1,0:T(8,128)(2,1)S(1)}, bf16[256,512]{1,0:T(8,128)(2,1)S(1)}, u32[]{:S(2)}, u32[]{:S(2)}) collective-permute-start(bf16[256,512]{1,0:T(8,128)(2,1)S(1)} %get-tuple-element.29), channel_id=1, source_target_pairs={{0,1},{1,0},{2,3},{3,2},{4,5},{5,4},{6,7},{7,6},{8,9},{9,8},{10,11... | collective-permute-start | bytes 786440 | tf_op jit(solution)/shard_map/ppermute | solution.py:43
  20.6 1.8 %collective-permute-start.8 = (bf16[384,512]{1,0:T(8,128)(2,1)S(1)}, bf16[384,512]{1,0:T(8,128)(2,1)S(1)}, u32[]{:S(2)}, u32[]{:S(2)}) collective-permute-start(bf16[384,512]{1,0:T(8,128)(2,1)S(1)} %pack.3), channel_id=1, source_target_pairs={{0,1},{1,0},{2,3},{3,2},{4,5},{5,4},{6,7},{7,6},{8,9},{9,8},{10,11... | collective-permute-start | bytes 1179656 | tf_op jit(solution)/shard_map/ppermute | solution.py:43

commit v30 on v29

--- a/solution.py
+++ b/solution.py
@@ -379,7 +379,7 @@
         out_shape=jax.ShapeDtypeStruct((rows, width), jnp.float32),
         in_specs=[pl.BlockSpec(memory_space=pltpu.VMEM)] * 3,
         out_specs=pl.BlockSpec(memory_space=pl.ANY),
-        scratch_shapes=[pltpu.VMEM((rows, width), jnp.float32), pltpu.SemaphoreType.DMA((4,))],
+        scratch_shapes=[pltpu.VMEM((rows, width), jnp.float32), pltpu.SemaphoreType.DMA((8,))],
         compiler_params=pltpu.CompilerParams(vmem_limit_bytes=16 * 1024 * 1024),
         cost_estimate=pl.CostEstimate(
             flops=2 * rows * width, bytes_accessed=12 * rows * width, transcendentals=0

time: 35.2 us -> 35.6 us (1.011)
  Pallas kernels: 3.8 us -> 2.48 us
  starting transfers between devices: 11.4 us -> 12.3 us
  waiting for transfers between devices: 6.9 us -> 7.43 us
  blocking collectives: 11.6 us -> 12 us
    pallas_call x4, Pallas kernels: 2.67 us -> 1.32 us  [add_pieces(): pl.pallas_call(functools.partial(pieces_kernel, places, len(arrays), pack...]
    ppermute x4, starting transfers between devices: 0.15 us -> 0.97 us  [to_other_core(): lax.ppermute(array, 'loop', [(at, at ^ 1) for at in range(loop_size)])]
    ppermute x1, waiting for transfers between devices: 2.73 us -> 3.26 us  [across(): return lax.ppermute(array, 'loop', pairs)]
  transfers between devices with their start and end apart: 11 -> 11, of which waited for: 4 -> 4; matrix products, arithmetic and copies ran while one was open for 0% -> 0% of each run, Pallas kernels for 8% -> 4%
where the time goes in v30:
time: 35.6 us
  starting transfers between devices  12.3 us (35%)
  blocking collectives  12 us (34%)
  waiting for transfers between devices  7.43 us (21%)
  Pallas kernels  2.48 us (7%)
  between operations  0.75 us (2%)
  local copies, waits for them, and re-layouts  0.66 us (2%)
    all_to_all x1, blocking collectives, local(): squares = lax.all_to_all(square, 'loop', 0, 0, tiled=True)  12 us
    ppermute x6, starting transfers between devices, to_next(): return lax.ppermute(array, 'loop', pairs)  7.99 us
    ppermute x1, starting transfers between devices, across(): return lax.ppermute(array, 'loop', pairs)  3.31 us
    ppermute x1, waiting for transfers between devices, across(): return lax.ppermute(array, 'loop', pairs)  3.26 us
    ppermute x6, waiting for transfers between devices, to_next(): return lax.ppermute(array, 'loop', pairs)  3.2 us
    pallas_call x4, Pallas kernels, add_pieces(): pl.pallas_call(functools.partial(pieces_kernel, places, len(arrays), pack...  1.32 us
    ppermute x4, starting transfers between devices, to_other_core(): lax.ppermute(array, 'loop', [(at, at ^ 1) for at in range(loop_size)])  0.97 us
    ppermute x4, waiting for transfers between devices, to_other_core(): lax.ppermute(array, 'loop', [(at, at ^ 1) for at in range(loop_size)])  0.96 us
  transfers between devices with their start and end apart: 11, of which 4 were waited for; matrix products, arithmetic and copies ran while one was open for 0% of the time, Pallas kernels for 4%

profile of v30, /device:TPU:0, one launch (start us, length us, event | category | flops | bytes accessed | tf_op | source)
XLA Modules:
  0.0 35.6 jit_solution(11389093115380130897)
XLA Ops:
  0.0 3.0 %collective-permute-start = (bf16[128,512]{1,0:T(8,128)(2,1)}, bf16[128,512]{1,0:T(8,128)(2,1)S(1)}, u32[]{:S(2)}, u32[]{:S(2)}) collective-permute-start(bf16[128,512]{1,0:T(8,128)(2,1)} %refs_0_.1), channel_id=1, source_target_pairs={{0,4},{4,8},{8,12},{12,14},{14,10},{10,6},{6,2},{2,0},{1,3},{5,1},... | collective-permute-start | bytes 393224 | tf_op jit(solution)/shard_map/ppermute | solution.py:29
  3.0 0.0 collective-permute-start.1
  3.7 0.0 copy-start.3
  3.7 0.6 %copy-done.3 = s32[1,8]{1,0:T(1,128)S(1)} copy-done((s32[1,8]{1,0:T(1,128)S(1)}, s32[1,8]{1,0:T(1,128)}, u32[]{:S(2)}) %copy-start.3) | copy-done | bytes 56
  4.3 0.0 copy-start.2
  4.3 0.1 slot_table.1.table_ref
  4.5 0.0 copy-start
  4.5 0.0 copy-start.1
  4.5 2.5 %collective-permute-done.rest_1_.refs_1_ = bf16[128,512]{1,0:T(8,128)(2,1)S(1)} collective-permute-done((bf16[128,512]{1,0:T(8,128)(2,1)}, bf16[128,512]{1,0:T(8,128)(2,1)S(1)}, u32[]{:S(2)}, u32[]{:S(2)}) %collective-permute-start) | collective-permute-done | bytes 131104 | tf_op jit(solution)/shard_map/ppermute | solution.py:29
  7.0 0.0 collective-permute-start.2
  7.0 1.5 %collective-permute-start.3 = (bf16[128,512]{1,0:T(8,128)(2,1)S(1)}, bf16[128,512]{1,0:T(8,128)(2,1)S(1)}, u32[]{:S(2)}, u32[]{:S(2)}) collective-permute-start(bf16[128,512]{1,0:T(8,128)(2,1)S(1)} %collective-permute-done.rest_1_.refs_1_), channel_id=1, source_target_pairs={{0,4},{4,8},{8,12},{12,14},{14,10},{10,6},{6,2},{2,0},{1,3},{5,1},... | collective-permute-start | bytes 393224 | tf_op jit(solution)/shard_map/ppermute | solution.py:29
  8.5 0.0 collective-permute-done.1.rest_2_.refs_2_
  8.5 1.0 %collective-permute-start.5 = (bf16[128,512]{1,0:T(8,128)(2,1)S(1)}, bf16[128,512]{1,0:T(8,128)(2,1)S(1)}, u32[]{:S(2)}, u32[]{:S(2)}) collective-permute-start(bf16[128,512]{1,0:T(8,128)(2,1)S(1)} %collective-permute-done.1.rest_2_.refs_2_), channel_id=1, source_target_pairs={{0,2},{4,0},{8,4},{12,8},{14,12},{10,14},{6,10},{2,6},{1,5},{5,9},... | collective-permute-start | bytes 393224 | tf_op jit(solution)/shard_map/ppermute | solution.py:29
  9.5 0.0 copy-done.2
  9.5 3.3 %collective-permute-start.7 = (bf16[128,512]{1,0:T(8,128)(2,1)S(1)}, bf16[128,512]{1,0:T(8,128)(2,1)S(1)}, u32[]{:S(2)}, u32[]{:S(2)}) collective-permute-start(bf16[128,512]{1,0:T(8,128)(2,1)S(1)} %get-tuple-element.22), channel_id=1, source_target_pairs={{0,12},{1,13},{4,6},{5,7},{8,10},{9,11},{12,0},{13,1},{14,2},{15,3... | collective-permute-start | bytes 393224 | tf_op jit(solution)/shard_map/ppermute | solution.py:39
  12.8 0.0 collective-permute-start.9
  12.8 0.0 collective-permute-done.3.rest_0_
  12.8 1.7 %collective-permute-start.4 = (bf16[128,512]{1,0:T(8,128)(2,1)S(1)}, bf16[128,512]{1,0:T(8,128)(2,1)S(1)}, u32[]{:S(2)}, u32[]{:S(2)}) collective-permute-start(bf16[128,512]{1,0:T(8,128)(2,1)S(1)} %collective-permute-done.3.rest_0_), channel_id=1, source_target_pairs={{0,4},{4,8},{8,12},{12,14},{14,10},{10,6},{6,2},{2,0},{1,3},{5,1},... | collective-permute-start | bytes 393224 | tf_op jit(solution)/shard_map/ppermute | solution.py:29
  14.5 0.0 collective-permute-done.5.rest_1_
  14.5 0.8 %collective-permute-start.6 = (bf16[128,512]{1,0:T(8,128)(2,1)S(1)}, bf16[128,512]{1,0:T(8,128)(2,1)S(1)}, u32[]{:S(2)}, u32[]{:S(2)}) collective-permute-start(bf16[128,512]{1,0:T(8,128)(2,1)S(1)} %collective-permute-done.5.rest_1_), channel_id=1, source_target_pairs={{0,2},{4,0},{8,4},{12,8},{14,12},{10,14},{6,10},{2,6},{1,5},{5,9},... | collective-permute-start | bytes 393224 | tf_op jit(solution)/shard_map/ppermute | solution.py:29
  15.3 0.0 collective-permute-done.2.rest_3_
  15.3 0.0 copy-done
  15.3 0.0 copy-done.1
  15.3 0.3 add_pieces.4
  15.6 0.1 add_pieces.5
  15.7 0.9 %collective-permute-start.10 = (bf16[256,512]{1,0:T(8,128)(2,1)S(1)}, bf16[256,512]{1,0:T(8,128)(2,1)S(1)}, u32[]{:S(2)}, u32[]{:S(2)}) collective-permute-start(bf16[256,512]{1,0:T(8,128)(2,1)S(1)} %get-tuple-element.29), channel_id=1, source_target_pairs={{0,1},{1,0},{2,3},{3,2},{4,5},{5,4},{6,7},{7,6},{8,9},{9,8},{10,11... | collective-permute-start | bytes 786440 | tf_op jit(solution)/shard_map/ppermute | solution.py:43
  16.6 3.3 %collective-permute-done.7.refs_2_.rest_2_ = bf16[128,512]{1,0:T(8,128)(2,1)S(1)} collective-permute-done((bf16[128,512]{1,0:T(8,128)(2,1)S(1)}, bf16[128,512]{1,0:T(8,128)(2,1)S(1)}, u32[]{:S(2)}, u32[]{:S(2)}) %collective-permute-start.7) | collective-permute-done | bytes 131104 | tf_op jit(solution)/shard_map/ppermute | solution.py:39
  19.9 0.0 collective-permute-done.4.refs_0_.rest_0_
  19.9 0.7 %collective-permute-done.6.refs_1_.rest_1_ = bf16[128,512]{1,0:T(8,128)(2,1)S(1)} collective-permute-done((bf16[128,512]{1,0:T(8,128)(2,1)S(1)}, bf16[128,512]{1,0:T(8,128)(2,1)S(1)}, u32[]{:S(2)}, u32[]{:S(2)}) %collective-permute-start.6) | collective-permute-done | bytes 131104 | tf_op jit(solution)/shard_map/ppermute | solution.py:29
  20.6 0.1 collective-permute-start.8
  20.7 0.0 collective-permute-done.9.rest_3_
  20.7 0.0 collective-permute-done.10.rest_4_
  20.7 0.7 %add_pieces.6.rest_1_ = f32[256,512]{1,0:T(8,128)S(1)} custom-call(s32[1,128]{1,0:T(1,128)S(1)} %slot_table.1.table_ref, bf16[256,1024]{1,0:T(8,128)(2,1)S(1)} %get-tuple-element.21.given_ref, s32[256,1024]{1,0:T(8,128)S(1)} %copy-done.1, bf16[128,512]{1,0:T(8,128)(2,1)S(1)} %collective-permute-done.4.refs_0_.rest_0_, ...), custom_call_target="tpu_custom_call", output_to_operand_aliasing={{}: (8, {})} | custom-call | flops 15032385536 | bytes 1048576 | tf_op jit(solution)/shard_map/add_pieces/pallas_call | solution.py:224
  21.5 1.0 %collective-permute-done.8.rest_0_ = bf16[384,512]{1,0:T(8,128)(2,1)S(1)} collective-permute-done((bf16[384,512]{1,0:T(8,128)(2,1)S(1)}, bf16[384,512]{1,0:T(8,128)(2,1)S(1)}, u32[]{:S(2)}, u32[]{:S(2)}) %collective-permute-start.8) | collective-permute-done | bytes 393248 | tf_op jit(solution)/shard_map/ppermute | solution.py:43
  22.4 0.2 add_pieces.7
  22.6 12.0 %all_to_all.11 = f32[16,1,128]{2,1,0:T(1,128)S(1)} all-to-all(f32[16,1,128]{2,1,0:T(1,128)S(1)} %bitcast.7), channel_id=1, replica_groups=mesh['group'=2,'loop'=16] {'loop'}, dimensions={0} | all-to-all | bytes 16384 | tf_op jit(solution)/shard_map/all_to_all | solution.py:376
  34.6 1.0 %update.1 = f32[256,512]{1,0:T(8,128)} custom-call(f32[256,512]{1,0:T(8,128)S(1)} %copy-done, f32[256,512]{1,0:T(8,128)S(1)} %get-tuple-element.31.grad_ref, f32[16,128]{1,0:T(8,128)S(1)} %bitcast.6), custom_call_target="tpu_custom_call" | custom-call | flops 262144 | bytes 1572864 | tf_op jit(solution)/shard_map/update/pallas_call | solution.py:377
  (2 shorter events, 0.1 us)
Async XLA Ops:
  0.0 7.0 %collective-permute-start = (bf16[128,512]{1,0:T(8,128)(2,1)}, bf16[128,512]{1,0:T(8,128)(2,1)S(1)}, u32[]{:S(2)}, u32[]{:S(2)}) collective-permute-start(bf16[128,512]{1,0:T(8,128)(2,1)} %refs_0_.1), channel_id=1, source_target_pairs={{0,4},{4,8},{8,12},{12,14},{14,10},{10,6},{6,2},{2,0},{1,3},{5,1},... | collective-permute-start | bytes 393224 | tf_op jit(solution)/shard_map/ppermute | solution.py:29
  3.0 5.5 %collective-permute-start.1 = (bf16[128,512]{1,0:T(8,128)(2,1)}, bf16[128,512]{1,0:T(8,128)(2,1)S(1)}, u32[]{:S(2)}, u32[]{:S(2)}) collective-permute-start(bf16[128,512]{1,0:T(8,128)(2,1)} %refs_0_.1), channel_id=1, source_target_pairs={{0,2},{4,0},{8,4},{12,8},{14,12},{10,14},{6,10},{2,6},{1,5},{5,9},... | collective-permute-start | bytes 393224 | tf_op jit(solution)/shard_map/ppermute | solution.py:29
  3.7 0.7 %copy-start.3 = (s32[1,8]{1,0:T(1,128)S(1)}, s32[1,8]{1,0:T(1,128)}, u32[]{:S(2)}) copy-start(s32[1,8]{1,0:T(1,128)} %list_ref.1) | copy-start | bytes 100
  4.3 5.1 %copy-start.2 = (bf16[128,512]{1,0:T(8,128)(2,1)S(1)}, bf16[128,512]{1,0:T(8,128)(2,1)}, u32[]{:S(2)}) copy-start(bf16[128,512]{1,0:T(8,128)(2,1)} %refs_0_.1) | copy-start | bytes 393220
  4.5 10.8 %copy-start = (f32[256,512]{1,0:T(8,128)S(1)}, f32[256,512]{1,0:T(8,128)}, u32[]{:S(2)}) copy-start(f32[256,512]{1,0:T(8,128)} %users_ref.1) | copy-start | bytes 1572868
  4.5 10.8 %copy-start.1 = (s32[256,1024]{1,0:T(8,128)S(1)}, s32[256,1024]{1,0:T(8,128)}, u32[]{:S(2)}) copy-start(s32[256,1024]{1,0:T(8,128)} %labels_ref.7) | copy-start | bytes 3145732
  7.0 8.3 %collective-permute-start.2 = (bf16[128,512]{1,0:T(8,128)(2,1)S(1)}, bf16[128,512]{1,0:T(8,128)(2,1)S(1)}, u32[]{:S(2)}, u32[]{:S(2)}) collective-permute-start(bf16[128,512]{1,0:T(8,128)(2,1)S(1)} %collective-permute-done.rest_1_.refs_1_), channel_id=1, source_target_pairs={{0,1},{1,0},{2,3},{3,2},{4,5},{5,4},{6,7},{7,6},{8,9},{9,8},{10,11... | collective-permute-start | bytes 393224 | tf_op jit(solution)/shard_map/ppermute | solution.py:43
  7.0 5.8 %collective-permute-start.3 = (bf16[128,512]{1,0:T(8,128)(2,1)S(1)}, bf16[128,512]{1,0:T(8,128)(2,1)S(1)}, u32[]{:S(2)}, u32[]{:S(2)}) collective-permute-start(bf16[128,512]{1,0:T(8,128)(2,1)S(1)} %collective-permute-done.rest_1_.refs_1_), channel_id=1, source_target_pairs={{0,4},{4,8},{8,12},{12,14},{14,10},{10,6},{6,2},{2,0},{1,3},{5,1},... | collective-permute-start | bytes 393224 | tf_op jit(solution)/shard_map/ppermute | solution.py:29
  8.5 6.0 %collective-permute-start.5 = (bf16[128,512]{1,0:T(8,128)(2,1)S(1)}, bf16[128,512]{1,0:T(8,128)(2,1)S(1)}, u32[]{:S(2)}, u32[]{:S(2)}) collective-permute-start(bf16[128,512]{1,0:T(8,128)(2,1)S(1)} %collective-permute-done.1.rest_2_.refs_2_), channel_id=1, source_target_pairs={{0,2},{4,0},{8,4},{12,8},{14,12},{10,14},{6,10},{2,6},{1,5},{5,9},... | collective-permute-start | bytes 393224 | tf_op jit(solution)/shard_map/ppermute | solution.py:29
  9.5 10.4 %collective-permute-start.7 = (bf16[128,512]{1,0:T(8,128)(2,1)S(1)}, bf16[128,512]{1,0:T(8,128)(2,1)S(1)}, u32[]{:S(2)}, u32[]{:S(2)}) collective-permute-start(bf16[128,512]{1,0:T(8,128)(2,1)S(1)} %get-tuple-element.22), channel_id=1, source_target_pairs={{0,12},{1,13},{4,6},{5,7},{8,10},{9,11},{12,0},{13,1},{14,2},{15,3... | collective-permute-start | bytes 393224 | tf_op jit(solution)/shard_map/ppermute | solution.py:39
  12.8 7.9 %collective-permute-start.9 = (bf16[256,512]{1,0:T(8,128)(2,1)S(1)}, bf16[256,512]{1,0:T(8,128)(2,1)S(1)}, u32[]{:S(2)}, u32[]{:S(2)}) collective-permute-start(bf16[256,512]{1,0:T(8,128)(2,1)S(1)} %get-tuple-element.28), channel_id=1, source_target_pairs={{0,1},{1,0},{2,3},{3,2},{4,5},{5,4},{6,7},{7,6},{8,9},{9,8},{10,11... | collective-permute-start | bytes 786440 | tf_op jit(solution)/shard_map/ppermute | solution.py:43
  12.8 7.1 %collective-permute-start.4 = (bf16[128,512]{1,0:T(8,128)(2,1)S(1)}, bf16[128,512]{1,0:T(8,128)(2,1)S(1)}, u32[]{:S(2)}, u32[]{:S(2)}) collective-permute-start(bf16[128,512]{1,0:T(8,128)(2,1)S(1)} %collective-permute-done.3.rest_0_), channel_id=1, source_target_pairs={{0,4},{4,8},{8,12},{12,14},{14,10},{10,6},{6,2},{2,0},{1,3},{5,1},... | collective-permute-start | bytes 393224 | tf_op jit(solution)/shard_map/ppermute | solution.py:29
  14.5 6.1 %collective-permute-start.6 = (bf16[128,512]{1,0:T(8,128)(2,1)S(1)}, bf16[128,512]{1,0:T(8,128)(2,1)S(1)}, u32[]{:S(2)}, u32[]{:S(2)}) collective-permute-start(bf16[128,512]{1,0:T(8,128)(2,1)S(1)} %collective-permute-done.5.rest_1_), channel_id=1, source_target_pairs={{0,2},{4,0},{8,4},{12,8},{14,12},{10,14},{6,10},{2,6},{1,5},{5,9},... | collective-permute-start | bytes 393224 | tf_op jit(solution)/shard_map/ppermute | solution.py:29
  15.7 5.0 %collective-permute-start.10 = (bf16[256,512]{1,0:T(8,128)(2,1)S(1)}, bf16[256,512]{1,0:T(8,128)(2,1)S(1)}, u32[]{:S(2)}, u32[]{:S(2)}) collective-permute-start(bf16[256,512]{1,0:T(8,128)(2,1)S(1)} %get-tuple-element.29), channel_id=1, source_target_pairs={{0,1},{1,0},{2,3},{3,2},{4,5},{5,4},{6,7},{7,6},{8,9},{9,8},{10,11... | collective-permute-start | bytes 786440 | tf_op jit(solution)/shard_map/ppermute | solution.py:43
  20.6 1.8 %collective-permute-start.8 = (bf16[384,512]{1,0:T(8,128)(2,1)S(1)}, bf16[384,512]{1,0:T(8,128)(2,1)S(1)}, u32[]{:S(2)}, u32[]{:S(2)}) collective-permute-start(bf16[384,512]{1,0:T(8,128)(2,1)S(1)} %pack.3), channel_id=1, source_target_pairs={{0,1},{1,0},{2,3},{3,2},{4,5},{5,4},{6,7},{7,6},{8,9},{9,8},{10,11... | collective-permute-start | bytes 1179656 | tf_op jit(solution)/shard_map/ppermute | solution.py:43

commit v31 on v30

--- a/solution.py
+++ b/solution.py
@@ -379,7 +379,7 @@
         out_shape=jax.ShapeDtypeStruct((rows, width), jnp.float32),
         in_specs=[pl.BlockSpec(memory_space=pltpu.VMEM)] * 3,
         out_specs=pl.BlockSpec(memory_space=pl.ANY),
-        scratch_shapes=[pltpu.VMEM((rows, width), jnp.float32), pltpu.SemaphoreType.DMA((8,))],
+        scratch_shapes=[pltpu.VMEM((rows, width), jnp.float32), pltpu.SemaphoreType.DMA((2,))],
         compiler_params=pltpu.CompilerParams(vmem_limit_bytes=16 * 1024 * 1024),
         cost_estimate=pl.CostEstimate(
             flops=2 * rows * width, bytes_accessed=12 * rows * width, transcendentals=0

time: 35.6 us -> 35.5 us (level)
  starting transfers between devices: 12.3 us -> 11.4 us
  waiting for transfers between devices: 7.43 us -> 8.24 us
    ppermute x4, starting transfers between devices: 0.97 us -> 0.15 us  [to_other_core(): lax.ppermute(array, 'loop', [(at, at ^ 1) for at in range(loop_size)])]
    ppermute x4, waiting for transfers between devices: 0.96 us -> 1.52 us  [to_other_core(): lax.ppermute(array, 'loop', [(at, at ^ 1) for at in range(loop_size)])]
where the time goes in v31:
time: 35.5 us; the launch traced here: 35.3 us
  blocking collectives  11.7 us (33%)
  starting transfers between devices  11.4 us (32%)
  waiting for transfers between devices  8.24 us (23%)
  Pallas kernels  2.47 us (7%)
  between operations  0.76 us (2%)
  local copies, waits for them, and re-layouts  0.66 us (2%)
    all_to_all x1, blocking collectives, local(): squares = lax.all_to_all(square, 'loop', 0, 0, tiled=True)  11.7 us
    ppermute x6, starting transfers between devices, to_next(): return lax.ppermute(array, 'loop', pairs)  7.99 us
    ppermute x1, waiting for transfers between devices, across(): return lax.ppermute(array, 'loop', pairs)  3.52 us
    ppermute x1, starting transfers between devices, across(): return lax.ppermute(array, 'loop', pairs)  3.31 us
    ppermute x6, waiting for transfers between devices, to_next(): return lax.ppermute(array, 'loop', pairs)  3.2 us
    ppermute x4, waiting for transfers between devices, to_other_core(): lax.ppermute(array, 'loop', [(at, at ^ 1) for at in range(loop_size)])  1.52 us
    pallas_call x4, Pallas kernels, add_pieces(): pl.pallas_call(functools.partial(pieces_kernel, places, len(arrays), pack...  1.32 us
    pallas_call x1, Pallas kernels, local(): pl.pallas_call(functools.partial(update_kernel, rows * loop_size * width)...  0.94 us
  transfers between devices with their start and end apart: 11, of which 4 were waited for; matrix products, arithmetic and copies ran while one was open for 0% of the time, Pallas kernels for 4%

profile of v31, /device:TPU:0, one launch (start us, length us, event | category | flops | bytes accessed | tf_op | source)
XLA Modules:
  0.0 35.3 jit_solution(1543240126387677139)
XLA Ops:
  0.0 3.0 %collective-permute-start = (bf16[128,512]{1,0:T(8,128)(2,1)}, bf16[128,512]{1,0:T(8,128)(2,1)S(1)}, u32[]{:S(2)}, u32[]{:S(2)}) collective-permute-start(bf16[128,512]{1,0:T(8,128)(2,1)} %refs_0_.1), channel_id=1, source_target_pairs={{0,4},{4,8},{8,12},{12,14},{14,10},{10,6},{6,2},{2,0},{1,3},{5,1},... | collective-permute-start | bytes 393224 | tf_op jit(solution)/shard_map/ppermute | solution.py:29
  3.0 0.0 collective-permute-start.1
  3.7 0.0 copy-start.3
  3.7 0.6 %copy-done.3 = s32[1,8]{1,0:T(1,128)S(1)} copy-done((s32[1,8]{1,0:T(1,128)S(1)}, s32[1,8]{1,0:T(1,128)}, u32[]{:S(2)}) %copy-start.3) | copy-done | bytes 56
  4.3 0.0 copy-start.2
  4.3 0.1 slot_table.1.table_ref
  4.5 0.0 copy-start
  4.5 0.0 copy-start.1
  4.5 2.5 %collective-permute-done.rest_1_.refs_1_ = bf16[128,512]{1,0:T(8,128)(2,1)S(1)} collective-permute-done((bf16[128,512]{1,0:T(8,128)(2,1)}, bf16[128,512]{1,0:T(8,128)(2,1)S(1)}, u32[]{:S(2)}, u32[]{:S(2)}) %collective-permute-start) | collective-permute-done | bytes 131104 | tf_op jit(solution)/shard_map/ppermute | solution.py:29
  7.0 0.0 collective-permute-start.2
  7.0 1.5 %collective-permute-start.3 = (bf16[128,512]{1,0:T(8,128)(2,1)S(1)}, bf16[128,512]{1,0:T(8,128)(2,1)S(1)}, u32[]{:S(2)}, u32[]{:S(2)}) collective-permute-start(bf16[128,512]{1,0:T(8,128)(2,1)S(1)} %collective-permute-done.rest_1_.refs_1_), channel_id=1, source_target_pairs={{0,4},{4,8},{8,12},{12,14},{14,10},{10,6},{6,2},{2,0},{1,3},{5,1},... | collective-permute-start | bytes 393224 | tf_op jit(solution)/shard_map/ppermute | solution.py:29
  8.5 0.0 collective-permute-done.1.rest_2_.refs_2_
  8.5 1.0 %collective-permute-start.5 = (bf16[128,512]{1,0:T(8,128)(2,1)S(1)}, bf16[128,512]{1,0:T(8,128)(2,1)S(1)}, u32[]{:S(2)}, u32[]{:S(2)}) collective-permute-start(bf16[128,512]{1,0:T(8,128)(2,1)S(1)} %collective-permute-done.1.rest_2_.refs_2_), channel_id=1, source_target_pairs={{0,2},{4,0},{8,4},{12,8},{14,12},{10,14},{6,10},{2,6},{1,5},{5,9},... | collective-permute-start | bytes 393224 | tf_op jit(solution)/shard_map/ppermute | solution.py:29
  9.5 0.0 copy-done.2
  9.5 3.3 %collective-permute-start.7 = (bf16[128,512]{1,0:T(8,128)(2,1)S(1)}, bf16[128,512]{1,0:T(8,128)(2,1)S(1)}, u32[]{:S(2)}, u32[]{:S(2)}) collective-permute-start(bf16[128,512]{1,0:T(8,128)(2,1)S(1)} %get-tuple-element.22), channel_id=1, source_target_pairs={{0,12},{1,13},{4,6},{5,7},{8,10},{9,11},{12,0},{13,1},{14,2},{15,3... | collective-permute-start | bytes 393224 | tf_op jit(solution)/shard_map/ppermute | solution.py:39
  12.8 0.0 collective-permute-start.9
  12.8 0.0 collective-permute-done.3.rest_0_
  12.8 1.7 %collective-permute-start.4 = (bf16[128,512]{1,0:T(8,128)(2,1)S(1)}, bf16[128,512]{1,0:T(8,128)(2,1)S(1)}, u32[]{:S(2)}, u32[]{:S(2)}) collective-permute-start(bf16[128,512]{1,0:T(8,128)(2,1)S(1)} %collective-permute-done.3.rest_0_), channel_id=1, source_target_pairs={{0,4},{4,8},{8,12},{12,14},{14,10},{10,6},{6,2},{2,0},{1,3},{5,1},... | collective-permute-start | bytes 393224 | tf_op jit(solution)/shard_map/ppermute | solution.py:29
  14.5 0.0 collective-permute-done.5.rest_1_
  14.5 0.8 %collective-permute-start.6 = (bf16[128,512]{1,0:T(8,128)(2,1)S(1)}, bf16[128,512]{1,0:T(8,128)(2,1)S(1)}, u32[]{:S(2)}, u32[]{:S(2)}) collective-permute-start(bf16[128,512]{1,0:T(8,128)(2,1)S(1)} %collective-permute-done.5.rest_1_), channel_id=1, source_target_pairs={{0,2},{4,0},{8,4},{12,8},{14,12},{10,14},{6,10},{2,6},{1,5},{5,9},... | collective-permute-start | bytes 393224 | tf_op jit(solution)/shard_map/ppermute | solution.py:29
  15.3 0.0 collective-permute-done.2.rest_3_
  15.3 0.0 copy-done
  15.3 0.0 copy-done.1
  15.3 0.8 %add_pieces.4 = (f32[256,512]{1,0:T(8,128)S(1)}, bf16[256,1024]{1,0:T(8,128)(2,1)S(1)}) custom-call(s32[1,128]{1,0:T(1,128)S(1)} %slot_table.1.table_ref, f32[256,512]{1,0:T(8,128)S(1)} %copy-done, s32[256,1024]{1,0:T(8,128)S(1)} %copy-done.1, bf16[128,512]{1,0:T(8,128)(2,1)S(1)} %copy-done.2, bf16[128,512]{1,0:T(8,128)(2,1)S(1)} %collective-permute-done.rest_1_.refs_1_, ...), custom_call_target="tpu_custom_call" | custom-call | flops 536870912 | bytes 1048576 | tf_op jit(solution)/shard_map/add_pieces/pallas_call | solution.py:224
  16.1 0.1 add_pieces.5
  16.3 0.1 collective-permute-start.10
  16.4 3.5 %collective-permute-done.7.refs_2_.rest_2_ = bf16[128,512]{1,0:T(8,128)(2,1)S(1)} collective-permute-done((bf16[128,512]{1,0:T(8,128)(2,1)S(1)}, bf16[128,512]{1,0:T(8,128)(2,1)S(1)}, u32[]{:S(2)}, u32[]{:S(2)}) %collective-permute-start.7) | collective-permute-done | bytes 131104 | tf_op jit(solution)/shard_map/ppermute | solution.py:39
  19.9 0.0 collective-permute-done.4.refs_0_.rest_0_
  19.9 0.7 %collective-permute-done.6.refs_1_.rest_1_ = bf16[128,512]{1,0:T(8,128)(2,1)S(1)} collective-permute-done((bf16[128,512]{1,0:T(8,128)(2,1)S(1)}, bf16[128,512]{1,0:T(8,128)(2,1)S(1)}, u32[]{:S(2)}, u32[]{:S(2)}) %collective-permute-start.6) | collective-permute-done | bytes 131104 | tf_op jit(solution)/shard_map/ppermute | solution.py:29
  20.6 0.1 collective-permute-start.8
  20.7 0.0 collective-permute-done.9.rest_3_
  20.7 0.0 collective-permute-done.10.rest_4_
  20.7 0.2 add_pieces.6.rest_1_
  20.9 1.5 %collective-permute-done.8.rest_0_ = bf16[384,512]{1,0:T(8,128)(2,1)S(1)} collective-permute-done((bf16[384,512]{1,0:T(8,128)(2,1)S(1)}, bf16[384,512]{1,0:T(8,128)(2,1)S(1)}, u32[]{:S(2)}, u32[]{:S(2)}) %collective-permute-start.8) | collective-permute-done | bytes 393248 | tf_op jit(solution)/shard_map/ppermute | solution.py:43
  22.4 0.2 add_pieces.7
  22.6 11.7 %all_to_all.11 = f32[16,1,128]{2,1,0:T(1,128)S(1)} all-to-all(f32[16,1,128]{2,1,0:T(1,128)S(1)} %bitcast.7), channel_id=1, replica_groups=mesh['group'=2,'loop'=16] {'loop'}, dimensions={0} | all-to-all | bytes 16384 | tf_op jit(solution)/shard_map/all_to_all | solution.py:376
  34.3 0.9 %update.1 = f32[256,512]{1,0:T(8,128)} custom-call(f32[256,512]{1,0:T(8,128)S(1)} %copy-done, f32[256,512]{1,0:T(8,128)S(1)} %get-tuple-element.31.grad_ref, f32[16,128]{1,0:T(8,128)S(1)} %bitcast.6), custom_call_target="tpu_custom_call" | custom-call | flops 262144 | bytes 1572864 | tf_op jit(solution)/shard_map/update/pallas_call | solution.py:377
  (2 shorter events, 0.1 us)
Async XLA Ops:
  0.0 7.0 %collective-permute-start = (bf16[128,512]{1,0:T(8,128)(2,1)}, bf16[128,512]{1,0:T(8,128)(2,1)S(1)}, u32[]{:S(2)}, u32[]{:S(2)}) collective-permute-start(bf16[128,512]{1,0:T(8,128)(2,1)} %refs_0_.1), channel_id=1, source_target_pairs={{0,4},{4,8},{8,12},{12,14},{14,10},{10,6},{6,2},{2,0},{1,3},{5,1},... | collective-permute-start | bytes 393224 | tf_op jit(solution)/shard_map/ppermute | solution.py:29
  3.0 5.5 %collective-permute-start.1 = (bf16[128,512]{1,0:T(8,128)(2,1)}, bf16[128,512]{1,0:T(8,128)(2,1)S(1)}, u32[]{:S(2)}, u32[]{:S(2)}) collective-permute-start(bf16[128,512]{1,0:T(8,128)(2,1)} %refs_0_.1), channel_id=1, source_target_pairs={{0,2},{4,0},{8,4},{12,8},{14,12},{10,14},{6,10},{2,6},{1,5},{5,9},... | collective-permute-start | bytes 393224 | tf_op jit(solution)/shard_map/ppermute | solution.py:29
  3.7 0.7 %copy-start.3 = (s32[1,8]{1,0:T(1,128)S(1)}, s32[1,8]{1,0:T(1,128)}, u32[]{:S(2)}) copy-start(s32[1,8]{1,0:T(1,128)} %list_ref.1) | copy-start | bytes 100
  4.3 5.1 %copy-start.2 = (bf16[128,512]{1,0:T(8,128)(2,1)S(1)}, bf16[128,512]{1,0:T(8,128)(2,1)}, u32[]{:S(2)}) copy-start(bf16[128,512]{1,0:T(8,128)(2,1)} %refs_0_.1) | copy-start | bytes 393220
  4.5 10.8 %copy-start = (f32[256,512]{1,0:T(8,128)S(1)}, f32[256,512]{1,0:T(8,128)}, u32[]{:S(2)}) copy-start(f32[256,512]{1,0:T(8,128)} %users_ref.1) | copy-start | bytes 1572868
  4.5 10.8 %copy-start.1 = (s32[256,1024]{1,0:T(8,128)S(1)}, s32[256,1024]{1,0:T(8,128)}, u32[]{:S(2)}) copy-start(s32[256,1024]{1,0:T(8,128)} %labels_ref.7) | copy-start | bytes 3145732
  7.0 8.3 %collective-permute-start.2 = (bf16[128,512]{1,0:T(8,128)(2,1)S(1)}, bf16[128,512]{1,0:T(8,128)(2,1)S(1)}, u32[]{:S(2)}, u32[]{:S(2)}) collective-permute-start(bf16[128,512]{1,0:T(8,128)(2,1)S(1)} %collective-permute-done.rest_1_.refs_1_), channel_id=1, source_target_pairs={{0,1},{1,0},{2,3},{3,2},{4,5},{5,4},{6,7},{7,6},{8,9},{9,8},{10,11... | collective-permute-start | bytes 393224 | tf_op jit(solution)/shard_map/ppermute | solution.py:43
  7.0 5.8 %collective-permute-start.3 = (bf16[128,512]{1,0:T(8,128)(2,1)S(1)}, bf16[128,512]{1,0:T(8,128)(2,1)S(1)}, u32[]{:S(2)}, u32[]{:S(2)}) collective-permute-start(bf16[128,512]{1,0:T(8,128)(2,1)S(1)} %collective-permute-done.rest_1_.refs_1_), channel_id=1, source_target_pairs={{0,4},{4,8},{8,12},{12,14},{14,10},{10,6},{6,2},{2,0},{1,3},{5,1},... | collective-permute-start | bytes 393224 | tf_op jit(solution)/shard_map/ppermute | solution.py:29
  8.5 6.0 %collective-permute-start.5 = (bf16[128,512]{1,0:T(8,128)(2,1)S(1)}, bf16[128,512]{1,0:T(8,128)(2,1)S(1)}, u32[]{:S(2)}, u32[]{:S(2)}) collective-permute-start(bf16[128,512]{1,0:T(8,128)(2,1)S(1)} %collective-permute-done.1.rest_2_.refs_2_), channel_id=1, source_target_pairs={{0,2},{4,0},{8,4},{12,8},{14,12},{10,14},{6,10},{2,6},{1,5},{5,9},... | collective-permute-start | bytes 393224 | tf_op jit(solution)/shard_map/ppermute | solution.py:29
  9.5 10.4 %collective-permute-start.7 = (bf16[128,512]{1,0:T(8,128)(2,1)S(1)}, bf16[128,512]{1,0:T(8,128)(2,1)S(1)}, u32[]{:S(2)}, u32[]{:S(2)}) collective-permute-start(bf16[128,512]{1,0:T(8,128)(2,1)S(1)} %get-tuple-element.22), channel_id=1, source_target_pairs={{0,12},{1,13},{4,6},{5,7},{8,10},{9,11},{12,0},{13,1},{14,2},{15,3... | collective-permute-start | bytes 393224 | tf_op jit(solution)/shard_map/ppermute | solution.py:39
  12.8 7.9 %collective-permute-start.9 = (bf16[256,512]{1,0:T(8,128)(2,1)S(1)}, bf16[256,512]{1,0:T(8,128)(2,1)S(1)}, u32[]{:S(2)}, u32[]{:S(2)}) collective-permute-start(bf16[256,512]{1,0:T(8,128)(2,1)S(1)} %get-tuple-element.28), channel_id=1, source_target_pairs={{0,1},{1,0},{2,3},{3,2},{4,5},{5,4},{6,7},{7,6},{8,9},{9,8},{10,11... | collective-permute-start | bytes 786440 | tf_op jit(solution)/shard_map/ppermute | solution.py:43
  12.8 7.1 %collective-permute-start.4 = (bf16[128,512]{1,0:T(8,128)(2,1)S(1)}, bf16[128,512]{1,0:T(8,128)(2,1)S(1)}, u32[]{:S(2)}, u32[]{:S(2)}) collective-permute-start(bf16[128,512]{1,0:T(8,128)(2,1)S(1)} %collective-permute-done.3.rest_0_), channel_id=1, source_target_pairs={{0,4},{4,8},{8,12},{12,14},{14,10},{10,6},{6,2},{2,0},{1,3},{5,1},... | collective-permute-start | bytes 393224 | tf_op jit(solution)/shard_map/ppermute | solution.py:29
  14.5 6.1 %collective-permute-start.6 = (bf16[128,512]{1,0:T(8,128)(2,1)S(1)}, bf16[128,512]{1,0:T(8,128)(2,1)S(1)}, u32[]{:S(2)}, u32[]{:S(2)}) collective-permute-start(bf16[128,512]{1,0:T(8,128)(2,1)S(1)} %collective-permute-done.5.rest_1_), channel_id=1, source_target_pairs={{0,2},{4,0},{8,4},{12,8},{14,12},{10,14},{6,10},{2,6},{1,5},{5,9},... | collective-permute-start | bytes 393224 | tf_op jit(solution)/shard_map/ppermute | solution.py:29
  16.3 4.5 %collective-permute-start.10 = (bf16[256,512]{1,0:T(8,128)(2,1)S(1)}, bf16[256,512]{1,0:T(8,128)(2,1)S(1)}, u32[]{:S(2)}, u32[]{:S(2)}) collective-permute-start(bf16[256,512]{1,0:T(8,128)(2,1)S(1)} %get-tuple-element.29), channel_id=1, source_target_pairs={{0,1},{1,0},{2,3},{3,2},{4,5},{5,4},{6,7},{7,6},{8,9},{9,8},{10,11... | collective-permute-start | bytes 786440 | tf_op jit(solution)/shard_map/ppermute | solution.py:43
  20.6 1.8 %collective-permute-start.8 = (bf16[384,512]{1,0:T(8,128)(2,1)S(1)}, bf16[384,512]{1,0:T(8,128)(2,1)S(1)}, u32[]{:S(2)}, u32[]{:S(2)}) collective-permute-start(bf16[384,512]{1,0:T(8,128)(2,1)S(1)} %pack.3), channel_id=1, source_target_pairs={{0,1},{1,0},{2,3},{3,2},{4,5},{5,4},{6,7},{7,6},{8,9},{9,8},{10,11... | collective-permute-start | bytes 1179656 | tf_op jit(solution)/shard_map/ppermute | solution.py:43
